TPU v7x, 32 devices: a whole 2x2x4 slice. The times are simulated.
32 devices in a mesh: grp: 4 (over y, x), tile: 8 (over z, core).
Axes of the slice: x: 2, y: 2, z: 4, core: 2. Of those that a mesh axis runs over, the one named last changes fastest.
Arguments:
- right_side: float32 [16, 32, 1024], P(None, 'grp', 'tile'), may hold values from -6 to 6
- amplitude: float32 [32, 1024], P('grp', 'tile'), may hold values from 0.2 to 1
- factor: bfloat16 [2048, 32, 1024], P('tile', 'grp'), may hold values from -6 to 6
- scale: float32 [2048], P('tile'), may hold values from 0.5 to 2
Outputs:
- solution_field: float32 [16, 32, 1024], P(None, 'grp', 'tile')
- residual: float32 [16, 32, 1024], P(None, 'grp', 'tile')
All inputs are finite; a program needn't handle non-finite values.
Results may differ from a plain program's by a relative error of at most 0.0041.
Values may be sent and summed in bfloat16 or wider, within the bound.
No kernel may reach another device: no remote copies, remote signals or barrier semaphores. Data moves between devices by JAX's collectives and lax.ppermute only.
A program may use at most 64 MiB of HBM per device.

v0:
```python
import math
from functools import partial

import jax
import jax.numpy as jnp
import numpy as np
from jax import lax
from jax.experimental import pallas as pl
from jax.experimental.pallas import tpu as pltpu
from jax.sharding import PartitionSpec as P

REACH = 8
ITERS = 2
LANES = 128


def taper(sigma):
    offsets = np.arange(-REACH, REACH + 1).astype(np.float64)
    values = np.exp(-offsets * offsets / (2.0 * sigma * sigma))
    values = values * np.cos(np.pi * offsets / (2.0 * REACH + 2.0)) ** 2
    return [float(v) for v in (values / values.sum()).astype(np.float32)]


ROW_TAPS = taper(3.0)
COL_TAPS = taper(5.0)


def stencil(low, own, high, taps, axis):
    size = own.shape[axis]
    place = lax.broadcasted_iota(jnp.int32, own.shape, axis)
    total = taps[REACH] * own
    for shift in range(1, REACH + 1):
        after = pltpu.roll(jnp.where(place < shift, high, own), size - shift, axis)
        before = pltpu.roll(jnp.where(place >= size - shift, low, own), shift, axis)
        total = total + taps[REACH + shift] * after + taps[REACH - shift] * before
    return total


def swap(value, axis, mask):
    return lax.ppermute(value, axis, [(i, i ^ mask) for i in range(lax.axis_size(axis))])


def project_kernel(rows, cols, halve, x_ref, fields_ref, factor_ref, pay_ref, along_ref, diag):
    tiles = fields_ref.shape[0]
    ranks = factor_ref.shape[0] // rows
    lines = cols * rows
    me = lax.axis_index("tile")
    near = tiles // 2

    def slot(t):
        return lax.rem(t, 2) * near + lax.div(t, 2)

    field = jnp.concatenate([fields_ref[t % 2 * near + t // 2] for t in range(tiles)], axis=1)
    step = min(256, ranks * rows)
    row_of = lax.broadcasted_iota(jnp.int32, (rows, lines), 0)
    lane_of = lax.broadcasted_iota(jnp.int32, (rows, lines), 1)
    same = (lax.rem(lane_of, rows) == row_of).astype(jnp.float32)
    if diag.shape[0] > ranks:
        diag[...] = jnp.zeros_like(diag)
    for at in range(0, ranks * rows, step):
        part = lax.dot_general(
            factor_ref[at : at + step, :],
            field,
            (((1,), (1,)), ((), ())),
            preferred_element_type=jnp.float32,
        )
        part = part.reshape(step // rows, rows, lines) * same[None]
        diag[at // rows : (at + step) // rows, :] = jnp.sum(part, axis=1)
    pick = (
        lax.broadcasted_iota(jnp.int32, (cols, lines), 1) // rows
        == lax.broadcasted_iota(jnp.int32, (cols, lines), 0)
    ).astype(jnp.bfloat16)
    for at in range(0, diag.shape[0], LANES):
        part = diag[at : at + LANES, :]
        upper = part.astype(jnp.bfloat16)
        lower = (part - upper.astype(jnp.float32)).astype(jnp.bfloat16)
        dims = (((1,), (1,)), ((), ()))
        proj = lax.dot_general(pick, upper, dims, preferred_element_type=jnp.float32)
        proj = proj + lax.dot_general(pick, lower, dims, preferred_element_type=jnp.float32)
        first = at // LANES * 2 * cols
        upper = proj.astype(jnp.bfloat16)
        pay_ref[first : first + cols, :] = upper
        lower = proj - upper.astype(jnp.float32)
        pay_ref[first + cols : first + 2 * cols, :] = lower.astype(jnp.bfloat16)

    head = diag.shape[0] // LANES * 2 * cols
    low = fields_ref[slot(jnp.maximum(me - 1, 0))].astype(jnp.float32)
    low = jnp.where(me > 0, low, 0.0)
    high = fields_ref[slot(jnp.minimum(me + 1, tiles - 1))].astype(jnp.float32)
    high = jnp.where(me < tiles - 1, high, 0.0)
    own = 0.5 * x_ref[...] if halve else x_ref[...]
    along = stencil(low, own, high, COL_TAPS, 1)
    along_ref[...] = along
    pay_ref[head:, :] = along.astype(jnp.bfloat16)


def term_kernel(rows, cols, groups, tiles, ncells, scale_ref, factor_ref, *refs):
    pay_refs, (mine_ref, other_ref, coef) = refs[:groups], refs[groups:]
    ranks = factor_ref.shape[0] // rows
    lines = cols * rows
    span = LANES // rows

    spread = (
        lax.broadcasted_iota(jnp.int32, (LANES, LANES), 1) // rows
        == lax.broadcasted_iota(jnp.int32, (LANES, LANES), 0)
    ).astype(jnp.bfloat16)
    same = (
        lax.rem(lax.broadcasted_iota(jnp.int32, (lines, LANES), 1), rows)
        == lax.rem(lax.broadcasted_iota(jnp.int32, (lines, LANES), 0), rows)
    ).astype(jnp.float32)
    for at in range(0, ranks, LANES):
        count = min(LANES, ranks - at)
        first = at // LANES * 2 * cols
        both = pay_refs[0][first : first + 2 * cols, :].astype(jnp.float32)
        for ref in pay_refs[1:]:
            both = both + ref[first : first + 2 * cols, :].astype(jnp.float32)
        proj = both[:cols] + both[cols:]
        scale = scale_ref[:, at : at + count]
        weights = scale * scale / ncells
        if count < LANES:
            weights = jnp.concatenate([weights, jnp.zeros((1, LANES - count), jnp.float32)], axis=1)
        c = proj * weights
        turned = [c if n == 0 else pltpu.roll(c, LANES - n * span, 1) for n in range(rows)]
        stacked = jnp.concatenate(turned, axis=0).astype(jnp.bfloat16)
        wide = jnp.dot(stacked, spread, preferred_element_type=jnp.float32)
        for n in range(rows):
            start = (at + n * span) * rows
            if start >= ranks * rows:
                break
            piece = wide[n * cols : (n + 1) * cols, :]
            piece = jnp.broadcast_to(piece[:, None, :], (cols, rows, LANES)).reshape(lines, LANES)
            coef[:, start : start + LANES] = (piece * same).astype(jnp.bfloat16)
    odd = lax.rem(lax.axis_index("tile"), 2) == 1
    for n in range(tiles // 2):
        term = jnp.dot(
            coef[...],
            factor_ref[:, 2 * n * LANES : 2 * (n + 1) * LANES],
            preferred_element_type=jnp.float32,
        )
        even_part, odd_part = term[:, :LANES], term[:, LANES:]
        mine_ref[n] = jnp.where(odd, odd_part, even_part)
        other_ref[n] = jnp.where(odd, even_part, odd_part).astype(jnp.bfloat16)


def pair_kernel(mine_ref, got_ref, *send_refs):
    me = lax.div(lax.axis_index("tile"), 2)
    for mask, ref in enumerate(send_refs):
        at = me ^ mask
        ref[...] = (mine_ref[at] + got_ref[at].astype(jnp.float32)).astype(ref.dtype)


def update_kernel(rows, cols, groups, near, first, b_ref, x_ref, amp_ref, along_ref, *refs):
    pay_refs, refs = refs[: groups - 1], refs[groups - 1 :]
    term_refs, (new_ref, res_ref, short_ref) = refs[:near], refs[near:]
    lines = cols * rows
    head = pay_refs[0].shape[0] - lines
    me = lax.axis_index("grp")
    low = jnp.zeros((lines, LANES), jnp.float32)
    high = low
    for mask, ref in enumerate(pay_refs, 1):
        part = ref[head:, :].astype(jnp.float32)
        low = jnp.where((me ^ mask) == me - 1, part, low)
        high = jnp.where((me ^ mask) == me + 1, part, high)
    low = low.reshape(cols, rows, LANES)
    high = high.reshape(cols, rows, LANES)
    own = along_ref[...].reshape(cols, rows, LANES)
    conv = stencil(low, own, high, ROW_TAPS, 1)
    rank_sum = term_refs[0][...]
    for ref in term_refs[1:]:
        rank_sum = rank_sum + ref[...].astype(jnp.float32)
    x = 0.5 * x_ref[...] if first else x_ref[...]
    scaled = (amp_ref[...][None] * conv).reshape(lines, LANES)
    residual = b_ref[...] - (x + scaled + rank_sum)
    new = x + 0.5 * residual
    new_ref[...] = new
    res_ref[...] = residual
    short_ref[...] = new.astype(jnp.bfloat16)


def on_device(right_side, amplitude, factor, scale):
    cols, rows, width = right_side.shape
    ranks = factor.shape[0]
    tiles = lax.axis_size("tile")
    groups = lax.axis_size("grp")
    near = tiles // 2
    lines = cols * rows
    ncells_all = rows * width * groups * tiles
    blocks = -(-ranks // LANES)
    flat = factor.reshape(ranks * rows, tiles * width)
    b = right_side.reshape(lines, width)
    scale = scale.reshape(1, ranks)
    x = b
    short = (0.5 * b).astype(jnp.bfloat16)
    pay_rows = blocks * 2 * cols + lines
    vmem = pltpu.CompilerParams(vmem_limit_bytes=32 * 1024 * 1024)

    def shape(dtype, *dims):
        return jax.ShapeDtypeStruct(dims, dtype)

    f32, bf16 = jnp.float32, jnp.bfloat16
    along_z = [[2 * z + core for z in range(near)] for core in range(2)]
    cores = [[2 * z, 2 * z + 1] for z in range(near)]
    for step in range(ITERS):
        fields = lax.all_gather(short, "tile", axis=0, axis_index_groups=along_z)
        fields = lax.all_gather(fields, "tile", axis=0, axis_index_groups=cores, tiled=True)
        pay, along = pl.pallas_call(
            partial(project_kernel, rows, cols, step == 0),
            out_shape=(shape(bf16, pay_rows, width), shape(f32, lines, width)),
            scratch_shapes=[pltpu.VMEM((blocks * LANES, lines), f32)],
            compiler_params=vmem,
            name="project",
        )(x, fields, flat)
        pays = [swap(pay, "grp", mask) for mask in range(1, groups)]
        mine, other = pl.pallas_call(
            partial(term_kernel, rows, cols, groups, tiles, ncells_all),
            out_shape=(shape(f32, near, lines, width), shape(bf16, near, lines, width)),
            scratch_shapes=[pltpu.VMEM((lines, ranks * rows), bf16)],
            compiler_params=vmem,
            name="term",
        )(scale, flat, pay, *pays)
        got = swap(other, "tile", 1)
        kept, *sends = pl.pallas_call(
            pair_kernel,
            out_shape=[shape(f32 if n == 0 else bf16, lines, width) for n in range(near)],
            compiler_params=vmem,
            name="pair",
        )(mine, got)
        terms = [swap(part, "tile", 2 * mask) for mask, part in enumerate(sends, 1)]
        x, residual, short = pl.pallas_call(
            partial(update_kernel, rows, cols, groups, near, step == 0),
            out_shape=(shape(f32, lines, width), shape(f32, lines, width), shape(bf16, lines, width)),
            compiler_params=vmem,
            name="update",
        )(b, x, amplitude, along, *pays, kept, *terms)
    return x.reshape(cols, rows, width), residual.reshape(cols, rows, width)


def solution(mesh):
    in_specs = (P(None, "grp", "tile"), P("grp", "tile"), P("tile", "grp", None), P("tile"))
    out_specs = (P(None, "grp", "tile"), P(None, "grp", "tile"))
    return jax.shard_map(
        on_device, mesh=mesh, in_specs=in_specs, out_specs=out_specs, check_vma=False
    )
```

profile of v0, /device:TPU:0, one launch (start us, length us, event | category | flops | bytes accessed | tf_op | source)
XLA Modules:
  0.0 76.6 jit_solution(10614021233516951427)
XLA Ops:
  0.6 0.0 copy-start.5
  0.6 0.9 %fusion = bf16[1,128,128]{2,1,0:T(8,128)(2,1)S(1)} fusion(f32[16,8,128]{2,1,0:T(8,128)} %param.4), kind=kLoop, calls=%fused_computation.1 | loop fusion | flops 32768 | bytes 98304 | tf_op jit(solution)/shard_map/convert_element_type | solution.py:193
  1.5 15.0 %all_gather.16 = bf16[4,128,128]{2,1,0:T(8,128)(2,1)S(1)} all-gather(bf16[1,128,128]{2,1,0:T(8,128)(2,1)S(1)} %fusion), channel_id=1, replica_groups={{0,2,4,6},{1,3,5,7},{8,10,12,14},{9,11,13,15},{16,18,20,22},{17,19,21,2..., dimensions={0}, use_global_device_ids=true | all-gather | bytes 163840 | tf_op jit(solution)/shard_map/all_gather | solution.py:204
  16.5 2.0 %all_gather.17.fields_ref = bf16[8,128,128]{2,1,0:T(8,128)(2,1)S(1)} all-gather(bf16[4,128,128]{2,1,0:T(8,128)(2,1)S(1)} %all_gather.16), channel_id=1, replica_groups={{0,1},{2,3},{4,5},{6,7},{8,9},{10,11},{12,13},{14,15},{16,17},{18,19},{..., dimensions={0}, use_global_device_ids=true | all-gather | bytes 393216 | tf_op jit(solution)/shard_map/all_gather | solution.py:205
  18.5 0.0 copy-start
  18.5 2.2 %copy-done = bf16[256,8,1024]{2,1,0:T(8,128)(2,1)S(1)} copy-done((bf16[256,8,1024]{2,1,0:T(8,128)(2,1)S(1)}, bf16[256,8,1024]{2,1,0:T(8,128)(2,1)}, u32[]{:S(2)}) %copy-start) | copy-done | bytes 4194328
  20.7 0.0 copy-start.2
  20.7 0.8 %copy-done.2 = f32[16,8,128]{2,1,0:T(8,128)S(1)} copy-done((f32[16,8,128]{2,1,0:T(8,128)S(1)}, f32[16,8,128]{2,1,0:T(8,128)}, u32[]{:S(2)}) %copy-start.2) | copy-done | bytes 65560
  21.6 0.0 copy-start.1
  21.6 0.0 copy-start.3
  21.6 0.0 copy-start.4
  21.6 1.4 %project.2 = (bf16[192,128]{1,0:T(8,128)(2,1)S(1)}, f32[128,128]{1,0:T(8,128)S(1)}) custom-call(f32[128,128]{1,0:T(8,128)S(1)} %bitcast.12, bf16[8,128,128]{2,1,0:T(8,128)(2,1)S(1)} %all_gather.17.fields_ref, bf16[2048,1024]{1,0:T(8,128)(2,1)S(1)} %bitcast.8), custom_call_target="tpu_custom_call" | custom-call | tf_op jit(solution)/shard_map/project/pallas_call | solution.py:206
  23.0 2.5 %collective-permute-start.2 = (bf16[192,128]{1,0:T(8,128)(2,1)S(1)}, bf16[192,128]{1,0:T(8,128)(2,1)S(1)}, u32[]{:S(2)}, u32[]{:S(2)}) collective-permute-start(bf16[192,128]{1,0:T(8,128)(2,1)S(1)} %get-tuple-element.23.refs_0_), channel_id=1, source_target_pairs={{0,24},{8,16},{16,8},{24,0},{1,25},{9,17},{17,9},{25,1},{2,26},{10... | collective-permute-start | bytes 147464 | tf_op jit(solution)/shard_map/ppermute | solution.py:40
  25.5 0.5 collective-permute-start.1
  26.0 0.5 collective-permute-start
  26.5 1.5 %collective-permute-done.2.refs_3_.refs_2_ = bf16[192,128]{1,0:T(8,128)(2,1)S(1)} collective-permute-done((bf16[192,128]{1,0:T(8,128)(2,1)S(1)}, bf16[192,128]{1,0:T(8,128)(2,1)S(1)}, u32[]{:S(2)}, u32[]{:S(2)}) %collective-permute-start.2) | collective-permute-done | bytes 49184 | tf_op jit(solution)/shard_map/ppermute | solution.py:40
  28.0 1.5 %collective-permute-done.1.refs_2_.refs_1_ = bf16[192,128]{1,0:T(8,128)(2,1)S(1)} collective-permute-done((bf16[192,128]{1,0:T(8,128)(2,1)S(1)}, bf16[192,128]{1,0:T(8,128)(2,1)S(1)}, u32[]{:S(2)}, u32[]{:S(2)}) %collective-permute-start.1) | collective-permute-done | bytes 49184 | tf_op jit(solution)/shard_map/ppermute | solution.py:40
  29.6 0.5 collective-permute-done.refs_1_.refs_0_
  30.1 0.0 copy-done.5
  30.1 0.0 copy-done.1
  30.1 1.0 %term.2 = (f32[4,128,128]{2,1,0:T(8,128)S(1)}, bf16[4,128,128]{2,1,0:T(8,128)(2,1)S(1)}) custom-call(f32[1,256]{1,0:T(1,128)S(1)} %bitcast.16, bf16[2048,1024]{1,0:T(8,128)(2,1)S(1)} %bitcast.9, bf16[192,128]{1,0:T(8,128)(2,1)S(1)} %get-tuple-element.23.refs_0_, bf16[192,128]{1,0:T(8,128)(2,1)S(1)} %collective-permute-done.refs_1_.refs_0_, ...), custom_call_target="tpu_custom_call" | custom-call | tf_op jit(solution)/shard_map/term/pallas_call | solution.py:214
  31.1 0.1 collective-permute-start.3
  31.2 1.3 %collective-permute-done.3.got_ref = bf16[4,128,128]{2,1,0:T(8,128)(2,1)S(1)} collective-permute-done((bf16[4,128,128]{2,1,0:T(8,128)(2,1)S(1)}, bf16[4,128,128]{2,1,0:T(8,128)(2,1)S(1)}, u32[]{:S(2)}, u32[]{:S(2)}) %collective-permute-start.3) | collective-permute-done | bytes 131104 | tf_op jit(solution)/shard_map/ppermute | solution.py:40
  32.6 1.9 %collective-permute-start.4 = (bf16[128,128]{1,0:T(8,128)(2,1)S(1)}, bf16[128,128]{1,0:T(8,128)(2,1)S(1)}, u32[]{:S(2)}, u32[]{:S(2)}) collective-permute-start(bf16[128,128]{1,0:T(8,128)(2,1)S(1)} %get-tuple-element.27), channel_id=1, source_target_pairs={{0,2},{1,3},{2,0},{3,1},{4,6},{5,7},{6,4},{7,5},{8,10},{9,11},{10,... | collective-permute-start | bytes 98312 | tf_op jit(solution)/shard_map/ppermute | solution.py:40
  34.5 2.4 %collective-permute-start.5 = (bf16[128,128]{1,0:T(8,128)(2,1)S(1)}, bf16[128,128]{1,0:T(8,128)(2,1)S(1)}, u32[]{:S(2)}, u32[]{:S(2)}) collective-permute-start(bf16[128,128]{1,0:T(8,128)(2,1)S(1)} %get-tuple-element.28), channel_id=1, source_target_pairs={{0,4},{1,5},{2,6},{3,7},{4,0},{5,1},{6,2},{7,3},{8,12},{9,13},{10,... | collective-permute-start | bytes 98312 | tf_op jit(solution)/shard_map/ppermute | solution.py:40
  36.9 0.1 collective-permute-start.6
  37.0 0.0 collective-permute-done.4.refs_4_
  37.0 2.6 %collective-permute-done.5.refs_5_ = bf16[128,128]{1,0:T(8,128)(2,1)S(1)} collective-permute-done((bf16[128,128]{1,0:T(8,128)(2,1)S(1)}, bf16[128,128]{1,0:T(8,128)(2,1)S(1)}, u32[]{:S(2)}, u32[]{:S(2)}) %collective-permute-start.5) | collective-permute-done | bytes 32800 | tf_op jit(solution)/shard_map/ppermute | solution.py:40
  39.6 3.0 %collective-permute-done.6.refs_6_ = bf16[128,128]{1,0:T(8,128)(2,1)S(1)} collective-permute-done((bf16[128,128]{1,0:T(8,128)(2,1)S(1)}, bf16[128,128]{1,0:T(8,128)(2,1)S(1)}, u32[]{:S(2)}, u32[]{:S(2)}) %collective-permute-start.6) | collective-permute-done | bytes 32800 | tf_op jit(solution)/shard_map/ppermute | solution.py:40
  42.6 0.0 copy-done.3
  42.6 0.0 copy-done.4
  42.6 0.8 %update.2 = (f32[128,128]{1,0:T(8,128)S(1)}, f32[128,128]{1,0:T(8,128)}, bf16[128,128]{1,0:T(8,128)(2,1)S(1)}) custom-call(f32[128,128]{1,0:T(8,128)S(1)} %bitcast.13, f32[128,128]{1,0:T(8,128)S(1)} %bitcast.14, f32[8,128]{1,0:T(8,128)S(1)} %copy-done.4, f32[128,128]{1,0:T(8,128)S(1)} %get-tuple-element.22.along_ref, ...), custom_call_target="tpu_custom_call" | custom-call | tf_op jit(solution)/shard_map/update/pallas_call | solution.py:229
  43.5 13.4 %all-gather = bf16[512,128]{1,0:T(8,128)(2,1)S(1)} all-gather(bf16[128,128]{1,0:T(8,128)(2,1)S(1)} %get-tuple-element.31), channel_id=2, replica_groups={{0,2,4,6},{1,3,5,7},{8,10,12,14},{9,11,13,15},{16,18,20,22},{17,19,21,2..., dimensions={0}, use_global_device_ids=true | all-gather | bytes 163840 | tf_op jit(solution)/shard_map/all_gather | solution.py:204
  56.9 2.0 %all_gather.20.fields_ref = bf16[8,128,128]{2,1,0:T(8,128)(2,1)S(1)} all-gather(bf16[4,128,128]{2,1,0:T(8,128)(2,1)S(1)} %bitcast.18), channel_id=1, replica_groups={{0,1},{2,3},{4,5},{6,7},{8,9},{10,11},{12,13},{14,15},{16,17},{18,19},{..., dimensions={0}, use_global_device_ids=true | all-gather | bytes 393216 | tf_op jit(solution)/shard_map/all_gather | solution.py:205
  58.8 1.5 %project.3 = (bf16[192,128]{1,0:T(8,128)(2,1)S(1)}, f32[128,128]{1,0:T(8,128)S(1)}) custom-call(f32[128,128]{1,0:T(8,128)S(1)} %get-tuple-element.30.x_ref, bf16[8,128,128]{2,1,0:T(8,128)(2,1)S(1)} %all_gather.20.fields_ref, bf16[2048,1024]{1,0:T(8,128)(2,1)S(1)} %bitcast.10), custom_call_target="tpu_custom_call" | custom-call | tf_op jit(solution)/shard_map/project/pallas_call | solution.py:206
  60.3 1.5 %collective-permute-start.9 = (bf16[192,128]{1,0:T(8,128)(2,1)S(1)}, bf16[192,128]{1,0:T(8,128)(2,1)S(1)}, u32[]{:S(2)}, u32[]{:S(2)}) collective-permute-start(bf16[192,128]{1,0:T(8,128)(2,1)S(1)} %get-tuple-element.33.refs_0_), channel_id=1, source_target_pairs={{0,24},{8,16},{16,8},{24,0},{1,25},{9,17},{17,9},{25,1},{2,26},{10... | collective-permute-start | bytes 147464 | tf_op jit(solution)/shard_map/ppermute | solution.py:40
  61.8 0.5 collective-permute-start.8
  62.3 1.5 %collective-permute-start.7 = (bf16[192,128]{1,0:T(8,128)(2,1)S(1)}, bf16[192,128]{1,0:T(8,128)(2,1)S(1)}, u32[]{:S(2)}, u32[]{:S(2)}) collective-permute-start(bf16[192,128]{1,0:T(8,128)(2,1)S(1)} %get-tuple-element.33.refs_0_), channel_id=1, source_target_pairs={{0,8},{8,0},{16,24},{24,16},{1,9},{9,1},{17,25},{25,17},{2,10},{10... | collective-permute-start | bytes 147464 | tf_op jit(solution)/shard_map/ppermute | solution.py:40
  63.8 1.6 %collective-permute-done.9.refs_3_.refs_2_ = bf16[192,128]{1,0:T(8,128)(2,1)S(1)} collective-permute-done((bf16[192,128]{1,0:T(8,128)(2,1)S(1)}, bf16[192,128]{1,0:T(8,128)(2,1)S(1)}, u32[]{:S(2)}, u32[]{:S(2)}) %collective-permute-start.9) | collective-permute-done | bytes 49184 | tf_op jit(solution)/shard_map/ppermute | solution.py:40
  65.4 0.7 collective-permute-done.8.refs_2_.refs_1_
  66.1 0.3 collective-permute-done.7.refs_1_.refs_0_
  66.4 1.0 %term.3 = (f32[4,128,128]{2,1,0:T(8,128)S(1)}, bf16[4,128,128]{2,1,0:T(8,128)(2,1)S(1)}) custom-call(f32[1,256]{1,0:T(1,128)S(1)} %bitcast.17, bf16[2048,1024]{1,0:T(8,128)(2,1)S(1)} %bitcast.11, bf16[192,128]{1,0:T(8,128)(2,1)S(1)} %get-tuple-element.33.refs_0_, bf16[192,128]{1,0:T(8,128)(2,1)S(1)} %collective-permute-done.7.refs_1_.refs_0_, ...), custom_call_target="tpu_custom_call" | custom-call | tf_op jit(solution)/shard_map/term/pallas_call | solution.py:214
  67.5 0.1 collective-permute-start.10
  67.5 1.3 %collective-permute-done.10.got_ref = bf16[4,128,128]{2,1,0:T(8,128)(2,1)S(1)} collective-permute-done((bf16[4,128,128]{2,1,0:T(8,128)(2,1)S(1)}, bf16[4,128,128]{2,1,0:T(8,128)(2,1)S(1)}, u32[]{:S(2)}, u32[]{:S(2)}) %collective-permute-start.10) | collective-permute-done | bytes 131104 | tf_op jit(solution)/shard_map/ppermute | solution.py:40
  68.9 0.1 collective-permute-start.11
  69.0 1.0 %collective-permute-start.12 = (bf16[128,128]{1,0:T(8,128)(2,1)S(1)}, bf16[128,128]{1,0:T(8,128)(2,1)S(1)}, u32[]{:S(2)}, u32[]{:S(2)}) collective-permute-start(bf16[128,128]{1,0:T(8,128)(2,1)S(1)} %get-tuple-element.38), channel_id=1, source_target_pairs={{0,4},{1,5},{2,6},{3,7},{4,0},{5,1},{6,2},{7,3},{8,12},{9,13},{10,... | collective-permute-start | bytes 98312 | tf_op jit(solution)/shard_map/ppermute | solution.py:40
  70.0 3.4 %collective-permute-start.13 = (bf16[128,128]{1,0:T(8,128)(2,1)S(1)}, bf16[128,128]{1,0:T(8,128)(2,1)S(1)}, u32[]{:S(2)}, u32[]{:S(2)}) collective-permute-start(bf16[128,128]{1,0:T(8,128)(2,1)S(1)} %get-tuple-element.39), channel_id=1, source_target_pairs={{0,6},{1,7},{2,4},{3,5},{4,2},{5,3},{6,0},{7,1},{8,14},{9,15},{10,... | collective-permute-start | bytes 98312 | tf_op jit(solution)/shard_map/ppermute | solution.py:40
  73.4 0.0 collective-permute-done.11.refs_4_
  73.4 1.3 %collective-permute-done.12.refs_5_ = bf16[128,128]{1,0:T(8,128)(2,1)S(1)} collective-permute-done((bf16[128,128]{1,0:T(8,128)(2,1)S(1)}, bf16[128,128]{1,0:T(8,128)(2,1)S(1)}, u32[]{:S(2)}, u32[]{:S(2)}) %collective-permute-start.12) | collective-permute-done | bytes 32800 | tf_op jit(solution)/shard_map/ppermute | solution.py:40
  74.6 1.1 %collective-permute-done.13.refs_6_ = bf16[128,128]{1,0:T(8,128)(2,1)S(1)} collective-permute-done((bf16[128,128]{1,0:T(8,128)(2,1)S(1)}, bf16[128,128]{1,0:T(8,128)(2,1)S(1)}, u32[]{:S(2)}, u32[]{:S(2)}) %collective-permute-start.13) | collective-permute-done | bytes 32800 | tf_op jit(solution)/shard_map/ppermute | solution.py:40
  75.7 0.9 %update.3 = (f32[128,128]{1,0:T(8,128)}, f32[128,128]{1,0:T(8,128)}, bf16[128,128]{1,0:T(8,128)(2,1)}) custom-call(f32[128,128]{1,0:T(8,128)S(1)} %bitcast.15, f32[128,128]{1,0:T(8,128)S(1)} %get-tuple-element.30.x_ref, f32[8,128]{1,0:T(8,128)S(1)} %copy-done.4, f32[128,128]{1,0:T(8,128)S(1)} %get-tuple-element.32.along_ref, ...), custom_call_target="tpu_custom_call" | custom-call | tf_op jit(solution)/shard_map/update/pallas_call | solution.py:229
  (2 shorter events, 0.1 us)
Async XLA Ops:
  0.6 29.4 %copy-start.5 = (f32[256]{0:T(256)S(1)}, f32[256]{0:T(256)}, u32[]{:S(2)}) copy-start(f32[256]{0:T(256)} %param.7) | copy-start | bytes 3076
  18.5 2.2 %copy-start = (bf16[256,8,1024]{2,1,0:T(8,128)(2,1)S(1)}, bf16[256,8,1024]{2,1,0:T(8,128)(2,1)}, u32[]{:S(2)}) copy-start(bf16[256,8,1024]{2,1,0:T(8,128)(2,1)} %param.6) | copy-start | bytes 12582916
  20.7 0.8 %copy-start.2 = (f32[16,8,128]{2,1,0:T(8,128)S(1)}, f32[16,8,128]{2,1,0:T(8,128)}, u32[]{:S(2)}) copy-start(f32[16,8,128]{2,1,0:T(8,128)} %param.4) | copy-start | bytes 196612
  21.6 8.5 %copy-start.1 = (bf16[256,8,1024]{2,1,0:T(8,128)(2,1)S(1)}, bf16[256,8,1024]{2,1,0:T(8,128)(2,1)}, u32[]{:S(2)}) copy-start(bf16[256,8,1024]{2,1,0:T(8,128)(2,1)} %param.6) | copy-start | bytes 12582916
  21.6 21.1 %copy-start.3 = (f32[16,8,128]{2,1,0:T(8,128)S(1)}, f32[16,8,128]{2,1,0:T(8,128)}, u32[]{:S(2)}) copy-start(f32[16,8,128]{2,1,0:T(8,128)} %param.4) | copy-start | bytes 196612
  21.6 21.1 %copy-start.4 = (f32[8,128]{1,0:T(8,128)S(1)}, f32[8,128]{1,0:T(8,128)}, u32[]{:S(2)}) copy-start(f32[8,128]{1,0:T(8,128)} %amp_ref.3) | copy-start | bytes 12292
  23.0 5.0 %collective-permute-start.2 = (bf16[192,128]{1,0:T(8,128)(2,1)S(1)}, bf16[192,128]{1,0:T(8,128)(2,1)S(1)}, u32[]{:S(2)}, u32[]{:S(2)}) collective-permute-start(bf16[192,128]{1,0:T(8,128)(2,1)S(1)} %get-tuple-element.23.refs_0_), channel_id=1, source_target_pairs={{0,24},{8,16},{16,8},{24,0},{1,25},{9,17},{17,9},{25,1},{2,26},{10... | collective-permute-start | bytes 147464 | tf_op jit(solution)/shard_map/ppermute | solution.py:40
  25.5 4.1 %collective-permute-start.1 = (bf16[192,128]{1,0:T(8,128)(2,1)S(1)}, bf16[192,128]{1,0:T(8,128)(2,1)S(1)}, u32[]{:S(2)}, u32[]{:S(2)}) collective-permute-start(bf16[192,128]{1,0:T(8,128)(2,1)S(1)} %get-tuple-element.23.refs_0_), channel_id=1, source_target_pairs={{0,16},{8,24},{16,0},{24,8},{1,17},{9,25},{17,1},{25,9},{2,18},{10... | collective-permute-start | bytes 147464 | tf_op jit(solution)/shard_map/ppermute | solution.py:40
  26.0 4.1 %collective-permute-start = (bf16[192,128]{1,0:T(8,128)(2,1)S(1)}, bf16[192,128]{1,0:T(8,128)(2,1)S(1)}, u32[]{:S(2)}, u32[]{:S(2)}) collective-permute-start(bf16[192,128]{1,0:T(8,128)(2,1)S(1)} %get-tuple-element.23.refs_0_), channel_id=1, source_target_pairs={{0,8},{8,0},{16,24},{24,16},{1,9},{9,1},{17,25},{25,17},{2,10},{10... | collective-permute-start | bytes 147464 | tf_op jit(solution)/shard_map/ppermute | solution.py:40
  31.1 1.4 %collective-permute-start.3 = (bf16[4,128,128]{2,1,0:T(8,128)(2,1)S(1)}, bf16[4,128,128]{2,1,0:T(8,128)(2,1)S(1)}, u32[]{:S(2)}, u32[]{:S(2)}) collective-permute-start(bf16[4,128,128]{2,1,0:T(8,128)(2,1)S(1)} %get-tuple-element.25), channel_id=1, source_target_pairs={{0,1},{1,0},{2,3},{3,2},{4,5},{5,4},{6,7},{7,6},{8,9},{9,8},{10,11... | collective-permute-start | bytes 393224 | tf_op jit(solution)/shard_map/ppermute | solution.py:40
  32.6 4.5 %collective-permute-start.4 = (bf16[128,128]{1,0:T(8,128)(2,1)S(1)}, bf16[128,128]{1,0:T(8,128)(2,1)S(1)}, u32[]{:S(2)}, u32[]{:S(2)}) collective-permute-start(bf16[128,128]{1,0:T(8,128)(2,1)S(1)} %get-tuple-element.27), channel_id=1, source_target_pairs={{0,2},{1,3},{2,0},{3,1},{4,6},{5,7},{6,4},{7,5},{8,10},{9,11},{10,... | collective-permute-start | bytes 98312 | tf_op jit(solution)/shard_map/ppermute | solution.py:40
  34.5 5.1 %collective-permute-start.5 = (bf16[128,128]{1,0:T(8,128)(2,1)S(1)}, bf16[128,128]{1,0:T(8,128)(2,1)S(1)}, u32[]{:S(2)}, u32[]{:S(2)}) collective-permute-start(bf16[128,128]{1,0:T(8,128)(2,1)S(1)} %get-tuple-element.28), channel_id=1, source_target_pairs={{0,4},{1,5},{2,6},{3,7},{4,0},{5,1},{6,2},{7,3},{8,12},{9,13},{10,... | collective-permute-start | bytes 98312 | tf_op jit(solution)/shard_map/ppermute | solution.py:40
  36.9 5.7 %collective-permute-start.6 = (bf16[128,128]{1,0:T(8,128)(2,1)S(1)}, bf16[128,128]{1,0:T(8,128)(2,1)S(1)}, u32[]{:S(2)}, u32[]{:S(2)}) collective-permute-start(bf16[128,128]{1,0:T(8,128)(2,1)S(1)} %get-tuple-element.29), channel_id=1, source_target_pairs={{0,6},{1,7},{2,4},{3,5},{4,2},{5,3},{6,0},{7,1},{8,14},{9,15},{10,... | collective-permute-start | bytes 98312 | tf_op jit(solution)/shard_map/ppermute | solution.py:40
  60.3 5.1 %collective-permute-start.9 = (bf16[192,128]{1,0:T(8,128)(2,1)S(1)}, bf16[192,128]{1,0:T(8,128)(2,1)S(1)}, u32[]{:S(2)}, u32[]{:S(2)}) collective-permute-start(bf16[192,128]{1,0:T(8,128)(2,1)S(1)} %get-tuple-element.33.refs_0_), channel_id=1, source_target_pairs={{0,24},{8,16},{16,8},{24,0},{1,25},{9,17},{17,9},{25,1},{2,26},{10... | collective-permute-start | bytes 147464 | tf_op jit(solution)/shard_map/ppermute | solution.py:40
  61.8 4.3 %collective-permute-start.8 = (bf16[192,128]{1,0:T(8,128)(2,1)S(1)}, bf16[192,128]{1,0:T(8,128)(2,1)S(1)}, u32[]{:S(2)}, u32[]{:S(2)}) collective-permute-start(bf16[192,128]{1,0:T(8,128)(2,1)S(1)} %get-tuple-element.33.refs_0_), channel_id=1, source_target_pairs={{0,16},{8,24},{16,0},{24,8},{1,17},{9,25},{17,1},{25,9},{2,18},{10... | collective-permute-start | bytes 147464 | tf_op jit(solution)/shard_map/ppermute | solution.py:40
  62.3 4.1 %collective-permute-start.7 = (bf16[192,128]{1,0:T(8,128)(2,1)S(1)}, bf16[192,128]{1,0:T(8,128)(2,1)S(1)}, u32[]{:S(2)}, u32[]{:S(2)}) collective-permute-start(bf16[192,128]{1,0:T(8,128)(2,1)S(1)} %get-tuple-element.33.refs_0_), channel_id=1, source_target_pairs={{0,8},{8,0},{16,24},{24,16},{1,9},{9,1},{17,25},{25,17},{2,10},{10... | collective-permute-start | bytes 147464 | tf_op jit(solution)/shard_map/ppermute | solution.py:40
  67.5 1.4 %collective-permute-start.10 = (bf16[4,128,128]{2,1,0:T(8,128)(2,1)S(1)}, bf16[4,128,128]{2,1,0:T(8,128)(2,1)S(1)}, u32[]{:S(2)}, u32[]{:S(2)}) collective-permute-start(bf16[4,128,128]{2,1,0:T(8,128)(2,1)S(1)} %get-tuple-element.35), channel_id=1, source_target_pairs={{0,1},{1,0},{2,3},{3,2},{4,5},{5,4},{6,7},{7,6},{8,9},{9,8},{10,11... | collective-permute-start | bytes 393224 | tf_op jit(solution)/shard_map/ppermute | solution.py:40
  68.9 4.5 %collective-permute-start.11 = (bf16[128,128]{1,0:T(8,128)(2,1)S(1)}, bf16[128,128]{1,0:T(8,128)(2,1)S(1)}, u32[]{:S(2)}, u32[]{:S(2)}) collective-permute-start(bf16[128,128]{1,0:T(8,128)(2,1)S(1)} %get-tuple-element.37), channel_id=1, source_target_pairs={{0,2},{1,3},{2,0},{3,1},{4,6},{5,7},{6,4},{7,5},{8,10},{9,11},{10,... | collective-permute-start | bytes 98312 | tf_op jit(solution)/shard_map/ppermute | solution.py:40
  69.0 5.6 %collective-permute-start.12 = (bf16[128,128]{1,0:T(8,128)(2,1)S(1)}, bf16[128,128]{1,0:T(8,128)(2,1)S(1)}, u32[]{:S(2)}, u32[]{:S(2)}) collective-permute-start(bf16[128,128]{1,0:T(8,128)(2,1)S(1)} %get-tuple-element.38), channel_id=1, source_target_pairs={{0,4},{1,5},{2,6},{3,7},{4,0},{5,1},{6,2},{7,3},{8,12},{9,13},{10,... | collective-permute-start | bytes 98312 | tf_op jit(solution)/shard_map/ppermute | solution.py:40
  70.0 5.7 %collective-permute-start.13 = (bf16[128,128]{1,0:T(8,128)(2,1)S(1)}, bf16[128,128]{1,0:T(8,128)(2,1)S(1)}, u32[]{:S(2)}, u32[]{:S(2)}) collective-permute-start(bf16[128,128]{1,0:T(8,128)(2,1)S(1)} %get-tuple-element.39), channel_id=1, source_target_pairs={{0,6},{1,7},{2,4},{3,5},{4,2},{5,3},{6,0},{7,1},{8,14},{9,15},{10,... | collective-permute-start | bytes 98312 | tf_op jit(solution)/shard_map/ppermute | solution.py:40
where the time goes:
time: 76.8 us; the launch traced here: 76.6 us
  blocking collectives  32.4 us (42%)
  waiting for transfers between devices  16.7 us (22%)
  starting transfers between devices  16.1 us (21%)
  Pallas kernels  6.75 us (9%)
  local copies, waits for them, and re-layouts  3.04 us (4%)
  other arithmetic  0.85 us (1%)
    all_gather x2, blocking collectives, on_device(): fields = lax.all_gather(short, 'tile', axis=0, axis_index_groups=along_z)  28.4 us
    ppermute x14, waiting for transfers between devices, swap(): lax.ppermute(value, axis, [(i, i ^ mask) for i in range(lax.axis_size(axi...  16.7 us
    ppermute x14, starting transfers between devices, swap(): lax.ppermute(value, axis, [(i, i ^ mask) for i in range(lax.axis_size(axi...  16.1 us
    all_gather x2, blocking collectives, on_device(): lax.all_gather(fields, 'tile', axis=0, axis_index_groups=cores, tiled=True)  3.96 us
    unnamed x12, local copies, waits for them, and re-layouts  3.04 us
    pallas_call x2, Pallas kernels, on_device(): pl.pallas_call(partial(project_kernel, rows, cols, step == 0), out_shape=...  2.92 us
    pallas_call x2, Pallas kernels, on_device(): pl.pallas_call(partial(term_kernel, rows, cols, groups, tiles, ncells_all...  2.08 us
    pallas_call x2, Pallas kernels, on_device(): pl.pallas_call(partial(update_kernel, rows, cols, groups, near, step == 0...  1.69 us
  transfers between devices with their start and end apart: 14, of which 12 were waited for; matrix products, arithmetic and copies ran while one was open for 0% of the time, Pallas kernels for 0%

commit v1 on v0

v1 whole, which is shorter than its diff:
```python
import math
from functools import partial

import jax
import jax.numpy as jnp
import numpy as np
from jax import lax
from jax.experimental import pallas as pl
from jax.experimental.pallas import tpu as pltpu
from jax.sharding import PartitionSpec as P

REACH = 8
ITERS = 2
LANES = 128


def taper(sigma):
    offsets = np.arange(-REACH, REACH + 1).astype(np.float64)
    values = np.exp(-offsets * offsets / (2.0 * sigma * sigma))
    values = values * np.cos(np.pi * offsets / (2.0 * REACH + 2.0)) ** 2
    return [float(v) for v in (values / values.sum()).astype(np.float32)]


ROW_TAPS = taper(3.0)
COL_TAPS = taper(5.0)


def stencil(low, own, high, taps, axis):
    size = own.shape[axis]
    place = lax.broadcasted_iota(jnp.int32, own.shape, axis)
    total = taps[REACH] * own
    for shift in range(1, REACH + 1):
        after = pltpu.roll(jnp.where(place < shift, high, own), size - shift, axis)
        before = pltpu.roll(jnp.where(place >= size - shift, low, own), shift, axis)
        total = total + taps[REACH + shift] * after + taps[REACH - shift] * before
    return total


def swap(value, axis, mask):
    return lax.ppermute(value, axis, [(i, i ^ mask) for i in range(lax.axis_size(axis))])


def gather_kernel(*refs):
    part_refs, out_ref = refs[1:-1], refs[-1]
    me = lax.div(lax.axis_index("tile"), 2)
    for mask, ref in enumerate(part_refs):
        out_ref[me ^ mask] = ref[...]


def load_kernel(source_ref, out_ref, sems):
    chunks = sems.shape[0]
    count = source_ref.shape[0] // chunks
    copies = [
        pltpu.make_async_copy(
            source_ref.at[pl.ds(n * count, count)], out_ref.at[pl.ds(n * count, count)], sems.at[n]
        )
        for n in range(chunks)
    ]
    for copy in copies:
        copy.start()
    for copy in copies:
        copy.wait()


def diagonal(rows, parity, fields_ref, factor_ref, store):
    near, lines, _ = fields_ref.shape
    count = factor_ref.shape[0]
    field = jnp.concatenate([fields_ref[z] for z in range(near)], axis=1)
    step = min(256, count)
    row_of = lax.broadcasted_iota(jnp.int32, (rows, lines), 0)
    lane_of = lax.broadcasted_iota(jnp.int32, (rows, lines), 1)
    same = (lax.rem(lane_of, rows) == row_of).astype(jnp.float32)
    starts = [pl.multiple_of((2 * z + parity) * LANES, LANES) for z in range(near)]
    for at in range(0, count, step):
        left = jnp.concatenate(
            [factor_ref[at : at + step, pl.ds(start, LANES)] for start in starts], axis=1
        )
        part = lax.dot_general(
            left, field, (((1,), (1,)), ((), ())), preferred_element_type=jnp.float32
        )
        part = part.reshape(step // rows, rows, lines) * same[None]
        store(at // rows, (at + step) // rows, jnp.sum(part, axis=1))


def first_kernel(rows, fields_ref, factor_ref, diag_ref):
    parity = lax.rem(lax.axis_index("tile"), 2)
    ranks = factor_ref.shape[0] // rows
    if diag_ref.shape[0] > ranks:
        diag_ref[...] = jnp.zeros_like(diag_ref)

    def store(start, end, value):
        diag_ref[start:end, :] = value

    diagonal(rows, parity, fields_ref, factor_ref, store)


def second_kernel(
    rows, cols, halve, x_ref, fields_ref, factor_ref, diag_ref, pay_ref, along_ref, total
):
    near = fields_ref.shape[0]
    lines = cols * rows
    me = lax.axis_index("tile")
    parity = lax.rem(me, 2)
    if total.shape[0] > factor_ref.shape[0] // rows:
        total[...] = jnp.zeros_like(total)

    def store(start, end, value):
        total[start:end, :] = diag_ref[start:end, :] + value

    diagonal(rows, 1 - parity, fields_ref, factor_ref, store)
    pick = (
        lax.broadcasted_iota(jnp.int32, (cols, lines), 1) // rows
        == lax.broadcasted_iota(jnp.int32, (cols, lines), 0)
    ).astype(jnp.bfloat16)
    for at in range(0, total.shape[0], LANES):
        part = total[at : at + LANES, :]
        upper = part.astype(jnp.bfloat16)
        lower = (part - upper.astype(jnp.float32)).astype(jnp.bfloat16)
        dims = (((1,), (1,)), ((), ()))
        proj = lax.dot_general(pick, upper, dims, preferred_element_type=jnp.float32)
        proj = proj + lax.dot_general(pick, lower, dims, preferred_element_type=jnp.float32)
        first = at // LANES * 2 * cols
        upper = proj.astype(jnp.bfloat16)
        pay_ref[first : first + cols, :] = upper
        lower = proj - upper.astype(jnp.float32)
        pay_ref[first + cols : first + 2 * cols, :] = lower.astype(jnp.bfloat16)

    head = total.shape[0] // LANES * 2 * cols
    left, right = lax.div(me + 1, 2) - 1, lax.div(me + 1, 2)
    low = fields_ref[jnp.maximum(left, 0)].astype(jnp.float32)
    low = jnp.where(left >= 0, low, 0.0)
    high = fields_ref[jnp.minimum(right, near - 1)].astype(jnp.float32)
    high = jnp.where(right < near, high, 0.0)
    own = 0.5 * x_ref[...] if halve else x_ref[...]
    along = stencil(low, own, high, COL_TAPS, 1)
    along_ref[...] = along
    pay_ref[head:, :] = along.astype(jnp.bfloat16)


def product(parity, coef, factor_ref, out_ref):
    near = out_ref.shape[0]
    pair = 2 if near % 2 == 0 else 1
    for z in range(0, near, pair):
        starts = [pl.multiple_of((2 * (z + n) + parity) * LANES, LANES) for n in range(pair)]
        right = jnp.concatenate([factor_ref[:, pl.ds(start, LANES)] for start in starts], axis=1)
        term = jnp.dot(coef, right, preferred_element_type=jnp.float32)
        for n in range(pair):
            out_ref[z + n] = term[:, n * LANES : (n + 1) * LANES].astype(out_ref.dtype)


def far_kernel(rows, cols, groups, ncells, scale_ref, factor_ref, *refs):
    pay_refs, (coef_ref, out_ref) = refs[:groups], refs[groups:]
    ranks = factor_ref.shape[0] // rows
    lines = cols * rows
    span = LANES // rows

    spread = (
        lax.broadcasted_iota(jnp.int32, (LANES, LANES), 1) // rows
        == lax.broadcasted_iota(jnp.int32, (LANES, LANES), 0)
    ).astype(jnp.bfloat16)
    same = (
        lax.rem(lax.broadcasted_iota(jnp.int32, (lines, LANES), 1), rows)
        == lax.rem(lax.broadcasted_iota(jnp.int32, (lines, LANES), 0), rows)
    ).astype(jnp.float32)
    for at in range(0, ranks, LANES):
        count = min(LANES, ranks - at)
        first = at // LANES * 2 * cols
        both = pay_refs[0][first : first + 2 * cols, :].astype(jnp.float32)
        for ref in pay_refs[1:]:
            both = both + ref[first : first + 2 * cols, :].astype(jnp.float32)
        proj = both[:cols] + both[cols:]
        scale = scale_ref[:, at : at + count]
        weights = scale * scale / ncells
        if count < LANES:
            weights = jnp.concatenate([weights, jnp.zeros((1, LANES - count), jnp.float32)], axis=1)
        c = proj * weights
        turned = [c if n == 0 else pltpu.roll(c, LANES - n * span, 1) for n in range(rows)]
        stacked = jnp.concatenate(turned, axis=0).astype(jnp.bfloat16)
        wide = jnp.dot(stacked, spread, preferred_element_type=jnp.float32)
        for n in range(rows):
            start = (at + n * span) * rows
            if start >= ranks * rows:
                break
            piece = wide[n * cols : (n + 1) * cols, :]
            piece = jnp.broadcast_to(piece[:, None, :], (cols, rows, LANES)).reshape(lines, LANES)
            coef_ref[:, start : start + LANES] = (piece * same).astype(jnp.bfloat16)
    parity = 1 - lax.rem(lax.axis_index("tile"), 2)
    product(parity, coef_ref[...], factor_ref, out_ref)


def near_kernel(coef_ref, factor_ref, out_ref):
    product(lax.rem(lax.axis_index("tile"), 2), coef_ref[...], factor_ref, out_ref)


def pair_kernel(mine_ref, got_ref, *send_refs):
    me = lax.div(lax.axis_index("tile"), 2)
    for mask, ref in enumerate(send_refs):
        at = me ^ mask
        ref[...] = (mine_ref[at] + got_ref[at].astype(jnp.float32)).astype(ref.dtype)


def local_kernel(rows, cols, halve, b_ref, x_ref, amp_ref, along_ref, *refs):
    pay_refs, base_ref = refs[:-1], refs[-1]
    lines = cols * rows
    head = pay_refs[0].shape[0] - lines
    me = lax.axis_index("grp")
    low = jnp.zeros((lines, LANES), jnp.float32)
    high = low
    for mask, ref in enumerate(pay_refs, 1):
        part = ref[head:, :].astype(jnp.float32)
        low = jnp.where((me ^ mask) == me - 1, part, low)
        high = jnp.where((me ^ mask) == me + 1, part, high)
    low = low.reshape(cols, rows, LANES)
    high = high.reshape(cols, rows, LANES)
    own = along_ref[...].reshape(cols, rows, LANES)
    conv = stencil(low, own, high, ROW_TAPS, 1)
    x = 0.5 * x_ref[...] if halve else x_ref[...]
    scaled = (amp_ref[...][None] * conv).reshape(lines, LANES)
    base_ref[...] = b_ref[...] - (x + scaled)


def update_kernel(near, halve, x_ref, base_ref, *refs):
    term_refs, out_refs = refs[:near], refs[near:]
    rank_sum = term_refs[0][...]
    for ref in term_refs[1:]:
        rank_sum = rank_sum + ref[...].astype(jnp.float32)
    x = 0.5 * x_ref[...] if halve else x_ref[...]
    residual = base_ref[...] - rank_sum
    new = x + 0.5 * residual
    out_refs[0][...] = new
    if len(out_refs) > 1:
        out_refs[1][...] = residual if out_refs[1].dtype == jnp.float32 else new.astype(jnp.bfloat16)


def on_device(right_side, amplitude, factor, scale):
    cols, rows, width = right_side.shape
    ranks = factor.shape[0]
    tiles = lax.axis_size("tile")
    groups = lax.axis_size("grp")
    near = tiles // 2
    lines = cols * rows
    ncells_all = rows * width * groups * tiles
    blocks = -(-ranks // LANES)
    flat = factor.reshape(ranks * rows, tiles * width)
    b = right_side.reshape(lines, width)
    scale = scale.reshape(1, ranks)
    x = b
    short = (0.5 * b).astype(jnp.bfloat16)
    pay_rows = blocks * 2 * cols + lines

    f32, bf16 = jnp.float32, jnp.bfloat16

    def shape(dtype, *dims):
        return jax.ShapeDtypeStruct(dims, dtype)

    def call(kernel, out_shape, flops=0, moved=1 << 18, **options):
        return pl.pallas_call(
            kernel,
            out_shape=out_shape,
            compiler_params=pltpu.CompilerParams(vmem_limit_bytes=32 * 1024 * 1024),
            cost_estimate=pl.CostEstimate(flops=flops, bytes_accessed=moved, transcendentals=0),
            **options,
        )

    work = lines * ranks * rows * tiles * width
    held = call(
        load_kernel,
        shape(bf16, *flat.shape),
        moved=4 * flat.size,
        in_specs=[pl.BlockSpec(memory_space=pltpu.HBM)],
        out_specs=pl.BlockSpec(memory_space=pltpu.VMEM),
        scratch_shapes=[pltpu.SemaphoreType.DMA((8,))],
        name="load",
    )(flat)
    for step in range(ITERS):
        halve = step == 0
        parts = [swap(short, "tile", 2 * mask) for mask in range(1, near)]
        whole = [pl.BlockSpec(memory_space=pl.ANY)] + [pl.BlockSpec(memory_space=pltpu.VMEM)] * near
        own = call(
            gather_kernel, shape(bf16, near, lines, width), in_specs=whole, name="order"
        )(held, short, *parts)
        across = swap(own, "tile", 1)
        diag = call(
            partial(first_kernel, rows),
            shape(f32, blocks * LANES, lines),
            flops=work,
            moved=flat.size,
            name="project_own",
        )(own, held)
        pay, along = call(
            partial(second_kernel, rows, cols, halve),
            (shape(bf16, pay_rows, width), shape(f32, lines, width)),
            flops=work,
            moved=flat.size,
            scratch_shapes=[pltpu.VMEM((blocks * LANES, lines), f32)],
            name="project_across",
        )(x, across, held, diag)
        pays = [swap(pay, "grp", mask) for mask in range(1, groups)]
        coef, far = call(
            partial(far_kernel, rows, cols, groups, ncells_all),
            (shape(bf16, lines, ranks * rows), shape(bf16, near, lines, width)),
            flops=work,
            moved=flat.size,
            name="term_across",
        )(scale, held, pay, *pays)
        got = swap(far, "tile", 1)
        mine = call(
            near_kernel,
            shape(f32, near, lines, width),
            flops=work,
            moved=flat.size,
            name="term_own",
        )(coef, held)
        kept, *sends = call(
            pair_kernel,
            [shape(f32 if n == 0 else bf16, lines, width) for n in range(near)],
            name="pair",
        )(mine, got)
        terms = [swap(part, "tile", 2 * mask) for mask, part in enumerate(sends, 1)]
        base = call(
            partial(local_kernel, rows, cols, halve), shape(f32, lines, width), name="local"
        )(b, x, amplitude, along, *pays)
        last = step == ITERS - 1
        x, residual = call(
            partial(update_kernel, near, halve),
            (shape(f32, lines, width), shape(f32 if last else bf16, lines, width)),
            name="update",
        )(x, base, kept, *terms)
        short = residual
    return x.reshape(cols, rows, width), residual.reshape(cols, rows, width)


def solution(mesh):
    in_specs = (P(None, "grp", "tile"), P("grp", "tile"), P("tile", "grp", None), P("tile"))
    out_specs = (P(None, "grp", "tile"), P(None, "grp", "tile"))
    return jax.shard_map(
        on_device, mesh=mesh, in_specs=in_specs, out_specs=out_specs, check_vma=False
    )
```

time: 76.8 us -> 59.3 us (0.77)
  blocking collectives: 32.4 us -> 0 us
  starting transfers between devices: 16.1 us -> 26.3 us
  Pallas kernels: 6.75 us -> 9.56 us
  waiting for transfers between devices: 16.7 us -> 19.3 us
  local copies, waits for them, and re-layouts: 3.04 us -> 2.2 us
    all_gather x4 -> x0, blocking collectives: 32.4 us -> none  [the longest x2 28.4 us: on_device(): fields = lax.all_gather(short, 'tile', axis=0, axis_index_groups=along_z)]
    ppermute x14 -> x22, starting transfers between devices: 16.1 us -> 26.3 us  [swap(): lax.ppermute(value, axis, [(i, i ^ mask) for i in range(lax.axis_size(axi...]
    pallas_call x8 -> x17, Pallas kernels: 6.75 us -> 9.56 us  [the longest x2 2.46 us: on_device(): call(partial(second_kernel, rows, cols, halve), (shape(bf16, pay_rows, wi...]
    ppermute x14 -> x22, waiting for transfers between devices: 16.7 us -> 19.3 us  [swap(): lax.ppermute(value, axis, [(i, i ^ mask) for i in range(lax.axis_size(axi...]
    unnamed x12 -> x8, local copies, waits for them, and re-layouts: 3.04 us -> 2.2 us
  transfers between devices with their start and end apart: 14 -> 22, of which waited for: 12 -> 18; matrix products, arithmetic and copies ran while one was open for 0% -> 0% of each run, Pallas kernels for 0% -> 7%
where the time goes in v1:
time: 59.3 us; the launch traced here: 59.1 us
  starting transfers between devices  26.3 us (44%)
  waiting for transfers between devices  19.3 us (33%)
  Pallas kernels  9.56 us (16%)
  local copies, waits for them, and re-layouts  2.2 us (4%)
  other arithmetic  0.85 us (1%)
  between operations  0.8 us (1%)
    ppermute x22, starting transfers between devices, swap(): lax.ppermute(value, axis, [(i, i ^ mask) for i in range(lax.axis_size(axi...  26.3 us
    ppermute x22, waiting for transfers between devices, swap(): lax.ppermute(value, axis, [(i, i ^ mask) for i in range(lax.axis_size(axi...  19.3 us
    pallas_call x2, Pallas kernels, on_device(): call(partial(second_kernel, rows, cols, halve), (shape(bf16, pay_rows, wi...  2.46 us
    unnamed x8, local copies, waits for them, and re-layouts  2.2 us
    pallas_call x2, Pallas kernels, on_device(): call(partial(far_kernel, rows, cols, groups, ncells_all), (shape(bf16, li...  2.01 us
    pallas_call x2, Pallas kernels, on_device(): call(partial(first_kernel, rows), shape(f32, blocks * LANES, lines), flop...  1.95 us
    pallas_call x2, Pallas kernels, on_device(): call(near_kernel, shape(f32, near, lines, width), flops=work, moved=flat....  1.6 us
  transfers between devices with their start and end apart: 22, of which 18 were waited for; matrix products, arithmetic and copies ran while one was open for 0% of the time, Pallas kernels for 7%

profile of v1, /device:TPU:0, one launch (start us, length us, event | category | flops | bytes accessed | tf_op | source)
XLA Modules:
  0.0 59.1 jit_solution(3253066989024122897)
XLA Ops:
  0.6 0.8 %multiply_convert_fusion.refs_1_ = bf16[128,128]{1,0:T(8,128)(2,1)S(1)} fusion(f32[16,8,128]{2,1,0:T(8,128)} %param.4), kind=kLoop, calls=%fused_computation | loop fusion | flops 32768 | bytes 98304 | tf_op jit(solution)/shard_map/convert_element_type | solution.py:248
  1.5 5.0 %collective-permute-start.2 = (bf16[128,128]{1,0:T(8,128)(2,1)S(1)}, bf16[128,128]{1,0:T(8,128)(2,1)S(1)}, u32[]{:S(2)}, u32[]{:S(2)}) collective-permute-start(bf16[128,128]{1,0:T(8,128)(2,1)S(1)} %multiply_convert_fusion.refs_1_), channel_id=1, source_target_pairs={{0,6},{1,7},{2,4},{3,5},{4,2},{5,3},{6,0},{7,1},{8,14},{9,15},{10,... | collective-permute-start | bytes 98312 | tf_op jit(solution)/shard_map/ppermute | solution.py:40
  6.5 0.0 collective-permute-start.1
  6.5 0.6 %collective-permute-start = (bf16[128,128]{1,0:T(8,128)(2,1)S(1)}, bf16[128,128]{1,0:T(8,128)(2,1)S(1)}, u32[]{:S(2)}, u32[]{:S(2)}) collective-permute-start(bf16[128,128]{1,0:T(8,128)(2,1)S(1)} %multiply_convert_fusion.refs_1_), channel_id=1, source_target_pairs={{0,2},{1,3},{2,0},{3,1},{4,6},{5,7},{6,4},{7,5},{8,10},{9,11},{10,... | collective-permute-start | bytes 98312 | tf_op jit(solution)/shard_map/ppermute | solution.py:40
  7.2 0.0 copy-start
  7.2 2.2 %copy-done = bf16[256,8,1024]{2,1,0:T(8,128)(2,1)S(1)} copy-done((bf16[256,8,1024]{2,1,0:T(8,128)(2,1)S(1)}, bf16[256,8,1024]{2,1,0:T(8,128)(2,1)}, u32[]{:S(2)}) %copy-start) | copy-done | bytes 4194328
  9.3 0.4 load.1.refs_0_.factor_ref
  9.7 0.0 copy-start.1
  9.7 0.0 collective-permute-done.2.refs_4_
  9.7 1.6 %collective-permute-done.1.refs_3_ = bf16[128,128]{1,0:T(8,128)(2,1)S(1)} collective-permute-done((bf16[128,128]{1,0:T(8,128)(2,1)S(1)}, bf16[128,128]{1,0:T(8,128)(2,1)S(1)}, u32[]{:S(2)}, u32[]{:S(2)}) %collective-permute-start.1) | collective-permute-done | bytes 32800 | tf_op jit(solution)/shard_map/ppermute | solution.py:40
  11.3 0.0 collective-permute-done.refs_2_
  11.4 0.0 copy-start.3
  11.4 0.1 collective-permute-start.3
  11.5 1.0 %project_own.2.diag_ref = f32[256,128]{1,0:T(8,128)S(1)} custom-call(bf16[4,128,128]{2,1,0:T(8,128)(2,1)S(1)} %order.2.fields_ref, bf16[2048,1024]{1,0:T(8,128)(2,1)S(1)} %load.1.refs_0_.factor_ref), custom_call_target="tpu_custom_call" | custom-call | flops 268435456 | bytes 2097152 | tf_op jit(solution)/shard_map/project_own/pallas_call | solution.py:283
  12.4 0.4 collective-permute-done.3.fields_ref
  12.8 0.0 copy-done.1
  12.8 1.2 %project_across.2 = (bf16[192,128]{1,0:T(8,128)(2,1)S(1)}, f32[128,128]{1,0:T(8,128)S(1)}) custom-call(f32[128,128]{1,0:T(8,128)S(1)} %bitcast.7, bf16[4,128,128]{2,1,0:T(8,128)(2,1)S(1)} %collective-permute-done.3.fields_ref, bf16[2048,1024]{1,0:T(8,128)(2,1)S(1)} %load.1.refs_0_.factor_ref, f32[256,128]{1,0:T(8,128)S(1)} %project_own.2.diag_ref), custom_call_target="tpu_custom_call" | custom-call | flops 268435456 | bytes 2097152 | tf_op jit(solution)/shard_map/project_across/pallas_call | solution.py:290
  14.0 2.5 %collective-permute-start.6 = (bf16[192,128]{1,0:T(8,128)(2,1)S(1)}, bf16[192,128]{1,0:T(8,128)(2,1)S(1)}, u32[]{:S(2)}, u32[]{:S(2)}) collective-permute-start(bf16[192,128]{1,0:T(8,128)(2,1)S(1)} %get-tuple-element.23.refs_0_), channel_id=1, source_target_pairs={{0,24},{8,16},{16,8},{24,0},{1,25},{9,17},{17,9},{25,1},{2,26},{10... | collective-permute-start | bytes 147464 | tf_op jit(solution)/shard_map/ppermute | solution.py:40
  16.5 0.5 collective-permute-start.5
  17.0 0.5 collective-permute-start.4
  17.5 1.5 %collective-permute-done.6.refs_2_.refs_3_ = bf16[192,128]{1,0:T(8,128)(2,1)S(1)} collective-permute-done((bf16[192,128]{1,0:T(8,128)(2,1)S(1)}, bf16[192,128]{1,0:T(8,128)(2,1)S(1)}, u32[]{:S(2)}, u32[]{:S(2)}) %collective-permute-start.6) | collective-permute-done | bytes 49184 | tf_op jit(solution)/shard_map/ppermute | solution.py:40
  19.0 1.5 %collective-permute-done.5.refs_1_.refs_2_ = bf16[192,128]{1,0:T(8,128)(2,1)S(1)} collective-permute-done((bf16[192,128]{1,0:T(8,128)(2,1)S(1)}, bf16[192,128]{1,0:T(8,128)(2,1)S(1)}, u32[]{:S(2)}, u32[]{:S(2)}) %collective-permute-start.5) | collective-permute-done | bytes 49184 | tf_op jit(solution)/shard_map/ppermute | solution.py:40
  20.6 0.5 collective-permute-done.4.refs_0_.refs_1_
  21.1 0.0 copy-done.3
  21.1 1.0 %term_across.2 = (bf16[128,2048]{1,0:T(8,128)(2,1)S(1)}, bf16[4,128,128]{2,1,0:T(8,128)(2,1)S(1)}) custom-call(f32[1,256]{1,0:T(1,128)S(1)} %bitcast.12, bf16[2048,1024]{1,0:T(8,128)(2,1)S(1)} %load.1.refs_0_.factor_ref, bf16[192,128]{1,0:T(8,128)(2,1)S(1)} %get-tuple-element.23.refs_0_, bf16[192,128]{1,0:T(8,128)(2,1)S(1)} %collective-permute-done.4.refs_0_.refs_1_, ...), custom_call_target="tpu_custom_call" | custom-call | flops 268435456 | bytes 2097152 | tf_op jit(solution)/shard_map/term_across/pallas_call | solution.py:299
  22.1 0.1 collective-permute-start.7
  22.2 0.8 %term_own.2.mine_ref = f32[4,128,128]{2,1,0:T(8,128)S(1)} custom-call(bf16[128,2048]{1,0:T(8,128)(2,1)S(1)} %get-tuple-element.24.coef_ref, bf16[2048,1024]{1,0:T(8,128)(2,1)S(1)} %load.1.refs_0_.factor_ref), custom_call_target="tpu_custom_call" | custom-call | flops 268435456 | bytes 2097152 | tf_op jit(solution)/shard_map/term_own/pallas_call | solution.py:307
  23.0 0.5 collective-permute-done.7.got_ref
  23.6 0.1 collective-permute-start.8
  23.6 2.7 %collective-permute-start.9 = (bf16[128,128]{1,0:T(8,128)(2,1)S(1)}, bf16[128,128]{1,0:T(8,128)(2,1)S(1)}, u32[]{:S(2)}, u32[]{:S(2)}) collective-permute-start(bf16[128,128]{1,0:T(8,128)(2,1)S(1)} %get-tuple-element.28), channel_id=1, source_target_pairs={{0,4},{1,5},{2,6},{3,7},{4,0},{5,1},{6,2},{7,3},{8,12},{9,13},{10,... | collective-permute-start | bytes 98312 | tf_op jit(solution)/shard_map/ppermute | solution.py:40
  26.4 1.6 %collective-permute-start.10 = (bf16[128,128]{1,0:T(8,128)(2,1)S(1)}, bf16[128,128]{1,0:T(8,128)(2,1)S(1)}, u32[]{:S(2)}, u32[]{:S(2)}) collective-permute-start(bf16[128,128]{1,0:T(8,128)(2,1)S(1)} %get-tuple-element.29), channel_id=1, source_target_pairs={{0,6},{1,7},{2,4},{3,5},{4,2},{5,3},{6,0},{7,1},{8,14},{9,15},{10,... | collective-permute-start | bytes 98312 | tf_op jit(solution)/shard_map/ppermute | solution.py:40
  28.0 0.0 copy-done.2
  28.0 0.2 local.2.base_ref
  28.2 0.0 collective-permute-done.8.refs_1_
  28.2 0.3 collective-permute-done.9.refs_2_
  28.5 3.5 %collective-permute-done.10.refs_3_ = bf16[128,128]{1,0:T(8,128)(2,1)S(1)} collective-permute-done((bf16[128,128]{1,0:T(8,128)(2,1)S(1)}, bf16[128,128]{1,0:T(8,128)(2,1)S(1)}, u32[]{:S(2)}, u32[]{:S(2)}) %collective-permute-start.10) | collective-permute-done | bytes 32800 | tf_op jit(solution)/shard_map/ppermute | solution.py:40
  32.1 1.7 %collective-permute-start.13 = (bf16[128,128]{1,0:T(8,128)(2,1)S(1)}, bf16[128,128]{1,0:T(8,128)(2,1)S(1)}, u32[]{:S(2)}, u32[]{:S(2)}) collective-permute-start(bf16[128,128]{1,0:T(8,128)(2,1)S(1)} %get-tuple-element.31.refs_1_), channel_id=1, source_target_pairs={{0,6},{1,7},{2,4},{3,5},{4,2},{5,3},{6,0},{7,1},{8,14},{9,15},{10,... | collective-permute-start | bytes 98312 | tf_op jit(solution)/shard_map/ppermute | solution.py:40
  33.8 0.0 collective-permute-start.12
  33.8 2.7 %collective-permute-start.11 = (bf16[128,128]{1,0:T(8,128)(2,1)S(1)}, bf16[128,128]{1,0:T(8,128)(2,1)S(1)}, u32[]{:S(2)}, u32[]{:S(2)}) collective-permute-start(bf16[128,128]{1,0:T(8,128)(2,1)S(1)} %get-tuple-element.31.refs_1_), channel_id=1, source_target_pairs={{0,2},{1,3},{2,0},{3,1},{4,6},{5,7},{6,4},{7,5},{8,10},{9,11},{10,... | collective-permute-start | bytes 98312 | tf_op jit(solution)/shard_map/ppermute | solution.py:40
  36.6 1.3 %collective-permute-done.13.refs_4_ = bf16[128,128]{1,0:T(8,128)(2,1)S(1)} collective-permute-done((bf16[128,128]{1,0:T(8,128)(2,1)S(1)}, bf16[128,128]{1,0:T(8,128)(2,1)S(1)}, u32[]{:S(2)}, u32[]{:S(2)}) %collective-permute-start.13) | collective-permute-done | bytes 32800 | tf_op jit(solution)/shard_map/ppermute | solution.py:40
  37.9 0.9 %collective-permute-done.12.refs_3_ = bf16[128,128]{1,0:T(8,128)(2,1)S(1)} collective-permute-done((bf16[128,128]{1,0:T(8,128)(2,1)S(1)}, bf16[128,128]{1,0:T(8,128)(2,1)S(1)}, u32[]{:S(2)}, u32[]{:S(2)}) %collective-permute-start.12) | collective-permute-done | bytes 32800 | tf_op jit(solution)/shard_map/ppermute | solution.py:40
  38.8 0.1 collective-permute-done.11.refs_2_
  38.8 0.1 collective-permute-start.14
  38.9 1.0 %project_own.3.diag_ref = f32[256,128]{1,0:T(8,128)S(1)} custom-call(bf16[4,128,128]{2,1,0:T(8,128)(2,1)S(1)} %order.3.fields_ref, bf16[2048,1024]{1,0:T(8,128)(2,1)S(1)} %load.1.refs_0_.factor_ref), custom_call_target="tpu_custom_call" | custom-call | flops 268435456 | bytes 2097152 | tf_op jit(solution)/shard_map/project_own/pallas_call | solution.py:283
  39.9 0.4 collective-permute-done.14.fields_ref
  40.2 1.2 %project_across.3 = (bf16[192,128]{1,0:T(8,128)(2,1)S(1)}, f32[128,128]{1,0:T(8,128)S(1)}) custom-call(f32[128,128]{1,0:T(8,128)S(1)} %get-tuple-element.30.x_ref, bf16[4,128,128]{2,1,0:T(8,128)(2,1)S(1)} %collective-permute-done.14.fields_ref, bf16[2048,1024]{1,0:T(8,128)(2,1)S(1)} %load.1.refs_0_.factor_ref, f32[256,128]{1,0:T(8,128)S(1)} %project_own.3.diag_ref), custom_call_target="tpu_custom_call" | custom-call | flops 268435456 | bytes 2097152 | tf_op jit(solution)/shard_map/project_across/pallas_call | solution.py:290
  41.5 1.5 %collective-permute-start.17 = (bf16[192,128]{1,0:T(8,128)(2,1)S(1)}, bf16[192,128]{1,0:T(8,128)(2,1)S(1)}, u32[]{:S(2)}, u32[]{:S(2)}) collective-permute-start(bf16[192,128]{1,0:T(8,128)(2,1)S(1)} %get-tuple-element.33.refs_0_), channel_id=1, source_target_pairs={{0,24},{8,16},{16,8},{24,0},{1,25},{9,17},{17,9},{25,1},{2,26},{10... | collective-permute-start | bytes 147464 | tf_op jit(solution)/shard_map/ppermute | solution.py:40
  43.0 0.5 collective-permute-start.16
  43.5 1.5 %collective-permute-start.15 = (bf16[192,128]{1,0:T(8,128)(2,1)S(1)}, bf16[192,128]{1,0:T(8,128)(2,1)S(1)}, u32[]{:S(2)}, u32[]{:S(2)}) collective-permute-start(bf16[192,128]{1,0:T(8,128)(2,1)S(1)} %get-tuple-element.33.refs_0_), channel_id=1, source_target_pairs={{0,8},{8,0},{16,24},{24,16},{1,9},{9,1},{17,25},{25,17},{2,10},{10... | collective-permute-start | bytes 147464 | tf_op jit(solution)/shard_map/ppermute | solution.py:40
  45.0 1.6 %collective-permute-done.17.refs_2_.refs_3_ = bf16[192,128]{1,0:T(8,128)(2,1)S(1)} collective-permute-done((bf16[192,128]{1,0:T(8,128)(2,1)S(1)}, bf16[192,128]{1,0:T(8,128)(2,1)S(1)}, u32[]{:S(2)}, u32[]{:S(2)}) %collective-permute-start.17) | collective-permute-done | bytes 49184 | tf_op jit(solution)/shard_map/ppermute | solution.py:40
  46.5 0.7 %collective-permute-done.16.refs_1_.refs_2_ = bf16[192,128]{1,0:T(8,128)(2,1)S(1)} collective-permute-done((bf16[192,128]{1,0:T(8,128)(2,1)S(1)}, bf16[192,128]{1,0:T(8,128)(2,1)S(1)}, u32[]{:S(2)}, u32[]{:S(2)}) %collective-permute-start.16) | collective-permute-done | bytes 49184 | tf_op jit(solution)/shard_map/ppermute | solution.py:40
  47.2 0.3 collective-permute-done.15.refs_0_.refs_1_
  47.6 1.0 %term_across.3 = (bf16[128,2048]{1,0:T(8,128)(2,1)S(1)}, bf16[4,128,128]{2,1,0:T(8,128)(2,1)S(1)}) custom-call(f32[1,256]{1,0:T(1,128)S(1)} %bitcast.13, bf16[2048,1024]{1,0:T(8,128)(2,1)S(1)} %load.1.refs_0_.factor_ref, bf16[192,128]{1,0:T(8,128)(2,1)S(1)} %get-tuple-element.33.refs_0_, bf16[192,128]{1,0:T(8,128)(2,1)S(1)} %collective-permute-done.15.refs_0_.refs_1_, ...), custom_call_target="tpu_custom_call" | custom-call | flops 268435456 | bytes 2097152 | tf_op jit(solution)/shard_map/term_across/pallas_call | solution.py:299
  48.6 0.1 collective-permute-start.18
  48.7 0.8 %term_own.3.mine_ref = f32[4,128,128]{2,1,0:T(8,128)S(1)} custom-call(bf16[128,2048]{1,0:T(8,128)(2,1)S(1)} %get-tuple-element.34.coef_ref, bf16[2048,1024]{1,0:T(8,128)(2,1)S(1)} %load.1.refs_0_.factor_ref), custom_call_target="tpu_custom_call" | custom-call | flops 268435456 | bytes 2097152 | tf_op jit(solution)/shard_map/term_own/pallas_call | solution.py:307
  49.5 0.5 collective-permute-done.18.got_ref
  50.0 1.7 %collective-permute-start.19 = (bf16[128,128]{1,0:T(8,128)(2,1)S(1)}, bf16[128,128]{1,0:T(8,128)(2,1)S(1)}, u32[]{:S(2)}, u32[]{:S(2)}) collective-permute-start(bf16[128,128]{1,0:T(8,128)(2,1)S(1)} %get-tuple-element.37), channel_id=1, source_target_pairs={{0,2},{1,3},{2,0},{3,1},{4,6},{5,7},{6,4},{7,5},{8,10},{9,11},{10,... | collective-permute-start | bytes 98312 | tf_op jit(solution)/shard_map/ppermute | solution.py:40
  51.8 0.9 %collective-permute-start.20 = (bf16[128,128]{1,0:T(8,128)(2,1)S(1)}, bf16[128,128]{1,0:T(8,128)(2,1)S(1)}, u32[]{:S(2)}, u32[]{:S(2)}) collective-permute-start(bf16[128,128]{1,0:T(8,128)(2,1)S(1)} %get-tuple-element.38), channel_id=1, source_target_pairs={{0,4},{1,5},{2,6},{3,7},{4,0},{5,1},{6,2},{7,3},{8,12},{9,13},{10,... | collective-permute-start | bytes 98312 | tf_op jit(solution)/shard_map/ppermute | solution.py:40
  52.7 1.8 %collective-permute-start.21 = (bf16[128,128]{1,0:T(8,128)(2,1)S(1)}, bf16[128,128]{1,0:T(8,128)(2,1)S(1)}, u32[]{:S(2)}, u32[]{:S(2)}) collective-permute-start(bf16[128,128]{1,0:T(8,128)(2,1)S(1)} %get-tuple-element.39), channel_id=1, source_target_pairs={{0,6},{1,7},{2,4},{3,5},{4,2},{5,3},{6,0},{7,1},{8,14},{9,15},{10,... | collective-permute-start | bytes 98312 | tf_op jit(solution)/shard_map/ppermute | solution.py:40
  54.5 0.2 local.3.base_ref
  54.7 0.0 collective-permute-done.19.refs_1_
  54.7 2.5 %collective-permute-done.20.refs_2_ = bf16[128,128]{1,0:T(8,128)(2,1)S(1)} collective-permute-done((bf16[128,128]{1,0:T(8,128)(2,1)S(1)}, bf16[128,128]{1,0:T(8,128)(2,1)S(1)}, u32[]{:S(2)}, u32[]{:S(2)}) %collective-permute-start.20) | collective-permute-done | bytes 32800 | tf_op jit(solution)/shard_map/ppermute | solution.py:40
  57.1 1.3 %collective-permute-done.21.refs_3_ = bf16[128,128]{1,0:T(8,128)(2,1)S(1)} collective-permute-done((bf16[128,128]{1,0:T(8,128)(2,1)S(1)}, bf16[128,128]{1,0:T(8,128)(2,1)S(1)}, u32[]{:S(2)}, u32[]{:S(2)}) %collective-permute-start.21) | collective-permute-done | bytes 32800 | tf_op jit(solution)/shard_map/ppermute | solution.py:40
  58.4 0.7 %update.3 = (f32[128,128]{1,0:T(8,128)}, f32[128,128]{1,0:T(8,128)}) custom-call(f32[128,128]{1,0:T(8,128)S(1)} %get-tuple-element.30.x_ref, f32[128,128]{1,0:T(8,128)S(1)} %local.3.base_ref, f32[128,128]{1,0:T(8,128)S(1)} %get-tuple-element.36.refs_0_, bf16[128,128]{1,0:T(8,128)(2,1)S(1)} %collective-permute-done.19.refs_1_, ...), custom_call_target="tpu_custom_call" | custom-call | bytes 262144 | tf_op jit(solution)/shard_map/update/pallas_call | solution.py:324
  (6 shorter events, 0.1 us)
Async XLA Ops:
  1.5 8.3 %collective-permute-start.2 = (bf16[128,128]{1,0:T(8,128)(2,1)S(1)}, bf16[128,128]{1,0:T(8,128)(2,1)S(1)}, u32[]{:S(2)}, u32[]{:S(2)}) collective-permute-start(bf16[128,128]{1,0:T(8,128)(2,1)S(1)} %multiply_convert_fusion.refs_1_), channel_id=1, source_target_pairs={{0,6},{1,7},{2,4},{3,5},{4,2},{5,3},{6,0},{7,1},{8,14},{9,15},{10,... | collective-permute-start | bytes 98312 | tf_op jit(solution)/shard_map/ppermute | solution.py:40
  6.5 4.8 %collective-permute-start.1 = (bf16[128,128]{1,0:T(8,128)(2,1)S(1)}, bf16[128,128]{1,0:T(8,128)(2,1)S(1)}, u32[]{:S(2)}, u32[]{:S(2)}) collective-permute-start(bf16[128,128]{1,0:T(8,128)(2,1)S(1)} %multiply_convert_fusion.refs_1_), channel_id=1, source_target_pairs={{0,4},{1,5},{2,6},{3,7},{4,0},{5,1},{6,2},{7,3},{8,12},{9,13},{10,... | collective-permute-start | bytes 98312 | tf_op jit(solution)/shard_map/ppermute | solution.py:40
  6.5 4.8 %collective-permute-start = (bf16[128,128]{1,0:T(8,128)(2,1)S(1)}, bf16[128,128]{1,0:T(8,128)(2,1)S(1)}, u32[]{:S(2)}, u32[]{:S(2)}) collective-permute-start(bf16[128,128]{1,0:T(8,128)(2,1)S(1)} %multiply_convert_fusion.refs_1_), channel_id=1, source_target_pairs={{0,2},{1,3},{2,0},{3,1},{4,6},{5,7},{6,4},{7,5},{8,10},{9,11},{10,... | collective-permute-start | bytes 98312 | tf_op jit(solution)/shard_map/ppermute | solution.py:40
  7.2 2.2 %copy-start = (bf16[256,8,1024]{2,1,0:T(8,128)(2,1)S(1)}, bf16[256,8,1024]{2,1,0:T(8,128)(2,1)}, u32[]{:S(2)}) copy-start(bf16[256,8,1024]{2,1,0:T(8,128)(2,1)} %param.6) | copy-start | bytes 12582916
  9.7 3.1 %copy-start.1 = (f32[16,8,128]{2,1,0:T(8,128)S(1)}, f32[16,8,128]{2,1,0:T(8,128)}, u32[]{:S(2)}) copy-start(f32[16,8,128]{2,1,0:T(8,128)} %param.4) | copy-start | bytes 196612
  11.4 9.7 %copy-start.3 = (f32[256]{0:T(256)S(1)}, f32[256]{0:T(256)}, u32[]{:S(2)}) copy-start(f32[256]{0:T(256)} %param.7) | copy-start | bytes 3076
  11.4 1.4 %collective-permute-start.3 = (bf16[4,128,128]{2,1,0:T(8,128)(2,1)S(1)}, bf16[4,128,128]{2,1,0:T(8,128)(2,1)S(1)}, u32[]{:S(2)}, u32[]{:S(2)}) collective-permute-start(bf16[4,128,128]{2,1,0:T(8,128)(2,1)S(1)} %order.2.fields_ref), channel_id=1, source_target_pairs={{0,1},{1,0},{2,3},{3,2},{4,5},{5,4},{6,7},{7,6},{8,9},{9,8},{10,11... | collective-permute-start | bytes 393224 | tf_op jit(solution)/shard_map/ppermute | solution.py:40
  14.0 5.0 %collective-permute-start.6 = (bf16[192,128]{1,0:T(8,128)(2,1)S(1)}, bf16[192,128]{1,0:T(8,128)(2,1)S(1)}, u32[]{:S(2)}, u32[]{:S(2)}) collective-permute-start(bf16[192,128]{1,0:T(8,128)(2,1)S(1)} %get-tuple-element.23.refs_0_), channel_id=1, source_target_pairs={{0,24},{8,16},{16,8},{24,0},{1,25},{9,17},{17,9},{25,1},{2,26},{10... | collective-permute-start | bytes 147464 | tf_op jit(solution)/shard_map/ppermute | solution.py:40
  16.5 4.1 %collective-permute-start.5 = (bf16[192,128]{1,0:T(8,128)(2,1)S(1)}, bf16[192,128]{1,0:T(8,128)(2,1)S(1)}, u32[]{:S(2)}, u32[]{:S(2)}) collective-permute-start(bf16[192,128]{1,0:T(8,128)(2,1)S(1)} %get-tuple-element.23.refs_0_), channel_id=1, source_target_pairs={{0,16},{8,24},{16,0},{24,8},{1,17},{9,25},{17,1},{25,9},{2,18},{10... | collective-permute-start | bytes 147464 | tf_op jit(solution)/shard_map/ppermute | solution.py:40
  17.0 4.1 %collective-permute-start.4 = (bf16[192,128]{1,0:T(8,128)(2,1)S(1)}, bf16[192,128]{1,0:T(8,128)(2,1)S(1)}, u32[]{:S(2)}, u32[]{:S(2)}) collective-permute-start(bf16[192,128]{1,0:T(8,128)(2,1)S(1)} %get-tuple-element.23.refs_0_), channel_id=1, source_target_pairs={{0,8},{8,0},{16,24},{24,16},{1,9},{9,1},{17,25},{25,17},{2,10},{10... | collective-permute-start | bytes 147464 | tf_op jit(solution)/shard_map/ppermute | solution.py:40
  21.1 6.9 %copy-start.2 = (f32[8,128]{1,0:T(8,128)S(1)}, f32[8,128]{1,0:T(8,128)}, u32[]{:S(2)}) copy-start(f32[8,128]{1,0:T(8,128)} %amp_ref.3) | copy-start | bytes 12292
  22.1 1.4 %collective-permute-start.7 = (bf16[4,128,128]{2,1,0:T(8,128)(2,1)S(1)}, bf16[4,128,128]{2,1,0:T(8,128)(2,1)S(1)}, u32[]{:S(2)}, u32[]{:S(2)}) collective-permute-start(bf16[4,128,128]{2,1,0:T(8,128)(2,1)S(1)} %get-tuple-element.25), channel_id=1, source_target_pairs={{0,1},{1,0},{2,3},{3,2},{4,5},{5,4},{6,7},{7,6},{8,9},{9,8},{10,11... | collective-permute-start | bytes 393224 | tf_op jit(solution)/shard_map/ppermute | solution.py:40
  23.6 4.7 %collective-permute-start.8 = (bf16[128,128]{1,0:T(8,128)(2,1)S(1)}, bf16[128,128]{1,0:T(8,128)(2,1)S(1)}, u32[]{:S(2)}, u32[]{:S(2)}) collective-permute-start(bf16[128,128]{1,0:T(8,128)(2,1)S(1)} %get-tuple-element.27), channel_id=1, source_target_pairs={{0,2},{1,3},{2,0},{3,1},{4,6},{5,7},{6,4},{7,5},{8,10},{9,11},{10,... | collective-permute-start | bytes 98312 | tf_op jit(solution)/shard_map/ppermute | solution.py:40
  23.6 4.9 %collective-permute-start.9 = (bf16[128,128]{1,0:T(8,128)(2,1)S(1)}, bf16[128,128]{1,0:T(8,128)(2,1)S(1)}, u32[]{:S(2)}, u32[]{:S(2)}) collective-permute-start(bf16[128,128]{1,0:T(8,128)(2,1)S(1)} %get-tuple-element.28), channel_id=1, source_target_pairs={{0,4},{1,5},{2,6},{3,7},{4,0},{5,1},{6,2},{7,3},{8,12},{9,13},{10,... | collective-permute-start | bytes 98312 | tf_op jit(solution)/shard_map/ppermute | solution.py:40
  26.4 5.7 %collective-permute-start.10 = (bf16[128,128]{1,0:T(8,128)(2,1)S(1)}, bf16[128,128]{1,0:T(8,128)(2,1)S(1)}, u32[]{:S(2)}, u32[]{:S(2)}) collective-permute-start(bf16[128,128]{1,0:T(8,128)(2,1)S(1)} %get-tuple-element.29), channel_id=1, source_target_pairs={{0,6},{1,7},{2,4},{3,5},{4,2},{5,3},{6,0},{7,1},{8,14},{9,15},{10,... | collective-permute-start | bytes 98312 | tf_op jit(solution)/shard_map/ppermute | solution.py:40
  32.1 5.8 %collective-permute-start.13 = (bf16[128,128]{1,0:T(8,128)(2,1)S(1)}, bf16[128,128]{1,0:T(8,128)(2,1)S(1)}, u32[]{:S(2)}, u32[]{:S(2)}) collective-permute-start(bf16[128,128]{1,0:T(8,128)(2,1)S(1)} %get-tuple-element.31.refs_1_), channel_id=1, source_target_pairs={{0,6},{1,7},{2,4},{3,5},{4,2},{5,3},{6,0},{7,1},{8,14},{9,15},{10,... | collective-permute-start | bytes 98312 | tf_op jit(solution)/shard_map/ppermute | solution.py:40
  33.8 4.9 %collective-permute-start.12 = (bf16[128,128]{1,0:T(8,128)(2,1)S(1)}, bf16[128,128]{1,0:T(8,128)(2,1)S(1)}, u32[]{:S(2)}, u32[]{:S(2)}) collective-permute-start(bf16[128,128]{1,0:T(8,128)(2,1)S(1)} %get-tuple-element.31.refs_1_), channel_id=1, source_target_pairs={{0,4},{1,5},{2,6},{3,7},{4,0},{5,1},{6,2},{7,3},{8,12},{9,13},{10,... | collective-permute-start | bytes 98312 | tf_op jit(solution)/shard_map/ppermute | solution.py:40
  33.8 5.0 %collective-permute-start.11 = (bf16[128,128]{1,0:T(8,128)(2,1)S(1)}, bf16[128,128]{1,0:T(8,128)(2,1)S(1)}, u32[]{:S(2)}, u32[]{:S(2)}) collective-permute-start(bf16[128,128]{1,0:T(8,128)(2,1)S(1)} %get-tuple-element.31.refs_1_), channel_id=1, source_target_pairs={{0,2},{1,3},{2,0},{3,1},{4,6},{5,7},{6,4},{7,5},{8,10},{9,11},{10,... | collective-permute-start | bytes 98312 | tf_op jit(solution)/shard_map/ppermute | solution.py:40
  38.8 1.4 %collective-permute-start.14 = (bf16[4,128,128]{2,1,0:T(8,128)(2,1)S(1)}, bf16[4,128,128]{2,1,0:T(8,128)(2,1)S(1)}, u32[]{:S(2)}, u32[]{:S(2)}) collective-permute-start(bf16[4,128,128]{2,1,0:T(8,128)(2,1)S(1)} %order.3.fields_ref), channel_id=1, source_target_pairs={{0,1},{1,0},{2,3},{3,2},{4,5},{5,4},{6,7},{7,6},{8,9},{9,8},{10,11... | collective-permute-start | bytes 393224 | tf_op jit(solution)/shard_map/ppermute | solution.py:40
  41.5 5.1 %collective-permute-start.17 = (bf16[192,128]{1,0:T(8,128)(2,1)S(1)}, bf16[192,128]{1,0:T(8,128)(2,1)S(1)}, u32[]{:S(2)}, u32[]{:S(2)}) collective-permute-start(bf16[192,128]{1,0:T(8,128)(2,1)S(1)} %get-tuple-element.33.refs_0_), channel_id=1, source_target_pairs={{0,24},{8,16},{16,8},{24,0},{1,25},{9,17},{17,9},{25,1},{2,26},{10... | collective-permute-start | bytes 147464 | tf_op jit(solution)/shard_map/ppermute | solution.py:40
  43.0 4.2 %collective-permute-start.16 = (bf16[192,128]{1,0:T(8,128)(2,1)S(1)}, bf16[192,128]{1,0:T(8,128)(2,1)S(1)}, u32[]{:S(2)}, u32[]{:S(2)}) collective-permute-start(bf16[192,128]{1,0:T(8,128)(2,1)S(1)} %get-tuple-element.33.refs_0_), channel_id=1, source_target_pairs={{0,16},{8,24},{16,0},{24,8},{1,17},{9,25},{17,1},{25,9},{2,18},{10... | collective-permute-start | bytes 147464 | tf_op jit(solution)/shard_map/ppermute | solution.py:40
  43.5 4.1 %collective-permute-start.15 = (bf16[192,128]{1,0:T(8,128)(2,1)S(1)}, bf16[192,128]{1,0:T(8,128)(2,1)S(1)}, u32[]{:S(2)}, u32[]{:S(2)}) collective-permute-start(bf16[192,128]{1,0:T(8,128)(2,1)S(1)} %get-tuple-element.33.refs_0_), channel_id=1, source_target_pairs={{0,8},{8,0},{16,24},{24,16},{1,9},{9,1},{17,25},{25,17},{2,10},{10... | collective-permute-start | bytes 147464 | tf_op jit(solution)/shard_map/ppermute | solution.py:40
  48.6 1.4 %collective-permute-start.18 = (bf16[4,128,128]{2,1,0:T(8,128)(2,1)S(1)}, bf16[4,128,128]{2,1,0:T(8,128)(2,1)S(1)}, u32[]{:S(2)}, u32[]{:S(2)}) collective-permute-start(bf16[4,128,128]{2,1,0:T(8,128)(2,1)S(1)} %get-tuple-element.35), channel_id=1, source_target_pairs={{0,1},{1,0},{2,3},{3,2},{4,5},{5,4},{6,7},{7,6},{8,9},{9,8},{10,11... | collective-permute-start | bytes 393224 | tf_op jit(solution)/shard_map/ppermute | solution.py:40
  50.0 4.6 %collective-permute-start.19 = (bf16[128,128]{1,0:T(8,128)(2,1)S(1)}, bf16[128,128]{1,0:T(8,128)(2,1)S(1)}, u32[]{:S(2)}, u32[]{:S(2)}) collective-permute-start(bf16[128,128]{1,0:T(8,128)(2,1)S(1)} %get-tuple-element.37), channel_id=1, source_target_pairs={{0,2},{1,3},{2,0},{3,1},{4,6},{5,7},{6,4},{7,5},{8,10},{9,11},{10,... | collective-permute-start | bytes 98312 | tf_op jit(solution)/shard_map/ppermute | solution.py:40
  51.8 5.4 %collective-permute-start.20 = (bf16[128,128]{1,0:T(8,128)(2,1)S(1)}, bf16[128,128]{1,0:T(8,128)(2,1)S(1)}, u32[]{:S(2)}, u32[]{:S(2)}) collective-permute-start(bf16[128,128]{1,0:T(8,128)(2,1)S(1)} %get-tuple-element.38), channel_id=1, source_target_pairs={{0,4},{1,5},{2,6},{3,7},{4,0},{5,1},{6,2},{7,3},{8,12},{9,13},{10,... | collective-permute-start | bytes 98312 | tf_op jit(solution)/shard_map/ppermute | solution.py:40
  52.7 5.7 %collective-permute-start.21 = (bf16[128,128]{1,0:T(8,128)(2,1)S(1)}, bf16[128,128]{1,0:T(8,128)(2,1)S(1)}, u32[]{:S(2)}, u32[]{:S(2)}) collective-permute-start(bf16[128,128]{1,0:T(8,128)(2,1)S(1)} %get-tuple-element.39), channel_id=1, source_target_pairs={{0,6},{1,7},{2,4},{3,5},{4,2},{5,3},{6,0},{7,1},{8,14},{9,15},{10,... | collective-permute-start | bytes 98312 | tf_op jit(solution)/shard_map/ppermute | solution.py:40

commit v2 on v1

v2 whole, which is shorter than its diff:
```python
import math
from functools import partial

import jax
import jax.numpy as jnp
import numpy as np
from jax import lax
from jax.experimental import pallas as pl
from jax.experimental.pallas import tpu as pltpu
from jax.sharding import PartitionSpec as P

REACH = 8
ITERS = 2
LANES = 128


def taper(sigma):
    offsets = np.arange(-REACH, REACH + 1).astype(np.float64)
    values = np.exp(-offsets * offsets / (2.0 * sigma * sigma))
    values = values * np.cos(np.pi * offsets / (2.0 * REACH + 2.0)) ** 2
    return [float(v) for v in (values / values.sum()).astype(np.float32)]


ROW_TAPS = taper(3.0)
COL_TAPS = taper(5.0)


def stencil(low, own, high, taps, axis):
    size = own.shape[axis]
    place = lax.broadcasted_iota(jnp.int32, own.shape, axis)
    total = taps[REACH] * own
    for shift in range(1, REACH + 1):
        after = pltpu.roll(jnp.where(place < shift, high, own), size - shift, axis)
        before = pltpu.roll(jnp.where(place >= size - shift, low, own), shift, axis)
        total = total + taps[REACH + shift] * after + taps[REACH - shift] * before
    return total


def swap(value, axis, mask):
    return lax.ppermute(value, axis, [(i, i ^ mask) for i in range(lax.axis_size(axis))])


def split(value):
    upper = value.astype(jnp.bfloat16)
    lower = (value - upper.astype(jnp.float32)).astype(jnp.bfloat16)
    return jnp.concatenate([upper, lower], axis=0)


def whole(both):
    half = both.shape[0] // 2
    both = both.astype(jnp.float32)
    return both[:half] + both[half:]


def load_kernel(source_ref, out_ref, sems):
    chunks = sems.shape[0]
    count = source_ref.shape[0] // chunks
    copies = [
        pltpu.make_async_copy(
            source_ref.at[pl.ds(n * count, count)], out_ref.at[pl.ds(n * count, count)], sems.at[n]
        )
        for n in range(chunks)
    ]
    for copy in copies:
        copy.start()
    for copy in copies:
        copy.wait()


def join_kernel(*refs):
    part_refs, out_ref = refs[-3:-1], refs[-1]
    half = out_ref.shape[0] // 2
    for n, ref in enumerate(part_refs):
        out_ref[n * half : (n + 1) * half] = ref[...]


def starts_of(masks, other):
    me = lax.axis_index("tile")
    chip, core = lax.div(me, 2), lax.rem(me, 2)
    core = 1 - core if other else core
    return [pl.multiple_of((2 * (chip ^ mask) + core) * LANES, LANES) for mask in masks]


def project_kernel(rows, masks, other, last, *refs):
    fields_ref, factor_ref = refs[:2]
    count, lines = factor_ref.shape[0], fields_ref.shape[1]
    cols = lines // rows
    before_ref = refs[2] if len(refs) > 3 + last else None
    out_ref = refs[-1]
    if out_ref.shape[0] > count // rows:
        out_ref[...] = jnp.zeros_like(out_ref)
    field = jnp.concatenate([fields_ref[n] for n in range(len(masks))], axis=1)
    step = min(256, count)
    row_of = lax.broadcasted_iota(jnp.int32, (rows, lines), 0)
    lane_of = lax.broadcasted_iota(jnp.int32, (rows, lines), 1)
    same = (lax.rem(lane_of, rows) == row_of).astype(jnp.float32)
    starts = starts_of(masks, other)
    for at in range(0, count, step):
        left = jnp.concatenate(
            [factor_ref[at : at + step, pl.ds(start, LANES)] for start in starts], axis=1
        )
        part = lax.dot_general(
            left, field, (((1,), (1,)), ((), ())), preferred_element_type=jnp.float32
        )
        part = part.reshape(step // rows, rows, lines) * same[None]
        part = jnp.sum(part, axis=1)
        first, end = at // rows, (at + step) // rows
        out_ref[first:end, :] = part if before_ref is None else before_ref[first:end, :] + part
    if not last:
        return
    pick = (
        lax.broadcasted_iota(jnp.int32, (cols, lines), 1) // rows
        == lax.broadcasted_iota(jnp.int32, (cols, lines), 0)
    ).astype(jnp.bfloat16)
    pay_ref = refs[-2]
    for at in range(0, out_ref.shape[0], LANES):
        both = split(out_ref[at : at + LANES, :])
        proj = lax.dot_general(
            pick, both, (((1,), (1,)), ((), ())), preferred_element_type=jnp.float32
        )
        first = at // LANES * cols
        pay_ref[first : first + cols, :] = proj[:, :LANES] + proj[:, LANES:]


def split_kernel(value_ref, out_ref):
    out_ref[...] = split(value_ref[...])


def merge_kernel(left_ref, right_ref, out_ref):
    out_ref[...] = split(whole(left_ref[...]) + whole(right_ref[...]))


def columns_kernel(masks, halve, x_ref, fields_ref, along_ref, short_ref):
    near = fields_ref.shape[0]
    me = lax.axis_index("tile")
    chip = lax.div(me, 2)
    left, right = lax.div(me + 1, 2) - 1, lax.div(me + 1, 2)
    low = jnp.zeros(x_ref.shape, jnp.float32)
    high = low
    for n in range(near):
        part = fields_ref[n].astype(jnp.float32)
        low = jnp.where((chip ^ masks[n]) == left, part, low)
        high = jnp.where((chip ^ masks[n]) == right, part, high)
    own = 0.5 * x_ref[...] if halve else x_ref[...]
    along = stencil(low, own, high, COL_TAPS, 1)
    along_ref[...] = along
    short_ref[...] = along.astype(jnp.bfloat16)


def product(coef, starts, factor_ref, out_ref):
    for n in range(0, len(starts), 2):
        pair = starts[n : n + 2]
        right = jnp.concatenate([factor_ref[:, pl.ds(start, LANES)] for start in pair], axis=1)
        term = jnp.dot(coef, right, preferred_element_type=jnp.float32)
        for m in range(len(pair)):
            out_ref[n + m] = term[:, m * LANES : (m + 1) * LANES].astype(out_ref.dtype)


def first_term_kernel(
    rows, cols, ncells, masks, scale_ref, factor_ref, left_ref, right_ref, coef_ref, out_ref
):
    ranks = factor_ref.shape[0] // rows
    lines = cols * rows
    span = LANES // rows

    spread = (
        lax.broadcasted_iota(jnp.int32, (LANES, LANES), 1) // rows
        == lax.broadcasted_iota(jnp.int32, (LANES, LANES), 0)
    ).astype(jnp.bfloat16)
    same = (
        lax.rem(lax.broadcasted_iota(jnp.int32, (lines, LANES), 1), rows)
        == lax.rem(lax.broadcasted_iota(jnp.int32, (lines, LANES), 0), rows)
    ).astype(jnp.float32)
    total = whole(left_ref[...]) + whole(right_ref[...])
    for at in range(0, ranks, LANES):
        count = min(LANES, ranks - at)
        first = at // LANES * cols
        proj = total[first : first + cols]
        scale = scale_ref[:, at : at + count]
        weights = scale * scale / ncells
        if count < LANES:
            weights = jnp.concatenate([weights, jnp.zeros((1, LANES - count), jnp.float32)], axis=1)
        c = proj * weights
        turned = [c if n == 0 else pltpu.roll(c, LANES - n * span, 1) for n in range(rows)]
        stacked = jnp.concatenate(turned, axis=0).astype(jnp.bfloat16)
        wide = jnp.dot(stacked, spread, preferred_element_type=jnp.float32)
        for n in range(rows):
            start = (at + n * span) * rows
            if start >= ranks * rows:
                break
            piece = wide[n * cols : (n + 1) * cols, :]
            piece = jnp.broadcast_to(piece[:, None, :], (cols, rows, LANES)).reshape(lines, LANES)
            coef_ref[:, start : start + LANES] = (piece * same).astype(jnp.bfloat16)
    product(coef_ref[...], starts_of(masks, True), factor_ref, out_ref)


def term_kernel(wanted, coef_ref, factor_ref, *out_refs):
    for (masks, other, _), out_ref in zip(wanted, out_refs):
        product(coef_ref[...], starts_of(masks, other), factor_ref, out_ref)


def add_kernel(mine_ref, got_ref, out_ref):
    out_ref[...] = (mine_ref[...] + got_ref[...].astype(jnp.float32)).astype(out_ref.dtype)


def halve_kernel(*refs):
    part_refs, (keep_ref, send_ref) = refs[:-2], refs[-2:]
    half = keep_ref.shape[0]
    total = part_refs[0][...]
    for ref in part_refs[1:]:
        total = total + ref[...].astype(jnp.float32)
    keep_ref[...] = total[:half]
    send_ref[...] = total[half:].astype(send_ref.dtype)


def local_kernel(rows, cols, halve, b_ref, x_ref, amp_ref, along_ref, twin_ref, beyond_ref, base_ref):
    lines = cols * rows
    odd = lax.rem(lax.axis_index("grp"), 2) == 1
    twin = twin_ref[...].astype(jnp.float32)
    beyond = beyond_ref[...].astype(jnp.float32)
    low = jnp.where(odd, twin, beyond).reshape(cols, rows, LANES)
    high = jnp.where(odd, beyond, twin).reshape(cols, rows, LANES)
    own = along_ref[...].reshape(cols, rows, LANES)
    conv = stencil(low, own, high, ROW_TAPS, 1)
    x = 0.5 * x_ref[...] if halve else x_ref[...]
    scaled = (amp_ref[...][None] * conv).reshape(lines, LANES)
    base_ref[...] = b_ref[...] - (x + scaled)


def update_kernel(count, halve, x_ref, base_ref, *refs):
    term_refs, (new_ref, other_ref) = refs[:count], refs[count:]
    rank_sum = term_refs[0][0].astype(jnp.float32)
    for ref in term_refs[1:]:
        rank_sum = rank_sum + ref[0].astype(jnp.float32)
    x = 0.5 * x_ref[...] if halve else x_ref[...]
    residual = base_ref[...] - rank_sum
    new = x + 0.5 * residual
    new_ref[...] = new
    if other_ref.dtype == jnp.float32:
        other_ref[...] = residual
    else:
        other_ref[0] = new.astype(jnp.bfloat16)


def on_device(right_side, amplitude, factor, scale):
    cols, rows, width = right_side.shape
    ranks = factor.shape[0]
    tiles = lax.axis_size("tile")
    groups = lax.axis_size("grp")
    near = tiles // 2
    lines = cols * rows
    ncells_all = rows * width * groups * tiles
    blocks = -(-ranks // LANES)
    flat = factor.reshape(ranks * rows, tiles * width)
    b = right_side.reshape(lines, width)
    scale = scale.reshape(1, ranks)
    x = b
    short = (0.5 * b).astype(jnp.bfloat16)[None]

    f32, bf16 = jnp.float32, jnp.bfloat16

    def shape(dtype, *dims):
        return jax.ShapeDtypeStruct(dims, dtype)

    def call(kernel, out_shape, flops=0, moved=1 << 18, outside=0, inside=0, **options):
        if outside:
            options["in_specs"] = [pl.BlockSpec(memory_space=pl.ANY)] * outside + [
                pl.BlockSpec(memory_space=pltpu.VMEM)
            ] * inside
        return pl.pallas_call(
            kernel,
            out_shape=out_shape,
            compiler_params=pltpu.CompilerParams(vmem_limit_bytes=32 << 20),
            cost_estimate=pl.CostEstimate(flops=flops, bytes_accessed=moved, transcendentals=0),
            **options,
        )

    work = 2 * lines * ranks * rows * width
    held = call(
        load_kernel,
        shape(bf16, *flat.shape),
        moved=4 * flat.size,
        in_specs=[pl.BlockSpec(memory_space=pltpu.HBM)],
        out_specs=pl.BlockSpec(memory_space=pltpu.VMEM),
        scratch_shapes=[pltpu.SemaphoreType.DMA((8,))],
        name="load",
    )(flat)
    bits = [1 << n for n in range(near.bit_length() - 1)]
    twins = [(i, i ^ 1) for i in range(groups)]
    beyond = [(i, i + 1 if i % 2 else i - 1) for i in range(1, groups - 1)]
    for step in range(ITERS):
        halve = step == 0

        def project(fields, masks, other, before=None, last=False):
            count = 2 * len(masks) * rows * ranks * width
            return call(
                partial(project_kernel, rows, masks, other, last),
                shape(f32, blocks * cols, LANES) if last else shape(f32, blocks * LANES, lines),
                flops=work * len(masks),
                moved=count,
                scratch_shapes=[pltpu.VMEM((blocks * LANES, lines), f32)] if last else [],
                name="project",
            )(fields, held, *([] if before is None else [before]))

        fields, masks = short, [0]
        fresh, fresh_masks = short, [0]
        diag = None
        for at, bit in enumerate(reversed(bits)):
            got = swap(fields, "tile", 2 * bit)
            if at:
                diag = project(fresh, fresh_masks, False, diag)
            size = 2 * len(masks)
            joined = call(
                join_kernel,
                shape(bf16, size, lines, width),
                outside=1,
                inside=2,
                name="join",
            )(held if diag is None else diag, fields, got)
            fresh_masks = [mask ^ bit for mask in masks]
            fresh = got
            masks = masks + fresh_masks
            fields = joined
            if at == 0:
                fresh, fresh_masks = fields, masks
        across = swap(fields, "tile", 1)
        diag = project(fresh, fresh_masks, False, diag)
        proj = project(across, masks, True, diag, True)
        along, along_short = call(
            partial(columns_kernel, masks, halve),
            (shape(f32, lines, width), shape(bf16, lines, width)),
            name="columns",
        )(x, across)
        both = shape(bf16, 2 * blocks * cols, LANES)
        part = call(split_kernel, both, name="split")(proj)
        mask = 1
        while 2 * mask < groups:
            part = call(merge_kernel, both, name="merge")(part, swap(part, "grp", mask))
            mask *= 2
        rest = swap(part, "grp", mask)

        first, second = masks[: near // 2], masks[near // 2 :]
        half = near // 2
        coef, far = call(
            partial(first_term_kernel, rows, cols, ncells_all, second),
            (shape(bf16, lines, ranks * rows), shape(bf16, half, lines, width)),
            flops=work * half,
            moved=flat.size // 2,
            name="term",
        )(scale, held, part, rest)
        got = swap(far, "tile", 1)

        def term(*wanted):
            count = sum(len(masks) for masks, _, _ in wanted)
            return call(
                partial(term_kernel, wanted),
                [shape(dtype, len(masks), lines, width) for masks, _, dtype in wanted],
                flops=work * count,
                moved=flat.size // 2,
                name="term",
            )(coef, held)

        mine, far = term((second, False, f32), (first, True, bf16))
        send = call(add_kernel, shape(bf16, half, lines, width), name="add")(mine, got)
        arrived = swap(send, "tile", 2)
        got = swap(far, "tile", 1)
        (mine,) = term((first, False, f32))
        terms = [mine, got, arrived]
        for bit in bits[1:]:
            half //= 2
            keep, send = call(
                halve_kernel,
                (shape(f32, half, lines, width), shape(bf16, half, lines, width)),
                name="halve",
            )(*terms)
            terms = [keep, swap(send, "tile", 2 * bit)]
        twin = lax.ppermute(along_short, "grp", twins)
        other = lax.ppermute(along_short, "grp", beyond)
        base = call(
            partial(local_kernel, rows, cols, halve), shape(f32, lines, width), name="local"
        )(b, x, amplitude, along, twin, other)
        last = step == ITERS - 1
        x, short = call(
            partial(update_kernel, len(terms), halve),
            (shape(f32, lines, width), shape(f32, lines, width) if last else shape(bf16, 1, lines, width)),
            name="update",
        )(x, base, *terms)
    return x.reshape(cols, rows, width), short.reshape(cols, rows, width)


def solution(mesh):
    in_specs = (P(None, "grp", "tile"), P("grp", "tile"), P("tile", "grp", None), P("tile"))
    out_specs = (P(None, "grp", "tile"), P(None, "grp", "tile"))
    return jax.shard_map(
        on_device, mesh=mesh, in_specs=in_specs, out_specs=out_specs, check_vma=False
    )
```

time: 59.3 us -> 69.3 us (1.17)
  waiting for transfers between devices: 19.3 us -> 26.9 us
  starting transfers between devices: 26.3 us -> 27.6 us
  Pallas kernels: 9.56 us -> 10.5 us
    ppermute x0 -> x4, starting transfers between devices: none -> 8.4 us  [the longest x2 7.07 us: on_device(): twin = lax.ppermute(along_short, 'grp', twins)]
    ppermute x22 -> x18, waiting for transfers between devices: 19.3 us -> 26.9 us  [swap(): lax.ppermute(value, axis, [(i, i ^ mask) for i in range(lax.axis_size(axi...]
    ppermute x22 -> x18, starting transfers between devices: 26.3 us -> 19.2 us  [swap(): lax.ppermute(value, axis, [(i, i ^ mask) for i in range(lax.axis_size(axi...]
    pallas_call x14 -> x28, Pallas kernels: 8.82 us -> 9.83 us  [the longest x6 4.23 us: project(): call(partial(project_kernel, rows, masks, other, last), shape(f32, blocks...]
  transfers between devices with their start and end apart: 22 -> 22, of which waited for: 18 -> 11; matrix products, arithmetic and copies ran while one was open for 0% -> 0% of each run, Pallas kernels for 7% -> 9%
where the time goes in v2:
time: 69.3 us; the launch traced here: 69 us
  starting transfers between devices  27.6 us (40%)
  waiting for transfers between devices  26.9 us (39%)
  Pallas kernels  10.5 us (15%)
  local copies, waits for them, and re-layouts  2.2 us (3%)
  between operations  0.94 us (1%)
  other arithmetic  0.85 us (1%)
    ppermute x18, waiting for transfers between devices, swap(): lax.ppermute(value, axis, [(i, i ^ mask) for i in range(lax.axis_size(axi...  26.9 us
    ppermute x18, starting transfers between devices, swap(): lax.ppermute(value, axis, [(i, i ^ mask) for i in range(lax.axis_size(axi...  19.2 us
    ppermute x2, starting transfers between devices, on_device(): twin = lax.ppermute(along_short, 'grp', twins)  7.07 us
    pallas_call x6, Pallas kernels, project(): call(partial(project_kernel, rows, masks, other, last), shape(f32, blocks...  4.23 us
    pallas_call x4, Pallas kernels, term(): call(partial(term_kernel, wanted), [shape(dtype, len(masks), lines, width...  2.57 us
    unnamed x8, local copies, waits for them, and re-layouts  2.2 us
    pallas_call x2, Pallas kernels, on_device(): call(partial(first_term_kernel, rows, cols, ncells_all, second), (shape(b...  1.46 us
  transfers between devices with their start and end apart: 22, of which 11 were waited for; matrix products, arithmetic and copies ran while one was open for 0% of the time, Pallas kernels for 9%

profile of v2, /device:TPU:0, one launch (start us, length us, event | category | flops | bytes accessed | tf_op | source)
XLA Modules:
  0.0 69.0 jit_solution(5366644945236000115)
XLA Ops:
  0.6 0.8 %fusion.refs_1_ = bf16[1,128,128]{2,1,0:T(8,128)(2,1)S(1)} fusion(f32[16,8,128]{2,1,0:T(8,128)} %param.4), kind=kLoop, calls=%fused_computation.1 | loop fusion | flops 32768 | bytes 98304 | tf_op jit(solution)/shard_map/convert_element_type | solution.py:258
  1.5 4.0 %collective-permute-start = (bf16[1,128,128]{2,1,0:T(8,128)(2,1)S(1)}, bf16[1,128,128]{2,1,0:T(8,128)(2,1)S(1)}, u32[]{:S(2)}, u32[]{:S(2)}) collective-permute-start(bf16[1,128,128]{2,1,0:T(8,128)(2,1)S(1)} %fusion.refs_1_), channel_id=1, source_target_pairs={{0,4},{1,5},{2,6},{3,7},{4,0},{5,1},{6,2},{7,3},{8,12},{9,13},{10,... | collective-permute-start | bytes 98312 | tf_op jit(solution)/shard_map/ppermute | solution.py:40
  5.5 2.2 %copy-done = bf16[256,8,1024]{2,1,0:T(8,128)(2,1)S(1)} copy-done((bf16[256,8,1024]{2,1,0:T(8,128)(2,1)S(1)}, bf16[256,8,1024]{2,1,0:T(8,128)(2,1)}, u32[]{:S(2)}) %copy-start) | copy-done | bytes 4194328
  7.7 0.4 load.1.refs_0_.refs_1_.factor_ref
  8.1 0.0 collective-permute-done.refs_2_
  8.1 1.6 %collective-permute-start.1 = (bf16[2,128,128]{2,1,0:T(8,128)(2,1)S(1)}, bf16[2,128,128]{2,1,0:T(8,128)(2,1)S(1)}, u32[]{:S(2)}, u32[]{:S(2)}) collective-permute-start(bf16[2,128,128]{2,1,0:T(8,128)(2,1)S(1)} %join.4.refs_0_.refs_1_), channel_id=1, source_target_pairs={{0,2},{1,3},{2,0},{3,1},{4,6},{5,7},{6,4},{7,5},{8,10},{9,11},{10,... | collective-permute-start | bytes 196616 | tf_op jit(solution)/shard_map/ppermute | solution.py:40
  9.7 0.6 project.6.refs_0_.refs_2_
  10.3 2.1 %collective-permute-done.1.refs_2_.refs_0_ = bf16[2,128,128]{2,1,0:T(8,128)(2,1)S(1)} collective-permute-done((bf16[2,128,128]{2,1,0:T(8,128)(2,1)S(1)}, bf16[2,128,128]{2,1,0:T(8,128)(2,1)S(1)}, u32[]{:S(2)}, u32[]{:S(2)}) %collective-permute-start.1) | collective-permute-done | bytes 65568 | tf_op jit(solution)/shard_map/ppermute | solution.py:40
  12.4 0.0 copy-start.3
  12.5 0.1 collective-permute-start.2
  12.5 0.6 project.7.refs_2_
  13.1 0.8 %collective-permute-done.2.fields_ref.refs_0_ = bf16[4,128,128]{2,1,0:T(8,128)(2,1)S(1)} collective-permute-done((bf16[4,128,128]{2,1,0:T(8,128)(2,1)S(1)}, bf16[4,128,128]{2,1,0:T(8,128)(2,1)S(1)}, u32[]{:S(2)}, u32[]{:S(2)}) %collective-permute-start.2) | collective-permute-done | bytes 131104 | tf_op jit(solution)/shard_map/ppermute | solution.py:40
  13.9 1.0 %project.8.value_ref = f32[32,128]{1,0:T(8,128)S(1)} custom-call(bf16[4,128,128]{2,1,0:T(8,128)(2,1)S(1)} %collective-permute-done.2.fields_ref.refs_0_, bf16[2048,1024]{1,0:T(8,128)(2,1)S(1)} %load.1.refs_0_.refs_1_.factor_ref, f32[256,128]{1,0:T(8,128)S(1)} %project.7.refs_2_), custom_call_target="tpu_custom_call" | custom-call | flops 268435456 | bytes 2097152 | tf_op jit(solution)/shard_map/project/pallas_call | solution.py:296
  14.9 1.6 %collective-permute-start.5 = (bf16[64,128]{1,0:T(8,128)(2,1)S(1)}, bf16[64,128]{1,0:T(8,128)(2,1)S(1)}, u32[]{:S(2)}, u32[]{:S(2)}) collective-permute-start(bf16[64,128]{1,0:T(8,128)(2,1)S(1)} %split.2.left_ref), channel_id=1, source_target_pairs={{0,8},{8,0},{16,24},{24,16},{1,9},{9,1},{17,25},{25,17},{2,10},{10... | collective-permute-start | bytes 49160 | tf_op jit(solution)/shard_map/ppermute | solution.py:40
  16.5 2.2 %collective-permute-done.5.right_ref = bf16[64,128]{1,0:T(8,128)(2,1)S(1)} collective-permute-done((bf16[64,128]{1,0:T(8,128)(2,1)S(1)}, bf16[64,128]{1,0:T(8,128)(2,1)S(1)}, u32[]{:S(2)}, u32[]{:S(2)}) %collective-permute-start.5) | collective-permute-done | bytes 16416 | tf_op jit(solution)/shard_map/ppermute | solution.py:40
  18.7 1.6 %collective-permute-start.6 = (bf16[64,128]{1,0:T(8,128)(2,1)S(1)}, bf16[64,128]{1,0:T(8,128)(2,1)S(1)}, u32[]{:S(2)}, u32[]{:S(2)}) collective-permute-start(bf16[64,128]{1,0:T(8,128)(2,1)S(1)} %merge.2.left_ref), channel_id=1, source_target_pairs={{0,16},{8,24},{16,0},{24,8},{1,17},{9,25},{17,1},{25,9},{2,18},{10... | collective-permute-start | bytes 49160 | tf_op jit(solution)/shard_map/ppermute | solution.py:40
  20.3 2.2 %collective-permute-done.6.right_ref = bf16[64,128]{1,0:T(8,128)(2,1)S(1)} collective-permute-done((bf16[64,128]{1,0:T(8,128)(2,1)S(1)}, bf16[64,128]{1,0:T(8,128)(2,1)S(1)}, u32[]{:S(2)}, u32[]{:S(2)}) %collective-permute-start.6) | collective-permute-done | bytes 16416 | tf_op jit(solution)/shard_map/ppermute | solution.py:40
  22.5 0.7 %term.6 = (bf16[128,2048]{1,0:T(8,128)(2,1)S(1)}, bf16[2,128,128]{2,1,0:T(8,128)(2,1)S(1)}) custom-call(f32[1,256]{1,0:T(1,128)S(1)} %bitcast.13, bf16[2048,1024]{1,0:T(8,128)(2,1)S(1)} %load.1.refs_0_.refs_1_.factor_ref, bf16[64,128]{1,0:T(8,128)(2,1)S(1)} %merge.2.left_ref, bf16[64,128]{1,0:T(8,128)(2,1)S(1)} %collective-permute-done.6.right_ref), custom_call_target="tpu_custom_call" | custom-call | flops 134217728 | bytes 1048576 | tf_op jit(solution)/shard_map/term/pallas_call | solution.py:344
  23.3 0.1 collective-permute-start.8
  23.4 0.0 copy-start.2
  23.4 0.8 %term.8 = (f32[2,128,128]{2,1,0:T(8,128)S(1)}, bf16[2,128,128]{2,1,0:T(8,128)(2,1)S(1)}) custom-call(bf16[128,2048]{1,0:T(8,128)(2,1)S(1)} %get-tuple-element.24.coef_ref, bf16[2048,1024]{1,0:T(8,128)(2,1)S(1)} %load.1.refs_0_.refs_1_.factor_ref), custom_call_target="tpu_custom_call" | custom-call | flops 268435456 | bytes 1048576 | tf_op jit(solution)/shard_map/term/pallas_call | solution.py:355
  24.2 0.5 collective-permute-start.7
  24.7 0.0 collective-permute-done.8.got_ref
  24.7 1.6 %collective-permute-start.9 = (bf16[2,128,128]{2,1,0:T(8,128)(2,1)S(1)}, bf16[2,128,128]{2,1,0:T(8,128)(2,1)S(1)}, u32[]{:S(2)}, u32[]{:S(2)}) collective-permute-start(bf16[2,128,128]{2,1,0:T(8,128)(2,1)S(1)} %add.2), channel_id=1, source_target_pairs={{0,2},{1,3},{2,0},{3,1},{4,6},{5,7},{6,4},{7,5},{8,10},{9,11},{10,... | collective-permute-start | bytes 196616 | tf_op jit(solution)/shard_map/ppermute | solution.py:40
  26.4 0.4 columns.2
  26.7 0.7 collective-permute-start.4
  27.4 4.3 %collective-permute-start.3 = (bf16[128,128]{1,0:T(8,128)(2,1)S(1)}, bf16[128,128]{1,0:T(8,128)(2,1)S(1)}, u32[]{:S(2)}, u32[]{:S(2)}) collective-permute-start(bf16[128,128]{1,0:T(8,128)(2,1)S(1)} %get-tuple-element.23), channel_id=1, source_target_pairs={{0,8},{8,0},{16,24},{24,16},{1,9},{9,1},{17,25},{25,17},{2,10},{10... | collective-permute-start | bytes 98312 | tf_op jit(solution)/shard_map/ppermute | solution.py:377
  31.7 0.5 term.7.refs_0_
  32.2 0.0 collective-permute-done.7.refs_1_
  32.2 0.0 collective-permute-done.9.refs_2_
  32.3 2.5 %collective-permute-start.10 = (bf16[1,128,128]{2,1,0:T(8,128)(2,1)S(1)}, bf16[1,128,128]{2,1,0:T(8,128)(2,1)S(1)}, u32[]{:S(2)}, u32[]{:S(2)}) collective-permute-start(bf16[1,128,128]{2,1,0:T(8,128)(2,1)S(1)} %get-tuple-element.29), channel_id=1, source_target_pairs={{0,4},{1,5},{2,6},{3,7},{4,0},{5,1},{6,2},{7,3},{8,12},{9,13},{10,... | collective-permute-start | bytes 98312 | tf_op jit(solution)/shard_map/ppermute | solution.py:40
  34.7 0.0 collective-permute-done.4.beyond_ref
  34.7 0.0 collective-permute-done.3.twin_ref
  34.7 0.2 local.2.base_ref
  34.9 2.5 %collective-permute-done.10.refs_1_ = bf16[1,128,128]{2,1,0:T(8,128)(2,1)S(1)} collective-permute-done((bf16[1,128,128]{2,1,0:T(8,128)(2,1)S(1)}, bf16[1,128,128]{2,1,0:T(8,128)(2,1)S(1)}, u32[]{:S(2)}, u32[]{:S(2)}) %collective-permute-start.10) | collective-permute-done | bytes 32800 | tf_op jit(solution)/shard_map/ppermute | solution.py:40
  37.4 2.2 %collective-permute-start.11 = (bf16[1,128,128]{2,1,0:T(8,128)(2,1)S(1)}, bf16[1,128,128]{2,1,0:T(8,128)(2,1)S(1)}, u32[]{:S(2)}, u32[]{:S(2)}) collective-permute-start(bf16[1,128,128]{2,1,0:T(8,128)(2,1)S(1)} %get-tuple-element.31.refs_1_), channel_id=1, source_target_pairs={{0,4},{1,5},{2,6},{3,7},{4,0},{5,1},{6,2},{7,3},{8,12},{9,13},{10,... | collective-permute-start | bytes 98312 | tf_op jit(solution)/shard_map/ppermute | solution.py:40
  39.6 2.8 %collective-permute-done.11.refs_2_ = bf16[1,128,128]{2,1,0:T(8,128)(2,1)S(1)} collective-permute-done((bf16[1,128,128]{2,1,0:T(8,128)(2,1)S(1)}, bf16[1,128,128]{2,1,0:T(8,128)(2,1)S(1)}, u32[]{:S(2)}, u32[]{:S(2)}) %collective-permute-start.11) | collective-permute-done | bytes 32800 | tf_op jit(solution)/shard_map/ppermute | solution.py:40
  42.4 0.1 collective-permute-start.12
  42.5 0.5 project.9.refs_0_.refs_2_
  43.1 3.6 %collective-permute-done.12.refs_2_.refs_0_ = bf16[2,128,128]{2,1,0:T(8,128)(2,1)S(1)} collective-permute-done((bf16[2,128,128]{2,1,0:T(8,128)(2,1)S(1)}, bf16[2,128,128]{2,1,0:T(8,128)(2,1)S(1)}, u32[]{:S(2)}, u32[]{:S(2)}) %collective-permute-start.12) | collective-permute-done | bytes 65568 | tf_op jit(solution)/shard_map/ppermute | solution.py:40
  46.7 0.1 collective-permute-start.13
  46.8 0.6 project.10.refs_2_
  47.3 0.8 %collective-permute-done.13.fields_ref.refs_0_ = bf16[4,128,128]{2,1,0:T(8,128)(2,1)S(1)} collective-permute-done((bf16[4,128,128]{2,1,0:T(8,128)(2,1)S(1)}, bf16[4,128,128]{2,1,0:T(8,128)(2,1)S(1)}, u32[]{:S(2)}, u32[]{:S(2)}) %collective-permute-start.13) | collective-permute-done | bytes 131104 | tf_op jit(solution)/shard_map/ppermute | solution.py:40
  48.1 1.0 %project.11.value_ref = f32[32,128]{1,0:T(8,128)S(1)} custom-call(bf16[4,128,128]{2,1,0:T(8,128)(2,1)S(1)} %collective-permute-done.13.fields_ref.refs_0_, bf16[2048,1024]{1,0:T(8,128)(2,1)S(1)} %load.1.refs_0_.refs_1_.factor_ref, f32[256,128]{1,0:T(8,128)S(1)} %project.10.refs_2_), custom_call_target="tpu_custom_call" | custom-call | flops 268435456 | bytes 2097152 | tf_op jit(solution)/shard_map/project/pallas_call | solution.py:296
  49.1 0.1 collective-permute-start.16
  49.2 3.7 %collective-permute-done.16.right_ref = bf16[64,128]{1,0:T(8,128)(2,1)S(1)} collective-permute-done((bf16[64,128]{1,0:T(8,128)(2,1)S(1)}, bf16[64,128]{1,0:T(8,128)(2,1)S(1)}, u32[]{:S(2)}, u32[]{:S(2)}) %collective-permute-start.16) | collective-permute-done | bytes 16416 | tf_op jit(solution)/shard_map/ppermute | solution.py:40
  53.0 0.1 collective-permute-start.17
  53.0 3.7 %collective-permute-done.17.right_ref = bf16[64,128]{1,0:T(8,128)(2,1)S(1)} collective-permute-done((bf16[64,128]{1,0:T(8,128)(2,1)S(1)}, bf16[64,128]{1,0:T(8,128)(2,1)S(1)}, u32[]{:S(2)}, u32[]{:S(2)}) %collective-permute-start.17) | collective-permute-done | bytes 16416 | tf_op jit(solution)/shard_map/ppermute | solution.py:40
  56.8 0.7 %term.9 = (bf16[128,2048]{1,0:T(8,128)(2,1)S(1)}, bf16[2,128,128]{2,1,0:T(8,128)(2,1)S(1)}) custom-call(f32[1,256]{1,0:T(1,128)S(1)} %bitcast.14, bf16[2048,1024]{1,0:T(8,128)(2,1)S(1)} %load.1.refs_0_.refs_1_.factor_ref, bf16[64,128]{1,0:T(8,128)(2,1)S(1)} %merge.3.left_ref, bf16[64,128]{1,0:T(8,128)(2,1)S(1)} %collective-permute-done.17.right_ref), custom_call_target="tpu_custom_call" | custom-call | flops 134217728 | bytes 1048576 | tf_op jit(solution)/shard_map/term/pallas_call | solution.py:344
  57.5 0.1 collective-permute-start.19
  57.6 0.8 %term.11 = (f32[2,128,128]{2,1,0:T(8,128)S(1)}, bf16[2,128,128]{2,1,0:T(8,128)(2,1)S(1)}) custom-call(bf16[128,2048]{1,0:T(8,128)(2,1)S(1)} %get-tuple-element.34.coef_ref, bf16[2048,1024]{1,0:T(8,128)(2,1)S(1)} %load.1.refs_0_.refs_1_.factor_ref), custom_call_target="tpu_custom_call" | custom-call | flops 268435456 | bytes 1048576 | tf_op jit(solution)/shard_map/term/pallas_call | solution.py:355
  58.4 0.6 collective-permute-start.18
  58.9 0.0 collective-permute-done.19.got_ref
  59.0 0.2 collective-permute-start.20
  59.1 0.3 columns.3
  59.5 0.7 collective-permute-start.15
  60.2 2.8 %collective-permute-start.14 = (bf16[128,128]{1,0:T(8,128)(2,1)S(1)}, bf16[128,128]{1,0:T(8,128)(2,1)S(1)}, u32[]{:S(2)}, u32[]{:S(2)}) collective-permute-start(bf16[128,128]{1,0:T(8,128)(2,1)S(1)} %get-tuple-element.33), channel_id=1, source_target_pairs={{0,8},{8,0},{16,24},{24,16},{1,9},{9,1},{17,25},{25,17},{2,10},{10... | collective-permute-start | bytes 98312 | tf_op jit(solution)/shard_map/ppermute | solution.py:377
  62.9 0.5 term.10.refs_0_
  63.4 0.0 collective-permute-done.18.refs_1_
  63.4 0.0 collective-permute-done.20.refs_2_
  63.5 2.3 %collective-permute-start.21 = (bf16[1,128,128]{2,1,0:T(8,128)(2,1)S(1)}, bf16[1,128,128]{2,1,0:T(8,128)(2,1)S(1)}, u32[]{:S(2)}, u32[]{:S(2)}) collective-permute-start(bf16[1,128,128]{2,1,0:T(8,128)(2,1)S(1)} %get-tuple-element.39), channel_id=1, source_target_pairs={{0,4},{1,5},{2,6},{3,7},{4,0},{5,1},{6,2},{7,3},{8,12},{9,13},{10,... | collective-permute-start | bytes 98312 | tf_op jit(solution)/shard_map/ppermute | solution.py:40
  65.8 0.2 local.3.base_ref
  66.0 2.4 %collective-permute-done.21.refs_1_ = bf16[1,128,128]{2,1,0:T(8,128)(2,1)S(1)} collective-permute-done((bf16[1,128,128]{2,1,0:T(8,128)(2,1)S(1)}, bf16[1,128,128]{2,1,0:T(8,128)(2,1)S(1)}, u32[]{:S(2)}, u32[]{:S(2)}) %collective-permute-start.21) | collective-permute-done | bytes 32800 | tf_op jit(solution)/shard_map/ppermute | solution.py:40
  68.4 0.7 update.3
  (20 shorter events, 0.2 us)
Async XLA Ops:
  1.5 6.6 %collective-permute-start = (bf16[1,128,128]{2,1,0:T(8,128)(2,1)S(1)}, bf16[1,128,128]{2,1,0:T(8,128)(2,1)S(1)}, u32[]{:S(2)}, u32[]{:S(2)}) collective-permute-start(bf16[1,128,128]{2,1,0:T(8,128)(2,1)S(1)} %fusion.refs_1_), channel_id=1, source_target_pairs={{0,4},{1,5},{2,6},{3,7},{4,0},{5,1},{6,2},{7,3},{8,12},{9,13},{10,... | collective-permute-start | bytes 98312 | tf_op jit(solution)/shard_map/ppermute | solution.py:40
  5.5 2.2 %copy-start = (bf16[256,8,1024]{2,1,0:T(8,128)(2,1)S(1)}, bf16[256,8,1024]{2,1,0:T(8,128)(2,1)}, u32[]{:S(2)}) copy-start(bf16[256,8,1024]{2,1,0:T(8,128)(2,1)} %param.6) | copy-start | bytes 12582916
  8.1 4.3 %collective-permute-start.1 = (bf16[2,128,128]{2,1,0:T(8,128)(2,1)S(1)}, bf16[2,128,128]{2,1,0:T(8,128)(2,1)S(1)}, u32[]{:S(2)}, u32[]{:S(2)}) collective-permute-start(bf16[2,128,128]{2,1,0:T(8,128)(2,1)S(1)} %join.4.refs_0_.refs_1_), channel_id=1, source_target_pairs={{0,2},{1,3},{2,0},{3,1},{4,6},{5,7},{6,4},{7,5},{8,10},{9,11},{10,... | collective-permute-start | bytes 196616 | tf_op jit(solution)/shard_map/ppermute | solution.py:40
  12.4 10.1 %copy-start.3 = (f32[256]{0:T(256)S(1)}, f32[256]{0:T(256)}, u32[]{:S(2)}) copy-start(f32[256]{0:T(256)} %param.7) | copy-start | bytes 3076
  12.5 1.4 %collective-permute-start.2 = (bf16[4,128,128]{2,1,0:T(8,128)(2,1)S(1)}, bf16[4,128,128]{2,1,0:T(8,128)(2,1)S(1)}, u32[]{:S(2)}, u32[]{:S(2)}) collective-permute-start(bf16[4,128,128]{2,1,0:T(8,128)(2,1)S(1)} %join.5), channel_id=1, source_target_pairs={{0,1},{1,0},{2,3},{3,2},{4,5},{5,4},{6,7},{7,6},{8,9},{9,8},{10,11... | collective-permute-start | bytes 393224 | tf_op jit(solution)/shard_map/ppermute | solution.py:40
  14.9 3.8 %collective-permute-start.5 = (bf16[64,128]{1,0:T(8,128)(2,1)S(1)}, bf16[64,128]{1,0:T(8,128)(2,1)S(1)}, u32[]{:S(2)}, u32[]{:S(2)}) collective-permute-start(bf16[64,128]{1,0:T(8,128)(2,1)S(1)} %split.2.left_ref), channel_id=1, source_target_pairs={{0,8},{8,0},{16,24},{24,16},{1,9},{9,1},{17,25},{25,17},{2,10},{10... | collective-permute-start | bytes 49160 | tf_op jit(solution)/shard_map/ppermute | solution.py:40
  18.7 3.8 %collective-permute-start.6 = (bf16[64,128]{1,0:T(8,128)(2,1)S(1)}, bf16[64,128]{1,0:T(8,128)(2,1)S(1)}, u32[]{:S(2)}, u32[]{:S(2)}) collective-permute-start(bf16[64,128]{1,0:T(8,128)(2,1)S(1)} %merge.2.left_ref), channel_id=1, source_target_pairs={{0,16},{8,24},{16,0},{24,8},{1,17},{9,25},{17,1},{25,9},{2,18},{10... | collective-permute-start | bytes 49160 | tf_op jit(solution)/shard_map/ppermute | solution.py:40
  22.5 3.8 %copy-start.1 = (f32[16,8,128]{2,1,0:T(8,128)S(1)}, f32[16,8,128]{2,1,0:T(8,128)}, u32[]{:S(2)}) copy-start(f32[16,8,128]{2,1,0:T(8,128)} %param.4) | copy-start | bytes 196612
  23.3 1.4 %collective-permute-start.8 = (bf16[2,128,128]{2,1,0:T(8,128)(2,1)S(1)}, bf16[2,128,128]{2,1,0:T(8,128)(2,1)S(1)}, u32[]{:S(2)}, u32[]{:S(2)}) collective-permute-start(bf16[2,128,128]{2,1,0:T(8,128)(2,1)S(1)} %get-tuple-element.27), channel_id=1, source_target_pairs={{0,1},{1,0},{2,3},{3,2},{4,5},{5,4},{6,7},{7,6},{8,9},{9,8},{10,11... | collective-permute-start | bytes 196616 | tf_op jit(solution)/shard_map/ppermute | solution.py:40
  23.4 11.4 %copy-start.2 = (f32[8,128]{1,0:T(8,128)S(1)}, f32[8,128]{1,0:T(8,128)}, u32[]{:S(2)}) copy-start(f32[8,128]{1,0:T(8,128)} %amp_ref.3) | copy-start | bytes 12292
  24.2 8.0 %collective-permute-start.7 = (bf16[2,128,128]{2,1,0:T(8,128)(2,1)S(1)}, bf16[2,128,128]{2,1,0:T(8,128)(2,1)S(1)}, u32[]{:S(2)}, u32[]{:S(2)}) collective-permute-start(bf16[2,128,128]{2,1,0:T(8,128)(2,1)S(1)} %get-tuple-element.25), channel_id=1, source_target_pairs={{0,1},{1,0},{2,3},{3,2},{4,5},{5,4},{6,7},{7,6},{8,9},{9,8},{10,11... | collective-permute-start | bytes 196616 | tf_op jit(solution)/shard_map/ppermute | solution.py:40
  24.7 7.5 %collective-permute-start.9 = (bf16[2,128,128]{2,1,0:T(8,128)(2,1)S(1)}, bf16[2,128,128]{2,1,0:T(8,128)(2,1)S(1)}, u32[]{:S(2)}, u32[]{:S(2)}) collective-permute-start(bf16[2,128,128]{2,1,0:T(8,128)(2,1)S(1)} %add.2), channel_id=1, source_target_pairs={{0,2},{1,3},{2,0},{3,1},{4,6},{5,7},{6,4},{7,5},{8,10},{9,11},{10,... | collective-permute-start | bytes 196616 | tf_op jit(solution)/shard_map/ppermute | solution.py:40
  26.7 8.0 %collective-permute-start.4 = (bf16[128,128]{1,0:T(8,128)(2,1)S(1)}, bf16[128,128]{1,0:T(8,128)(2,1)S(1)}, u32[]{:S(2)}, u32[]{:S(2)}) collective-permute-start(bf16[128,128]{1,0:T(8,128)(2,1)S(1)} %get-tuple-element.23), channel_id=1, source_target_pairs={{8,16},{16,8},{9,17},{17,9},{10,18},{18,10},{11,19},{19,11},{12,20... | collective-permute-start | bytes 98312 | tf_op jit(solution)/shard_map/ppermute | solution.py:378
  27.4 7.3 %collective-permute-start.3 = (bf16[128,128]{1,0:T(8,128)(2,1)S(1)}, bf16[128,128]{1,0:T(8,128)(2,1)S(1)}, u32[]{:S(2)}, u32[]{:S(2)}) collective-permute-start(bf16[128,128]{1,0:T(8,128)(2,1)S(1)} %get-tuple-element.23), channel_id=1, source_target_pairs={{0,8},{8,0},{16,24},{24,16},{1,9},{9,1},{17,25},{25,17},{2,10},{10... | collective-permute-start | bytes 98312 | tf_op jit(solution)/shard_map/ppermute | solution.py:377
  32.3 5.1 %collective-permute-start.10 = (bf16[1,128,128]{2,1,0:T(8,128)(2,1)S(1)}, bf16[1,128,128]{2,1,0:T(8,128)(2,1)S(1)}, u32[]{:S(2)}, u32[]{:S(2)}) collective-permute-start(bf16[1,128,128]{2,1,0:T(8,128)(2,1)S(1)} %get-tuple-element.29), channel_id=1, source_target_pairs={{0,4},{1,5},{2,6},{3,7},{4,0},{5,1},{6,2},{7,3},{8,12},{9,13},{10,... | collective-permute-start | bytes 98312 | tf_op jit(solution)/shard_map/ppermute | solution.py:40
  37.4 5.0 %collective-permute-start.11 = (bf16[1,128,128]{2,1,0:T(8,128)(2,1)S(1)}, bf16[1,128,128]{2,1,0:T(8,128)(2,1)S(1)}, u32[]{:S(2)}, u32[]{:S(2)}) collective-permute-start(bf16[1,128,128]{2,1,0:T(8,128)(2,1)S(1)} %get-tuple-element.31.refs_1_), channel_id=1, source_target_pairs={{0,4},{1,5},{2,6},{3,7},{4,0},{5,1},{6,2},{7,3},{8,12},{9,13},{10,... | collective-permute-start | bytes 98312 | tf_op jit(solution)/shard_map/ppermute | solution.py:40
  42.4 4.3 %collective-permute-start.12 = (bf16[2,128,128]{2,1,0:T(8,128)(2,1)S(1)}, bf16[2,128,128]{2,1,0:T(8,128)(2,1)S(1)}, u32[]{:S(2)}, u32[]{:S(2)}) collective-permute-start(bf16[2,128,128]{2,1,0:T(8,128)(2,1)S(1)} %join.6.refs_0_.refs_1_), channel_id=1, source_target_pairs={{0,2},{1,3},{2,0},{3,1},{4,6},{5,7},{6,4},{7,5},{8,10},{9,11},{10,... | collective-permute-start | bytes 196616 | tf_op jit(solution)/shard_map/ppermute | solution.py:40
  46.7 1.4 %collective-permute-start.13 = (bf16[4,128,128]{2,1,0:T(8,128)(2,1)S(1)}, bf16[4,128,128]{2,1,0:T(8,128)(2,1)S(1)}, u32[]{:S(2)}, u32[]{:S(2)}) collective-permute-start(bf16[4,128,128]{2,1,0:T(8,128)(2,1)S(1)} %join.7), channel_id=1, source_target_pairs={{0,1},{1,0},{2,3},{3,2},{4,5},{5,4},{6,7},{7,6},{8,9},{9,8},{10,11... | collective-permute-start | bytes 393224 | tf_op jit(solution)/shard_map/ppermute | solution.py:40
  49.1 3.8 %collective-permute-start.16 = (bf16[64,128]{1,0:T(8,128)(2,1)S(1)}, bf16[64,128]{1,0:T(8,128)(2,1)S(1)}, u32[]{:S(2)}, u32[]{:S(2)}) collective-permute-start(bf16[64,128]{1,0:T(8,128)(2,1)S(1)} %split.3.left_ref), channel_id=1, source_target_pairs={{0,8},{8,0},{16,24},{24,16},{1,9},{9,1},{17,25},{25,17},{2,10},{10... | collective-permute-start | bytes 49160 | tf_op jit(solution)/shard_map/ppermute | solution.py:40
  53.0 3.8 %collective-permute-start.17 = (bf16[64,128]{1,0:T(8,128)(2,1)S(1)}, bf16[64,128]{1,0:T(8,128)(2,1)S(1)}, u32[]{:S(2)}, u32[]{:S(2)}) collective-permute-start(bf16[64,128]{1,0:T(8,128)(2,1)S(1)} %merge.3.left_ref), channel_id=1, source_target_pairs={{0,16},{8,24},{16,0},{24,8},{1,17},{9,25},{17,1},{25,9},{2,18},{10... | collective-permute-start | bytes 49160 | tf_op jit(solution)/shard_map/ppermute | solution.py:40
  57.5 1.4 %collective-permute-start.19 = (bf16[2,128,128]{2,1,0:T(8,128)(2,1)S(1)}, bf16[2,128,128]{2,1,0:T(8,128)(2,1)S(1)}, u32[]{:S(2)}, u32[]{:S(2)}) collective-permute-start(bf16[2,128,128]{2,1,0:T(8,128)(2,1)S(1)} %get-tuple-element.37), channel_id=1, source_target_pairs={{0,1},{1,0},{2,3},{3,2},{4,5},{5,4},{6,7},{7,6},{8,9},{9,8},{10,11... | collective-permute-start | bytes 196616 | tf_op jit(solution)/shard_map/ppermute | solution.py:40
  58.4 5.0 %collective-permute-start.18 = (bf16[2,128,128]{2,1,0:T(8,128)(2,1)S(1)}, bf16[2,128,128]{2,1,0:T(8,128)(2,1)S(1)}, u32[]{:S(2)}, u32[]{:S(2)}) collective-permute-start(bf16[2,128,128]{2,1,0:T(8,128)(2,1)S(1)} %get-tuple-element.35), channel_id=1, source_target_pairs={{0,1},{1,0},{2,3},{3,2},{4,5},{5,4},{6,7},{7,6},{8,9},{9,8},{10,11... | collective-permute-start | bytes 196616 | tf_op jit(solution)/shard_map/ppermute | solution.py:40
  59.0 4.5 %collective-permute-start.20 = (bf16[2,128,128]{2,1,0:T(8,128)(2,1)S(1)}, bf16[2,128,128]{2,1,0:T(8,128)(2,1)S(1)}, u32[]{:S(2)}, u32[]{:S(2)}) collective-permute-start(bf16[2,128,128]{2,1,0:T(8,128)(2,1)S(1)} %add.3), channel_id=1, source_target_pairs={{0,2},{1,3},{2,0},{3,1},{4,6},{5,7},{6,4},{7,5},{8,10},{9,11},{10,... | collective-permute-start | bytes 196616 | tf_op jit(solution)/shard_map/ppermute | solution.py:40
  59.5 6.3 %collective-permute-start.15 = (bf16[128,128]{1,0:T(8,128)(2,1)S(1)}, bf16[128,128]{1,0:T(8,128)(2,1)S(1)}, u32[]{:S(2)}, u32[]{:S(2)}) collective-permute-start(bf16[128,128]{1,0:T(8,128)(2,1)S(1)} %get-tuple-element.33), channel_id=1, source_target_pairs={{8,16},{16,8},{9,17},{17,9},{10,18},{18,10},{11,19},{19,11},{12,20... | collective-permute-start | bytes 98312 | tf_op jit(solution)/shard_map/ppermute | solution.py:378
  60.2 5.7 %collective-permute-start.14 = (bf16[128,128]{1,0:T(8,128)(2,1)S(1)}, bf16[128,128]{1,0:T(8,128)(2,1)S(1)}, u32[]{:S(2)}, u32[]{:S(2)}) collective-permute-start(bf16[128,128]{1,0:T(8,128)(2,1)S(1)} %get-tuple-element.33), channel_id=1, source_target_pairs={{0,8},{8,0},{16,24},{24,16},{1,9},{9,1},{17,25},{25,17},{2,10},{10... | collective-permute-start | bytes 98312 | tf_op jit(solution)/shard_map/ppermute | solution.py:377
  63.5 4.9 %collective-permute-start.21 = (bf16[1,128,128]{2,1,0:T(8,128)(2,1)S(1)}, bf16[1,128,128]{2,1,0:T(8,128)(2,1)S(1)}, u32[]{:S(2)}, u32[]{:S(2)}) collective-permute-start(bf16[1,128,128]{2,1,0:T(8,128)(2,1)S(1)} %get-tuple-element.39), channel_id=1, source_target_pairs={{0,4},{1,5},{2,6},{3,7},{4,0},{5,1},{6,2},{7,3},{8,12},{9,13},{10,... | collective-permute-start | bytes 98312 | tf_op jit(solution)/shard_map/ppermute | solution.py:40

commit v3 on v1

--- a/solution.py
+++ b/solution.py
@@ -95,7 +95,7 @@
 
 
 def second_kernel(
-    rows, cols, halve, x_ref, fields_ref, factor_ref, diag_ref, pay_ref, along_ref, total
+    rows, cols, halve, x_ref, fields_ref, factor_ref, diag_ref, pay_ref, part_ref, along_ref, total
 ):
     near = fields_ref.shape[0]
     lines = cols * rows
@@ -121,9 +121,10 @@
         proj = proj + lax.dot_general(pick, lower, dims, preferred_element_type=jnp.float32)
         first = at // LANES * 2 * cols
         upper = proj.astype(jnp.bfloat16)
-        pay_ref[first : first + cols, :] = upper
-        lower = proj - upper.astype(jnp.float32)
-        pay_ref[first + cols : first + 2 * cols, :] = lower.astype(jnp.bfloat16)
+        lower = (proj - upper.astype(jnp.float32)).astype(jnp.bfloat16)
+        for ref in (pay_ref, part_ref):
+            ref[first : first + cols, :] = upper
+            ref[first + cols : first + 2 * cols, :] = lower
 
     head = total.shape[0] // LANES * 2 * cols
     left, right = lax.div(me + 1, 2) - 1, lax.div(me + 1, 2)
@@ -137,18 +138,20 @@
     pay_ref[head:, :] = along.astype(jnp.bfloat16)
 
 
-def product(parity, coef, factor_ref, out_ref):
-    near = out_ref.shape[0]
-    pair = 2 if near % 2 == 0 else 1
-    for z in range(0, near, pair):
-        starts = [pl.multiple_of((2 * (z + n) + parity) * LANES, LANES) for n in range(pair)]
-        right = jnp.concatenate([factor_ref[:, pl.ds(start, LANES)] for start in starts], axis=1)
+def product(coef, masks, other, factor_ref, out_ref):
+    me = lax.axis_index("tile")
+    chip, core = lax.div(me, 2), lax.rem(me, 2)
+    core = 1 - core if other else core
+    starts = [pl.multiple_of((2 * (chip ^ mask) + core) * LANES, LANES) for mask in masks]
+    for n in range(0, len(starts), 2):
+        pair = starts[n : n + 2]
+        right = jnp.concatenate([factor_ref[:, pl.ds(start, LANES)] for start in pair], axis=1)
         term = jnp.dot(coef, right, preferred_element_type=jnp.float32)
-        for n in range(pair):
-            out_ref[z + n] = term[:, n * LANES : (n + 1) * LANES].astype(out_ref.dtype)
-
-
-def far_kernel(rows, cols, groups, ncells, scale_ref, factor_ref, *refs):
+        for m in range(len(pair)):
+            out_ref[n + m] = term[:, m * LANES : (m + 1) * LANES].astype(out_ref.dtype)
+
+
+def far_kernel(rows, cols, groups, ncells, masks, scale_ref, factor_ref, *refs):
     pay_refs, (coef_ref, out_ref) = refs[:groups], refs[groups:]
     ranks = factor_ref.shape[0] // rows
     lines = cols * rows
@@ -184,19 +187,17 @@
             piece = wide[n * cols : (n + 1) * cols, :]
             piece = jnp.broadcast_to(piece[:, None, :], (cols, rows, LANES)).reshape(lines, LANES)
             coef_ref[:, start : start + LANES] = (piece * same).astype(jnp.bfloat16)
-    parity = 1 - lax.rem(lax.axis_index("tile"), 2)
-    product(parity, coef_ref[...], factor_ref, out_ref)
-
-
-def near_kernel(coef_ref, factor_ref, out_ref):
-    product(lax.rem(lax.axis_index("tile"), 2), coef_ref[...], factor_ref, out_ref)
-
-
-def pair_kernel(mine_ref, got_ref, *send_refs):
-    me = lax.div(lax.axis_index("tile"), 2)
-    for mask, ref in enumerate(send_refs):
-        at = me ^ mask
-        ref[...] = (mine_ref[at] + got_ref[at].astype(jnp.float32)).astype(ref.dtype)
+    product(coef_ref[...], masks, True, factor_ref, out_ref)
+
+
+def term_kernel(wanted, after, coef_ref, factor_ref, *refs):
+    for (masks, other, _), out_ref in zip(wanted, refs[after:]):
+        product(coef_ref[...], masks, other, factor_ref, out_ref)
+
+
+def pair_kernel(mine_ref, got_ref, *out_refs):
+    for n, ref in enumerate(out_refs):
+        ref[...] = (mine_ref[n] + got_ref[n].astype(jnp.float32)).astype(ref.dtype)
 
 
 def local_kernel(rows, cols, halve, b_ref, x_ref, amp_ref, along_ref, *refs):
@@ -206,7 +207,8 @@
     me = lax.axis_index("grp")
     low = jnp.zeros((lines, LANES), jnp.float32)
     high = low
-    for mask, ref in enumerate(pay_refs, 1):
+    for n, ref in enumerate(pay_refs, 1):
+        mask = (1 << n) - 1
         part = ref[head:, :].astype(jnp.float32)
         low = jnp.where((me ^ mask) == me - 1, part, low)
         high = jnp.where((me ^ mask) == me + 1, part, high)
@@ -287,39 +289,59 @@
             moved=flat.size,
             name="project_own",
         )(own, held)
-        pay, along = call(
+        pay, part, along = call(
             partial(second_kernel, rows, cols, halve),
-            (shape(bf16, pay_rows, width), shape(f32, lines, width)),
+            (
+                shape(bf16, pay_rows, width),
+                shape(bf16, pay_rows - lines, width),
+                shape(f32, lines, width),
+            ),
             flops=work,
             moved=flat.size,
             scratch_shapes=[pltpu.VMEM((blocks * LANES, lines), f32)],
             name="project_across",
         )(x, across, held, diag)
-        pays = [swap(pay, "grp", mask) for mask in range(1, groups)]
+        pays = [swap(part if mask & (mask + 1) else pay, "grp", mask) for mask in range(1, groups)]
+        half = near // 2
+        close, away = list(range(half)), list(range(near - 1, half - 1, -1))
         coef, far = call(
-            partial(far_kernel, rows, cols, groups, ncells_all),
-            (shape(bf16, lines, ranks * rows), shape(bf16, near, lines, width)),
-            flops=work,
+            partial(far_kernel, rows, cols, groups, ncells_all, away),
+            (shape(bf16, lines, ranks * rows), shape(bf16, half, lines, width)),
+            flops=work // 2,
             moved=flat.size,
-            name="term_across",
-        )(scale, held, pay, *pays)
+            name="term_first",
+        )(scale, held, part, *pays)
         got = swap(far, "tile", 1)
-        mine = call(
-            near_kernel,
-            shape(f32, near, lines, width),
-            flops=work,
-            moved=flat.size,
-            name="term_own",
-        )(coef, held)
-        kept, *sends = call(
-            pair_kernel,
-            [shape(f32 if n == 0 else bf16, lines, width) for n in range(near)],
-            name="pair",
-        )(mine, got)
-        terms = [swap(part, "tile", 2 * mask) for mask, part in enumerate(sends, 1)]
+
+        def term(*wanted, after=()):
+            return call(
+                partial(term_kernel, wanted, len(after)),
+                in_specs=[pl.BlockSpec(memory_space=pltpu.VMEM)] * 2
+                + [pl.BlockSpec(memory_space=pl.ANY)] * len(after),
+                out_shape=[shape(dtype, len(masks), lines, width) for masks, _, dtype in wanted],
+                flops=work // 2 * len(wanted),
+                moved=flat.size,
+                name="term",
+            )(coef, held, *after)
+
+        def pair(mine, got, masks):
+            return call(
+                pair_kernel,
+                [shape(bf16 if mask else f32, lines, width) for mask in masks],
+                name="pair",
+            )(mine, got)
+
+        mine, far = term((away, False, f32), (close, True, bf16))
+        sends = pair(mine, got, away)
+        terms = [swap(send, "tile", 2 * mask) for send, mask in zip(sends, away)]
+        got = swap(far, "tile", 1)
+        (mine,) = term((close, False, f32), after=sends)
+        kept, *sends = pair(mine, got, close)
+        terms += [swap(send, "tile", 2 * mask) for send, mask in zip(sends, close[1:])]
+        rims = [pay for mask, pay in enumerate(pays, 1) if not mask & (mask + 1)]
         base = call(
             partial(local_kernel, rows, cols, halve), shape(f32, lines, width), name="local"
-        )(b, x, amplitude, along, *pays)
+        )(b, x, amplitude, along, *rims)
         last = step == ITERS - 1
         x, residual = call(
             partial(update_kernel, near, halve),

time: 59.3 us -> 56.5 us (0.953)
  waiting for transfers between devices: 19.3 us -> 14.9 us
  starting transfers between devices: 26.3 us -> 27.6 us
    ppermute x22 -> x24, waiting for transfers between devices: 19.3 us -> 14.9 us  [swap(): lax.ppermute(value, axis, [(i, i ^ mask) for i in range(lax.axis_size(axi...]
    ppermute x22 -> x24, starting transfers between devices: 26.3 us -> 27.6 us  [swap(): lax.ppermute(value, axis, [(i, i ^ mask) for i in range(lax.axis_size(axi...]
    pallas_call x6 -> x10, Pallas kernels: 3.67 us -> 4.09 us  [the longest x4 2.58 us: term(): call(partial(term_kernel, wanted, len(after)), in_specs=[pl.BlockSpec(mem...]
  transfers between devices with their start and end apart: 22 -> 24, of which waited for: 18 -> 12; matrix products, arithmetic and copies ran while one was open for 0% -> 0% of each run, Pallas kernels for 7% -> 9%
where the time goes in v3:
time: 56.5 us; the launch traced here: 56.3 us
  starting transfers between devices  27.6 us (49%)
  waiting for transfers between devices  14.9 us (26%)
  Pallas kernels  9.94 us (18%)
  local copies, waits for them, and re-layouts  2.21 us (4%)
  other arithmetic  0.85 us (2%)
  between operations  0.85 us (2%)
    ppermute x24, starting transfers between devices, swap(): lax.ppermute(value, axis, [(i, i ^ mask) for i in range(lax.axis_size(axi...  27.6 us
    ppermute x24, waiting for transfers between devices, swap(): lax.ppermute(value, axis, [(i, i ^ mask) for i in range(lax.axis_size(axi...  14.9 us
    pallas_call x4, Pallas kernels, term(): call(partial(term_kernel, wanted, len(after)), in_specs=[pl.BlockSpec(mem...  2.58 us
    pallas_call x2, Pallas kernels, on_device(): call(partial(second_kernel, rows, cols, halve), (shape(bf16, pay_rows, wi...  2.46 us
    unnamed x8, local copies, waits for them, and re-layouts  2.21 us
    pallas_call x2, Pallas kernels, on_device(): call(partial(first_kernel, rows), shape(f32, blocks * LANES, lines), flop...  1.94 us
    pallas_call x2, Pallas kernels, on_device(): call(partial(far_kernel, rows, cols, groups, ncells_all, away), (shape(bf...  1.45 us
  transfers between devices with their start and end apart: 24, of which 12 were waited for; matrix products, arithmetic and copies ran while one was open for 0% of the time, Pallas kernels for 9%

profile of v3, /device:TPU:0, one launch (start us, length us, event | category | flops | bytes accessed | tf_op | source)
XLA Modules:
  0.0 56.3 jit_solution(14421649361067574706)
XLA Ops:
  0.6 0.8 %multiply_convert_fusion.refs_1_ = bf16[128,128]{1,0:T(8,128)(2,1)S(1)} fusion(f32[16,8,128]{2,1,0:T(8,128)} %param.4), kind=kLoop, calls=%fused_computation | loop fusion | flops 32768 | bytes 98304 | tf_op jit(solution)/shard_map/convert_element_type | solution.py:250
  1.5 5.0 %collective-permute-start.2 = (bf16[128,128]{1,0:T(8,128)(2,1)S(1)}, bf16[128,128]{1,0:T(8,128)(2,1)S(1)}, u32[]{:S(2)}, u32[]{:S(2)}) collective-permute-start(bf16[128,128]{1,0:T(8,128)(2,1)S(1)} %multiply_convert_fusion.refs_1_), channel_id=1, source_target_pairs={{0,6},{1,7},{2,4},{3,5},{4,2},{5,3},{6,0},{7,1},{8,14},{9,15},{10,... | collective-permute-start | bytes 98312 | tf_op jit(solution)/shard_map/ppermute | solution.py:40
  6.5 0.0 collective-permute-start.1
  6.5 0.6 %collective-permute-start = (bf16[128,128]{1,0:T(8,128)(2,1)S(1)}, bf16[128,128]{1,0:T(8,128)(2,1)S(1)}, u32[]{:S(2)}, u32[]{:S(2)}) collective-permute-start(bf16[128,128]{1,0:T(8,128)(2,1)S(1)} %multiply_convert_fusion.refs_1_), channel_id=1, source_target_pairs={{0,2},{1,3},{2,0},{3,1},{4,6},{5,7},{6,4},{7,5},{8,10},{9,11},{10,... | collective-permute-start | bytes 98312 | tf_op jit(solution)/shard_map/ppermute | solution.py:40
  7.2 2.2 %copy-done = bf16[256,8,1024]{2,1,0:T(8,128)(2,1)S(1)} copy-done((bf16[256,8,1024]{2,1,0:T(8,128)(2,1)S(1)}, bf16[256,8,1024]{2,1,0:T(8,128)(2,1)}, u32[]{:S(2)}) %copy-start) | copy-done | bytes 4194328
  9.3 0.4 load.1.refs_0_.factor_ref
  9.7 0.0 copy-start.1
  9.7 0.0 collective-permute-done.2.refs_4_
  9.7 1.6 %collective-permute-done.1.refs_3_ = bf16[128,128]{1,0:T(8,128)(2,1)S(1)} collective-permute-done((bf16[128,128]{1,0:T(8,128)(2,1)S(1)}, bf16[128,128]{1,0:T(8,128)(2,1)S(1)}, u32[]{:S(2)}, u32[]{:S(2)}) %collective-permute-start.1) | collective-permute-done | bytes 32800 | tf_op jit(solution)/shard_map/ppermute | solution.py:40
  11.3 0.0 collective-permute-done.refs_2_
  11.4 0.0 copy-start.3
  11.4 0.1 collective-permute-start.3
  11.5 1.0 %project_own.2.diag_ref = f32[256,128]{1,0:T(8,128)S(1)} custom-call(bf16[4,128,128]{2,1,0:T(8,128)(2,1)S(1)} %order.2.fields_ref, bf16[2048,1024]{1,0:T(8,128)(2,1)S(1)} %load.1.refs_0_.factor_ref), custom_call_target="tpu_custom_call" | custom-call | flops 268435456 | bytes 2097152 | tf_op jit(solution)/shard_map/project_own/pallas_call | solution.py:285
  12.4 0.4 collective-permute-done.3.fields_ref
  12.8 1.2 %project_across.2 = (bf16[192,128]{1,0:T(8,128)(2,1)S(1)}, bf16[64,128]{1,0:T(8,128)(2,1)S(1)}, f32[128,128]{1,0:T(8,128)S(1)}) custom-call(f32[128,128]{1,0:T(8,128)S(1)} %bitcast.7, bf16[4,128,128]{2,1,0:T(8,128)(2,1)S(1)} %collective-permute-done.3.fields_ref, bf16[2048,1024]{1,0:T(8,128)(2,1)S(1)} %load.1.refs_0_.factor_ref, ...), custom_call_target="tpu_custom_call" | custom-call | flops 268435456 | bytes 2097152 | tf_op jit(solution)/shard_map/project_across/pallas_call | solution.py:292
  14.0 2.5 %collective-permute-start.5 = (bf16[192,128]{1,0:T(8,128)(2,1)S(1)}, bf16[192,128]{1,0:T(8,128)(2,1)S(1)}, u32[]{:S(2)}, u32[]{:S(2)}) collective-permute-start(bf16[192,128]{1,0:T(8,128)(2,1)S(1)} %get-tuple-element.29), channel_id=1, source_target_pairs={{0,24},{8,16},{16,8},{24,0},{1,25},{9,17},{17,9},{25,1},{2,26},{10... | collective-permute-start | bytes 147464 | tf_op jit(solution)/shard_map/ppermute | solution.py:40
  16.5 0.5 collective-permute-start.4
  17.0 0.5 collective-permute-start.6
  17.5 3.2 %collective-permute-done.6.refs_2_ = bf16[64,128]{1,0:T(8,128)(2,1)S(1)} collective-permute-done((bf16[64,128]{1,0:T(8,128)(2,1)S(1)}, bf16[64,128]{1,0:T(8,128)(2,1)S(1)}, u32[]{:S(2)}, u32[]{:S(2)}) %collective-permute-start.6) | collective-permute-done | bytes 16416 | tf_op jit(solution)/shard_map/ppermute | solution.py:40
  20.8 0.0 collective-permute-done.5.refs_1_.refs_3_
  20.8 0.0 collective-permute-done.4.refs_0_.refs_1_
  20.8 0.7 %term_first.2 = (bf16[128,2048]{1,0:T(8,128)(2,1)S(1)}, bf16[2,128,128]{2,1,0:T(8,128)(2,1)S(1)}) custom-call(f32[1,256]{1,0:T(1,128)S(1)} %bitcast.12, bf16[2048,1024]{1,0:T(8,128)(2,1)S(1)} %load.1.refs_0_.factor_ref, bf16[64,128]{1,0:T(8,128)(2,1)S(1)} %get-tuple-element.30.refs_0_, bf16[192,128]{1,0:T(8,128)(2,1)S(1)} %collective-permute-done.4.refs_0_.refs_1_, ...), custom_call_target="tpu_custom_call" | custom-call | flops 134217728 | bytes 2097152 | tf_op jit(solution)/shard_map/term_first/pallas_call | solution.py:307
  21.5 0.1 collective-permute-start.7
  21.6 0.0 copy-start.2
  21.6 0.8 %term.4 = (f32[2,128,128]{2,1,0:T(8,128)S(1)}, bf16[2,128,128]{2,1,0:T(8,128)(2,1)S(1)}) custom-call(bf16[128,2048]{1,0:T(8,128)(2,1)S(1)} %get-tuple-element.31.coef_ref, bf16[2048,1024]{1,0:T(8,128)(2,1)S(1)} %load.1.refs_0_.factor_ref), custom_call_target="tpu_custom_call" | custom-call | flops 268435456 | bytes 2097152 | tf_op jit(solution)/shard_map/term/pallas_call | solution.py:317
  22.4 0.5 collective-permute-start.8
  23.0 0.0 collective-permute-done.7.got_ref
  23.0 2.3 %collective-permute-start.9 = (bf16[128,128]{1,0:T(8,128)(2,1)S(1)}, bf16[128,128]{1,0:T(8,128)(2,1)S(1)}, u32[]{:S(2)}, u32[]{:S(2)}) collective-permute-start(bf16[128,128]{1,0:T(8,128)(2,1)S(1)} %get-tuple-element.34.refs_0_), channel_id=1, source_target_pairs={{0,6},{1,7},{2,4},{3,5},{4,2},{5,3},{6,0},{7,1},{8,14},{9,15},{10,... | collective-permute-start | bytes 98312 | tf_op jit(solution)/shard_map/ppermute | solution.py:40
  25.2 0.0 collective-permute-start.10
  25.2 0.5 term.5.mine_ref
  25.7 0.0 collective-permute-done.8.got_ref
  25.8 2.3 %collective-permute-start.11 = (bf16[128,128]{1,0:T(8,128)(2,1)S(1)}, bf16[128,128]{1,0:T(8,128)(2,1)S(1)}, u32[]{:S(2)}, u32[]{:S(2)}) collective-permute-start(bf16[128,128]{1,0:T(8,128)(2,1)S(1)} %get-tuple-element.38), channel_id=1, source_target_pairs={{0,2},{1,3},{2,0},{3,1},{4,6},{5,7},{6,4},{7,5},{8,10},{9,11},{10,... | collective-permute-start | bytes 98312 | tf_op jit(solution)/shard_map/ppermute | solution.py:40
  28.0 0.2 local.2.base_ref
  28.2 0.9 %collective-permute-done.9.refs_1_ = bf16[128,128]{1,0:T(8,128)(2,1)S(1)} collective-permute-done((bf16[128,128]{1,0:T(8,128)(2,1)S(1)}, bf16[128,128]{1,0:T(8,128)(2,1)S(1)}, u32[]{:S(2)}, u32[]{:S(2)}) %collective-permute-start.9) | collective-permute-done | bytes 32800 | tf_op jit(solution)/shard_map/ppermute | solution.py:40
  29.1 1.2 %collective-permute-done.10.refs_2_ = bf16[128,128]{1,0:T(8,128)(2,1)S(1)} collective-permute-done((bf16[128,128]{1,0:T(8,128)(2,1)S(1)}, bf16[128,128]{1,0:T(8,128)(2,1)S(1)}, u32[]{:S(2)}, u32[]{:S(2)}) %collective-permute-start.10) | collective-permute-done | bytes 32800 | tf_op jit(solution)/shard_map/ppermute | solution.py:40
  30.3 0.0 collective-permute-done.11.refs_3_
  30.3 2.3 %collective-permute-start.14 = (bf16[128,128]{1,0:T(8,128)(2,1)S(1)}, bf16[128,128]{1,0:T(8,128)(2,1)S(1)}, u32[]{:S(2)}, u32[]{:S(2)}) collective-permute-start(bf16[128,128]{1,0:T(8,128)(2,1)S(1)} %get-tuple-element.40.refs_1_), channel_id=1, source_target_pairs={{0,6},{1,7},{2,4},{3,5},{4,2},{5,3},{6,0},{7,1},{8,14},{9,15},{10,... | collective-permute-start | bytes 98312 | tf_op jit(solution)/shard_map/ppermute | solution.py:40
  32.6 0.9 %collective-permute-start.13 = (bf16[128,128]{1,0:T(8,128)(2,1)S(1)}, bf16[128,128]{1,0:T(8,128)(2,1)S(1)}, u32[]{:S(2)}, u32[]{:S(2)}) collective-permute-start(bf16[128,128]{1,0:T(8,128)(2,1)S(1)} %get-tuple-element.40.refs_1_), channel_id=1, source_target_pairs={{0,4},{1,5},{2,6},{3,7},{4,0},{5,1},{6,2},{7,3},{8,12},{9,13},{10,... | collective-permute-start | bytes 98312 | tf_op jit(solution)/shard_map/ppermute | solution.py:40
  33.5 1.3 %collective-permute-start.12 = (bf16[128,128]{1,0:T(8,128)(2,1)S(1)}, bf16[128,128]{1,0:T(8,128)(2,1)S(1)}, u32[]{:S(2)}, u32[]{:S(2)}) collective-permute-start(bf16[128,128]{1,0:T(8,128)(2,1)S(1)} %get-tuple-element.40.refs_1_), channel_id=1, source_target_pairs={{0,2},{1,3},{2,0},{3,1},{4,6},{5,7},{6,4},{7,5},{8,10},{9,11},{10,... | collective-permute-start | bytes 98312 | tf_op jit(solution)/shard_map/ppermute | solution.py:40
  34.8 1.3 %collective-permute-done.14.refs_4_ = bf16[128,128]{1,0:T(8,128)(2,1)S(1)} collective-permute-done((bf16[128,128]{1,0:T(8,128)(2,1)S(1)}, bf16[128,128]{1,0:T(8,128)(2,1)S(1)}, u32[]{:S(2)}, u32[]{:S(2)}) %collective-permute-start.14) | collective-permute-done | bytes 32800 | tf_op jit(solution)/shard_map/ppermute | solution.py:40
  36.1 1.7 %collective-permute-done.13.refs_3_ = bf16[128,128]{1,0:T(8,128)(2,1)S(1)} collective-permute-done((bf16[128,128]{1,0:T(8,128)(2,1)S(1)}, bf16[128,128]{1,0:T(8,128)(2,1)S(1)}, u32[]{:S(2)}, u32[]{:S(2)}) %collective-permute-start.13) | collective-permute-done | bytes 32800 | tf_op jit(solution)/shard_map/ppermute | solution.py:40
  37.8 0.1 collective-permute-start.15
  37.9 1.0 %project_own.3.diag_ref = f32[256,128]{1,0:T(8,128)S(1)} custom-call(bf16[4,128,128]{2,1,0:T(8,128)(2,1)S(1)} %order.3.fields_ref, bf16[2048,1024]{1,0:T(8,128)(2,1)S(1)} %load.1.refs_0_.factor_ref), custom_call_target="tpu_custom_call" | custom-call | flops 268435456 | bytes 2097152 | tf_op jit(solution)/shard_map/project_own/pallas_call | solution.py:285
  38.9 0.4 collective-permute-done.15.fields_ref
  39.2 1.2 %project_across.3 = (bf16[192,128]{1,0:T(8,128)(2,1)S(1)}, bf16[64,128]{1,0:T(8,128)(2,1)S(1)}, f32[128,128]{1,0:T(8,128)S(1)}) custom-call(f32[128,128]{1,0:T(8,128)S(1)} %get-tuple-element.39.x_ref, bf16[4,128,128]{2,1,0:T(8,128)(2,1)S(1)} %collective-permute-done.15.fields_ref, bf16[2048,1024]{1,0:T(8,128)(2,1)S(1)} %load.1.refs_0_.factor_ref, ...), custom_call_target="tpu_custom_call" | custom-call | flops 268435456 | bytes 2097152 | tf_op jit(solution)/shard_map/project_across/pallas_call | solution.py:292
  40.5 1.5 %collective-permute-start.17 = (bf16[192,128]{1,0:T(8,128)(2,1)S(1)}, bf16[192,128]{1,0:T(8,128)(2,1)S(1)}, u32[]{:S(2)}, u32[]{:S(2)}) collective-permute-start(bf16[192,128]{1,0:T(8,128)(2,1)S(1)} %get-tuple-element.42), channel_id=1, source_target_pairs={{0,24},{8,16},{16,8},{24,0},{1,25},{9,17},{17,9},{25,1},{2,26},{10... | collective-permute-start | bytes 147464 | tf_op jit(solution)/shard_map/ppermute | solution.py:40
  41.9 0.5 collective-permute-start.16
  42.4 1.5 %collective-permute-start.18 = (bf16[64,128]{1,0:T(8,128)(2,1)S(1)}, bf16[64,128]{1,0:T(8,128)(2,1)S(1)}, u32[]{:S(2)}, u32[]{:S(2)}) collective-permute-start(bf16[64,128]{1,0:T(8,128)(2,1)S(1)} %get-tuple-element.43.refs_0_), channel_id=1, source_target_pairs={{0,16},{8,24},{16,0},{24,8},{1,17},{9,25},{17,1},{25,9},{2,18},{10... | collective-permute-start | bytes 49160 | tf_op jit(solution)/shard_map/ppermute | solution.py:40
  44.0 2.2 %collective-permute-done.18.refs_2_ = bf16[64,128]{1,0:T(8,128)(2,1)S(1)} collective-permute-done((bf16[64,128]{1,0:T(8,128)(2,1)S(1)}, bf16[64,128]{1,0:T(8,128)(2,1)S(1)}, u32[]{:S(2)}, u32[]{:S(2)}) %collective-permute-start.18) | collective-permute-done | bytes 16416 | tf_op jit(solution)/shard_map/ppermute | solution.py:40
  46.2 0.7 %term_first.3 = (bf16[128,2048]{1,0:T(8,128)(2,1)S(1)}, bf16[2,128,128]{2,1,0:T(8,128)(2,1)S(1)}) custom-call(f32[1,256]{1,0:T(1,128)S(1)} %bitcast.13, bf16[2048,1024]{1,0:T(8,128)(2,1)S(1)} %load.1.refs_0_.factor_ref, bf16[64,128]{1,0:T(8,128)(2,1)S(1)} %get-tuple-element.43.refs_0_, bf16[192,128]{1,0:T(8,128)(2,1)S(1)} %collective-permute-done.16.refs_0_.refs_1_, ...), custom_call_target="tpu_custom_call" | custom-call | flops 134217728 | bytes 2097152 | tf_op jit(solution)/shard_map/term_first/pallas_call | solution.py:307
  46.9 0.1 collective-permute-start.19
  47.0 0.8 %term.6 = (f32[2,128,128]{2,1,0:T(8,128)S(1)}, bf16[2,128,128]{2,1,0:T(8,128)(2,1)S(1)}) custom-call(bf16[128,2048]{1,0:T(8,128)(2,1)S(1)} %get-tuple-element.44.coef_ref, bf16[2048,1024]{1,0:T(8,128)(2,1)S(1)} %load.1.refs_0_.factor_ref), custom_call_target="tpu_custom_call" | custom-call | flops 268435456 | bytes 2097152 | tf_op jit(solution)/shard_map/term/pallas_call | solution.py:317
  47.8 0.6 collective-permute-start.20
  48.3 0.0 collective-permute-done.19.got_ref
  48.4 2.0 %collective-permute-start.21 = (bf16[128,128]{1,0:T(8,128)(2,1)S(1)}, bf16[128,128]{1,0:T(8,128)(2,1)S(1)}, u32[]{:S(2)}, u32[]{:S(2)}) collective-permute-start(bf16[128,128]{1,0:T(8,128)(2,1)S(1)} %get-tuple-element.47.refs_0_), channel_id=1, source_target_pairs={{0,6},{1,7},{2,4},{3,5},{4,2},{5,3},{6,0},{7,1},{8,14},{9,15},{10,... | collective-permute-start | bytes 98312 | tf_op jit(solution)/shard_map/ppermute | solution.py:40
  50.3 0.5 collective-permute-start.22
  50.8 0.5 term.7.mine_ref
  51.3 0.0 collective-permute-done.20.got_ref
  51.3 2.1 %collective-permute-start.23 = (bf16[128,128]{1,0:T(8,128)(2,1)S(1)}, bf16[128,128]{1,0:T(8,128)(2,1)S(1)}, u32[]{:S(2)}, u32[]{:S(2)}) collective-permute-start(bf16[128,128]{1,0:T(8,128)(2,1)S(1)} %get-tuple-element.51), channel_id=1, source_target_pairs={{0,2},{1,3},{2,0},{3,1},{4,6},{5,7},{6,4},{7,5},{8,10},{9,11},{10,... | collective-permute-start | bytes 98312 | tf_op jit(solution)/shard_map/ppermute | solution.py:40
  53.4 0.2 local.3.base_ref
  53.6 0.6 %collective-permute-done.21.refs_1_ = bf16[128,128]{1,0:T(8,128)(2,1)S(1)} collective-permute-done((bf16[128,128]{1,0:T(8,128)(2,1)S(1)}, bf16[128,128]{1,0:T(8,128)(2,1)S(1)}, u32[]{:S(2)}, u32[]{:S(2)}) %collective-permute-start.21) | collective-permute-done | bytes 32800 | tf_op jit(solution)/shard_map/ppermute | solution.py:40
  54.2 1.1 %collective-permute-done.22.refs_2_ = bf16[128,128]{1,0:T(8,128)(2,1)S(1)} collective-permute-done((bf16[128,128]{1,0:T(8,128)(2,1)S(1)}, bf16[128,128]{1,0:T(8,128)(2,1)S(1)}, u32[]{:S(2)}, u32[]{:S(2)}) %collective-permute-start.22) | collective-permute-done | bytes 32800 | tf_op jit(solution)/shard_map/ppermute | solution.py:40
  55.3 0.3 collective-permute-done.23.refs_3_
  55.6 0.7 %update.3 = (f32[128,128]{1,0:T(8,128)}, f32[128,128]{1,0:T(8,128)}) custom-call(f32[128,128]{1,0:T(8,128)S(1)} %get-tuple-element.39.x_ref, f32[128,128]{1,0:T(8,128)S(1)} %local.3.base_ref, f32[128,128]{1,0:T(8,128)S(1)} %get-tuple-element.50.refs_0_, bf16[128,128]{1,0:T(8,128)(2,1)S(1)} %collective-permute-done.21.refs_1_, ...), custom_call_target="tpu_custom_call" | custom-call | bytes 262144 | tf_op jit(solution)/shard_map/update/pallas_call | solution.py:346
  (14 shorter events, 0.1 us)
Async XLA Ops:
  1.5 8.3 %collective-permute-start.2 = (bf16[128,128]{1,0:T(8,128)(2,1)S(1)}, bf16[128,128]{1,0:T(8,128)(2,1)S(1)}, u32[]{:S(2)}, u32[]{:S(2)}) collective-permute-start(bf16[128,128]{1,0:T(8,128)(2,1)S(1)} %multiply_convert_fusion.refs_1_), channel_id=1, source_target_pairs={{0,6},{1,7},{2,4},{3,5},{4,2},{5,3},{6,0},{7,1},{8,14},{9,15},{10,... | collective-permute-start | bytes 98312 | tf_op jit(solution)/shard_map/ppermute | solution.py:40
  6.5 4.8 %collective-permute-start.1 = (bf16[128,128]{1,0:T(8,128)(2,1)S(1)}, bf16[128,128]{1,0:T(8,128)(2,1)S(1)}, u32[]{:S(2)}, u32[]{:S(2)}) collective-permute-start(bf16[128,128]{1,0:T(8,128)(2,1)S(1)} %multiply_convert_fusion.refs_1_), channel_id=1, source_target_pairs={{0,4},{1,5},{2,6},{3,7},{4,0},{5,1},{6,2},{7,3},{8,12},{9,13},{10,... | collective-permute-start | bytes 98312 | tf_op jit(solution)/shard_map/ppermute | solution.py:40
  6.5 4.8 %collective-permute-start = (bf16[128,128]{1,0:T(8,128)(2,1)S(1)}, bf16[128,128]{1,0:T(8,128)(2,1)S(1)}, u32[]{:S(2)}, u32[]{:S(2)}) collective-permute-start(bf16[128,128]{1,0:T(8,128)(2,1)S(1)} %multiply_convert_fusion.refs_1_), channel_id=1, source_target_pairs={{0,2},{1,3},{2,0},{3,1},{4,6},{5,7},{6,4},{7,5},{8,10},{9,11},{10,... | collective-permute-start | bytes 98312 | tf_op jit(solution)/shard_map/ppermute | solution.py:40
  7.2 2.2 %copy-start = (bf16[256,8,1024]{2,1,0:T(8,128)(2,1)S(1)}, bf16[256,8,1024]{2,1,0:T(8,128)(2,1)}, u32[]{:S(2)}) copy-start(bf16[256,8,1024]{2,1,0:T(8,128)(2,1)} %param.6) | copy-start | bytes 12582916
  9.7 3.1 %copy-start.1 = (f32[16,8,128]{2,1,0:T(8,128)S(1)}, f32[16,8,128]{2,1,0:T(8,128)}, u32[]{:S(2)}) copy-start(f32[16,8,128]{2,1,0:T(8,128)} %param.4) | copy-start | bytes 196612
  11.4 9.4 %copy-start.3 = (f32[256]{0:T(256)S(1)}, f32[256]{0:T(256)}, u32[]{:S(2)}) copy-start(f32[256]{0:T(256)} %param.7) | copy-start | bytes 3076
  11.4 1.4 %collective-permute-start.3 = (bf16[4,128,128]{2,1,0:T(8,128)(2,1)S(1)}, bf16[4,128,128]{2,1,0:T(8,128)(2,1)S(1)}, u32[]{:S(2)}, u32[]{:S(2)}) collective-permute-start(bf16[4,128,128]{2,1,0:T(8,128)(2,1)S(1)} %order.2.fields_ref), channel_id=1, source_target_pairs={{0,1},{1,0},{2,3},{3,2},{4,5},{5,4},{6,7},{7,6},{8,9},{9,8},{10,11... | collective-permute-start | bytes 393224 | tf_op jit(solution)/shard_map/ppermute | solution.py:40
  14.0 6.8 %collective-permute-start.5 = (bf16[192,128]{1,0:T(8,128)(2,1)S(1)}, bf16[192,128]{1,0:T(8,128)(2,1)S(1)}, u32[]{:S(2)}, u32[]{:S(2)}) collective-permute-start(bf16[192,128]{1,0:T(8,128)(2,1)S(1)} %get-tuple-element.29), channel_id=1, source_target_pairs={{0,24},{8,16},{16,8},{24,0},{1,25},{9,17},{17,9},{25,1},{2,26},{10... | collective-permute-start | bytes 147464 | tf_op jit(solution)/shard_map/ppermute | solution.py:40
  16.5 4.3 %collective-permute-start.4 = (bf16[192,128]{1,0:T(8,128)(2,1)S(1)}, bf16[192,128]{1,0:T(8,128)(2,1)S(1)}, u32[]{:S(2)}, u32[]{:S(2)}) collective-permute-start(bf16[192,128]{1,0:T(8,128)(2,1)S(1)} %get-tuple-element.29), channel_id=1, source_target_pairs={{0,8},{8,0},{16,24},{24,16},{1,9},{9,1},{17,25},{25,17},{2,10},{10... | collective-permute-start | bytes 147464 | tf_op jit(solution)/shard_map/ppermute | solution.py:40
  17.0 3.7 %collective-permute-start.6 = (bf16[64,128]{1,0:T(8,128)(2,1)S(1)}, bf16[64,128]{1,0:T(8,128)(2,1)S(1)}, u32[]{:S(2)}, u32[]{:S(2)}) collective-permute-start(bf16[64,128]{1,0:T(8,128)(2,1)S(1)} %get-tuple-element.30.refs_0_), channel_id=1, source_target_pairs={{0,16},{8,24},{16,0},{24,8},{1,17},{9,25},{17,1},{25,9},{2,18},{10... | collective-permute-start | bytes 49160 | tf_op jit(solution)/shard_map/ppermute | solution.py:40
  21.5 1.4 %collective-permute-start.7 = (bf16[2,128,128]{2,1,0:T(8,128)(2,1)S(1)}, bf16[2,128,128]{2,1,0:T(8,128)(2,1)S(1)}, u32[]{:S(2)}, u32[]{:S(2)}) collective-permute-start(bf16[2,128,128]{2,1,0:T(8,128)(2,1)S(1)} %get-tuple-element.33), channel_id=1, source_target_pairs={{0,1},{1,0},{2,3},{3,2},{4,5},{5,4},{6,7},{7,6},{8,9},{9,8},{10,11... | collective-permute-start | bytes 196616 | tf_op jit(solution)/shard_map/ppermute | solution.py:40
  21.6 6.4 %copy-start.2 = (f32[8,128]{1,0:T(8,128)S(1)}, f32[8,128]{1,0:T(8,128)}, u32[]{:S(2)}) copy-start(f32[8,128]{1,0:T(8,128)} %amp_ref.3) | copy-start | bytes 12292
  22.4 3.3 %collective-permute-start.8 = (bf16[2,128,128]{2,1,0:T(8,128)(2,1)S(1)}, bf16[2,128,128]{2,1,0:T(8,128)(2,1)S(1)}, u32[]{:S(2)}, u32[]{:S(2)}) collective-permute-start(bf16[2,128,128]{2,1,0:T(8,128)(2,1)S(1)} %get-tuple-element.36), channel_id=1, source_target_pairs={{0,1},{1,0},{2,3},{3,2},{4,5},{5,4},{6,7},{7,6},{8,9},{9,8},{10,11... | collective-permute-start | bytes 196616 | tf_op jit(solution)/shard_map/ppermute | solution.py:40
  23.0 6.1 %collective-permute-start.9 = (bf16[128,128]{1,0:T(8,128)(2,1)S(1)}, bf16[128,128]{1,0:T(8,128)(2,1)S(1)}, u32[]{:S(2)}, u32[]{:S(2)}) collective-permute-start(bf16[128,128]{1,0:T(8,128)(2,1)S(1)} %get-tuple-element.34.refs_0_), channel_id=1, source_target_pairs={{0,6},{1,7},{2,4},{3,5},{4,2},{5,3},{6,0},{7,1},{8,14},{9,15},{10,... | collective-permute-start | bytes 98312 | tf_op jit(solution)/shard_map/ppermute | solution.py:40
  25.2 5.0 %collective-permute-start.10 = (bf16[128,128]{1,0:T(8,128)(2,1)S(1)}, bf16[128,128]{1,0:T(8,128)(2,1)S(1)}, u32[]{:S(2)}, u32[]{:S(2)}) collective-permute-start(bf16[128,128]{1,0:T(8,128)(2,1)S(1)} %get-tuple-element.35.refs_1_), channel_id=1, source_target_pairs={{0,4},{1,5},{2,6},{3,7},{4,0},{5,1},{6,2},{7,3},{8,12},{9,13},{10,... | collective-permute-start | bytes 98312 | tf_op jit(solution)/shard_map/ppermute | solution.py:40
  25.8 4.5 %collective-permute-start.11 = (bf16[128,128]{1,0:T(8,128)(2,1)S(1)}, bf16[128,128]{1,0:T(8,128)(2,1)S(1)}, u32[]{:S(2)}, u32[]{:S(2)}) collective-permute-start(bf16[128,128]{1,0:T(8,128)(2,1)S(1)} %get-tuple-element.38), channel_id=1, source_target_pairs={{0,2},{1,3},{2,0},{3,1},{4,6},{5,7},{6,4},{7,5},{8,10},{9,11},{10,... | collective-permute-start | bytes 98312 | tf_op jit(solution)/shard_map/ppermute | solution.py:40
  30.3 5.8 %collective-permute-start.14 = (bf16[128,128]{1,0:T(8,128)(2,1)S(1)}, bf16[128,128]{1,0:T(8,128)(2,1)S(1)}, u32[]{:S(2)}, u32[]{:S(2)}) collective-permute-start(bf16[128,128]{1,0:T(8,128)(2,1)S(1)} %get-tuple-element.40.refs_1_), channel_id=1, source_target_pairs={{0,6},{1,7},{2,4},{3,5},{4,2},{5,3},{6,0},{7,1},{8,14},{9,15},{10,... | collective-permute-start | bytes 98312 | tf_op jit(solution)/shard_map/ppermute | solution.py:40
  32.6 5.2 %collective-permute-start.13 = (bf16[128,128]{1,0:T(8,128)(2,1)S(1)}, bf16[128,128]{1,0:T(8,128)(2,1)S(1)}, u32[]{:S(2)}, u32[]{:S(2)}) collective-permute-start(bf16[128,128]{1,0:T(8,128)(2,1)S(1)} %get-tuple-element.40.refs_1_), channel_id=1, source_target_pairs={{0,4},{1,5},{2,6},{3,7},{4,0},{5,1},{6,2},{7,3},{8,12},{9,13},{10,... | collective-permute-start | bytes 98312 | tf_op jit(solution)/shard_map/ppermute | solution.py:40
  33.5 4.3 %collective-permute-start.12 = (bf16[128,128]{1,0:T(8,128)(2,1)S(1)}, bf16[128,128]{1,0:T(8,128)(2,1)S(1)}, u32[]{:S(2)}, u32[]{:S(2)}) collective-permute-start(bf16[128,128]{1,0:T(8,128)(2,1)S(1)} %get-tuple-element.40.refs_1_), channel_id=1, source_target_pairs={{0,2},{1,3},{2,0},{3,1},{4,6},{5,7},{6,4},{7,5},{8,10},{9,11},{10,... | collective-permute-start | bytes 98312 | tf_op jit(solution)/shard_map/ppermute | solution.py:40
  37.8 1.4 %collective-permute-start.15 = (bf16[4,128,128]{2,1,0:T(8,128)(2,1)S(1)}, bf16[4,128,128]{2,1,0:T(8,128)(2,1)S(1)}, u32[]{:S(2)}, u32[]{:S(2)}) collective-permute-start(bf16[4,128,128]{2,1,0:T(8,128)(2,1)S(1)} %order.3.fields_ref), channel_id=1, source_target_pairs={{0,1},{1,0},{2,3},{3,2},{4,5},{5,4},{6,7},{7,6},{8,9},{9,8},{10,11... | collective-permute-start | bytes 393224 | tf_op jit(solution)/shard_map/ppermute | solution.py:40
  40.5 5.7 %collective-permute-start.17 = (bf16[192,128]{1,0:T(8,128)(2,1)S(1)}, bf16[192,128]{1,0:T(8,128)(2,1)S(1)}, u32[]{:S(2)}, u32[]{:S(2)}) collective-permute-start(bf16[192,128]{1,0:T(8,128)(2,1)S(1)} %get-tuple-element.42), channel_id=1, source_target_pairs={{0,24},{8,16},{16,8},{24,0},{1,25},{9,17},{17,9},{25,1},{2,26},{10... | collective-permute-start | bytes 147464 | tf_op jit(solution)/shard_map/ppermute | solution.py:40
  41.9 4.3 %collective-permute-start.16 = (bf16[192,128]{1,0:T(8,128)(2,1)S(1)}, bf16[192,128]{1,0:T(8,128)(2,1)S(1)}, u32[]{:S(2)}, u32[]{:S(2)}) collective-permute-start(bf16[192,128]{1,0:T(8,128)(2,1)S(1)} %get-tuple-element.42), channel_id=1, source_target_pairs={{0,8},{8,0},{16,24},{24,16},{1,9},{9,1},{17,25},{25,17},{2,10},{10... | collective-permute-start | bytes 147464 | tf_op jit(solution)/shard_map/ppermute | solution.py:40
  42.4 3.7 %collective-permute-start.18 = (bf16[64,128]{1,0:T(8,128)(2,1)S(1)}, bf16[64,128]{1,0:T(8,128)(2,1)S(1)}, u32[]{:S(2)}, u32[]{:S(2)}) collective-permute-start(bf16[64,128]{1,0:T(8,128)(2,1)S(1)} %get-tuple-element.43.refs_0_), channel_id=1, source_target_pairs={{0,16},{8,24},{16,0},{24,8},{1,17},{9,25},{17,1},{25,9},{2,18},{10... | collective-permute-start | bytes 49160 | tf_op jit(solution)/shard_map/ppermute | solution.py:40
  46.9 1.4 %collective-permute-start.19 = (bf16[2,128,128]{2,1,0:T(8,128)(2,1)S(1)}, bf16[2,128,128]{2,1,0:T(8,128)(2,1)S(1)}, u32[]{:S(2)}, u32[]{:S(2)}) collective-permute-start(bf16[2,128,128]{2,1,0:T(8,128)(2,1)S(1)} %get-tuple-element.46), channel_id=1, source_target_pairs={{0,1},{1,0},{2,3},{3,2},{4,5},{5,4},{6,7},{7,6},{8,9},{9,8},{10,11... | collective-permute-start | bytes 196616 | tf_op jit(solution)/shard_map/ppermute | solution.py:40
  47.8 3.5 %collective-permute-start.20 = (bf16[2,128,128]{2,1,0:T(8,128)(2,1)S(1)}, bf16[2,128,128]{2,1,0:T(8,128)(2,1)S(1)}, u32[]{:S(2)}, u32[]{:S(2)}) collective-permute-start(bf16[2,128,128]{2,1,0:T(8,128)(2,1)S(1)} %get-tuple-element.49), channel_id=1, source_target_pairs={{0,1},{1,0},{2,3},{3,2},{4,5},{5,4},{6,7},{7,6},{8,9},{9,8},{10,11... | collective-permute-start | bytes 196616 | tf_op jit(solution)/shard_map/ppermute | solution.py:40
  48.4 5.8 %collective-permute-start.21 = (bf16[128,128]{1,0:T(8,128)(2,1)S(1)}, bf16[128,128]{1,0:T(8,128)(2,1)S(1)}, u32[]{:S(2)}, u32[]{:S(2)}) collective-permute-start(bf16[128,128]{1,0:T(8,128)(2,1)S(1)} %get-tuple-element.47.refs_0_), channel_id=1, source_target_pairs={{0,6},{1,7},{2,4},{3,5},{4,2},{5,3},{6,0},{7,1},{8,14},{9,15},{10,... | collective-permute-start | bytes 98312 | tf_op jit(solution)/shard_map/ppermute | solution.py:40
  50.3 5.0 %collective-permute-start.22 = (bf16[128,128]{1,0:T(8,128)(2,1)S(1)}, bf16[128,128]{1,0:T(8,128)(2,1)S(1)}, u32[]{:S(2)}, u32[]{:S(2)}) collective-permute-start(bf16[128,128]{1,0:T(8,128)(2,1)S(1)} %get-tuple-element.48.refs_1_), channel_id=1, source_target_pairs={{0,4},{1,5},{2,6},{3,7},{4,0},{5,1},{6,2},{7,3},{8,12},{9,13},{10,... | collective-permute-start | bytes 98312 | tf_op jit(solution)/shard_map/ppermute | solution.py:40
  51.3 4.3 %collective-permute-start.23 = (bf16[128,128]{1,0:T(8,128)(2,1)S(1)}, bf16[128,128]{1,0:T(8,128)(2,1)S(1)}, u32[]{:S(2)}, u32[]{:S(2)}) collective-permute-start(bf16[128,128]{1,0:T(8,128)(2,1)S(1)} %get-tuple-element.51), channel_id=1, source_target_pairs={{0,2},{1,3},{2,0},{3,1},{4,6},{5,7},{6,4},{7,5},{8,10},{9,11},{10,... | collective-permute-start | bytes 98312 | tf_op jit(solution)/shard_map/ppermute | solution.py:40

commit v4 on v3

--- a/solution.py
+++ b/solution.py
@@ -40,11 +40,34 @@
     return lax.ppermute(value, axis, [(i, i ^ mask) for i in range(lax.axis_size(axis))])
 
 
-def gather_kernel(*refs):
+def place_of(spot):
+    even, odd, which = spot
+    me = lax.axis_index("tile")
+    chip, core = lax.div(me, 2), lax.rem(me, 2)
+    chip = chip ^ jnp.where(core == 0, even, odd)
+    if which == "own":
+        which = core
+    elif which == "other":
+        which = 1 - core
+    return 2 * chip + which
+
+
+def columns_of(spots):
+    return [pl.multiple_of(place_of(spot) * LANES, LANES) for spot in spots]
+
+
+def duo_kernel(short_ref, twin_ref, out_ref):
+    core = lax.rem(lax.axis_index("tile"), 2)
+    out_ref[core] = short_ref[0]
+    out_ref[1 - core] = twin_ref[0]
+
+
+def join_kernel(*refs):
     part_refs, out_ref = refs[1:-1], refs[-1]
-    me = lax.div(lax.axis_index("tile"), 2)
-    for mask, ref in enumerate(part_refs):
-        out_ref[me ^ mask] = ref[...]
+    at = 0
+    for ref in part_refs:
+        out_ref[at : at + ref.shape[0]] = ref[...]
+        at += ref.shape[0]
 
 
 def load_kernel(source_ref, out_ref, sems):
@@ -62,15 +85,15 @@
         copy.wait()
 
 
-def diagonal(rows, parity, fields_ref, factor_ref, store):
-    near, lines, _ = fields_ref.shape
+def diagonal(rows, spots, fields, factor_ref, store):
+    lines = fields[0].shape[0]
     count = factor_ref.shape[0]
-    field = jnp.concatenate([fields_ref[z] for z in range(near)], axis=1)
+    field = jnp.concatenate(fields, axis=1)
     step = min(256, count)
     row_of = lax.broadcasted_iota(jnp.int32, (rows, lines), 0)
     lane_of = lax.broadcasted_iota(jnp.int32, (rows, lines), 1)
     same = (lax.rem(lane_of, rows) == row_of).astype(jnp.float32)
-    starts = [pl.multiple_of((2 * z + parity) * LANES, LANES) for z in range(near)]
+    starts = columns_of(spots)
     for at in range(0, count, step):
         left = jnp.concatenate(
             [factor_ref[at : at + step, pl.ds(start, LANES)] for start in starts], axis=1
@@ -82,32 +105,33 @@
         store(at // rows, (at + step) // rows, jnp.sum(part, axis=1))
 
 
-def first_kernel(rows, fields_ref, factor_ref, diag_ref):
-    parity = lax.rem(lax.axis_index("tile"), 2)
+def blocks_of(refs):
+    return [ref[n] for ref in refs for n in range(ref.shape[0])]
+
+
+def first_kernel(rows, spots, added, factor_ref, *refs):
+    diag_ref = refs[-1]
+    field_refs = refs[: len(refs) - 1 - added]
     ranks = factor_ref.shape[0] // rows
     if diag_ref.shape[0] > ranks:
         diag_ref[...] = jnp.zeros_like(diag_ref)
 
     def store(start, end, value):
-        diag_ref[start:end, :] = value
-
-    diagonal(rows, parity, fields_ref, factor_ref, store)
-
-
-def second_kernel(
-    rows, cols, halve, x_ref, fields_ref, factor_ref, diag_ref, pay_ref, part_ref, along_ref, total
-):
-    near = fields_ref.shape[0]
+        diag_ref[start:end, :] = refs[-2][start:end, :] + value if added else value
+
+    diagonal(rows, spots, blocks_of(field_refs), factor_ref, store)
+
+
+def second_kernel(rows, cols, halve, spots, known, x_ref, factor_ref, diag_ref, fields_ref, *refs):
+    other_refs, (pay_ref, part_ref, along_ref, total) = refs[:-4], refs[-4:]
     lines = cols * rows
-    me = lax.axis_index("tile")
-    parity = lax.rem(me, 2)
     if total.shape[0] > factor_ref.shape[0] // rows:
         total[...] = jnp.zeros_like(total)
 
     def store(start, end, value):
         total[start:end, :] = diag_ref[start:end, :] + value
 
-    diagonal(rows, 1 - parity, fields_ref, factor_ref, store)
+    diagonal(rows, spots, blocks_of([fields_ref]), factor_ref, store)
     pick = (
         lax.broadcasted_iota(jnp.int32, (cols, lines), 1) // rows
         == lax.broadcasted_iota(jnp.int32, (cols, lines), 0)
@@ -127,22 +151,21 @@
             ref[first + cols : first + 2 * cols, :] = lower
 
     head = total.shape[0] // LANES * 2 * cols
-    left, right = lax.div(me + 1, 2) - 1, lax.div(me + 1, 2)
-    low = fields_ref[jnp.maximum(left, 0)].astype(jnp.float32)
-    low = jnp.where(left >= 0, low, 0.0)
-    high = fields_ref[jnp.minimum(right, near - 1)].astype(jnp.float32)
-    high = jnp.where(right < near, high, 0.0)
+    me = lax.axis_index("tile")
+    low = jnp.zeros((lines, LANES), jnp.float32)
+    high = low
+    for spot, block in zip(spots + known, blocks_of((fields_ref,) + other_refs)):
+        part, place = block.astype(jnp.float32), place_of(spot)
+        low = jnp.where(place == me - 1, part, low)
+        high = jnp.where(place == me + 1, part, high)
     own = 0.5 * x_ref[...] if halve else x_ref[...]
     along = stencil(low, own, high, COL_TAPS, 1)
     along_ref[...] = along
     pay_ref[head:, :] = along.astype(jnp.bfloat16)
 
 
-def product(coef, masks, other, factor_ref, out_ref):
-    me = lax.axis_index("tile")
-    chip, core = lax.div(me, 2), lax.rem(me, 2)
-    core = 1 - core if other else core
-    starts = [pl.multiple_of((2 * (chip ^ mask) + core) * LANES, LANES) for mask in masks]
+def product(coef, spots, factor_ref, out_ref):
+    starts = columns_of(spots)
     for n in range(0, len(starts), 2):
         pair = starts[n : n + 2]
         right = jnp.concatenate([factor_ref[:, pl.ds(start, LANES)] for start in pair], axis=1)
@@ -151,7 +174,7 @@
             out_ref[n + m] = term[:, m * LANES : (m + 1) * LANES].astype(out_ref.dtype)
 
 
-def far_kernel(rows, cols, groups, ncells, masks, scale_ref, factor_ref, *refs):
+def far_kernel(rows, cols, groups, ncells, spots, scale_ref, factor_ref, *refs):
     pay_refs, (coef_ref, out_ref) = refs[:groups], refs[groups:]
     ranks = factor_ref.shape[0] // rows
     lines = cols * rows
@@ -187,17 +210,29 @@
             piece = wide[n * cols : (n + 1) * cols, :]
             piece = jnp.broadcast_to(piece[:, None, :], (cols, rows, LANES)).reshape(lines, LANES)
             coef_ref[:, start : start + LANES] = (piece * same).astype(jnp.bfloat16)
-    product(coef_ref[...], masks, True, factor_ref, out_ref)
+    product(coef_ref[...], spots, factor_ref, out_ref)
 
 
 def term_kernel(wanted, after, coef_ref, factor_ref, *refs):
-    for (masks, other, _), out_ref in zip(wanted, refs[after:]):
-        product(coef_ref[...], masks, other, factor_ref, out_ref)
+    for (spots, _), out_ref in zip(wanted, refs[after:]):
+        product(coef_ref[...], spots, factor_ref, out_ref)
 
 
 def pair_kernel(mine_ref, got_ref, *out_refs):
-    for n, ref in enumerate(out_refs):
-        ref[...] = (mine_ref[n] + got_ref[n].astype(jnp.float32)).astype(ref.dtype)
+    at = 0
+    for ref in out_refs:
+        end = at + ref.shape[0]
+        ref[...] = (mine_ref[at:end] + got_ref[at:end].astype(jnp.float32)).astype(ref.dtype)
+        at = end
+
+
+def give_kernel(*refs):
+    part_refs, out_ref = refs[:-1], refs[-1]
+    other = 1 - lax.rem(lax.axis_index("tile"), 2)
+    total = part_refs[0][other].astype(jnp.float32)
+    for ref in part_refs[1:]:
+        total = total + ref[other].astype(jnp.float32)
+    out_ref[...] = total.astype(out_ref.dtype)
 
 
 def local_kernel(rows, cols, halve, b_ref, x_ref, amp_ref, along_ref, *refs):
@@ -221,17 +256,20 @@
     base_ref[...] = b_ref[...] - (x + scaled)
 
 
-def update_kernel(near, halve, x_ref, base_ref, *refs):
-    term_refs, out_refs = refs[:near], refs[near:]
-    rank_sum = term_refs[0][...]
-    for ref in term_refs[1:]:
-        rank_sum = rank_sum + ref[...].astype(jnp.float32)
+def update_kernel(halve, last, x_ref, base_ref, kept_ref, one_ref, given_ref, *refs):
+    part_refs, (new_ref, other_ref) = refs[:-2], refs[-2:]
+    core = lax.rem(lax.axis_index("tile"), 2)
+    rank_sum = kept_ref[0] + one_ref[0].astype(jnp.float32) + given_ref[...].astype(jnp.float32)
+    for ref in part_refs:
+        rank_sum = rank_sum + ref[core].astype(jnp.float32)
     x = 0.5 * x_ref[...] if halve else x_ref[...]
     residual = base_ref[...] - rank_sum
     new = x + 0.5 * residual
-    out_refs[0][...] = new
-    if len(out_refs) > 1:
-        out_refs[1][...] = residual if out_refs[1].dtype == jnp.float32 else new.astype(jnp.bfloat16)
+    new_ref[...] = new
+    if last:
+        other_ref[...] = residual
+    else:
+        other_ref[0] = new.astype(jnp.bfloat16)
 
 
 def on_device(right_side, amplitude, factor, scale):
@@ -247,7 +285,7 @@
     b = right_side.reshape(lines, width)
     scale = scale.reshape(1, ranks)
     x = b
-    short = (0.5 * b).astype(jnp.bfloat16)
+    short = (0.5 * b).astype(jnp.bfloat16)[None]
     pay_rows = blocks * 2 * cols + lines
 
     f32, bf16 = jnp.float32, jnp.bfloat16
@@ -274,23 +312,47 @@
         scratch_shapes=[pltpu.SemaphoreType.DMA((8,))],
         name="load",
     )(flat)
-    for step in range(ITERS):
-        halve = step == 0
-        parts = [swap(short, "tile", 2 * mask) for mask in range(1, near)]
-        whole = [pl.BlockSpec(memory_space=pl.ANY)] + [pl.BlockSpec(memory_space=pltpu.VMEM)] * near
-        own = call(
-            gather_kernel, shape(bf16, near, lines, width), in_specs=whole, name="order"
-        )(held, short, *parts)
-        across = swap(own, "tile", 1)
-        diag = call(
-            partial(first_kernel, rows),
+    rounds = [
+        [(2 * (chip ^ (2 * n + 1 - core)) + core) for chip in range(near) for core in range(2)]
+        for n in range(near // 2 - 1, 0, -1)
+    ]
+    own_away = [(2 * n + 1, 2 * n, q) for n in range(near // 2 - 1, 0, -1) for q in range(2)]
+    other_away = [(2 * n, 2 * n + 1, q) for n in range(near // 2 - 1, 0, -1) for q in range(2)]
+    home = [(0, 0, 0), (0, 0, 1)]
+    own_close = [(0, 0, "own"), (1, 1, "own")]
+    other_close = [(0, 0, "other"), (1, 1, "other")]
+
+    def travel(value, targets):
+        return lax.ppermute(value, "tile", list(enumerate(targets)))
+
+    def first(fields, spots, *before):
+        return call(
+            partial(first_kernel, rows, spots, len(before)),
             shape(f32, blocks * LANES, lines),
             flops=work,
             moved=flat.size,
             name="project_own",
-        )(own, held)
+        )(held, *fields, *before)
+
+    for step in range(ITERS):
+        halve = step == 0
+        twin = swap(short, "tile", 1)
+        one = swap(short, "tile", 2)
+        duo = call(duo_kernel, shape(bf16, 2, lines, width), name="duo")(short, twin)
+        gots = [travel(duo, targets) for targets in rounds]
+        diag = first([duo], home)
+        bundle = call(
+            join_kernel,
+            shape(bf16, near - 1, lines, width),
+            in_specs=[pl.BlockSpec(memory_space=pl.ANY)]
+            + [pl.BlockSpec(memory_space=pltpu.VMEM)] * (len(gots) + 1),
+            name="join",
+        )(diag, *gots, one)
+        across = swap(bundle, "tile", 1)
+        diag = first([bundle], own_away + own_close[1:], diag)
+        spots = other_away + other_close[1:]
         pay, part, along = call(
-            partial(second_kernel, rows, cols, halve),
+            partial(second_kernel, rows, cols, halve, spots, home + own_away + own_close[1:]),
             (
                 shape(bf16, pay_rows, width),
                 shape(bf16, pay_rows - lines, width),
@@ -300,13 +362,11 @@
             moved=flat.size,
             scratch_shapes=[pltpu.VMEM((blocks * LANES, lines), f32)],
             name="project_across",
-        )(x, across, held, diag)
+        )(x, held, diag, across, duo, bundle)
         pays = [swap(part if mask & (mask + 1) else pay, "grp", mask) for mask in range(1, groups)]
-        half = near // 2
-        close, away = list(range(half)), list(range(near - 1, half - 1, -1))
         coef, far = call(
-            partial(far_kernel, rows, cols, groups, ncells_all, away),
-            (shape(bf16, lines, ranks * rows), shape(bf16, half, lines, width)),
+            partial(far_kernel, rows, cols, groups, ncells_all, other_away),
+            (shape(bf16, lines, ranks * rows), shape(bf16, near - 2, lines, width)),
             flops=work // 2,
             moved=flat.size,
             name="term_first",
@@ -318,38 +378,40 @@
                 partial(term_kernel, wanted, len(after)),
                 in_specs=[pl.BlockSpec(memory_space=pltpu.VMEM)] * 2
                 + [pl.BlockSpec(memory_space=pl.ANY)] * len(after),
-                out_shape=[shape(dtype, len(masks), lines, width) for masks, _, dtype in wanted],
+                out_shape=[shape(dtype, len(spots), lines, width) for spots, dtype in wanted],
                 flops=work // 2 * len(wanted),
                 moved=flat.size,
                 name="term",
             )(coef, held, *after)
 
-        def pair(mine, got, masks):
-            return call(
-                pair_kernel,
-                [shape(bf16 if mask else f32, lines, width) for mask in masks],
-                name="pair",
-            )(mine, got)
-
-        mine, far = term((away, False, f32), (close, True, bf16))
-        sends = pair(mine, got, away)
-        terms = [swap(send, "tile", 2 * mask) for send, mask in zip(sends, away)]
+        mine, far = term((own_away, f32), (other_close, bf16))
+        sends = call(
+            pair_kernel, [shape(bf16, 2, lines, width) for _ in rounds], name="pair"
+        )(mine, got)
+        terms = [travel(send, targets) for send, targets in zip(sends, rounds)]
         got = swap(far, "tile", 1)
-        (mine,) = term((close, False, f32), after=sends)
-        kept, *sends = pair(mine, got, close)
-        terms += [swap(send, "tile", 2 * mask) for send, mask in zip(sends, close[1:])]
+        (mine,) = term((own_close, f32), after=sends)
+        kept, send = call(
+            pair_kernel,
+            [shape(f32, 1, lines, width), shape(bf16, 1, lines, width)],
+            name="pair",
+        )(mine, got)
+        close = swap(send, "tile", 2)
+        given = swap(call(give_kernel, shape(bf16, lines, width), name="give")(*terms), "tile", 1)
         rims = [pay for mask, pay in enumerate(pays, 1) if not mask & (mask + 1)]
         base = call(
             partial(local_kernel, rows, cols, halve), shape(f32, lines, width), name="local"
         )(b, x, amplitude, along, *rims)
         last = step == ITERS - 1
-        x, residual = call(
-            partial(update_kernel, near, halve),
-            (shape(f32, lines, width), shape(f32 if last else bf16, lines, width)),
+        x, short = call(
+            partial(update_kernel, halve, last),
+            (
+                shape(f32, lines, width),
+                shape(f32, lines, width) if last else shape(bf16, 1, lines, width),
+            ),
             name="update",
-        )(x, base, kept, *terms)
-        short = residual
-    return x.reshape(cols, rows, width), residual.reshape(cols, rows, width)
+        )(x, base, kept, close, given, *terms)
+    return x.reshape(cols, rows, width), short.reshape(cols, rows, width)
 
 
 def solution(mesh):

time: 56.5 us -> 57.5 us (1.018)
  waiting for transfers between devices: 14.9 us -> 22.1 us
  starting transfers between devices: 27.6 us -> 21 us
    ppermute x24 -> x20, starting transfers between devices: 27.6 us -> 9.24 us  [swap(): lax.ppermute(value, axis, [(i, i ^ mask) for i in range(lax.axis_size(axi...]
    ppermute x0 -> x4, starting transfers between devices: none -> 11.7 us  [travel(): return lax.ppermute(value, 'tile', list(enumerate(targets)))]
    ppermute x0 -> x4, waiting for transfers between devices: none -> 7.28 us  [travel(): return lax.ppermute(value, 'tile', list(enumerate(targets)))]
    pallas_call x14 -> x20, Pallas kernels: 6.65 us -> 6.93 us  [the longest x4 2.53 us: first(): call(partial(first_kernel, rows, spots, len(before)), shape(f32, blocks *...]
    ppermute x24 -> x20, waiting for transfers between devices: 14.9 us -> 14.9 us  [swap(): lax.ppermute(value, axis, [(i, i ^ mask) for i in range(lax.axis_size(axi...]
  transfers between devices with their start and end apart: 24 -> 24, of which waited for: 12 -> 14; matrix products, arithmetic and copies ran while one was open for 0% -> 0% of each run, Pallas kernels for 9% -> 10%
where the time goes in v4:
time: 57.5 us; the launch traced here: 57.3 us
  waiting for transfers between devices  22.1 us (38%)
  starting transfers between devices  21 us (37%)
  Pallas kernels  10.2 us (18%)
  local copies, waits for them, and re-layouts  2.21 us (4%)
  between operations  0.89 us (2%)
  other arithmetic  0.85 us (1%)
    ppermute x20, waiting for transfers between devices, swap(): lax.ppermute(value, axis, [(i, i ^ mask) for i in range(lax.axis_size(axi...  14.9 us
    ppermute x4, starting transfers between devices, travel(): return lax.ppermute(value, 'tile', list(enumerate(targets)))  11.7 us
    ppermute x20, starting transfers between devices, swap(): lax.ppermute(value, axis, [(i, i ^ mask) for i in range(lax.axis_size(axi...  9.24 us
    ppermute x4, waiting for transfers between devices, travel(): return lax.ppermute(value, 'tile', list(enumerate(targets)))  7.28 us
    pallas_call x4, Pallas kernels, term(): call(partial(term_kernel, wanted, len(after)), in_specs=[pl.BlockSpec(mem...  2.57 us
    pallas_call x4, Pallas kernels, first(): call(partial(first_kernel, rows, spots, len(before)), shape(f32, blocks *...  2.53 us
    unnamed x8, local copies, waits for them, and re-layouts  2.21 us
    pallas_call x2, Pallas kernels, on_device(): call(partial(second_kernel, rows, cols, halve, spots, home + own_away + o...  2.13 us
  transfers between devices with their start and end apart: 24, of which 14 were waited for; matrix products, arithmetic and copies ran while one was open for 0% of the time, Pallas kernels for 10%

profile of v4, /device:TPU:0, one launch (start us, length us, event | category | flops | bytes accessed | tf_op | source)
XLA Modules:
  0.0 57.3 jit_solution(17999032516405798486)
XLA Ops:
  0.6 0.8 %fusion.short_ref = bf16[1,128,128]{2,1,0:T(8,128)(2,1)S(1)} fusion(f32[16,8,128]{2,1,0:T(8,128)} %param.4), kind=kLoop, calls=%fused_computation.1 | loop fusion | flops 32768 | bytes 98304 | tf_op jit(solution)/shard_map/convert_element_type | solution.py:288
  1.5 0.5 collective-permute-start
  1.9 0.9 %collective-permute-done.twin_ref = bf16[1,128,128]{2,1,0:T(8,128)(2,1)S(1)} collective-permute-done((bf16[1,128,128]{2,1,0:T(8,128)(2,1)S(1)}, bf16[1,128,128]{2,1,0:T(8,128)(2,1)S(1)}, u32[]{:S(2)}, u32[]{:S(2)}) %collective-permute-start) | collective-permute-done | bytes 32800 | tf_op jit(solution)/shard_map/ppermute | solution.py:40
  2.8 5.0 %collective-permute-start.1 = (bf16[2,128,128]{2,1,0:T(8,128)(2,1)S(1)}, bf16[2,128,128]{2,1,0:T(8,128)(2,1)S(1)}, u32[]{:S(2)}, u32[]{:S(2)}) collective-permute-start(bf16[2,128,128]{2,1,0:T(8,128)(2,1)S(1)} %duo.2.refs_0_), channel_id=1, source_target_pairs={{0,6},{1,5},{2,4},{3,7},{4,2},{5,1},{6,0},{7,3},{8,14},{9,13},{10,... | collective-permute-start | bytes 196616 | tf_op jit(solution)/shard_map/ppermute | solution.py:326
  7.8 0.0 collective-permute-start.2
  7.8 2.2 %copy-done = bf16[256,8,1024]{2,1,0:T(8,128)(2,1)S(1)} copy-done((bf16[256,8,1024]{2,1,0:T(8,128)(2,1)S(1)}, bf16[256,8,1024]{2,1,0:T(8,128)(2,1)}, u32[]{:S(2)}) %copy-start) | copy-done | bytes 4194328
  10.0 0.4 load.1.factor_ref
  10.4 0.0 copy-start.1
  10.4 0.5 project_own.4.refs_0_.refs_1_
  10.9 0.8 %collective-permute-done.2.refs_2_ = bf16[1,128,128]{2,1,0:T(8,128)(2,1)S(1)} collective-permute-done((bf16[1,128,128]{2,1,0:T(8,128)(2,1)S(1)}, bf16[1,128,128]{2,1,0:T(8,128)(2,1)S(1)}, u32[]{:S(2)}, u32[]{:S(2)}) %collective-permute-start.2) | collective-permute-done | bytes 32800 | tf_op jit(solution)/shard_map/ppermute | solution.py:40
  11.7 0.0 collective-permute-done.1.refs_1_
  11.7 0.0 copy-start.3
  11.8 0.1 collective-permute-start.3
  11.8 0.7 %project_own.5.diag_ref = f32[256,128]{1,0:T(8,128)S(1)} custom-call(bf16[2048,1024]{1,0:T(8,128)(2,1)S(1)} %load.1.factor_ref, bf16[3,128,128]{2,1,0:T(8,128)(2,1)S(1)} %join.2.refs_0_.refs_1_, f32[256,128]{1,0:T(8,128)S(1)} %project_own.4.refs_0_.refs_1_), custom_call_target="tpu_custom_call" | custom-call | flops 268435456 | bytes 2097152 | tf_op jit(solution)/shard_map/project_own/pallas_call | solution.py:329
  12.6 0.6 collective-permute-done.3.fields_ref
  13.1 1.1 %project_across.2 = (bf16[192,128]{1,0:T(8,128)(2,1)S(1)}, bf16[64,128]{1,0:T(8,128)(2,1)S(1)}, f32[128,128]{1,0:T(8,128)S(1)}) custom-call(f32[128,128]{1,0:T(8,128)S(1)} %bitcast.8, bf16[2048,1024]{1,0:T(8,128)(2,1)S(1)} %load.1.factor_ref, f32[256,128]{1,0:T(8,128)S(1)} %project_own.5.diag_ref, ...), custom_call_target="tpu_custom_call" | custom-call | flops 268435456 | bytes 2097152 | tf_op jit(solution)/shard_map/project_across/pallas_call | solution.py:354
  14.2 2.5 %collective-permute-start.5 = (bf16[192,128]{1,0:T(8,128)(2,1)S(1)}, bf16[192,128]{1,0:T(8,128)(2,1)S(1)}, u32[]{:S(2)}, u32[]{:S(2)}) collective-permute-start(bf16[192,128]{1,0:T(8,128)(2,1)S(1)} %get-tuple-element.25), channel_id=1, source_target_pairs={{0,24},{8,16},{16,8},{24,0},{1,25},{9,17},{17,9},{25,1},{2,26},{10... | collective-permute-start | bytes 147464 | tf_op jit(solution)/shard_map/ppermute | solution.py:40
  16.7 0.5 collective-permute-start.4
  17.2 0.5 collective-permute-start.6
  17.7 3.2 %collective-permute-done.6.refs_2_ = bf16[64,128]{1,0:T(8,128)(2,1)S(1)} collective-permute-done((bf16[64,128]{1,0:T(8,128)(2,1)S(1)}, bf16[64,128]{1,0:T(8,128)(2,1)S(1)}, u32[]{:S(2)}, u32[]{:S(2)}) %collective-permute-start.6) | collective-permute-done | bytes 16416 | tf_op jit(solution)/shard_map/ppermute | solution.py:40
  20.9 0.0 collective-permute-done.5.refs_1_.refs_3_
  20.9 0.0 collective-permute-done.4.refs_0_.refs_1_
  21.0 0.7 %term_first.2 = (bf16[128,2048]{1,0:T(8,128)(2,1)S(1)}, bf16[2,128,128]{2,1,0:T(8,128)(2,1)S(1)}) custom-call(f32[1,256]{1,0:T(1,128)S(1)} %bitcast.13, bf16[2048,1024]{1,0:T(8,128)(2,1)S(1)} %load.1.factor_ref, bf16[64,128]{1,0:T(8,128)(2,1)S(1)} %get-tuple-element.26.refs_0_, bf16[192,128]{1,0:T(8,128)(2,1)S(1)} %collective-permute-done.4.refs_0_.refs_1_, ...), custom_call_target="tpu_custom_call" | custom-call | flops 134217728 | bytes 2097152 | tf_op jit(solution)/shard_map/term_first/pallas_call | solution.py:367
  21.7 0.1 collective-permute-start.7
  21.8 0.0 copy-start.2
  21.8 0.8 %term.4 = (f32[2,128,128]{2,1,0:T(8,128)S(1)}, bf16[2,128,128]{2,1,0:T(8,128)(2,1)S(1)}) custom-call(bf16[128,2048]{1,0:T(8,128)(2,1)S(1)} %get-tuple-element.27.coef_ref, bf16[2048,1024]{1,0:T(8,128)(2,1)S(1)} %load.1.factor_ref), custom_call_target="tpu_custom_call" | custom-call | flops 268435456 | bytes 2097152 | tf_op jit(solution)/shard_map/term/pallas_call | solution.py:377
  22.6 0.5 collective-permute-start.8
  23.2 2.3 %collective-permute-start.10 = (bf16[2,128,128]{2,1,0:T(8,128)(2,1)S(1)}, bf16[2,128,128]{2,1,0:T(8,128)(2,1)S(1)}, u32[]{:S(2)}, u32[]{:S(2)}) collective-permute-start(bf16[2,128,128]{2,1,0:T(8,128)(2,1)S(1)} %pair.4.refs_0_), channel_id=1, source_target_pairs={{0,6},{1,5},{2,4},{3,7},{4,2},{5,1},{6,0},{7,3},{8,14},{9,13},{10,... | collective-permute-start | bytes 196616 | tf_op jit(solution)/shard_map/ppermute | solution.py:326
  25.4 0.5 term.5.mine_ref
  26.0 0.1 collective-permute-start.9
  26.1 3.5 %collective-permute-done.10.refs_0_ = bf16[2,128,128]{2,1,0:T(8,128)(2,1)S(1)} collective-permute-done((bf16[2,128,128]{2,1,0:T(8,128)(2,1)S(1)}, bf16[2,128,128]{2,1,0:T(8,128)(2,1)S(1)}, u32[]{:S(2)}, u32[]{:S(2)}) %collective-permute-start.10) | collective-permute-done | bytes 65568 | tf_op jit(solution)/shard_map/ppermute | solution.py:326
  29.6 0.2 local.2.base_ref
  29.8 0.2 collective-permute-done.9.one_ref
  30.0 0.8 %collective-permute-done.11.given_ref = bf16[128,128]{1,0:T(8,128)(2,1)S(1)} collective-permute-done((bf16[128,128]{1,0:T(8,128)(2,1)S(1)}, bf16[128,128]{1,0:T(8,128)(2,1)S(1)}, u32[]{:S(2)}, u32[]{:S(2)}) %collective-permute-start.11) | collective-permute-done | bytes 32800 | tf_op jit(solution)/shard_map/ppermute | solution.py:40
  30.8 0.2 collective-permute-start.12
  31.1 1.0 %collective-permute-done.12.twin_ref = bf16[1,128,128]{2,1,0:T(8,128)(2,1)S(1)} collective-permute-done((bf16[1,128,128]{2,1,0:T(8,128)(2,1)S(1)}, bf16[1,128,128]{2,1,0:T(8,128)(2,1)S(1)}, u32[]{:S(2)}, u32[]{:S(2)}) %collective-permute-start.12) | collective-permute-done | bytes 32800 | tf_op jit(solution)/shard_map/ppermute | solution.py:40
  32.1 2.4 %collective-permute-start.13 = (bf16[2,128,128]{2,1,0:T(8,128)(2,1)S(1)}, bf16[2,128,128]{2,1,0:T(8,128)(2,1)S(1)}, u32[]{:S(2)}, u32[]{:S(2)}) collective-permute-start(bf16[2,128,128]{2,1,0:T(8,128)(2,1)S(1)} %duo.3.refs_0_), channel_id=1, source_target_pairs={{0,6},{1,5},{2,4},{3,7},{4,2},{5,1},{6,0},{7,3},{8,14},{9,13},{10,... | collective-permute-start | bytes 196616 | tf_op jit(solution)/shard_map/ppermute | solution.py:326
  34.5 0.0 collective-permute-start.14
  34.5 0.5 project_own.6.refs_0_.refs_1_
  35.0 3.6 %collective-permute-done.14.refs_2_ = bf16[1,128,128]{2,1,0:T(8,128)(2,1)S(1)} collective-permute-done((bf16[1,128,128]{2,1,0:T(8,128)(2,1)S(1)}, bf16[1,128,128]{2,1,0:T(8,128)(2,1)S(1)}, u32[]{:S(2)}, u32[]{:S(2)}) %collective-permute-start.14) | collective-permute-done | bytes 32800 | tf_op jit(solution)/shard_map/ppermute | solution.py:40
  38.6 0.1 collective-permute-start.15
  38.7 0.7 %project_own.7.diag_ref = f32[256,128]{1,0:T(8,128)S(1)} custom-call(bf16[2048,1024]{1,0:T(8,128)(2,1)S(1)} %load.1.factor_ref, bf16[3,128,128]{2,1,0:T(8,128)(2,1)S(1)} %join.3.refs_0_.refs_1_, f32[256,128]{1,0:T(8,128)S(1)} %project_own.6.refs_0_.refs_1_), custom_call_target="tpu_custom_call" | custom-call | flops 268435456 | bytes 2097152 | tf_op jit(solution)/shard_map/project_own/pallas_call | solution.py:329
  39.4 0.6 collective-permute-done.15.fields_ref
  40.0 1.1 %project_across.3 = (bf16[192,128]{1,0:T(8,128)(2,1)S(1)}, bf16[64,128]{1,0:T(8,128)(2,1)S(1)}, f32[128,128]{1,0:T(8,128)S(1)}) custom-call(f32[128,128]{1,0:T(8,128)S(1)} %get-tuple-element.33.x_ref, bf16[2048,1024]{1,0:T(8,128)(2,1)S(1)} %load.1.factor_ref, f32[256,128]{1,0:T(8,128)S(1)} %project_own.7.diag_ref, ...), custom_call_target="tpu_custom_call" | custom-call | flops 268435456 | bytes 2097152 | tf_op jit(solution)/shard_map/project_across/pallas_call | solution.py:354
  41.0 1.5 %collective-permute-start.17 = (bf16[192,128]{1,0:T(8,128)(2,1)S(1)}, bf16[192,128]{1,0:T(8,128)(2,1)S(1)}, u32[]{:S(2)}, u32[]{:S(2)}) collective-permute-start(bf16[192,128]{1,0:T(8,128)(2,1)S(1)} %get-tuple-element.36), channel_id=1, source_target_pairs={{0,24},{8,16},{16,8},{24,0},{1,25},{9,17},{17,9},{25,1},{2,26},{10... | collective-permute-start | bytes 147464 | tf_op jit(solution)/shard_map/ppermute | solution.py:40
  42.5 0.5 collective-permute-start.16
  43.0 1.5 %collective-permute-start.18 = (bf16[64,128]{1,0:T(8,128)(2,1)S(1)}, bf16[64,128]{1,0:T(8,128)(2,1)S(1)}, u32[]{:S(2)}, u32[]{:S(2)}) collective-permute-start(bf16[64,128]{1,0:T(8,128)(2,1)S(1)} %get-tuple-element.37.refs_0_), channel_id=1, source_target_pairs={{0,16},{8,24},{16,0},{24,8},{1,17},{9,25},{17,1},{25,9},{2,18},{10... | collective-permute-start | bytes 49160 | tf_op jit(solution)/shard_map/ppermute | solution.py:40
  44.5 2.2 %collective-permute-done.18.refs_2_ = bf16[64,128]{1,0:T(8,128)(2,1)S(1)} collective-permute-done((bf16[64,128]{1,0:T(8,128)(2,1)S(1)}, bf16[64,128]{1,0:T(8,128)(2,1)S(1)}, u32[]{:S(2)}, u32[]{:S(2)}) %collective-permute-start.18) | collective-permute-done | bytes 16416 | tf_op jit(solution)/shard_map/ppermute | solution.py:40
  46.8 0.0 collective-permute-done.17.refs_1_.refs_3_
  46.8 0.0 collective-permute-done.16.refs_0_.refs_1_
  46.8 0.7 %term_first.3 = (bf16[128,2048]{1,0:T(8,128)(2,1)S(1)}, bf16[2,128,128]{2,1,0:T(8,128)(2,1)S(1)}) custom-call(f32[1,256]{1,0:T(1,128)S(1)} %bitcast.14, bf16[2048,1024]{1,0:T(8,128)(2,1)S(1)} %load.1.factor_ref, bf16[64,128]{1,0:T(8,128)(2,1)S(1)} %get-tuple-element.37.refs_0_, bf16[192,128]{1,0:T(8,128)(2,1)S(1)} %collective-permute-done.16.refs_0_.refs_1_, ...), custom_call_target="tpu_custom_call" | custom-call | flops 134217728 | bytes 2097152 | tf_op jit(solution)/shard_map/term_first/pallas_call | solution.py:367
  47.5 0.1 collective-permute-start.19
  47.6 0.8 %term.6 = (f32[2,128,128]{2,1,0:T(8,128)S(1)}, bf16[2,128,128]{2,1,0:T(8,128)(2,1)S(1)}) custom-call(bf16[128,2048]{1,0:T(8,128)(2,1)S(1)} %get-tuple-element.38.coef_ref, bf16[2048,1024]{1,0:T(8,128)(2,1)S(1)} %load.1.factor_ref), custom_call_target="tpu_custom_call" | custom-call | flops 268435456 | bytes 2097152 | tf_op jit(solution)/shard_map/term/pallas_call | solution.py:377
  48.4 0.6 collective-permute-start.20
  48.9 0.0 collective-permute-done.19.got_ref
  49.0 2.1 %collective-permute-start.22 = (bf16[2,128,128]{2,1,0:T(8,128)(2,1)S(1)}, bf16[2,128,128]{2,1,0:T(8,128)(2,1)S(1)}, u32[]{:S(2)}, u32[]{:S(2)}) collective-permute-start(bf16[2,128,128]{2,1,0:T(8,128)(2,1)S(1)} %pair.6.refs_0_), channel_id=1, source_target_pairs={{0,6},{1,5},{2,4},{3,7},{4,2},{5,1},{6,0},{7,3},{8,14},{9,13},{10,... | collective-permute-start | bytes 196616 | tf_op jit(solution)/shard_map/ppermute | solution.py:326
  51.0 0.5 term.7.mine_ref
  51.5 0.0 collective-permute-done.20.got_ref
  51.6 0.1 collective-permute-start.21
  51.7 3.8 %collective-permute-done.22.refs_0_ = bf16[2,128,128]{2,1,0:T(8,128)(2,1)S(1)} collective-permute-done((bf16[2,128,128]{2,1,0:T(8,128)(2,1)S(1)}, bf16[2,128,128]{2,1,0:T(8,128)(2,1)S(1)}, u32[]{:S(2)}, u32[]{:S(2)}) %collective-permute-start.22) | collective-permute-done | bytes 65568 | tf_op jit(solution)/shard_map/ppermute | solution.py:326
  55.4 0.2 local.3.base_ref
  55.6 0.1 collective-permute-done.21.one_ref
  55.7 0.9 %collective-permute-done.23.given_ref = bf16[128,128]{1,0:T(8,128)(2,1)S(1)} collective-permute-done((bf16[128,128]{1,0:T(8,128)(2,1)S(1)}, bf16[128,128]{1,0:T(8,128)(2,1)S(1)}, u32[]{:S(2)}, u32[]{:S(2)}) %collective-permute-start.23) | collective-permute-done | bytes 32800 | tf_op jit(solution)/shard_map/ppermute | solution.py:40
  56.6 0.7 %update.3 = (f32[128,128]{1,0:T(8,128)}, f32[128,128]{1,0:T(8,128)}) custom-call(f32[128,128]{1,0:T(8,128)S(1)} %get-tuple-element.33.x_ref, f32[128,128]{1,0:T(8,128)S(1)} %local.3.base_ref, f32[1,128,128]{2,1,0:T(8,128)S(1)} %get-tuple-element.42.kept_ref, bf16[1,128,128]{2,1,0:T(8,128)(2,1)S(1)} %collective-permute-done.21.one_ref, ...), custom_call_target="tpu_custom_call" | custom-call | bytes 262144 | tf_op jit(solution)/shard_map/update/pallas_call | solution.py:406
  (20 shorter events, 0.2 us)
Async XLA Ops:
  1.5 1.3 %collective-permute-start = (bf16[1,128,128]{2,1,0:T(8,128)(2,1)S(1)}, bf16[1,128,128]{2,1,0:T(8,128)(2,1)S(1)}, u32[]{:S(2)}, u32[]{:S(2)}) collective-permute-start(bf16[1,128,128]{2,1,0:T(8,128)(2,1)S(1)} %fusion.short_ref), channel_id=1, source_target_pairs={{0,1},{1,0},{2,3},{3,2},{4,5},{5,4},{6,7},{7,6},{8,9},{9,8},{10,11... | collective-permute-start | bytes 98312 | tf_op jit(solution)/shard_map/ppermute | solution.py:40
  2.8 8.9 %collective-permute-start.1 = (bf16[2,128,128]{2,1,0:T(8,128)(2,1)S(1)}, bf16[2,128,128]{2,1,0:T(8,128)(2,1)S(1)}, u32[]{:S(2)}, u32[]{:S(2)}) collective-permute-start(bf16[2,128,128]{2,1,0:T(8,128)(2,1)S(1)} %duo.2.refs_0_), channel_id=1, source_target_pairs={{0,6},{1,5},{2,4},{3,7},{4,2},{5,1},{6,0},{7,3},{8,14},{9,13},{10,... | collective-permute-start | bytes 196616 | tf_op jit(solution)/shard_map/ppermute | solution.py:326
  7.8 3.9 %collective-permute-start.2 = (bf16[1,128,128]{2,1,0:T(8,128)(2,1)S(1)}, bf16[1,128,128]{2,1,0:T(8,128)(2,1)S(1)}, u32[]{:S(2)}, u32[]{:S(2)}) collective-permute-start(bf16[1,128,128]{2,1,0:T(8,128)(2,1)S(1)} %fusion.short_ref), channel_id=1, source_target_pairs={{0,2},{1,3},{2,0},{3,1},{4,6},{5,7},{6,4},{7,5},{8,10},{9,11},{10,... | collective-permute-start | bytes 98312 | tf_op jit(solution)/shard_map/ppermute | solution.py:40
  7.8 2.2 %copy-start = (bf16[256,8,1024]{2,1,0:T(8,128)(2,1)S(1)}, bf16[256,8,1024]{2,1,0:T(8,128)(2,1)}, u32[]{:S(2)}) copy-start(bf16[256,8,1024]{2,1,0:T(8,128)(2,1)} %param.6) | copy-start | bytes 12582916
  10.4 2.7 %copy-start.1 = (f32[16,8,128]{2,1,0:T(8,128)S(1)}, f32[16,8,128]{2,1,0:T(8,128)}, u32[]{:S(2)}) copy-start(f32[16,8,128]{2,1,0:T(8,128)} %param.4) | copy-start | bytes 196612
  11.7 9.2 %copy-start.3 = (f32[256]{0:T(256)S(1)}, f32[256]{0:T(256)}, u32[]{:S(2)}) copy-start(f32[256]{0:T(256)} %param.7) | copy-start | bytes 3076
  11.8 1.4 %collective-permute-start.3 = (bf16[3,128,128]{2,1,0:T(8,128)(2,1)S(1)}, bf16[3,128,128]{2,1,0:T(8,128)(2,1)S(1)}, u32[]{:S(2)}, u32[]{:S(2)}) collective-permute-start(bf16[3,128,128]{2,1,0:T(8,128)(2,1)S(1)} %join.2.refs_0_.refs_1_), channel_id=1, source_target_pairs={{0,1},{1,0},{2,3},{3,2},{4,5},{5,4},{6,7},{7,6},{8,9},{9,8},{10,11... | collective-permute-start | bytes 294920 | tf_op jit(solution)/shard_map/ppermute | solution.py:40
  14.2 6.7 %collective-permute-start.5 = (bf16[192,128]{1,0:T(8,128)(2,1)S(1)}, bf16[192,128]{1,0:T(8,128)(2,1)S(1)}, u32[]{:S(2)}, u32[]{:S(2)}) collective-permute-start(bf16[192,128]{1,0:T(8,128)(2,1)S(1)} %get-tuple-element.25), channel_id=1, source_target_pairs={{0,24},{8,16},{16,8},{24,0},{1,25},{9,17},{17,9},{25,1},{2,26},{10... | collective-permute-start | bytes 147464 | tf_op jit(solution)/shard_map/ppermute | solution.py:40
  16.7 4.3 %collective-permute-start.4 = (bf16[192,128]{1,0:T(8,128)(2,1)S(1)}, bf16[192,128]{1,0:T(8,128)(2,1)S(1)}, u32[]{:S(2)}, u32[]{:S(2)}) collective-permute-start(bf16[192,128]{1,0:T(8,128)(2,1)S(1)} %get-tuple-element.25), channel_id=1, source_target_pairs={{0,8},{8,0},{16,24},{24,16},{1,9},{9,1},{17,25},{25,17},{2,10},{10... | collective-permute-start | bytes 147464 | tf_op jit(solution)/shard_map/ppermute | solution.py:40
  17.2 3.7 %collective-permute-start.6 = (bf16[64,128]{1,0:T(8,128)(2,1)S(1)}, bf16[64,128]{1,0:T(8,128)(2,1)S(1)}, u32[]{:S(2)}, u32[]{:S(2)}) collective-permute-start(bf16[64,128]{1,0:T(8,128)(2,1)S(1)} %get-tuple-element.26.refs_0_), channel_id=1, source_target_pairs={{0,16},{8,24},{16,0},{24,8},{1,17},{9,25},{17,1},{25,9},{2,18},{10... | collective-permute-start | bytes 49160 | tf_op jit(solution)/shard_map/ppermute | solution.py:40
  21.7 1.4 %collective-permute-start.7 = (bf16[2,128,128]{2,1,0:T(8,128)(2,1)S(1)}, bf16[2,128,128]{2,1,0:T(8,128)(2,1)S(1)}, u32[]{:S(2)}, u32[]{:S(2)}) collective-permute-start(bf16[2,128,128]{2,1,0:T(8,128)(2,1)S(1)} %get-tuple-element.29), channel_id=1, source_target_pairs={{0,1},{1,0},{2,3},{3,2},{4,5},{5,4},{6,7},{7,6},{8,9},{9,8},{10,11... | collective-permute-start | bytes 196616 | tf_op jit(solution)/shard_map/ppermute | solution.py:40
  21.8 7.8 %copy-start.2 = (f32[8,128]{1,0:T(8,128)S(1)}, f32[8,128]{1,0:T(8,128)}, u32[]{:S(2)}) copy-start(f32[8,128]{1,0:T(8,128)} %amp_ref.3) | copy-start | bytes 12292
  22.6 3.4 %collective-permute-start.8 = (bf16[2,128,128]{2,1,0:T(8,128)(2,1)S(1)}, bf16[2,128,128]{2,1,0:T(8,128)(2,1)S(1)}, u32[]{:S(2)}, u32[]{:S(2)}) collective-permute-start(bf16[2,128,128]{2,1,0:T(8,128)(2,1)S(1)} %get-tuple-element.30), channel_id=1, source_target_pairs={{0,1},{1,0},{2,3},{3,2},{4,5},{5,4},{6,7},{7,6},{8,9},{9,8},{10,11... | collective-permute-start | bytes 196616 | tf_op jit(solution)/shard_map/ppermute | solution.py:40
  23.2 6.4 %collective-permute-start.10 = (bf16[2,128,128]{2,1,0:T(8,128)(2,1)S(1)}, bf16[2,128,128]{2,1,0:T(8,128)(2,1)S(1)}, u32[]{:S(2)}, u32[]{:S(2)}) collective-permute-start(bf16[2,128,128]{2,1,0:T(8,128)(2,1)S(1)} %pair.4.refs_0_), channel_id=1, source_target_pairs={{0,6},{1,5},{2,4},{3,7},{4,2},{5,1},{6,0},{7,3},{8,14},{9,13},{10,... | collective-permute-start | bytes 196616 | tf_op jit(solution)/shard_map/ppermute | solution.py:326
  26.0 4.0 %collective-permute-start.9 = (bf16[1,128,128]{2,1,0:T(8,128)(2,1)S(1)}, bf16[1,128,128]{2,1,0:T(8,128)(2,1)S(1)}, u32[]{:S(2)}, u32[]{:S(2)}) collective-permute-start(bf16[1,128,128]{2,1,0:T(8,128)(2,1)S(1)} %get-tuple-element.32), channel_id=1, source_target_pairs={{0,2},{1,3},{2,0},{3,1},{4,6},{5,7},{6,4},{7,5},{8,10},{9,11},{10,... | collective-permute-start | bytes 98312 | tf_op jit(solution)/shard_map/ppermute | solution.py:40
  29.6 1.2 %collective-permute-start.11 = (bf16[128,128]{1,0:T(8,128)(2,1)S(1)}, bf16[128,128]{1,0:T(8,128)(2,1)S(1)}, u32[]{:S(2)}, u32[]{:S(2)}) collective-permute-start(bf16[128,128]{1,0:T(8,128)(2,1)S(1)} %give.2), channel_id=1, source_target_pairs={{0,1},{1,0},{2,3},{3,2},{4,5},{5,4},{6,7},{7,6},{8,9},{9,8},{10,11... | collective-permute-start | bytes 98312 | tf_op jit(solution)/shard_map/ppermute | solution.py:40
  30.8 1.3 %collective-permute-start.12 = (bf16[1,128,128]{2,1,0:T(8,128)(2,1)S(1)}, bf16[1,128,128]{2,1,0:T(8,128)(2,1)S(1)}, u32[]{:S(2)}, u32[]{:S(2)}) collective-permute-start(bf16[1,128,128]{2,1,0:T(8,128)(2,1)S(1)} %get-tuple-element.34.short_ref), channel_id=1, source_target_pairs={{0,1},{1,0},{2,3},{3,2},{4,5},{5,4},{6,7},{7,6},{8,9},{9,8},{10,11... | collective-permute-start | bytes 98312 | tf_op jit(solution)/shard_map/ppermute | solution.py:40
  32.1 6.5 %collective-permute-start.13 = (bf16[2,128,128]{2,1,0:T(8,128)(2,1)S(1)}, bf16[2,128,128]{2,1,0:T(8,128)(2,1)S(1)}, u32[]{:S(2)}, u32[]{:S(2)}) collective-permute-start(bf16[2,128,128]{2,1,0:T(8,128)(2,1)S(1)} %duo.3.refs_0_), channel_id=1, source_target_pairs={{0,6},{1,5},{2,4},{3,7},{4,2},{5,1},{6,0},{7,3},{8,14},{9,13},{10,... | collective-permute-start | bytes 196616 | tf_op jit(solution)/shard_map/ppermute | solution.py:326
  34.5 4.1 %collective-permute-start.14 = (bf16[1,128,128]{2,1,0:T(8,128)(2,1)S(1)}, bf16[1,128,128]{2,1,0:T(8,128)(2,1)S(1)}, u32[]{:S(2)}, u32[]{:S(2)}) collective-permute-start(bf16[1,128,128]{2,1,0:T(8,128)(2,1)S(1)} %get-tuple-element.34.short_ref), channel_id=1, source_target_pairs={{0,2},{1,3},{2,0},{3,1},{4,6},{5,7},{6,4},{7,5},{8,10},{9,11},{10,... | collective-permute-start | bytes 98312 | tf_op jit(solution)/shard_map/ppermute | solution.py:40
  38.6 1.4 %collective-permute-start.15 = (bf16[3,128,128]{2,1,0:T(8,128)(2,1)S(1)}, bf16[3,128,128]{2,1,0:T(8,128)(2,1)S(1)}, u32[]{:S(2)}, u32[]{:S(2)}) collective-permute-start(bf16[3,128,128]{2,1,0:T(8,128)(2,1)S(1)} %join.3.refs_0_.refs_1_), channel_id=1, source_target_pairs={{0,1},{1,0},{2,3},{3,2},{4,5},{5,4},{6,7},{7,6},{8,9},{9,8},{10,11... | collective-permute-start | bytes 294920 | tf_op jit(solution)/shard_map/ppermute | solution.py:40
  41.0 5.7 %collective-permute-start.17 = (bf16[192,128]{1,0:T(8,128)(2,1)S(1)}, bf16[192,128]{1,0:T(8,128)(2,1)S(1)}, u32[]{:S(2)}, u32[]{:S(2)}) collective-permute-start(bf16[192,128]{1,0:T(8,128)(2,1)S(1)} %get-tuple-element.36), channel_id=1, source_target_pairs={{0,24},{8,16},{16,8},{24,0},{1,25},{9,17},{17,9},{25,1},{2,26},{10... | collective-permute-start | bytes 147464 | tf_op jit(solution)/shard_map/ppermute | solution.py:40
  42.5 4.3 %collective-permute-start.16 = (bf16[192,128]{1,0:T(8,128)(2,1)S(1)}, bf16[192,128]{1,0:T(8,128)(2,1)S(1)}, u32[]{:S(2)}, u32[]{:S(2)}) collective-permute-start(bf16[192,128]{1,0:T(8,128)(2,1)S(1)} %get-tuple-element.36), channel_id=1, source_target_pairs={{0,8},{8,0},{16,24},{24,16},{1,9},{9,1},{17,25},{25,17},{2,10},{10... | collective-permute-start | bytes 147464 | tf_op jit(solution)/shard_map/ppermute | solution.py:40
  43.0 3.7 %collective-permute-start.18 = (bf16[64,128]{1,0:T(8,128)(2,1)S(1)}, bf16[64,128]{1,0:T(8,128)(2,1)S(1)}, u32[]{:S(2)}, u32[]{:S(2)}) collective-permute-start(bf16[64,128]{1,0:T(8,128)(2,1)S(1)} %get-tuple-element.37.refs_0_), channel_id=1, source_target_pairs={{0,16},{8,24},{16,0},{24,8},{1,17},{9,25},{17,1},{25,9},{2,18},{10... | collective-permute-start | bytes 49160 | tf_op jit(solution)/shard_map/ppermute | solution.py:40
  47.5 1.4 %collective-permute-start.19 = (bf16[2,128,128]{2,1,0:T(8,128)(2,1)S(1)}, bf16[2,128,128]{2,1,0:T(8,128)(2,1)S(1)}, u32[]{:S(2)}, u32[]{:S(2)}) collective-permute-start(bf16[2,128,128]{2,1,0:T(8,128)(2,1)S(1)} %get-tuple-element.40), channel_id=1, source_target_pairs={{0,1},{1,0},{2,3},{3,2},{4,5},{5,4},{6,7},{7,6},{8,9},{9,8},{10,11... | collective-permute-start | bytes 196616 | tf_op jit(solution)/shard_map/ppermute | solution.py:40
  48.4 3.2 %collective-permute-start.20 = (bf16[2,128,128]{2,1,0:T(8,128)(2,1)S(1)}, bf16[2,128,128]{2,1,0:T(8,128)(2,1)S(1)}, u32[]{:S(2)}, u32[]{:S(2)}) collective-permute-start(bf16[2,128,128]{2,1,0:T(8,128)(2,1)S(1)} %get-tuple-element.41), channel_id=1, source_target_pairs={{0,1},{1,0},{2,3},{3,2},{4,5},{5,4},{6,7},{7,6},{8,9},{9,8},{10,11... | collective-permute-start | bytes 196616 | tf_op jit(solution)/shard_map/ppermute | solution.py:40
  49.0 6.4 %collective-permute-start.22 = (bf16[2,128,128]{2,1,0:T(8,128)(2,1)S(1)}, bf16[2,128,128]{2,1,0:T(8,128)(2,1)S(1)}, u32[]{:S(2)}, u32[]{:S(2)}) collective-permute-start(bf16[2,128,128]{2,1,0:T(8,128)(2,1)S(1)} %pair.6.refs_0_), channel_id=1, source_target_pairs={{0,6},{1,5},{2,4},{3,7},{4,2},{5,1},{6,0},{7,3},{8,14},{9,13},{10,... | collective-permute-start | bytes 196616 | tf_op jit(solution)/shard_map/ppermute | solution.py:326
  51.6 4.2 %collective-permute-start.21 = (bf16[1,128,128]{2,1,0:T(8,128)(2,1)S(1)}, bf16[1,128,128]{2,1,0:T(8,128)(2,1)S(1)}, u32[]{:S(2)}, u32[]{:S(2)}) collective-permute-start(bf16[1,128,128]{2,1,0:T(8,128)(2,1)S(1)} %get-tuple-element.43), channel_id=1, source_target_pairs={{0,2},{1,3},{2,0},{3,1},{4,6},{5,7},{6,4},{7,5},{8,10},{9,11},{10,... | collective-permute-start | bytes 98312 | tf_op jit(solution)/shard_map/ppermute | solution.py:40
  55.4 1.2 %collective-permute-start.23 = (bf16[128,128]{1,0:T(8,128)(2,1)S(1)}, bf16[128,128]{1,0:T(8,128)(2,1)S(1)}, u32[]{:S(2)}, u32[]{:S(2)}) collective-permute-start(bf16[128,128]{1,0:T(8,128)(2,1)S(1)} %give.3), channel_id=1, source_target_pairs={{0,1},{1,0},{2,3},{3,2},{4,5},{5,4},{6,7},{7,6},{8,9},{9,8},{10,11... | collective-permute-start | bytes 98312 | tf_op jit(solution)/shard_map/ppermute | solution.py:40

commit v5 on v3

--- a/solution.py
+++ b/solution.py
@@ -40,10 +40,10 @@
     return lax.ppermute(value, axis, [(i, i ^ mask) for i in range(lax.axis_size(axis))])
 
 
-def gather_kernel(*refs):
+def gather_kernel(masks, *refs):
     part_refs, out_ref = refs[1:-1], refs[-1]
     me = lax.div(lax.axis_index("tile"), 2)
-    for mask, ref in enumerate(part_refs):
+    for mask, ref in zip(masks, part_refs):
         out_ref[me ^ mask] = ref[...]
 
 
@@ -66,7 +66,7 @@
     near, lines, _ = fields_ref.shape
     count = factor_ref.shape[0]
     field = jnp.concatenate([fields_ref[z] for z in range(near)], axis=1)
-    step = min(256, count)
+    step = min(1024, count)
     row_of = lax.broadcasted_iota(jnp.int32, (rows, lines), 0)
     lane_of = lax.broadcasted_iota(jnp.int32, (rows, lines), 1)
     same = (lax.rem(lane_of, rows) == row_of).astype(jnp.float32)
@@ -276,11 +276,14 @@
     )(flat)
     for step in range(ITERS):
         halve = step == 0
-        parts = [swap(short, "tile", 2 * mask) for mask in range(1, near)]
+        order = list(range(1, near))
+        if step == 0:
+            order.sort(key=lambda mask: (mask == near // 2, mask))
+        parts = {mask: swap(short, "tile", 2 * mask) for mask in order}
         whole = [pl.BlockSpec(memory_space=pl.ANY)] + [pl.BlockSpec(memory_space=pltpu.VMEM)] * near
         own = call(
-            gather_kernel, shape(bf16, near, lines, width), in_specs=whole, name="order"
-        )(held, short, *parts)
+            partial(gather_kernel, [0] + order), shape(bf16, near, lines, width), in_specs=whole, name="order"
+        )(held, short, *[parts[mask] for mask in order])
         across = swap(own, "tile", 1)
         diag = call(
             partial(first_kernel, rows),

time: 56.5 us -> 55.8 us (0.988)
  Pallas kernels: 9.94 us -> 9.33 us
  transfers between devices with their start and end apart: 24 -> 24, of which waited for: 12 -> 14; matrix products, arithmetic and copies ran while one was open for 0% -> 0% of each run, Pallas kernels for 9% -> 9%
where the time goes in v5:
time: 55.8 us; the launch traced here: 55.6 us
  starting transfers between devices  27.5 us (49%)
  waiting for transfers between devices  14.8 us (27%)
  Pallas kernels  9.33 us (17%)
  local copies, waits for them, and re-layouts  2.21 us (4%)
  other arithmetic  0.85 us (2%)
  between operations  0.85 us (2%)
    ppermute x24, starting transfers between devices, swap(): lax.ppermute(value, axis, [(i, i ^ mask) for i in range(lax.axis_size(axi...  27.5 us
    ppermute x24, waiting for transfers between devices, swap(): lax.ppermute(value, axis, [(i, i ^ mask) for i in range(lax.axis_size(axi...  14.8 us
    pallas_call x4, Pallas kernels, term(): call(partial(term_kernel, wanted, len(after)), in_specs=[pl.BlockSpec(mem...  2.58 us
    unnamed x8, local copies, waits for them, and re-layouts  2.21 us
    pallas_call x2, Pallas kernels, on_device(): call(partial(second_kernel, rows, cols, halve), (shape(bf16, pay_rows, wi...  2.16 us
    pallas_call x2, Pallas kernels, on_device(): call(partial(first_kernel, rows), shape(f32, blocks * LANES, lines), flop...  1.63 us
    pallas_call x2, Pallas kernels, on_device(): call(partial(far_kernel, rows, cols, groups, ncells_all, away), (shape(bf...  1.45 us
  transfers between devices with their start and end apart: 24, of which 14 were waited for; matrix products, arithmetic and copies ran while one was open for 0% of the time, Pallas kernels for 9%

profile of v5, /device:TPU:0, one launch (start us, length us, event | category | flops | bytes accessed | tf_op | source)
XLA Modules:
  0.0 55.6 jit_solution(1808614355736118473)
XLA Ops:
  0.6 0.8 %multiply_convert_fusion.refs_1_ = bf16[128,128]{1,0:T(8,128)(2,1)S(1)} fusion(f32[16,8,128]{2,1,0:T(8,128)} %param.4), kind=kLoop, calls=%fused_computation | loop fusion | flops 32768 | bytes 98304 | tf_op jit(solution)/shard_map/convert_element_type | solution.py:250
  1.5 4.0 %collective-permute-start.2 = (bf16[128,128]{1,0:T(8,128)(2,1)S(1)}, bf16[128,128]{1,0:T(8,128)(2,1)S(1)}, u32[]{:S(2)}, u32[]{:S(2)}) collective-permute-start(bf16[128,128]{1,0:T(8,128)(2,1)S(1)} %multiply_convert_fusion.refs_1_), channel_id=1, source_target_pairs={{0,4},{1,5},{2,6},{3,7},{4,0},{5,1},{6,2},{7,3},{8,12},{9,13},{10,... | collective-permute-start | bytes 98312 | tf_op jit(solution)/shard_map/ppermute | solution.py:40
  5.5 1.3 %collective-permute-start.1 = (bf16[128,128]{1,0:T(8,128)(2,1)S(1)}, bf16[128,128]{1,0:T(8,128)(2,1)S(1)}, u32[]{:S(2)}, u32[]{:S(2)}) collective-permute-start(bf16[128,128]{1,0:T(8,128)(2,1)S(1)} %multiply_convert_fusion.refs_1_), channel_id=1, source_target_pairs={{0,6},{1,7},{2,4},{3,5},{4,2},{5,3},{6,0},{7,1},{8,14},{9,15},{10,... | collective-permute-start | bytes 98312 | tf_op jit(solution)/shard_map/ppermute | solution.py:40
  6.9 0.2 collective-permute-start
  7.1 2.2 %copy-done = bf16[256,8,1024]{2,1,0:T(8,128)(2,1)S(1)} copy-done((bf16[256,8,1024]{2,1,0:T(8,128)(2,1)S(1)}, bf16[256,8,1024]{2,1,0:T(8,128)(2,1)}, u32[]{:S(2)}) %copy-start) | copy-done | bytes 4194328
  9.3 0.4 load.1.refs_0_.factor_ref
  9.7 0.0 copy-start.1
  9.7 1.5 %collective-permute-done.1.refs_3_ = bf16[128,128]{1,0:T(8,128)(2,1)S(1)} collective-permute-done((bf16[128,128]{1,0:T(8,128)(2,1)S(1)}, bf16[128,128]{1,0:T(8,128)(2,1)S(1)}, u32[]{:S(2)}, u32[]{:S(2)}) %collective-permute-start.1) | collective-permute-done | bytes 32800 | tf_op jit(solution)/shard_map/ppermute | solution.py:40
  11.3 0.0 copy-start.3
  11.3 0.1 collective-permute-start.3
  11.3 0.8 %project_own.2.diag_ref = f32[256,128]{1,0:T(8,128)S(1)} custom-call(bf16[4,128,128]{2,1,0:T(8,128)(2,1)S(1)} %order.2.fields_ref, bf16[2048,1024]{1,0:T(8,128)(2,1)S(1)} %load.1.refs_0_.factor_ref), custom_call_target="tpu_custom_call" | custom-call | flops 268435456 | bytes 2097152 | tf_op jit(solution)/shard_map/project_own/pallas_call | solution.py:288
  12.2 0.5 collective-permute-done.3.fields_ref
  12.7 1.1 %project_across.2 = (bf16[192,128]{1,0:T(8,128)(2,1)S(1)}, bf16[64,128]{1,0:T(8,128)(2,1)S(1)}, f32[128,128]{1,0:T(8,128)S(1)}) custom-call(f32[128,128]{1,0:T(8,128)S(1)} %bitcast.7, bf16[4,128,128]{2,1,0:T(8,128)(2,1)S(1)} %collective-permute-done.3.fields_ref, bf16[2048,1024]{1,0:T(8,128)(2,1)S(1)} %load.1.refs_0_.factor_ref, ...), custom_call_target="tpu_custom_call" | custom-call | flops 268435456 | bytes 2097152 | tf_op jit(solution)/shard_map/project_across/pallas_call | solution.py:295
  13.8 2.5 %collective-permute-start.5 = (bf16[192,128]{1,0:T(8,128)(2,1)S(1)}, bf16[192,128]{1,0:T(8,128)(2,1)S(1)}, u32[]{:S(2)}, u32[]{:S(2)}) collective-permute-start(bf16[192,128]{1,0:T(8,128)(2,1)S(1)} %get-tuple-element.29), channel_id=1, source_target_pairs={{0,24},{8,16},{16,8},{24,0},{1,25},{9,17},{17,9},{25,1},{2,26},{10... | collective-permute-start | bytes 147464 | tf_op jit(solution)/shard_map/ppermute | solution.py:40
  16.2 0.5 collective-permute-start.4
  16.8 0.5 collective-permute-start.6
  17.3 3.2 %collective-permute-done.6.refs_2_ = bf16[64,128]{1,0:T(8,128)(2,1)S(1)} collective-permute-done((bf16[64,128]{1,0:T(8,128)(2,1)S(1)}, bf16[64,128]{1,0:T(8,128)(2,1)S(1)}, u32[]{:S(2)}, u32[]{:S(2)}) %collective-permute-start.6) | collective-permute-done | bytes 16416 | tf_op jit(solution)/shard_map/ppermute | solution.py:40
  20.5 0.0 collective-permute-done.5.refs_1_.refs_3_
  20.5 0.0 collective-permute-done.4.refs_0_.refs_1_
  20.5 0.7 %term_first.2 = (bf16[128,2048]{1,0:T(8,128)(2,1)S(1)}, bf16[2,128,128]{2,1,0:T(8,128)(2,1)S(1)}) custom-call(f32[1,256]{1,0:T(1,128)S(1)} %bitcast.12, bf16[2048,1024]{1,0:T(8,128)(2,1)S(1)} %load.1.refs_0_.factor_ref, bf16[64,128]{1,0:T(8,128)(2,1)S(1)} %get-tuple-element.30.refs_0_, bf16[192,128]{1,0:T(8,128)(2,1)S(1)} %collective-permute-done.4.refs_0_.refs_1_, ...), custom_call_target="tpu_custom_call" | custom-call | flops 134217728 | bytes 2097152 | tf_op jit(solution)/shard_map/term_first/pallas_call | solution.py:310
  21.2 0.1 collective-permute-start.7
  21.3 0.0 copy-start.2
  21.3 0.8 %term.4 = (f32[2,128,128]{2,1,0:T(8,128)S(1)}, bf16[2,128,128]{2,1,0:T(8,128)(2,1)S(1)}) custom-call(bf16[128,2048]{1,0:T(8,128)(2,1)S(1)} %get-tuple-element.31.coef_ref, bf16[2048,1024]{1,0:T(8,128)(2,1)S(1)} %load.1.refs_0_.factor_ref), custom_call_target="tpu_custom_call" | custom-call | flops 268435456 | bytes 2097152 | tf_op jit(solution)/shard_map/term/pallas_call | solution.py:320
  22.1 0.5 collective-permute-start.8
  22.7 0.0 collective-permute-done.7.got_ref
  22.7 2.1 %collective-permute-start.9 = (bf16[128,128]{1,0:T(8,128)(2,1)S(1)}, bf16[128,128]{1,0:T(8,128)(2,1)S(1)}, u32[]{:S(2)}, u32[]{:S(2)}) collective-permute-start(bf16[128,128]{1,0:T(8,128)(2,1)S(1)} %get-tuple-element.34.refs_0_), channel_id=1, source_target_pairs={{0,6},{1,7},{2,4},{3,5},{4,2},{5,3},{6,0},{7,1},{8,14},{9,15},{10,... | collective-permute-start | bytes 98312 | tf_op jit(solution)/shard_map/ppermute | solution.py:40
  24.8 0.0 collective-permute-start.10
  24.8 0.5 term.5.mine_ref
  25.3 2.4 %collective-permute-start.11 = (bf16[128,128]{1,0:T(8,128)(2,1)S(1)}, bf16[128,128]{1,0:T(8,128)(2,1)S(1)}, u32[]{:S(2)}, u32[]{:S(2)}) collective-permute-start(bf16[128,128]{1,0:T(8,128)(2,1)S(1)} %get-tuple-element.38), channel_id=1, source_target_pairs={{0,2},{1,3},{2,0},{3,1},{4,6},{5,7},{6,4},{7,5},{8,10},{9,11},{10,... | collective-permute-start | bytes 98312 | tf_op jit(solution)/shard_map/ppermute | solution.py:40
  27.8 0.2 local.2.base_ref
  27.9 0.7 %collective-permute-done.9.refs_1_ = bf16[128,128]{1,0:T(8,128)(2,1)S(1)} collective-permute-done((bf16[128,128]{1,0:T(8,128)(2,1)S(1)}, bf16[128,128]{1,0:T(8,128)(2,1)S(1)}, u32[]{:S(2)}, u32[]{:S(2)}) %collective-permute-start.9) | collective-permute-done | bytes 32800 | tf_op jit(solution)/shard_map/ppermute | solution.py:40
  28.6 1.0 %collective-permute-done.10.refs_2_ = bf16[128,128]{1,0:T(8,128)(2,1)S(1)} collective-permute-done((bf16[128,128]{1,0:T(8,128)(2,1)S(1)}, bf16[128,128]{1,0:T(8,128)(2,1)S(1)}, u32[]{:S(2)}, u32[]{:S(2)}) %collective-permute-start.10) | collective-permute-done | bytes 32800 | tf_op jit(solution)/shard_map/ppermute | solution.py:40
  29.7 0.3 collective-permute-done.11.refs_3_
  30.0 1.8 %collective-permute-start.14 = (bf16[128,128]{1,0:T(8,128)(2,1)S(1)}, bf16[128,128]{1,0:T(8,128)(2,1)S(1)}, u32[]{:S(2)}, u32[]{:S(2)}) collective-permute-start(bf16[128,128]{1,0:T(8,128)(2,1)S(1)} %get-tuple-element.40.refs_1_), channel_id=1, source_target_pairs={{0,6},{1,7},{2,4},{3,5},{4,2},{5,3},{6,0},{7,1},{8,14},{9,15},{10,... | collective-permute-start | bytes 98312 | tf_op jit(solution)/shard_map/ppermute | solution.py:40
  31.9 1.4 %collective-permute-start.13 = (bf16[128,128]{1,0:T(8,128)(2,1)S(1)}, bf16[128,128]{1,0:T(8,128)(2,1)S(1)}, u32[]{:S(2)}, u32[]{:S(2)}) collective-permute-start(bf16[128,128]{1,0:T(8,128)(2,1)S(1)} %get-tuple-element.40.refs_1_), channel_id=1, source_target_pairs={{0,4},{1,5},{2,6},{3,7},{4,0},{5,1},{6,2},{7,3},{8,12},{9,13},{10,... | collective-permute-start | bytes 98312 | tf_op jit(solution)/shard_map/ppermute | solution.py:40
  33.2 1.2 %collective-permute-start.12 = (bf16[128,128]{1,0:T(8,128)(2,1)S(1)}, bf16[128,128]{1,0:T(8,128)(2,1)S(1)}, u32[]{:S(2)}, u32[]{:S(2)}) collective-permute-start(bf16[128,128]{1,0:T(8,128)(2,1)S(1)} %get-tuple-element.40.refs_1_), channel_id=1, source_target_pairs={{0,2},{1,3},{2,0},{3,1},{4,6},{5,7},{6,4},{7,5},{8,10},{9,11},{10,... | collective-permute-start | bytes 98312 | tf_op jit(solution)/shard_map/ppermute | solution.py:40
  34.5 1.5 %collective-permute-done.14.refs_4_ = bf16[128,128]{1,0:T(8,128)(2,1)S(1)} collective-permute-done((bf16[128,128]{1,0:T(8,128)(2,1)S(1)}, bf16[128,128]{1,0:T(8,128)(2,1)S(1)}, u32[]{:S(2)}, u32[]{:S(2)}) %collective-permute-start.14) | collective-permute-done | bytes 32800 | tf_op jit(solution)/shard_map/ppermute | solution.py:40
  36.0 0.7 %collective-permute-done.13.refs_3_ = bf16[128,128]{1,0:T(8,128)(2,1)S(1)} collective-permute-done((bf16[128,128]{1,0:T(8,128)(2,1)S(1)}, bf16[128,128]{1,0:T(8,128)(2,1)S(1)}, u32[]{:S(2)}, u32[]{:S(2)}) %collective-permute-start.13) | collective-permute-done | bytes 32800 | tf_op jit(solution)/shard_map/ppermute | solution.py:40
  36.7 0.5 collective-permute-done.12.refs_2_
  37.2 0.1 collective-permute-start.15
  37.2 0.8 %project_own.3.diag_ref = f32[256,128]{1,0:T(8,128)S(1)} custom-call(bf16[4,128,128]{2,1,0:T(8,128)(2,1)S(1)} %order.3.fields_ref, bf16[2048,1024]{1,0:T(8,128)(2,1)S(1)} %load.1.refs_0_.factor_ref), custom_call_target="tpu_custom_call" | custom-call | flops 268435456 | bytes 2097152 | tf_op jit(solution)/shard_map/project_own/pallas_call | solution.py:288
  38.1 0.5 collective-permute-done.15.fields_ref
  38.6 1.1 %project_across.3 = (bf16[192,128]{1,0:T(8,128)(2,1)S(1)}, bf16[64,128]{1,0:T(8,128)(2,1)S(1)}, f32[128,128]{1,0:T(8,128)S(1)}) custom-call(f32[128,128]{1,0:T(8,128)S(1)} %get-tuple-element.39.x_ref, bf16[4,128,128]{2,1,0:T(8,128)(2,1)S(1)} %collective-permute-done.15.fields_ref, bf16[2048,1024]{1,0:T(8,128)(2,1)S(1)} %load.1.refs_0_.factor_ref, ...), custom_call_target="tpu_custom_call" | custom-call | flops 268435456 | bytes 2097152 | tf_op jit(solution)/shard_map/project_across/pallas_call | solution.py:295
  39.7 1.5 %collective-permute-start.17 = (bf16[192,128]{1,0:T(8,128)(2,1)S(1)}, bf16[192,128]{1,0:T(8,128)(2,1)S(1)}, u32[]{:S(2)}, u32[]{:S(2)}) collective-permute-start(bf16[192,128]{1,0:T(8,128)(2,1)S(1)} %get-tuple-element.42), channel_id=1, source_target_pairs={{0,24},{8,16},{16,8},{24,0},{1,25},{9,17},{17,9},{25,1},{2,26},{10... | collective-permute-start | bytes 147464 | tf_op jit(solution)/shard_map/ppermute | solution.py:40
  41.1 0.5 collective-permute-start.16
  41.6 1.5 %collective-permute-start.18 = (bf16[64,128]{1,0:T(8,128)(2,1)S(1)}, bf16[64,128]{1,0:T(8,128)(2,1)S(1)}, u32[]{:S(2)}, u32[]{:S(2)}) collective-permute-start(bf16[64,128]{1,0:T(8,128)(2,1)S(1)} %get-tuple-element.43.refs_0_), channel_id=1, source_target_pairs={{0,16},{8,24},{16,0},{24,8},{1,17},{9,25},{17,1},{25,9},{2,18},{10... | collective-permute-start | bytes 49160 | tf_op jit(solution)/shard_map/ppermute | solution.py:40
  43.2 2.2 %collective-permute-done.18.refs_2_ = bf16[64,128]{1,0:T(8,128)(2,1)S(1)} collective-permute-done((bf16[64,128]{1,0:T(8,128)(2,1)S(1)}, bf16[64,128]{1,0:T(8,128)(2,1)S(1)}, u32[]{:S(2)}, u32[]{:S(2)}) %collective-permute-start.18) | collective-permute-done | bytes 16416 | tf_op jit(solution)/shard_map/ppermute | solution.py:40
  45.4 0.0 collective-permute-done.17.refs_1_.refs_3_
  45.4 0.0 collective-permute-done.16.refs_0_.refs_1_
  45.4 0.7 %term_first.3 = (bf16[128,2048]{1,0:T(8,128)(2,1)S(1)}, bf16[2,128,128]{2,1,0:T(8,128)(2,1)S(1)}) custom-call(f32[1,256]{1,0:T(1,128)S(1)} %bitcast.13, bf16[2048,1024]{1,0:T(8,128)(2,1)S(1)} %load.1.refs_0_.factor_ref, bf16[64,128]{1,0:T(8,128)(2,1)S(1)} %get-tuple-element.43.refs_0_, bf16[192,128]{1,0:T(8,128)(2,1)S(1)} %collective-permute-done.16.refs_0_.refs_1_, ...), custom_call_target="tpu_custom_call" | custom-call | flops 134217728 | bytes 2097152 | tf_op jit(solution)/shard_map/term_first/pallas_call | solution.py:310
  46.1 0.1 collective-permute-start.19
  46.2 0.8 %term.6 = (f32[2,128,128]{2,1,0:T(8,128)S(1)}, bf16[2,128,128]{2,1,0:T(8,128)(2,1)S(1)}) custom-call(bf16[128,2048]{1,0:T(8,128)(2,1)S(1)} %get-tuple-element.44.coef_ref, bf16[2048,1024]{1,0:T(8,128)(2,1)S(1)} %load.1.refs_0_.factor_ref), custom_call_target="tpu_custom_call" | custom-call | flops 268435456 | bytes 2097152 | tf_op jit(solution)/shard_map/term/pallas_call | solution.py:320
  47.0 0.6 collective-permute-start.20
  47.6 0.0 collective-permute-done.19.got_ref
  47.6 2.1 %collective-permute-start.21 = (bf16[128,128]{1,0:T(8,128)(2,1)S(1)}, bf16[128,128]{1,0:T(8,128)(2,1)S(1)}, u32[]{:S(2)}, u32[]{:S(2)}) collective-permute-start(bf16[128,128]{1,0:T(8,128)(2,1)S(1)} %get-tuple-element.47.refs_0_), channel_id=1, source_target_pairs={{0,6},{1,7},{2,4},{3,5},{4,2},{5,3},{6,0},{7,1},{8,14},{9,15},{10,... | collective-permute-start | bytes 98312 | tf_op jit(solution)/shard_map/ppermute | solution.py:40
  49.7 0.6 %collective-permute-start.22 = (bf16[128,128]{1,0:T(8,128)(2,1)S(1)}, bf16[128,128]{1,0:T(8,128)(2,1)S(1)}, u32[]{:S(2)}, u32[]{:S(2)}) collective-permute-start(bf16[128,128]{1,0:T(8,128)(2,1)S(1)} %get-tuple-element.48.refs_1_), channel_id=1, source_target_pairs={{0,4},{1,5},{2,6},{3,7},{4,0},{5,1},{6,2},{7,3},{8,12},{9,13},{10,... | collective-permute-start | bytes 98312 | tf_op jit(solution)/shard_map/ppermute | solution.py:40
  50.3 0.5 term.7.mine_ref
  50.8 0.0 collective-permute-done.20.got_ref
  50.9 1.8 %collective-permute-start.23 = (bf16[128,128]{1,0:T(8,128)(2,1)S(1)}, bf16[128,128]{1,0:T(8,128)(2,1)S(1)}, u32[]{:S(2)}, u32[]{:S(2)}) collective-permute-start(bf16[128,128]{1,0:T(8,128)(2,1)S(1)} %get-tuple-element.51), channel_id=1, source_target_pairs={{0,2},{1,3},{2,0},{3,1},{4,6},{5,7},{6,4},{7,5},{8,10},{9,11},{10,... | collective-permute-start | bytes 98312 | tf_op jit(solution)/shard_map/ppermute | solution.py:40
  52.6 0.2 local.3.base_ref
  52.8 0.6 %collective-permute-done.21.refs_1_ = bf16[128,128]{1,0:T(8,128)(2,1)S(1)} collective-permute-done((bf16[128,128]{1,0:T(8,128)(2,1)S(1)}, bf16[128,128]{1,0:T(8,128)(2,1)S(1)}, u32[]{:S(2)}, u32[]{:S(2)}) %collective-permute-start.21) | collective-permute-done | bytes 32800 | tf_op jit(solution)/shard_map/ppermute | solution.py:40
  53.4 1.1 %collective-permute-done.22.refs_2_ = bf16[128,128]{1,0:T(8,128)(2,1)S(1)} collective-permute-done((bf16[128,128]{1,0:T(8,128)(2,1)S(1)}, bf16[128,128]{1,0:T(8,128)(2,1)S(1)}, u32[]{:S(2)}, u32[]{:S(2)}) %collective-permute-start.22) | collective-permute-done | bytes 32800 | tf_op jit(solution)/shard_map/ppermute | solution.py:40
  54.5 0.4 collective-permute-done.23.refs_3_
  54.9 0.7 %update.3 = (f32[128,128]{1,0:T(8,128)}, f32[128,128]{1,0:T(8,128)}) custom-call(f32[128,128]{1,0:T(8,128)S(1)} %get-tuple-element.39.x_ref, f32[128,128]{1,0:T(8,128)S(1)} %local.3.base_ref, f32[128,128]{1,0:T(8,128)S(1)} %get-tuple-element.50.refs_0_, bf16[128,128]{1,0:T(8,128)(2,1)S(1)} %collective-permute-done.21.refs_1_, ...), custom_call_target="tpu_custom_call" | custom-call | bytes 262144 | tf_op jit(solution)/shard_map/update/pallas_call | solution.py:349
  (14 shorter events, 0.1 us)
Async XLA Ops:
  1.5 8.2 %collective-permute-start.2 = (bf16[128,128]{1,0:T(8,128)(2,1)S(1)}, bf16[128,128]{1,0:T(8,128)(2,1)S(1)}, u32[]{:S(2)}, u32[]{:S(2)}) collective-permute-start(bf16[128,128]{1,0:T(8,128)(2,1)S(1)} %multiply_convert_fusion.refs_1_), channel_id=1, source_target_pairs={{0,4},{1,5},{2,6},{3,7},{4,0},{5,1},{6,2},{7,3},{8,12},{9,13},{10,... | collective-permute-start | bytes 98312 | tf_op jit(solution)/shard_map/ppermute | solution.py:40
  5.5 5.7 %collective-permute-start.1 = (bf16[128,128]{1,0:T(8,128)(2,1)S(1)}, bf16[128,128]{1,0:T(8,128)(2,1)S(1)}, u32[]{:S(2)}, u32[]{:S(2)}) collective-permute-start(bf16[128,128]{1,0:T(8,128)(2,1)S(1)} %multiply_convert_fusion.refs_1_), channel_id=1, source_target_pairs={{0,6},{1,7},{2,4},{3,5},{4,2},{5,3},{6,0},{7,1},{8,14},{9,15},{10,... | collective-permute-start | bytes 98312 | tf_op jit(solution)/shard_map/ppermute | solution.py:40
  6.9 4.4 %collective-permute-start = (bf16[128,128]{1,0:T(8,128)(2,1)S(1)}, bf16[128,128]{1,0:T(8,128)(2,1)S(1)}, u32[]{:S(2)}, u32[]{:S(2)}) collective-permute-start(bf16[128,128]{1,0:T(8,128)(2,1)S(1)} %multiply_convert_fusion.refs_1_), channel_id=1, source_target_pairs={{0,2},{1,3},{2,0},{3,1},{4,6},{5,7},{6,4},{7,5},{8,10},{9,11},{10,... | collective-permute-start | bytes 98312 | tf_op jit(solution)/shard_map/ppermute | solution.py:40
  7.1 2.2 %copy-start = (bf16[256,8,1024]{2,1,0:T(8,128)(2,1)S(1)}, bf16[256,8,1024]{2,1,0:T(8,128)(2,1)}, u32[]{:S(2)}) copy-start(bf16[256,8,1024]{2,1,0:T(8,128)(2,1)} %param.6) | copy-start | bytes 12582916
  9.7 3.0 %copy-start.1 = (f32[16,8,128]{2,1,0:T(8,128)S(1)}, f32[16,8,128]{2,1,0:T(8,128)}, u32[]{:S(2)}) copy-start(f32[16,8,128]{2,1,0:T(8,128)} %param.4) | copy-start | bytes 196612
  11.3 9.3 %copy-start.3 = (f32[256]{0:T(256)S(1)}, f32[256]{0:T(256)}, u32[]{:S(2)}) copy-start(f32[256]{0:T(256)} %param.7) | copy-start | bytes 3076
  11.3 1.4 %collective-permute-start.3 = (bf16[4,128,128]{2,1,0:T(8,128)(2,1)S(1)}, bf16[4,128,128]{2,1,0:T(8,128)(2,1)S(1)}, u32[]{:S(2)}, u32[]{:S(2)}) collective-permute-start(bf16[4,128,128]{2,1,0:T(8,128)(2,1)S(1)} %order.2.fields_ref), channel_id=1, source_target_pairs={{0,1},{1,0},{2,3},{3,2},{4,5},{5,4},{6,7},{7,6},{8,9},{9,8},{10,11... | collective-permute-start | bytes 393224 | tf_op jit(solution)/shard_map/ppermute | solution.py:40
  13.8 6.7 %collective-permute-start.5 = (bf16[192,128]{1,0:T(8,128)(2,1)S(1)}, bf16[192,128]{1,0:T(8,128)(2,1)S(1)}, u32[]{:S(2)}, u32[]{:S(2)}) collective-permute-start(bf16[192,128]{1,0:T(8,128)(2,1)S(1)} %get-tuple-element.29), channel_id=1, source_target_pairs={{0,24},{8,16},{16,8},{24,0},{1,25},{9,17},{17,9},{25,1},{2,26},{10... | collective-permute-start | bytes 147464 | tf_op jit(solution)/shard_map/ppermute | solution.py:40
  16.2 4.3 %collective-permute-start.4 = (bf16[192,128]{1,0:T(8,128)(2,1)S(1)}, bf16[192,128]{1,0:T(8,128)(2,1)S(1)}, u32[]{:S(2)}, u32[]{:S(2)}) collective-permute-start(bf16[192,128]{1,0:T(8,128)(2,1)S(1)} %get-tuple-element.29), channel_id=1, source_target_pairs={{0,8},{8,0},{16,24},{24,16},{1,9},{9,1},{17,25},{25,17},{2,10},{10... | collective-permute-start | bytes 147464 | tf_op jit(solution)/shard_map/ppermute | solution.py:40
  16.8 3.7 %collective-permute-start.6 = (bf16[64,128]{1,0:T(8,128)(2,1)S(1)}, bf16[64,128]{1,0:T(8,128)(2,1)S(1)}, u32[]{:S(2)}, u32[]{:S(2)}) collective-permute-start(bf16[64,128]{1,0:T(8,128)(2,1)S(1)} %get-tuple-element.30.refs_0_), channel_id=1, source_target_pairs={{0,16},{8,24},{16,0},{24,8},{1,17},{9,25},{17,1},{25,9},{2,18},{10... | collective-permute-start | bytes 49160 | tf_op jit(solution)/shard_map/ppermute | solution.py:40
  21.2 1.4 %collective-permute-start.7 = (bf16[2,128,128]{2,1,0:T(8,128)(2,1)S(1)}, bf16[2,128,128]{2,1,0:T(8,128)(2,1)S(1)}, u32[]{:S(2)}, u32[]{:S(2)}) collective-permute-start(bf16[2,128,128]{2,1,0:T(8,128)(2,1)S(1)} %get-tuple-element.33), channel_id=1, source_target_pairs={{0,1},{1,0},{2,3},{3,2},{4,5},{5,4},{6,7},{7,6},{8,9},{9,8},{10,11... | collective-permute-start | bytes 196616 | tf_op jit(solution)/shard_map/ppermute | solution.py:40
  21.3 6.4 %copy-start.2 = (f32[8,128]{1,0:T(8,128)S(1)}, f32[8,128]{1,0:T(8,128)}, u32[]{:S(2)}) copy-start(f32[8,128]{1,0:T(8,128)} %amp_ref.3) | copy-start | bytes 12292
  22.1 3.2 %collective-permute-start.8 = (bf16[2,128,128]{2,1,0:T(8,128)(2,1)S(1)}, bf16[2,128,128]{2,1,0:T(8,128)(2,1)S(1)}, u32[]{:S(2)}, u32[]{:S(2)}) collective-permute-start(bf16[2,128,128]{2,1,0:T(8,128)(2,1)S(1)} %get-tuple-element.36), channel_id=1, source_target_pairs={{0,1},{1,0},{2,3},{3,2},{4,5},{5,4},{6,7},{7,6},{8,9},{9,8},{10,11... | collective-permute-start | bytes 196616 | tf_op jit(solution)/shard_map/ppermute | solution.py:40
  22.7 5.9 %collective-permute-start.9 = (bf16[128,128]{1,0:T(8,128)(2,1)S(1)}, bf16[128,128]{1,0:T(8,128)(2,1)S(1)}, u32[]{:S(2)}, u32[]{:S(2)}) collective-permute-start(bf16[128,128]{1,0:T(8,128)(2,1)S(1)} %get-tuple-element.34.refs_0_), channel_id=1, source_target_pairs={{0,6},{1,7},{2,4},{3,5},{4,2},{5,3},{6,0},{7,1},{8,14},{9,15},{10,... | collective-permute-start | bytes 98312 | tf_op jit(solution)/shard_map/ppermute | solution.py:40
  24.8 4.8 %collective-permute-start.10 = (bf16[128,128]{1,0:T(8,128)(2,1)S(1)}, bf16[128,128]{1,0:T(8,128)(2,1)S(1)}, u32[]{:S(2)}, u32[]{:S(2)}) collective-permute-start(bf16[128,128]{1,0:T(8,128)(2,1)S(1)} %get-tuple-element.35.refs_1_), channel_id=1, source_target_pairs={{0,4},{1,5},{2,6},{3,7},{4,0},{5,1},{6,2},{7,3},{8,12},{9,13},{10,... | collective-permute-start | bytes 98312 | tf_op jit(solution)/shard_map/ppermute | solution.py:40
  25.3 4.6 %collective-permute-start.11 = (bf16[128,128]{1,0:T(8,128)(2,1)S(1)}, bf16[128,128]{1,0:T(8,128)(2,1)S(1)}, u32[]{:S(2)}, u32[]{:S(2)}) collective-permute-start(bf16[128,128]{1,0:T(8,128)(2,1)S(1)} %get-tuple-element.38), channel_id=1, source_target_pairs={{0,2},{1,3},{2,0},{3,1},{4,6},{5,7},{6,4},{7,5},{8,10},{9,11},{10,... | collective-permute-start | bytes 98312 | tf_op jit(solution)/shard_map/ppermute | solution.py:40
  30.0 6.0 %collective-permute-start.14 = (bf16[128,128]{1,0:T(8,128)(2,1)S(1)}, bf16[128,128]{1,0:T(8,128)(2,1)S(1)}, u32[]{:S(2)}, u32[]{:S(2)}) collective-permute-start(bf16[128,128]{1,0:T(8,128)(2,1)S(1)} %get-tuple-element.40.refs_1_), channel_id=1, source_target_pairs={{0,6},{1,7},{2,4},{3,5},{4,2},{5,3},{6,0},{7,1},{8,14},{9,15},{10,... | collective-permute-start | bytes 98312 | tf_op jit(solution)/shard_map/ppermute | solution.py:40
  31.9 4.8 %collective-permute-start.13 = (bf16[128,128]{1,0:T(8,128)(2,1)S(1)}, bf16[128,128]{1,0:T(8,128)(2,1)S(1)}, u32[]{:S(2)}, u32[]{:S(2)}) collective-permute-start(bf16[128,128]{1,0:T(8,128)(2,1)S(1)} %get-tuple-element.40.refs_1_), channel_id=1, source_target_pairs={{0,4},{1,5},{2,6},{3,7},{4,0},{5,1},{6,2},{7,3},{8,12},{9,13},{10,... | collective-permute-start | bytes 98312 | tf_op jit(solution)/shard_map/ppermute | solution.py:40
  33.2 3.9 %collective-permute-start.12 = (bf16[128,128]{1,0:T(8,128)(2,1)S(1)}, bf16[128,128]{1,0:T(8,128)(2,1)S(1)}, u32[]{:S(2)}, u32[]{:S(2)}) collective-permute-start(bf16[128,128]{1,0:T(8,128)(2,1)S(1)} %get-tuple-element.40.refs_1_), channel_id=1, source_target_pairs={{0,2},{1,3},{2,0},{3,1},{4,6},{5,7},{6,4},{7,5},{8,10},{9,11},{10,... | collective-permute-start | bytes 98312 | tf_op jit(solution)/shard_map/ppermute | solution.py:40
  37.2 1.4 %collective-permute-start.15 = (bf16[4,128,128]{2,1,0:T(8,128)(2,1)S(1)}, bf16[4,128,128]{2,1,0:T(8,128)(2,1)S(1)}, u32[]{:S(2)}, u32[]{:S(2)}) collective-permute-start(bf16[4,128,128]{2,1,0:T(8,128)(2,1)S(1)} %order.3.fields_ref), channel_id=1, source_target_pairs={{0,1},{1,0},{2,3},{3,2},{4,5},{5,4},{6,7},{7,6},{8,9},{9,8},{10,11... | collective-permute-start | bytes 393224 | tf_op jit(solution)/shard_map/ppermute | solution.py:40
  39.7 5.7 %collective-permute-start.17 = (bf16[192,128]{1,0:T(8,128)(2,1)S(1)}, bf16[192,128]{1,0:T(8,128)(2,1)S(1)}, u32[]{:S(2)}, u32[]{:S(2)}) collective-permute-start(bf16[192,128]{1,0:T(8,128)(2,1)S(1)} %get-tuple-element.42), channel_id=1, source_target_pairs={{0,24},{8,16},{16,8},{24,0},{1,25},{9,17},{17,9},{25,1},{2,26},{10... | collective-permute-start | bytes 147464 | tf_op jit(solution)/shard_map/ppermute | solution.py:40
  41.1 4.3 %collective-permute-start.16 = (bf16[192,128]{1,0:T(8,128)(2,1)S(1)}, bf16[192,128]{1,0:T(8,128)(2,1)S(1)}, u32[]{:S(2)}, u32[]{:S(2)}) collective-permute-start(bf16[192,128]{1,0:T(8,128)(2,1)S(1)} %get-tuple-element.42), channel_id=1, source_target_pairs={{0,8},{8,0},{16,24},{24,16},{1,9},{9,1},{17,25},{25,17},{2,10},{10... | collective-permute-start | bytes 147464 | tf_op jit(solution)/shard_map/ppermute | solution.py:40
  41.6 3.7 %collective-permute-start.18 = (bf16[64,128]{1,0:T(8,128)(2,1)S(1)}, bf16[64,128]{1,0:T(8,128)(2,1)S(1)}, u32[]{:S(2)}, u32[]{:S(2)}) collective-permute-start(bf16[64,128]{1,0:T(8,128)(2,1)S(1)} %get-tuple-element.43.refs_0_), channel_id=1, source_target_pairs={{0,16},{8,24},{16,0},{24,8},{1,17},{9,25},{17,1},{25,9},{2,18},{10... | collective-permute-start | bytes 49160 | tf_op jit(solution)/shard_map/ppermute | solution.py:40
  46.1 1.4 %collective-permute-start.19 = (bf16[2,128,128]{2,1,0:T(8,128)(2,1)S(1)}, bf16[2,128,128]{2,1,0:T(8,128)(2,1)S(1)}, u32[]{:S(2)}, u32[]{:S(2)}) collective-permute-start(bf16[2,128,128]{2,1,0:T(8,128)(2,1)S(1)} %get-tuple-element.46), channel_id=1, source_target_pairs={{0,1},{1,0},{2,3},{3,2},{4,5},{5,4},{6,7},{7,6},{8,9},{9,8},{10,11... | collective-permute-start | bytes 196616 | tf_op jit(solution)/shard_map/ppermute | solution.py:40
  47.0 3.8 %collective-permute-start.20 = (bf16[2,128,128]{2,1,0:T(8,128)(2,1)S(1)}, bf16[2,128,128]{2,1,0:T(8,128)(2,1)S(1)}, u32[]{:S(2)}, u32[]{:S(2)}) collective-permute-start(bf16[2,128,128]{2,1,0:T(8,128)(2,1)S(1)} %get-tuple-element.49), channel_id=1, source_target_pairs={{0,1},{1,0},{2,3},{3,2},{4,5},{5,4},{6,7},{7,6},{8,9},{9,8},{10,11... | collective-permute-start | bytes 196616 | tf_op jit(solution)/shard_map/ppermute | solution.py:40
  47.6 5.8 %collective-permute-start.21 = (bf16[128,128]{1,0:T(8,128)(2,1)S(1)}, bf16[128,128]{1,0:T(8,128)(2,1)S(1)}, u32[]{:S(2)}, u32[]{:S(2)}) collective-permute-start(bf16[128,128]{1,0:T(8,128)(2,1)S(1)} %get-tuple-element.47.refs_0_), channel_id=1, source_target_pairs={{0,6},{1,7},{2,4},{3,5},{4,2},{5,3},{6,0},{7,1},{8,14},{9,15},{10,... | collective-permute-start | bytes 98312 | tf_op jit(solution)/shard_map/ppermute | solution.py:40
  49.7 4.8 %collective-permute-start.22 = (bf16[128,128]{1,0:T(8,128)(2,1)S(1)}, bf16[128,128]{1,0:T(8,128)(2,1)S(1)}, u32[]{:S(2)}, u32[]{:S(2)}) collective-permute-start(bf16[128,128]{1,0:T(8,128)(2,1)S(1)} %get-tuple-element.48.refs_1_), channel_id=1, source_target_pairs={{0,4},{1,5},{2,6},{3,7},{4,0},{5,1},{6,2},{7,3},{8,12},{9,13},{10,... | collective-permute-start | bytes 98312 | tf_op jit(solution)/shard_map/ppermute | solution.py:40
  50.9 4.0 %collective-permute-start.23 = (bf16[128,128]{1,0:T(8,128)(2,1)S(1)}, bf16[128,128]{1,0:T(8,128)(2,1)S(1)}, u32[]{:S(2)}, u32[]{:S(2)}) collective-permute-start(bf16[128,128]{1,0:T(8,128)(2,1)S(1)} %get-tuple-element.51), channel_id=1, source_target_pairs={{0,2},{1,3},{2,0},{3,1},{4,6},{5,7},{6,4},{7,5},{8,10},{9,11},{10,... | collective-permute-start | bytes 98312 | tf_op jit(solution)/shard_map/ppermute | solution.py:40

commit v6 on v4

--- a/solution.py
+++ b/solution.py
@@ -41,25 +41,14 @@
 
 
 def place_of(spot):
-    even, odd, which = spot
+    mask, other = spot
     me = lax.axis_index("tile")
-    chip, core = lax.div(me, 2), lax.rem(me, 2)
-    chip = chip ^ jnp.where(core == 0, even, odd)
-    if which == "own":
-        which = core
-    elif which == "other":
-        which = 1 - core
-    return 2 * chip + which
+    core = lax.rem(me, 2)
+    return 2 * (lax.div(me, 2) ^ mask) + (1 - core if other else core)
 
 
 def columns_of(spots):
     return [pl.multiple_of(place_of(spot) * LANES, LANES) for spot in spots]
-
-
-def duo_kernel(short_ref, twin_ref, out_ref):
-    core = lax.rem(lax.axis_index("tile"), 2)
-    out_ref[core] = short_ref[0]
-    out_ref[1 - core] = twin_ref[0]
 
 
 def join_kernel(*refs):
@@ -89,7 +78,7 @@
     lines = fields[0].shape[0]
     count = factor_ref.shape[0]
     field = jnp.concatenate(fields, axis=1)
-    step = min(256, count)
+    step = min(1024, count)
     row_of = lax.broadcasted_iota(jnp.int32, (rows, lines), 0)
     lane_of = lax.broadcasted_iota(jnp.int32, (rows, lines), 1)
     same = (lax.rem(lane_of, rows) == row_of).astype(jnp.float32)
@@ -226,15 +215,6 @@
         at = end
 
 
-def give_kernel(*refs):
-    part_refs, out_ref = refs[:-1], refs[-1]
-    other = 1 - lax.rem(lax.axis_index("tile"), 2)
-    total = part_refs[0][other].astype(jnp.float32)
-    for ref in part_refs[1:]:
-        total = total + ref[other].astype(jnp.float32)
-    out_ref[...] = total.astype(out_ref.dtype)
-
-
 def local_kernel(rows, cols, halve, b_ref, x_ref, amp_ref, along_ref, *refs):
     pay_refs, base_ref = refs[:-1], refs[-1]
     lines = cols * rows
@@ -256,12 +236,11 @@
     base_ref[...] = b_ref[...] - (x + scaled)
 
 
-def update_kernel(halve, last, x_ref, base_ref, kept_ref, one_ref, given_ref, *refs):
+def update_kernel(halve, last, x_ref, base_ref, *refs):
     part_refs, (new_ref, other_ref) = refs[:-2], refs[-2:]
-    core = lax.rem(lax.axis_index("tile"), 2)
-    rank_sum = kept_ref[0] + one_ref[0].astype(jnp.float32) + given_ref[...].astype(jnp.float32)
-    for ref in part_refs:
-        rank_sum = rank_sum + ref[core].astype(jnp.float32)
+    rank_sum = part_refs[0][0]
+    for ref in part_refs[1:]:
+        rank_sum = rank_sum + ref[0].astype(jnp.float32)
     x = 0.5 * x_ref[...] if halve else x_ref[...]
     residual = base_ref[...] - rank_sum
     new = x + 0.5 * residual
@@ -312,18 +291,14 @@
         scratch_shapes=[pltpu.SemaphoreType.DMA((8,))],
         name="load",
     )(flat)
-    rounds = [
-        [(2 * (chip ^ (2 * n + 1 - core)) + core) for chip in range(near) for core in range(2)]
-        for n in range(near // 2 - 1, 0, -1)
-    ]
-    own_away = [(2 * n + 1, 2 * n, q) for n in range(near // 2 - 1, 0, -1) for q in range(2)]
-    other_away = [(2 * n, 2 * n + 1, q) for n in range(near // 2 - 1, 0, -1) for q in range(2)]
-    home = [(0, 0, 0), (0, 0, 1)]
-    own_close = [(0, 0, "own"), (1, 1, "own")]
-    other_close = [(0, 0, "other"), (1, 1, "other")]
-
-    def travel(value, targets):
-        return lax.ppermute(value, "tile", list(enumerate(targets)))
+    half = near // 2
+    close, away = list(range(half)), list(range(near - 1, half - 1, -1))
+
+    def spots_of(masks, other):
+        return [(mask, other != (mask > 0)) for mask in masks]
+
+    def cross(value, mask):
+        return swap(value, "tile", 2 * mask + 1)
 
     def first(fields, spots, *before):
         return call(
@@ -336,23 +311,23 @@
 
     for step in range(ITERS):
         halve = step == 0
-        twin = swap(short, "tile", 1)
-        one = swap(short, "tile", 2)
-        duo = call(duo_kernel, shape(bf16, 2, lines, width), name="duo")(short, twin)
-        gots = [travel(duo, targets) for targets in rounds]
-        diag = first([duo], home)
+        order = list(range(1, near))
+        if step == 0:
+            order.sort(key=lambda mask: (mask == near // 2, mask))
+        parts = [cross(short, mask) for mask in order]
         bundle = call(
             join_kernel,
-            shape(bf16, near - 1, lines, width),
+            shape(bf16, near, lines, width),
             in_specs=[pl.BlockSpec(memory_space=pl.ANY)]
-            + [pl.BlockSpec(memory_space=pltpu.VMEM)] * (len(gots) + 1),
+            + [pl.BlockSpec(memory_space=pltpu.VMEM)] * near,
             name="join",
-        )(diag, *gots, one)
+        )(held, short, *parts)
         across = swap(bundle, "tile", 1)
-        diag = first([bundle], own_away + own_close[1:], diag)
-        spots = other_away + other_close[1:]
+        known = spots_of([0] + order, False)
+        diag = first([bundle], known)
+        spots = spots_of([0] + order, True)
         pay, part, along = call(
-            partial(second_kernel, rows, cols, halve, spots, home + own_away + own_close[1:]),
+            partial(second_kernel, rows, cols, halve, spots, known),
             (
                 shape(bf16, pay_rows, width),
                 shape(bf16, pay_rows - lines, width),
@@ -362,11 +337,11 @@
             moved=flat.size,
             scratch_shapes=[pltpu.VMEM((blocks * LANES, lines), f32)],
             name="project_across",
-        )(x, held, diag, across, duo, bundle)
+        )(x, held, diag, across, bundle)
         pays = [swap(part if mask & (mask + 1) else pay, "grp", mask) for mask in range(1, groups)]
         coef, far = call(
-            partial(far_kernel, rows, cols, groups, ncells_all, other_away),
-            (shape(bf16, lines, ranks * rows), shape(bf16, near - 2, lines, width)),
+            partial(far_kernel, rows, cols, groups, ncells_all, spots_of(away, True)),
+            (shape(bf16, lines, ranks * rows), shape(bf16, half, lines, width)),
             flops=work // 2,
             moved=flat.size,
             name="term_first",
@@ -384,20 +359,20 @@
                 name="term",
             )(coef, held, *after)
 
-        mine, far = term((own_away, f32), (other_close, bf16))
-        sends = call(
-            pair_kernel, [shape(bf16, 2, lines, width) for _ in rounds], name="pair"
-        )(mine, got)
-        terms = [travel(send, targets) for send, targets in zip(sends, rounds)]
+        def pair(mine, got, masks):
+            return call(
+                pair_kernel,
+                [shape(bf16 if mask else f32, 1, lines, width) for mask in masks],
+                name="pair",
+            )(mine, got)
+
+        mine, far = term((spots_of(away, False), f32), (spots_of(close, True), bf16))
+        sends = pair(mine, got, away)
+        terms = [cross(send, mask) for send, mask in zip(sends, away)]
         got = swap(far, "tile", 1)
-        (mine,) = term((own_close, f32), after=sends)
-        kept, send = call(
-            pair_kernel,
-            [shape(f32, 1, lines, width), shape(bf16, 1, lines, width)],
-            name="pair",
-        )(mine, got)
-        close = swap(send, "tile", 2)
-        given = swap(call(give_kernel, shape(bf16, lines, width), name="give")(*terms), "tile", 1)
+        (mine,) = term((spots_of(close, False), f32), after=sends)
+        kept, *sends = pair(mine, got, close)
+        terms += [cross(send, mask) for send, mask in zip(sends, close[1:])]
         rims = [pay for mask, pay in enumerate(pays, 1) if not mask & (mask + 1)]
         base = call(
             partial(local_kernel, rows, cols, halve), shape(f32, lines, width), name="local"
@@ -410,7 +385,7 @@
                 shape(f32, lines, width) if last else shape(bf16, 1, lines, width),
             ),
             name="update",
-        )(x, base, kept, close, given, *terms)
+        )(x, base, kept, *terms)
     return x.reshape(cols, rows, width), short.reshape(cols, rows, width)
 
 

time: 57.5 us -> 54.4 us (0.946)
  waiting for transfers between devices: 22.1 us -> 14.2 us
  starting transfers between devices: 21 us -> 26.5 us
  Pallas kernels: 10.2 us -> 9.48 us
    ppermute x20 -> x24, starting transfers between devices: 9.24 us -> 26.5 us  [swap(): lax.ppermute(value, axis, [(i, i ^ mask) for i in range(lax.axis_size(axi...]
    ppermute x4 -> x0, starting transfers between devices: 11.7 us -> none  [travel(): return lax.ppermute(value, 'tile', list(enumerate(targets)))]
    ppermute x4 -> x0, waiting for transfers between devices: 7.28 us -> none  [travel(): return lax.ppermute(value, 'tile', list(enumerate(targets)))]
    pallas_call x4 -> x2, Pallas kernels: 2.53 us -> 1.62 us  [first(): call(partial(first_kernel, rows, spots, len(before)), shape(f32, blocks *...]
    ppermute x20 -> x24, waiting for transfers between devices: 14.9 us -> 14.2 us  [swap(): lax.ppermute(value, axis, [(i, i ^ mask) for i in range(lax.axis_size(axi...]
    pallas_call x14 -> x10, Pallas kernels: 3.7 us -> 3.83 us  [the longest x2 2.3 us: on_device(): call(partial(second_kernel, rows, cols, halve, spots, known), (shape(bf16...]
  transfers between devices with their start and end apart: 24 -> 24, of which waited for: 14 -> 12; matrix products, arithmetic and copies ran while one was open for 0% -> 0% of each run, Pallas kernels for 10% -> 9%
where the time goes in v6:
time: 54.4 us; the launch traced here: 54.1 us
  starting transfers between devices  26.5 us (49%)
  waiting for transfers between devices  14.2 us (26%)
  Pallas kernels  9.48 us (17%)
  local copies, waits for them, and re-layouts  2.21 us (4%)
  other arithmetic  0.85 us (2%)
  between operations  0.83 us (2%)
    ppermute x24, starting transfers between devices, swap(): lax.ppermute(value, axis, [(i, i ^ mask) for i in range(lax.axis_size(axi...  26.5 us
    ppermute x24, waiting for transfers between devices, swap(): lax.ppermute(value, axis, [(i, i ^ mask) for i in range(lax.axis_size(axi...  14.2 us
    pallas_call x4, Pallas kernels, term(): call(partial(term_kernel, wanted, len(after)), in_specs=[pl.BlockSpec(mem...  2.6 us
    pallas_call x2, Pallas kernels, on_device(): call(partial(second_kernel, rows, cols, halve, spots, known), (shape(bf16...  2.3 us
    unnamed x8, local copies, waits for them, and re-layouts  2.21 us
    pallas_call x2, Pallas kernels, first(): call(partial(first_kernel, rows, spots, len(before)), shape(f32, blocks *...  1.62 us
    pallas_call x2, Pallas kernels, on_device(): call(partial(far_kernel, rows, cols, groups, ncells_all, spots_of(away, T...  1.45 us
  transfers between devices with their start and end apart: 24, of which 12 were waited for; matrix products, arithmetic and copies ran while one was open for 0% of the time, Pallas kernels for 9%

profile of v6, /device:TPU:0, one launch (start us, length us, event | category | flops | bytes accessed | tf_op | source)
XLA Modules:
  0.0 54.1 jit_solution(14920113436682482680)
XLA Ops:
  0.6 0.8 %fusion.refs_1_ = bf16[1,128,128]{2,1,0:T(8,128)(2,1)S(1)} fusion(f32[16,8,128]{2,1,0:T(8,128)} %param.4), kind=kLoop, calls=%fused_computation.1 | loop fusion | flops 32768 | bytes 98304 | tf_op jit(solution)/shard_map/convert_element_type | solution.py:267
  1.5 3.5 %collective-permute-start.2 = (bf16[1,128,128]{2,1,0:T(8,128)(2,1)S(1)}, bf16[1,128,128]{2,1,0:T(8,128)(2,1)S(1)}, u32[]{:S(2)}, u32[]{:S(2)}) collective-permute-start(bf16[1,128,128]{2,1,0:T(8,128)(2,1)S(1)} %fusion.refs_1_), channel_id=1, source_target_pairs={{0,5},{1,4},{2,7},{3,6},{4,1},{5,0},{6,3},{7,2},{8,13},{9,12},{10,... | collective-permute-start | bytes 98312 | tf_op jit(solution)/shard_map/ppermute | solution.py:40
  5.0 1.6 %collective-permute-start.1 = (bf16[1,128,128]{2,1,0:T(8,128)(2,1)S(1)}, bf16[1,128,128]{2,1,0:T(8,128)(2,1)S(1)}, u32[]{:S(2)}, u32[]{:S(2)}) collective-permute-start(bf16[1,128,128]{2,1,0:T(8,128)(2,1)S(1)} %fusion.refs_1_), channel_id=1, source_target_pairs={{0,7},{1,6},{2,5},{3,4},{4,3},{5,2},{6,1},{7,0},{8,15},{9,14},{10,... | collective-permute-start | bytes 98312 | tf_op jit(solution)/shard_map/ppermute | solution.py:40
  6.6 0.2 collective-permute-start
  6.8 2.2 %copy-done = bf16[256,8,1024]{2,1,0:T(8,128)(2,1)S(1)} copy-done((bf16[256,8,1024]{2,1,0:T(8,128)(2,1)S(1)}, bf16[256,8,1024]{2,1,0:T(8,128)(2,1)}, u32[]{:S(2)}) %copy-start) | copy-done | bytes 4194328
  9.0 0.4 load.1.refs_0_.factor_ref
  9.4 0.0 copy-start.1
  9.4 0.0 collective-permute-done.2.refs_4_
  9.4 0.8 %collective-permute-done.1.refs_3_ = bf16[1,128,128]{2,1,0:T(8,128)(2,1)S(1)} collective-permute-done((bf16[1,128,128]{2,1,0:T(8,128)(2,1)S(1)}, bf16[1,128,128]{2,1,0:T(8,128)(2,1)S(1)}, u32[]{:S(2)}, u32[]{:S(2)}) %collective-permute-start.1) | collective-permute-done | bytes 32800 | tf_op jit(solution)/shard_map/ppermute | solution.py:40
  10.2 0.2 collective-permute-done.refs_2_
  10.4 0.0 copy-start.3
  10.4 0.7 %collective-permute-start.3 = (bf16[4,128,128]{2,1,0:T(8,128)(2,1)S(1)}, bf16[4,128,128]{2,1,0:T(8,128)(2,1)S(1)}, u32[]{:S(2)}, u32[]{:S(2)}) collective-permute-start(bf16[4,128,128]{2,1,0:T(8,128)(2,1)S(1)} %join.2.refs_0_), channel_id=1, source_target_pairs={{0,1},{1,0},{2,3},{3,2},{4,5},{5,4},{6,7},{7,6},{8,9},{9,8},{10,11... | collective-permute-start | bytes 393224 | tf_op jit(solution)/shard_map/ppermute | solution.py:40
  11.1 0.8 %project_own.2.diag_ref = f32[256,128]{1,0:T(8,128)S(1)} custom-call(bf16[2048,1024]{1,0:T(8,128)(2,1)S(1)} %load.1.refs_0_.factor_ref, bf16[4,128,128]{2,1,0:T(8,128)(2,1)S(1)} %join.2.refs_0_), custom_call_target="tpu_custom_call" | custom-call | flops 268435456 | bytes 2097152 | tf_op jit(solution)/shard_map/project_own/pallas_call | solution.py:304
  11.9 0.2 collective-permute-done.3.fields_ref
  12.1 1.2 %project_across.2 = (bf16[192,128]{1,0:T(8,128)(2,1)S(1)}, bf16[64,128]{1,0:T(8,128)(2,1)S(1)}, f32[128,128]{1,0:T(8,128)S(1)}) custom-call(f32[128,128]{1,0:T(8,128)S(1)} %bitcast.8, bf16[2048,1024]{1,0:T(8,128)(2,1)S(1)} %load.1.refs_0_.factor_ref, f32[256,128]{1,0:T(8,128)S(1)} %project_own.2.diag_ref, ...), custom_call_target="tpu_custom_call" | custom-call | flops 268435456 | bytes 2097152 | tf_op jit(solution)/shard_map/project_across/pallas_call | solution.py:329
  13.3 2.5 %collective-permute-start.5 = (bf16[192,128]{1,0:T(8,128)(2,1)S(1)}, bf16[192,128]{1,0:T(8,128)(2,1)S(1)}, u32[]{:S(2)}, u32[]{:S(2)}) collective-permute-start(bf16[192,128]{1,0:T(8,128)(2,1)S(1)} %get-tuple-element.29), channel_id=1, source_target_pairs={{0,24},{8,16},{16,8},{24,0},{1,25},{9,17},{17,9},{25,1},{2,26},{10... | collective-permute-start | bytes 147464 | tf_op jit(solution)/shard_map/ppermute | solution.py:40
  15.7 0.5 collective-permute-start.4
  16.3 0.5 collective-permute-start.6
  16.8 3.2 %collective-permute-done.6.refs_2_ = bf16[64,128]{1,0:T(8,128)(2,1)S(1)} collective-permute-done((bf16[64,128]{1,0:T(8,128)(2,1)S(1)}, bf16[64,128]{1,0:T(8,128)(2,1)S(1)}, u32[]{:S(2)}, u32[]{:S(2)}) %collective-permute-start.6) | collective-permute-done | bytes 16416 | tf_op jit(solution)/shard_map/ppermute | solution.py:40
  20.0 0.0 collective-permute-done.5.refs_1_.refs_3_
  20.0 0.0 collective-permute-done.4.refs_0_.refs_1_
  20.0 0.7 %term_first.2 = (bf16[128,2048]{1,0:T(8,128)(2,1)S(1)}, bf16[2,128,128]{2,1,0:T(8,128)(2,1)S(1)}) custom-call(f32[1,256]{1,0:T(1,128)S(1)} %bitcast.13, bf16[2048,1024]{1,0:T(8,128)(2,1)S(1)} %load.1.refs_0_.factor_ref, bf16[64,128]{1,0:T(8,128)(2,1)S(1)} %get-tuple-element.30.refs_0_, bf16[192,128]{1,0:T(8,128)(2,1)S(1)} %collective-permute-done.4.refs_0_.refs_1_, ...), custom_call_target="tpu_custom_call" | custom-call | flops 134217728 | bytes 2097152 | tf_op jit(solution)/shard_map/term_first/pallas_call | solution.py:342
  20.8 0.1 collective-permute-start.7
  20.8 0.0 copy-start.2
  20.8 0.8 %term.4 = (f32[2,128,128]{2,1,0:T(8,128)S(1)}, bf16[2,128,128]{2,1,0:T(8,128)(2,1)S(1)}) custom-call(bf16[128,2048]{1,0:T(8,128)(2,1)S(1)} %get-tuple-element.31.coef_ref, bf16[2048,1024]{1,0:T(8,128)(2,1)S(1)} %load.1.refs_0_.factor_ref), custom_call_target="tpu_custom_call" | custom-call | flops 268435456 | bytes 2097152 | tf_op jit(solution)/shard_map/term/pallas_call | solution.py:352
  21.7 0.5 %collective-permute-start.8 = (bf16[2,128,128]{2,1,0:T(8,128)(2,1)S(1)}, bf16[2,128,128]{2,1,0:T(8,128)(2,1)S(1)}, u32[]{:S(2)}, u32[]{:S(2)}) collective-permute-start(bf16[2,128,128]{2,1,0:T(8,128)(2,1)S(1)} %get-tuple-element.36), channel_id=1, source_target_pairs={{0,1},{1,0},{2,3},{3,2},{4,5},{5,4},{6,7},{7,6},{8,9},{9,8},{10,11... | collective-permute-start | bytes 196616 | tf_op jit(solution)/shard_map/ppermute | solution.py:40
  22.2 0.0 collective-permute-done.7.got_ref
  22.2 2.2 %collective-permute-start.9 = (bf16[1,128,128]{2,1,0:T(8,128)(2,1)S(1)}, bf16[1,128,128]{2,1,0:T(8,128)(2,1)S(1)}, u32[]{:S(2)}, u32[]{:S(2)}) collective-permute-start(bf16[1,128,128]{2,1,0:T(8,128)(2,1)S(1)} %get-tuple-element.34.refs_0_), channel_id=1, source_target_pairs={{0,7},{1,6},{2,5},{3,4},{4,3},{5,2},{6,1},{7,0},{8,15},{9,14},{10,... | collective-permute-start | bytes 98312 | tf_op jit(solution)/shard_map/ppermute | solution.py:40
  24.4 0.0 collective-permute-start.10
  24.4 0.5 term.5.mine_ref
  24.9 0.0 collective-permute-done.8.got_ref
  24.9 1.7 %collective-permute-start.11 = (bf16[1,128,128]{2,1,0:T(8,128)(2,1)S(1)}, bf16[1,128,128]{2,1,0:T(8,128)(2,1)S(1)}, u32[]{:S(2)}, u32[]{:S(2)}) collective-permute-start(bf16[1,128,128]{2,1,0:T(8,128)(2,1)S(1)} %get-tuple-element.38), channel_id=1, source_target_pairs={{0,3},{1,2},{2,1},{3,0},{4,7},{5,6},{6,5},{7,4},{8,11},{9,10},{10,... | collective-permute-start | bytes 98312 | tf_op jit(solution)/shard_map/ppermute | solution.py:40
  26.6 0.2 local.2.base_ref
  26.8 0.7 %collective-permute-done.9.refs_1_ = bf16[1,128,128]{2,1,0:T(8,128)(2,1)S(1)} collective-permute-done((bf16[1,128,128]{2,1,0:T(8,128)(2,1)S(1)}, bf16[1,128,128]{2,1,0:T(8,128)(2,1)S(1)}, u32[]{:S(2)}, u32[]{:S(2)}) %collective-permute-start.9) | collective-permute-done | bytes 32800 | tf_op jit(solution)/shard_map/ppermute | solution.py:40
  27.6 1.3 %collective-permute-done.10.refs_2_ = bf16[1,128,128]{2,1,0:T(8,128)(2,1)S(1)} collective-permute-done((bf16[1,128,128]{2,1,0:T(8,128)(2,1)S(1)}, bf16[1,128,128]{2,1,0:T(8,128)(2,1)S(1)}, u32[]{:S(2)}, u32[]{:S(2)}) %collective-permute-start.10) | collective-permute-done | bytes 32800 | tf_op jit(solution)/shard_map/ppermute | solution.py:40
  28.8 0.0 collective-permute-done.11.refs_3_
  28.9 2.6 %collective-permute-start.14 = (bf16[1,128,128]{2,1,0:T(8,128)(2,1)S(1)}, bf16[1,128,128]{2,1,0:T(8,128)(2,1)S(1)}, u32[]{:S(2)}, u32[]{:S(2)}) collective-permute-start(bf16[1,128,128]{2,1,0:T(8,128)(2,1)S(1)} %get-tuple-element.40.refs_1_), channel_id=1, source_target_pairs={{0,7},{1,6},{2,5},{3,4},{4,3},{5,2},{6,1},{7,0},{8,15},{9,14},{10,... | collective-permute-start | bytes 98312 | tf_op jit(solution)/shard_map/ppermute | solution.py:40
  31.5 0.3 collective-permute-start.13
  31.8 1.4 %collective-permute-start.12 = (bf16[1,128,128]{2,1,0:T(8,128)(2,1)S(1)}, bf16[1,128,128]{2,1,0:T(8,128)(2,1)S(1)}, u32[]{:S(2)}, u32[]{:S(2)}) collective-permute-start(bf16[1,128,128]{2,1,0:T(8,128)(2,1)S(1)} %get-tuple-element.40.refs_1_), channel_id=1, source_target_pairs={{0,3},{1,2},{2,1},{3,0},{4,7},{5,6},{6,5},{7,4},{8,11},{9,10},{10,... | collective-permute-start | bytes 98312 | tf_op jit(solution)/shard_map/ppermute | solution.py:40
  33.2 0.9 %collective-permute-done.14.refs_4_ = bf16[1,128,128]{2,1,0:T(8,128)(2,1)S(1)} collective-permute-done((bf16[1,128,128]{2,1,0:T(8,128)(2,1)S(1)}, bf16[1,128,128]{2,1,0:T(8,128)(2,1)S(1)}, u32[]{:S(2)}, u32[]{:S(2)}) %collective-permute-start.14) | collective-permute-done | bytes 32800 | tf_op jit(solution)/shard_map/ppermute | solution.py:40
  34.1 2.2 %collective-permute-done.13.refs_3_ = bf16[1,128,128]{2,1,0:T(8,128)(2,1)S(1)} collective-permute-done((bf16[1,128,128]{2,1,0:T(8,128)(2,1)S(1)}, bf16[1,128,128]{2,1,0:T(8,128)(2,1)S(1)}, u32[]{:S(2)}, u32[]{:S(2)}) %collective-permute-start.13) | collective-permute-done | bytes 32800 | tf_op jit(solution)/shard_map/ppermute | solution.py:40
  36.3 0.0 collective-permute-done.12.refs_2_
  36.3 0.2 collective-permute-start.15
  36.5 0.8 %project_own.3.diag_ref = f32[256,128]{1,0:T(8,128)S(1)} custom-call(bf16[2048,1024]{1,0:T(8,128)(2,1)S(1)} %load.1.refs_0_.factor_ref, bf16[4,128,128]{2,1,0:T(8,128)(2,1)S(1)} %join.3.refs_0_), custom_call_target="tpu_custom_call" | custom-call | flops 268435456 | bytes 2097152 | tf_op jit(solution)/shard_map/project_own/pallas_call | solution.py:304
  37.3 0.4 collective-permute-done.15.fields_ref
  37.8 1.1 %project_across.3 = (bf16[192,128]{1,0:T(8,128)(2,1)S(1)}, bf16[64,128]{1,0:T(8,128)(2,1)S(1)}, f32[128,128]{1,0:T(8,128)S(1)}) custom-call(f32[128,128]{1,0:T(8,128)S(1)} %get-tuple-element.39.x_ref, bf16[2048,1024]{1,0:T(8,128)(2,1)S(1)} %load.1.refs_0_.factor_ref, f32[256,128]{1,0:T(8,128)S(1)} %project_own.3.diag_ref, ...), custom_call_target="tpu_custom_call" | custom-call | flops 268435456 | bytes 2097152 | tf_op jit(solution)/shard_map/project_across/pallas_call | solution.py:329
  38.9 1.5 %collective-permute-start.17 = (bf16[192,128]{1,0:T(8,128)(2,1)S(1)}, bf16[192,128]{1,0:T(8,128)(2,1)S(1)}, u32[]{:S(2)}, u32[]{:S(2)}) collective-permute-start(bf16[192,128]{1,0:T(8,128)(2,1)S(1)} %get-tuple-element.42), channel_id=1, source_target_pairs={{0,24},{8,16},{16,8},{24,0},{1,25},{9,17},{17,9},{25,1},{2,26},{10... | collective-permute-start | bytes 147464 | tf_op jit(solution)/shard_map/ppermute | solution.py:40
  40.3 0.5 collective-permute-start.16
  40.9 1.5 %collective-permute-start.18 = (bf16[64,128]{1,0:T(8,128)(2,1)S(1)}, bf16[64,128]{1,0:T(8,128)(2,1)S(1)}, u32[]{:S(2)}, u32[]{:S(2)}) collective-permute-start(bf16[64,128]{1,0:T(8,128)(2,1)S(1)} %get-tuple-element.43.refs_0_), channel_id=1, source_target_pairs={{0,16},{8,24},{16,0},{24,8},{1,17},{9,25},{17,1},{25,9},{2,18},{10... | collective-permute-start | bytes 49160 | tf_op jit(solution)/shard_map/ppermute | solution.py:40
  42.4 2.2 %collective-permute-done.18.refs_2_ = bf16[64,128]{1,0:T(8,128)(2,1)S(1)} collective-permute-done((bf16[64,128]{1,0:T(8,128)(2,1)S(1)}, bf16[64,128]{1,0:T(8,128)(2,1)S(1)}, u32[]{:S(2)}, u32[]{:S(2)}) %collective-permute-start.18) | collective-permute-done | bytes 16416 | tf_op jit(solution)/shard_map/ppermute | solution.py:40
  44.6 0.0 collective-permute-done.17.refs_1_.refs_3_
  44.6 0.0 collective-permute-done.16.refs_0_.refs_1_
  44.6 0.7 %term_first.3 = (bf16[128,2048]{1,0:T(8,128)(2,1)S(1)}, bf16[2,128,128]{2,1,0:T(8,128)(2,1)S(1)}) custom-call(f32[1,256]{1,0:T(1,128)S(1)} %bitcast.14, bf16[2048,1024]{1,0:T(8,128)(2,1)S(1)} %load.1.refs_0_.factor_ref, bf16[64,128]{1,0:T(8,128)(2,1)S(1)} %get-tuple-element.43.refs_0_, bf16[192,128]{1,0:T(8,128)(2,1)S(1)} %collective-permute-done.16.refs_0_.refs_1_, ...), custom_call_target="tpu_custom_call" | custom-call | flops 134217728 | bytes 2097152 | tf_op jit(solution)/shard_map/term_first/pallas_call | solution.py:342
  45.4 0.1 collective-permute-start.19
  45.4 0.8 %term.6 = (f32[2,128,128]{2,1,0:T(8,128)S(1)}, bf16[2,128,128]{2,1,0:T(8,128)(2,1)S(1)}) custom-call(bf16[128,2048]{1,0:T(8,128)(2,1)S(1)} %get-tuple-element.44.coef_ref, bf16[2048,1024]{1,0:T(8,128)(2,1)S(1)} %load.1.refs_0_.factor_ref), custom_call_target="tpu_custom_call" | custom-call | flops 268435456 | bytes 2097152 | tf_op jit(solution)/shard_map/term/pallas_call | solution.py:352
  46.2 0.6 %collective-permute-start.20 = (bf16[2,128,128]{2,1,0:T(8,128)(2,1)S(1)}, bf16[2,128,128]{2,1,0:T(8,128)(2,1)S(1)}, u32[]{:S(2)}, u32[]{:S(2)}) collective-permute-start(bf16[2,128,128]{2,1,0:T(8,128)(2,1)S(1)} %get-tuple-element.49), channel_id=1, source_target_pairs={{0,1},{1,0},{2,3},{3,2},{4,5},{5,4},{6,7},{7,6},{8,9},{9,8},{10,11... | collective-permute-start | bytes 196616 | tf_op jit(solution)/shard_map/ppermute | solution.py:40
  46.8 2.1 %collective-permute-start.21 = (bf16[1,128,128]{2,1,0:T(8,128)(2,1)S(1)}, bf16[1,128,128]{2,1,0:T(8,128)(2,1)S(1)}, u32[]{:S(2)}, u32[]{:S(2)}) collective-permute-start(bf16[1,128,128]{2,1,0:T(8,128)(2,1)S(1)} %get-tuple-element.47.refs_0_), channel_id=1, source_target_pairs={{0,7},{1,6},{2,5},{3,4},{4,3},{5,2},{6,1},{7,0},{8,15},{9,14},{10,... | collective-permute-start | bytes 98312 | tf_op jit(solution)/shard_map/ppermute | solution.py:40
  48.9 0.0 collective-permute-start.22
  48.9 0.5 term.7.mine_ref
  49.5 1.8 %collective-permute-start.23 = (bf16[1,128,128]{2,1,0:T(8,128)(2,1)S(1)}, bf16[1,128,128]{2,1,0:T(8,128)(2,1)S(1)}, u32[]{:S(2)}, u32[]{:S(2)}) collective-permute-start(bf16[1,128,128]{2,1,0:T(8,128)(2,1)S(1)} %get-tuple-element.51), channel_id=1, source_target_pairs={{0,3},{1,2},{2,1},{3,0},{4,7},{5,6},{6,5},{7,4},{8,11},{9,10},{10,... | collective-permute-start | bytes 98312 | tf_op jit(solution)/shard_map/ppermute | solution.py:40
  51.2 0.2 local.3.base_ref
  51.4 0.8 %collective-permute-done.21.refs_1_ = bf16[1,128,128]{2,1,0:T(8,128)(2,1)S(1)} collective-permute-done((bf16[1,128,128]{2,1,0:T(8,128)(2,1)S(1)}, bf16[1,128,128]{2,1,0:T(8,128)(2,1)S(1)}, u32[]{:S(2)}, u32[]{:S(2)}) %collective-permute-start.21) | collective-permute-done | bytes 32800 | tf_op jit(solution)/shard_map/ppermute | solution.py:40
  52.2 1.3 %collective-permute-done.22.refs_2_ = bf16[1,128,128]{2,1,0:T(8,128)(2,1)S(1)} collective-permute-done((bf16[1,128,128]{2,1,0:T(8,128)(2,1)S(1)}, bf16[1,128,128]{2,1,0:T(8,128)(2,1)S(1)}, u32[]{:S(2)}, u32[]{:S(2)}) %collective-permute-start.22) | collective-permute-done | bytes 32800 | tf_op jit(solution)/shard_map/ppermute | solution.py:40
  53.5 0.7 %update.3 = (f32[128,128]{1,0:T(8,128)}, f32[128,128]{1,0:T(8,128)}) custom-call(f32[128,128]{1,0:T(8,128)S(1)} %get-tuple-element.39.x_ref, f32[128,128]{1,0:T(8,128)S(1)} %local.3.base_ref, f32[1,128,128]{2,1,0:T(8,128)S(1)} %get-tuple-element.50.refs_0_, bf16[1,128,128]{2,1,0:T(8,128)(2,1)S(1)} %collective-permute-done.21.refs_1_, ...), custom_call_target="tpu_custom_call" | custom-call | bytes 262144 | tf_op jit(solution)/shard_map/update/pallas_call | solution.py:381
  (14 shorter events, 0.1 us)
Async XLA Ops:
  1.5 7.9 %collective-permute-start.2 = (bf16[1,128,128]{2,1,0:T(8,128)(2,1)S(1)}, bf16[1,128,128]{2,1,0:T(8,128)(2,1)S(1)}, u32[]{:S(2)}, u32[]{:S(2)}) collective-permute-start(bf16[1,128,128]{2,1,0:T(8,128)(2,1)S(1)} %fusion.refs_1_), channel_id=1, source_target_pairs={{0,5},{1,4},{2,7},{3,6},{4,1},{5,0},{6,3},{7,2},{8,13},{9,12},{10,... | collective-permute-start | bytes 98312 | tf_op jit(solution)/shard_map/ppermute | solution.py:40
  5.0 5.2 %collective-permute-start.1 = (bf16[1,128,128]{2,1,0:T(8,128)(2,1)S(1)}, bf16[1,128,128]{2,1,0:T(8,128)(2,1)S(1)}, u32[]{:S(2)}, u32[]{:S(2)}) collective-permute-start(bf16[1,128,128]{2,1,0:T(8,128)(2,1)S(1)} %fusion.refs_1_), channel_id=1, source_target_pairs={{0,7},{1,6},{2,5},{3,4},{4,3},{5,2},{6,1},{7,0},{8,15},{9,14},{10,... | collective-permute-start | bytes 98312 | tf_op jit(solution)/shard_map/ppermute | solution.py:40
  6.6 3.8 %collective-permute-start = (bf16[1,128,128]{2,1,0:T(8,128)(2,1)S(1)}, bf16[1,128,128]{2,1,0:T(8,128)(2,1)S(1)}, u32[]{:S(2)}, u32[]{:S(2)}) collective-permute-start(bf16[1,128,128]{2,1,0:T(8,128)(2,1)S(1)} %fusion.refs_1_), channel_id=1, source_target_pairs={{0,3},{1,2},{2,1},{3,0},{4,7},{5,6},{6,5},{7,4},{8,11},{9,10},{10,... | collective-permute-start | bytes 98312 | tf_op jit(solution)/shard_map/ppermute | solution.py:40
  6.8 2.2 %copy-start = (bf16[256,8,1024]{2,1,0:T(8,128)(2,1)S(1)}, bf16[256,8,1024]{2,1,0:T(8,128)(2,1)}, u32[]{:S(2)}) copy-start(bf16[256,8,1024]{2,1,0:T(8,128)(2,1)} %param.6) | copy-start | bytes 12582916
  9.4 2.7 %copy-start.1 = (f32[16,8,128]{2,1,0:T(8,128)S(1)}, f32[16,8,128]{2,1,0:T(8,128)}, u32[]{:S(2)}) copy-start(f32[16,8,128]{2,1,0:T(8,128)} %param.4) | copy-start | bytes 196612
  10.4 9.7 %copy-start.3 = (f32[256]{0:T(256)S(1)}, f32[256]{0:T(256)}, u32[]{:S(2)}) copy-start(f32[256]{0:T(256)} %param.7) | copy-start | bytes 3076
  10.4 1.7 %collective-permute-start.3 = (bf16[4,128,128]{2,1,0:T(8,128)(2,1)S(1)}, bf16[4,128,128]{2,1,0:T(8,128)(2,1)S(1)}, u32[]{:S(2)}, u32[]{:S(2)}) collective-permute-start(bf16[4,128,128]{2,1,0:T(8,128)(2,1)S(1)} %join.2.refs_0_), channel_id=1, source_target_pairs={{0,1},{1,0},{2,3},{3,2},{4,5},{5,4},{6,7},{7,6},{8,9},{9,8},{10,11... | collective-permute-start | bytes 393224 | tf_op jit(solution)/shard_map/ppermute | solution.py:40
  13.3 6.8 %collective-permute-start.5 = (bf16[192,128]{1,0:T(8,128)(2,1)S(1)}, bf16[192,128]{1,0:T(8,128)(2,1)S(1)}, u32[]{:S(2)}, u32[]{:S(2)}) collective-permute-start(bf16[192,128]{1,0:T(8,128)(2,1)S(1)} %get-tuple-element.29), channel_id=1, source_target_pairs={{0,24},{8,16},{16,8},{24,0},{1,25},{9,17},{17,9},{25,1},{2,26},{10... | collective-permute-start | bytes 147464 | tf_op jit(solution)/shard_map/ppermute | solution.py:40
  15.7 4.3 %collective-permute-start.4 = (bf16[192,128]{1,0:T(8,128)(2,1)S(1)}, bf16[192,128]{1,0:T(8,128)(2,1)S(1)}, u32[]{:S(2)}, u32[]{:S(2)}) collective-permute-start(bf16[192,128]{1,0:T(8,128)(2,1)S(1)} %get-tuple-element.29), channel_id=1, source_target_pairs={{0,8},{8,0},{16,24},{24,16},{1,9},{9,1},{17,25},{25,17},{2,10},{10... | collective-permute-start | bytes 147464 | tf_op jit(solution)/shard_map/ppermute | solution.py:40
  16.3 3.7 %collective-permute-start.6 = (bf16[64,128]{1,0:T(8,128)(2,1)S(1)}, bf16[64,128]{1,0:T(8,128)(2,1)S(1)}, u32[]{:S(2)}, u32[]{:S(2)}) collective-permute-start(bf16[64,128]{1,0:T(8,128)(2,1)S(1)} %get-tuple-element.30.refs_0_), channel_id=1, source_target_pairs={{0,16},{8,24},{16,0},{24,8},{1,17},{9,25},{17,1},{25,9},{2,18},{10... | collective-permute-start | bytes 49160 | tf_op jit(solution)/shard_map/ppermute | solution.py:40
  20.8 1.4 %collective-permute-start.7 = (bf16[2,128,128]{2,1,0:T(8,128)(2,1)S(1)}, bf16[2,128,128]{2,1,0:T(8,128)(2,1)S(1)}, u32[]{:S(2)}, u32[]{:S(2)}) collective-permute-start(bf16[2,128,128]{2,1,0:T(8,128)(2,1)S(1)} %get-tuple-element.33), channel_id=1, source_target_pairs={{0,1},{1,0},{2,3},{3,2},{4,5},{5,4},{6,7},{7,6},{8,9},{9,8},{10,11... | collective-permute-start | bytes 196616 | tf_op jit(solution)/shard_map/ppermute | solution.py:40
  20.8 5.8 %copy-start.2 = (f32[8,128]{1,0:T(8,128)S(1)}, f32[8,128]{1,0:T(8,128)}, u32[]{:S(2)}) copy-start(f32[8,128]{1,0:T(8,128)} %amp_ref.3) | copy-start | bytes 12292
  21.7 3.2 %collective-permute-start.8 = (bf16[2,128,128]{2,1,0:T(8,128)(2,1)S(1)}, bf16[2,128,128]{2,1,0:T(8,128)(2,1)S(1)}, u32[]{:S(2)}, u32[]{:S(2)}) collective-permute-start(bf16[2,128,128]{2,1,0:T(8,128)(2,1)S(1)} %get-tuple-element.36), channel_id=1, source_target_pairs={{0,1},{1,0},{2,3},{3,2},{4,5},{5,4},{6,7},{7,6},{8,9},{9,8},{10,11... | collective-permute-start | bytes 196616 | tf_op jit(solution)/shard_map/ppermute | solution.py:40
  22.2 5.3 %collective-permute-start.9 = (bf16[1,128,128]{2,1,0:T(8,128)(2,1)S(1)}, bf16[1,128,128]{2,1,0:T(8,128)(2,1)S(1)}, u32[]{:S(2)}, u32[]{:S(2)}) collective-permute-start(bf16[1,128,128]{2,1,0:T(8,128)(2,1)S(1)} %get-tuple-element.34.refs_0_), channel_id=1, source_target_pairs={{0,7},{1,6},{2,5},{3,4},{4,3},{5,2},{6,1},{7,0},{8,15},{9,14},{10,... | collective-permute-start | bytes 98312 | tf_op jit(solution)/shard_map/ppermute | solution.py:40
  24.4 4.5 %collective-permute-start.10 = (bf16[1,128,128]{2,1,0:T(8,128)(2,1)S(1)}, bf16[1,128,128]{2,1,0:T(8,128)(2,1)S(1)}, u32[]{:S(2)}, u32[]{:S(2)}) collective-permute-start(bf16[1,128,128]{2,1,0:T(8,128)(2,1)S(1)} %get-tuple-element.35.refs_1_), channel_id=1, source_target_pairs={{0,5},{1,4},{2,7},{3,6},{4,1},{5,0},{6,3},{7,2},{8,13},{9,12},{10,... | collective-permute-start | bytes 98312 | tf_op jit(solution)/shard_map/ppermute | solution.py:40
  24.9 3.9 %collective-permute-start.11 = (bf16[1,128,128]{2,1,0:T(8,128)(2,1)S(1)}, bf16[1,128,128]{2,1,0:T(8,128)(2,1)S(1)}, u32[]{:S(2)}, u32[]{:S(2)}) collective-permute-start(bf16[1,128,128]{2,1,0:T(8,128)(2,1)S(1)} %get-tuple-element.38), channel_id=1, source_target_pairs={{0,3},{1,2},{2,1},{3,0},{4,7},{5,6},{6,5},{7,4},{8,11},{9,10},{10,... | collective-permute-start | bytes 98312 | tf_op jit(solution)/shard_map/ppermute | solution.py:40
  28.9 5.2 %collective-permute-start.14 = (bf16[1,128,128]{2,1,0:T(8,128)(2,1)S(1)}, bf16[1,128,128]{2,1,0:T(8,128)(2,1)S(1)}, u32[]{:S(2)}, u32[]{:S(2)}) collective-permute-start(bf16[1,128,128]{2,1,0:T(8,128)(2,1)S(1)} %get-tuple-element.40.refs_1_), channel_id=1, source_target_pairs={{0,7},{1,6},{2,5},{3,4},{4,3},{5,2},{6,1},{7,0},{8,15},{9,14},{10,... | collective-permute-start | bytes 98312 | tf_op jit(solution)/shard_map/ppermute | solution.py:40
  31.5 4.8 %collective-permute-start.13 = (bf16[1,128,128]{2,1,0:T(8,128)(2,1)S(1)}, bf16[1,128,128]{2,1,0:T(8,128)(2,1)S(1)}, u32[]{:S(2)}, u32[]{:S(2)}) collective-permute-start(bf16[1,128,128]{2,1,0:T(8,128)(2,1)S(1)} %get-tuple-element.40.refs_1_), channel_id=1, source_target_pairs={{0,5},{1,4},{2,7},{3,6},{4,1},{5,0},{6,3},{7,2},{8,13},{9,12},{10,... | collective-permute-start | bytes 98312 | tf_op jit(solution)/shard_map/ppermute | solution.py:40
  31.8 4.5 %collective-permute-start.12 = (bf16[1,128,128]{2,1,0:T(8,128)(2,1)S(1)}, bf16[1,128,128]{2,1,0:T(8,128)(2,1)S(1)}, u32[]{:S(2)}, u32[]{:S(2)}) collective-permute-start(bf16[1,128,128]{2,1,0:T(8,128)(2,1)S(1)} %get-tuple-element.40.refs_1_), channel_id=1, source_target_pairs={{0,3},{1,2},{2,1},{3,0},{4,7},{5,6},{6,5},{7,4},{8,11},{9,10},{10,... | collective-permute-start | bytes 98312 | tf_op jit(solution)/shard_map/ppermute | solution.py:40
  36.3 1.4 %collective-permute-start.15 = (bf16[4,128,128]{2,1,0:T(8,128)(2,1)S(1)}, bf16[4,128,128]{2,1,0:T(8,128)(2,1)S(1)}, u32[]{:S(2)}, u32[]{:S(2)}) collective-permute-start(bf16[4,128,128]{2,1,0:T(8,128)(2,1)S(1)} %join.3.refs_0_), channel_id=1, source_target_pairs={{0,1},{1,0},{2,3},{3,2},{4,5},{5,4},{6,7},{7,6},{8,9},{9,8},{10,11... | collective-permute-start | bytes 393224 | tf_op jit(solution)/shard_map/ppermute | solution.py:40
  38.9 5.7 %collective-permute-start.17 = (bf16[192,128]{1,0:T(8,128)(2,1)S(1)}, bf16[192,128]{1,0:T(8,128)(2,1)S(1)}, u32[]{:S(2)}, u32[]{:S(2)}) collective-permute-start(bf16[192,128]{1,0:T(8,128)(2,1)S(1)} %get-tuple-element.42), channel_id=1, source_target_pairs={{0,24},{8,16},{16,8},{24,0},{1,25},{9,17},{17,9},{25,1},{2,26},{10... | collective-permute-start | bytes 147464 | tf_op jit(solution)/shard_map/ppermute | solution.py:40
  40.3 4.3 %collective-permute-start.16 = (bf16[192,128]{1,0:T(8,128)(2,1)S(1)}, bf16[192,128]{1,0:T(8,128)(2,1)S(1)}, u32[]{:S(2)}, u32[]{:S(2)}) collective-permute-start(bf16[192,128]{1,0:T(8,128)(2,1)S(1)} %get-tuple-element.42), channel_id=1, source_target_pairs={{0,8},{8,0},{16,24},{24,16},{1,9},{9,1},{17,25},{25,17},{2,10},{10... | collective-permute-start | bytes 147464 | tf_op jit(solution)/shard_map/ppermute | solution.py:40
  40.9 3.7 %collective-permute-start.18 = (bf16[64,128]{1,0:T(8,128)(2,1)S(1)}, bf16[64,128]{1,0:T(8,128)(2,1)S(1)}, u32[]{:S(2)}, u32[]{:S(2)}) collective-permute-start(bf16[64,128]{1,0:T(8,128)(2,1)S(1)} %get-tuple-element.43.refs_0_), channel_id=1, source_target_pairs={{0,16},{8,24},{16,0},{24,8},{1,17},{9,25},{17,1},{25,9},{2,18},{10... | collective-permute-start | bytes 49160 | tf_op jit(solution)/shard_map/ppermute | solution.py:40
  45.4 1.4 %collective-permute-start.19 = (bf16[2,128,128]{2,1,0:T(8,128)(2,1)S(1)}, bf16[2,128,128]{2,1,0:T(8,128)(2,1)S(1)}, u32[]{:S(2)}, u32[]{:S(2)}) collective-permute-start(bf16[2,128,128]{2,1,0:T(8,128)(2,1)S(1)} %get-tuple-element.46), channel_id=1, source_target_pairs={{0,1},{1,0},{2,3},{3,2},{4,5},{5,4},{6,7},{7,6},{8,9},{9,8},{10,11... | collective-permute-start | bytes 196616 | tf_op jit(solution)/shard_map/ppermute | solution.py:40
  46.2 3.2 %collective-permute-start.20 = (bf16[2,128,128]{2,1,0:T(8,128)(2,1)S(1)}, bf16[2,128,128]{2,1,0:T(8,128)(2,1)S(1)}, u32[]{:S(2)}, u32[]{:S(2)}) collective-permute-start(bf16[2,128,128]{2,1,0:T(8,128)(2,1)S(1)} %get-tuple-element.49), channel_id=1, source_target_pairs={{0,1},{1,0},{2,3},{3,2},{4,5},{5,4},{6,7},{7,6},{8,9},{9,8},{10,11... | collective-permute-start | bytes 196616 | tf_op jit(solution)/shard_map/ppermute | solution.py:40
  46.8 5.3 %collective-permute-start.21 = (bf16[1,128,128]{2,1,0:T(8,128)(2,1)S(1)}, bf16[1,128,128]{2,1,0:T(8,128)(2,1)S(1)}, u32[]{:S(2)}, u32[]{:S(2)}) collective-permute-start(bf16[1,128,128]{2,1,0:T(8,128)(2,1)S(1)} %get-tuple-element.47.refs_0_), channel_id=1, source_target_pairs={{0,7},{1,6},{2,5},{3,4},{4,3},{5,2},{6,1},{7,0},{8,15},{9,14},{10,... | collective-permute-start | bytes 98312 | tf_op jit(solution)/shard_map/ppermute | solution.py:40
  48.9 4.5 %collective-permute-start.22 = (bf16[1,128,128]{2,1,0:T(8,128)(2,1)S(1)}, bf16[1,128,128]{2,1,0:T(8,128)(2,1)S(1)}, u32[]{:S(2)}, u32[]{:S(2)}) collective-permute-start(bf16[1,128,128]{2,1,0:T(8,128)(2,1)S(1)} %get-tuple-element.48.refs_1_), channel_id=1, source_target_pairs={{0,5},{1,4},{2,7},{3,6},{4,1},{5,0},{6,3},{7,2},{8,13},{9,12},{10,... | collective-permute-start | bytes 98312 | tf_op jit(solution)/shard_map/ppermute | solution.py:40
  49.5 4.0 %collective-permute-start.23 = (bf16[1,128,128]{2,1,0:T(8,128)(2,1)S(1)}, bf16[1,128,128]{2,1,0:T(8,128)(2,1)S(1)}, u32[]{:S(2)}, u32[]{:S(2)}) collective-permute-start(bf16[1,128,128]{2,1,0:T(8,128)(2,1)S(1)} %get-tuple-element.51), channel_id=1, source_target_pairs={{0,3},{1,2},{2,1},{3,0},{4,7},{5,6},{6,5},{7,4},{8,11},{9,10},{10,... | collective-permute-start | bytes 98312 | tf_op jit(solution)/shard_map/ppermute | solution.py:40

commit v7 on v6

--- a/solution.py
+++ b/solution.py
@@ -292,7 +292,7 @@
         name="load",
     )(flat)
     half = near // 2
-    close, away = list(range(half)), list(range(near - 1, half - 1, -1))
+    close, away = list(range(half)), list(range(half, near))
 
     def spots_of(masks, other):
         return [(mask, other != (mask > 0)) for mask in masks]
@@ -312,8 +312,7 @@
     for step in range(ITERS):
         halve = step == 0
         order = list(range(1, near))
-        if step == 0:
-            order.sort(key=lambda mask: (mask == near // 2, mask))
+        order.sort(key=lambda mask: (mask == half, mask))
         parts = [cross(short, mask) for mask in order]
         bundle = call(
             join_kernel,

time: 54.4 us -> 54.7 us (level)
  waiting for transfers between devices: 14.2 us -> 17.2 us
  starting transfers between devices: 26.5 us -> 24 us
    ppermute x24, waiting for transfers between devices: 14.2 us -> 17.2 us  [swap(): lax.ppermute(value, axis, [(i, i ^ mask) for i in range(lax.axis_size(axi...]
    ppermute x24, starting transfers between devices: 26.5 us -> 24 us  [swap(): lax.ppermute(value, axis, [(i, i ^ mask) for i in range(lax.axis_size(axi...]
  transfers between devices with their start and end apart: 24 -> 24, of which waited for: 12 -> 14; matrix products, arithmetic and copies ran while one was open for 0% -> 0% of each run, Pallas kernels for 9% -> 9%
where the time goes in v7:
time: 54.7 us; the launch traced here: 54.5 us
  starting transfers between devices  24 us (44%)
  waiting for transfers between devices  17.2 us (31%)
  Pallas kernels  9.47 us (17%)
  local copies, waits for them, and re-layouts  2.21 us (4%)
  other arithmetic  0.85 us (2%)
  between operations  0.83 us (2%)
    ppermute x24, starting transfers between devices, swap(): lax.ppermute(value, axis, [(i, i ^ mask) for i in range(lax.axis_size(axi...  24 us
    ppermute x24, waiting for transfers between devices, swap(): lax.ppermute(value, axis, [(i, i ^ mask) for i in range(lax.axis_size(axi...  17.2 us
    pallas_call x4, Pallas kernels, term(): call(partial(term_kernel, wanted, len(after)), in_specs=[pl.BlockSpec(mem...  2.59 us
    pallas_call x2, Pallas kernels, on_device(): call(partial(second_kernel, rows, cols, halve, spots, known), (shape(bf16...  2.3 us
    unnamed x8, local copies, waits for them, and re-layouts  2.21 us
    pallas_call x2, Pallas kernels, first(): call(partial(first_kernel, rows, spots, len(before)), shape(f32, blocks *...  1.62 us
    pallas_call x2, Pallas kernels, on_device(): call(partial(far_kernel, rows, cols, groups, ncells_all, spots_of(away, T...  1.45 us
  transfers between devices with their start and end apart: 24, of which 14 were waited for; matrix products, arithmetic and copies ran while one was open for 0% of the time, Pallas kernels for 9%

profile of v7, /device:TPU:0, one launch (start us, length us, event | category | flops | bytes accessed | tf_op | source)
XLA Modules:
  0.0 54.5 jit_solution(3011232570663776970)
XLA Ops:
  0.6 0.8 %fusion.refs_1_ = bf16[1,128,128]{2,1,0:T(8,128)(2,1)S(1)} fusion(f32[16,8,128]{2,1,0:T(8,128)} %param.4), kind=kLoop, calls=%fused_computation.1 | loop fusion | flops 32768 | bytes 98304 | tf_op jit(solution)/shard_map/convert_element_type | solution.py:267
  1.5 3.5 %collective-permute-start.2 = (bf16[1,128,128]{2,1,0:T(8,128)(2,1)S(1)}, bf16[1,128,128]{2,1,0:T(8,128)(2,1)S(1)}, u32[]{:S(2)}, u32[]{:S(2)}) collective-permute-start(bf16[1,128,128]{2,1,0:T(8,128)(2,1)S(1)} %fusion.refs_1_), channel_id=1, source_target_pairs={{0,5},{1,4},{2,7},{3,6},{4,1},{5,0},{6,3},{7,2},{8,13},{9,12},{10,... | collective-permute-start | bytes 98312 | tf_op jit(solution)/shard_map/ppermute | solution.py:40
  5.0 1.6 %collective-permute-start.1 = (bf16[1,128,128]{2,1,0:T(8,128)(2,1)S(1)}, bf16[1,128,128]{2,1,0:T(8,128)(2,1)S(1)}, u32[]{:S(2)}, u32[]{:S(2)}) collective-permute-start(bf16[1,128,128]{2,1,0:T(8,128)(2,1)S(1)} %fusion.refs_1_), channel_id=1, source_target_pairs={{0,7},{1,6},{2,5},{3,4},{4,3},{5,2},{6,1},{7,0},{8,15},{9,14},{10,... | collective-permute-start | bytes 98312 | tf_op jit(solution)/shard_map/ppermute | solution.py:40
  6.6 0.2 collective-permute-start
  6.8 2.2 %copy-done = bf16[256,8,1024]{2,1,0:T(8,128)(2,1)S(1)} copy-done((bf16[256,8,1024]{2,1,0:T(8,128)(2,1)S(1)}, bf16[256,8,1024]{2,1,0:T(8,128)(2,1)}, u32[]{:S(2)}) %copy-start) | copy-done | bytes 4194328
  9.0 0.4 load.1.refs_0_.factor_ref
  9.4 0.0 copy-start.1
  9.4 0.0 collective-permute-done.2.refs_4_
  9.4 0.8 %collective-permute-done.1.refs_3_ = bf16[1,128,128]{2,1,0:T(8,128)(2,1)S(1)} collective-permute-done((bf16[1,128,128]{2,1,0:T(8,128)(2,1)S(1)}, bf16[1,128,128]{2,1,0:T(8,128)(2,1)S(1)}, u32[]{:S(2)}, u32[]{:S(2)}) %collective-permute-start.1) | collective-permute-done | bytes 32800 | tf_op jit(solution)/shard_map/ppermute | solution.py:40
  10.2 0.2 collective-permute-done.refs_2_
  10.4 0.0 copy-start.3
  10.4 0.7 %collective-permute-start.3 = (bf16[4,128,128]{2,1,0:T(8,128)(2,1)S(1)}, bf16[4,128,128]{2,1,0:T(8,128)(2,1)S(1)}, u32[]{:S(2)}, u32[]{:S(2)}) collective-permute-start(bf16[4,128,128]{2,1,0:T(8,128)(2,1)S(1)} %join.2.refs_0_), channel_id=1, source_target_pairs={{0,1},{1,0},{2,3},{3,2},{4,5},{5,4},{6,7},{7,6},{8,9},{9,8},{10,11... | collective-permute-start | bytes 393224 | tf_op jit(solution)/shard_map/ppermute | solution.py:40
  11.1 0.8 %project_own.2.diag_ref = f32[256,128]{1,0:T(8,128)S(1)} custom-call(bf16[2048,1024]{1,0:T(8,128)(2,1)S(1)} %load.1.refs_0_.factor_ref, bf16[4,128,128]{2,1,0:T(8,128)(2,1)S(1)} %join.2.refs_0_), custom_call_target="tpu_custom_call" | custom-call | flops 268435456 | bytes 2097152 | tf_op jit(solution)/shard_map/project_own/pallas_call | solution.py:304
  11.9 0.2 collective-permute-done.3.fields_ref
  12.1 1.2 %project_across.2 = (bf16[192,128]{1,0:T(8,128)(2,1)S(1)}, bf16[64,128]{1,0:T(8,128)(2,1)S(1)}, f32[128,128]{1,0:T(8,128)S(1)}) custom-call(f32[128,128]{1,0:T(8,128)S(1)} %bitcast.8, bf16[2048,1024]{1,0:T(8,128)(2,1)S(1)} %load.1.refs_0_.factor_ref, f32[256,128]{1,0:T(8,128)S(1)} %project_own.2.diag_ref, ...), custom_call_target="tpu_custom_call" | custom-call | flops 268435456 | bytes 2097152 | tf_op jit(solution)/shard_map/project_across/pallas_call | solution.py:328
  13.3 2.5 %collective-permute-start.5 = (bf16[192,128]{1,0:T(8,128)(2,1)S(1)}, bf16[192,128]{1,0:T(8,128)(2,1)S(1)}, u32[]{:S(2)}, u32[]{:S(2)}) collective-permute-start(bf16[192,128]{1,0:T(8,128)(2,1)S(1)} %get-tuple-element.29), channel_id=1, source_target_pairs={{0,24},{8,16},{16,8},{24,0},{1,25},{9,17},{17,9},{25,1},{2,26},{10... | collective-permute-start | bytes 147464 | tf_op jit(solution)/shard_map/ppermute | solution.py:40
  15.7 0.5 collective-permute-start.4
  16.3 0.5 collective-permute-start.6
  16.8 3.2 %collective-permute-done.6.refs_2_ = bf16[64,128]{1,0:T(8,128)(2,1)S(1)} collective-permute-done((bf16[64,128]{1,0:T(8,128)(2,1)S(1)}, bf16[64,128]{1,0:T(8,128)(2,1)S(1)}, u32[]{:S(2)}, u32[]{:S(2)}) %collective-permute-start.6) | collective-permute-done | bytes 16416 | tf_op jit(solution)/shard_map/ppermute | solution.py:40
  20.0 0.0 collective-permute-done.5.refs_1_.refs_3_
  20.0 0.0 collective-permute-done.4.refs_0_.refs_1_
  20.0 0.7 %term_first.2 = (bf16[128,2048]{1,0:T(8,128)(2,1)S(1)}, bf16[2,128,128]{2,1,0:T(8,128)(2,1)S(1)}) custom-call(f32[1,256]{1,0:T(1,128)S(1)} %bitcast.13, bf16[2048,1024]{1,0:T(8,128)(2,1)S(1)} %load.1.refs_0_.factor_ref, bf16[64,128]{1,0:T(8,128)(2,1)S(1)} %get-tuple-element.30.refs_0_, bf16[192,128]{1,0:T(8,128)(2,1)S(1)} %collective-permute-done.4.refs_0_.refs_1_, ...), custom_call_target="tpu_custom_call" | custom-call | flops 134217728 | bytes 2097152 | tf_op jit(solution)/shard_map/term_first/pallas_call | solution.py:341
  20.8 0.1 collective-permute-start.7
  20.8 0.0 copy-start.2
  20.8 0.8 %term.4 = (f32[2,128,128]{2,1,0:T(8,128)S(1)}, bf16[2,128,128]{2,1,0:T(8,128)(2,1)S(1)}) custom-call(bf16[128,2048]{1,0:T(8,128)(2,1)S(1)} %get-tuple-element.31.coef_ref, bf16[2048,1024]{1,0:T(8,128)(2,1)S(1)} %load.1.refs_0_.factor_ref), custom_call_target="tpu_custom_call" | custom-call | flops 268435456 | bytes 2097152 | tf_op jit(solution)/shard_map/term/pallas_call | solution.py:351
  21.7 0.5 collective-permute-start.8
  22.2 0.0 collective-permute-done.7.got_ref
  22.2 1.3 %collective-permute-start.9 = (bf16[1,128,128]{2,1,0:T(8,128)(2,1)S(1)}, bf16[1,128,128]{2,1,0:T(8,128)(2,1)S(1)}, u32[]{:S(2)}, u32[]{:S(2)}) collective-permute-start(bf16[1,128,128]{2,1,0:T(8,128)(2,1)S(1)} %get-tuple-element.34.refs_0_), channel_id=1, source_target_pairs={{0,5},{1,4},{2,7},{3,6},{4,1},{5,0},{6,3},{7,2},{8,13},{9,12},{10,... | collective-permute-start | bytes 98312 | tf_op jit(solution)/shard_map/ppermute | solution.py:40
  23.5 1.2 %collective-permute-start.10 = (bf16[1,128,128]{2,1,0:T(8,128)(2,1)S(1)}, bf16[1,128,128]{2,1,0:T(8,128)(2,1)S(1)}, u32[]{:S(2)}, u32[]{:S(2)}) collective-permute-start(bf16[1,128,128]{2,1,0:T(8,128)(2,1)S(1)} %get-tuple-element.35.refs_1_), channel_id=1, source_target_pairs={{0,7},{1,6},{2,5},{3,4},{4,3},{5,2},{6,1},{7,0},{8,15},{9,14},{10,... | collective-permute-start | bytes 98312 | tf_op jit(solution)/shard_map/ppermute | solution.py:40
  24.7 0.5 term.5.mine_ref
  25.2 0.5 collective-permute-start.11
  25.7 0.2 local.2.base_ref
  25.9 1.4 %collective-permute-done.9.refs_1_ = bf16[1,128,128]{2,1,0:T(8,128)(2,1)S(1)} collective-permute-done((bf16[1,128,128]{2,1,0:T(8,128)(2,1)S(1)}, bf16[1,128,128]{2,1,0:T(8,128)(2,1)S(1)}, u32[]{:S(2)}, u32[]{:S(2)}) %collective-permute-start.9) | collective-permute-done | bytes 32800 | tf_op jit(solution)/shard_map/ppermute | solution.py:40
  27.3 1.4 %collective-permute-done.10.refs_2_ = bf16[1,128,128]{2,1,0:T(8,128)(2,1)S(1)} collective-permute-done((bf16[1,128,128]{2,1,0:T(8,128)(2,1)S(1)}, bf16[1,128,128]{2,1,0:T(8,128)(2,1)S(1)}, u32[]{:S(2)}, u32[]{:S(2)}) %collective-permute-start.10) | collective-permute-done | bytes 32800 | tf_op jit(solution)/shard_map/ppermute | solution.py:40
  28.8 0.8 %collective-permute-done.11.refs_3_ = bf16[1,128,128]{2,1,0:T(8,128)(2,1)S(1)} collective-permute-done((bf16[1,128,128]{2,1,0:T(8,128)(2,1)S(1)}, bf16[1,128,128]{2,1,0:T(8,128)(2,1)S(1)}, u32[]{:S(2)}, u32[]{:S(2)}) %collective-permute-start.11) | collective-permute-done | bytes 32800 | tf_op jit(solution)/shard_map/ppermute | solution.py:40
  29.6 0.8 %collective-permute-start.14 = (bf16[1,128,128]{2,1,0:T(8,128)(2,1)S(1)}, bf16[1,128,128]{2,1,0:T(8,128)(2,1)S(1)}, u32[]{:S(2)}, u32[]{:S(2)}) collective-permute-start(bf16[1,128,128]{2,1,0:T(8,128)(2,1)S(1)} %get-tuple-element.40.refs_1_), channel_id=1, source_target_pairs={{0,5},{1,4},{2,7},{3,6},{4,1},{5,0},{6,3},{7,2},{8,13},{9,12},{10,... | collective-permute-start | bytes 98312 | tf_op jit(solution)/shard_map/ppermute | solution.py:40
  30.4 1.4 %collective-permute-start.13 = (bf16[1,128,128]{2,1,0:T(8,128)(2,1)S(1)}, bf16[1,128,128]{2,1,0:T(8,128)(2,1)S(1)}, u32[]{:S(2)}, u32[]{:S(2)}) collective-permute-start(bf16[1,128,128]{2,1,0:T(8,128)(2,1)S(1)} %get-tuple-element.40.refs_1_), channel_id=1, source_target_pairs={{0,7},{1,6},{2,5},{3,4},{4,3},{5,2},{6,1},{7,0},{8,15},{9,14},{10,... | collective-permute-start | bytes 98312 | tf_op jit(solution)/shard_map/ppermute | solution.py:40
  31.8 0.8 %collective-permute-start.12 = (bf16[1,128,128]{2,1,0:T(8,128)(2,1)S(1)}, bf16[1,128,128]{2,1,0:T(8,128)(2,1)S(1)}, u32[]{:S(2)}, u32[]{:S(2)}) collective-permute-start(bf16[1,128,128]{2,1,0:T(8,128)(2,1)S(1)} %get-tuple-element.40.refs_1_), channel_id=1, source_target_pairs={{0,3},{1,2},{2,1},{3,0},{4,7},{5,6},{6,5},{7,4},{8,11},{9,10},{10,... | collective-permute-start | bytes 98312 | tf_op jit(solution)/shard_map/ppermute | solution.py:40
  32.6 1.7 %collective-permute-done.14.refs_4_ = bf16[1,128,128]{2,1,0:T(8,128)(2,1)S(1)} collective-permute-done((bf16[1,128,128]{2,1,0:T(8,128)(2,1)S(1)}, bf16[1,128,128]{2,1,0:T(8,128)(2,1)S(1)}, u32[]{:S(2)}, u32[]{:S(2)}) %collective-permute-start.14) | collective-permute-done | bytes 32800 | tf_op jit(solution)/shard_map/ppermute | solution.py:40
  34.2 1.4 %collective-permute-done.13.refs_3_ = bf16[1,128,128]{2,1,0:T(8,128)(2,1)S(1)} collective-permute-done((bf16[1,128,128]{2,1,0:T(8,128)(2,1)S(1)}, bf16[1,128,128]{2,1,0:T(8,128)(2,1)S(1)}, u32[]{:S(2)}, u32[]{:S(2)}) %collective-permute-start.13) | collective-permute-done | bytes 32800 | tf_op jit(solution)/shard_map/ppermute | solution.py:40
  35.6 0.0 collective-permute-done.12.refs_2_
  35.7 0.7 %collective-permute-start.15 = (bf16[4,128,128]{2,1,0:T(8,128)(2,1)S(1)}, bf16[4,128,128]{2,1,0:T(8,128)(2,1)S(1)}, u32[]{:S(2)}, u32[]{:S(2)}) collective-permute-start(bf16[4,128,128]{2,1,0:T(8,128)(2,1)S(1)} %join.3.refs_0_), channel_id=1, source_target_pairs={{0,1},{1,0},{2,3},{3,2},{4,5},{5,4},{6,7},{7,6},{8,9},{9,8},{10,11... | collective-permute-start | bytes 393224 | tf_op jit(solution)/shard_map/ppermute | solution.py:40
  36.4 0.8 %project_own.3.diag_ref = f32[256,128]{1,0:T(8,128)S(1)} custom-call(bf16[2048,1024]{1,0:T(8,128)(2,1)S(1)} %load.1.refs_0_.factor_ref, bf16[4,128,128]{2,1,0:T(8,128)(2,1)S(1)} %join.3.refs_0_), custom_call_target="tpu_custom_call" | custom-call | flops 268435456 | bytes 2097152 | tf_op jit(solution)/shard_map/project_own/pallas_call | solution.py:304
  37.2 0.2 collective-permute-done.15.fields_ref
  37.4 1.1 %project_across.3 = (bf16[192,128]{1,0:T(8,128)(2,1)S(1)}, bf16[64,128]{1,0:T(8,128)(2,1)S(1)}, f32[128,128]{1,0:T(8,128)S(1)}) custom-call(f32[128,128]{1,0:T(8,128)S(1)} %get-tuple-element.39.x_ref, bf16[2048,1024]{1,0:T(8,128)(2,1)S(1)} %load.1.refs_0_.factor_ref, f32[256,128]{1,0:T(8,128)S(1)} %project_own.3.diag_ref, ...), custom_call_target="tpu_custom_call" | custom-call | flops 268435456 | bytes 2097152 | tf_op jit(solution)/shard_map/project_across/pallas_call | solution.py:328
  38.5 1.4 %collective-permute-start.17 = (bf16[192,128]{1,0:T(8,128)(2,1)S(1)}, bf16[192,128]{1,0:T(8,128)(2,1)S(1)}, u32[]{:S(2)}, u32[]{:S(2)}) collective-permute-start(bf16[192,128]{1,0:T(8,128)(2,1)S(1)} %get-tuple-element.42), channel_id=1, source_target_pairs={{0,24},{8,16},{16,8},{24,0},{1,25},{9,17},{17,9},{25,1},{2,26},{10... | collective-permute-start | bytes 147464 | tf_op jit(solution)/shard_map/ppermute | solution.py:40
  39.9 0.5 %collective-permute-start.16 = (bf16[192,128]{1,0:T(8,128)(2,1)S(1)}, bf16[192,128]{1,0:T(8,128)(2,1)S(1)}, u32[]{:S(2)}, u32[]{:S(2)}) collective-permute-start(bf16[192,128]{1,0:T(8,128)(2,1)S(1)} %get-tuple-element.42), channel_id=1, source_target_pairs={{0,8},{8,0},{16,24},{24,16},{1,9},{9,1},{17,25},{25,17},{2,10},{10... | collective-permute-start | bytes 147464 | tf_op jit(solution)/shard_map/ppermute | solution.py:40
  40.5 1.5 %collective-permute-start.18 = (bf16[64,128]{1,0:T(8,128)(2,1)S(1)}, bf16[64,128]{1,0:T(8,128)(2,1)S(1)}, u32[]{:S(2)}, u32[]{:S(2)}) collective-permute-start(bf16[64,128]{1,0:T(8,128)(2,1)S(1)} %get-tuple-element.43.refs_0_), channel_id=1, source_target_pairs={{0,16},{8,24},{16,0},{24,8},{1,17},{9,25},{17,1},{25,9},{2,18},{10... | collective-permute-start | bytes 49160 | tf_op jit(solution)/shard_map/ppermute | solution.py:40
  42.0 2.2 %collective-permute-done.18.refs_2_ = bf16[64,128]{1,0:T(8,128)(2,1)S(1)} collective-permute-done((bf16[64,128]{1,0:T(8,128)(2,1)S(1)}, bf16[64,128]{1,0:T(8,128)(2,1)S(1)}, u32[]{:S(2)}, u32[]{:S(2)}) %collective-permute-start.18) | collective-permute-done | bytes 16416 | tf_op jit(solution)/shard_map/ppermute | solution.py:40
  44.2 0.0 collective-permute-done.17.refs_1_.refs_3_
  44.2 0.7 %term_first.3 = (bf16[128,2048]{1,0:T(8,128)(2,1)S(1)}, bf16[2,128,128]{2,1,0:T(8,128)(2,1)S(1)}) custom-call(f32[1,256]{1,0:T(1,128)S(1)} %bitcast.14, bf16[2048,1024]{1,0:T(8,128)(2,1)S(1)} %load.1.refs_0_.factor_ref, bf16[64,128]{1,0:T(8,128)(2,1)S(1)} %get-tuple-element.43.refs_0_, bf16[192,128]{1,0:T(8,128)(2,1)S(1)} %collective-permute-done.16.refs_0_.refs_1_, ...), custom_call_target="tpu_custom_call" | custom-call | flops 134217728 | bytes 2097152 | tf_op jit(solution)/shard_map/term_first/pallas_call | solution.py:341
  45.0 0.1 collective-permute-start.19
  45.0 0.8 %term.6 = (f32[2,128,128]{2,1,0:T(8,128)S(1)}, bf16[2,128,128]{2,1,0:T(8,128)(2,1)S(1)}) custom-call(bf16[128,2048]{1,0:T(8,128)(2,1)S(1)} %get-tuple-element.44.coef_ref, bf16[2048,1024]{1,0:T(8,128)(2,1)S(1)} %load.1.refs_0_.factor_ref), custom_call_target="tpu_custom_call" | custom-call | flops 268435456 | bytes 2097152 | tf_op jit(solution)/shard_map/term/pallas_call | solution.py:351
  45.9 0.6 %collective-permute-start.20 = (bf16[2,128,128]{2,1,0:T(8,128)(2,1)S(1)}, bf16[2,128,128]{2,1,0:T(8,128)(2,1)S(1)}, u32[]{:S(2)}, u32[]{:S(2)}) collective-permute-start(bf16[2,128,128]{2,1,0:T(8,128)(2,1)S(1)} %get-tuple-element.49), channel_id=1, source_target_pairs={{0,1},{1,0},{2,3},{3,2},{4,5},{5,4},{6,7},{7,6},{8,9},{9,8},{10,11... | collective-permute-start | bytes 196616 | tf_op jit(solution)/shard_map/ppermute | solution.py:40
  46.4 0.0 collective-permute-done.19.got_ref
  46.4 1.1 %collective-permute-start.21 = (bf16[1,128,128]{2,1,0:T(8,128)(2,1)S(1)}, bf16[1,128,128]{2,1,0:T(8,128)(2,1)S(1)}, u32[]{:S(2)}, u32[]{:S(2)}) collective-permute-start(bf16[1,128,128]{2,1,0:T(8,128)(2,1)S(1)} %get-tuple-element.47.refs_0_), channel_id=1, source_target_pairs={{0,5},{1,4},{2,7},{3,6},{4,1},{5,0},{6,3},{7,2},{8,13},{9,12},{10,... | collective-permute-start | bytes 98312 | tf_op jit(solution)/shard_map/ppermute | solution.py:40
  47.6 1.4 %collective-permute-start.22 = (bf16[1,128,128]{2,1,0:T(8,128)(2,1)S(1)}, bf16[1,128,128]{2,1,0:T(8,128)(2,1)S(1)}, u32[]{:S(2)}, u32[]{:S(2)}) collective-permute-start(bf16[1,128,128]{2,1,0:T(8,128)(2,1)S(1)} %get-tuple-element.48.refs_1_), channel_id=1, source_target_pairs={{0,7},{1,6},{2,5},{3,4},{4,3},{5,2},{6,1},{7,0},{8,15},{9,14},{10,... | collective-permute-start | bytes 98312 | tf_op jit(solution)/shard_map/ppermute | solution.py:40
  49.0 0.5 term.7.mine_ref
  49.5 0.5 collective-permute-start.23
  49.9 0.2 local.3.base_ref
  50.1 1.5 %collective-permute-done.21.refs_1_ = bf16[1,128,128]{2,1,0:T(8,128)(2,1)S(1)} collective-permute-done((bf16[1,128,128]{2,1,0:T(8,128)(2,1)S(1)}, bf16[1,128,128]{2,1,0:T(8,128)(2,1)S(1)}, u32[]{:S(2)}, u32[]{:S(2)}) %collective-permute-start.21) | collective-permute-done | bytes 32800 | tf_op jit(solution)/shard_map/ppermute | solution.py:40
  51.6 1.2 %collective-permute-done.22.refs_2_ = bf16[1,128,128]{2,1,0:T(8,128)(2,1)S(1)} collective-permute-done((bf16[1,128,128]{2,1,0:T(8,128)(2,1)S(1)}, bf16[1,128,128]{2,1,0:T(8,128)(2,1)S(1)}, u32[]{:S(2)}, u32[]{:S(2)}) %collective-permute-start.22) | collective-permute-done | bytes 32800 | tf_op jit(solution)/shard_map/ppermute | solution.py:40
  52.8 1.0 %collective-permute-done.23.refs_3_ = bf16[1,128,128]{2,1,0:T(8,128)(2,1)S(1)} collective-permute-done((bf16[1,128,128]{2,1,0:T(8,128)(2,1)S(1)}, bf16[1,128,128]{2,1,0:T(8,128)(2,1)S(1)}, u32[]{:S(2)}, u32[]{:S(2)}) %collective-permute-start.23) | collective-permute-done | bytes 32800 | tf_op jit(solution)/shard_map/ppermute | solution.py:40
  53.8 0.7 %update.3 = (f32[128,128]{1,0:T(8,128)}, f32[128,128]{1,0:T(8,128)}) custom-call(f32[128,128]{1,0:T(8,128)S(1)} %get-tuple-element.39.x_ref, f32[128,128]{1,0:T(8,128)S(1)} %local.3.base_ref, f32[1,128,128]{2,1,0:T(8,128)S(1)} %get-tuple-element.50.refs_0_, bf16[1,128,128]{2,1,0:T(8,128)(2,1)S(1)} %collective-permute-done.21.refs_1_, ...), custom_call_target="tpu_custom_call" | custom-call | bytes 262144 | tf_op jit(solution)/shard_map/update/pallas_call | solution.py:380
  (14 shorter events, 0.1 us)
Async XLA Ops:
  1.5 7.9 %collective-permute-start.2 = (bf16[1,128,128]{2,1,0:T(8,128)(2,1)S(1)}, bf16[1,128,128]{2,1,0:T(8,128)(2,1)S(1)}, u32[]{:S(2)}, u32[]{:S(2)}) collective-permute-start(bf16[1,128,128]{2,1,0:T(8,128)(2,1)S(1)} %fusion.refs_1_), channel_id=1, source_target_pairs={{0,5},{1,4},{2,7},{3,6},{4,1},{5,0},{6,3},{7,2},{8,13},{9,12},{10,... | collective-permute-start | bytes 98312 | tf_op jit(solution)/shard_map/ppermute | solution.py:40
  5.0 5.2 %collective-permute-start.1 = (bf16[1,128,128]{2,1,0:T(8,128)(2,1)S(1)}, bf16[1,128,128]{2,1,0:T(8,128)(2,1)S(1)}, u32[]{:S(2)}, u32[]{:S(2)}) collective-permute-start(bf16[1,128,128]{2,1,0:T(8,128)(2,1)S(1)} %fusion.refs_1_), channel_id=1, source_target_pairs={{0,7},{1,6},{2,5},{3,4},{4,3},{5,2},{6,1},{7,0},{8,15},{9,14},{10,... | collective-permute-start | bytes 98312 | tf_op jit(solution)/shard_map/ppermute | solution.py:40
  6.6 3.8 %collective-permute-start = (bf16[1,128,128]{2,1,0:T(8,128)(2,1)S(1)}, bf16[1,128,128]{2,1,0:T(8,128)(2,1)S(1)}, u32[]{:S(2)}, u32[]{:S(2)}) collective-permute-start(bf16[1,128,128]{2,1,0:T(8,128)(2,1)S(1)} %fusion.refs_1_), channel_id=1, source_target_pairs={{0,3},{1,2},{2,1},{3,0},{4,7},{5,6},{6,5},{7,4},{8,11},{9,10},{10,... | collective-permute-start | bytes 98312 | tf_op jit(solution)/shard_map/ppermute | solution.py:40
  6.8 2.2 %copy-start = (bf16[256,8,1024]{2,1,0:T(8,128)(2,1)S(1)}, bf16[256,8,1024]{2,1,0:T(8,128)(2,1)}, u32[]{:S(2)}) copy-start(bf16[256,8,1024]{2,1,0:T(8,128)(2,1)} %param.6) | copy-start | bytes 12582916
  9.4 2.7 %copy-start.1 = (f32[16,8,128]{2,1,0:T(8,128)S(1)}, f32[16,8,128]{2,1,0:T(8,128)}, u32[]{:S(2)}) copy-start(f32[16,8,128]{2,1,0:T(8,128)} %param.4) | copy-start | bytes 196612
  10.4 9.7 %copy-start.3 = (f32[256]{0:T(256)S(1)}, f32[256]{0:T(256)}, u32[]{:S(2)}) copy-start(f32[256]{0:T(256)} %param.7) | copy-start | bytes 3076
  10.4 1.7 %collective-permute-start.3 = (bf16[4,128,128]{2,1,0:T(8,128)(2,1)S(1)}, bf16[4,128,128]{2,1,0:T(8,128)(2,1)S(1)}, u32[]{:S(2)}, u32[]{:S(2)}) collective-permute-start(bf16[4,128,128]{2,1,0:T(8,128)(2,1)S(1)} %join.2.refs_0_), channel_id=1, source_target_pairs={{0,1},{1,0},{2,3},{3,2},{4,5},{5,4},{6,7},{7,6},{8,9},{9,8},{10,11... | collective-permute-start | bytes 393224 | tf_op jit(solution)/shard_map/ppermute | solution.py:40
  13.3 6.8 %collective-permute-start.5 = (bf16[192,128]{1,0:T(8,128)(2,1)S(1)}, bf16[192,128]{1,0:T(8,128)(2,1)S(1)}, u32[]{:S(2)}, u32[]{:S(2)}) collective-permute-start(bf16[192,128]{1,0:T(8,128)(2,1)S(1)} %get-tuple-element.29), channel_id=1, source_target_pairs={{0,24},{8,16},{16,8},{24,0},{1,25},{9,17},{17,9},{25,1},{2,26},{10... | collective-permute-start | bytes 147464 | tf_op jit(solution)/shard_map/ppermute | solution.py:40
  15.7 4.3 %collective-permute-start.4 = (bf16[192,128]{1,0:T(8,128)(2,1)S(1)}, bf16[192,128]{1,0:T(8,128)(2,1)S(1)}, u32[]{:S(2)}, u32[]{:S(2)}) collective-permute-start(bf16[192,128]{1,0:T(8,128)(2,1)S(1)} %get-tuple-element.29), channel_id=1, source_target_pairs={{0,8},{8,0},{16,24},{24,16},{1,9},{9,1},{17,25},{25,17},{2,10},{10... | collective-permute-start | bytes 147464 | tf_op jit(solution)/shard_map/ppermute | solution.py:40
  16.3 3.7 %collective-permute-start.6 = (bf16[64,128]{1,0:T(8,128)(2,1)S(1)}, bf16[64,128]{1,0:T(8,128)(2,1)S(1)}, u32[]{:S(2)}, u32[]{:S(2)}) collective-permute-start(bf16[64,128]{1,0:T(8,128)(2,1)S(1)} %get-tuple-element.30.refs_0_), channel_id=1, source_target_pairs={{0,16},{8,24},{16,0},{24,8},{1,17},{9,25},{17,1},{25,9},{2,18},{10... | collective-permute-start | bytes 49160 | tf_op jit(solution)/shard_map/ppermute | solution.py:40
  20.8 1.4 %collective-permute-start.7 = (bf16[2,128,128]{2,1,0:T(8,128)(2,1)S(1)}, bf16[2,128,128]{2,1,0:T(8,128)(2,1)S(1)}, u32[]{:S(2)}, u32[]{:S(2)}) collective-permute-start(bf16[2,128,128]{2,1,0:T(8,128)(2,1)S(1)} %get-tuple-element.33), channel_id=1, source_target_pairs={{0,1},{1,0},{2,3},{3,2},{4,5},{5,4},{6,7},{7,6},{8,9},{9,8},{10,11... | collective-permute-start | bytes 196616 | tf_op jit(solution)/shard_map/ppermute | solution.py:40
  20.8 4.9 %copy-start.2 = (f32[8,128]{1,0:T(8,128)S(1)}, f32[8,128]{1,0:T(8,128)}, u32[]{:S(2)}) copy-start(f32[8,128]{1,0:T(8,128)} %amp_ref.3) | copy-start | bytes 12292
  21.7 3.5 %collective-permute-start.8 = (bf16[2,128,128]{2,1,0:T(8,128)(2,1)S(1)}, bf16[2,128,128]{2,1,0:T(8,128)(2,1)S(1)}, u32[]{:S(2)}, u32[]{:S(2)}) collective-permute-start(bf16[2,128,128]{2,1,0:T(8,128)(2,1)S(1)} %get-tuple-element.36), channel_id=1, source_target_pairs={{0,1},{1,0},{2,3},{3,2},{4,5},{5,4},{6,7},{7,6},{8,9},{9,8},{10,11... | collective-permute-start | bytes 196616 | tf_op jit(solution)/shard_map/ppermute | solution.py:40
  22.2 5.1 %collective-permute-start.9 = (bf16[1,128,128]{2,1,0:T(8,128)(2,1)S(1)}, bf16[1,128,128]{2,1,0:T(8,128)(2,1)S(1)}, u32[]{:S(2)}, u32[]{:S(2)}) collective-permute-start(bf16[1,128,128]{2,1,0:T(8,128)(2,1)S(1)} %get-tuple-element.34.refs_0_), channel_id=1, source_target_pairs={{0,5},{1,4},{2,7},{3,6},{4,1},{5,0},{6,3},{7,2},{8,13},{9,12},{10,... | collective-permute-start | bytes 98312 | tf_op jit(solution)/shard_map/ppermute | solution.py:40
  23.5 5.3 %collective-permute-start.10 = (bf16[1,128,128]{2,1,0:T(8,128)(2,1)S(1)}, bf16[1,128,128]{2,1,0:T(8,128)(2,1)S(1)}, u32[]{:S(2)}, u32[]{:S(2)}) collective-permute-start(bf16[1,128,128]{2,1,0:T(8,128)(2,1)S(1)} %get-tuple-element.35.refs_1_), channel_id=1, source_target_pairs={{0,7},{1,6},{2,5},{3,4},{4,3},{5,2},{6,1},{7,0},{8,15},{9,14},{10,... | collective-permute-start | bytes 98312 | tf_op jit(solution)/shard_map/ppermute | solution.py:40
  25.2 4.3 %collective-permute-start.11 = (bf16[1,128,128]{2,1,0:T(8,128)(2,1)S(1)}, bf16[1,128,128]{2,1,0:T(8,128)(2,1)S(1)}, u32[]{:S(2)}, u32[]{:S(2)}) collective-permute-start(bf16[1,128,128]{2,1,0:T(8,128)(2,1)S(1)} %get-tuple-element.38), channel_id=1, source_target_pairs={{0,3},{1,2},{2,1},{3,0},{4,7},{5,6},{6,5},{7,4},{8,11},{9,10},{10,... | collective-permute-start | bytes 98312 | tf_op jit(solution)/shard_map/ppermute | solution.py:40
  29.6 4.7 %collective-permute-start.14 = (bf16[1,128,128]{2,1,0:T(8,128)(2,1)S(1)}, bf16[1,128,128]{2,1,0:T(8,128)(2,1)S(1)}, u32[]{:S(2)}, u32[]{:S(2)}) collective-permute-start(bf16[1,128,128]{2,1,0:T(8,128)(2,1)S(1)} %get-tuple-element.40.refs_1_), channel_id=1, source_target_pairs={{0,5},{1,4},{2,7},{3,6},{4,1},{5,0},{6,3},{7,2},{8,13},{9,12},{10,... | collective-permute-start | bytes 98312 | tf_op jit(solution)/shard_map/ppermute | solution.py:40
  30.4 5.3 %collective-permute-start.13 = (bf16[1,128,128]{2,1,0:T(8,128)(2,1)S(1)}, bf16[1,128,128]{2,1,0:T(8,128)(2,1)S(1)}, u32[]{:S(2)}, u32[]{:S(2)}) collective-permute-start(bf16[1,128,128]{2,1,0:T(8,128)(2,1)S(1)} %get-tuple-element.40.refs_1_), channel_id=1, source_target_pairs={{0,7},{1,6},{2,5},{3,4},{4,3},{5,2},{6,1},{7,0},{8,15},{9,14},{10,... | collective-permute-start | bytes 98312 | tf_op jit(solution)/shard_map/ppermute | solution.py:40
  31.8 3.9 %collective-permute-start.12 = (bf16[1,128,128]{2,1,0:T(8,128)(2,1)S(1)}, bf16[1,128,128]{2,1,0:T(8,128)(2,1)S(1)}, u32[]{:S(2)}, u32[]{:S(2)}) collective-permute-start(bf16[1,128,128]{2,1,0:T(8,128)(2,1)S(1)} %get-tuple-element.40.refs_1_), channel_id=1, source_target_pairs={{0,3},{1,2},{2,1},{3,0},{4,7},{5,6},{6,5},{7,4},{8,11},{9,10},{10,... | collective-permute-start | bytes 98312 | tf_op jit(solution)/shard_map/ppermute | solution.py:40
  35.7 1.7 %collective-permute-start.15 = (bf16[4,128,128]{2,1,0:T(8,128)(2,1)S(1)}, bf16[4,128,128]{2,1,0:T(8,128)(2,1)S(1)}, u32[]{:S(2)}, u32[]{:S(2)}) collective-permute-start(bf16[4,128,128]{2,1,0:T(8,128)(2,1)S(1)} %join.3.refs_0_), channel_id=1, source_target_pairs={{0,1},{1,0},{2,3},{3,2},{4,5},{5,4},{6,7},{7,6},{8,9},{9,8},{10,11... | collective-permute-start | bytes 393224 | tf_op jit(solution)/shard_map/ppermute | solution.py:40
  38.5 5.7 %collective-permute-start.17 = (bf16[192,128]{1,0:T(8,128)(2,1)S(1)}, bf16[192,128]{1,0:T(8,128)(2,1)S(1)}, u32[]{:S(2)}, u32[]{:S(2)}) collective-permute-start(bf16[192,128]{1,0:T(8,128)(2,1)S(1)} %get-tuple-element.42), channel_id=1, source_target_pairs={{0,24},{8,16},{16,8},{24,0},{1,25},{9,17},{17,9},{25,1},{2,26},{10... | collective-permute-start | bytes 147464 | tf_op jit(solution)/shard_map/ppermute | solution.py:40
  39.9 4.3 %collective-permute-start.16 = (bf16[192,128]{1,0:T(8,128)(2,1)S(1)}, bf16[192,128]{1,0:T(8,128)(2,1)S(1)}, u32[]{:S(2)}, u32[]{:S(2)}) collective-permute-start(bf16[192,128]{1,0:T(8,128)(2,1)S(1)} %get-tuple-element.42), channel_id=1, source_target_pairs={{0,8},{8,0},{16,24},{24,16},{1,9},{9,1},{17,25},{25,17},{2,10},{10... | collective-permute-start | bytes 147464 | tf_op jit(solution)/shard_map/ppermute | solution.py:40
  40.5 3.7 %collective-permute-start.18 = (bf16[64,128]{1,0:T(8,128)(2,1)S(1)}, bf16[64,128]{1,0:T(8,128)(2,1)S(1)}, u32[]{:S(2)}, u32[]{:S(2)}) collective-permute-start(bf16[64,128]{1,0:T(8,128)(2,1)S(1)} %get-tuple-element.43.refs_0_), channel_id=1, source_target_pairs={{0,16},{8,24},{16,0},{24,8},{1,17},{9,25},{17,1},{25,9},{2,18},{10... | collective-permute-start | bytes 49160 | tf_op jit(solution)/shard_map/ppermute | solution.py:40
  45.0 1.4 %collective-permute-start.19 = (bf16[2,128,128]{2,1,0:T(8,128)(2,1)S(1)}, bf16[2,128,128]{2,1,0:T(8,128)(2,1)S(1)}, u32[]{:S(2)}, u32[]{:S(2)}) collective-permute-start(bf16[2,128,128]{2,1,0:T(8,128)(2,1)S(1)} %get-tuple-element.46), channel_id=1, source_target_pairs={{0,1},{1,0},{2,3},{3,2},{4,5},{5,4},{6,7},{7,6},{8,9},{9,8},{10,11... | collective-permute-start | bytes 196616 | tf_op jit(solution)/shard_map/ppermute | solution.py:40
  45.9 3.6 %collective-permute-start.20 = (bf16[2,128,128]{2,1,0:T(8,128)(2,1)S(1)}, bf16[2,128,128]{2,1,0:T(8,128)(2,1)S(1)}, u32[]{:S(2)}, u32[]{:S(2)}) collective-permute-start(bf16[2,128,128]{2,1,0:T(8,128)(2,1)S(1)} %get-tuple-element.49), channel_id=1, source_target_pairs={{0,1},{1,0},{2,3},{3,2},{4,5},{5,4},{6,7},{7,6},{8,9},{9,8},{10,11... | collective-permute-start | bytes 196616 | tf_op jit(solution)/shard_map/ppermute | solution.py:40
  46.4 5.2 %collective-permute-start.21 = (bf16[1,128,128]{2,1,0:T(8,128)(2,1)S(1)}, bf16[1,128,128]{2,1,0:T(8,128)(2,1)S(1)}, u32[]{:S(2)}, u32[]{:S(2)}) collective-permute-start(bf16[1,128,128]{2,1,0:T(8,128)(2,1)S(1)} %get-tuple-element.47.refs_0_), channel_id=1, source_target_pairs={{0,5},{1,4},{2,7},{3,6},{4,1},{5,0},{6,3},{7,2},{8,13},{9,12},{10,... | collective-permute-start | bytes 98312 | tf_op jit(solution)/shard_map/ppermute | solution.py:40
  47.6 5.3 %collective-permute-start.22 = (bf16[1,128,128]{2,1,0:T(8,128)(2,1)S(1)}, bf16[1,128,128]{2,1,0:T(8,128)(2,1)S(1)}, u32[]{:S(2)}, u32[]{:S(2)}) collective-permute-start(bf16[1,128,128]{2,1,0:T(8,128)(2,1)S(1)} %get-tuple-element.48.refs_1_), channel_id=1, source_target_pairs={{0,7},{1,6},{2,5},{3,4},{4,3},{5,2},{6,1},{7,0},{8,15},{9,14},{10,... | collective-permute-start | bytes 98312 | tf_op jit(solution)/shard_map/ppermute | solution.py:40
  49.5 4.3 %collective-permute-start.23 = (bf16[1,128,128]{2,1,0:T(8,128)(2,1)S(1)}, bf16[1,128,128]{2,1,0:T(8,128)(2,1)S(1)}, u32[]{:S(2)}, u32[]{:S(2)}) collective-permute-start(bf16[1,128,128]{2,1,0:T(8,128)(2,1)S(1)} %get-tuple-element.51), channel_id=1, source_target_pairs={{0,3},{1,2},{2,1},{3,0},{4,7},{5,6},{6,5},{7,4},{8,11},{9,10},{10,... | collective-permute-start | bytes 98312 | tf_op jit(solution)/shard_map/ppermute | solution.py:40

commit v8 on v7

--- a/solution.py
+++ b/solution.py
@@ -292,7 +292,7 @@
         name="load",
     )(flat)
     half = near // 2
-    close, away = list(range(half)), list(range(half, near))
+    close, away = list(range(half)), list(range(near - 1, half - 1, -1))
 
     def spots_of(masks, other):
         return [(mask, other != (mask > 0)) for mask in masks]

time: 54.7 us -> 54.6 us (level)
  waiting for transfers between devices: 17.2 us -> 14.7 us
  starting transfers between devices: 24 us -> 26.4 us
    ppermute x24, waiting for transfers between devices: 17.2 us -> 14.7 us  [swap(): lax.ppermute(value, axis, [(i, i ^ mask) for i in range(lax.axis_size(axi...]
    ppermute x24, starting transfers between devices: 24 us -> 26.4 us  [swap(): lax.ppermute(value, axis, [(i, i ^ mask) for i in range(lax.axis_size(axi...]
  transfers between devices with their start and end apart: 24 -> 24, of which waited for: 14 -> 12; matrix products, arithmetic and copies ran while one was open for 0% -> 0% of each run, Pallas kernels for 9% -> 9%
where the time goes in v8:
time: 54.6 us; the launch traced here: 54.4 us
  starting transfers between devices  26.4 us (48%)
  waiting for transfers between devices  14.7 us (27%)
  Pallas kernels  9.48 us (17%)
  local copies, waits for them, and re-layouts  2.21 us (4%)
  other arithmetic  0.85 us (2%)
  between operations  0.83 us (2%)
    ppermute x24, starting transfers between devices, swap(): lax.ppermute(value, axis, [(i, i ^ mask) for i in range(lax.axis_size(axi...  26.4 us
    ppermute x24, waiting for transfers between devices, swap(): lax.ppermute(value, axis, [(i, i ^ mask) for i in range(lax.axis_size(axi...  14.7 us
    pallas_call x4, Pallas kernels, term(): call(partial(term_kernel, wanted, len(after)), in_specs=[pl.BlockSpec(mem...  2.59 us
    pallas_call x2, Pallas kernels, on_device(): call(partial(second_kernel, rows, cols, halve, spots, known), (shape(bf16...  2.31 us
    unnamed x8, local copies, waits for them, and re-layouts  2.21 us
    pallas_call x2, Pallas kernels, first(): call(partial(first_kernel, rows, spots, len(before)), shape(f32, blocks *...  1.62 us
    pallas_call x2, Pallas kernels, on_device(): call(partial(far_kernel, rows, cols, groups, ncells_all, spots_of(away, T...  1.45 us
  transfers between devices with their start and end apart: 24, of which 12 were waited for; matrix products, arithmetic and copies ran while one was open for 0% of the time, Pallas kernels for 9%

profile of v8, /device:TPU:0, one launch (start us, length us, event | category | flops | bytes accessed | tf_op | source)
XLA Modules:
  0.0 54.4 jit_solution(16173417098512219110)
XLA Ops:
  0.6 0.8 %fusion.refs_1_ = bf16[1,128,128]{2,1,0:T(8,128)(2,1)S(1)} fusion(f32[16,8,128]{2,1,0:T(8,128)} %param.4), kind=kLoop, calls=%fused_computation.1 | loop fusion | flops 32768 | bytes 98304 | tf_op jit(solution)/shard_map/convert_element_type | solution.py:267
  1.5 3.5 %collective-permute-start.2 = (bf16[1,128,128]{2,1,0:T(8,128)(2,1)S(1)}, bf16[1,128,128]{2,1,0:T(8,128)(2,1)S(1)}, u32[]{:S(2)}, u32[]{:S(2)}) collective-permute-start(bf16[1,128,128]{2,1,0:T(8,128)(2,1)S(1)} %fusion.refs_1_), channel_id=1, source_target_pairs={{0,5},{1,4},{2,7},{3,6},{4,1},{5,0},{6,3},{7,2},{8,13},{9,12},{10,... | collective-permute-start | bytes 98312 | tf_op jit(solution)/shard_map/ppermute | solution.py:40
  5.0 1.6 %collective-permute-start.1 = (bf16[1,128,128]{2,1,0:T(8,128)(2,1)S(1)}, bf16[1,128,128]{2,1,0:T(8,128)(2,1)S(1)}, u32[]{:S(2)}, u32[]{:S(2)}) collective-permute-start(bf16[1,128,128]{2,1,0:T(8,128)(2,1)S(1)} %fusion.refs_1_), channel_id=1, source_target_pairs={{0,7},{1,6},{2,5},{3,4},{4,3},{5,2},{6,1},{7,0},{8,15},{9,14},{10,... | collective-permute-start | bytes 98312 | tf_op jit(solution)/shard_map/ppermute | solution.py:40
  6.6 0.2 collective-permute-start
  6.8 2.2 %copy-done = bf16[256,8,1024]{2,1,0:T(8,128)(2,1)S(1)} copy-done((bf16[256,8,1024]{2,1,0:T(8,128)(2,1)S(1)}, bf16[256,8,1024]{2,1,0:T(8,128)(2,1)}, u32[]{:S(2)}) %copy-start) | copy-done | bytes 4194328
  9.0 0.4 load.1.refs_0_.factor_ref
  9.4 0.0 copy-start.1
  9.4 0.0 collective-permute-done.2.refs_4_
  9.4 0.8 %collective-permute-done.1.refs_3_ = bf16[1,128,128]{2,1,0:T(8,128)(2,1)S(1)} collective-permute-done((bf16[1,128,128]{2,1,0:T(8,128)(2,1)S(1)}, bf16[1,128,128]{2,1,0:T(8,128)(2,1)S(1)}, u32[]{:S(2)}, u32[]{:S(2)}) %collective-permute-start.1) | collective-permute-done | bytes 32800 | tf_op jit(solution)/shard_map/ppermute | solution.py:40
  10.2 0.2 collective-permute-done.refs_2_
  10.4 0.0 copy-start.3
  10.4 0.7 %collective-permute-start.3 = (bf16[4,128,128]{2,1,0:T(8,128)(2,1)S(1)}, bf16[4,128,128]{2,1,0:T(8,128)(2,1)S(1)}, u32[]{:S(2)}, u32[]{:S(2)}) collective-permute-start(bf16[4,128,128]{2,1,0:T(8,128)(2,1)S(1)} %join.2.refs_0_), channel_id=1, source_target_pairs={{0,1},{1,0},{2,3},{3,2},{4,5},{5,4},{6,7},{7,6},{8,9},{9,8},{10,11... | collective-permute-start | bytes 393224 | tf_op jit(solution)/shard_map/ppermute | solution.py:40
  11.1 0.8 %project_own.2.diag_ref = f32[256,128]{1,0:T(8,128)S(1)} custom-call(bf16[2048,1024]{1,0:T(8,128)(2,1)S(1)} %load.1.refs_0_.factor_ref, bf16[4,128,128]{2,1,0:T(8,128)(2,1)S(1)} %join.2.refs_0_), custom_call_target="tpu_custom_call" | custom-call | flops 268435456 | bytes 2097152 | tf_op jit(solution)/shard_map/project_own/pallas_call | solution.py:304
  11.9 0.2 collective-permute-done.3.fields_ref
  12.1 1.2 %project_across.2 = (bf16[192,128]{1,0:T(8,128)(2,1)S(1)}, bf16[64,128]{1,0:T(8,128)(2,1)S(1)}, f32[128,128]{1,0:T(8,128)S(1)}) custom-call(f32[128,128]{1,0:T(8,128)S(1)} %bitcast.8, bf16[2048,1024]{1,0:T(8,128)(2,1)S(1)} %load.1.refs_0_.factor_ref, f32[256,128]{1,0:T(8,128)S(1)} %project_own.2.diag_ref, ...), custom_call_target="tpu_custom_call" | custom-call | flops 268435456 | bytes 2097152 | tf_op jit(solution)/shard_map/project_across/pallas_call | solution.py:328
  13.3 2.5 %collective-permute-start.5 = (bf16[192,128]{1,0:T(8,128)(2,1)S(1)}, bf16[192,128]{1,0:T(8,128)(2,1)S(1)}, u32[]{:S(2)}, u32[]{:S(2)}) collective-permute-start(bf16[192,128]{1,0:T(8,128)(2,1)S(1)} %get-tuple-element.29), channel_id=1, source_target_pairs={{0,24},{8,16},{16,8},{24,0},{1,25},{9,17},{17,9},{25,1},{2,26},{10... | collective-permute-start | bytes 147464 | tf_op jit(solution)/shard_map/ppermute | solution.py:40
  15.7 0.5 collective-permute-start.4
  16.3 0.5 collective-permute-start.6
  16.8 3.2 %collective-permute-done.6.refs_2_ = bf16[64,128]{1,0:T(8,128)(2,1)S(1)} collective-permute-done((bf16[64,128]{1,0:T(8,128)(2,1)S(1)}, bf16[64,128]{1,0:T(8,128)(2,1)S(1)}, u32[]{:S(2)}, u32[]{:S(2)}) %collective-permute-start.6) | collective-permute-done | bytes 16416 | tf_op jit(solution)/shard_map/ppermute | solution.py:40
  20.0 0.0 collective-permute-done.5.refs_1_.refs_3_
  20.0 0.0 collective-permute-done.4.refs_0_.refs_1_
  20.0 0.7 %term_first.2 = (bf16[128,2048]{1,0:T(8,128)(2,1)S(1)}, bf16[2,128,128]{2,1,0:T(8,128)(2,1)S(1)}) custom-call(f32[1,256]{1,0:T(1,128)S(1)} %bitcast.13, bf16[2048,1024]{1,0:T(8,128)(2,1)S(1)} %load.1.refs_0_.factor_ref, bf16[64,128]{1,0:T(8,128)(2,1)S(1)} %get-tuple-element.30.refs_0_, bf16[192,128]{1,0:T(8,128)(2,1)S(1)} %collective-permute-done.4.refs_0_.refs_1_, ...), custom_call_target="tpu_custom_call" | custom-call | flops 134217728 | bytes 2097152 | tf_op jit(solution)/shard_map/term_first/pallas_call | solution.py:341
  20.8 0.1 collective-permute-start.7
  20.8 0.0 copy-start.2
  20.8 0.8 %term.4 = (f32[2,128,128]{2,1,0:T(8,128)S(1)}, bf16[2,128,128]{2,1,0:T(8,128)(2,1)S(1)}) custom-call(bf16[128,2048]{1,0:T(8,128)(2,1)S(1)} %get-tuple-element.31.coef_ref, bf16[2048,1024]{1,0:T(8,128)(2,1)S(1)} %load.1.refs_0_.factor_ref), custom_call_target="tpu_custom_call" | custom-call | flops 268435456 | bytes 2097152 | tf_op jit(solution)/shard_map/term/pallas_call | solution.py:351
  21.7 0.5 collective-permute-start.8
  22.2 0.0 collective-permute-done.7.got_ref
  22.2 2.2 %collective-permute-start.9 = (bf16[1,128,128]{2,1,0:T(8,128)(2,1)S(1)}, bf16[1,128,128]{2,1,0:T(8,128)(2,1)S(1)}, u32[]{:S(2)}, u32[]{:S(2)}) collective-permute-start(bf16[1,128,128]{2,1,0:T(8,128)(2,1)S(1)} %get-tuple-element.34.refs_0_), channel_id=1, source_target_pairs={{0,7},{1,6},{2,5},{3,4},{4,3},{5,2},{6,1},{7,0},{8,15},{9,14},{10,... | collective-permute-start | bytes 98312 | tf_op jit(solution)/shard_map/ppermute | solution.py:40
  24.4 0.5 term.5.mine_ref
  24.9 0.0 collective-permute-done.8.got_ref
  24.9 1.7 %collective-permute-start.11 = (bf16[1,128,128]{2,1,0:T(8,128)(2,1)S(1)}, bf16[1,128,128]{2,1,0:T(8,128)(2,1)S(1)}, u32[]{:S(2)}, u32[]{:S(2)}) collective-permute-start(bf16[1,128,128]{2,1,0:T(8,128)(2,1)S(1)} %get-tuple-element.38), channel_id=1, source_target_pairs={{0,3},{1,2},{2,1},{3,0},{4,7},{5,6},{6,5},{7,4},{8,11},{9,10},{10,... | collective-permute-start | bytes 98312 | tf_op jit(solution)/shard_map/ppermute | solution.py:40
  26.6 0.2 local.2.base_ref
  26.8 0.7 %collective-permute-done.9.refs_1_ = bf16[1,128,128]{2,1,0:T(8,128)(2,1)S(1)} collective-permute-done((bf16[1,128,128]{2,1,0:T(8,128)(2,1)S(1)}, bf16[1,128,128]{2,1,0:T(8,128)(2,1)S(1)}, u32[]{:S(2)}, u32[]{:S(2)}) %collective-permute-start.9) | collective-permute-done | bytes 32800 | tf_op jit(solution)/shard_map/ppermute | solution.py:40
  27.6 1.3 %collective-permute-done.10.refs_2_ = bf16[1,128,128]{2,1,0:T(8,128)(2,1)S(1)} collective-permute-done((bf16[1,128,128]{2,1,0:T(8,128)(2,1)S(1)}, bf16[1,128,128]{2,1,0:T(8,128)(2,1)S(1)}, u32[]{:S(2)}, u32[]{:S(2)}) %collective-permute-start.10) | collective-permute-done | bytes 32800 | tf_op jit(solution)/shard_map/ppermute | solution.py:40
  28.8 0.0 collective-permute-done.11.refs_3_
  28.9 2.4 %collective-permute-start.14 = (bf16[1,128,128]{2,1,0:T(8,128)(2,1)S(1)}, bf16[1,128,128]{2,1,0:T(8,128)(2,1)S(1)}, u32[]{:S(2)}, u32[]{:S(2)}) collective-permute-start(bf16[1,128,128]{2,1,0:T(8,128)(2,1)S(1)} %get-tuple-element.40.refs_1_), channel_id=1, source_target_pairs={{0,5},{1,4},{2,7},{3,6},{4,1},{5,0},{6,3},{7,2},{8,13},{9,12},{10,... | collective-permute-start | bytes 98312 | tf_op jit(solution)/shard_map/ppermute | solution.py:40
  31.3 1.4 %collective-permute-start.13 = (bf16[1,128,128]{2,1,0:T(8,128)(2,1)S(1)}, bf16[1,128,128]{2,1,0:T(8,128)(2,1)S(1)}, u32[]{:S(2)}, u32[]{:S(2)}) collective-permute-start(bf16[1,128,128]{2,1,0:T(8,128)(2,1)S(1)} %get-tuple-element.40.refs_1_), channel_id=1, source_target_pairs={{0,7},{1,6},{2,5},{3,4},{4,3},{5,2},{6,1},{7,0},{8,15},{9,14},{10,... | collective-permute-start | bytes 98312 | tf_op jit(solution)/shard_map/ppermute | solution.py:40
  32.7 0.0 collective-permute-start.12
  32.7 0.5 collective-permute-done.14.refs_4_
  33.2 3.3 %collective-permute-done.13.refs_3_ = bf16[1,128,128]{2,1,0:T(8,128)(2,1)S(1)} collective-permute-done((bf16[1,128,128]{2,1,0:T(8,128)(2,1)S(1)}, bf16[1,128,128]{2,1,0:T(8,128)(2,1)S(1)}, u32[]{:S(2)}, u32[]{:S(2)}) %collective-permute-start.13) | collective-permute-done | bytes 32800 | tf_op jit(solution)/shard_map/ppermute | solution.py:40
  36.5 0.5 collective-permute-start.15
  37.0 0.8 %project_own.3.diag_ref = f32[256,128]{1,0:T(8,128)S(1)} custom-call(bf16[2048,1024]{1,0:T(8,128)(2,1)S(1)} %load.1.refs_0_.factor_ref, bf16[4,128,128]{2,1,0:T(8,128)(2,1)S(1)} %join.3.refs_0_), custom_call_target="tpu_custom_call" | custom-call | flops 268435456 | bytes 2097152 | tf_op jit(solution)/shard_map/project_own/pallas_call | solution.py:304
  37.9 0.2 collective-permute-done.15.fields_ref
  38.0 1.1 %project_across.3 = (bf16[192,128]{1,0:T(8,128)(2,1)S(1)}, bf16[64,128]{1,0:T(8,128)(2,1)S(1)}, f32[128,128]{1,0:T(8,128)S(1)}) custom-call(f32[128,128]{1,0:T(8,128)S(1)} %get-tuple-element.39.x_ref, bf16[2048,1024]{1,0:T(8,128)(2,1)S(1)} %load.1.refs_0_.factor_ref, f32[256,128]{1,0:T(8,128)S(1)} %project_own.3.diag_ref, ...), custom_call_target="tpu_custom_call" | custom-call | flops 268435456 | bytes 2097152 | tf_op jit(solution)/shard_map/project_across/pallas_call | solution.py:328
  39.2 1.5 %collective-permute-start.17 = (bf16[192,128]{1,0:T(8,128)(2,1)S(1)}, bf16[192,128]{1,0:T(8,128)(2,1)S(1)}, u32[]{:S(2)}, u32[]{:S(2)}) collective-permute-start(bf16[192,128]{1,0:T(8,128)(2,1)S(1)} %get-tuple-element.42), channel_id=1, source_target_pairs={{0,24},{8,16},{16,8},{24,0},{1,25},{9,17},{17,9},{25,1},{2,26},{10... | collective-permute-start | bytes 147464 | tf_op jit(solution)/shard_map/ppermute | solution.py:40
  40.6 0.5 collective-permute-start.16
  41.1 1.5 %collective-permute-start.18 = (bf16[64,128]{1,0:T(8,128)(2,1)S(1)}, bf16[64,128]{1,0:T(8,128)(2,1)S(1)}, u32[]{:S(2)}, u32[]{:S(2)}) collective-permute-start(bf16[64,128]{1,0:T(8,128)(2,1)S(1)} %get-tuple-element.43.refs_0_), channel_id=1, source_target_pairs={{0,16},{8,24},{16,0},{24,8},{1,17},{9,25},{17,1},{25,9},{2,18},{10... | collective-permute-start | bytes 49160 | tf_op jit(solution)/shard_map/ppermute | solution.py:40
  42.7 2.2 %collective-permute-done.18.refs_2_ = bf16[64,128]{1,0:T(8,128)(2,1)S(1)} collective-permute-done((bf16[64,128]{1,0:T(8,128)(2,1)S(1)}, bf16[64,128]{1,0:T(8,128)(2,1)S(1)}, u32[]{:S(2)}, u32[]{:S(2)}) %collective-permute-start.18) | collective-permute-done | bytes 16416 | tf_op jit(solution)/shard_map/ppermute | solution.py:40
  44.9 0.0 collective-permute-done.17.refs_1_.refs_3_
  44.9 0.7 %term_first.3 = (bf16[128,2048]{1,0:T(8,128)(2,1)S(1)}, bf16[2,128,128]{2,1,0:T(8,128)(2,1)S(1)}) custom-call(f32[1,256]{1,0:T(1,128)S(1)} %bitcast.14, bf16[2048,1024]{1,0:T(8,128)(2,1)S(1)} %load.1.refs_0_.factor_ref, bf16[64,128]{1,0:T(8,128)(2,1)S(1)} %get-tuple-element.43.refs_0_, bf16[192,128]{1,0:T(8,128)(2,1)S(1)} %collective-permute-done.16.refs_0_.refs_1_, ...), custom_call_target="tpu_custom_call" | custom-call | flops 134217728 | bytes 2097152 | tf_op jit(solution)/shard_map/term_first/pallas_call | solution.py:341
  45.6 0.1 collective-permute-start.19
  45.7 0.8 %term.6 = (f32[2,128,128]{2,1,0:T(8,128)S(1)}, bf16[2,128,128]{2,1,0:T(8,128)(2,1)S(1)}) custom-call(bf16[128,2048]{1,0:T(8,128)(2,1)S(1)} %get-tuple-element.44.coef_ref, bf16[2048,1024]{1,0:T(8,128)(2,1)S(1)} %load.1.refs_0_.factor_ref), custom_call_target="tpu_custom_call" | custom-call | flops 268435456 | bytes 2097152 | tf_op jit(solution)/shard_map/term/pallas_call | solution.py:351
  46.5 0.6 %collective-permute-start.20 = (bf16[2,128,128]{2,1,0:T(8,128)(2,1)S(1)}, bf16[2,128,128]{2,1,0:T(8,128)(2,1)S(1)}, u32[]{:S(2)}, u32[]{:S(2)}) collective-permute-start(bf16[2,128,128]{2,1,0:T(8,128)(2,1)S(1)} %get-tuple-element.49), channel_id=1, source_target_pairs={{0,1},{1,0},{2,3},{3,2},{4,5},{5,4},{6,7},{7,6},{8,9},{9,8},{10,11... | collective-permute-start | bytes 196616 | tf_op jit(solution)/shard_map/ppermute | solution.py:40
  47.1 0.0 collective-permute-done.19.got_ref
  47.1 2.1 %collective-permute-start.21 = (bf16[1,128,128]{2,1,0:T(8,128)(2,1)S(1)}, bf16[1,128,128]{2,1,0:T(8,128)(2,1)S(1)}, u32[]{:S(2)}, u32[]{:S(2)}) collective-permute-start(bf16[1,128,128]{2,1,0:T(8,128)(2,1)S(1)} %get-tuple-element.47.refs_0_), channel_id=1, source_target_pairs={{0,7},{1,6},{2,5},{3,4},{4,3},{5,2},{6,1},{7,0},{8,15},{9,14},{10,... | collective-permute-start | bytes 98312 | tf_op jit(solution)/shard_map/ppermute | solution.py:40
  49.2 0.0 collective-permute-start.22
  49.2 0.5 term.7.mine_ref
  49.7 0.0 collective-permute-done.20.got_ref
  49.7 1.8 %collective-permute-start.23 = (bf16[1,128,128]{2,1,0:T(8,128)(2,1)S(1)}, bf16[1,128,128]{2,1,0:T(8,128)(2,1)S(1)}, u32[]{:S(2)}, u32[]{:S(2)}) collective-permute-start(bf16[1,128,128]{2,1,0:T(8,128)(2,1)S(1)} %get-tuple-element.51), channel_id=1, source_target_pairs={{0,3},{1,2},{2,1},{3,0},{4,7},{5,6},{6,5},{7,4},{8,11},{9,10},{10,... | collective-permute-start | bytes 98312 | tf_op jit(solution)/shard_map/ppermute | solution.py:40
  51.5 0.2 local.3.base_ref
  51.7 0.8 %collective-permute-done.21.refs_1_ = bf16[1,128,128]{2,1,0:T(8,128)(2,1)S(1)} collective-permute-done((bf16[1,128,128]{2,1,0:T(8,128)(2,1)S(1)}, bf16[1,128,128]{2,1,0:T(8,128)(2,1)S(1)}, u32[]{:S(2)}, u32[]{:S(2)}) %collective-permute-start.21) | collective-permute-done | bytes 32800 | tf_op jit(solution)/shard_map/ppermute | solution.py:40
  52.4 1.3 %collective-permute-done.22.refs_2_ = bf16[1,128,128]{2,1,0:T(8,128)(2,1)S(1)} collective-permute-done((bf16[1,128,128]{2,1,0:T(8,128)(2,1)S(1)}, bf16[1,128,128]{2,1,0:T(8,128)(2,1)S(1)}, u32[]{:S(2)}, u32[]{:S(2)}) %collective-permute-start.22) | collective-permute-done | bytes 32800 | tf_op jit(solution)/shard_map/ppermute | solution.py:40
  53.7 0.0 collective-permute-done.23.refs_3_
  53.7 0.7 %update.3 = (f32[128,128]{1,0:T(8,128)}, f32[128,128]{1,0:T(8,128)}) custom-call(f32[128,128]{1,0:T(8,128)S(1)} %get-tuple-element.39.x_ref, f32[128,128]{1,0:T(8,128)S(1)} %local.3.base_ref, f32[1,128,128]{2,1,0:T(8,128)S(1)} %get-tuple-element.50.refs_0_, bf16[1,128,128]{2,1,0:T(8,128)(2,1)S(1)} %collective-permute-done.21.refs_1_, ...), custom_call_target="tpu_custom_call" | custom-call | bytes 262144 | tf_op jit(solution)/shard_map/update/pallas_call | solution.py:380
  (14 shorter events, 0.1 us)
Async XLA Ops:
  1.5 7.9 %collective-permute-start.2 = (bf16[1,128,128]{2,1,0:T(8,128)(2,1)S(1)}, bf16[1,128,128]{2,1,0:T(8,128)(2,1)S(1)}, u32[]{:S(2)}, u32[]{:S(2)}) collective-permute-start(bf16[1,128,128]{2,1,0:T(8,128)(2,1)S(1)} %fusion.refs_1_), channel_id=1, source_target_pairs={{0,5},{1,4},{2,7},{3,6},{4,1},{5,0},{6,3},{7,2},{8,13},{9,12},{10,... | collective-permute-start | bytes 98312 | tf_op jit(solution)/shard_map/ppermute | solution.py:40
  5.0 5.2 %collective-permute-start.1 = (bf16[1,128,128]{2,1,0:T(8,128)(2,1)S(1)}, bf16[1,128,128]{2,1,0:T(8,128)(2,1)S(1)}, u32[]{:S(2)}, u32[]{:S(2)}) collective-permute-start(bf16[1,128,128]{2,1,0:T(8,128)(2,1)S(1)} %fusion.refs_1_), channel_id=1, source_target_pairs={{0,7},{1,6},{2,5},{3,4},{4,3},{5,2},{6,1},{7,0},{8,15},{9,14},{10,... | collective-permute-start | bytes 98312 | tf_op jit(solution)/shard_map/ppermute | solution.py:40
  6.6 3.8 %collective-permute-start = (bf16[1,128,128]{2,1,0:T(8,128)(2,1)S(1)}, bf16[1,128,128]{2,1,0:T(8,128)(2,1)S(1)}, u32[]{:S(2)}, u32[]{:S(2)}) collective-permute-start(bf16[1,128,128]{2,1,0:T(8,128)(2,1)S(1)} %fusion.refs_1_), channel_id=1, source_target_pairs={{0,3},{1,2},{2,1},{3,0},{4,7},{5,6},{6,5},{7,4},{8,11},{9,10},{10,... | collective-permute-start | bytes 98312 | tf_op jit(solution)/shard_map/ppermute | solution.py:40
  6.8 2.2 %copy-start = (bf16[256,8,1024]{2,1,0:T(8,128)(2,1)S(1)}, bf16[256,8,1024]{2,1,0:T(8,128)(2,1)}, u32[]{:S(2)}) copy-start(bf16[256,8,1024]{2,1,0:T(8,128)(2,1)} %param.6) | copy-start | bytes 12582916
  9.4 2.7 %copy-start.1 = (f32[16,8,128]{2,1,0:T(8,128)S(1)}, f32[16,8,128]{2,1,0:T(8,128)}, u32[]{:S(2)}) copy-start(f32[16,8,128]{2,1,0:T(8,128)} %param.4) | copy-start | bytes 196612
  10.4 9.7 %copy-start.3 = (f32[256]{0:T(256)S(1)}, f32[256]{0:T(256)}, u32[]{:S(2)}) copy-start(f32[256]{0:T(256)} %param.7) | copy-start | bytes 3076
  10.4 1.7 %collective-permute-start.3 = (bf16[4,128,128]{2,1,0:T(8,128)(2,1)S(1)}, bf16[4,128,128]{2,1,0:T(8,128)(2,1)S(1)}, u32[]{:S(2)}, u32[]{:S(2)}) collective-permute-start(bf16[4,128,128]{2,1,0:T(8,128)(2,1)S(1)} %join.2.refs_0_), channel_id=1, source_target_pairs={{0,1},{1,0},{2,3},{3,2},{4,5},{5,4},{6,7},{7,6},{8,9},{9,8},{10,11... | collective-permute-start | bytes 393224 | tf_op jit(solution)/shard_map/ppermute | solution.py:40
  13.3 6.8 %collective-permute-start.5 = (bf16[192,128]{1,0:T(8,128)(2,1)S(1)}, bf16[192,128]{1,0:T(8,128)(2,1)S(1)}, u32[]{:S(2)}, u32[]{:S(2)}) collective-permute-start(bf16[192,128]{1,0:T(8,128)(2,1)S(1)} %get-tuple-element.29), channel_id=1, source_target_pairs={{0,24},{8,16},{16,8},{24,0},{1,25},{9,17},{17,9},{25,1},{2,26},{10... | collective-permute-start | bytes 147464 | tf_op jit(solution)/shard_map/ppermute | solution.py:40
  15.7 4.3 %collective-permute-start.4 = (bf16[192,128]{1,0:T(8,128)(2,1)S(1)}, bf16[192,128]{1,0:T(8,128)(2,1)S(1)}, u32[]{:S(2)}, u32[]{:S(2)}) collective-permute-start(bf16[192,128]{1,0:T(8,128)(2,1)S(1)} %get-tuple-element.29), channel_id=1, source_target_pairs={{0,8},{8,0},{16,24},{24,16},{1,9},{9,1},{17,25},{25,17},{2,10},{10... | collective-permute-start | bytes 147464 | tf_op jit(solution)/shard_map/ppermute | solution.py:40
  16.3 3.7 %collective-permute-start.6 = (bf16[64,128]{1,0:T(8,128)(2,1)S(1)}, bf16[64,128]{1,0:T(8,128)(2,1)S(1)}, u32[]{:S(2)}, u32[]{:S(2)}) collective-permute-start(bf16[64,128]{1,0:T(8,128)(2,1)S(1)} %get-tuple-element.30.refs_0_), channel_id=1, source_target_pairs={{0,16},{8,24},{16,0},{24,8},{1,17},{9,25},{17,1},{25,9},{2,18},{10... | collective-permute-start | bytes 49160 | tf_op jit(solution)/shard_map/ppermute | solution.py:40
  20.8 1.4 %collective-permute-start.7 = (bf16[2,128,128]{2,1,0:T(8,128)(2,1)S(1)}, bf16[2,128,128]{2,1,0:T(8,128)(2,1)S(1)}, u32[]{:S(2)}, u32[]{:S(2)}) collective-permute-start(bf16[2,128,128]{2,1,0:T(8,128)(2,1)S(1)} %get-tuple-element.33), channel_id=1, source_target_pairs={{0,1},{1,0},{2,3},{3,2},{4,5},{5,4},{6,7},{7,6},{8,9},{9,8},{10,11... | collective-permute-start | bytes 196616 | tf_op jit(solution)/shard_map/ppermute | solution.py:40
  20.8 5.8 %copy-start.2 = (f32[8,128]{1,0:T(8,128)S(1)}, f32[8,128]{1,0:T(8,128)}, u32[]{:S(2)}) copy-start(f32[8,128]{1,0:T(8,128)} %amp_ref.3) | copy-start | bytes 12292
  21.7 3.2 %collective-permute-start.8 = (bf16[2,128,128]{2,1,0:T(8,128)(2,1)S(1)}, bf16[2,128,128]{2,1,0:T(8,128)(2,1)S(1)}, u32[]{:S(2)}, u32[]{:S(2)}) collective-permute-start(bf16[2,128,128]{2,1,0:T(8,128)(2,1)S(1)} %get-tuple-element.36), channel_id=1, source_target_pairs={{0,1},{1,0},{2,3},{3,2},{4,5},{5,4},{6,7},{7,6},{8,9},{9,8},{10,11... | collective-permute-start | bytes 196616 | tf_op jit(solution)/shard_map/ppermute | solution.py:40
  22.2 5.3 %collective-permute-start.9 = (bf16[1,128,128]{2,1,0:T(8,128)(2,1)S(1)}, bf16[1,128,128]{2,1,0:T(8,128)(2,1)S(1)}, u32[]{:S(2)}, u32[]{:S(2)}) collective-permute-start(bf16[1,128,128]{2,1,0:T(8,128)(2,1)S(1)} %get-tuple-element.34.refs_0_), channel_id=1, source_target_pairs={{0,7},{1,6},{2,5},{3,4},{4,3},{5,2},{6,1},{7,0},{8,15},{9,14},{10,... | collective-permute-start | bytes 98312 | tf_op jit(solution)/shard_map/ppermute | solution.py:40
  24.4 4.5 %collective-permute-start.10 = (bf16[1,128,128]{2,1,0:T(8,128)(2,1)S(1)}, bf16[1,128,128]{2,1,0:T(8,128)(2,1)S(1)}, u32[]{:S(2)}, u32[]{:S(2)}) collective-permute-start(bf16[1,128,128]{2,1,0:T(8,128)(2,1)S(1)} %get-tuple-element.35.refs_1_), channel_id=1, source_target_pairs={{0,5},{1,4},{2,7},{3,6},{4,1},{5,0},{6,3},{7,2},{8,13},{9,12},{10,... | collective-permute-start | bytes 98312 | tf_op jit(solution)/shard_map/ppermute | solution.py:40
  24.9 3.9 %collective-permute-start.11 = (bf16[1,128,128]{2,1,0:T(8,128)(2,1)S(1)}, bf16[1,128,128]{2,1,0:T(8,128)(2,1)S(1)}, u32[]{:S(2)}, u32[]{:S(2)}) collective-permute-start(bf16[1,128,128]{2,1,0:T(8,128)(2,1)S(1)} %get-tuple-element.38), channel_id=1, source_target_pairs={{0,3},{1,2},{2,1},{3,0},{4,7},{5,6},{6,5},{7,4},{8,11},{9,10},{10,... | collective-permute-start | bytes 98312 | tf_op jit(solution)/shard_map/ppermute | solution.py:40
  28.9 4.3 %collective-permute-start.14 = (bf16[1,128,128]{2,1,0:T(8,128)(2,1)S(1)}, bf16[1,128,128]{2,1,0:T(8,128)(2,1)S(1)}, u32[]{:S(2)}, u32[]{:S(2)}) collective-permute-start(bf16[1,128,128]{2,1,0:T(8,128)(2,1)S(1)} %get-tuple-element.40.refs_1_), channel_id=1, source_target_pairs={{0,5},{1,4},{2,7},{3,6},{4,1},{5,0},{6,3},{7,2},{8,13},{9,12},{10,... | collective-permute-start | bytes 98312 | tf_op jit(solution)/shard_map/ppermute | solution.py:40
  31.3 5.2 %collective-permute-start.13 = (bf16[1,128,128]{2,1,0:T(8,128)(2,1)S(1)}, bf16[1,128,128]{2,1,0:T(8,128)(2,1)S(1)}, u32[]{:S(2)}, u32[]{:S(2)}) collective-permute-start(bf16[1,128,128]{2,1,0:T(8,128)(2,1)S(1)} %get-tuple-element.40.refs_1_), channel_id=1, source_target_pairs={{0,7},{1,6},{2,5},{3,4},{4,3},{5,2},{6,1},{7,0},{8,15},{9,14},{10,... | collective-permute-start | bytes 98312 | tf_op jit(solution)/shard_map/ppermute | solution.py:40
  32.7 3.8 %collective-permute-start.12 = (bf16[1,128,128]{2,1,0:T(8,128)(2,1)S(1)}, bf16[1,128,128]{2,1,0:T(8,128)(2,1)S(1)}, u32[]{:S(2)}, u32[]{:S(2)}) collective-permute-start(bf16[1,128,128]{2,1,0:T(8,128)(2,1)S(1)} %get-tuple-element.40.refs_1_), channel_id=1, source_target_pairs={{0,3},{1,2},{2,1},{3,0},{4,7},{5,6},{6,5},{7,4},{8,11},{9,10},{10,... | collective-permute-start | bytes 98312 | tf_op jit(solution)/shard_map/ppermute | solution.py:40
  36.5 1.5 %collective-permute-start.15 = (bf16[4,128,128]{2,1,0:T(8,128)(2,1)S(1)}, bf16[4,128,128]{2,1,0:T(8,128)(2,1)S(1)}, u32[]{:S(2)}, u32[]{:S(2)}) collective-permute-start(bf16[4,128,128]{2,1,0:T(8,128)(2,1)S(1)} %join.3.refs_0_), channel_id=1, source_target_pairs={{0,1},{1,0},{2,3},{3,2},{4,5},{5,4},{6,7},{7,6},{8,9},{9,8},{10,11... | collective-permute-start | bytes 393224 | tf_op jit(solution)/shard_map/ppermute | solution.py:40
  39.2 5.7 %collective-permute-start.17 = (bf16[192,128]{1,0:T(8,128)(2,1)S(1)}, bf16[192,128]{1,0:T(8,128)(2,1)S(1)}, u32[]{:S(2)}, u32[]{:S(2)}) collective-permute-start(bf16[192,128]{1,0:T(8,128)(2,1)S(1)} %get-tuple-element.42), channel_id=1, source_target_pairs={{0,24},{8,16},{16,8},{24,0},{1,25},{9,17},{17,9},{25,1},{2,26},{10... | collective-permute-start | bytes 147464 | tf_op jit(solution)/shard_map/ppermute | solution.py:40
  40.6 4.3 %collective-permute-start.16 = (bf16[192,128]{1,0:T(8,128)(2,1)S(1)}, bf16[192,128]{1,0:T(8,128)(2,1)S(1)}, u32[]{:S(2)}, u32[]{:S(2)}) collective-permute-start(bf16[192,128]{1,0:T(8,128)(2,1)S(1)} %get-tuple-element.42), channel_id=1, source_target_pairs={{0,8},{8,0},{16,24},{24,16},{1,9},{9,1},{17,25},{25,17},{2,10},{10... | collective-permute-start | bytes 147464 | tf_op jit(solution)/shard_map/ppermute | solution.py:40
  41.1 3.7 %collective-permute-start.18 = (bf16[64,128]{1,0:T(8,128)(2,1)S(1)}, bf16[64,128]{1,0:T(8,128)(2,1)S(1)}, u32[]{:S(2)}, u32[]{:S(2)}) collective-permute-start(bf16[64,128]{1,0:T(8,128)(2,1)S(1)} %get-tuple-element.43.refs_0_), channel_id=1, source_target_pairs={{0,16},{8,24},{16,0},{24,8},{1,17},{9,25},{17,1},{25,9},{2,18},{10... | collective-permute-start | bytes 49160 | tf_op jit(solution)/shard_map/ppermute | solution.py:40
  45.6 1.4 %collective-permute-start.19 = (bf16[2,128,128]{2,1,0:T(8,128)(2,1)S(1)}, bf16[2,128,128]{2,1,0:T(8,128)(2,1)S(1)}, u32[]{:S(2)}, u32[]{:S(2)}) collective-permute-start(bf16[2,128,128]{2,1,0:T(8,128)(2,1)S(1)} %get-tuple-element.46), channel_id=1, source_target_pairs={{0,1},{1,0},{2,3},{3,2},{4,5},{5,4},{6,7},{7,6},{8,9},{9,8},{10,11... | collective-permute-start | bytes 196616 | tf_op jit(solution)/shard_map/ppermute | solution.py:40
  46.5 3.2 %collective-permute-start.20 = (bf16[2,128,128]{2,1,0:T(8,128)(2,1)S(1)}, bf16[2,128,128]{2,1,0:T(8,128)(2,1)S(1)}, u32[]{:S(2)}, u32[]{:S(2)}) collective-permute-start(bf16[2,128,128]{2,1,0:T(8,128)(2,1)S(1)} %get-tuple-element.49), channel_id=1, source_target_pairs={{0,1},{1,0},{2,3},{3,2},{4,5},{5,4},{6,7},{7,6},{8,9},{9,8},{10,11... | collective-permute-start | bytes 196616 | tf_op jit(solution)/shard_map/ppermute | solution.py:40
  47.1 5.3 %collective-permute-start.21 = (bf16[1,128,128]{2,1,0:T(8,128)(2,1)S(1)}, bf16[1,128,128]{2,1,0:T(8,128)(2,1)S(1)}, u32[]{:S(2)}, u32[]{:S(2)}) collective-permute-start(bf16[1,128,128]{2,1,0:T(8,128)(2,1)S(1)} %get-tuple-element.47.refs_0_), channel_id=1, source_target_pairs={{0,7},{1,6},{2,5},{3,4},{4,3},{5,2},{6,1},{7,0},{8,15},{9,14},{10,... | collective-permute-start | bytes 98312 | tf_op jit(solution)/shard_map/ppermute | solution.py:40
  49.2 4.6 %collective-permute-start.22 = (bf16[1,128,128]{2,1,0:T(8,128)(2,1)S(1)}, bf16[1,128,128]{2,1,0:T(8,128)(2,1)S(1)}, u32[]{:S(2)}, u32[]{:S(2)}) collective-permute-start(bf16[1,128,128]{2,1,0:T(8,128)(2,1)S(1)} %get-tuple-element.48.refs_1_), channel_id=1, source_target_pairs={{0,5},{1,4},{2,7},{3,6},{4,1},{5,0},{6,3},{7,2},{8,13},{9,12},{10,... | collective-permute-start | bytes 98312 | tf_op jit(solution)/shard_map/ppermute | solution.py:40
  49.7 4.0 %collective-permute-start.23 = (bf16[1,128,128]{2,1,0:T(8,128)(2,1)S(1)}, bf16[1,128,128]{2,1,0:T(8,128)(2,1)S(1)}, u32[]{:S(2)}, u32[]{:S(2)}) collective-permute-start(bf16[1,128,128]{2,1,0:T(8,128)(2,1)S(1)} %get-tuple-element.51), channel_id=1, source_target_pairs={{0,3},{1,2},{2,1},{3,0},{4,7},{5,6},{6,5},{7,4},{8,11},{9,10},{10,... | collective-permute-start | bytes 98312 | tf_op jit(solution)/shard_map/ppermute | solution.py:40

commit v9 on v8

--- a/solution.py
+++ b/solution.py
@@ -52,7 +52,7 @@
 
 
 def join_kernel(*refs):
-    part_refs, out_ref = refs[1:-1], refs[-1]
+    part_refs, out_ref = refs[2:-1], refs[-1]
     at = 0
     for ref in part_refs:
         out_ref[at : at + ref.shape[0]] = ref[...]
@@ -78,7 +78,7 @@
     lines = fields[0].shape[0]
     count = factor_ref.shape[0]
     field = jnp.concatenate(fields, axis=1)
-    step = min(1024, count)
+    step = min(2048, count)
     row_of = lax.broadcasted_iota(jnp.int32, (rows, lines), 0)
     lane_of = lax.broadcasted_iota(jnp.int32, (rows, lines), 1)
     same = (lax.rem(lane_of, rows) == row_of).astype(jnp.float32)
@@ -111,8 +111,23 @@
     diagonal(rows, spots, blocks_of(field_refs), factor_ref, store)
 
 
-def second_kernel(rows, cols, halve, spots, known, x_ref, factor_ref, diag_ref, fields_ref, *refs):
-    other_refs, (pay_ref, part_ref, along_ref, total) = refs[:-4], refs[-4:]
+def columns_kernel(halve, spots, x_ref, bundle_ref, twin_ref, along_ref, short_ref):
+    me = lax.axis_index("tile")
+    low = jnp.zeros(x_ref.shape, jnp.float32)
+    high = low
+    for spot, block in zip(spots, blocks_of([bundle_ref, twin_ref])):
+        part, place = block.astype(jnp.float32), place_of(spot)
+        low = jnp.where(place == me - 1, part, low)
+        high = jnp.where(place == me + 1, part, high)
+    own = 0.5 * x_ref[...] if halve else x_ref[...]
+    along = stencil(low, own, high, COL_TAPS, 1)
+    along_ref[...] = along
+    short_ref[...] = along.astype(jnp.bfloat16)
+
+
+def second_kernel(
+    rows, cols, spots, factor_ref, diag_ref, fields_ref, short_ref, pay_ref, part_ref, total
+):
     lines = cols * rows
     if total.shape[0] > factor_ref.shape[0] // rows:
         total[...] = jnp.zeros_like(total)
@@ -140,17 +155,7 @@
             ref[first + cols : first + 2 * cols, :] = lower
 
     head = total.shape[0] // LANES * 2 * cols
-    me = lax.axis_index("tile")
-    low = jnp.zeros((lines, LANES), jnp.float32)
-    high = low
-    for spot, block in zip(spots + known, blocks_of((fields_ref,) + other_refs)):
-        part, place = block.astype(jnp.float32), place_of(spot)
-        low = jnp.where(place == me - 1, part, low)
-        high = jnp.where(place == me + 1, part, high)
-    own = 0.5 * x_ref[...] if halve else x_ref[...]
-    along = stencil(low, own, high, COL_TAPS, 1)
-    along_ref[...] = along
-    pay_ref[head:, :] = along.astype(jnp.bfloat16)
+    pay_ref[head:, :] = short_ref[...]
 
 
 def product(coef, spots, factor_ref, out_ref):
@@ -292,7 +297,7 @@
         name="load",
     )(flat)
     half = near // 2
-    close, away = list(range(half)), list(range(near - 1, half - 1, -1))
+    close = list(range(half))
 
     def spots_of(masks, other):
         return [(mask, other != (mask > 0)) for mask in masks]
@@ -311,32 +316,36 @@
 
     for step in range(ITERS):
         halve = step == 0
+        last = step == ITERS - 1
+        away = sorted(range(half, near), reverse=last)
         order = list(range(1, near))
         order.sort(key=lambda mask: (mask == half, mask))
         parts = [cross(short, mask) for mask in order]
+        twin = swap(short, "tile", 1)
         bundle = call(
             join_kernel,
-            shape(bf16, near, lines, width),
-            in_specs=[pl.BlockSpec(memory_space=pl.ANY)]
-            + [pl.BlockSpec(memory_space=pltpu.VMEM)] * near,
+            shape(bf16, near - 1, lines, width),
+            in_specs=[pl.BlockSpec(memory_space=pl.ANY)] * 2
+            + [pl.BlockSpec(memory_space=pltpu.VMEM)] * (near - 1),
             name="join",
-        )(held, short, *parts)
+        )(held, twin, *parts)
         across = swap(bundle, "tile", 1)
-        known = spots_of([0] + order, False)
-        diag = first([bundle], known)
-        spots = spots_of([0] + order, True)
-        pay, part, along = call(
-            partial(second_kernel, rows, cols, halve, spots, known),
-            (
-                shape(bf16, pay_rows, width),
-                shape(bf16, pay_rows - lines, width),
-                shape(f32, lines, width),
-            ),
+        known = spots_of(order, False) + [(0, True)]
+        diag = first([bundle, twin, short], known + [(0, False)])
+        spots = spots_of(order, True)
+        along, along_short = call(
+            partial(columns_kernel, halve, known),
+            (shape(f32, lines, width), shape(bf16, lines, width)),
+            name="columns",
+        )(x, bundle, twin)
+        pay, part = call(
+            partial(second_kernel, rows, cols, spots),
+            (shape(bf16, pay_rows, width), shape(bf16, pay_rows - lines, width)),
             flops=work,
             moved=flat.size,
             scratch_shapes=[pltpu.VMEM((blocks * LANES, lines), f32)],
             name="project_across",
-        )(x, held, diag, across, bundle)
+        )(held, diag, across, along_short)
         pays = [swap(part if mask & (mask + 1) else pay, "grp", mask) for mask in range(1, groups)]
         coef, far = call(
             partial(far_kernel, rows, cols, groups, ncells_all, spots_of(away, True)),
@@ -376,7 +385,6 @@
         base = call(
             partial(local_kernel, rows, cols, halve), shape(f32, lines, width), name="local"
         )(b, x, amplitude, along, *rims)
-        last = step == ITERS - 1
         x, short = call(
             partial(update_kernel, halve, last),
             (

time: 54.6 us -> 54.2 us (level)
  starting transfers between devices: 26.4 us -> 25.4 us
  Pallas kernels: 9.48 us -> 10.1 us
    ppermute x24 -> x26, starting transfers between devices: 26.4 us -> 25.4 us  [swap(): lax.ppermute(value, axis, [(i, i ^ mask) for i in range(lax.axis_size(axi...]
    ppermute x24 -> x26, waiting for transfers between devices: 14.7 us -> 14.5 us  [swap(): lax.ppermute(value, axis, [(i, i ^ mask) for i in range(lax.axis_size(axi...]
    pallas_call x4 -> x6, Pallas kernels: 2.32 us -> 2.48 us  [the longest x2 1.75 us: on_device(): call(partial(second_kernel, rows, cols, spots), (shape(bf16, pay_rows, wi...]
  transfers between devices with their start and end apart: 24 -> 26, of which waited for: 12 -> 11; matrix products, arithmetic and copies ran while one was open for 0% -> 0% of each run, Pallas kernels for 9% -> 11%
where the time goes in v9:
time: 54.2 us; the launch traced here: 53.9 us
  starting transfers between devices  25.4 us (47%)
  waiting for transfers between devices  14.5 us (27%)
  Pallas kernels  10.1 us (19%)
  local copies, waits for them, and re-layouts  2.21 us (4%)
  between operations  0.87 us (2%)
  other arithmetic  0.85 us (2%)
    ppermute x26, starting transfers between devices, swap(): lax.ppermute(value, axis, [(i, i ^ mask) for i in range(lax.axis_size(axi...  25.4 us
    ppermute x26, waiting for transfers between devices, swap(): lax.ppermute(value, axis, [(i, i ^ mask) for i in range(lax.axis_size(axi...  14.5 us
    pallas_call x4, Pallas kernels, term(): call(partial(term_kernel, wanted, len(after)), in_specs=[pl.BlockSpec(mem...  2.59 us
    unnamed x8, local copies, waits for them, and re-layouts  2.21 us
    pallas_call x2, Pallas kernels, first(): call(partial(first_kernel, rows, spots, len(before)), shape(f32, blocks *...  2.06 us
    pallas_call x2, Pallas kernels, on_device(): call(partial(second_kernel, rows, cols, spots), (shape(bf16, pay_rows, wi...  1.75 us
    pallas_call x2, Pallas kernels, on_device(): call(partial(far_kernel, rows, cols, groups, ncells_all, spots_of(away, T...  1.45 us
  transfers between devices with their start and end apart: 26, of which 11 were waited for; matrix products, arithmetic and copies ran while one was open for 0% of the time, Pallas kernels for 11%

profile of v9, /device:TPU:0, one launch (start us, length us, event | category | flops | bytes accessed | tf_op | source)
XLA Modules:
  0.0 53.9 jit_solution(15991265826007186101)
XLA Ops:
  0.6 0.8 %fusion.refs_2_ = bf16[1,128,128]{2,1,0:T(8,128)(2,1)S(1)} fusion(f32[16,8,128]{2,1,0:T(8,128)} %param.4), kind=kLoop, calls=%fused_computation.1 | loop fusion | flops 32768 | bytes 98304 | tf_op jit(solution)/shard_map/convert_element_type | solution.py:272
  1.5 3.5 %collective-permute-start.3 = (bf16[1,128,128]{2,1,0:T(8,128)(2,1)S(1)}, bf16[1,128,128]{2,1,0:T(8,128)(2,1)S(1)}, u32[]{:S(2)}, u32[]{:S(2)}) collective-permute-start(bf16[1,128,128]{2,1,0:T(8,128)(2,1)S(1)} %fusion.refs_2_), channel_id=1, source_target_pairs={{0,5},{1,4},{2,7},{3,6},{4,1},{5,0},{6,3},{7,2},{8,13},{9,12},{10,... | collective-permute-start | bytes 98312 | tf_op jit(solution)/shard_map/ppermute | solution.py:40
  5.0 1.6 %collective-permute-start.2 = (bf16[1,128,128]{2,1,0:T(8,128)(2,1)S(1)}, bf16[1,128,128]{2,1,0:T(8,128)(2,1)S(1)}, u32[]{:S(2)}, u32[]{:S(2)}) collective-permute-start(bf16[1,128,128]{2,1,0:T(8,128)(2,1)S(1)} %fusion.refs_2_), channel_id=1, source_target_pairs={{0,7},{1,6},{2,5},{3,4},{4,3},{5,2},{6,1},{7,0},{8,15},{9,14},{10,... | collective-permute-start | bytes 98312 | tf_op jit(solution)/shard_map/ppermute | solution.py:40
  6.6 0.2 collective-permute-start.1
  6.8 2.2 %copy-done = bf16[256,8,1024]{2,1,0:T(8,128)(2,1)S(1)} copy-done((bf16[256,8,1024]{2,1,0:T(8,128)(2,1)S(1)}, bf16[256,8,1024]{2,1,0:T(8,128)(2,1)}, u32[]{:S(2)}) %copy-start) | copy-done | bytes 4194328
  9.0 0.4 load.1.refs_0_.factor_ref
  9.4 0.0 copy-start.1
  9.4 0.8 %collective-permute-done.2.refs_3_ = bf16[1,128,128]{2,1,0:T(8,128)(2,1)S(1)} collective-permute-done((bf16[1,128,128]{2,1,0:T(8,128)(2,1)S(1)}, bf16[1,128,128]{2,1,0:T(8,128)(2,1)S(1)}, u32[]{:S(2)}, u32[]{:S(2)}) %collective-permute-start.2) | collective-permute-done | bytes 32800 | tf_op jit(solution)/shard_map/ppermute | solution.py:40
  10.2 0.2 collective-permute-done.1.refs_2_
  10.4 0.0 collective-permute-done.refs_1_.twin_ref
  10.4 0.7 %collective-permute-start.4 = (bf16[3,128,128]{2,1,0:T(8,128)(2,1)S(1)}, bf16[3,128,128]{2,1,0:T(8,128)(2,1)S(1)}, u32[]{:S(2)}, u32[]{:S(2)}) collective-permute-start(bf16[3,128,128]{2,1,0:T(8,128)(2,1)S(1)} %join.2.bundle_ref.refs_0_), channel_id=1, source_target_pairs={{0,1},{1,0},{2,3},{3,2},{4,5},{5,4},{6,7},{7,6},{8,9},{9,8},{10,11... | collective-permute-start | bytes 294920 | tf_op jit(solution)/shard_map/ppermute | solution.py:40
  11.1 0.4 columns.2
  11.5 0.0 copy-start.3
  11.5 1.0 %project_own.2.diag_ref = f32[256,128]{1,0:T(8,128)S(1)} custom-call(bf16[2048,1024]{1,0:T(8,128)(2,1)S(1)} %load.1.refs_0_.factor_ref, bf16[3,128,128]{2,1,0:T(8,128)(2,1)S(1)} %join.2.bundle_ref.refs_0_, bf16[1,128,128]{2,1,0:T(8,128)(2,1)S(1)} %collective-permute-done.refs_1_.twin_ref, bf16[1,128,128]{2,1,0:T(8,128)(2,1)S(1)} %fusion.refs_2_), custom_call_target="tpu_custom_call" | custom-call | flops 268435456 | bytes 2097152 | tf_op jit(solution)/shard_map/project_own/pallas_call | solution.py:309
  12.5 0.0 collective-permute-done.4.fields_ref
  12.5 0.9 %project_across.2 = (bf16[192,128]{1,0:T(8,128)(2,1)S(1)}, bf16[64,128]{1,0:T(8,128)(2,1)S(1)}) custom-call(bf16[2048,1024]{1,0:T(8,128)(2,1)S(1)} %load.1.refs_0_.factor_ref, f32[256,128]{1,0:T(8,128)S(1)} %project_own.2.diag_ref, bf16[3,128,128]{2,1,0:T(8,128)(2,1)S(1)} %collective-permute-done.4.fields_ref, bf16[128,128]{1,0:T(8,128)(2,1)S(1)} %get-tuple-element.31.short_ref), custom_call_target="tpu_custom_call" | custom-call | flops 268435456 | bytes 2097152 | tf_op jit(solution)/shard_map/project_across/pallas_call | solution.py:341
  13.4 2.5 %collective-permute-start.6 = (bf16[192,128]{1,0:T(8,128)(2,1)S(1)}, bf16[192,128]{1,0:T(8,128)(2,1)S(1)}, u32[]{:S(2)}, u32[]{:S(2)}) collective-permute-start(bf16[192,128]{1,0:T(8,128)(2,1)S(1)} %get-tuple-element.32), channel_id=1, source_target_pairs={{0,24},{8,16},{16,8},{24,0},{1,25},{9,17},{17,9},{25,1},{2,26},{10... | collective-permute-start | bytes 147464 | tf_op jit(solution)/shard_map/ppermute | solution.py:40
  15.9 0.5 collective-permute-start.5
  16.4 0.5 collective-permute-start.7
  16.9 3.2 %collective-permute-done.7.refs_2_ = bf16[64,128]{1,0:T(8,128)(2,1)S(1)} collective-permute-done((bf16[64,128]{1,0:T(8,128)(2,1)S(1)}, bf16[64,128]{1,0:T(8,128)(2,1)S(1)}, u32[]{:S(2)}, u32[]{:S(2)}) %collective-permute-start.7) | collective-permute-done | bytes 16416 | tf_op jit(solution)/shard_map/ppermute | solution.py:40
  20.2 0.0 collective-permute-done.6.refs_1_.refs_3_
  20.2 0.0 collective-permute-done.5.refs_0_.refs_1_
  20.2 0.7 %term_first.2 = (bf16[128,2048]{1,0:T(8,128)(2,1)S(1)}, bf16[2,128,128]{2,1,0:T(8,128)(2,1)S(1)}) custom-call(f32[1,256]{1,0:T(1,128)S(1)} %bitcast.13, bf16[2048,1024]{1,0:T(8,128)(2,1)S(1)} %load.1.refs_0_.factor_ref, bf16[64,128]{1,0:T(8,128)(2,1)S(1)} %get-tuple-element.33.refs_0_, bf16[192,128]{1,0:T(8,128)(2,1)S(1)} %collective-permute-done.5.refs_0_.refs_1_, ...), custom_call_target="tpu_custom_call" | custom-call | flops 134217728 | bytes 2097152 | tf_op jit(solution)/shard_map/term_first/pallas_call | solution.py:350
  20.9 0.1 collective-permute-start.8
  21.0 0.0 copy-start.2
  21.0 0.8 %term.4 = (f32[2,128,128]{2,1,0:T(8,128)S(1)}, bf16[2,128,128]{2,1,0:T(8,128)(2,1)S(1)}) custom-call(bf16[128,2048]{1,0:T(8,128)(2,1)S(1)} %get-tuple-element.34.coef_ref, bf16[2048,1024]{1,0:T(8,128)(2,1)S(1)} %load.1.refs_0_.factor_ref), custom_call_target="tpu_custom_call" | custom-call | flops 268435456 | bytes 2097152 | tf_op jit(solution)/shard_map/term/pallas_call | solution.py:360
  21.8 0.5 collective-permute-start.9
  22.4 1.8 %collective-permute-start.10 = (bf16[1,128,128]{2,1,0:T(8,128)(2,1)S(1)}, bf16[1,128,128]{2,1,0:T(8,128)(2,1)S(1)}, u32[]{:S(2)}, u32[]{:S(2)}) collective-permute-start(bf16[1,128,128]{2,1,0:T(8,128)(2,1)S(1)} %get-tuple-element.37.refs_0_), channel_id=1, source_target_pairs={{0,5},{1,4},{2,7},{3,6},{4,1},{5,0},{6,3},{7,2},{8,13},{9,12},{10,... | collective-permute-start | bytes 98312 | tf_op jit(solution)/shard_map/ppermute | solution.py:40
  24.1 1.4 %collective-permute-start.11 = (bf16[1,128,128]{2,1,0:T(8,128)(2,1)S(1)}, bf16[1,128,128]{2,1,0:T(8,128)(2,1)S(1)}, u32[]{:S(2)}, u32[]{:S(2)}) collective-permute-start(bf16[1,128,128]{2,1,0:T(8,128)(2,1)S(1)} %get-tuple-element.38.refs_1_), channel_id=1, source_target_pairs={{0,7},{1,6},{2,5},{3,4},{4,3},{5,2},{6,1},{7,0},{8,15},{9,14},{10,... | collective-permute-start | bytes 98312 | tf_op jit(solution)/shard_map/ppermute | solution.py:40
  25.5 0.5 term.5.mine_ref
  26.0 0.0 collective-permute-done.9.got_ref
  26.1 0.1 collective-permute-start.12
  26.2 0.2 local.2.base_ref
  26.4 0.5 collective-permute-done.10.refs_1_
  26.8 2.5 %collective-permute-done.11.refs_2_ = bf16[1,128,128]{2,1,0:T(8,128)(2,1)S(1)} collective-permute-done((bf16[1,128,128]{2,1,0:T(8,128)(2,1)S(1)}, bf16[1,128,128]{2,1,0:T(8,128)(2,1)S(1)}, u32[]{:S(2)}, u32[]{:S(2)}) %collective-permute-start.11) | collective-permute-done | bytes 32800 | tf_op jit(solution)/shard_map/ppermute | solution.py:40
  29.3 0.9 %collective-permute-done.12.refs_3_ = bf16[1,128,128]{2,1,0:T(8,128)(2,1)S(1)} collective-permute-done((bf16[1,128,128]{2,1,0:T(8,128)(2,1)S(1)}, bf16[1,128,128]{2,1,0:T(8,128)(2,1)S(1)}, u32[]{:S(2)}, u32[]{:S(2)}) %collective-permute-start.12) | collective-permute-done | bytes 32800 | tf_op jit(solution)/shard_map/ppermute | solution.py:40
  30.2 0.4 collective-permute-start.16
  30.6 1.4 %collective-permute-start.15 = (bf16[1,128,128]{2,1,0:T(8,128)(2,1)S(1)}, bf16[1,128,128]{2,1,0:T(8,128)(2,1)S(1)}, u32[]{:S(2)}, u32[]{:S(2)}) collective-permute-start(bf16[1,128,128]{2,1,0:T(8,128)(2,1)S(1)} %get-tuple-element.43.refs_2_), channel_id=1, source_target_pairs={{0,7},{1,6},{2,5},{3,4},{4,3},{5,2},{6,1},{7,0},{8,15},{9,14},{10,... | collective-permute-start | bytes 98312 | tf_op jit(solution)/shard_map/ppermute | solution.py:40
  32.1 1.2 %collective-permute-start.14 = (bf16[1,128,128]{2,1,0:T(8,128)(2,1)S(1)}, bf16[1,128,128]{2,1,0:T(8,128)(2,1)S(1)}, u32[]{:S(2)}, u32[]{:S(2)}) collective-permute-start(bf16[1,128,128]{2,1,0:T(8,128)(2,1)S(1)} %get-tuple-element.43.refs_2_), channel_id=1, source_target_pairs={{0,3},{1,2},{2,1},{3,0},{4,7},{5,6},{6,5},{7,4},{8,11},{9,10},{10,... | collective-permute-start | bytes 98312 | tf_op jit(solution)/shard_map/ppermute | solution.py:40
  33.2 0.4 collective-permute-start.13
  33.7 0.9 %collective-permute-done.16.refs_4_ = bf16[1,128,128]{2,1,0:T(8,128)(2,1)S(1)} collective-permute-done((bf16[1,128,128]{2,1,0:T(8,128)(2,1)S(1)}, bf16[1,128,128]{2,1,0:T(8,128)(2,1)S(1)}, u32[]{:S(2)}, u32[]{:S(2)}) %collective-permute-start.16) | collective-permute-done | bytes 32800 | tf_op jit(solution)/shard_map/ppermute | solution.py:40
  34.6 1.2 %collective-permute-done.15.refs_3_ = bf16[1,128,128]{2,1,0:T(8,128)(2,1)S(1)} collective-permute-done((bf16[1,128,128]{2,1,0:T(8,128)(2,1)S(1)}, bf16[1,128,128]{2,1,0:T(8,128)(2,1)S(1)}, u32[]{:S(2)}, u32[]{:S(2)}) %collective-permute-start.15) | collective-permute-done | bytes 32800 | tf_op jit(solution)/shard_map/ppermute | solution.py:40
  35.8 0.6 %collective-permute-start.17 = (bf16[3,128,128]{2,1,0:T(8,128)(2,1)S(1)}, bf16[3,128,128]{2,1,0:T(8,128)(2,1)S(1)}, u32[]{:S(2)}, u32[]{:S(2)}) collective-permute-start(bf16[3,128,128]{2,1,0:T(8,128)(2,1)S(1)} %join.3.bundle_ref.refs_0_), channel_id=1, source_target_pairs={{0,1},{1,0},{2,3},{3,2},{4,5},{5,4},{6,7},{7,6},{8,9},{9,8},{10,11... | collective-permute-start | bytes 294920 | tf_op jit(solution)/shard_map/ppermute | solution.py:40
  36.4 0.3 columns.3
  36.7 1.0 %project_own.3.diag_ref = f32[256,128]{1,0:T(8,128)S(1)} custom-call(bf16[2048,1024]{1,0:T(8,128)(2,1)S(1)} %load.1.refs_0_.factor_ref, bf16[3,128,128]{2,1,0:T(8,128)(2,1)S(1)} %join.3.bundle_ref.refs_0_, bf16[1,128,128]{2,1,0:T(8,128)(2,1)S(1)} %collective-permute-done.13.refs_1_.twin_ref, bf16[1,128,128]{2,1,0:T(8,128)(2,1)S(1)} %get-tuple-element.43.refs_2_), custom_call_target="tpu_custom_call" | custom-call | flops 268435456 | bytes 2097152 | tf_op jit(solution)/shard_map/project_own/pallas_call | solution.py:309
  37.8 0.9 %project_across.3 = (bf16[192,128]{1,0:T(8,128)(2,1)S(1)}, bf16[64,128]{1,0:T(8,128)(2,1)S(1)}) custom-call(bf16[2048,1024]{1,0:T(8,128)(2,1)S(1)} %load.1.refs_0_.factor_ref, f32[256,128]{1,0:T(8,128)S(1)} %project_own.3.diag_ref, bf16[3,128,128]{2,1,0:T(8,128)(2,1)S(1)} %collective-permute-done.17.fields_ref, bf16[128,128]{1,0:T(8,128)(2,1)S(1)} %get-tuple-element.45.short_ref), custom_call_target="tpu_custom_call" | custom-call | flops 268435456 | bytes 2097152 | tf_op jit(solution)/shard_map/project_across/pallas_call | solution.py:341
  38.7 1.5 %collective-permute-start.19 = (bf16[192,128]{1,0:T(8,128)(2,1)S(1)}, bf16[192,128]{1,0:T(8,128)(2,1)S(1)}, u32[]{:S(2)}, u32[]{:S(2)}) collective-permute-start(bf16[192,128]{1,0:T(8,128)(2,1)S(1)} %get-tuple-element.46), channel_id=1, source_target_pairs={{0,24},{8,16},{16,8},{24,0},{1,25},{9,17},{17,9},{25,1},{2,26},{10... | collective-permute-start | bytes 147464 | tf_op jit(solution)/shard_map/ppermute | solution.py:40
  40.1 0.5 collective-permute-start.18
  40.7 1.5 %collective-permute-start.20 = (bf16[64,128]{1,0:T(8,128)(2,1)S(1)}, bf16[64,128]{1,0:T(8,128)(2,1)S(1)}, u32[]{:S(2)}, u32[]{:S(2)}) collective-permute-start(bf16[64,128]{1,0:T(8,128)(2,1)S(1)} %get-tuple-element.47.refs_0_), channel_id=1, source_target_pairs={{0,16},{8,24},{16,0},{24,8},{1,17},{9,25},{17,1},{25,9},{2,18},{10... | collective-permute-start | bytes 49160 | tf_op jit(solution)/shard_map/ppermute | solution.py:40
  42.2 2.2 %collective-permute-done.20.refs_2_ = bf16[64,128]{1,0:T(8,128)(2,1)S(1)} collective-permute-done((bf16[64,128]{1,0:T(8,128)(2,1)S(1)}, bf16[64,128]{1,0:T(8,128)(2,1)S(1)}, u32[]{:S(2)}, u32[]{:S(2)}) %collective-permute-start.20) | collective-permute-done | bytes 16416 | tf_op jit(solution)/shard_map/ppermute | solution.py:40
  44.4 0.0 collective-permute-done.18.refs_0_.refs_1_
  44.4 0.7 %term_first.3 = (bf16[128,2048]{1,0:T(8,128)(2,1)S(1)}, bf16[2,128,128]{2,1,0:T(8,128)(2,1)S(1)}) custom-call(f32[1,256]{1,0:T(1,128)S(1)} %bitcast.14, bf16[2048,1024]{1,0:T(8,128)(2,1)S(1)} %load.1.refs_0_.factor_ref, bf16[64,128]{1,0:T(8,128)(2,1)S(1)} %get-tuple-element.47.refs_0_, bf16[192,128]{1,0:T(8,128)(2,1)S(1)} %collective-permute-done.18.refs_0_.refs_1_, ...), custom_call_target="tpu_custom_call" | custom-call | flops 134217728 | bytes 2097152 | tf_op jit(solution)/shard_map/term_first/pallas_call | solution.py:350
  45.1 0.1 collective-permute-start.21
  45.2 0.8 %term.6 = (f32[2,128,128]{2,1,0:T(8,128)S(1)}, bf16[2,128,128]{2,1,0:T(8,128)(2,1)S(1)}) custom-call(bf16[128,2048]{1,0:T(8,128)(2,1)S(1)} %get-tuple-element.48.coef_ref, bf16[2048,1024]{1,0:T(8,128)(2,1)S(1)} %load.1.refs_0_.factor_ref), custom_call_target="tpu_custom_call" | custom-call | flops 268435456 | bytes 2097152 | tf_op jit(solution)/shard_map/term/pallas_call | solution.py:360
  46.0 0.6 %collective-permute-start.22 = (bf16[2,128,128]{2,1,0:T(8,128)(2,1)S(1)}, bf16[2,128,128]{2,1,0:T(8,128)(2,1)S(1)}, u32[]{:S(2)}, u32[]{:S(2)}) collective-permute-start(bf16[2,128,128]{2,1,0:T(8,128)(2,1)S(1)} %get-tuple-element.53), channel_id=1, source_target_pairs={{0,1},{1,0},{2,3},{3,2},{4,5},{5,4},{6,7},{7,6},{8,9},{9,8},{10,11... | collective-permute-start | bytes 196616 | tf_op jit(solution)/shard_map/ppermute | solution.py:40
  46.6 2.1 %collective-permute-start.23 = (bf16[1,128,128]{2,1,0:T(8,128)(2,1)S(1)}, bf16[1,128,128]{2,1,0:T(8,128)(2,1)S(1)}, u32[]{:S(2)}, u32[]{:S(2)}) collective-permute-start(bf16[1,128,128]{2,1,0:T(8,128)(2,1)S(1)} %get-tuple-element.51.refs_0_), channel_id=1, source_target_pairs={{0,7},{1,6},{2,5},{3,4},{4,3},{5,2},{6,1},{7,0},{8,15},{9,14},{10,... | collective-permute-start | bytes 98312 | tf_op jit(solution)/shard_map/ppermute | solution.py:40
  48.7 0.0 collective-permute-start.24
  48.7 0.5 term.7.mine_ref
  49.2 0.0 collective-permute-done.22.got_ref
  49.2 1.8 %collective-permute-start.25 = (bf16[1,128,128]{2,1,0:T(8,128)(2,1)S(1)}, bf16[1,128,128]{2,1,0:T(8,128)(2,1)S(1)}, u32[]{:S(2)}, u32[]{:S(2)}) collective-permute-start(bf16[1,128,128]{2,1,0:T(8,128)(2,1)S(1)} %get-tuple-element.55), channel_id=1, source_target_pairs={{0,3},{1,2},{2,1},{3,0},{4,7},{5,6},{6,5},{7,4},{8,11},{9,10},{10,... | collective-permute-start | bytes 98312 | tf_op jit(solution)/shard_map/ppermute | solution.py:40
  51.0 0.2 local.3.base_ref
  51.2 0.8 %collective-permute-done.23.refs_1_ = bf16[1,128,128]{2,1,0:T(8,128)(2,1)S(1)} collective-permute-done((bf16[1,128,128]{2,1,0:T(8,128)(2,1)S(1)}, bf16[1,128,128]{2,1,0:T(8,128)(2,1)S(1)}, u32[]{:S(2)}, u32[]{:S(2)}) %collective-permute-start.23) | collective-permute-done | bytes 32800 | tf_op jit(solution)/shard_map/ppermute | solution.py:40
  51.9 1.3 %collective-permute-done.24.refs_2_ = bf16[1,128,128]{2,1,0:T(8,128)(2,1)S(1)} collective-permute-done((bf16[1,128,128]{2,1,0:T(8,128)(2,1)S(1)}, bf16[1,128,128]{2,1,0:T(8,128)(2,1)S(1)}, u32[]{:S(2)}, u32[]{:S(2)}) %collective-permute-start.24) | collective-permute-done | bytes 32800 | tf_op jit(solution)/shard_map/ppermute | solution.py:40
  53.2 0.7 %update.3 = (f32[128,128]{1,0:T(8,128)}, f32[128,128]{1,0:T(8,128)}) custom-call(f32[128,128]{1,0:T(8,128)S(1)} %get-tuple-element.42.x_ref, f32[128,128]{1,0:T(8,128)S(1)} %local.3.base_ref, f32[1,128,128]{2,1,0:T(8,128)S(1)} %get-tuple-element.54.refs_0_, bf16[1,128,128]{2,1,0:T(8,128)(2,1)S(1)} %collective-permute-done.23.refs_1_, ...), custom_call_target="tpu_custom_call" | custom-call | bytes 262144 | tf_op jit(solution)/shard_map/update/pallas_call | solution.py:388
  (20 shorter events, 0.1 us)
Async XLA Ops:
  1.5 7.9 %collective-permute-start.3 = (bf16[1,128,128]{2,1,0:T(8,128)(2,1)S(1)}, bf16[1,128,128]{2,1,0:T(8,128)(2,1)S(1)}, u32[]{:S(2)}, u32[]{:S(2)}) collective-permute-start(bf16[1,128,128]{2,1,0:T(8,128)(2,1)S(1)} %fusion.refs_2_), channel_id=1, source_target_pairs={{0,5},{1,4},{2,7},{3,6},{4,1},{5,0},{6,3},{7,2},{8,13},{9,12},{10,... | collective-permute-start | bytes 98312 | tf_op jit(solution)/shard_map/ppermute | solution.py:40
  5.0 5.2 %collective-permute-start.2 = (bf16[1,128,128]{2,1,0:T(8,128)(2,1)S(1)}, bf16[1,128,128]{2,1,0:T(8,128)(2,1)S(1)}, u32[]{:S(2)}, u32[]{:S(2)}) collective-permute-start(bf16[1,128,128]{2,1,0:T(8,128)(2,1)S(1)} %fusion.refs_2_), channel_id=1, source_target_pairs={{0,7},{1,6},{2,5},{3,4},{4,3},{5,2},{6,1},{7,0},{8,15},{9,14},{10,... | collective-permute-start | bytes 98312 | tf_op jit(solution)/shard_map/ppermute | solution.py:40
  6.6 3.8 %collective-permute-start.1 = (bf16[1,128,128]{2,1,0:T(8,128)(2,1)S(1)}, bf16[1,128,128]{2,1,0:T(8,128)(2,1)S(1)}, u32[]{:S(2)}, u32[]{:S(2)}) collective-permute-start(bf16[1,128,128]{2,1,0:T(8,128)(2,1)S(1)} %fusion.refs_2_), channel_id=1, source_target_pairs={{0,3},{1,2},{2,1},{3,0},{4,7},{5,6},{6,5},{7,4},{8,11},{9,10},{10,... | collective-permute-start | bytes 98312 | tf_op jit(solution)/shard_map/ppermute | solution.py:40
  6.8 3.5 %collective-permute-start = (bf16[1,128,128]{2,1,0:T(8,128)(2,1)S(1)}, bf16[1,128,128]{2,1,0:T(8,128)(2,1)S(1)}, u32[]{:S(2)}, u32[]{:S(2)}) collective-permute-start(bf16[1,128,128]{2,1,0:T(8,128)(2,1)S(1)} %fusion.refs_2_), channel_id=1, source_target_pairs={{0,1},{1,0},{2,3},{3,2},{4,5},{5,4},{6,7},{7,6},{8,9},{9,8},{10,11... | collective-permute-start | bytes 98312 | tf_op jit(solution)/shard_map/ppermute | solution.py:40
  6.8 2.2 %copy-start = (bf16[256,8,1024]{2,1,0:T(8,128)(2,1)S(1)}, bf16[256,8,1024]{2,1,0:T(8,128)(2,1)}, u32[]{:S(2)}) copy-start(bf16[256,8,1024]{2,1,0:T(8,128)(2,1)} %param.6) | copy-start | bytes 12582916
  9.4 1.7 %copy-start.1 = (f32[16,8,128]{2,1,0:T(8,128)S(1)}, f32[16,8,128]{2,1,0:T(8,128)}, u32[]{:S(2)}) copy-start(f32[16,8,128]{2,1,0:T(8,128)} %param.4) | copy-start | bytes 196612
  10.4 2.1 %collective-permute-start.4 = (bf16[3,128,128]{2,1,0:T(8,128)(2,1)S(1)}, bf16[3,128,128]{2,1,0:T(8,128)(2,1)S(1)}, u32[]{:S(2)}, u32[]{:S(2)}) collective-permute-start(bf16[3,128,128]{2,1,0:T(8,128)(2,1)S(1)} %join.2.bundle_ref.refs_0_), channel_id=1, source_target_pairs={{0,1},{1,0},{2,3},{3,2},{4,5},{5,4},{6,7},{7,6},{8,9},{9,8},{10,11... | collective-permute-start | bytes 294920 | tf_op jit(solution)/shard_map/ppermute | solution.py:40
  11.5 8.7 %copy-start.3 = (f32[256]{0:T(256)S(1)}, f32[256]{0:T(256)}, u32[]{:S(2)}) copy-start(f32[256]{0:T(256)} %param.7) | copy-start | bytes 3076
  13.4 6.8 %collective-permute-start.6 = (bf16[192,128]{1,0:T(8,128)(2,1)S(1)}, bf16[192,128]{1,0:T(8,128)(2,1)S(1)}, u32[]{:S(2)}, u32[]{:S(2)}) collective-permute-start(bf16[192,128]{1,0:T(8,128)(2,1)S(1)} %get-tuple-element.32), channel_id=1, source_target_pairs={{0,24},{8,16},{16,8},{24,0},{1,25},{9,17},{17,9},{25,1},{2,26},{10... | collective-permute-start | bytes 147464 | tf_op jit(solution)/shard_map/ppermute | solution.py:40
  15.9 4.3 %collective-permute-start.5 = (bf16[192,128]{1,0:T(8,128)(2,1)S(1)}, bf16[192,128]{1,0:T(8,128)(2,1)S(1)}, u32[]{:S(2)}, u32[]{:S(2)}) collective-permute-start(bf16[192,128]{1,0:T(8,128)(2,1)S(1)} %get-tuple-element.32), channel_id=1, source_target_pairs={{0,8},{8,0},{16,24},{24,16},{1,9},{9,1},{17,25},{25,17},{2,10},{10... | collective-permute-start | bytes 147464 | tf_op jit(solution)/shard_map/ppermute | solution.py:40
  16.4 3.7 %collective-permute-start.7 = (bf16[64,128]{1,0:T(8,128)(2,1)S(1)}, bf16[64,128]{1,0:T(8,128)(2,1)S(1)}, u32[]{:S(2)}, u32[]{:S(2)}) collective-permute-start(bf16[64,128]{1,0:T(8,128)(2,1)S(1)} %get-tuple-element.33.refs_0_), channel_id=1, source_target_pairs={{0,16},{8,24},{16,0},{24,8},{1,17},{9,25},{17,1},{25,9},{2,18},{10... | collective-permute-start | bytes 49160 | tf_op jit(solution)/shard_map/ppermute | solution.py:40
  20.9 1.4 %collective-permute-start.8 = (bf16[2,128,128]{2,1,0:T(8,128)(2,1)S(1)}, bf16[2,128,128]{2,1,0:T(8,128)(2,1)S(1)}, u32[]{:S(2)}, u32[]{:S(2)}) collective-permute-start(bf16[2,128,128]{2,1,0:T(8,128)(2,1)S(1)} %get-tuple-element.36), channel_id=1, source_target_pairs={{0,1},{1,0},{2,3},{3,2},{4,5},{5,4},{6,7},{7,6},{8,9},{9,8},{10,11... | collective-permute-start | bytes 196616 | tf_op jit(solution)/shard_map/ppermute | solution.py:40
  21.0 5.2 %copy-start.2 = (f32[8,128]{1,0:T(8,128)S(1)}, f32[8,128]{1,0:T(8,128)}, u32[]{:S(2)}) copy-start(f32[8,128]{1,0:T(8,128)} %amp_ref.3) | copy-start | bytes 12292
  21.8 4.2 %collective-permute-start.9 = (bf16[2,128,128]{2,1,0:T(8,128)(2,1)S(1)}, bf16[2,128,128]{2,1,0:T(8,128)(2,1)S(1)}, u32[]{:S(2)}, u32[]{:S(2)}) collective-permute-start(bf16[2,128,128]{2,1,0:T(8,128)(2,1)S(1)} %get-tuple-element.39), channel_id=1, source_target_pairs={{0,1},{1,0},{2,3},{3,2},{4,5},{5,4},{6,7},{7,6},{8,9},{9,8},{10,11... | collective-permute-start | bytes 196616 | tf_op jit(solution)/shard_map/ppermute | solution.py:40
  22.4 4.4 %collective-permute-start.10 = (bf16[1,128,128]{2,1,0:T(8,128)(2,1)S(1)}, bf16[1,128,128]{2,1,0:T(8,128)(2,1)S(1)}, u32[]{:S(2)}, u32[]{:S(2)}) collective-permute-start(bf16[1,128,128]{2,1,0:T(8,128)(2,1)S(1)} %get-tuple-element.37.refs_0_), channel_id=1, source_target_pairs={{0,5},{1,4},{2,7},{3,6},{4,1},{5,0},{6,3},{7,2},{8,13},{9,12},{10,... | collective-permute-start | bytes 98312 | tf_op jit(solution)/shard_map/ppermute | solution.py:40
  24.1 5.1 %collective-permute-start.11 = (bf16[1,128,128]{2,1,0:T(8,128)(2,1)S(1)}, bf16[1,128,128]{2,1,0:T(8,128)(2,1)S(1)}, u32[]{:S(2)}, u32[]{:S(2)}) collective-permute-start(bf16[1,128,128]{2,1,0:T(8,128)(2,1)S(1)} %get-tuple-element.38.refs_1_), channel_id=1, source_target_pairs={{0,7},{1,6},{2,5},{3,4},{4,3},{5,2},{6,1},{7,0},{8,15},{9,14},{10,... | collective-permute-start | bytes 98312 | tf_op jit(solution)/shard_map/ppermute | solution.py:40
  26.1 4.1 %collective-permute-start.12 = (bf16[1,128,128]{2,1,0:T(8,128)(2,1)S(1)}, bf16[1,128,128]{2,1,0:T(8,128)(2,1)S(1)}, u32[]{:S(2)}, u32[]{:S(2)}) collective-permute-start(bf16[1,128,128]{2,1,0:T(8,128)(2,1)S(1)} %get-tuple-element.41), channel_id=1, source_target_pairs={{0,3},{1,2},{2,1},{3,0},{4,7},{5,6},{6,5},{7,4},{8,11},{9,10},{10,... | collective-permute-start | bytes 98312 | tf_op jit(solution)/shard_map/ppermute | solution.py:40
  30.2 4.4 %collective-permute-start.16 = (bf16[1,128,128]{2,1,0:T(8,128)(2,1)S(1)}, bf16[1,128,128]{2,1,0:T(8,128)(2,1)S(1)}, u32[]{:S(2)}, u32[]{:S(2)}) collective-permute-start(bf16[1,128,128]{2,1,0:T(8,128)(2,1)S(1)} %get-tuple-element.43.refs_2_), channel_id=1, source_target_pairs={{0,5},{1,4},{2,7},{3,6},{4,1},{5,0},{6,3},{7,2},{8,13},{9,12},{10,... | collective-permute-start | bytes 98312 | tf_op jit(solution)/shard_map/ppermute | solution.py:40
  30.6 5.2 %collective-permute-start.15 = (bf16[1,128,128]{2,1,0:T(8,128)(2,1)S(1)}, bf16[1,128,128]{2,1,0:T(8,128)(2,1)S(1)}, u32[]{:S(2)}, u32[]{:S(2)}) collective-permute-start(bf16[1,128,128]{2,1,0:T(8,128)(2,1)S(1)} %get-tuple-element.43.refs_2_), channel_id=1, source_target_pairs={{0,7},{1,6},{2,5},{3,4},{4,3},{5,2},{6,1},{7,0},{8,15},{9,14},{10,... | collective-permute-start | bytes 98312 | tf_op jit(solution)/shard_map/ppermute | solution.py:40
  32.1 3.7 %collective-permute-start.14 = (bf16[1,128,128]{2,1,0:T(8,128)(2,1)S(1)}, bf16[1,128,128]{2,1,0:T(8,128)(2,1)S(1)}, u32[]{:S(2)}, u32[]{:S(2)}) collective-permute-start(bf16[1,128,128]{2,1,0:T(8,128)(2,1)S(1)} %get-tuple-element.43.refs_2_), channel_id=1, source_target_pairs={{0,3},{1,2},{2,1},{3,0},{4,7},{5,6},{6,5},{7,4},{8,11},{9,10},{10,... | collective-permute-start | bytes 98312 | tf_op jit(solution)/shard_map/ppermute | solution.py:40
  33.2 2.6 %collective-permute-start.13 = (bf16[1,128,128]{2,1,0:T(8,128)(2,1)S(1)}, bf16[1,128,128]{2,1,0:T(8,128)(2,1)S(1)}, u32[]{:S(2)}, u32[]{:S(2)}) collective-permute-start(bf16[1,128,128]{2,1,0:T(8,128)(2,1)S(1)} %get-tuple-element.43.refs_2_), channel_id=1, source_target_pairs={{0,1},{1,0},{2,3},{3,2},{4,5},{5,4},{6,7},{7,6},{8,9},{9,8},{10,11... | collective-permute-start | bytes 98312 | tf_op jit(solution)/shard_map/ppermute | solution.py:40
  35.8 2.0 %collective-permute-start.17 = (bf16[3,128,128]{2,1,0:T(8,128)(2,1)S(1)}, bf16[3,128,128]{2,1,0:T(8,128)(2,1)S(1)}, u32[]{:S(2)}, u32[]{:S(2)}) collective-permute-start(bf16[3,128,128]{2,1,0:T(8,128)(2,1)S(1)} %join.3.bundle_ref.refs_0_), channel_id=1, source_target_pairs={{0,1},{1,0},{2,3},{3,2},{4,5},{5,4},{6,7},{7,6},{8,9},{9,8},{10,11... | collective-permute-start | bytes 294920 | tf_op jit(solution)/shard_map/ppermute | solution.py:40
  38.7 5.7 %collective-permute-start.19 = (bf16[192,128]{1,0:T(8,128)(2,1)S(1)}, bf16[192,128]{1,0:T(8,128)(2,1)S(1)}, u32[]{:S(2)}, u32[]{:S(2)}) collective-permute-start(bf16[192,128]{1,0:T(8,128)(2,1)S(1)} %get-tuple-element.46), channel_id=1, source_target_pairs={{0,24},{8,16},{16,8},{24,0},{1,25},{9,17},{17,9},{25,1},{2,26},{10... | collective-permute-start | bytes 147464 | tf_op jit(solution)/shard_map/ppermute | solution.py:40
  40.1 4.3 %collective-permute-start.18 = (bf16[192,128]{1,0:T(8,128)(2,1)S(1)}, bf16[192,128]{1,0:T(8,128)(2,1)S(1)}, u32[]{:S(2)}, u32[]{:S(2)}) collective-permute-start(bf16[192,128]{1,0:T(8,128)(2,1)S(1)} %get-tuple-element.46), channel_id=1, source_target_pairs={{0,8},{8,0},{16,24},{24,16},{1,9},{9,1},{17,25},{25,17},{2,10},{10... | collective-permute-start | bytes 147464 | tf_op jit(solution)/shard_map/ppermute | solution.py:40
  40.7 3.7 %collective-permute-start.20 = (bf16[64,128]{1,0:T(8,128)(2,1)S(1)}, bf16[64,128]{1,0:T(8,128)(2,1)S(1)}, u32[]{:S(2)}, u32[]{:S(2)}) collective-permute-start(bf16[64,128]{1,0:T(8,128)(2,1)S(1)} %get-tuple-element.47.refs_0_), channel_id=1, source_target_pairs={{0,16},{8,24},{16,0},{24,8},{1,17},{9,25},{17,1},{25,9},{2,18},{10... | collective-permute-start | bytes 49160 | tf_op jit(solution)/shard_map/ppermute | solution.py:40
  45.1 1.4 %collective-permute-start.21 = (bf16[2,128,128]{2,1,0:T(8,128)(2,1)S(1)}, bf16[2,128,128]{2,1,0:T(8,128)(2,1)S(1)}, u32[]{:S(2)}, u32[]{:S(2)}) collective-permute-start(bf16[2,128,128]{2,1,0:T(8,128)(2,1)S(1)} %get-tuple-element.50), channel_id=1, source_target_pairs={{0,1},{1,0},{2,3},{3,2},{4,5},{5,4},{6,7},{7,6},{8,9},{9,8},{10,11... | collective-permute-start | bytes 196616 | tf_op jit(solution)/shard_map/ppermute | solution.py:40
  46.0 3.2 %collective-permute-start.22 = (bf16[2,128,128]{2,1,0:T(8,128)(2,1)S(1)}, bf16[2,128,128]{2,1,0:T(8,128)(2,1)S(1)}, u32[]{:S(2)}, u32[]{:S(2)}) collective-permute-start(bf16[2,128,128]{2,1,0:T(8,128)(2,1)S(1)} %get-tuple-element.53), channel_id=1, source_target_pairs={{0,1},{1,0},{2,3},{3,2},{4,5},{5,4},{6,7},{7,6},{8,9},{9,8},{10,11... | collective-permute-start | bytes 196616 | tf_op jit(solution)/shard_map/ppermute | solution.py:40
  46.6 5.3 %collective-permute-start.23 = (bf16[1,128,128]{2,1,0:T(8,128)(2,1)S(1)}, bf16[1,128,128]{2,1,0:T(8,128)(2,1)S(1)}, u32[]{:S(2)}, u32[]{:S(2)}) collective-permute-start(bf16[1,128,128]{2,1,0:T(8,128)(2,1)S(1)} %get-tuple-element.51.refs_0_), channel_id=1, source_target_pairs={{0,7},{1,6},{2,5},{3,4},{4,3},{5,2},{6,1},{7,0},{8,15},{9,14},{10,... | collective-permute-start | bytes 98312 | tf_op jit(solution)/shard_map/ppermute | solution.py:40
  48.7 4.6 %collective-permute-start.24 = (bf16[1,128,128]{2,1,0:T(8,128)(2,1)S(1)}, bf16[1,128,128]{2,1,0:T(8,128)(2,1)S(1)}, u32[]{:S(2)}, u32[]{:S(2)}) collective-permute-start(bf16[1,128,128]{2,1,0:T(8,128)(2,1)S(1)} %get-tuple-element.52.refs_1_), channel_id=1, source_target_pairs={{0,5},{1,4},{2,7},{3,6},{4,1},{5,0},{6,3},{7,2},{8,13},{9,12},{10,... | collective-permute-start | bytes 98312 | tf_op jit(solution)/shard_map/ppermute | solution.py:40
  49.2 4.0 %collective-permute-start.25 = (bf16[1,128,128]{2,1,0:T(8,128)(2,1)S(1)}, bf16[1,128,128]{2,1,0:T(8,128)(2,1)S(1)}, u32[]{:S(2)}, u32[]{:S(2)}) collective-permute-start(bf16[1,128,128]{2,1,0:T(8,128)(2,1)S(1)} %get-tuple-element.55), channel_id=1, source_target_pairs={{0,3},{1,2},{2,1},{3,0},{4,7},{5,6},{6,5},{7,4},{8,11},{9,10},{10,... | collective-permute-start | bytes 98312 | tf_op jit(solution)/shard_map/ppermute | solution.py:40

commit v10 on v9

--- a/solution.py
+++ b/solution.py
@@ -322,16 +322,17 @@
         order.sort(key=lambda mask: (mask == half, mask))
         parts = [cross(short, mask) for mask in order]
         twin = swap(short, "tile", 1)
+        diag = first([twin, short], [(0, True), (0, False)])
         bundle = call(
             join_kernel,
             shape(bf16, near - 1, lines, width),
             in_specs=[pl.BlockSpec(memory_space=pl.ANY)] * 2
             + [pl.BlockSpec(memory_space=pltpu.VMEM)] * (near - 1),
             name="join",
-        )(held, twin, *parts)
+        )(diag, twin, *parts)
         across = swap(bundle, "tile", 1)
         known = spots_of(order, False) + [(0, True)]
-        diag = first([bundle, twin, short], known + [(0, False)])
+        diag = first([bundle], spots_of(order, False), diag)
         spots = spots_of(order, True)
         along, along_short = call(
             partial(columns_kernel, halve, known),

time: 54.2 us -> 54 us (level)
  starting transfers between devices: 25.4 us -> 24.7 us
    ppermute x26, starting transfers between devices: 25.4 us -> 24.7 us  [swap(): lax.ppermute(value, axis, [(i, i ^ mask) for i in range(lax.axis_size(axi...]
    pallas_call x2 -> x4, Pallas kernels: 2.06 us -> 2.57 us  [first(): call(partial(first_kernel, rows, spots, len(before)), shape(f32, blocks *...]
  transfers between devices with their start and end apart: 26 -> 26, of which waited for: 11 -> 10; matrix products, arithmetic and copies ran while one was open for 0% -> 0% of each run, Pallas kernels for 11% -> 12%
where the time goes in v10:
time: 54 us; the launch traced here: 53.8 us
  starting transfers between devices  24.7 us (46%)
  waiting for transfers between devices  14.5 us (27%)
  Pallas kernels  10.6 us (20%)
  local copies, waits for them, and re-layouts  2.21 us (4%)
  between operations  0.89 us (2%)
  other arithmetic  0.85 us (2%)
    ppermute x26, starting transfers between devices, swap(): lax.ppermute(value, axis, [(i, i ^ mask) for i in range(lax.axis_size(axi...  24.7 us
    ppermute x26, waiting for transfers between devices, swap(): lax.ppermute(value, axis, [(i, i ^ mask) for i in range(lax.axis_size(axi...  14.5 us
    pallas_call x4, Pallas kernels, term(): call(partial(term_kernel, wanted, len(after)), in_specs=[pl.BlockSpec(mem...  2.59 us
    pallas_call x4, Pallas kernels, first(): call(partial(first_kernel, rows, spots, len(before)), shape(f32, blocks *...  2.57 us
    unnamed x8, local copies, waits for them, and re-layouts  2.21 us
    pallas_call x2, Pallas kernels, on_device(): call(partial(second_kernel, rows, cols, spots), (shape(bf16, pay_rows, wi...  1.74 us
    pallas_call x2, Pallas kernels, on_device(): call(partial(far_kernel, rows, cols, groups, ncells_all, spots_of(away, T...  1.45 us
  transfers between devices with their start and end apart: 26, of which 10 were waited for; matrix products, arithmetic and copies ran while one was open for 0% of the time, Pallas kernels for 12%

profile of v10, /device:TPU:0, one launch (start us, length us, event | category | flops | bytes accessed | tf_op | source)
XLA Modules:
  0.0 53.8 jit_solution(16043944067766552558)
XLA Ops:
  0.6 0.8 %fusion.refs_1_ = bf16[1,128,128]{2,1,0:T(8,128)(2,1)S(1)} fusion(f32[16,8,128]{2,1,0:T(8,128)} %param.4), kind=kLoop, calls=%fused_computation.1 | loop fusion | flops 32768 | bytes 98304 | tf_op jit(solution)/shard_map/convert_element_type | solution.py:272
  1.5 0.5 collective-permute-start
  1.9 3.7 %collective-permute-start.3 = (bf16[1,128,128]{2,1,0:T(8,128)(2,1)S(1)}, bf16[1,128,128]{2,1,0:T(8,128)(2,1)S(1)}, u32[]{:S(2)}, u32[]{:S(2)}) collective-permute-start(bf16[1,128,128]{2,1,0:T(8,128)(2,1)S(1)} %fusion.refs_1_), channel_id=1, source_target_pairs={{0,5},{1,4},{2,7},{3,6},{4,1},{5,0},{6,3},{7,2},{8,13},{9,12},{10,... | collective-permute-start | bytes 98312 | tf_op jit(solution)/shard_map/ppermute | solution.py:40
  5.6 1.0 %collective-permute-start.2 = (bf16[1,128,128]{2,1,0:T(8,128)(2,1)S(1)}, bf16[1,128,128]{2,1,0:T(8,128)(2,1)S(1)}, u32[]{:S(2)}, u32[]{:S(2)}) collective-permute-start(bf16[1,128,128]{2,1,0:T(8,128)(2,1)S(1)} %fusion.refs_1_), channel_id=1, source_target_pairs={{0,7},{1,6},{2,5},{3,4},{4,3},{5,2},{6,1},{7,0},{8,15},{9,14},{10,... | collective-permute-start | bytes 98312 | tf_op jit(solution)/shard_map/ppermute | solution.py:40
  6.7 0.2 collective-permute-start.1
  6.9 2.2 %copy-done = bf16[256,8,1024]{2,1,0:T(8,128)(2,1)S(1)} copy-done((bf16[256,8,1024]{2,1,0:T(8,128)(2,1)S(1)}, bf16[256,8,1024]{2,1,0:T(8,128)(2,1)}, u32[]{:S(2)}) %copy-start) | copy-done | bytes 4194328
  9.1 0.4 load.1.factor_ref
  9.4 0.0 copy-start.1
  9.5 0.0 collective-permute-done.refs_0_.refs_1_.twin_ref
  9.5 0.5 %project_own.4.refs_0_.refs_1_ = f32[256,128]{1,0:T(8,128)S(1)} custom-call(bf16[2048,1024]{1,0:T(8,128)(2,1)S(1)} %load.1.factor_ref, bf16[1,128,128]{2,1,0:T(8,128)(2,1)S(1)} %collective-permute-done.refs_0_.refs_1_.twin_ref, bf16[1,128,128]{2,1,0:T(8,128)(2,1)S(1)} %fusion.refs_1_), custom_call_target="tpu_custom_call" | custom-call | flops 268435456 | bytes 2097152 | tf_op jit(solution)/shard_map/project_own/pallas_call | solution.py:309
  10.0 0.9 %collective-permute-done.2.refs_3_ = bf16[1,128,128]{2,1,0:T(8,128)(2,1)S(1)} collective-permute-done((bf16[1,128,128]{2,1,0:T(8,128)(2,1)S(1)}, bf16[1,128,128]{2,1,0:T(8,128)(2,1)S(1)}, u32[]{:S(2)}, u32[]{:S(2)}) %collective-permute-start.2) | collective-permute-done | bytes 32800 | tf_op jit(solution)/shard_map/ppermute | solution.py:40
  11.0 0.0 collective-permute-done.1.refs_2_
  11.0 0.3 collective-permute-start.4
  11.3 0.4 columns.2
  11.6 0.0 copy-start.3
  11.7 0.7 %project_own.5.diag_ref = f32[256,128]{1,0:T(8,128)S(1)} custom-call(bf16[2048,1024]{1,0:T(8,128)(2,1)S(1)} %load.1.factor_ref, bf16[3,128,128]{2,1,0:T(8,128)(2,1)S(1)} %join.2.bundle_ref.refs_0_, f32[256,128]{1,0:T(8,128)S(1)} %project_own.4.refs_0_.refs_1_), custom_call_target="tpu_custom_call" | custom-call | flops 268435456 | bytes 2097152 | tf_op jit(solution)/shard_map/project_own/pallas_call | solution.py:309
  12.4 0.0 collective-permute-done.4.fields_ref
  12.4 0.9 %project_across.2 = (bf16[192,128]{1,0:T(8,128)(2,1)S(1)}, bf16[64,128]{1,0:T(8,128)(2,1)S(1)}) custom-call(bf16[2048,1024]{1,0:T(8,128)(2,1)S(1)} %load.1.factor_ref, f32[256,128]{1,0:T(8,128)S(1)} %project_own.5.diag_ref, bf16[3,128,128]{2,1,0:T(8,128)(2,1)S(1)} %collective-permute-done.4.fields_ref, bf16[128,128]{1,0:T(8,128)(2,1)S(1)} %get-tuple-element.31.short_ref), custom_call_target="tpu_custom_call" | custom-call | flops 268435456 | bytes 2097152 | tf_op jit(solution)/shard_map/project_across/pallas_call | solution.py:342
  13.3 2.5 %collective-permute-start.6 = (bf16[192,128]{1,0:T(8,128)(2,1)S(1)}, bf16[192,128]{1,0:T(8,128)(2,1)S(1)}, u32[]{:S(2)}, u32[]{:S(2)}) collective-permute-start(bf16[192,128]{1,0:T(8,128)(2,1)S(1)} %get-tuple-element.32), channel_id=1, source_target_pairs={{0,24},{8,16},{16,8},{24,0},{1,25},{9,17},{17,9},{25,1},{2,26},{10... | collective-permute-start | bytes 147464 | tf_op jit(solution)/shard_map/ppermute | solution.py:40
  15.8 0.6 %collective-permute-start.5 = (bf16[192,128]{1,0:T(8,128)(2,1)S(1)}, bf16[192,128]{1,0:T(8,128)(2,1)S(1)}, u32[]{:S(2)}, u32[]{:S(2)}) collective-permute-start(bf16[192,128]{1,0:T(8,128)(2,1)S(1)} %get-tuple-element.32), channel_id=1, source_target_pairs={{0,8},{8,0},{16,24},{24,16},{1,9},{9,1},{17,25},{25,17},{2,10},{10... | collective-permute-start | bytes 147464 | tf_op jit(solution)/shard_map/ppermute | solution.py:40
  16.3 0.5 collective-permute-start.7
  16.8 3.2 %collective-permute-done.7.refs_2_ = bf16[64,128]{1,0:T(8,128)(2,1)S(1)} collective-permute-done((bf16[64,128]{1,0:T(8,128)(2,1)S(1)}, bf16[64,128]{1,0:T(8,128)(2,1)S(1)}, u32[]{:S(2)}, u32[]{:S(2)}) %collective-permute-start.7) | collective-permute-done | bytes 16416 | tf_op jit(solution)/shard_map/ppermute | solution.py:40
  20.1 0.0 collective-permute-done.6.refs_1_.refs_3_
  20.1 0.0 collective-permute-done.5.refs_0_.refs_1_
  20.1 0.7 %term_first.2 = (bf16[128,2048]{1,0:T(8,128)(2,1)S(1)}, bf16[2,128,128]{2,1,0:T(8,128)(2,1)S(1)}) custom-call(f32[1,256]{1,0:T(1,128)S(1)} %bitcast.13, bf16[2048,1024]{1,0:T(8,128)(2,1)S(1)} %load.1.factor_ref, bf16[64,128]{1,0:T(8,128)(2,1)S(1)} %get-tuple-element.33.refs_0_, bf16[192,128]{1,0:T(8,128)(2,1)S(1)} %collective-permute-done.5.refs_0_.refs_1_, ...), custom_call_target="tpu_custom_call" | custom-call | flops 134217728 | bytes 2097152 | tf_op jit(solution)/shard_map/term_first/pallas_call | solution.py:351
  20.8 0.1 collective-permute-start.8
  20.9 0.0 copy-start.2
  20.9 0.8 %term.4 = (f32[2,128,128]{2,1,0:T(8,128)S(1)}, bf16[2,128,128]{2,1,0:T(8,128)(2,1)S(1)}) custom-call(bf16[128,2048]{1,0:T(8,128)(2,1)S(1)} %get-tuple-element.34.coef_ref, bf16[2048,1024]{1,0:T(8,128)(2,1)S(1)} %load.1.factor_ref), custom_call_target="tpu_custom_call" | custom-call | flops 268435456 | bytes 2097152 | tf_op jit(solution)/shard_map/term/pallas_call | solution.py:361
  21.7 0.5 %collective-permute-start.9 = (bf16[2,128,128]{2,1,0:T(8,128)(2,1)S(1)}, bf16[2,128,128]{2,1,0:T(8,128)(2,1)S(1)}, u32[]{:S(2)}, u32[]{:S(2)}) collective-permute-start(bf16[2,128,128]{2,1,0:T(8,128)(2,1)S(1)} %get-tuple-element.39), channel_id=1, source_target_pairs={{0,1},{1,0},{2,3},{3,2},{4,5},{5,4},{6,7},{7,6},{8,9},{9,8},{10,11... | collective-permute-start | bytes 196616 | tf_op jit(solution)/shard_map/ppermute | solution.py:40
  22.3 1.6 %collective-permute-start.10 = (bf16[1,128,128]{2,1,0:T(8,128)(2,1)S(1)}, bf16[1,128,128]{2,1,0:T(8,128)(2,1)S(1)}, u32[]{:S(2)}, u32[]{:S(2)}) collective-permute-start(bf16[1,128,128]{2,1,0:T(8,128)(2,1)S(1)} %get-tuple-element.37.refs_0_), channel_id=1, source_target_pairs={{0,5},{1,4},{2,7},{3,6},{4,1},{5,0},{6,3},{7,2},{8,13},{9,12},{10,... | collective-permute-start | bytes 98312 | tf_op jit(solution)/shard_map/ppermute | solution.py:40
  23.9 1.4 %collective-permute-start.11 = (bf16[1,128,128]{2,1,0:T(8,128)(2,1)S(1)}, bf16[1,128,128]{2,1,0:T(8,128)(2,1)S(1)}, u32[]{:S(2)}, u32[]{:S(2)}) collective-permute-start(bf16[1,128,128]{2,1,0:T(8,128)(2,1)S(1)} %get-tuple-element.38.refs_1_), channel_id=1, source_target_pairs={{0,7},{1,6},{2,5},{3,4},{4,3},{5,2},{6,1},{7,0},{8,15},{9,14},{10,... | collective-permute-start | bytes 98312 | tf_op jit(solution)/shard_map/ppermute | solution.py:40
  25.3 0.5 term.5.mine_ref
  25.8 0.0 collective-permute-done.9.got_ref
  25.8 0.1 collective-permute-start.12
  25.9 0.2 local.2.base_ref
  26.1 1.3 %collective-permute-done.10.refs_1_ = bf16[1,128,128]{2,1,0:T(8,128)(2,1)S(1)} collective-permute-done((bf16[1,128,128]{2,1,0:T(8,128)(2,1)S(1)}, bf16[1,128,128]{2,1,0:T(8,128)(2,1)S(1)}, u32[]{:S(2)}, u32[]{:S(2)}) %collective-permute-start.10) | collective-permute-done | bytes 32800 | tf_op jit(solution)/shard_map/ppermute | solution.py:40
  27.4 1.6 %collective-permute-done.11.refs_2_ = bf16[1,128,128]{2,1,0:T(8,128)(2,1)S(1)} collective-permute-done((bf16[1,128,128]{2,1,0:T(8,128)(2,1)S(1)}, bf16[1,128,128]{2,1,0:T(8,128)(2,1)S(1)}, u32[]{:S(2)}, u32[]{:S(2)}) %collective-permute-start.11) | collective-permute-done | bytes 32800 | tf_op jit(solution)/shard_map/ppermute | solution.py:40
  29.0 0.9 %collective-permute-done.12.refs_3_ = bf16[1,128,128]{2,1,0:T(8,128)(2,1)S(1)} collective-permute-done((bf16[1,128,128]{2,1,0:T(8,128)(2,1)S(1)}, bf16[1,128,128]{2,1,0:T(8,128)(2,1)S(1)}, u32[]{:S(2)}, u32[]{:S(2)}) %collective-permute-start.12) | collective-permute-done | bytes 32800 | tf_op jit(solution)/shard_map/ppermute | solution.py:40
  30.0 0.2 collective-permute-start.13
  30.2 0.5 collective-permute-start.16
  30.7 1.4 %collective-permute-start.15 = (bf16[1,128,128]{2,1,0:T(8,128)(2,1)S(1)}, bf16[1,128,128]{2,1,0:T(8,128)(2,1)S(1)}, u32[]{:S(2)}, u32[]{:S(2)}) collective-permute-start(bf16[1,128,128]{2,1,0:T(8,128)(2,1)S(1)} %get-tuple-element.43.refs_1_), channel_id=1, source_target_pairs={{0,7},{1,6},{2,5},{3,4},{4,3},{5,2},{6,1},{7,0},{8,15},{9,14},{10,... | collective-permute-start | bytes 98312 | tf_op jit(solution)/shard_map/ppermute | solution.py:40
  32.0 1.3 %collective-permute-start.14 = (bf16[1,128,128]{2,1,0:T(8,128)(2,1)S(1)}, bf16[1,128,128]{2,1,0:T(8,128)(2,1)S(1)}, u32[]{:S(2)}, u32[]{:S(2)}) collective-permute-start(bf16[1,128,128]{2,1,0:T(8,128)(2,1)S(1)} %get-tuple-element.43.refs_1_), channel_id=1, source_target_pairs={{0,3},{1,2},{2,1},{3,0},{4,7},{5,6},{6,5},{7,4},{8,11},{9,10},{10,... | collective-permute-start | bytes 98312 | tf_op jit(solution)/shard_map/ppermute | solution.py:40
  33.4 0.5 %project_own.6.refs_0_.refs_1_ = f32[256,128]{1,0:T(8,128)S(1)} custom-call(bf16[2048,1024]{1,0:T(8,128)(2,1)S(1)} %load.1.factor_ref, bf16[1,128,128]{2,1,0:T(8,128)(2,1)S(1)} %collective-permute-done.13.refs_0_.refs_1_.twin_ref, bf16[1,128,128]{2,1,0:T(8,128)(2,1)S(1)} %get-tuple-element.43.refs_1_), custom_call_target="tpu_custom_call" | custom-call | flops 268435456 | bytes 2097152 | tf_op jit(solution)/shard_map/project_own/pallas_call | solution.py:309
  33.9 0.5 collective-permute-done.16.refs_4_
  34.5 1.6 %collective-permute-done.15.refs_3_ = bf16[1,128,128]{2,1,0:T(8,128)(2,1)S(1)} collective-permute-done((bf16[1,128,128]{2,1,0:T(8,128)(2,1)S(1)}, bf16[1,128,128]{2,1,0:T(8,128)(2,1)S(1)}, u32[]{:S(2)}, u32[]{:S(2)}) %collective-permute-start.15) | collective-permute-done | bytes 32800 | tf_op jit(solution)/shard_map/ppermute | solution.py:40
  36.0 0.4 collective-permute-start.17
  36.4 0.3 columns.3
  36.8 0.7 %project_own.7.diag_ref = f32[256,128]{1,0:T(8,128)S(1)} custom-call(bf16[2048,1024]{1,0:T(8,128)(2,1)S(1)} %load.1.factor_ref, bf16[3,128,128]{2,1,0:T(8,128)(2,1)S(1)} %join.3.bundle_ref.refs_0_, f32[256,128]{1,0:T(8,128)S(1)} %project_own.6.refs_0_.refs_1_), custom_call_target="tpu_custom_call" | custom-call | flops 268435456 | bytes 2097152 | tf_op jit(solution)/shard_map/project_own/pallas_call | solution.py:309
  37.5 0.9 %project_across.3 = (bf16[192,128]{1,0:T(8,128)(2,1)S(1)}, bf16[64,128]{1,0:T(8,128)(2,1)S(1)}) custom-call(bf16[2048,1024]{1,0:T(8,128)(2,1)S(1)} %load.1.factor_ref, f32[256,128]{1,0:T(8,128)S(1)} %project_own.7.diag_ref, bf16[3,128,128]{2,1,0:T(8,128)(2,1)S(1)} %collective-permute-done.17.fields_ref, bf16[128,128]{1,0:T(8,128)(2,1)S(1)} %get-tuple-element.45.short_ref), custom_call_target="tpu_custom_call" | custom-call | flops 268435456 | bytes 2097152 | tf_op jit(solution)/shard_map/project_across/pallas_call | solution.py:342
  38.4 1.5 %collective-permute-start.19 = (bf16[192,128]{1,0:T(8,128)(2,1)S(1)}, bf16[192,128]{1,0:T(8,128)(2,1)S(1)}, u32[]{:S(2)}, u32[]{:S(2)}) collective-permute-start(bf16[192,128]{1,0:T(8,128)(2,1)S(1)} %get-tuple-element.46), channel_id=1, source_target_pairs={{0,24},{8,16},{16,8},{24,0},{1,25},{9,17},{17,9},{25,1},{2,26},{10... | collective-permute-start | bytes 147464 | tf_op jit(solution)/shard_map/ppermute | solution.py:40
  39.9 0.5 collective-permute-start.18
  40.4 1.5 %collective-permute-start.20 = (bf16[64,128]{1,0:T(8,128)(2,1)S(1)}, bf16[64,128]{1,0:T(8,128)(2,1)S(1)}, u32[]{:S(2)}, u32[]{:S(2)}) collective-permute-start(bf16[64,128]{1,0:T(8,128)(2,1)S(1)} %get-tuple-element.47.refs_0_), channel_id=1, source_target_pairs={{0,16},{8,24},{16,0},{24,8},{1,17},{9,25},{17,1},{25,9},{2,18},{10... | collective-permute-start | bytes 49160 | tf_op jit(solution)/shard_map/ppermute | solution.py:40
  41.9 2.2 %collective-permute-done.20.refs_2_ = bf16[64,128]{1,0:T(8,128)(2,1)S(1)} collective-permute-done((bf16[64,128]{1,0:T(8,128)(2,1)S(1)}, bf16[64,128]{1,0:T(8,128)(2,1)S(1)}, u32[]{:S(2)}, u32[]{:S(2)}) %collective-permute-start.20) | collective-permute-done | bytes 16416 | tf_op jit(solution)/shard_map/ppermute | solution.py:40
  44.2 0.7 %term_first.3 = (bf16[128,2048]{1,0:T(8,128)(2,1)S(1)}, bf16[2,128,128]{2,1,0:T(8,128)(2,1)S(1)}) custom-call(f32[1,256]{1,0:T(1,128)S(1)} %bitcast.14, bf16[2048,1024]{1,0:T(8,128)(2,1)S(1)} %load.1.factor_ref, bf16[64,128]{1,0:T(8,128)(2,1)S(1)} %get-tuple-element.47.refs_0_, bf16[192,128]{1,0:T(8,128)(2,1)S(1)} %collective-permute-done.18.refs_0_.refs_1_, ...), custom_call_target="tpu_custom_call" | custom-call | flops 134217728 | bytes 2097152 | tf_op jit(solution)/shard_map/term_first/pallas_call | solution.py:351
  44.9 0.1 collective-permute-start.21
  45.0 0.8 %term.6 = (f32[2,128,128]{2,1,0:T(8,128)S(1)}, bf16[2,128,128]{2,1,0:T(8,128)(2,1)S(1)}) custom-call(bf16[128,2048]{1,0:T(8,128)(2,1)S(1)} %get-tuple-element.48.coef_ref, bf16[2048,1024]{1,0:T(8,128)(2,1)S(1)} %load.1.factor_ref), custom_call_target="tpu_custom_call" | custom-call | flops 268435456 | bytes 2097152 | tf_op jit(solution)/shard_map/term/pallas_call | solution.py:361
  45.8 0.6 %collective-permute-start.22 = (bf16[2,128,128]{2,1,0:T(8,128)(2,1)S(1)}, bf16[2,128,128]{2,1,0:T(8,128)(2,1)S(1)}, u32[]{:S(2)}, u32[]{:S(2)}) collective-permute-start(bf16[2,128,128]{2,1,0:T(8,128)(2,1)S(1)} %get-tuple-element.53), channel_id=1, source_target_pairs={{0,1},{1,0},{2,3},{3,2},{4,5},{5,4},{6,7},{7,6},{8,9},{9,8},{10,11... | collective-permute-start | bytes 196616 | tf_op jit(solution)/shard_map/ppermute | solution.py:40
  46.4 2.0 %collective-permute-start.23 = (bf16[1,128,128]{2,1,0:T(8,128)(2,1)S(1)}, bf16[1,128,128]{2,1,0:T(8,128)(2,1)S(1)}, u32[]{:S(2)}, u32[]{:S(2)}) collective-permute-start(bf16[1,128,128]{2,1,0:T(8,128)(2,1)S(1)} %get-tuple-element.51.refs_0_), channel_id=1, source_target_pairs={{0,7},{1,6},{2,5},{3,4},{4,3},{5,2},{6,1},{7,0},{8,15},{9,14},{10,... | collective-permute-start | bytes 98312 | tf_op jit(solution)/shard_map/ppermute | solution.py:40
  48.4 0.5 term.7.mine_ref
  48.9 1.9 %collective-permute-start.25 = (bf16[1,128,128]{2,1,0:T(8,128)(2,1)S(1)}, bf16[1,128,128]{2,1,0:T(8,128)(2,1)S(1)}, u32[]{:S(2)}, u32[]{:S(2)}) collective-permute-start(bf16[1,128,128]{2,1,0:T(8,128)(2,1)S(1)} %get-tuple-element.55), channel_id=1, source_target_pairs={{0,3},{1,2},{2,1},{3,0},{4,7},{5,6},{6,5},{7,4},{8,11},{9,10},{10,... | collective-permute-start | bytes 98312 | tf_op jit(solution)/shard_map/ppermute | solution.py:40
  50.8 0.2 local.3.base_ref
  51.0 0.8 %collective-permute-done.23.refs_1_ = bf16[1,128,128]{2,1,0:T(8,128)(2,1)S(1)} collective-permute-done((bf16[1,128,128]{2,1,0:T(8,128)(2,1)S(1)}, bf16[1,128,128]{2,1,0:T(8,128)(2,1)S(1)}, u32[]{:S(2)}, u32[]{:S(2)}) %collective-permute-start.23) | collective-permute-done | bytes 32800 | tf_op jit(solution)/shard_map/ppermute | solution.py:40
  51.7 1.4 %collective-permute-done.24.refs_2_ = bf16[1,128,128]{2,1,0:T(8,128)(2,1)S(1)} collective-permute-done((bf16[1,128,128]{2,1,0:T(8,128)(2,1)S(1)}, bf16[1,128,128]{2,1,0:T(8,128)(2,1)S(1)}, u32[]{:S(2)}, u32[]{:S(2)}) %collective-permute-start.24) | collective-permute-done | bytes 32800 | tf_op jit(solution)/shard_map/ppermute | solution.py:40
  53.1 0.7 %update.3 = (f32[128,128]{1,0:T(8,128)}, f32[128,128]{1,0:T(8,128)}) custom-call(f32[128,128]{1,0:T(8,128)S(1)} %get-tuple-element.42.x_ref, f32[128,128]{1,0:T(8,128)S(1)} %local.3.base_ref, f32[1,128,128]{2,1,0:T(8,128)S(1)} %get-tuple-element.54.refs_0_, bf16[1,128,128]{2,1,0:T(8,128)(2,1)S(1)} %collective-permute-done.23.refs_1_, ...), custom_call_target="tpu_custom_call" | custom-call | bytes 262144 | tf_op jit(solution)/shard_map/update/pallas_call | solution.py:389
  (22 shorter events, 0.1 us)
Async XLA Ops:
  1.5 8.0 %collective-permute-start = (bf16[1,128,128]{2,1,0:T(8,128)(2,1)S(1)}, bf16[1,128,128]{2,1,0:T(8,128)(2,1)S(1)}, u32[]{:S(2)}, u32[]{:S(2)}) collective-permute-start(bf16[1,128,128]{2,1,0:T(8,128)(2,1)S(1)} %fusion.refs_1_), channel_id=1, source_target_pairs={{0,1},{1,0},{2,3},{3,2},{4,5},{5,4},{6,7},{7,6},{8,9},{9,8},{10,11... | collective-permute-start | bytes 98312 | tf_op jit(solution)/shard_map/ppermute | solution.py:40
  1.9 8.1 %collective-permute-start.3 = (bf16[1,128,128]{2,1,0:T(8,128)(2,1)S(1)}, bf16[1,128,128]{2,1,0:T(8,128)(2,1)S(1)}, u32[]{:S(2)}, u32[]{:S(2)}) collective-permute-start(bf16[1,128,128]{2,1,0:T(8,128)(2,1)S(1)} %fusion.refs_1_), channel_id=1, source_target_pairs={{0,5},{1,4},{2,7},{3,6},{4,1},{5,0},{6,3},{7,2},{8,13},{9,12},{10,... | collective-permute-start | bytes 98312 | tf_op jit(solution)/shard_map/ppermute | solution.py:40
  5.6 5.3 %collective-permute-start.2 = (bf16[1,128,128]{2,1,0:T(8,128)(2,1)S(1)}, bf16[1,128,128]{2,1,0:T(8,128)(2,1)S(1)}, u32[]{:S(2)}, u32[]{:S(2)}) collective-permute-start(bf16[1,128,128]{2,1,0:T(8,128)(2,1)S(1)} %fusion.refs_1_), channel_id=1, source_target_pairs={{0,7},{1,6},{2,5},{3,4},{4,3},{5,2},{6,1},{7,0},{8,15},{9,14},{10,... | collective-permute-start | bytes 98312 | tf_op jit(solution)/shard_map/ppermute | solution.py:40
  6.7 4.3 %collective-permute-start.1 = (bf16[1,128,128]{2,1,0:T(8,128)(2,1)S(1)}, bf16[1,128,128]{2,1,0:T(8,128)(2,1)S(1)}, u32[]{:S(2)}, u32[]{:S(2)}) collective-permute-start(bf16[1,128,128]{2,1,0:T(8,128)(2,1)S(1)} %fusion.refs_1_), channel_id=1, source_target_pairs={{0,3},{1,2},{2,1},{3,0},{4,7},{5,6},{6,5},{7,4},{8,11},{9,10},{10,... | collective-permute-start | bytes 98312 | tf_op jit(solution)/shard_map/ppermute | solution.py:40
  6.9 2.2 %copy-start = (bf16[256,8,1024]{2,1,0:T(8,128)(2,1)S(1)}, bf16[256,8,1024]{2,1,0:T(8,128)(2,1)}, u32[]{:S(2)}) copy-start(bf16[256,8,1024]{2,1,0:T(8,128)(2,1)} %param.6) | copy-start | bytes 12582916
  9.4 1.8 %copy-start.1 = (f32[16,8,128]{2,1,0:T(8,128)S(1)}, f32[16,8,128]{2,1,0:T(8,128)}, u32[]{:S(2)}) copy-start(f32[16,8,128]{2,1,0:T(8,128)} %param.4) | copy-start | bytes 196612
  11.0 1.4 %collective-permute-start.4 = (bf16[3,128,128]{2,1,0:T(8,128)(2,1)S(1)}, bf16[3,128,128]{2,1,0:T(8,128)(2,1)S(1)}, u32[]{:S(2)}, u32[]{:S(2)}) collective-permute-start(bf16[3,128,128]{2,1,0:T(8,128)(2,1)S(1)} %join.2.bundle_ref.refs_0_), channel_id=1, source_target_pairs={{0,1},{1,0},{2,3},{3,2},{4,5},{5,4},{6,7},{7,6},{8,9},{9,8},{10,11... | collective-permute-start | bytes 294920 | tf_op jit(solution)/shard_map/ppermute | solution.py:40
  11.6 8.4 %copy-start.3 = (f32[256]{0:T(256)S(1)}, f32[256]{0:T(256)}, u32[]{:S(2)}) copy-start(f32[256]{0:T(256)} %param.7) | copy-start | bytes 3076
  13.3 6.8 %collective-permute-start.6 = (bf16[192,128]{1,0:T(8,128)(2,1)S(1)}, bf16[192,128]{1,0:T(8,128)(2,1)S(1)}, u32[]{:S(2)}, u32[]{:S(2)}) collective-permute-start(bf16[192,128]{1,0:T(8,128)(2,1)S(1)} %get-tuple-element.32), channel_id=1, source_target_pairs={{0,24},{8,16},{16,8},{24,0},{1,25},{9,17},{17,9},{25,1},{2,26},{10... | collective-permute-start | bytes 147464 | tf_op jit(solution)/shard_map/ppermute | solution.py:40
  15.8 4.3 %collective-permute-start.5 = (bf16[192,128]{1,0:T(8,128)(2,1)S(1)}, bf16[192,128]{1,0:T(8,128)(2,1)S(1)}, u32[]{:S(2)}, u32[]{:S(2)}) collective-permute-start(bf16[192,128]{1,0:T(8,128)(2,1)S(1)} %get-tuple-element.32), channel_id=1, source_target_pairs={{0,8},{8,0},{16,24},{24,16},{1,9},{9,1},{17,25},{25,17},{2,10},{10... | collective-permute-start | bytes 147464 | tf_op jit(solution)/shard_map/ppermute | solution.py:40
  16.3 3.7 %collective-permute-start.7 = (bf16[64,128]{1,0:T(8,128)(2,1)S(1)}, bf16[64,128]{1,0:T(8,128)(2,1)S(1)}, u32[]{:S(2)}, u32[]{:S(2)}) collective-permute-start(bf16[64,128]{1,0:T(8,128)(2,1)S(1)} %get-tuple-element.33.refs_0_), channel_id=1, source_target_pairs={{0,16},{8,24},{16,0},{24,8},{1,17},{9,25},{17,1},{25,9},{2,18},{10... | collective-permute-start | bytes 49160 | tf_op jit(solution)/shard_map/ppermute | solution.py:40
  20.8 1.4 %collective-permute-start.8 = (bf16[2,128,128]{2,1,0:T(8,128)(2,1)S(1)}, bf16[2,128,128]{2,1,0:T(8,128)(2,1)S(1)}, u32[]{:S(2)}, u32[]{:S(2)}) collective-permute-start(bf16[2,128,128]{2,1,0:T(8,128)(2,1)S(1)} %get-tuple-element.36), channel_id=1, source_target_pairs={{0,1},{1,0},{2,3},{3,2},{4,5},{5,4},{6,7},{7,6},{8,9},{9,8},{10,11... | collective-permute-start | bytes 196616 | tf_op jit(solution)/shard_map/ppermute | solution.py:40
  20.9 5.0 %copy-start.2 = (f32[8,128]{1,0:T(8,128)S(1)}, f32[8,128]{1,0:T(8,128)}, u32[]{:S(2)}) copy-start(f32[8,128]{1,0:T(8,128)} %amp_ref.3) | copy-start | bytes 12292
  21.7 4.1 %collective-permute-start.9 = (bf16[2,128,128]{2,1,0:T(8,128)(2,1)S(1)}, bf16[2,128,128]{2,1,0:T(8,128)(2,1)S(1)}, u32[]{:S(2)}, u32[]{:S(2)}) collective-permute-start(bf16[2,128,128]{2,1,0:T(8,128)(2,1)S(1)} %get-tuple-element.39), channel_id=1, source_target_pairs={{0,1},{1,0},{2,3},{3,2},{4,5},{5,4},{6,7},{7,6},{8,9},{9,8},{10,11... | collective-permute-start | bytes 196616 | tf_op jit(solution)/shard_map/ppermute | solution.py:40
  22.3 5.1 %collective-permute-start.10 = (bf16[1,128,128]{2,1,0:T(8,128)(2,1)S(1)}, bf16[1,128,128]{2,1,0:T(8,128)(2,1)S(1)}, u32[]{:S(2)}, u32[]{:S(2)}) collective-permute-start(bf16[1,128,128]{2,1,0:T(8,128)(2,1)S(1)} %get-tuple-element.37.refs_0_), channel_id=1, source_target_pairs={{0,5},{1,4},{2,7},{3,6},{4,1},{5,0},{6,3},{7,2},{8,13},{9,12},{10,... | collective-permute-start | bytes 98312 | tf_op jit(solution)/shard_map/ppermute | solution.py:40
  23.9 5.1 %collective-permute-start.11 = (bf16[1,128,128]{2,1,0:T(8,128)(2,1)S(1)}, bf16[1,128,128]{2,1,0:T(8,128)(2,1)S(1)}, u32[]{:S(2)}, u32[]{:S(2)}) collective-permute-start(bf16[1,128,128]{2,1,0:T(8,128)(2,1)S(1)} %get-tuple-element.38.refs_1_), channel_id=1, source_target_pairs={{0,7},{1,6},{2,5},{3,4},{4,3},{5,2},{6,1},{7,0},{8,15},{9,14},{10,... | collective-permute-start | bytes 98312 | tf_op jit(solution)/shard_map/ppermute | solution.py:40
  25.8 4.1 %collective-permute-start.12 = (bf16[1,128,128]{2,1,0:T(8,128)(2,1)S(1)}, bf16[1,128,128]{2,1,0:T(8,128)(2,1)S(1)}, u32[]{:S(2)}, u32[]{:S(2)}) collective-permute-start(bf16[1,128,128]{2,1,0:T(8,128)(2,1)S(1)} %get-tuple-element.41), channel_id=1, source_target_pairs={{0,3},{1,2},{2,1},{3,0},{4,7},{5,6},{6,5},{7,4},{8,11},{9,10},{10,... | collective-permute-start | bytes 98312 | tf_op jit(solution)/shard_map/ppermute | solution.py:40
  30.0 3.4 %collective-permute-start.13 = (bf16[1,128,128]{2,1,0:T(8,128)(2,1)S(1)}, bf16[1,128,128]{2,1,0:T(8,128)(2,1)S(1)}, u32[]{:S(2)}, u32[]{:S(2)}) collective-permute-start(bf16[1,128,128]{2,1,0:T(8,128)(2,1)S(1)} %get-tuple-element.43.refs_1_), channel_id=1, source_target_pairs={{0,1},{1,0},{2,3},{3,2},{4,5},{5,4},{6,7},{7,6},{8,9},{9,8},{10,11... | collective-permute-start | bytes 98312 | tf_op jit(solution)/shard_map/ppermute | solution.py:40
  30.2 4.3 %collective-permute-start.16 = (bf16[1,128,128]{2,1,0:T(8,128)(2,1)S(1)}, bf16[1,128,128]{2,1,0:T(8,128)(2,1)S(1)}, u32[]{:S(2)}, u32[]{:S(2)}) collective-permute-start(bf16[1,128,128]{2,1,0:T(8,128)(2,1)S(1)} %get-tuple-element.43.refs_1_), channel_id=1, source_target_pairs={{0,5},{1,4},{2,7},{3,6},{4,1},{5,0},{6,3},{7,2},{8,13},{9,12},{10,... | collective-permute-start | bytes 98312 | tf_op jit(solution)/shard_map/ppermute | solution.py:40
  30.7 5.3 %collective-permute-start.15 = (bf16[1,128,128]{2,1,0:T(8,128)(2,1)S(1)}, bf16[1,128,128]{2,1,0:T(8,128)(2,1)S(1)}, u32[]{:S(2)}, u32[]{:S(2)}) collective-permute-start(bf16[1,128,128]{2,1,0:T(8,128)(2,1)S(1)} %get-tuple-element.43.refs_1_), channel_id=1, source_target_pairs={{0,7},{1,6},{2,5},{3,4},{4,3},{5,2},{6,1},{7,0},{8,15},{9,14},{10,... | collective-permute-start | bytes 98312 | tf_op jit(solution)/shard_map/ppermute | solution.py:40
  32.0 4.0 %collective-permute-start.14 = (bf16[1,128,128]{2,1,0:T(8,128)(2,1)S(1)}, bf16[1,128,128]{2,1,0:T(8,128)(2,1)S(1)}, u32[]{:S(2)}, u32[]{:S(2)}) collective-permute-start(bf16[1,128,128]{2,1,0:T(8,128)(2,1)S(1)} %get-tuple-element.43.refs_1_), channel_id=1, source_target_pairs={{0,3},{1,2},{2,1},{3,0},{4,7},{5,6},{6,5},{7,4},{8,11},{9,10},{10,... | collective-permute-start | bytes 98312 | tf_op jit(solution)/shard_map/ppermute | solution.py:40
  36.0 1.5 %collective-permute-start.17 = (bf16[3,128,128]{2,1,0:T(8,128)(2,1)S(1)}, bf16[3,128,128]{2,1,0:T(8,128)(2,1)S(1)}, u32[]{:S(2)}, u32[]{:S(2)}) collective-permute-start(bf16[3,128,128]{2,1,0:T(8,128)(2,1)S(1)} %join.3.bundle_ref.refs_0_), channel_id=1, source_target_pairs={{0,1},{1,0},{2,3},{3,2},{4,5},{5,4},{6,7},{7,6},{8,9},{9,8},{10,11... | collective-permute-start | bytes 294920 | tf_op jit(solution)/shard_map/ppermute | solution.py:40
  38.4 5.8 %collective-permute-start.19 = (bf16[192,128]{1,0:T(8,128)(2,1)S(1)}, bf16[192,128]{1,0:T(8,128)(2,1)S(1)}, u32[]{:S(2)}, u32[]{:S(2)}) collective-permute-start(bf16[192,128]{1,0:T(8,128)(2,1)S(1)} %get-tuple-element.46), channel_id=1, source_target_pairs={{0,24},{8,16},{16,8},{24,0},{1,25},{9,17},{17,9},{25,1},{2,26},{10... | collective-permute-start | bytes 147464 | tf_op jit(solution)/shard_map/ppermute | solution.py:40
  39.9 4.3 %collective-permute-start.18 = (bf16[192,128]{1,0:T(8,128)(2,1)S(1)}, bf16[192,128]{1,0:T(8,128)(2,1)S(1)}, u32[]{:S(2)}, u32[]{:S(2)}) collective-permute-start(bf16[192,128]{1,0:T(8,128)(2,1)S(1)} %get-tuple-element.46), channel_id=1, source_target_pairs={{0,8},{8,0},{16,24},{24,16},{1,9},{9,1},{17,25},{25,17},{2,10},{10... | collective-permute-start | bytes 147464 | tf_op jit(solution)/shard_map/ppermute | solution.py:40
  40.4 3.7 %collective-permute-start.20 = (bf16[64,128]{1,0:T(8,128)(2,1)S(1)}, bf16[64,128]{1,0:T(8,128)(2,1)S(1)}, u32[]{:S(2)}, u32[]{:S(2)}) collective-permute-start(bf16[64,128]{1,0:T(8,128)(2,1)S(1)} %get-tuple-element.47.refs_0_), channel_id=1, source_target_pairs={{0,16},{8,24},{16,0},{24,8},{1,17},{9,25},{17,1},{25,9},{2,18},{10... | collective-permute-start | bytes 49160 | tf_op jit(solution)/shard_map/ppermute | solution.py:40
  44.9 1.4 %collective-permute-start.21 = (bf16[2,128,128]{2,1,0:T(8,128)(2,1)S(1)}, bf16[2,128,128]{2,1,0:T(8,128)(2,1)S(1)}, u32[]{:S(2)}, u32[]{:S(2)}) collective-permute-start(bf16[2,128,128]{2,1,0:T(8,128)(2,1)S(1)} %get-tuple-element.50), channel_id=1, source_target_pairs={{0,1},{1,0},{2,3},{3,2},{4,5},{5,4},{6,7},{7,6},{8,9},{9,8},{10,11... | collective-permute-start | bytes 196616 | tf_op jit(solution)/shard_map/ppermute | solution.py:40
  45.8 3.1 %collective-permute-start.22 = (bf16[2,128,128]{2,1,0:T(8,128)(2,1)S(1)}, bf16[2,128,128]{2,1,0:T(8,128)(2,1)S(1)}, u32[]{:S(2)}, u32[]{:S(2)}) collective-permute-start(bf16[2,128,128]{2,1,0:T(8,128)(2,1)S(1)} %get-tuple-element.53), channel_id=1, source_target_pairs={{0,1},{1,0},{2,3},{3,2},{4,5},{5,4},{6,7},{7,6},{8,9},{9,8},{10,11... | collective-permute-start | bytes 196616 | tf_op jit(solution)/shard_map/ppermute | solution.py:40
  46.4 5.3 %collective-permute-start.23 = (bf16[1,128,128]{2,1,0:T(8,128)(2,1)S(1)}, bf16[1,128,128]{2,1,0:T(8,128)(2,1)S(1)}, u32[]{:S(2)}, u32[]{:S(2)}) collective-permute-start(bf16[1,128,128]{2,1,0:T(8,128)(2,1)S(1)} %get-tuple-element.51.refs_0_), channel_id=1, source_target_pairs={{0,7},{1,6},{2,5},{3,4},{4,3},{5,2},{6,1},{7,0},{8,15},{9,14},{10,... | collective-permute-start | bytes 98312 | tf_op jit(solution)/shard_map/ppermute | solution.py:40
  48.4 4.7 %collective-permute-start.24 = (bf16[1,128,128]{2,1,0:T(8,128)(2,1)S(1)}, bf16[1,128,128]{2,1,0:T(8,128)(2,1)S(1)}, u32[]{:S(2)}, u32[]{:S(2)}) collective-permute-start(bf16[1,128,128]{2,1,0:T(8,128)(2,1)S(1)} %get-tuple-element.52.refs_1_), channel_id=1, source_target_pairs={{0,5},{1,4},{2,7},{3,6},{4,1},{5,0},{6,3},{7,2},{8,13},{9,12},{10,... | collective-permute-start | bytes 98312 | tf_op jit(solution)/shard_map/ppermute | solution.py:40
  48.9 4.2 %collective-permute-start.25 = (bf16[1,128,128]{2,1,0:T(8,128)(2,1)S(1)}, bf16[1,128,128]{2,1,0:T(8,128)(2,1)S(1)}, u32[]{:S(2)}, u32[]{:S(2)}) collective-permute-start(bf16[1,128,128]{2,1,0:T(8,128)(2,1)S(1)} %get-tuple-element.55), channel_id=1, source_target_pairs={{0,3},{1,2},{2,1},{3,0},{4,7},{5,6},{6,5},{7,4},{8,11},{9,10},{10,... | collective-permute-start | bytes 98312 | tf_op jit(solution)/shard_map/ppermute | solution.py:40

commit v11 on v10

--- a/solution.py
+++ b/solution.py
@@ -111,14 +111,19 @@
     diagonal(rows, spots, blocks_of(field_refs), factor_ref, store)
 
 
-def columns_kernel(halve, spots, x_ref, bundle_ref, twin_ref, along_ref, short_ref):
+def columns_kernel(halve, masks, x_ref, bundle_ref, twin_ref, along_ref, short_ref):
     me = lax.axis_index("tile")
-    low = jnp.zeros(x_ref.shape, jnp.float32)
-    high = low
-    for spot, block in zip(spots, blocks_of([bundle_ref, twin_ref])):
-        part, place = block.astype(jnp.float32), place_of(spot)
-        low = jnp.where(place == me - 1, part, low)
-        high = jnp.where(place == me + 1, part, high)
+    chip, core = lax.div(me, 2), lax.rem(me, 2)
+    near = bundle_ref.shape[0] + 1
+    beside = chip + 2 * core - 1
+    slot = 0
+    for n, mask in enumerate(masks):
+        slot = jnp.where((chip ^ beside) == mask, n, slot)
+    far = bundle_ref[slot].astype(jnp.float32)
+    far = jnp.where((beside >= 0) & (beside < near), far, 0.0)
+    twin = twin_ref[0].astype(jnp.float32)
+    low = jnp.where(core == 0, far, twin)
+    high = jnp.where(core == 0, twin, far)
     own = 0.5 * x_ref[...] if halve else x_ref[...]
     along = stencil(low, own, high, COL_TAPS, 1)
     along_ref[...] = along
@@ -322,7 +327,7 @@
         order.sort(key=lambda mask: (mask == half, mask))
         parts = [cross(short, mask) for mask in order]
         twin = swap(short, "tile", 1)
-        diag = first([twin, short], [(0, True), (0, False)])
+        diag = first([short], [(0, False)])
         bundle = call(
             join_kernel,
             shape(bf16, near - 1, lines, width),
@@ -332,10 +337,10 @@
         )(diag, twin, *parts)
         across = swap(bundle, "tile", 1)
         known = spots_of(order, False) + [(0, True)]
-        diag = first([bundle], spots_of(order, False), diag)
+        diag = first([bundle, twin], known, diag)
         spots = spots_of(order, True)
         along, along_short = call(
-            partial(columns_kernel, halve, known),
+            partial(columns_kernel, halve, order),
             (shape(f32, lines, width), shape(bf16, lines, width)),
             name="columns",
         )(x, bundle, twin)

time: 54 us -> 53.6 us (level)
  waiting for transfers between devices: 14.5 us -> 13.6 us
  starting transfers between devices: 24.7 us -> 25.4 us
    ppermute x26, waiting for transfers between devices: 14.5 us -> 13.6 us  [swap(): lax.ppermute(value, axis, [(i, i ^ mask) for i in range(lax.axis_size(axi...]
    ppermute x26, starting transfers between devices: 24.7 us -> 25.4 us  [swap(): lax.ppermute(value, axis, [(i, i ^ mask) for i in range(lax.axis_size(axi...]
  transfers between devices with their start and end apart: 26 -> 26, of which waited for: 10 -> 11; matrix products, arithmetic and copies ran while one was open for 0% -> 0% of each run, Pallas kernels for 12% -> 12%
where the time goes in v11:
time: 53.6 us; the launch traced here: 53.3 us
  starting transfers between devices  25.4 us (47%)
  waiting for transfers between devices  13.6 us (25%)
  Pallas kernels  10.4 us (19%)
  local copies, waits for them, and re-layouts  2.21 us (4%)
  between operations  0.89 us (2%)
  other arithmetic  0.85 us (2%)
    ppermute x26, starting transfers between devices, swap(): lax.ppermute(value, axis, [(i, i ^ mask) for i in range(lax.axis_size(axi...  25.4 us
    ppermute x26, waiting for transfers between devices, swap(): lax.ppermute(value, axis, [(i, i ^ mask) for i in range(lax.axis_size(axi...  13.6 us
    pallas_call x4, Pallas kernels, term(): call(partial(term_kernel, wanted, len(after)), in_specs=[pl.BlockSpec(mem...  2.59 us
    pallas_call x4, Pallas kernels, first(): call(partial(first_kernel, rows, spots, len(before)), shape(f32, blocks *...  2.37 us
    unnamed x8, local copies, waits for them, and re-layouts  2.21 us
    pallas_call x2, Pallas kernels, on_device(): call(partial(second_kernel, rows, cols, spots), (shape(bf16, pay_rows, wi...  1.75 us
    pallas_call x2, Pallas kernels, on_device(): call(partial(far_kernel, rows, cols, groups, ncells_all, spots_of(away, T...  1.45 us
  transfers between devices with their start and end apart: 26, of which 11 were waited for; matrix products, arithmetic and copies ran while one was open for 0% of the time, Pallas kernels for 12%

profile of v11, /device:TPU:0, one launch (start us, length us, event | category | flops | bytes accessed | tf_op | source)
XLA Modules:
  0.0 53.3 jit_solution(5447622372922185446)
XLA Ops:
  0.6 0.8 %fusion.refs_0_ = bf16[1,128,128]{2,1,0:T(8,128)(2,1)S(1)} fusion(f32[16,8,128]{2,1,0:T(8,128)} %param.4), kind=kLoop, calls=%fused_computation.1 | loop fusion | flops 32768 | bytes 98304 | tf_op jit(solution)/shard_map/convert_element_type | solution.py:277
  1.5 3.5 %collective-permute-start.3 = (bf16[1,128,128]{2,1,0:T(8,128)(2,1)S(1)}, bf16[1,128,128]{2,1,0:T(8,128)(2,1)S(1)}, u32[]{:S(2)}, u32[]{:S(2)}) collective-permute-start(bf16[1,128,128]{2,1,0:T(8,128)(2,1)S(1)} %fusion.refs_0_), channel_id=1, source_target_pairs={{0,5},{1,4},{2,7},{3,6},{4,1},{5,0},{6,3},{7,2},{8,13},{9,12},{10,... | collective-permute-start | bytes 98312 | tf_op jit(solution)/shard_map/ppermute | solution.py:40
  5.0 1.6 %collective-permute-start.2 = (bf16[1,128,128]{2,1,0:T(8,128)(2,1)S(1)}, bf16[1,128,128]{2,1,0:T(8,128)(2,1)S(1)}, u32[]{:S(2)}, u32[]{:S(2)}) collective-permute-start(bf16[1,128,128]{2,1,0:T(8,128)(2,1)S(1)} %fusion.refs_0_), channel_id=1, source_target_pairs={{0,7},{1,6},{2,5},{3,4},{4,3},{5,2},{6,1},{7,0},{8,15},{9,14},{10,... | collective-permute-start | bytes 98312 | tf_op jit(solution)/shard_map/ppermute | solution.py:40
  6.6 0.2 collective-permute-start.1
  6.8 2.2 %copy-done = bf16[256,8,1024]{2,1,0:T(8,128)(2,1)S(1)} copy-done((bf16[256,8,1024]{2,1,0:T(8,128)(2,1)S(1)}, bf16[256,8,1024]{2,1,0:T(8,128)(2,1)}, u32[]{:S(2)}) %copy-start) | copy-done | bytes 4194328
  9.0 0.4 load.1.factor_ref
  9.4 0.0 copy-start.1
  9.4 0.5 project_own.4.refs_0_.refs_2_
  9.9 0.3 collective-permute-done.2.refs_3_
  10.2 0.2 collective-permute-done.1.refs_2_
  10.4 0.0 collective-permute-done.refs_1_.twin_ref
  10.4 0.7 %collective-permute-start.4 = (bf16[3,128,128]{2,1,0:T(8,128)(2,1)S(1)}, bf16[3,128,128]{2,1,0:T(8,128)(2,1)S(1)}, u32[]{:S(2)}, u32[]{:S(2)}) collective-permute-start(bf16[3,128,128]{2,1,0:T(8,128)(2,1)S(1)} %join.2.bundle_ref.refs_0_), channel_id=1, source_target_pairs={{0,1},{1,0},{2,3},{3,2},{4,5},{5,4},{6,7},{7,6},{8,9},{9,8},{10,11... | collective-permute-start | bytes 294920 | tf_op jit(solution)/shard_map/ppermute | solution.py:40
  11.1 0.4 columns.2
  11.5 0.0 copy-start.3
  11.5 0.7 %project_own.5.diag_ref = f32[256,128]{1,0:T(8,128)S(1)} custom-call(bf16[2048,1024]{1,0:T(8,128)(2,1)S(1)} %load.1.factor_ref, bf16[3,128,128]{2,1,0:T(8,128)(2,1)S(1)} %join.2.bundle_ref.refs_0_, bf16[1,128,128]{2,1,0:T(8,128)(2,1)S(1)} %collective-permute-done.refs_1_.twin_ref, f32[256,128]{1,0:T(8,128)S(1)} %project_own.4.refs_0_.refs_2_), custom_call_target="tpu_custom_call" | custom-call | flops 268435456 | bytes 2097152 | tf_op jit(solution)/shard_map/project_own/pallas_call | solution.py:314
  12.2 0.9 %project_across.2 = (bf16[192,128]{1,0:T(8,128)(2,1)S(1)}, bf16[64,128]{1,0:T(8,128)(2,1)S(1)}) custom-call(bf16[2048,1024]{1,0:T(8,128)(2,1)S(1)} %load.1.factor_ref, f32[256,128]{1,0:T(8,128)S(1)} %project_own.5.diag_ref, bf16[3,128,128]{2,1,0:T(8,128)(2,1)S(1)} %collective-permute-done.4.fields_ref, bf16[128,128]{1,0:T(8,128)(2,1)S(1)} %get-tuple-element.31.short_ref), custom_call_target="tpu_custom_call" | custom-call | flops 268435456 | bytes 2097152 | tf_op jit(solution)/shard_map/project_across/pallas_call | solution.py:347
  13.1 2.5 %collective-permute-start.6 = (bf16[192,128]{1,0:T(8,128)(2,1)S(1)}, bf16[192,128]{1,0:T(8,128)(2,1)S(1)}, u32[]{:S(2)}, u32[]{:S(2)}) collective-permute-start(bf16[192,128]{1,0:T(8,128)(2,1)S(1)} %get-tuple-element.32), channel_id=1, source_target_pairs={{0,24},{8,16},{16,8},{24,0},{1,25},{9,17},{17,9},{25,1},{2,26},{10... | collective-permute-start | bytes 147464 | tf_op jit(solution)/shard_map/ppermute | solution.py:40
  15.6 0.5 %collective-permute-start.5 = (bf16[192,128]{1,0:T(8,128)(2,1)S(1)}, bf16[192,128]{1,0:T(8,128)(2,1)S(1)}, u32[]{:S(2)}, u32[]{:S(2)}) collective-permute-start(bf16[192,128]{1,0:T(8,128)(2,1)S(1)} %get-tuple-element.32), channel_id=1, source_target_pairs={{0,8},{8,0},{16,24},{24,16},{1,9},{9,1},{17,25},{25,17},{2,10},{10... | collective-permute-start | bytes 147464 | tf_op jit(solution)/shard_map/ppermute | solution.py:40
  16.1 0.5 collective-permute-start.7
  16.6 3.2 %collective-permute-done.7.refs_2_ = bf16[64,128]{1,0:T(8,128)(2,1)S(1)} collective-permute-done((bf16[64,128]{1,0:T(8,128)(2,1)S(1)}, bf16[64,128]{1,0:T(8,128)(2,1)S(1)}, u32[]{:S(2)}, u32[]{:S(2)}) %collective-permute-start.7) | collective-permute-done | bytes 16416 | tf_op jit(solution)/shard_map/ppermute | solution.py:40
  19.9 0.7 %term_first.2 = (bf16[128,2048]{1,0:T(8,128)(2,1)S(1)}, bf16[2,128,128]{2,1,0:T(8,128)(2,1)S(1)}) custom-call(f32[1,256]{1,0:T(1,128)S(1)} %bitcast.13, bf16[2048,1024]{1,0:T(8,128)(2,1)S(1)} %load.1.factor_ref, bf16[64,128]{1,0:T(8,128)(2,1)S(1)} %get-tuple-element.33.refs_0_, bf16[192,128]{1,0:T(8,128)(2,1)S(1)} %collective-permute-done.5.refs_0_.refs_1_, ...), custom_call_target="tpu_custom_call" | custom-call | flops 134217728 | bytes 2097152 | tf_op jit(solution)/shard_map/term_first/pallas_call | solution.py:356
  20.6 0.1 collective-permute-start.8
  20.7 0.0 copy-start.2
  20.7 0.8 %term.4 = (f32[2,128,128]{2,1,0:T(8,128)S(1)}, bf16[2,128,128]{2,1,0:T(8,128)(2,1)S(1)}) custom-call(bf16[128,2048]{1,0:T(8,128)(2,1)S(1)} %get-tuple-element.34.coef_ref, bf16[2048,1024]{1,0:T(8,128)(2,1)S(1)} %load.1.factor_ref), custom_call_target="tpu_custom_call" | custom-call | flops 268435456 | bytes 2097152 | tf_op jit(solution)/shard_map/term/pallas_call | solution.py:366
  21.5 0.5 %collective-permute-start.9 = (bf16[2,128,128]{2,1,0:T(8,128)(2,1)S(1)}, bf16[2,128,128]{2,1,0:T(8,128)(2,1)S(1)}, u32[]{:S(2)}, u32[]{:S(2)}) collective-permute-start(bf16[2,128,128]{2,1,0:T(8,128)(2,1)S(1)} %get-tuple-element.39), channel_id=1, source_target_pairs={{0,1},{1,0},{2,3},{3,2},{4,5},{5,4},{6,7},{7,6},{8,9},{9,8},{10,11... | collective-permute-start | bytes 196616 | tf_op jit(solution)/shard_map/ppermute | solution.py:40
  22.1 1.8 %collective-permute-start.10 = (bf16[1,128,128]{2,1,0:T(8,128)(2,1)S(1)}, bf16[1,128,128]{2,1,0:T(8,128)(2,1)S(1)}, u32[]{:S(2)}, u32[]{:S(2)}) collective-permute-start(bf16[1,128,128]{2,1,0:T(8,128)(2,1)S(1)} %get-tuple-element.37.refs_0_), channel_id=1, source_target_pairs={{0,5},{1,4},{2,7},{3,6},{4,1},{5,0},{6,3},{7,2},{8,13},{9,12},{10,... | collective-permute-start | bytes 98312 | tf_op jit(solution)/shard_map/ppermute | solution.py:40
  23.8 1.4 %collective-permute-start.11 = (bf16[1,128,128]{2,1,0:T(8,128)(2,1)S(1)}, bf16[1,128,128]{2,1,0:T(8,128)(2,1)S(1)}, u32[]{:S(2)}, u32[]{:S(2)}) collective-permute-start(bf16[1,128,128]{2,1,0:T(8,128)(2,1)S(1)} %get-tuple-element.38.refs_1_), channel_id=1, source_target_pairs={{0,7},{1,6},{2,5},{3,4},{4,3},{5,2},{6,1},{7,0},{8,15},{9,14},{10,... | collective-permute-start | bytes 98312 | tf_op jit(solution)/shard_map/ppermute | solution.py:40
  25.2 0.5 term.5.mine_ref
  25.7 0.0 collective-permute-done.9.got_ref
  25.8 0.1 collective-permute-start.12
  25.8 0.2 local.2.base_ref
  26.0 0.5 collective-permute-done.10.refs_1_
  26.5 2.4 %collective-permute-done.11.refs_2_ = bf16[1,128,128]{2,1,0:T(8,128)(2,1)S(1)} collective-permute-done((bf16[1,128,128]{2,1,0:T(8,128)(2,1)S(1)}, bf16[1,128,128]{2,1,0:T(8,128)(2,1)S(1)}, u32[]{:S(2)}, u32[]{:S(2)}) %collective-permute-start.11) | collective-permute-done | bytes 32800 | tf_op jit(solution)/shard_map/ppermute | solution.py:40
  29.0 1.0 %collective-permute-done.12.refs_3_ = bf16[1,128,128]{2,1,0:T(8,128)(2,1)S(1)} collective-permute-done((bf16[1,128,128]{2,1,0:T(8,128)(2,1)S(1)}, bf16[1,128,128]{2,1,0:T(8,128)(2,1)S(1)}, u32[]{:S(2)}, u32[]{:S(2)}) %collective-permute-start.12) | collective-permute-done | bytes 32800 | tf_op jit(solution)/shard_map/ppermute | solution.py:40
  30.0 0.4 collective-permute-start.16
  30.3 1.4 %collective-permute-start.15 = (bf16[1,128,128]{2,1,0:T(8,128)(2,1)S(1)}, bf16[1,128,128]{2,1,0:T(8,128)(2,1)S(1)}, u32[]{:S(2)}, u32[]{:S(2)}) collective-permute-start(bf16[1,128,128]{2,1,0:T(8,128)(2,1)S(1)} %get-tuple-element.43.refs_0_), channel_id=1, source_target_pairs={{0,7},{1,6},{2,5},{3,4},{4,3},{5,2},{6,1},{7,0},{8,15},{9,14},{10,... | collective-permute-start | bytes 98312 | tf_op jit(solution)/shard_map/ppermute | solution.py:40
  31.8 1.2 %collective-permute-start.14 = (bf16[1,128,128]{2,1,0:T(8,128)(2,1)S(1)}, bf16[1,128,128]{2,1,0:T(8,128)(2,1)S(1)}, u32[]{:S(2)}, u32[]{:S(2)}) collective-permute-start(bf16[1,128,128]{2,1,0:T(8,128)(2,1)S(1)} %get-tuple-element.43.refs_0_), channel_id=1, source_target_pairs={{0,3},{1,2},{2,1},{3,0},{4,7},{5,6},{6,5},{7,4},{8,11},{9,10},{10,... | collective-permute-start | bytes 98312 | tf_op jit(solution)/shard_map/ppermute | solution.py:40
  33.0 0.4 collective-permute-start.13
  33.4 0.5 project_own.6.refs_0_.refs_2_
  33.9 0.5 collective-permute-done.16.refs_4_
  34.3 1.2 %collective-permute-done.15.refs_3_ = bf16[1,128,128]{2,1,0:T(8,128)(2,1)S(1)} collective-permute-done((bf16[1,128,128]{2,1,0:T(8,128)(2,1)S(1)}, bf16[1,128,128]{2,1,0:T(8,128)(2,1)S(1)}, u32[]{:S(2)}, u32[]{:S(2)}) %collective-permute-start.15) | collective-permute-done | bytes 32800 | tf_op jit(solution)/shard_map/ppermute | solution.py:40
  35.5 0.6 %collective-permute-start.17 = (bf16[3,128,128]{2,1,0:T(8,128)(2,1)S(1)}, bf16[3,128,128]{2,1,0:T(8,128)(2,1)S(1)}, u32[]{:S(2)}, u32[]{:S(2)}) collective-permute-start(bf16[3,128,128]{2,1,0:T(8,128)(2,1)S(1)} %join.3.bundle_ref.refs_0_), channel_id=1, source_target_pairs={{0,1},{1,0},{2,3},{3,2},{4,5},{5,4},{6,7},{7,6},{8,9},{9,8},{10,11... | collective-permute-start | bytes 294920 | tf_op jit(solution)/shard_map/ppermute | solution.py:40
  36.1 0.3 columns.3
  36.4 0.7 %project_own.7.diag_ref = f32[256,128]{1,0:T(8,128)S(1)} custom-call(bf16[2048,1024]{1,0:T(8,128)(2,1)S(1)} %load.1.factor_ref, bf16[3,128,128]{2,1,0:T(8,128)(2,1)S(1)} %join.3.bundle_ref.refs_0_, bf16[1,128,128]{2,1,0:T(8,128)(2,1)S(1)} %collective-permute-done.13.refs_1_.twin_ref, f32[256,128]{1,0:T(8,128)S(1)} %project_own.6.refs_0_.refs_2_), custom_call_target="tpu_custom_call" | custom-call | flops 268435456 | bytes 2097152 | tf_op jit(solution)/shard_map/project_own/pallas_call | solution.py:314
  37.2 0.0 collective-permute-done.17.fields_ref
  37.2 0.9 %project_across.3 = (bf16[192,128]{1,0:T(8,128)(2,1)S(1)}, bf16[64,128]{1,0:T(8,128)(2,1)S(1)}) custom-call(bf16[2048,1024]{1,0:T(8,128)(2,1)S(1)} %load.1.factor_ref, f32[256,128]{1,0:T(8,128)S(1)} %project_own.7.diag_ref, bf16[3,128,128]{2,1,0:T(8,128)(2,1)S(1)} %collective-permute-done.17.fields_ref, bf16[128,128]{1,0:T(8,128)(2,1)S(1)} %get-tuple-element.45.short_ref), custom_call_target="tpu_custom_call" | custom-call | flops 268435456 | bytes 2097152 | tf_op jit(solution)/shard_map/project_across/pallas_call | solution.py:347
  38.1 1.5 %collective-permute-start.19 = (bf16[192,128]{1,0:T(8,128)(2,1)S(1)}, bf16[192,128]{1,0:T(8,128)(2,1)S(1)}, u32[]{:S(2)}, u32[]{:S(2)}) collective-permute-start(bf16[192,128]{1,0:T(8,128)(2,1)S(1)} %get-tuple-element.46), channel_id=1, source_target_pairs={{0,24},{8,16},{16,8},{24,0},{1,25},{9,17},{17,9},{25,1},{2,26},{10... | collective-permute-start | bytes 147464 | tf_op jit(solution)/shard_map/ppermute | solution.py:40
  39.5 0.5 %collective-permute-start.18 = (bf16[192,128]{1,0:T(8,128)(2,1)S(1)}, bf16[192,128]{1,0:T(8,128)(2,1)S(1)}, u32[]{:S(2)}, u32[]{:S(2)}) collective-permute-start(bf16[192,128]{1,0:T(8,128)(2,1)S(1)} %get-tuple-element.46), channel_id=1, source_target_pairs={{0,8},{8,0},{16,24},{24,16},{1,9},{9,1},{17,25},{25,17},{2,10},{10... | collective-permute-start | bytes 147464 | tf_op jit(solution)/shard_map/ppermute | solution.py:40
  40.1 1.5 %collective-permute-start.20 = (bf16[64,128]{1,0:T(8,128)(2,1)S(1)}, bf16[64,128]{1,0:T(8,128)(2,1)S(1)}, u32[]{:S(2)}, u32[]{:S(2)}) collective-permute-start(bf16[64,128]{1,0:T(8,128)(2,1)S(1)} %get-tuple-element.47.refs_0_), channel_id=1, source_target_pairs={{0,16},{8,24},{16,0},{24,8},{1,17},{9,25},{17,1},{25,9},{2,18},{10... | collective-permute-start | bytes 49160 | tf_op jit(solution)/shard_map/ppermute | solution.py:40
  41.6 2.2 %collective-permute-done.20.refs_2_ = bf16[64,128]{1,0:T(8,128)(2,1)S(1)} collective-permute-done((bf16[64,128]{1,0:T(8,128)(2,1)S(1)}, bf16[64,128]{1,0:T(8,128)(2,1)S(1)}, u32[]{:S(2)}, u32[]{:S(2)}) %collective-permute-start.20) | collective-permute-done | bytes 16416 | tf_op jit(solution)/shard_map/ppermute | solution.py:40
  43.8 0.0 collective-permute-done.18.refs_0_.refs_1_
  43.8 0.7 %term_first.3 = (bf16[128,2048]{1,0:T(8,128)(2,1)S(1)}, bf16[2,128,128]{2,1,0:T(8,128)(2,1)S(1)}) custom-call(f32[1,256]{1,0:T(1,128)S(1)} %bitcast.14, bf16[2048,1024]{1,0:T(8,128)(2,1)S(1)} %load.1.factor_ref, bf16[64,128]{1,0:T(8,128)(2,1)S(1)} %get-tuple-element.47.refs_0_, bf16[192,128]{1,0:T(8,128)(2,1)S(1)} %collective-permute-done.18.refs_0_.refs_1_, ...), custom_call_target="tpu_custom_call" | custom-call | flops 134217728 | bytes 2097152 | tf_op jit(solution)/shard_map/term_first/pallas_call | solution.py:356
  44.5 0.1 collective-permute-start.21
  44.6 0.8 %term.6 = (f32[2,128,128]{2,1,0:T(8,128)S(1)}, bf16[2,128,128]{2,1,0:T(8,128)(2,1)S(1)}) custom-call(bf16[128,2048]{1,0:T(8,128)(2,1)S(1)} %get-tuple-element.48.coef_ref, bf16[2048,1024]{1,0:T(8,128)(2,1)S(1)} %load.1.factor_ref), custom_call_target="tpu_custom_call" | custom-call | flops 268435456 | bytes 2097152 | tf_op jit(solution)/shard_map/term/pallas_call | solution.py:366
  45.4 0.6 %collective-permute-start.22 = (bf16[2,128,128]{2,1,0:T(8,128)(2,1)S(1)}, bf16[2,128,128]{2,1,0:T(8,128)(2,1)S(1)}, u32[]{:S(2)}, u32[]{:S(2)}) collective-permute-start(bf16[2,128,128]{2,1,0:T(8,128)(2,1)S(1)} %get-tuple-element.53), channel_id=1, source_target_pairs={{0,1},{1,0},{2,3},{3,2},{4,5},{5,4},{6,7},{7,6},{8,9},{9,8},{10,11... | collective-permute-start | bytes 196616 | tf_op jit(solution)/shard_map/ppermute | solution.py:40
  46.0 2.1 %collective-permute-start.23 = (bf16[1,128,128]{2,1,0:T(8,128)(2,1)S(1)}, bf16[1,128,128]{2,1,0:T(8,128)(2,1)S(1)}, u32[]{:S(2)}, u32[]{:S(2)}) collective-permute-start(bf16[1,128,128]{2,1,0:T(8,128)(2,1)S(1)} %get-tuple-element.51.refs_0_), channel_id=1, source_target_pairs={{0,7},{1,6},{2,5},{3,4},{4,3},{5,2},{6,1},{7,0},{8,15},{9,14},{10,... | collective-permute-start | bytes 98312 | tf_op jit(solution)/shard_map/ppermute | solution.py:40
  48.1 0.0 collective-permute-start.24
  48.1 0.5 term.7.mine_ref
  48.7 1.7 %collective-permute-start.25 = (bf16[1,128,128]{2,1,0:T(8,128)(2,1)S(1)}, bf16[1,128,128]{2,1,0:T(8,128)(2,1)S(1)}, u32[]{:S(2)}, u32[]{:S(2)}) collective-permute-start(bf16[1,128,128]{2,1,0:T(8,128)(2,1)S(1)} %get-tuple-element.55), channel_id=1, source_target_pairs={{0,3},{1,2},{2,1},{3,0},{4,7},{5,6},{6,5},{7,4},{8,11},{9,10},{10,... | collective-permute-start | bytes 98312 | tf_op jit(solution)/shard_map/ppermute | solution.py:40
  50.4 0.2 local.3.base_ref
  50.6 0.8 %collective-permute-done.23.refs_1_ = bf16[1,128,128]{2,1,0:T(8,128)(2,1)S(1)} collective-permute-done((bf16[1,128,128]{2,1,0:T(8,128)(2,1)S(1)}, bf16[1,128,128]{2,1,0:T(8,128)(2,1)S(1)}, u32[]{:S(2)}, u32[]{:S(2)}) %collective-permute-start.23) | collective-permute-done | bytes 32800 | tf_op jit(solution)/shard_map/ppermute | solution.py:40
  51.3 1.3 %collective-permute-done.24.refs_2_ = bf16[1,128,128]{2,1,0:T(8,128)(2,1)S(1)} collective-permute-done((bf16[1,128,128]{2,1,0:T(8,128)(2,1)S(1)}, bf16[1,128,128]{2,1,0:T(8,128)(2,1)S(1)}, u32[]{:S(2)}, u32[]{:S(2)}) %collective-permute-start.24) | collective-permute-done | bytes 32800 | tf_op jit(solution)/shard_map/ppermute | solution.py:40
  52.6 0.0 collective-permute-done.25.refs_3_
  52.6 0.7 %update.3 = (f32[128,128]{1,0:T(8,128)}, f32[128,128]{1,0:T(8,128)}) custom-call(f32[128,128]{1,0:T(8,128)S(1)} %get-tuple-element.42.x_ref, f32[128,128]{1,0:T(8,128)S(1)} %local.3.base_ref, f32[1,128,128]{2,1,0:T(8,128)S(1)} %get-tuple-element.54.refs_0_, bf16[1,128,128]{2,1,0:T(8,128)(2,1)S(1)} %collective-permute-done.23.refs_1_, ...), custom_call_target="tpu_custom_call" | custom-call | bytes 262144 | tf_op jit(solution)/shard_map/update/pallas_call | solution.py:394
  (22 shorter events, 0.1 us)
Async XLA Ops:
  1.5 8.4 %collective-permute-start.3 = (bf16[1,128,128]{2,1,0:T(8,128)(2,1)S(1)}, bf16[1,128,128]{2,1,0:T(8,128)(2,1)S(1)}, u32[]{:S(2)}, u32[]{:S(2)}) collective-permute-start(bf16[1,128,128]{2,1,0:T(8,128)(2,1)S(1)} %fusion.refs_0_), channel_id=1, source_target_pairs={{0,5},{1,4},{2,7},{3,6},{4,1},{5,0},{6,3},{7,2},{8,13},{9,12},{10,... | collective-permute-start | bytes 98312 | tf_op jit(solution)/shard_map/ppermute | solution.py:40
  5.0 5.2 %collective-permute-start.2 = (bf16[1,128,128]{2,1,0:T(8,128)(2,1)S(1)}, bf16[1,128,128]{2,1,0:T(8,128)(2,1)S(1)}, u32[]{:S(2)}, u32[]{:S(2)}) collective-permute-start(bf16[1,128,128]{2,1,0:T(8,128)(2,1)S(1)} %fusion.refs_0_), channel_id=1, source_target_pairs={{0,7},{1,6},{2,5},{3,4},{4,3},{5,2},{6,1},{7,0},{8,15},{9,14},{10,... | collective-permute-start | bytes 98312 | tf_op jit(solution)/shard_map/ppermute | solution.py:40
  6.6 3.8 %collective-permute-start.1 = (bf16[1,128,128]{2,1,0:T(8,128)(2,1)S(1)}, bf16[1,128,128]{2,1,0:T(8,128)(2,1)S(1)}, u32[]{:S(2)}, u32[]{:S(2)}) collective-permute-start(bf16[1,128,128]{2,1,0:T(8,128)(2,1)S(1)} %fusion.refs_0_), channel_id=1, source_target_pairs={{0,3},{1,2},{2,1},{3,0},{4,7},{5,6},{6,5},{7,4},{8,11},{9,10},{10,... | collective-permute-start | bytes 98312 | tf_op jit(solution)/shard_map/ppermute | solution.py:40
  6.8 3.5 %collective-permute-start = (bf16[1,128,128]{2,1,0:T(8,128)(2,1)S(1)}, bf16[1,128,128]{2,1,0:T(8,128)(2,1)S(1)}, u32[]{:S(2)}, u32[]{:S(2)}) collective-permute-start(bf16[1,128,128]{2,1,0:T(8,128)(2,1)S(1)} %fusion.refs_0_), channel_id=1, source_target_pairs={{0,1},{1,0},{2,3},{3,2},{4,5},{5,4},{6,7},{7,6},{8,9},{9,8},{10,11... | collective-permute-start | bytes 98312 | tf_op jit(solution)/shard_map/ppermute | solution.py:40
  6.8 2.2 %copy-start = (bf16[256,8,1024]{2,1,0:T(8,128)(2,1)S(1)}, bf16[256,8,1024]{2,1,0:T(8,128)(2,1)}, u32[]{:S(2)}) copy-start(bf16[256,8,1024]{2,1,0:T(8,128)(2,1)} %param.6) | copy-start | bytes 12582916
  9.4 1.7 %copy-start.1 = (f32[16,8,128]{2,1,0:T(8,128)S(1)}, f32[16,8,128]{2,1,0:T(8,128)}, u32[]{:S(2)}) copy-start(f32[16,8,128]{2,1,0:T(8,128)} %param.4) | copy-start | bytes 196612
  10.4 1.8 %collective-permute-start.4 = (bf16[3,128,128]{2,1,0:T(8,128)(2,1)S(1)}, bf16[3,128,128]{2,1,0:T(8,128)(2,1)S(1)}, u32[]{:S(2)}, u32[]{:S(2)}) collective-permute-start(bf16[3,128,128]{2,1,0:T(8,128)(2,1)S(1)} %join.2.bundle_ref.refs_0_), channel_id=1, source_target_pairs={{0,1},{1,0},{2,3},{3,2},{4,5},{5,4},{6,7},{7,6},{8,9},{9,8},{10,11... | collective-permute-start | bytes 294920 | tf_op jit(solution)/shard_map/ppermute | solution.py:40
  11.5 8.4 %copy-start.3 = (f32[256]{0:T(256)S(1)}, f32[256]{0:T(256)}, u32[]{:S(2)}) copy-start(f32[256]{0:T(256)} %param.7) | copy-start | bytes 3076
  13.1 6.8 %collective-permute-start.6 = (bf16[192,128]{1,0:T(8,128)(2,1)S(1)}, bf16[192,128]{1,0:T(8,128)(2,1)S(1)}, u32[]{:S(2)}, u32[]{:S(2)}) collective-permute-start(bf16[192,128]{1,0:T(8,128)(2,1)S(1)} %get-tuple-element.32), channel_id=1, source_target_pairs={{0,24},{8,16},{16,8},{24,0},{1,25},{9,17},{17,9},{25,1},{2,26},{10... | collective-permute-start | bytes 147464 | tf_op jit(solution)/shard_map/ppermute | solution.py:40
  15.6 4.3 %collective-permute-start.5 = (bf16[192,128]{1,0:T(8,128)(2,1)S(1)}, bf16[192,128]{1,0:T(8,128)(2,1)S(1)}, u32[]{:S(2)}, u32[]{:S(2)}) collective-permute-start(bf16[192,128]{1,0:T(8,128)(2,1)S(1)} %get-tuple-element.32), channel_id=1, source_target_pairs={{0,8},{8,0},{16,24},{24,16},{1,9},{9,1},{17,25},{25,17},{2,10},{10... | collective-permute-start | bytes 147464 | tf_op jit(solution)/shard_map/ppermute | solution.py:40
  16.1 3.7 %collective-permute-start.7 = (bf16[64,128]{1,0:T(8,128)(2,1)S(1)}, bf16[64,128]{1,0:T(8,128)(2,1)S(1)}, u32[]{:S(2)}, u32[]{:S(2)}) collective-permute-start(bf16[64,128]{1,0:T(8,128)(2,1)S(1)} %get-tuple-element.33.refs_0_), channel_id=1, source_target_pairs={{0,16},{8,24},{16,0},{24,8},{1,17},{9,25},{17,1},{25,9},{2,18},{10... | collective-permute-start | bytes 49160 | tf_op jit(solution)/shard_map/ppermute | solution.py:40
  20.6 1.4 %collective-permute-start.8 = (bf16[2,128,128]{2,1,0:T(8,128)(2,1)S(1)}, bf16[2,128,128]{2,1,0:T(8,128)(2,1)S(1)}, u32[]{:S(2)}, u32[]{:S(2)}) collective-permute-start(bf16[2,128,128]{2,1,0:T(8,128)(2,1)S(1)} %get-tuple-element.36), channel_id=1, source_target_pairs={{0,1},{1,0},{2,3},{3,2},{4,5},{5,4},{6,7},{7,6},{8,9},{9,8},{10,11... | collective-permute-start | bytes 196616 | tf_op jit(solution)/shard_map/ppermute | solution.py:40
  20.7 5.2 %copy-start.2 = (f32[8,128]{1,0:T(8,128)S(1)}, f32[8,128]{1,0:T(8,128)}, u32[]{:S(2)}) copy-start(f32[8,128]{1,0:T(8,128)} %amp_ref.3) | copy-start | bytes 12292
  21.5 4.2 %collective-permute-start.9 = (bf16[2,128,128]{2,1,0:T(8,128)(2,1)S(1)}, bf16[2,128,128]{2,1,0:T(8,128)(2,1)S(1)}, u32[]{:S(2)}, u32[]{:S(2)}) collective-permute-start(bf16[2,128,128]{2,1,0:T(8,128)(2,1)S(1)} %get-tuple-element.39), channel_id=1, source_target_pairs={{0,1},{1,0},{2,3},{3,2},{4,5},{5,4},{6,7},{7,6},{8,9},{9,8},{10,11... | collective-permute-start | bytes 196616 | tf_op jit(solution)/shard_map/ppermute | solution.py:40
  22.1 4.5 %collective-permute-start.10 = (bf16[1,128,128]{2,1,0:T(8,128)(2,1)S(1)}, bf16[1,128,128]{2,1,0:T(8,128)(2,1)S(1)}, u32[]{:S(2)}, u32[]{:S(2)}) collective-permute-start(bf16[1,128,128]{2,1,0:T(8,128)(2,1)S(1)} %get-tuple-element.37.refs_0_), channel_id=1, source_target_pairs={{0,5},{1,4},{2,7},{3,6},{4,1},{5,0},{6,3},{7,2},{8,13},{9,12},{10,... | collective-permute-start | bytes 98312 | tf_op jit(solution)/shard_map/ppermute | solution.py:40
  23.8 5.1 %collective-permute-start.11 = (bf16[1,128,128]{2,1,0:T(8,128)(2,1)S(1)}, bf16[1,128,128]{2,1,0:T(8,128)(2,1)S(1)}, u32[]{:S(2)}, u32[]{:S(2)}) collective-permute-start(bf16[1,128,128]{2,1,0:T(8,128)(2,1)S(1)} %get-tuple-element.38.refs_1_), channel_id=1, source_target_pairs={{0,7},{1,6},{2,5},{3,4},{4,3},{5,2},{6,1},{7,0},{8,15},{9,14},{10,... | collective-permute-start | bytes 98312 | tf_op jit(solution)/shard_map/ppermute | solution.py:40
  25.8 4.2 %collective-permute-start.12 = (bf16[1,128,128]{2,1,0:T(8,128)(2,1)S(1)}, bf16[1,128,128]{2,1,0:T(8,128)(2,1)S(1)}, u32[]{:S(2)}, u32[]{:S(2)}) collective-permute-start(bf16[1,128,128]{2,1,0:T(8,128)(2,1)S(1)} %get-tuple-element.41), channel_id=1, source_target_pairs={{0,3},{1,2},{2,1},{3,0},{4,7},{5,6},{6,5},{7,4},{8,11},{9,10},{10,... | collective-permute-start | bytes 98312 | tf_op jit(solution)/shard_map/ppermute | solution.py:40
  30.0 4.4 %collective-permute-start.16 = (bf16[1,128,128]{2,1,0:T(8,128)(2,1)S(1)}, bf16[1,128,128]{2,1,0:T(8,128)(2,1)S(1)}, u32[]{:S(2)}, u32[]{:S(2)}) collective-permute-start(bf16[1,128,128]{2,1,0:T(8,128)(2,1)S(1)} %get-tuple-element.43.refs_0_), channel_id=1, source_target_pairs={{0,5},{1,4},{2,7},{3,6},{4,1},{5,0},{6,3},{7,2},{8,13},{9,12},{10,... | collective-permute-start | bytes 98312 | tf_op jit(solution)/shard_map/ppermute | solution.py:40
  30.3 5.2 %collective-permute-start.15 = (bf16[1,128,128]{2,1,0:T(8,128)(2,1)S(1)}, bf16[1,128,128]{2,1,0:T(8,128)(2,1)S(1)}, u32[]{:S(2)}, u32[]{:S(2)}) collective-permute-start(bf16[1,128,128]{2,1,0:T(8,128)(2,1)S(1)} %get-tuple-element.43.refs_0_), channel_id=1, source_target_pairs={{0,7},{1,6},{2,5},{3,4},{4,3},{5,2},{6,1},{7,0},{8,15},{9,14},{10,... | collective-permute-start | bytes 98312 | tf_op jit(solution)/shard_map/ppermute | solution.py:40
  31.8 3.8 %collective-permute-start.14 = (bf16[1,128,128]{2,1,0:T(8,128)(2,1)S(1)}, bf16[1,128,128]{2,1,0:T(8,128)(2,1)S(1)}, u32[]{:S(2)}, u32[]{:S(2)}) collective-permute-start(bf16[1,128,128]{2,1,0:T(8,128)(2,1)S(1)} %get-tuple-element.43.refs_0_), channel_id=1, source_target_pairs={{0,3},{1,2},{2,1},{3,0},{4,7},{5,6},{6,5},{7,4},{8,11},{9,10},{10,... | collective-permute-start | bytes 98312 | tf_op jit(solution)/shard_map/ppermute | solution.py:40
  33.0 2.6 %collective-permute-start.13 = (bf16[1,128,128]{2,1,0:T(8,128)(2,1)S(1)}, bf16[1,128,128]{2,1,0:T(8,128)(2,1)S(1)}, u32[]{:S(2)}, u32[]{:S(2)}) collective-permute-start(bf16[1,128,128]{2,1,0:T(8,128)(2,1)S(1)} %get-tuple-element.43.refs_0_), channel_id=1, source_target_pairs={{0,1},{1,0},{2,3},{3,2},{4,5},{5,4},{6,7},{7,6},{8,9},{9,8},{10,11... | collective-permute-start | bytes 98312 | tf_op jit(solution)/shard_map/ppermute | solution.py:40
  35.5 1.6 %collective-permute-start.17 = (bf16[3,128,128]{2,1,0:T(8,128)(2,1)S(1)}, bf16[3,128,128]{2,1,0:T(8,128)(2,1)S(1)}, u32[]{:S(2)}, u32[]{:S(2)}) collective-permute-start(bf16[3,128,128]{2,1,0:T(8,128)(2,1)S(1)} %join.3.bundle_ref.refs_0_), channel_id=1, source_target_pairs={{0,1},{1,0},{2,3},{3,2},{4,5},{5,4},{6,7},{7,6},{8,9},{9,8},{10,11... | collective-permute-start | bytes 294920 | tf_op jit(solution)/shard_map/ppermute | solution.py:40
  38.1 5.7 %collective-permute-start.19 = (bf16[192,128]{1,0:T(8,128)(2,1)S(1)}, bf16[192,128]{1,0:T(8,128)(2,1)S(1)}, u32[]{:S(2)}, u32[]{:S(2)}) collective-permute-start(bf16[192,128]{1,0:T(8,128)(2,1)S(1)} %get-tuple-element.46), channel_id=1, source_target_pairs={{0,24},{8,16},{16,8},{24,0},{1,25},{9,17},{17,9},{25,1},{2,26},{10... | collective-permute-start | bytes 147464 | tf_op jit(solution)/shard_map/ppermute | solution.py:40
  39.5 4.3 %collective-permute-start.18 = (bf16[192,128]{1,0:T(8,128)(2,1)S(1)}, bf16[192,128]{1,0:T(8,128)(2,1)S(1)}, u32[]{:S(2)}, u32[]{:S(2)}) collective-permute-start(bf16[192,128]{1,0:T(8,128)(2,1)S(1)} %get-tuple-element.46), channel_id=1, source_target_pairs={{0,8},{8,0},{16,24},{24,16},{1,9},{9,1},{17,25},{25,17},{2,10},{10... | collective-permute-start | bytes 147464 | tf_op jit(solution)/shard_map/ppermute | solution.py:40
  40.1 3.7 %collective-permute-start.20 = (bf16[64,128]{1,0:T(8,128)(2,1)S(1)}, bf16[64,128]{1,0:T(8,128)(2,1)S(1)}, u32[]{:S(2)}, u32[]{:S(2)}) collective-permute-start(bf16[64,128]{1,0:T(8,128)(2,1)S(1)} %get-tuple-element.47.refs_0_), channel_id=1, source_target_pairs={{0,16},{8,24},{16,0},{24,8},{1,17},{9,25},{17,1},{25,9},{2,18},{10... | collective-permute-start | bytes 49160 | tf_op jit(solution)/shard_map/ppermute | solution.py:40
  44.5 1.4 %collective-permute-start.21 = (bf16[2,128,128]{2,1,0:T(8,128)(2,1)S(1)}, bf16[2,128,128]{2,1,0:T(8,128)(2,1)S(1)}, u32[]{:S(2)}, u32[]{:S(2)}) collective-permute-start(bf16[2,128,128]{2,1,0:T(8,128)(2,1)S(1)} %get-tuple-element.50), channel_id=1, source_target_pairs={{0,1},{1,0},{2,3},{3,2},{4,5},{5,4},{6,7},{7,6},{8,9},{9,8},{10,11... | collective-permute-start | bytes 196616 | tf_op jit(solution)/shard_map/ppermute | solution.py:40
  45.4 3.2 %collective-permute-start.22 = (bf16[2,128,128]{2,1,0:T(8,128)(2,1)S(1)}, bf16[2,128,128]{2,1,0:T(8,128)(2,1)S(1)}, u32[]{:S(2)}, u32[]{:S(2)}) collective-permute-start(bf16[2,128,128]{2,1,0:T(8,128)(2,1)S(1)} %get-tuple-element.53), channel_id=1, source_target_pairs={{0,1},{1,0},{2,3},{3,2},{4,5},{5,4},{6,7},{7,6},{8,9},{9,8},{10,11... | collective-permute-start | bytes 196616 | tf_op jit(solution)/shard_map/ppermute | solution.py:40
  46.0 5.3 %collective-permute-start.23 = (bf16[1,128,128]{2,1,0:T(8,128)(2,1)S(1)}, bf16[1,128,128]{2,1,0:T(8,128)(2,1)S(1)}, u32[]{:S(2)}, u32[]{:S(2)}) collective-permute-start(bf16[1,128,128]{2,1,0:T(8,128)(2,1)S(1)} %get-tuple-element.51.refs_0_), channel_id=1, source_target_pairs={{0,7},{1,6},{2,5},{3,4},{4,3},{5,2},{6,1},{7,0},{8,15},{9,14},{10,... | collective-permute-start | bytes 98312 | tf_op jit(solution)/shard_map/ppermute | solution.py:40
  48.1 4.5 %collective-permute-start.24 = (bf16[1,128,128]{2,1,0:T(8,128)(2,1)S(1)}, bf16[1,128,128]{2,1,0:T(8,128)(2,1)S(1)}, u32[]{:S(2)}, u32[]{:S(2)}) collective-permute-start(bf16[1,128,128]{2,1,0:T(8,128)(2,1)S(1)} %get-tuple-element.52.refs_1_), channel_id=1, source_target_pairs={{0,5},{1,4},{2,7},{3,6},{4,1},{5,0},{6,3},{7,2},{8,13},{9,12},{10,... | collective-permute-start | bytes 98312 | tf_op jit(solution)/shard_map/ppermute | solution.py:40
  48.7 4.0 %collective-permute-start.25 = (bf16[1,128,128]{2,1,0:T(8,128)(2,1)S(1)}, bf16[1,128,128]{2,1,0:T(8,128)(2,1)S(1)}, u32[]{:S(2)}, u32[]{:S(2)}) collective-permute-start(bf16[1,128,128]{2,1,0:T(8,128)(2,1)S(1)} %get-tuple-element.55), channel_id=1, source_target_pairs={{0,3},{1,2},{2,1},{3,0},{4,7},{5,6},{6,5},{7,4},{8,11},{9,10},{10,... | collective-permute-start | bytes 98312 | tf_op jit(solution)/shard_map/ppermute | solution.py:40

commit v12 on v11

--- a/solution.py
+++ b/solution.py
@@ -145,16 +145,20 @@
         lax.broadcasted_iota(jnp.int32, (cols, lines), 1) // rows
         == lax.broadcasted_iota(jnp.int32, (cols, lines), 0)
     ).astype(jnp.bfloat16)
+    value = total[...]
+    upper = value.astype(jnp.bfloat16)
+    lower = (value - upper.astype(jnp.float32)).astype(jnp.bfloat16)
+    both = lax.dot_general(
+        pick,
+        jnp.concatenate([upper, lower], axis=0),
+        (((1,), (1,)), ((), ())),
+        preferred_element_type=jnp.float32,
+    )
+    proj = both[:, : total.shape[0]] + both[:, total.shape[0] :]
     for at in range(0, total.shape[0], LANES):
-        part = total[at : at + LANES, :]
-        upper = part.astype(jnp.bfloat16)
-        lower = (part - upper.astype(jnp.float32)).astype(jnp.bfloat16)
-        dims = (((1,), (1,)), ((), ()))
-        proj = lax.dot_general(pick, upper, dims, preferred_element_type=jnp.float32)
-        proj = proj + lax.dot_general(pick, lower, dims, preferred_element_type=jnp.float32)
+        upper = proj[:, at : at + LANES].astype(jnp.bfloat16)
+        lower = (proj[:, at : at + LANES] - upper.astype(jnp.float32)).astype(jnp.bfloat16)
         first = at // LANES * 2 * cols
-        upper = proj.astype(jnp.bfloat16)
-        lower = (proj - upper.astype(jnp.float32)).astype(jnp.bfloat16)
         for ref in (pay_ref, part_ref):
             ref[first : first + cols, :] = upper
             ref[first + cols : first + 2 * cols, :] = lower
@@ -187,6 +191,7 @@
         lax.rem(lax.broadcasted_iota(jnp.int32, (lines, LANES), 1), rows)
         == lax.rem(lax.broadcasted_iota(jnp.int32, (lines, LANES), 0), rows)
     ).astype(jnp.float32)
+    turned = []
     for at in range(0, ranks, LANES):
         count = min(LANES, ranks - at)
         first = at // LANES * 2 * cols
@@ -199,16 +204,13 @@
         if count < LANES:
             weights = jnp.concatenate([weights, jnp.zeros((1, LANES - count), jnp.float32)], axis=1)
         c = proj * weights
-        turned = [c if n == 0 else pltpu.roll(c, LANES - n * span, 1) for n in range(rows)]
-        stacked = jnp.concatenate(turned, axis=0).astype(jnp.bfloat16)
-        wide = jnp.dot(stacked, spread, preferred_element_type=jnp.float32)
-        for n in range(rows):
-            start = (at + n * span) * rows
-            if start >= ranks * rows:
-                break
-            piece = wide[n * cols : (n + 1) * cols, :]
-            piece = jnp.broadcast_to(piece[:, None, :], (cols, rows, LANES)).reshape(lines, LANES)
-            coef_ref[:, start : start + LANES] = (piece * same).astype(jnp.bfloat16)
+        turned += [c if n == 0 else pltpu.roll(c, LANES - n * span, 1) for n in range(rows)]
+    stacked = jnp.concatenate(turned, axis=0).astype(jnp.bfloat16)
+    wide = jnp.dot(stacked, spread, preferred_element_type=jnp.float32)
+    for n in range(ranks * rows // LANES):
+        piece = wide[n * cols : (n + 1) * cols, :]
+        piece = jnp.broadcast_to(piece[:, None, :], (cols, rows, LANES)).reshape(lines, LANES)
+        coef_ref[:, n * LANES : (n + 1) * LANES] = (piece * same).astype(jnp.bfloat16)
     product(coef_ref[...], spots, factor_ref, out_ref)
 
 

time: 53.6 us -> 53.5 us (level)
  no operation moved by 1% of the time
where the time goes in v12:
time: 53.5 us; the launch traced here: 53.2 us
  starting transfers between devices  25.3 us (47%)
  waiting for transfers between devices  13.7 us (26%)
  Pallas kernels  10.3 us (19%)
  local copies, waits for them, and re-layouts  2.21 us (4%)
  between operations  0.87 us (2%)
  other arithmetic  0.85 us (2%)
    ppermute x26, starting transfers between devices, swap(): lax.ppermute(value, axis, [(i, i ^ mask) for i in range(lax.axis_size(axi...  25.3 us
    ppermute x26, waiting for transfers between devices, swap(): lax.ppermute(value, axis, [(i, i ^ mask) for i in range(lax.axis_size(axi...  13.7 us
    pallas_call x4, Pallas kernels, term(): call(partial(term_kernel, wanted, len(after)), in_specs=[pl.BlockSpec(mem...  2.59 us
    pallas_call x4, Pallas kernels, first(): call(partial(first_kernel, rows, spots, len(before)), shape(f32, blocks *...  2.37 us
    unnamed x8, local copies, waits for them, and re-layouts  2.21 us
    pallas_call x2, Pallas kernels, on_device(): call(partial(second_kernel, rows, cols, spots), (shape(bf16, pay_rows, wi...  1.63 us
    pallas_call x2, Pallas kernels, on_device(): call(partial(far_kernel, rows, cols, groups, ncells_all, spots_of(away, T...  1.48 us
  transfers between devices with their start and end apart: 26, of which 11 were waited for; matrix products, arithmetic and copies ran while one was open for 0% of the time, Pallas kernels for 12%

profile of v12, /device:TPU:0, one launch (start us, length us, event | category | flops | bytes accessed | tf_op | source)
XLA Modules:
  0.0 53.2 jit_solution(14062833695463654121)
XLA Ops:
  0.6 0.8 %fusion.refs_0_ = bf16[1,128,128]{2,1,0:T(8,128)(2,1)S(1)} fusion(f32[16,8,128]{2,1,0:T(8,128)} %param.4), kind=kLoop, calls=%fused_computation.1 | loop fusion | flops 32768 | bytes 98304 | tf_op jit(solution)/shard_map/convert_element_type | solution.py:279
  1.5 3.5 %collective-permute-start.3 = (bf16[1,128,128]{2,1,0:T(8,128)(2,1)S(1)}, bf16[1,128,128]{2,1,0:T(8,128)(2,1)S(1)}, u32[]{:S(2)}, u32[]{:S(2)}) collective-permute-start(bf16[1,128,128]{2,1,0:T(8,128)(2,1)S(1)} %fusion.refs_0_), channel_id=1, source_target_pairs={{0,5},{1,4},{2,7},{3,6},{4,1},{5,0},{6,3},{7,2},{8,13},{9,12},{10,... | collective-permute-start | bytes 98312 | tf_op jit(solution)/shard_map/ppermute | solution.py:40
  5.0 1.6 %collective-permute-start.2 = (bf16[1,128,128]{2,1,0:T(8,128)(2,1)S(1)}, bf16[1,128,128]{2,1,0:T(8,128)(2,1)S(1)}, u32[]{:S(2)}, u32[]{:S(2)}) collective-permute-start(bf16[1,128,128]{2,1,0:T(8,128)(2,1)S(1)} %fusion.refs_0_), channel_id=1, source_target_pairs={{0,7},{1,6},{2,5},{3,4},{4,3},{5,2},{6,1},{7,0},{8,15},{9,14},{10,... | collective-permute-start | bytes 98312 | tf_op jit(solution)/shard_map/ppermute | solution.py:40
  6.6 0.2 collective-permute-start.1
  6.8 0.0 collective-permute-start
  6.8 2.2 %copy-done = bf16[256,8,1024]{2,1,0:T(8,128)(2,1)S(1)} copy-done((bf16[256,8,1024]{2,1,0:T(8,128)(2,1)S(1)}, bf16[256,8,1024]{2,1,0:T(8,128)(2,1)}, u32[]{:S(2)}) %copy-start) | copy-done | bytes 4194328
  9.0 0.4 load.1.factor_ref
  9.4 0.0 copy-start.1
  9.4 0.5 project_own.4.refs_0_.refs_2_
  9.9 0.0 collective-permute-done.3.refs_4_
  9.9 0.3 collective-permute-done.2.refs_3_
  10.2 0.2 collective-permute-done.1.refs_2_
  10.4 0.7 %collective-permute-start.4 = (bf16[3,128,128]{2,1,0:T(8,128)(2,1)S(1)}, bf16[3,128,128]{2,1,0:T(8,128)(2,1)S(1)}, u32[]{:S(2)}, u32[]{:S(2)}) collective-permute-start(bf16[3,128,128]{2,1,0:T(8,128)(2,1)S(1)} %join.2.bundle_ref.refs_0_), channel_id=1, source_target_pairs={{0,1},{1,0},{2,3},{3,2},{4,5},{5,4},{6,7},{7,6},{8,9},{9,8},{10,11... | collective-permute-start | bytes 294920 | tf_op jit(solution)/shard_map/ppermute | solution.py:40
  11.1 0.4 columns.2
  11.5 0.0 copy-start.3
  11.5 0.7 %project_own.5.diag_ref = f32[256,128]{1,0:T(8,128)S(1)} custom-call(bf16[2048,1024]{1,0:T(8,128)(2,1)S(1)} %load.1.factor_ref, bf16[3,128,128]{2,1,0:T(8,128)(2,1)S(1)} %join.2.bundle_ref.refs_0_, bf16[1,128,128]{2,1,0:T(8,128)(2,1)S(1)} %collective-permute-done.refs_1_.twin_ref, f32[256,128]{1,0:T(8,128)S(1)} %project_own.4.refs_0_.refs_2_), custom_call_target="tpu_custom_call" | custom-call | flops 268435456 | bytes 2097152 | tf_op jit(solution)/shard_map/project_own/pallas_call | solution.py:316
  12.2 0.0 collective-permute-done.4.fields_ref
  12.2 0.8 %project_across.2 = (bf16[192,128]{1,0:T(8,128)(2,1)S(1)}, bf16[64,128]{1,0:T(8,128)(2,1)S(1)}) custom-call(bf16[2048,1024]{1,0:T(8,128)(2,1)S(1)} %load.1.factor_ref, f32[256,128]{1,0:T(8,128)S(1)} %project_own.5.diag_ref, bf16[3,128,128]{2,1,0:T(8,128)(2,1)S(1)} %collective-permute-done.4.fields_ref, bf16[128,128]{1,0:T(8,128)(2,1)S(1)} %get-tuple-element.31.short_ref), custom_call_target="tpu_custom_call" | custom-call | flops 268435456 | bytes 2097152 | tf_op jit(solution)/shard_map/project_across/pallas_call | solution.py:349
  13.0 2.5 %collective-permute-start.6 = (bf16[192,128]{1,0:T(8,128)(2,1)S(1)}, bf16[192,128]{1,0:T(8,128)(2,1)S(1)}, u32[]{:S(2)}, u32[]{:S(2)}) collective-permute-start(bf16[192,128]{1,0:T(8,128)(2,1)S(1)} %get-tuple-element.32), channel_id=1, source_target_pairs={{0,24},{8,16},{16,8},{24,0},{1,25},{9,17},{17,9},{25,1},{2,26},{10... | collective-permute-start | bytes 147464 | tf_op jit(solution)/shard_map/ppermute | solution.py:40
  15.5 0.5 %collective-permute-start.5 = (bf16[192,128]{1,0:T(8,128)(2,1)S(1)}, bf16[192,128]{1,0:T(8,128)(2,1)S(1)}, u32[]{:S(2)}, u32[]{:S(2)}) collective-permute-start(bf16[192,128]{1,0:T(8,128)(2,1)S(1)} %get-tuple-element.32), channel_id=1, source_target_pairs={{0,8},{8,0},{16,24},{24,16},{1,9},{9,1},{17,25},{25,17},{2,10},{10... | collective-permute-start | bytes 147464 | tf_op jit(solution)/shard_map/ppermute | solution.py:40
  16.1 0.5 collective-permute-start.7
  16.6 3.2 %collective-permute-done.7.refs_2_ = bf16[64,128]{1,0:T(8,128)(2,1)S(1)} collective-permute-done((bf16[64,128]{1,0:T(8,128)(2,1)S(1)}, bf16[64,128]{1,0:T(8,128)(2,1)S(1)}, u32[]{:S(2)}, u32[]{:S(2)}) %collective-permute-start.7) | collective-permute-done | bytes 16416 | tf_op jit(solution)/shard_map/ppermute | solution.py:40
  19.8 0.0 collective-permute-done.6.refs_1_.refs_3_
  19.8 0.0 collective-permute-done.5.refs_0_.refs_1_
  19.8 0.7 %term_first.2 = (bf16[128,2048]{1,0:T(8,128)(2,1)S(1)}, bf16[2,128,128]{2,1,0:T(8,128)(2,1)S(1)}) custom-call(f32[1,256]{1,0:T(1,128)S(1)} %bitcast.13, bf16[2048,1024]{1,0:T(8,128)(2,1)S(1)} %load.1.factor_ref, bf16[64,128]{1,0:T(8,128)(2,1)S(1)} %get-tuple-element.33.refs_0_, bf16[192,128]{1,0:T(8,128)(2,1)S(1)} %collective-permute-done.5.refs_0_.refs_1_, ...), custom_call_target="tpu_custom_call" | custom-call | flops 134217728 | bytes 2097152 | tf_op jit(solution)/shard_map/term_first/pallas_call | solution.py:358
  20.5 0.1 collective-permute-start.8
  20.6 0.0 copy-start.2
  20.6 0.8 %term.4 = (f32[2,128,128]{2,1,0:T(8,128)S(1)}, bf16[2,128,128]{2,1,0:T(8,128)(2,1)S(1)}) custom-call(bf16[128,2048]{1,0:T(8,128)(2,1)S(1)} %get-tuple-element.34.coef_ref, bf16[2048,1024]{1,0:T(8,128)(2,1)S(1)} %load.1.factor_ref), custom_call_target="tpu_custom_call" | custom-call | flops 268435456 | bytes 2097152 | tf_op jit(solution)/shard_map/term/pallas_call | solution.py:368
  21.4 0.5 %collective-permute-start.9 = (bf16[2,128,128]{2,1,0:T(8,128)(2,1)S(1)}, bf16[2,128,128]{2,1,0:T(8,128)(2,1)S(1)}, u32[]{:S(2)}, u32[]{:S(2)}) collective-permute-start(bf16[2,128,128]{2,1,0:T(8,128)(2,1)S(1)} %get-tuple-element.39), channel_id=1, source_target_pairs={{0,1},{1,0},{2,3},{3,2},{4,5},{5,4},{6,7},{7,6},{8,9},{9,8},{10,11... | collective-permute-start | bytes 196616 | tf_op jit(solution)/shard_map/ppermute | solution.py:40
  22.0 1.8 %collective-permute-start.10 = (bf16[1,128,128]{2,1,0:T(8,128)(2,1)S(1)}, bf16[1,128,128]{2,1,0:T(8,128)(2,1)S(1)}, u32[]{:S(2)}, u32[]{:S(2)}) collective-permute-start(bf16[1,128,128]{2,1,0:T(8,128)(2,1)S(1)} %get-tuple-element.37.refs_0_), channel_id=1, source_target_pairs={{0,5},{1,4},{2,7},{3,6},{4,1},{5,0},{6,3},{7,2},{8,13},{9,12},{10,... | collective-permute-start | bytes 98312 | tf_op jit(solution)/shard_map/ppermute | solution.py:40
  23.8 1.4 %collective-permute-start.11 = (bf16[1,128,128]{2,1,0:T(8,128)(2,1)S(1)}, bf16[1,128,128]{2,1,0:T(8,128)(2,1)S(1)}, u32[]{:S(2)}, u32[]{:S(2)}) collective-permute-start(bf16[1,128,128]{2,1,0:T(8,128)(2,1)S(1)} %get-tuple-element.38.refs_1_), channel_id=1, source_target_pairs={{0,7},{1,6},{2,5},{3,4},{4,3},{5,2},{6,1},{7,0},{8,15},{9,14},{10,... | collective-permute-start | bytes 98312 | tf_op jit(solution)/shard_map/ppermute | solution.py:40
  25.2 0.5 term.5.mine_ref
  25.7 0.0 collective-permute-done.9.got_ref
  25.7 0.1 collective-permute-start.12
  25.8 0.2 local.2.base_ref
  26.0 0.5 collective-permute-done.10.refs_1_
  26.5 2.4 %collective-permute-done.11.refs_2_ = bf16[1,128,128]{2,1,0:T(8,128)(2,1)S(1)} collective-permute-done((bf16[1,128,128]{2,1,0:T(8,128)(2,1)S(1)}, bf16[1,128,128]{2,1,0:T(8,128)(2,1)S(1)}, u32[]{:S(2)}, u32[]{:S(2)}) %collective-permute-start.11) | collective-permute-done | bytes 32800 | tf_op jit(solution)/shard_map/ppermute | solution.py:40
  28.9 1.0 %collective-permute-done.12.refs_3_ = bf16[1,128,128]{2,1,0:T(8,128)(2,1)S(1)} collective-permute-done((bf16[1,128,128]{2,1,0:T(8,128)(2,1)S(1)}, bf16[1,128,128]{2,1,0:T(8,128)(2,1)S(1)}, u32[]{:S(2)}, u32[]{:S(2)}) %collective-permute-start.12) | collective-permute-done | bytes 32800 | tf_op jit(solution)/shard_map/ppermute | solution.py:40
  29.9 0.4 collective-permute-start.16
  30.3 1.4 %collective-permute-start.15 = (bf16[1,128,128]{2,1,0:T(8,128)(2,1)S(1)}, bf16[1,128,128]{2,1,0:T(8,128)(2,1)S(1)}, u32[]{:S(2)}, u32[]{:S(2)}) collective-permute-start(bf16[1,128,128]{2,1,0:T(8,128)(2,1)S(1)} %get-tuple-element.43.refs_0_), channel_id=1, source_target_pairs={{0,7},{1,6},{2,5},{3,4},{4,3},{5,2},{6,1},{7,0},{8,15},{9,14},{10,... | collective-permute-start | bytes 98312 | tf_op jit(solution)/shard_map/ppermute | solution.py:40
  31.7 1.2 %collective-permute-start.14 = (bf16[1,128,128]{2,1,0:T(8,128)(2,1)S(1)}, bf16[1,128,128]{2,1,0:T(8,128)(2,1)S(1)}, u32[]{:S(2)}, u32[]{:S(2)}) collective-permute-start(bf16[1,128,128]{2,1,0:T(8,128)(2,1)S(1)} %get-tuple-element.43.refs_0_), channel_id=1, source_target_pairs={{0,3},{1,2},{2,1},{3,0},{4,7},{5,6},{6,5},{7,4},{8,11},{9,10},{10,... | collective-permute-start | bytes 98312 | tf_op jit(solution)/shard_map/ppermute | solution.py:40
  32.9 0.4 collective-permute-start.13
  33.3 0.5 project_own.6.refs_0_.refs_2_
  33.8 0.5 collective-permute-done.16.refs_4_
  34.3 1.3 %collective-permute-done.15.refs_3_ = bf16[1,128,128]{2,1,0:T(8,128)(2,1)S(1)} collective-permute-done((bf16[1,128,128]{2,1,0:T(8,128)(2,1)S(1)}, bf16[1,128,128]{2,1,0:T(8,128)(2,1)S(1)}, u32[]{:S(2)}, u32[]{:S(2)}) %collective-permute-start.15) | collective-permute-done | bytes 32800 | tf_op jit(solution)/shard_map/ppermute | solution.py:40
  35.6 0.5 collective-permute-start.17
  36.0 0.3 columns.3
  36.4 0.7 %project_own.7.diag_ref = f32[256,128]{1,0:T(8,128)S(1)} custom-call(bf16[2048,1024]{1,0:T(8,128)(2,1)S(1)} %load.1.factor_ref, bf16[3,128,128]{2,1,0:T(8,128)(2,1)S(1)} %join.3.bundle_ref.refs_0_, bf16[1,128,128]{2,1,0:T(8,128)(2,1)S(1)} %collective-permute-done.13.refs_1_.twin_ref, f32[256,128]{1,0:T(8,128)S(1)} %project_own.6.refs_0_.refs_2_), custom_call_target="tpu_custom_call" | custom-call | flops 268435456 | bytes 2097152 | tf_op jit(solution)/shard_map/project_own/pallas_call | solution.py:316
  37.1 0.8 %project_across.3 = (bf16[192,128]{1,0:T(8,128)(2,1)S(1)}, bf16[64,128]{1,0:T(8,128)(2,1)S(1)}) custom-call(bf16[2048,1024]{1,0:T(8,128)(2,1)S(1)} %load.1.factor_ref, f32[256,128]{1,0:T(8,128)S(1)} %project_own.7.diag_ref, bf16[3,128,128]{2,1,0:T(8,128)(2,1)S(1)} %collective-permute-done.17.fields_ref, bf16[128,128]{1,0:T(8,128)(2,1)S(1)} %get-tuple-element.45.short_ref), custom_call_target="tpu_custom_call" | custom-call | flops 268435456 | bytes 2097152 | tf_op jit(solution)/shard_map/project_across/pallas_call | solution.py:349
  37.9 1.5 %collective-permute-start.19 = (bf16[192,128]{1,0:T(8,128)(2,1)S(1)}, bf16[192,128]{1,0:T(8,128)(2,1)S(1)}, u32[]{:S(2)}, u32[]{:S(2)}) collective-permute-start(bf16[192,128]{1,0:T(8,128)(2,1)S(1)} %get-tuple-element.46), channel_id=1, source_target_pairs={{0,24},{8,16},{16,8},{24,0},{1,25},{9,17},{17,9},{25,1},{2,26},{10... | collective-permute-start | bytes 147464 | tf_op jit(solution)/shard_map/ppermute | solution.py:40
  39.4 0.5 %collective-permute-start.18 = (bf16[192,128]{1,0:T(8,128)(2,1)S(1)}, bf16[192,128]{1,0:T(8,128)(2,1)S(1)}, u32[]{:S(2)}, u32[]{:S(2)}) collective-permute-start(bf16[192,128]{1,0:T(8,128)(2,1)S(1)} %get-tuple-element.46), channel_id=1, source_target_pairs={{0,8},{8,0},{16,24},{24,16},{1,9},{9,1},{17,25},{25,17},{2,10},{10... | collective-permute-start | bytes 147464 | tf_op jit(solution)/shard_map/ppermute | solution.py:40
  39.9 1.5 %collective-permute-start.20 = (bf16[64,128]{1,0:T(8,128)(2,1)S(1)}, bf16[64,128]{1,0:T(8,128)(2,1)S(1)}, u32[]{:S(2)}, u32[]{:S(2)}) collective-permute-start(bf16[64,128]{1,0:T(8,128)(2,1)S(1)} %get-tuple-element.47.refs_0_), channel_id=1, source_target_pairs={{0,16},{8,24},{16,0},{24,8},{1,17},{9,25},{17,1},{25,9},{2,18},{10... | collective-permute-start | bytes 49160 | tf_op jit(solution)/shard_map/ppermute | solution.py:40
  41.5 2.2 %collective-permute-done.20.refs_2_ = bf16[64,128]{1,0:T(8,128)(2,1)S(1)} collective-permute-done((bf16[64,128]{1,0:T(8,128)(2,1)S(1)}, bf16[64,128]{1,0:T(8,128)(2,1)S(1)}, u32[]{:S(2)}, u32[]{:S(2)}) %collective-permute-start.20) | collective-permute-done | bytes 16416 | tf_op jit(solution)/shard_map/ppermute | solution.py:40
  43.7 0.7 %term_first.3 = (bf16[128,2048]{1,0:T(8,128)(2,1)S(1)}, bf16[2,128,128]{2,1,0:T(8,128)(2,1)S(1)}) custom-call(f32[1,256]{1,0:T(1,128)S(1)} %bitcast.14, bf16[2048,1024]{1,0:T(8,128)(2,1)S(1)} %load.1.factor_ref, bf16[64,128]{1,0:T(8,128)(2,1)S(1)} %get-tuple-element.47.refs_0_, bf16[192,128]{1,0:T(8,128)(2,1)S(1)} %collective-permute-done.18.refs_0_.refs_1_, ...), custom_call_target="tpu_custom_call" | custom-call | flops 134217728 | bytes 2097152 | tf_op jit(solution)/shard_map/term_first/pallas_call | solution.py:358
  44.4 0.1 collective-permute-start.21
  44.5 0.8 %term.6 = (f32[2,128,128]{2,1,0:T(8,128)S(1)}, bf16[2,128,128]{2,1,0:T(8,128)(2,1)S(1)}) custom-call(bf16[128,2048]{1,0:T(8,128)(2,1)S(1)} %get-tuple-element.48.coef_ref, bf16[2048,1024]{1,0:T(8,128)(2,1)S(1)} %load.1.factor_ref), custom_call_target="tpu_custom_call" | custom-call | flops 268435456 | bytes 2097152 | tf_op jit(solution)/shard_map/term/pallas_call | solution.py:368
  45.3 0.6 %collective-permute-start.22 = (bf16[2,128,128]{2,1,0:T(8,128)(2,1)S(1)}, bf16[2,128,128]{2,1,0:T(8,128)(2,1)S(1)}, u32[]{:S(2)}, u32[]{:S(2)}) collective-permute-start(bf16[2,128,128]{2,1,0:T(8,128)(2,1)S(1)} %get-tuple-element.53), channel_id=1, source_target_pairs={{0,1},{1,0},{2,3},{3,2},{4,5},{5,4},{6,7},{7,6},{8,9},{9,8},{10,11... | collective-permute-start | bytes 196616 | tf_op jit(solution)/shard_map/ppermute | solution.py:40
  45.9 2.1 %collective-permute-start.23 = (bf16[1,128,128]{2,1,0:T(8,128)(2,1)S(1)}, bf16[1,128,128]{2,1,0:T(8,128)(2,1)S(1)}, u32[]{:S(2)}, u32[]{:S(2)}) collective-permute-start(bf16[1,128,128]{2,1,0:T(8,128)(2,1)S(1)} %get-tuple-element.51.refs_0_), channel_id=1, source_target_pairs={{0,7},{1,6},{2,5},{3,4},{4,3},{5,2},{6,1},{7,0},{8,15},{9,14},{10,... | collective-permute-start | bytes 98312 | tf_op jit(solution)/shard_map/ppermute | solution.py:40
  48.0 0.5 term.7.mine_ref
  48.6 1.7 %collective-permute-start.25 = (bf16[1,128,128]{2,1,0:T(8,128)(2,1)S(1)}, bf16[1,128,128]{2,1,0:T(8,128)(2,1)S(1)}, u32[]{:S(2)}, u32[]{:S(2)}) collective-permute-start(bf16[1,128,128]{2,1,0:T(8,128)(2,1)S(1)} %get-tuple-element.55), channel_id=1, source_target_pairs={{0,3},{1,2},{2,1},{3,0},{4,7},{5,6},{6,5},{7,4},{8,11},{9,10},{10,... | collective-permute-start | bytes 98312 | tf_op jit(solution)/shard_map/ppermute | solution.py:40
  50.3 0.2 local.3.base_ref
  50.5 0.8 %collective-permute-done.23.refs_1_ = bf16[1,128,128]{2,1,0:T(8,128)(2,1)S(1)} collective-permute-done((bf16[1,128,128]{2,1,0:T(8,128)(2,1)S(1)}, bf16[1,128,128]{2,1,0:T(8,128)(2,1)S(1)}, u32[]{:S(2)}, u32[]{:S(2)}) %collective-permute-start.23) | collective-permute-done | bytes 32800 | tf_op jit(solution)/shard_map/ppermute | solution.py:40
  51.2 1.3 %collective-permute-done.24.refs_2_ = bf16[1,128,128]{2,1,0:T(8,128)(2,1)S(1)} collective-permute-done((bf16[1,128,128]{2,1,0:T(8,128)(2,1)S(1)}, bf16[1,128,128]{2,1,0:T(8,128)(2,1)S(1)}, u32[]{:S(2)}, u32[]{:S(2)}) %collective-permute-start.24) | collective-permute-done | bytes 32800 | tf_op jit(solution)/shard_map/ppermute | solution.py:40
  52.5 0.7 %update.3 = (f32[128,128]{1,0:T(8,128)}, f32[128,128]{1,0:T(8,128)}) custom-call(f32[128,128]{1,0:T(8,128)S(1)} %get-tuple-element.42.x_ref, f32[128,128]{1,0:T(8,128)S(1)} %local.3.base_ref, f32[1,128,128]{2,1,0:T(8,128)S(1)} %get-tuple-element.54.refs_0_, bf16[1,128,128]{2,1,0:T(8,128)(2,1)S(1)} %collective-permute-done.23.refs_1_, ...), custom_call_target="tpu_custom_call" | custom-call | bytes 262144 | tf_op jit(solution)/shard_map/update/pallas_call | solution.py:396
  (22 shorter events, 0.1 us)
Async XLA Ops:
  1.5 8.4 %collective-permute-start.3 = (bf16[1,128,128]{2,1,0:T(8,128)(2,1)S(1)}, bf16[1,128,128]{2,1,0:T(8,128)(2,1)S(1)}, u32[]{:S(2)}, u32[]{:S(2)}) collective-permute-start(bf16[1,128,128]{2,1,0:T(8,128)(2,1)S(1)} %fusion.refs_0_), channel_id=1, source_target_pairs={{0,5},{1,4},{2,7},{3,6},{4,1},{5,0},{6,3},{7,2},{8,13},{9,12},{10,... | collective-permute-start | bytes 98312 | tf_op jit(solution)/shard_map/ppermute | solution.py:40
  5.0 5.2 %collective-permute-start.2 = (bf16[1,128,128]{2,1,0:T(8,128)(2,1)S(1)}, bf16[1,128,128]{2,1,0:T(8,128)(2,1)S(1)}, u32[]{:S(2)}, u32[]{:S(2)}) collective-permute-start(bf16[1,128,128]{2,1,0:T(8,128)(2,1)S(1)} %fusion.refs_0_), channel_id=1, source_target_pairs={{0,7},{1,6},{2,5},{3,4},{4,3},{5,2},{6,1},{7,0},{8,15},{9,14},{10,... | collective-permute-start | bytes 98312 | tf_op jit(solution)/shard_map/ppermute | solution.py:40
  6.6 3.8 %collective-permute-start.1 = (bf16[1,128,128]{2,1,0:T(8,128)(2,1)S(1)}, bf16[1,128,128]{2,1,0:T(8,128)(2,1)S(1)}, u32[]{:S(2)}, u32[]{:S(2)}) collective-permute-start(bf16[1,128,128]{2,1,0:T(8,128)(2,1)S(1)} %fusion.refs_0_), channel_id=1, source_target_pairs={{0,3},{1,2},{2,1},{3,0},{4,7},{5,6},{6,5},{7,4},{8,11},{9,10},{10,... | collective-permute-start | bytes 98312 | tf_op jit(solution)/shard_map/ppermute | solution.py:40
  6.8 3.5 %collective-permute-start = (bf16[1,128,128]{2,1,0:T(8,128)(2,1)S(1)}, bf16[1,128,128]{2,1,0:T(8,128)(2,1)S(1)}, u32[]{:S(2)}, u32[]{:S(2)}) collective-permute-start(bf16[1,128,128]{2,1,0:T(8,128)(2,1)S(1)} %fusion.refs_0_), channel_id=1, source_target_pairs={{0,1},{1,0},{2,3},{3,2},{4,5},{5,4},{6,7},{7,6},{8,9},{9,8},{10,11... | collective-permute-start | bytes 98312 | tf_op jit(solution)/shard_map/ppermute | solution.py:40
  6.8 2.2 %copy-start = (bf16[256,8,1024]{2,1,0:T(8,128)(2,1)S(1)}, bf16[256,8,1024]{2,1,0:T(8,128)(2,1)}, u32[]{:S(2)}) copy-start(bf16[256,8,1024]{2,1,0:T(8,128)(2,1)} %param.6) | copy-start | bytes 12582916
  9.4 1.7 %copy-start.1 = (f32[16,8,128]{2,1,0:T(8,128)S(1)}, f32[16,8,128]{2,1,0:T(8,128)}, u32[]{:S(2)}) copy-start(f32[16,8,128]{2,1,0:T(8,128)} %param.4) | copy-start | bytes 196612
  10.4 1.8 %collective-permute-start.4 = (bf16[3,128,128]{2,1,0:T(8,128)(2,1)S(1)}, bf16[3,128,128]{2,1,0:T(8,128)(2,1)S(1)}, u32[]{:S(2)}, u32[]{:S(2)}) collective-permute-start(bf16[3,128,128]{2,1,0:T(8,128)(2,1)S(1)} %join.2.bundle_ref.refs_0_), channel_id=1, source_target_pairs={{0,1},{1,0},{2,3},{3,2},{4,5},{5,4},{6,7},{7,6},{8,9},{9,8},{10,11... | collective-permute-start | bytes 294920 | tf_op jit(solution)/shard_map/ppermute | solution.py:40
  11.5 8.3 %copy-start.3 = (f32[256]{0:T(256)S(1)}, f32[256]{0:T(256)}, u32[]{:S(2)}) copy-start(f32[256]{0:T(256)} %param.7) | copy-start | bytes 3076
  13.0 6.7 %collective-permute-start.6 = (bf16[192,128]{1,0:T(8,128)(2,1)S(1)}, bf16[192,128]{1,0:T(8,128)(2,1)S(1)}, u32[]{:S(2)}, u32[]{:S(2)}) collective-permute-start(bf16[192,128]{1,0:T(8,128)(2,1)S(1)} %get-tuple-element.32), channel_id=1, source_target_pairs={{0,24},{8,16},{16,8},{24,0},{1,25},{9,17},{17,9},{25,1},{2,26},{10... | collective-permute-start | bytes 147464 | tf_op jit(solution)/shard_map/ppermute | solution.py:40
  15.5 4.3 %collective-permute-start.5 = (bf16[192,128]{1,0:T(8,128)(2,1)S(1)}, bf16[192,128]{1,0:T(8,128)(2,1)S(1)}, u32[]{:S(2)}, u32[]{:S(2)}) collective-permute-start(bf16[192,128]{1,0:T(8,128)(2,1)S(1)} %get-tuple-element.32), channel_id=1, source_target_pairs={{0,8},{8,0},{16,24},{24,16},{1,9},{9,1},{17,25},{25,17},{2,10},{10... | collective-permute-start | bytes 147464 | tf_op jit(solution)/shard_map/ppermute | solution.py:40
  16.1 3.7 %collective-permute-start.7 = (bf16[64,128]{1,0:T(8,128)(2,1)S(1)}, bf16[64,128]{1,0:T(8,128)(2,1)S(1)}, u32[]{:S(2)}, u32[]{:S(2)}) collective-permute-start(bf16[64,128]{1,0:T(8,128)(2,1)S(1)} %get-tuple-element.33.refs_0_), channel_id=1, source_target_pairs={{0,16},{8,24},{16,0},{24,8},{1,17},{9,25},{17,1},{25,9},{2,18},{10... | collective-permute-start | bytes 49160 | tf_op jit(solution)/shard_map/ppermute | solution.py:40
  20.5 1.4 %collective-permute-start.8 = (bf16[2,128,128]{2,1,0:T(8,128)(2,1)S(1)}, bf16[2,128,128]{2,1,0:T(8,128)(2,1)S(1)}, u32[]{:S(2)}, u32[]{:S(2)}) collective-permute-start(bf16[2,128,128]{2,1,0:T(8,128)(2,1)S(1)} %get-tuple-element.36), channel_id=1, source_target_pairs={{0,1},{1,0},{2,3},{3,2},{4,5},{5,4},{6,7},{7,6},{8,9},{9,8},{10,11... | collective-permute-start | bytes 196616 | tf_op jit(solution)/shard_map/ppermute | solution.py:40
  20.6 5.2 %copy-start.2 = (f32[8,128]{1,0:T(8,128)S(1)}, f32[8,128]{1,0:T(8,128)}, u32[]{:S(2)}) copy-start(f32[8,128]{1,0:T(8,128)} %amp_ref.3) | copy-start | bytes 12292
  21.4 4.2 %collective-permute-start.9 = (bf16[2,128,128]{2,1,0:T(8,128)(2,1)S(1)}, bf16[2,128,128]{2,1,0:T(8,128)(2,1)S(1)}, u32[]{:S(2)}, u32[]{:S(2)}) collective-permute-start(bf16[2,128,128]{2,1,0:T(8,128)(2,1)S(1)} %get-tuple-element.39), channel_id=1, source_target_pairs={{0,1},{1,0},{2,3},{3,2},{4,5},{5,4},{6,7},{7,6},{8,9},{9,8},{10,11... | collective-permute-start | bytes 196616 | tf_op jit(solution)/shard_map/ppermute | solution.py:40
  22.0 4.5 %collective-permute-start.10 = (bf16[1,128,128]{2,1,0:T(8,128)(2,1)S(1)}, bf16[1,128,128]{2,1,0:T(8,128)(2,1)S(1)}, u32[]{:S(2)}, u32[]{:S(2)}) collective-permute-start(bf16[1,128,128]{2,1,0:T(8,128)(2,1)S(1)} %get-tuple-element.37.refs_0_), channel_id=1, source_target_pairs={{0,5},{1,4},{2,7},{3,6},{4,1},{5,0},{6,3},{7,2},{8,13},{9,12},{10,... | collective-permute-start | bytes 98312 | tf_op jit(solution)/shard_map/ppermute | solution.py:40
  23.8 5.1 %collective-permute-start.11 = (bf16[1,128,128]{2,1,0:T(8,128)(2,1)S(1)}, bf16[1,128,128]{2,1,0:T(8,128)(2,1)S(1)}, u32[]{:S(2)}, u32[]{:S(2)}) collective-permute-start(bf16[1,128,128]{2,1,0:T(8,128)(2,1)S(1)} %get-tuple-element.38.refs_1_), channel_id=1, source_target_pairs={{0,7},{1,6},{2,5},{3,4},{4,3},{5,2},{6,1},{7,0},{8,15},{9,14},{10,... | collective-permute-start | bytes 98312 | tf_op jit(solution)/shard_map/ppermute | solution.py:40
  25.7 4.2 %collective-permute-start.12 = (bf16[1,128,128]{2,1,0:T(8,128)(2,1)S(1)}, bf16[1,128,128]{2,1,0:T(8,128)(2,1)S(1)}, u32[]{:S(2)}, u32[]{:S(2)}) collective-permute-start(bf16[1,128,128]{2,1,0:T(8,128)(2,1)S(1)} %get-tuple-element.41), channel_id=1, source_target_pairs={{0,3},{1,2},{2,1},{3,0},{4,7},{5,6},{6,5},{7,4},{8,11},{9,10},{10,... | collective-permute-start | bytes 98312 | tf_op jit(solution)/shard_map/ppermute | solution.py:40
  29.9 4.4 %collective-permute-start.16 = (bf16[1,128,128]{2,1,0:T(8,128)(2,1)S(1)}, bf16[1,128,128]{2,1,0:T(8,128)(2,1)S(1)}, u32[]{:S(2)}, u32[]{:S(2)}) collective-permute-start(bf16[1,128,128]{2,1,0:T(8,128)(2,1)S(1)} %get-tuple-element.43.refs_0_), channel_id=1, source_target_pairs={{0,5},{1,4},{2,7},{3,6},{4,1},{5,0},{6,3},{7,2},{8,13},{9,12},{10,... | collective-permute-start | bytes 98312 | tf_op jit(solution)/shard_map/ppermute | solution.py:40
  30.3 5.2 %collective-permute-start.15 = (bf16[1,128,128]{2,1,0:T(8,128)(2,1)S(1)}, bf16[1,128,128]{2,1,0:T(8,128)(2,1)S(1)}, u32[]{:S(2)}, u32[]{:S(2)}) collective-permute-start(bf16[1,128,128]{2,1,0:T(8,128)(2,1)S(1)} %get-tuple-element.43.refs_0_), channel_id=1, source_target_pairs={{0,7},{1,6},{2,5},{3,4},{4,3},{5,2},{6,1},{7,0},{8,15},{9,14},{10,... | collective-permute-start | bytes 98312 | tf_op jit(solution)/shard_map/ppermute | solution.py:40
  31.7 3.8 %collective-permute-start.14 = (bf16[1,128,128]{2,1,0:T(8,128)(2,1)S(1)}, bf16[1,128,128]{2,1,0:T(8,128)(2,1)S(1)}, u32[]{:S(2)}, u32[]{:S(2)}) collective-permute-start(bf16[1,128,128]{2,1,0:T(8,128)(2,1)S(1)} %get-tuple-element.43.refs_0_), channel_id=1, source_target_pairs={{0,3},{1,2},{2,1},{3,0},{4,7},{5,6},{6,5},{7,4},{8,11},{9,10},{10,... | collective-permute-start | bytes 98312 | tf_op jit(solution)/shard_map/ppermute | solution.py:40
  32.9 2.7 %collective-permute-start.13 = (bf16[1,128,128]{2,1,0:T(8,128)(2,1)S(1)}, bf16[1,128,128]{2,1,0:T(8,128)(2,1)S(1)}, u32[]{:S(2)}, u32[]{:S(2)}) collective-permute-start(bf16[1,128,128]{2,1,0:T(8,128)(2,1)S(1)} %get-tuple-element.43.refs_0_), channel_id=1, source_target_pairs={{0,1},{1,0},{2,3},{3,2},{4,5},{5,4},{6,7},{7,6},{8,9},{9,8},{10,11... | collective-permute-start | bytes 98312 | tf_op jit(solution)/shard_map/ppermute | solution.py:40
  35.6 1.6 %collective-permute-start.17 = (bf16[3,128,128]{2,1,0:T(8,128)(2,1)S(1)}, bf16[3,128,128]{2,1,0:T(8,128)(2,1)S(1)}, u32[]{:S(2)}, u32[]{:S(2)}) collective-permute-start(bf16[3,128,128]{2,1,0:T(8,128)(2,1)S(1)} %join.3.bundle_ref.refs_0_), channel_id=1, source_target_pairs={{0,1},{1,0},{2,3},{3,2},{4,5},{5,4},{6,7},{7,6},{8,9},{9,8},{10,11... | collective-permute-start | bytes 294920 | tf_op jit(solution)/shard_map/ppermute | solution.py:40
  37.9 5.7 %collective-permute-start.19 = (bf16[192,128]{1,0:T(8,128)(2,1)S(1)}, bf16[192,128]{1,0:T(8,128)(2,1)S(1)}, u32[]{:S(2)}, u32[]{:S(2)}) collective-permute-start(bf16[192,128]{1,0:T(8,128)(2,1)S(1)} %get-tuple-element.46), channel_id=1, source_target_pairs={{0,24},{8,16},{16,8},{24,0},{1,25},{9,17},{17,9},{25,1},{2,26},{10... | collective-permute-start | bytes 147464 | tf_op jit(solution)/shard_map/ppermute | solution.py:40
  39.4 4.3 %collective-permute-start.18 = (bf16[192,128]{1,0:T(8,128)(2,1)S(1)}, bf16[192,128]{1,0:T(8,128)(2,1)S(1)}, u32[]{:S(2)}, u32[]{:S(2)}) collective-permute-start(bf16[192,128]{1,0:T(8,128)(2,1)S(1)} %get-tuple-element.46), channel_id=1, source_target_pairs={{0,8},{8,0},{16,24},{24,16},{1,9},{9,1},{17,25},{25,17},{2,10},{10... | collective-permute-start | bytes 147464 | tf_op jit(solution)/shard_map/ppermute | solution.py:40
  39.9 3.7 %collective-permute-start.20 = (bf16[64,128]{1,0:T(8,128)(2,1)S(1)}, bf16[64,128]{1,0:T(8,128)(2,1)S(1)}, u32[]{:S(2)}, u32[]{:S(2)}) collective-permute-start(bf16[64,128]{1,0:T(8,128)(2,1)S(1)} %get-tuple-element.47.refs_0_), channel_id=1, source_target_pairs={{0,16},{8,24},{16,0},{24,8},{1,17},{9,25},{17,1},{25,9},{2,18},{10... | collective-permute-start | bytes 49160 | tf_op jit(solution)/shard_map/ppermute | solution.py:40
  44.4 1.4 %collective-permute-start.21 = (bf16[2,128,128]{2,1,0:T(8,128)(2,1)S(1)}, bf16[2,128,128]{2,1,0:T(8,128)(2,1)S(1)}, u32[]{:S(2)}, u32[]{:S(2)}) collective-permute-start(bf16[2,128,128]{2,1,0:T(8,128)(2,1)S(1)} %get-tuple-element.50), channel_id=1, source_target_pairs={{0,1},{1,0},{2,3},{3,2},{4,5},{5,4},{6,7},{7,6},{8,9},{9,8},{10,11... | collective-permute-start | bytes 196616 | tf_op jit(solution)/shard_map/ppermute | solution.py:40
  45.3 3.2 %collective-permute-start.22 = (bf16[2,128,128]{2,1,0:T(8,128)(2,1)S(1)}, bf16[2,128,128]{2,1,0:T(8,128)(2,1)S(1)}, u32[]{:S(2)}, u32[]{:S(2)}) collective-permute-start(bf16[2,128,128]{2,1,0:T(8,128)(2,1)S(1)} %get-tuple-element.53), channel_id=1, source_target_pairs={{0,1},{1,0},{2,3},{3,2},{4,5},{5,4},{6,7},{7,6},{8,9},{9,8},{10,11... | collective-permute-start | bytes 196616 | tf_op jit(solution)/shard_map/ppermute | solution.py:40
  45.9 5.3 %collective-permute-start.23 = (bf16[1,128,128]{2,1,0:T(8,128)(2,1)S(1)}, bf16[1,128,128]{2,1,0:T(8,128)(2,1)S(1)}, u32[]{:S(2)}, u32[]{:S(2)}) collective-permute-start(bf16[1,128,128]{2,1,0:T(8,128)(2,1)S(1)} %get-tuple-element.51.refs_0_), channel_id=1, source_target_pairs={{0,7},{1,6},{2,5},{3,4},{4,3},{5,2},{6,1},{7,0},{8,15},{9,14},{10,... | collective-permute-start | bytes 98312 | tf_op jit(solution)/shard_map/ppermute | solution.py:40
  48.0 4.5 %collective-permute-start.24 = (bf16[1,128,128]{2,1,0:T(8,128)(2,1)S(1)}, bf16[1,128,128]{2,1,0:T(8,128)(2,1)S(1)}, u32[]{:S(2)}, u32[]{:S(2)}) collective-permute-start(bf16[1,128,128]{2,1,0:T(8,128)(2,1)S(1)} %get-tuple-element.52.refs_1_), channel_id=1, source_target_pairs={{0,5},{1,4},{2,7},{3,6},{4,1},{5,0},{6,3},{7,2},{8,13},{9,12},{10,... | collective-permute-start | bytes 98312 | tf_op jit(solution)/shard_map/ppermute | solution.py:40
  48.6 4.0 %collective-permute-start.25 = (bf16[1,128,128]{2,1,0:T(8,128)(2,1)S(1)}, bf16[1,128,128]{2,1,0:T(8,128)(2,1)S(1)}, u32[]{:S(2)}, u32[]{:S(2)}) collective-permute-start(bf16[1,128,128]{2,1,0:T(8,128)(2,1)S(1)} %get-tuple-element.55), channel_id=1, source_target_pairs={{0,3},{1,2},{2,1},{3,0},{4,7},{5,6},{6,5},{7,4},{8,11},{9,10},{10,... | collective-permute-start | bytes 98312 | tf_op jit(solution)/shard_map/ppermute | solution.py:40

commit v13 on v12

--- a/solution.py
+++ b/solution.py
@@ -227,15 +227,14 @@
         at = end
 
 
-def local_kernel(rows, cols, halve, b_ref, x_ref, amp_ref, along_ref, *refs):
+def local_kernel(rows, cols, halve, masks, b_ref, x_ref, amp_ref, along_ref, *refs):
     pay_refs, base_ref = refs[:-1], refs[-1]
     lines = cols * rows
     head = pay_refs[0].shape[0] - lines
     me = lax.axis_index("grp")
     low = jnp.zeros((lines, LANES), jnp.float32)
     high = low
-    for n, ref in enumerate(pay_refs, 1):
-        mask = (1 << n) - 1
+    for mask, ref in zip(masks, pay_refs):
         part = ref[head:, :].astype(jnp.float32)
         low = jnp.where((me ^ mask) == me - 1, part, low)
         high = jnp.where((me ^ mask) == me + 1, part, high)
@@ -354,14 +353,17 @@
             scratch_shapes=[pltpu.VMEM((blocks * LANES, lines), f32)],
             name="project_across",
         )(held, diag, across, along_short)
-        pays = [swap(part if mask & (mask + 1) else pay, "grp", mask) for mask in range(1, groups)]
+        pays = {
+            mask: swap(part if mask & (mask + 1) else pay, "grp", mask)
+            for mask in reversed(range(1, groups))
+        }
         coef, far = call(
             partial(far_kernel, rows, cols, groups, ncells_all, spots_of(away, True)),
             (shape(bf16, lines, ranks * rows), shape(bf16, half, lines, width)),
             flops=work // 2,
             moved=flat.size,
             name="term_first",
-        )(scale, held, part, *pays)
+        )(scale, held, part, *pays.values())
         got = swap(far, "tile", 1)
 
         def term(*wanted, after=()):
@@ -389,10 +391,10 @@
         (mine,) = term((spots_of(close, False), f32), after=sends)
         kept, *sends = pair(mine, got, close)
         terms += [cross(send, mask) for send, mask in zip(sends, close[1:])]
-        rims = [pay for mask, pay in enumerate(pays, 1) if not mask & (mask + 1)]
+        rims = [mask for mask in pays if not mask & (mask + 1)]
         base = call(
-            partial(local_kernel, rows, cols, halve), shape(f32, lines, width), name="local"
-        )(b, x, amplitude, along, *rims)
+            partial(local_kernel, rows, cols, halve, rims), shape(f32, lines, width), name="local"
+        )(b, x, amplitude, along, *[pays[mask] for mask in rims])
         x, short = call(
             partial(update_kernel, halve, last),
             (

time: 53.5 us -> 54.4 us (1.017)
  waiting for transfers between devices: 13.7 us -> 14.5 us
    ppermute x26, waiting for transfers between devices: 13.7 us -> 14.5 us  [swap(): lax.ppermute(value, axis, [(i, i ^ mask) for i in range(lax.axis_size(axi...]
where the time goes in v13:
time: 54.4 us; the launch traced here: 54.2 us
  starting transfers between devices  25.4 us (47%)
  waiting for transfers between devices  14.5 us (27%)
  Pallas kernels  10.3 us (19%)
  local copies, waits for them, and re-layouts  2.21 us (4%)
  between operations  0.87 us (2%)
  other arithmetic  0.85 us (2%)
    ppermute x26, starting transfers between devices, swap(): lax.ppermute(value, axis, [(i, i ^ mask) for i in range(lax.axis_size(axi...  25.4 us
    ppermute x26, waiting for transfers between devices, swap(): lax.ppermute(value, axis, [(i, i ^ mask) for i in range(lax.axis_size(axi...  14.5 us
    pallas_call x4, Pallas kernels, term(): call(partial(term_kernel, wanted, len(after)), in_specs=[pl.BlockSpec(mem...  2.59 us
    pallas_call x4, Pallas kernels, first(): call(partial(first_kernel, rows, spots, len(before)), shape(f32, blocks *...  2.37 us
    unnamed x8, local copies, waits for them, and re-layouts  2.21 us
    pallas_call x2, Pallas kernels, on_device(): call(partial(second_kernel, rows, cols, spots), (shape(bf16, pay_rows, wi...  1.63 us
    pallas_call x2, Pallas kernels, on_device(): call(partial(far_kernel, rows, cols, groups, ncells_all, spots_of(away, T...  1.48 us
  transfers between devices with their start and end apart: 26, of which 11 were waited for; matrix products, arithmetic and copies ran while one was open for 0% of the time, Pallas kernels for 12%

profile of v13, /device:TPU:0, one launch (start us, length us, event | category | flops | bytes accessed | tf_op | source)
XLA Modules:
  0.0 54.2 jit_solution(508361458286112409)
XLA Ops:
  0.6 0.8 %fusion.refs_0_ = bf16[1,128,128]{2,1,0:T(8,128)(2,1)S(1)} fusion(f32[16,8,128]{2,1,0:T(8,128)} %param.4), kind=kLoop, calls=%fused_computation.1 | loop fusion | flops 32768 | bytes 98304 | tf_op jit(solution)/shard_map/convert_element_type | solution.py:278
  1.5 3.5 %collective-permute-start.3 = (bf16[1,128,128]{2,1,0:T(8,128)(2,1)S(1)}, bf16[1,128,128]{2,1,0:T(8,128)(2,1)S(1)}, u32[]{:S(2)}, u32[]{:S(2)}) collective-permute-start(bf16[1,128,128]{2,1,0:T(8,128)(2,1)S(1)} %fusion.refs_0_), channel_id=1, source_target_pairs={{0,5},{1,4},{2,7},{3,6},{4,1},{5,0},{6,3},{7,2},{8,13},{9,12},{10,... | collective-permute-start | bytes 98312 | tf_op jit(solution)/shard_map/ppermute | solution.py:40
  5.0 1.6 %collective-permute-start.2 = (bf16[1,128,128]{2,1,0:T(8,128)(2,1)S(1)}, bf16[1,128,128]{2,1,0:T(8,128)(2,1)S(1)}, u32[]{:S(2)}, u32[]{:S(2)}) collective-permute-start(bf16[1,128,128]{2,1,0:T(8,128)(2,1)S(1)} %fusion.refs_0_), channel_id=1, source_target_pairs={{0,7},{1,6},{2,5},{3,4},{4,3},{5,2},{6,1},{7,0},{8,15},{9,14},{10,... | collective-permute-start | bytes 98312 | tf_op jit(solution)/shard_map/ppermute | solution.py:40
  6.6 0.2 collective-permute-start.1
  6.8 0.0 collective-permute-start
  6.8 2.2 %copy-done = bf16[256,8,1024]{2,1,0:T(8,128)(2,1)S(1)} copy-done((bf16[256,8,1024]{2,1,0:T(8,128)(2,1)S(1)}, bf16[256,8,1024]{2,1,0:T(8,128)(2,1)}, u32[]{:S(2)}) %copy-start) | copy-done | bytes 4194328
  9.0 0.4 load.1.factor_ref
  9.4 0.0 copy-start.1
  9.4 0.5 project_own.4.refs_0_.refs_2_
  9.9 0.3 collective-permute-done.2.refs_3_
  10.2 0.2 collective-permute-done.1.refs_2_
  10.4 0.0 collective-permute-done.refs_1_.twin_ref
  10.4 0.7 %collective-permute-start.4 = (bf16[3,128,128]{2,1,0:T(8,128)(2,1)S(1)}, bf16[3,128,128]{2,1,0:T(8,128)(2,1)S(1)}, u32[]{:S(2)}, u32[]{:S(2)}) collective-permute-start(bf16[3,128,128]{2,1,0:T(8,128)(2,1)S(1)} %join.2.bundle_ref.refs_0_), channel_id=1, source_target_pairs={{0,1},{1,0},{2,3},{3,2},{4,5},{5,4},{6,7},{7,6},{8,9},{9,8},{10,11... | collective-permute-start | bytes 294920 | tf_op jit(solution)/shard_map/ppermute | solution.py:40
  11.1 0.4 columns.2
  11.5 0.0 copy-start.3
  11.5 0.7 %project_own.5.diag_ref = f32[256,128]{1,0:T(8,128)S(1)} custom-call(bf16[2048,1024]{1,0:T(8,128)(2,1)S(1)} %load.1.factor_ref, bf16[3,128,128]{2,1,0:T(8,128)(2,1)S(1)} %join.2.bundle_ref.refs_0_, bf16[1,128,128]{2,1,0:T(8,128)(2,1)S(1)} %collective-permute-done.refs_1_.twin_ref, f32[256,128]{1,0:T(8,128)S(1)} %project_own.4.refs_0_.refs_2_), custom_call_target="tpu_custom_call" | custom-call | flops 268435456 | bytes 2097152 | tf_op jit(solution)/shard_map/project_own/pallas_call | solution.py:315
  12.2 0.8 %project_across.2 = (bf16[192,128]{1,0:T(8,128)(2,1)S(1)}, bf16[64,128]{1,0:T(8,128)(2,1)S(1)}) custom-call(bf16[2048,1024]{1,0:T(8,128)(2,1)S(1)} %load.1.factor_ref, f32[256,128]{1,0:T(8,128)S(1)} %project_own.5.diag_ref, bf16[3,128,128]{2,1,0:T(8,128)(2,1)S(1)} %collective-permute-done.4.fields_ref, bf16[128,128]{1,0:T(8,128)(2,1)S(1)} %get-tuple-element.31.short_ref), custom_call_target="tpu_custom_call" | custom-call | flops 268435456 | bytes 2097152 | tf_op jit(solution)/shard_map/project_across/pallas_call | solution.py:348
  13.0 1.5 %collective-permute-start.6 = (bf16[192,128]{1,0:T(8,128)(2,1)S(1)}, bf16[192,128]{1,0:T(8,128)(2,1)S(1)}, u32[]{:S(2)}, u32[]{:S(2)}) collective-permute-start(bf16[192,128]{1,0:T(8,128)(2,1)S(1)} %get-tuple-element.32), channel_id=1, source_target_pairs={{0,8},{8,0},{16,24},{24,16},{1,9},{9,1},{17,25},{25,17},{2,10},{10... | collective-permute-start | bytes 147464 | tf_op jit(solution)/shard_map/ppermute | solution.py:40
  14.6 1.5 %collective-permute-start.5 = (bf16[192,128]{1,0:T(8,128)(2,1)S(1)}, bf16[192,128]{1,0:T(8,128)(2,1)S(1)}, u32[]{:S(2)}, u32[]{:S(2)}) collective-permute-start(bf16[192,128]{1,0:T(8,128)(2,1)S(1)} %get-tuple-element.32), channel_id=1, source_target_pairs={{0,24},{8,16},{16,8},{24,0},{1,25},{9,17},{17,9},{25,1},{2,26},{10... | collective-permute-start | bytes 147464 | tf_op jit(solution)/shard_map/ppermute | solution.py:40
  16.1 0.5 collective-permute-start.7
  16.6 3.2 %collective-permute-done.7.refs_2_ = bf16[64,128]{1,0:T(8,128)(2,1)S(1)} collective-permute-done((bf16[64,128]{1,0:T(8,128)(2,1)S(1)}, bf16[64,128]{1,0:T(8,128)(2,1)S(1)}, u32[]{:S(2)}, u32[]{:S(2)}) %collective-permute-start.7) | collective-permute-done | bytes 16416 | tf_op jit(solution)/shard_map/ppermute | solution.py:40
  19.8 0.0 collective-permute-done.6.refs_1_.refs_3_
  19.8 0.0 collective-permute-done.5.refs_0_.refs_1_
  19.8 0.7 %term_first.2 = (bf16[128,2048]{1,0:T(8,128)(2,1)S(1)}, bf16[2,128,128]{2,1,0:T(8,128)(2,1)S(1)}) custom-call(f32[1,256]{1,0:T(1,128)S(1)} %bitcast.13, bf16[2048,1024]{1,0:T(8,128)(2,1)S(1)} %load.1.factor_ref, bf16[64,128]{1,0:T(8,128)(2,1)S(1)} %get-tuple-element.33.refs_0_, bf16[192,128]{1,0:T(8,128)(2,1)S(1)} %collective-permute-done.5.refs_0_.refs_1_, ...), custom_call_target="tpu_custom_call" | custom-call | flops 134217728 | bytes 2097152 | tf_op jit(solution)/shard_map/term_first/pallas_call | solution.py:360
  20.5 0.1 collective-permute-start.8
  20.6 0.0 copy-start.2
  20.6 0.8 %term.4 = (f32[2,128,128]{2,1,0:T(8,128)S(1)}, bf16[2,128,128]{2,1,0:T(8,128)(2,1)S(1)}) custom-call(bf16[128,2048]{1,0:T(8,128)(2,1)S(1)} %get-tuple-element.34.coef_ref, bf16[2048,1024]{1,0:T(8,128)(2,1)S(1)} %load.1.factor_ref), custom_call_target="tpu_custom_call" | custom-call | flops 268435456 | bytes 2097152 | tf_op jit(solution)/shard_map/term/pallas_call | solution.py:370
  21.4 0.5 %collective-permute-start.9 = (bf16[2,128,128]{2,1,0:T(8,128)(2,1)S(1)}, bf16[2,128,128]{2,1,0:T(8,128)(2,1)S(1)}, u32[]{:S(2)}, u32[]{:S(2)}) collective-permute-start(bf16[2,128,128]{2,1,0:T(8,128)(2,1)S(1)} %get-tuple-element.39), channel_id=1, source_target_pairs={{0,1},{1,0},{2,3},{3,2},{4,5},{5,4},{6,7},{7,6},{8,9},{9,8},{10,11... | collective-permute-start | bytes 196616 | tf_op jit(solution)/shard_map/ppermute | solution.py:40
  22.0 0.0 collective-permute-done.8.got_ref
  22.0 1.7 %collective-permute-start.10 = (bf16[1,128,128]{2,1,0:T(8,128)(2,1)S(1)}, bf16[1,128,128]{2,1,0:T(8,128)(2,1)S(1)}, u32[]{:S(2)}, u32[]{:S(2)}) collective-permute-start(bf16[1,128,128]{2,1,0:T(8,128)(2,1)S(1)} %get-tuple-element.37.refs_0_), channel_id=1, source_target_pairs={{0,5},{1,4},{2,7},{3,6},{4,1},{5,0},{6,3},{7,2},{8,13},{9,12},{10,... | collective-permute-start | bytes 98312 | tf_op jit(solution)/shard_map/ppermute | solution.py:40
  23.8 1.4 %collective-permute-start.11 = (bf16[1,128,128]{2,1,0:T(8,128)(2,1)S(1)}, bf16[1,128,128]{2,1,0:T(8,128)(2,1)S(1)}, u32[]{:S(2)}, u32[]{:S(2)}) collective-permute-start(bf16[1,128,128]{2,1,0:T(8,128)(2,1)S(1)} %get-tuple-element.38.refs_1_), channel_id=1, source_target_pairs={{0,7},{1,6},{2,5},{3,4},{4,3},{5,2},{6,1},{7,0},{8,15},{9,14},{10,... | collective-permute-start | bytes 98312 | tf_op jit(solution)/shard_map/ppermute | solution.py:40
  25.2 0.5 term.5.mine_ref
  25.7 0.1 collective-permute-start.12
  25.8 0.2 local.2.base_ref
  26.0 0.5 collective-permute-done.10.refs_1_
  26.5 2.4 %collective-permute-done.11.refs_2_ = bf16[1,128,128]{2,1,0:T(8,128)(2,1)S(1)} collective-permute-done((bf16[1,128,128]{2,1,0:T(8,128)(2,1)S(1)}, bf16[1,128,128]{2,1,0:T(8,128)(2,1)S(1)}, u32[]{:S(2)}, u32[]{:S(2)}) %collective-permute-start.11) | collective-permute-done | bytes 32800 | tf_op jit(solution)/shard_map/ppermute | solution.py:40
  28.9 1.0 %collective-permute-done.12.refs_3_ = bf16[1,128,128]{2,1,0:T(8,128)(2,1)S(1)} collective-permute-done((bf16[1,128,128]{2,1,0:T(8,128)(2,1)S(1)}, bf16[1,128,128]{2,1,0:T(8,128)(2,1)S(1)}, u32[]{:S(2)}, u32[]{:S(2)}) %collective-permute-start.12) | collective-permute-done | bytes 32800 | tf_op jit(solution)/shard_map/ppermute | solution.py:40
  29.9 0.4 collective-permute-start.16
  30.3 1.4 %collective-permute-start.15 = (bf16[1,128,128]{2,1,0:T(8,128)(2,1)S(1)}, bf16[1,128,128]{2,1,0:T(8,128)(2,1)S(1)}, u32[]{:S(2)}, u32[]{:S(2)}) collective-permute-start(bf16[1,128,128]{2,1,0:T(8,128)(2,1)S(1)} %get-tuple-element.43.refs_0_), channel_id=1, source_target_pairs={{0,7},{1,6},{2,5},{3,4},{4,3},{5,2},{6,1},{7,0},{8,15},{9,14},{10,... | collective-permute-start | bytes 98312 | tf_op jit(solution)/shard_map/ppermute | solution.py:40
  31.7 1.2 %collective-permute-start.14 = (bf16[1,128,128]{2,1,0:T(8,128)(2,1)S(1)}, bf16[1,128,128]{2,1,0:T(8,128)(2,1)S(1)}, u32[]{:S(2)}, u32[]{:S(2)}) collective-permute-start(bf16[1,128,128]{2,1,0:T(8,128)(2,1)S(1)} %get-tuple-element.43.refs_0_), channel_id=1, source_target_pairs={{0,3},{1,2},{2,1},{3,0},{4,7},{5,6},{6,5},{7,4},{8,11},{9,10},{10,... | collective-permute-start | bytes 98312 | tf_op jit(solution)/shard_map/ppermute | solution.py:40
  32.9 0.4 collective-permute-start.13
  33.3 0.5 project_own.6.refs_0_.refs_2_
  33.8 0.5 collective-permute-done.16.refs_4_
  34.3 1.2 %collective-permute-done.15.refs_3_ = bf16[1,128,128]{2,1,0:T(8,128)(2,1)S(1)} collective-permute-done((bf16[1,128,128]{2,1,0:T(8,128)(2,1)S(1)}, bf16[1,128,128]{2,1,0:T(8,128)(2,1)S(1)}, u32[]{:S(2)}, u32[]{:S(2)}) %collective-permute-start.15) | collective-permute-done | bytes 32800 | tf_op jit(solution)/shard_map/ppermute | solution.py:40
  35.5 0.0 collective-permute-done.13.refs_1_.twin_ref
  35.5 0.6 %collective-permute-start.17 = (bf16[3,128,128]{2,1,0:T(8,128)(2,1)S(1)}, bf16[3,128,128]{2,1,0:T(8,128)(2,1)S(1)}, u32[]{:S(2)}, u32[]{:S(2)}) collective-permute-start(bf16[3,128,128]{2,1,0:T(8,128)(2,1)S(1)} %join.3.bundle_ref.refs_0_), channel_id=1, source_target_pairs={{0,1},{1,0},{2,3},{3,2},{4,5},{5,4},{6,7},{7,6},{8,9},{9,8},{10,11... | collective-permute-start | bytes 294920 | tf_op jit(solution)/shard_map/ppermute | solution.py:40
  36.0 0.3 columns.3
  36.4 0.7 %project_own.7.diag_ref = f32[256,128]{1,0:T(8,128)S(1)} custom-call(bf16[2048,1024]{1,0:T(8,128)(2,1)S(1)} %load.1.factor_ref, bf16[3,128,128]{2,1,0:T(8,128)(2,1)S(1)} %join.3.bundle_ref.refs_0_, bf16[1,128,128]{2,1,0:T(8,128)(2,1)S(1)} %collective-permute-done.13.refs_1_.twin_ref, f32[256,128]{1,0:T(8,128)S(1)} %project_own.6.refs_0_.refs_2_), custom_call_target="tpu_custom_call" | custom-call | flops 268435456 | bytes 2097152 | tf_op jit(solution)/shard_map/project_own/pallas_call | solution.py:315
  37.1 0.8 %project_across.3 = (bf16[192,128]{1,0:T(8,128)(2,1)S(1)}, bf16[64,128]{1,0:T(8,128)(2,1)S(1)}) custom-call(bf16[2048,1024]{1,0:T(8,128)(2,1)S(1)} %load.1.factor_ref, f32[256,128]{1,0:T(8,128)S(1)} %project_own.7.diag_ref, bf16[3,128,128]{2,1,0:T(8,128)(2,1)S(1)} %collective-permute-done.17.fields_ref, bf16[128,128]{1,0:T(8,128)(2,1)S(1)} %get-tuple-element.45.short_ref), custom_call_target="tpu_custom_call" | custom-call | flops 268435456 | bytes 2097152 | tf_op jit(solution)/shard_map/project_across/pallas_call | solution.py:348
  37.9 1.5 %collective-permute-start.19 = (bf16[192,128]{1,0:T(8,128)(2,1)S(1)}, bf16[192,128]{1,0:T(8,128)(2,1)S(1)}, u32[]{:S(2)}, u32[]{:S(2)}) collective-permute-start(bf16[192,128]{1,0:T(8,128)(2,1)S(1)} %get-tuple-element.46), channel_id=1, source_target_pairs={{0,8},{8,0},{16,24},{24,16},{1,9},{9,1},{17,25},{25,17},{2,10},{10... | collective-permute-start | bytes 147464 | tf_op jit(solution)/shard_map/ppermute | solution.py:40
  39.5 1.2 %collective-permute-start.18 = (bf16[192,128]{1,0:T(8,128)(2,1)S(1)}, bf16[192,128]{1,0:T(8,128)(2,1)S(1)}, u32[]{:S(2)}, u32[]{:S(2)}) collective-permute-start(bf16[192,128]{1,0:T(8,128)(2,1)S(1)} %get-tuple-element.46), channel_id=1, source_target_pairs={{0,24},{8,16},{16,8},{24,0},{1,25},{9,17},{17,9},{25,1},{2,26},{10... | collective-permute-start | bytes 147464 | tf_op jit(solution)/shard_map/ppermute | solution.py:40
  40.7 0.8 %collective-permute-start.20 = (bf16[64,128]{1,0:T(8,128)(2,1)S(1)}, bf16[64,128]{1,0:T(8,128)(2,1)S(1)}, u32[]{:S(2)}, u32[]{:S(2)}) collective-permute-start(bf16[64,128]{1,0:T(8,128)(2,1)S(1)} %get-tuple-element.47.refs_0_), channel_id=1, source_target_pairs={{0,16},{8,24},{16,0},{24,8},{1,17},{9,25},{17,1},{25,9},{2,18},{10... | collective-permute-start | bytes 49160 | tf_op jit(solution)/shard_map/ppermute | solution.py:40
  41.5 3.2 %collective-permute-done.20.refs_2_ = bf16[64,128]{1,0:T(8,128)(2,1)S(1)} collective-permute-done((bf16[64,128]{1,0:T(8,128)(2,1)S(1)}, bf16[64,128]{1,0:T(8,128)(2,1)S(1)}, u32[]{:S(2)}, u32[]{:S(2)}) %collective-permute-start.20) | collective-permute-done | bytes 16416 | tf_op jit(solution)/shard_map/ppermute | solution.py:40
  44.6 0.7 %term_first.3 = (bf16[128,2048]{1,0:T(8,128)(2,1)S(1)}, bf16[2,128,128]{2,1,0:T(8,128)(2,1)S(1)}) custom-call(f32[1,256]{1,0:T(1,128)S(1)} %bitcast.14, bf16[2048,1024]{1,0:T(8,128)(2,1)S(1)} %load.1.factor_ref, bf16[64,128]{1,0:T(8,128)(2,1)S(1)} %get-tuple-element.47.refs_0_, bf16[192,128]{1,0:T(8,128)(2,1)S(1)} %collective-permute-done.18.refs_0_.refs_1_, ...), custom_call_target="tpu_custom_call" | custom-call | flops 134217728 | bytes 2097152 | tf_op jit(solution)/shard_map/term_first/pallas_call | solution.py:360
  45.4 0.1 collective-permute-start.21
  45.5 0.8 %term.6 = (f32[2,128,128]{2,1,0:T(8,128)S(1)}, bf16[2,128,128]{2,1,0:T(8,128)(2,1)S(1)}) custom-call(bf16[128,2048]{1,0:T(8,128)(2,1)S(1)} %get-tuple-element.48.coef_ref, bf16[2048,1024]{1,0:T(8,128)(2,1)S(1)} %load.1.factor_ref), custom_call_target="tpu_custom_call" | custom-call | flops 268435456 | bytes 2097152 | tf_op jit(solution)/shard_map/term/pallas_call | solution.py:370
  46.3 0.6 %collective-permute-start.22 = (bf16[2,128,128]{2,1,0:T(8,128)(2,1)S(1)}, bf16[2,128,128]{2,1,0:T(8,128)(2,1)S(1)}, u32[]{:S(2)}, u32[]{:S(2)}) collective-permute-start(bf16[2,128,128]{2,1,0:T(8,128)(2,1)S(1)} %get-tuple-element.53), channel_id=1, source_target_pairs={{0,1},{1,0},{2,3},{3,2},{4,5},{5,4},{6,7},{7,6},{8,9},{9,8},{10,11... | collective-permute-start | bytes 196616 | tf_op jit(solution)/shard_map/ppermute | solution.py:40
  46.8 2.1 %collective-permute-start.23 = (bf16[1,128,128]{2,1,0:T(8,128)(2,1)S(1)}, bf16[1,128,128]{2,1,0:T(8,128)(2,1)S(1)}, u32[]{:S(2)}, u32[]{:S(2)}) collective-permute-start(bf16[1,128,128]{2,1,0:T(8,128)(2,1)S(1)} %get-tuple-element.51.refs_0_), channel_id=1, source_target_pairs={{0,7},{1,6},{2,5},{3,4},{4,3},{5,2},{6,1},{7,0},{8,15},{9,14},{10,... | collective-permute-start | bytes 98312 | tf_op jit(solution)/shard_map/ppermute | solution.py:40
  49.0 0.5 term.7.mine_ref
  49.5 1.7 %collective-permute-start.25 = (bf16[1,128,128]{2,1,0:T(8,128)(2,1)S(1)}, bf16[1,128,128]{2,1,0:T(8,128)(2,1)S(1)}, u32[]{:S(2)}, u32[]{:S(2)}) collective-permute-start(bf16[1,128,128]{2,1,0:T(8,128)(2,1)S(1)} %get-tuple-element.55), channel_id=1, source_target_pairs={{0,3},{1,2},{2,1},{3,0},{4,7},{5,6},{6,5},{7,4},{8,11},{9,10},{10,... | collective-permute-start | bytes 98312 | tf_op jit(solution)/shard_map/ppermute | solution.py:40
  51.3 0.2 local.3.base_ref
  51.4 0.8 %collective-permute-done.23.refs_1_ = bf16[1,128,128]{2,1,0:T(8,128)(2,1)S(1)} collective-permute-done((bf16[1,128,128]{2,1,0:T(8,128)(2,1)S(1)}, bf16[1,128,128]{2,1,0:T(8,128)(2,1)S(1)}, u32[]{:S(2)}, u32[]{:S(2)}) %collective-permute-start.23) | collective-permute-done | bytes 32800 | tf_op jit(solution)/shard_map/ppermute | solution.py:40
  52.2 1.3 %collective-permute-done.24.refs_2_ = bf16[1,128,128]{2,1,0:T(8,128)(2,1)S(1)} collective-permute-done((bf16[1,128,128]{2,1,0:T(8,128)(2,1)S(1)}, bf16[1,128,128]{2,1,0:T(8,128)(2,1)S(1)}, u32[]{:S(2)}, u32[]{:S(2)}) %collective-permute-start.24) | collective-permute-done | bytes 32800 | tf_op jit(solution)/shard_map/ppermute | solution.py:40
  53.5 0.7 %update.3 = (f32[128,128]{1,0:T(8,128)}, f32[128,128]{1,0:T(8,128)}) custom-call(f32[128,128]{1,0:T(8,128)S(1)} %get-tuple-element.42.x_ref, f32[128,128]{1,0:T(8,128)S(1)} %local.3.base_ref, f32[1,128,128]{2,1,0:T(8,128)S(1)} %get-tuple-element.54.refs_0_, bf16[1,128,128]{2,1,0:T(8,128)(2,1)S(1)} %collective-permute-done.23.refs_1_, ...), custom_call_target="tpu_custom_call" | custom-call | bytes 262144 | tf_op jit(solution)/shard_map/update/pallas_call | solution.py:398
  (22 shorter events, 0.1 us)
Async XLA Ops:
  1.5 8.4 %collective-permute-start.3 = (bf16[1,128,128]{2,1,0:T(8,128)(2,1)S(1)}, bf16[1,128,128]{2,1,0:T(8,128)(2,1)S(1)}, u32[]{:S(2)}, u32[]{:S(2)}) collective-permute-start(bf16[1,128,128]{2,1,0:T(8,128)(2,1)S(1)} %fusion.refs_0_), channel_id=1, source_target_pairs={{0,5},{1,4},{2,7},{3,6},{4,1},{5,0},{6,3},{7,2},{8,13},{9,12},{10,... | collective-permute-start | bytes 98312 | tf_op jit(solution)/shard_map/ppermute | solution.py:40
  5.0 5.2 %collective-permute-start.2 = (bf16[1,128,128]{2,1,0:T(8,128)(2,1)S(1)}, bf16[1,128,128]{2,1,0:T(8,128)(2,1)S(1)}, u32[]{:S(2)}, u32[]{:S(2)}) collective-permute-start(bf16[1,128,128]{2,1,0:T(8,128)(2,1)S(1)} %fusion.refs_0_), channel_id=1, source_target_pairs={{0,7},{1,6},{2,5},{3,4},{4,3},{5,2},{6,1},{7,0},{8,15},{9,14},{10,... | collective-permute-start | bytes 98312 | tf_op jit(solution)/shard_map/ppermute | solution.py:40
  6.6 3.8 %collective-permute-start.1 = (bf16[1,128,128]{2,1,0:T(8,128)(2,1)S(1)}, bf16[1,128,128]{2,1,0:T(8,128)(2,1)S(1)}, u32[]{:S(2)}, u32[]{:S(2)}) collective-permute-start(bf16[1,128,128]{2,1,0:T(8,128)(2,1)S(1)} %fusion.refs_0_), channel_id=1, source_target_pairs={{0,3},{1,2},{2,1},{3,0},{4,7},{5,6},{6,5},{7,4},{8,11},{9,10},{10,... | collective-permute-start | bytes 98312 | tf_op jit(solution)/shard_map/ppermute | solution.py:40
  6.8 3.5 %collective-permute-start = (bf16[1,128,128]{2,1,0:T(8,128)(2,1)S(1)}, bf16[1,128,128]{2,1,0:T(8,128)(2,1)S(1)}, u32[]{:S(2)}, u32[]{:S(2)}) collective-permute-start(bf16[1,128,128]{2,1,0:T(8,128)(2,1)S(1)} %fusion.refs_0_), channel_id=1, source_target_pairs={{0,1},{1,0},{2,3},{3,2},{4,5},{5,4},{6,7},{7,6},{8,9},{9,8},{10,11... | collective-permute-start | bytes 98312 | tf_op jit(solution)/shard_map/ppermute | solution.py:40
  6.8 2.2 %copy-start = (bf16[256,8,1024]{2,1,0:T(8,128)(2,1)S(1)}, bf16[256,8,1024]{2,1,0:T(8,128)(2,1)}, u32[]{:S(2)}) copy-start(bf16[256,8,1024]{2,1,0:T(8,128)(2,1)} %param.6) | copy-start | bytes 12582916
  9.4 1.7 %copy-start.1 = (f32[16,8,128]{2,1,0:T(8,128)S(1)}, f32[16,8,128]{2,1,0:T(8,128)}, u32[]{:S(2)}) copy-start(f32[16,8,128]{2,1,0:T(8,128)} %param.4) | copy-start | bytes 196612
  10.4 1.8 %collective-permute-start.4 = (bf16[3,128,128]{2,1,0:T(8,128)(2,1)S(1)}, bf16[3,128,128]{2,1,0:T(8,128)(2,1)S(1)}, u32[]{:S(2)}, u32[]{:S(2)}) collective-permute-start(bf16[3,128,128]{2,1,0:T(8,128)(2,1)S(1)} %join.2.bundle_ref.refs_0_), channel_id=1, source_target_pairs={{0,1},{1,0},{2,3},{3,2},{4,5},{5,4},{6,7},{7,6},{8,9},{9,8},{10,11... | collective-permute-start | bytes 294920 | tf_op jit(solution)/shard_map/ppermute | solution.py:40
  11.5 8.3 %copy-start.3 = (f32[256]{0:T(256)S(1)}, f32[256]{0:T(256)}, u32[]{:S(2)}) copy-start(f32[256]{0:T(256)} %param.7) | copy-start | bytes 3076
  13.0 6.7 %collective-permute-start.6 = (bf16[192,128]{1,0:T(8,128)(2,1)S(1)}, bf16[192,128]{1,0:T(8,128)(2,1)S(1)}, u32[]{:S(2)}, u32[]{:S(2)}) collective-permute-start(bf16[192,128]{1,0:T(8,128)(2,1)S(1)} %get-tuple-element.32), channel_id=1, source_target_pairs={{0,8},{8,0},{16,24},{24,16},{1,9},{9,1},{17,25},{25,17},{2,10},{10... | collective-permute-start | bytes 147464 | tf_op jit(solution)/shard_map/ppermute | solution.py:40
  14.6 5.2 %collective-permute-start.5 = (bf16[192,128]{1,0:T(8,128)(2,1)S(1)}, bf16[192,128]{1,0:T(8,128)(2,1)S(1)}, u32[]{:S(2)}, u32[]{:S(2)}) collective-permute-start(bf16[192,128]{1,0:T(8,128)(2,1)S(1)} %get-tuple-element.32), channel_id=1, source_target_pairs={{0,24},{8,16},{16,8},{24,0},{1,25},{9,17},{17,9},{25,1},{2,26},{10... | collective-permute-start | bytes 147464 | tf_op jit(solution)/shard_map/ppermute | solution.py:40
  16.1 3.7 %collective-permute-start.7 = (bf16[64,128]{1,0:T(8,128)(2,1)S(1)}, bf16[64,128]{1,0:T(8,128)(2,1)S(1)}, u32[]{:S(2)}, u32[]{:S(2)}) collective-permute-start(bf16[64,128]{1,0:T(8,128)(2,1)S(1)} %get-tuple-element.33.refs_0_), channel_id=1, source_target_pairs={{0,16},{8,24},{16,0},{24,8},{1,17},{9,25},{17,1},{25,9},{2,18},{10... | collective-permute-start | bytes 49160 | tf_op jit(solution)/shard_map/ppermute | solution.py:40
  20.5 1.4 %collective-permute-start.8 = (bf16[2,128,128]{2,1,0:T(8,128)(2,1)S(1)}, bf16[2,128,128]{2,1,0:T(8,128)(2,1)S(1)}, u32[]{:S(2)}, u32[]{:S(2)}) collective-permute-start(bf16[2,128,128]{2,1,0:T(8,128)(2,1)S(1)} %get-tuple-element.36), channel_id=1, source_target_pairs={{0,1},{1,0},{2,3},{3,2},{4,5},{5,4},{6,7},{7,6},{8,9},{9,8},{10,11... | collective-permute-start | bytes 196616 | tf_op jit(solution)/shard_map/ppermute | solution.py:40
  20.6 5.2 %copy-start.2 = (f32[8,128]{1,0:T(8,128)S(1)}, f32[8,128]{1,0:T(8,128)}, u32[]{:S(2)}) copy-start(f32[8,128]{1,0:T(8,128)} %amp_ref.3) | copy-start | bytes 12292
  21.4 4.2 %collective-permute-start.9 = (bf16[2,128,128]{2,1,0:T(8,128)(2,1)S(1)}, bf16[2,128,128]{2,1,0:T(8,128)(2,1)S(1)}, u32[]{:S(2)}, u32[]{:S(2)}) collective-permute-start(bf16[2,128,128]{2,1,0:T(8,128)(2,1)S(1)} %get-tuple-element.39), channel_id=1, source_target_pairs={{0,1},{1,0},{2,3},{3,2},{4,5},{5,4},{6,7},{7,6},{8,9},{9,8},{10,11... | collective-permute-start | bytes 196616 | tf_op jit(solution)/shard_map/ppermute | solution.py:40
  22.0 4.5 %collective-permute-start.10 = (bf16[1,128,128]{2,1,0:T(8,128)(2,1)S(1)}, bf16[1,128,128]{2,1,0:T(8,128)(2,1)S(1)}, u32[]{:S(2)}, u32[]{:S(2)}) collective-permute-start(bf16[1,128,128]{2,1,0:T(8,128)(2,1)S(1)} %get-tuple-element.37.refs_0_), channel_id=1, source_target_pairs={{0,5},{1,4},{2,7},{3,6},{4,1},{5,0},{6,3},{7,2},{8,13},{9,12},{10,... | collective-permute-start | bytes 98312 | tf_op jit(solution)/shard_map/ppermute | solution.py:40
  23.8 5.1 %collective-permute-start.11 = (bf16[1,128,128]{2,1,0:T(8,128)(2,1)S(1)}, bf16[1,128,128]{2,1,0:T(8,128)(2,1)S(1)}, u32[]{:S(2)}, u32[]{:S(2)}) collective-permute-start(bf16[1,128,128]{2,1,0:T(8,128)(2,1)S(1)} %get-tuple-element.38.refs_1_), channel_id=1, source_target_pairs={{0,7},{1,6},{2,5},{3,4},{4,3},{5,2},{6,1},{7,0},{8,15},{9,14},{10,... | collective-permute-start | bytes 98312 | tf_op jit(solution)/shard_map/ppermute | solution.py:40
  25.7 4.2 %collective-permute-start.12 = (bf16[1,128,128]{2,1,0:T(8,128)(2,1)S(1)}, bf16[1,128,128]{2,1,0:T(8,128)(2,1)S(1)}, u32[]{:S(2)}, u32[]{:S(2)}) collective-permute-start(bf16[1,128,128]{2,1,0:T(8,128)(2,1)S(1)} %get-tuple-element.41), channel_id=1, source_target_pairs={{0,3},{1,2},{2,1},{3,0},{4,7},{5,6},{6,5},{7,4},{8,11},{9,10},{10,... | collective-permute-start | bytes 98312 | tf_op jit(solution)/shard_map/ppermute | solution.py:40
  29.9 4.4 %collective-permute-start.16 = (bf16[1,128,128]{2,1,0:T(8,128)(2,1)S(1)}, bf16[1,128,128]{2,1,0:T(8,128)(2,1)S(1)}, u32[]{:S(2)}, u32[]{:S(2)}) collective-permute-start(bf16[1,128,128]{2,1,0:T(8,128)(2,1)S(1)} %get-tuple-element.43.refs_0_), channel_id=1, source_target_pairs={{0,5},{1,4},{2,7},{3,6},{4,1},{5,0},{6,3},{7,2},{8,13},{9,12},{10,... | collective-permute-start | bytes 98312 | tf_op jit(solution)/shard_map/ppermute | solution.py:40
  30.3 5.2 %collective-permute-start.15 = (bf16[1,128,128]{2,1,0:T(8,128)(2,1)S(1)}, bf16[1,128,128]{2,1,0:T(8,128)(2,1)S(1)}, u32[]{:S(2)}, u32[]{:S(2)}) collective-permute-start(bf16[1,128,128]{2,1,0:T(8,128)(2,1)S(1)} %get-tuple-element.43.refs_0_), channel_id=1, source_target_pairs={{0,7},{1,6},{2,5},{3,4},{4,3},{5,2},{6,1},{7,0},{8,15},{9,14},{10,... | collective-permute-start | bytes 98312 | tf_op jit(solution)/shard_map/ppermute | solution.py:40
  31.7 3.7 %collective-permute-start.14 = (bf16[1,128,128]{2,1,0:T(8,128)(2,1)S(1)}, bf16[1,128,128]{2,1,0:T(8,128)(2,1)S(1)}, u32[]{:S(2)}, u32[]{:S(2)}) collective-permute-start(bf16[1,128,128]{2,1,0:T(8,128)(2,1)S(1)} %get-tuple-element.43.refs_0_), channel_id=1, source_target_pairs={{0,3},{1,2},{2,1},{3,0},{4,7},{5,6},{6,5},{7,4},{8,11},{9,10},{10,... | collective-permute-start | bytes 98312 | tf_op jit(solution)/shard_map/ppermute | solution.py:40
  32.9 2.6 %collective-permute-start.13 = (bf16[1,128,128]{2,1,0:T(8,128)(2,1)S(1)}, bf16[1,128,128]{2,1,0:T(8,128)(2,1)S(1)}, u32[]{:S(2)}, u32[]{:S(2)}) collective-permute-start(bf16[1,128,128]{2,1,0:T(8,128)(2,1)S(1)} %get-tuple-element.43.refs_0_), channel_id=1, source_target_pairs={{0,1},{1,0},{2,3},{3,2},{4,5},{5,4},{6,7},{7,6},{8,9},{9,8},{10,11... | collective-permute-start | bytes 98312 | tf_op jit(solution)/shard_map/ppermute | solution.py:40
  35.5 1.6 %collective-permute-start.17 = (bf16[3,128,128]{2,1,0:T(8,128)(2,1)S(1)}, bf16[3,128,128]{2,1,0:T(8,128)(2,1)S(1)}, u32[]{:S(2)}, u32[]{:S(2)}) collective-permute-start(bf16[3,128,128]{2,1,0:T(8,128)(2,1)S(1)} %join.3.bundle_ref.refs_0_), channel_id=1, source_target_pairs={{0,1},{1,0},{2,3},{3,2},{4,5},{5,4},{6,7},{7,6},{8,9},{9,8},{10,11... | collective-permute-start | bytes 294920 | tf_op jit(solution)/shard_map/ppermute | solution.py:40
  37.9 6.7 %collective-permute-start.19 = (bf16[192,128]{1,0:T(8,128)(2,1)S(1)}, bf16[192,128]{1,0:T(8,128)(2,1)S(1)}, u32[]{:S(2)}, u32[]{:S(2)}) collective-permute-start(bf16[192,128]{1,0:T(8,128)(2,1)S(1)} %get-tuple-element.46), channel_id=1, source_target_pairs={{0,8},{8,0},{16,24},{24,16},{1,9},{9,1},{17,25},{25,17},{2,10},{10... | collective-permute-start | bytes 147464 | tf_op jit(solution)/shard_map/ppermute | solution.py:40
  39.5 5.2 %collective-permute-start.18 = (bf16[192,128]{1,0:T(8,128)(2,1)S(1)}, bf16[192,128]{1,0:T(8,128)(2,1)S(1)}, u32[]{:S(2)}, u32[]{:S(2)}) collective-permute-start(bf16[192,128]{1,0:T(8,128)(2,1)S(1)} %get-tuple-element.46), channel_id=1, source_target_pairs={{0,24},{8,16},{16,8},{24,0},{1,25},{9,17},{17,9},{25,1},{2,26},{10... | collective-permute-start | bytes 147464 | tf_op jit(solution)/shard_map/ppermute | solution.py:40
  40.7 3.9 %collective-permute-start.20 = (bf16[64,128]{1,0:T(8,128)(2,1)S(1)}, bf16[64,128]{1,0:T(8,128)(2,1)S(1)}, u32[]{:S(2)}, u32[]{:S(2)}) collective-permute-start(bf16[64,128]{1,0:T(8,128)(2,1)S(1)} %get-tuple-element.47.refs_0_), channel_id=1, source_target_pairs={{0,16},{8,24},{16,0},{24,8},{1,17},{9,25},{17,1},{25,9},{2,18},{10... | collective-permute-start | bytes 49160 | tf_op jit(solution)/shard_map/ppermute | solution.py:40
  45.4 1.4 %collective-permute-start.21 = (bf16[2,128,128]{2,1,0:T(8,128)(2,1)S(1)}, bf16[2,128,128]{2,1,0:T(8,128)(2,1)S(1)}, u32[]{:S(2)}, u32[]{:S(2)}) collective-permute-start(bf16[2,128,128]{2,1,0:T(8,128)(2,1)S(1)} %get-tuple-element.50), channel_id=1, source_target_pairs={{0,1},{1,0},{2,3},{3,2},{4,5},{5,4},{6,7},{7,6},{8,9},{9,8},{10,11... | collective-permute-start | bytes 196616 | tf_op jit(solution)/shard_map/ppermute | solution.py:40
  46.3 3.2 %collective-permute-start.22 = (bf16[2,128,128]{2,1,0:T(8,128)(2,1)S(1)}, bf16[2,128,128]{2,1,0:T(8,128)(2,1)S(1)}, u32[]{:S(2)}, u32[]{:S(2)}) collective-permute-start(bf16[2,128,128]{2,1,0:T(8,128)(2,1)S(1)} %get-tuple-element.53), channel_id=1, source_target_pairs={{0,1},{1,0},{2,3},{3,2},{4,5},{5,4},{6,7},{7,6},{8,9},{9,8},{10,11... | collective-permute-start | bytes 196616 | tf_op jit(solution)/shard_map/ppermute | solution.py:40
  46.8 5.3 %collective-permute-start.23 = (bf16[1,128,128]{2,1,0:T(8,128)(2,1)S(1)}, bf16[1,128,128]{2,1,0:T(8,128)(2,1)S(1)}, u32[]{:S(2)}, u32[]{:S(2)}) collective-permute-start(bf16[1,128,128]{2,1,0:T(8,128)(2,1)S(1)} %get-tuple-element.51.refs_0_), channel_id=1, source_target_pairs={{0,7},{1,6},{2,5},{3,4},{4,3},{5,2},{6,1},{7,0},{8,15},{9,14},{10,... | collective-permute-start | bytes 98312 | tf_op jit(solution)/shard_map/ppermute | solution.py:40
  49.0 4.5 %collective-permute-start.24 = (bf16[1,128,128]{2,1,0:T(8,128)(2,1)S(1)}, bf16[1,128,128]{2,1,0:T(8,128)(2,1)S(1)}, u32[]{:S(2)}, u32[]{:S(2)}) collective-permute-start(bf16[1,128,128]{2,1,0:T(8,128)(2,1)S(1)} %get-tuple-element.52.refs_1_), channel_id=1, source_target_pairs={{0,5},{1,4},{2,7},{3,6},{4,1},{5,0},{6,3},{7,2},{8,13},{9,12},{10,... | collective-permute-start | bytes 98312 | tf_op jit(solution)/shard_map/ppermute | solution.py:40
  49.5 4.0 %collective-permute-start.25 = (bf16[1,128,128]{2,1,0:T(8,128)(2,1)S(1)}, bf16[1,128,128]{2,1,0:T(8,128)(2,1)S(1)}, u32[]{:S(2)}, u32[]{:S(2)}) collective-permute-start(bf16[1,128,128]{2,1,0:T(8,128)(2,1)S(1)} %get-tuple-element.55), channel_id=1, source_target_pairs={{0,3},{1,2},{2,1},{3,0},{4,7},{5,6},{6,5},{7,4},{8,11},{9,10},{10,... | collective-permute-start | bytes 98312 | tf_op jit(solution)/shard_map/ppermute | solution.py:40

commit v14 on v11

--- a/solution.py
+++ b/solution.py
@@ -324,7 +324,8 @@
         last = step == ITERS - 1
         away = sorted(range(half, near), reverse=last)
         order = list(range(1, near))
-        order.sort(key=lambda mask: (mask == half, mask))
+        if step == 0:
+            order.sort(key=lambda mask: (mask == half, mask))
         parts = [cross(short, mask) for mask in order]
         twin = swap(short, "tile", 1)
         diag = first([short], [(0, False)])

time: 53.6 us -> 54.9 us (1.024)
  waiting for transfers between devices: 13.6 us -> 14.4 us
  starting transfers between devices: 25.4 us -> 26 us
    ppermute x26, waiting for transfers between devices: 13.6 us -> 14.4 us  [swap(): lax.ppermute(value, axis, [(i, i ^ mask) for i in range(lax.axis_size(axi...]
  transfers between devices with their start and end apart: 26 -> 26, of which waited for: 11 -> 12; matrix products, arithmetic and copies ran while one was open for 0% -> 0% of each run, Pallas kernels for 12% -> 12%
where the time goes in v14:
time: 54.9 us; the launch traced here: 54.7 us
  starting transfers between devices  26 us (47%)
  waiting for transfers between devices  14.4 us (26%)
  Pallas kernels  10.4 us (19%)
  local copies, waits for them, and re-layouts  2.21 us (4%)
  between operations  0.88 us (2%)
  other arithmetic  0.85 us (2%)
    ppermute x26, starting transfers between devices, swap(): lax.ppermute(value, axis, [(i, i ^ mask) for i in range(lax.axis_size(axi...  26 us
    ppermute x26, waiting for transfers between devices, swap(): lax.ppermute(value, axis, [(i, i ^ mask) for i in range(lax.axis_size(axi...  14.4 us
    pallas_call x4, Pallas kernels, term(): call(partial(term_kernel, wanted, len(after)), in_specs=[pl.BlockSpec(mem...  2.59 us
    pallas_call x4, Pallas kernels, first(): call(partial(first_kernel, rows, spots, len(before)), shape(f32, blocks *...  2.37 us
    unnamed x8, local copies, waits for them, and re-layouts  2.21 us
    pallas_call x2, Pallas kernels, on_device(): call(partial(second_kernel, rows, cols, spots), (shape(bf16, pay_rows, wi...  1.75 us
    pallas_call x2, Pallas kernels, on_device(): call(partial(far_kernel, rows, cols, groups, ncells_all, spots_of(away, T...  1.45 us
  transfers between devices with their start and end apart: 26, of which 12 were waited for; matrix products, arithmetic and copies ran while one was open for 0% of the time, Pallas kernels for 12%

profile of v14, /device:TPU:0, one launch (start us, length us, event | category | flops | bytes accessed | tf_op | source)
XLA Modules:
  0.0 54.7 jit_solution(11120352881056347493)
XLA Ops:
  0.6 0.8 %fusion.refs_0_ = bf16[1,128,128]{2,1,0:T(8,128)(2,1)S(1)} fusion(f32[16,8,128]{2,1,0:T(8,128)} %param.4), kind=kLoop, calls=%fused_computation.1 | loop fusion | flops 32768 | bytes 98304 | tf_op jit(solution)/shard_map/convert_element_type | solution.py:277
  1.5 3.5 %collective-permute-start.3 = (bf16[1,128,128]{2,1,0:T(8,128)(2,1)S(1)}, bf16[1,128,128]{2,1,0:T(8,128)(2,1)S(1)}, u32[]{:S(2)}, u32[]{:S(2)}) collective-permute-start(bf16[1,128,128]{2,1,0:T(8,128)(2,1)S(1)} %fusion.refs_0_), channel_id=1, source_target_pairs={{0,5},{1,4},{2,7},{3,6},{4,1},{5,0},{6,3},{7,2},{8,13},{9,12},{10,... | collective-permute-start | bytes 98312 | tf_op jit(solution)/shard_map/ppermute | solution.py:40
  5.0 1.6 %collective-permute-start.2 = (bf16[1,128,128]{2,1,0:T(8,128)(2,1)S(1)}, bf16[1,128,128]{2,1,0:T(8,128)(2,1)S(1)}, u32[]{:S(2)}, u32[]{:S(2)}) collective-permute-start(bf16[1,128,128]{2,1,0:T(8,128)(2,1)S(1)} %fusion.refs_0_), channel_id=1, source_target_pairs={{0,7},{1,6},{2,5},{3,4},{4,3},{5,2},{6,1},{7,0},{8,15},{9,14},{10,... | collective-permute-start | bytes 98312 | tf_op jit(solution)/shard_map/ppermute | solution.py:40
  6.6 0.2 collective-permute-start.1
  6.8 2.2 %copy-done = bf16[256,8,1024]{2,1,0:T(8,128)(2,1)S(1)} copy-done((bf16[256,8,1024]{2,1,0:T(8,128)(2,1)S(1)}, bf16[256,8,1024]{2,1,0:T(8,128)(2,1)}, u32[]{:S(2)}) %copy-start) | copy-done | bytes 4194328
  9.0 0.4 load.1.factor_ref
  9.4 0.0 copy-start.1
  9.4 0.5 project_own.4.refs_0_.refs_2_
  9.9 0.0 collective-permute-done.3.refs_4_
  9.9 0.3 collective-permute-done.2.refs_3_
  10.2 0.2 collective-permute-done.1.refs_2_
  10.4 0.0 collective-permute-done.refs_1_.twin_ref
  10.4 0.7 %collective-permute-start.4 = (bf16[3,128,128]{2,1,0:T(8,128)(2,1)S(1)}, bf16[3,128,128]{2,1,0:T(8,128)(2,1)S(1)}, u32[]{:S(2)}, u32[]{:S(2)}) collective-permute-start(bf16[3,128,128]{2,1,0:T(8,128)(2,1)S(1)} %join.2.bundle_ref.refs_0_), channel_id=1, source_target_pairs={{0,1},{1,0},{2,3},{3,2},{4,5},{5,4},{6,7},{7,6},{8,9},{9,8},{10,11... | collective-permute-start | bytes 294920 | tf_op jit(solution)/shard_map/ppermute | solution.py:40
  11.1 0.4 columns.2
  11.5 0.0 copy-start.3
  11.5 0.7 %project_own.5.diag_ref = f32[256,128]{1,0:T(8,128)S(1)} custom-call(bf16[2048,1024]{1,0:T(8,128)(2,1)S(1)} %load.1.factor_ref, bf16[3,128,128]{2,1,0:T(8,128)(2,1)S(1)} %join.2.bundle_ref.refs_0_, bf16[1,128,128]{2,1,0:T(8,128)(2,1)S(1)} %collective-permute-done.refs_1_.twin_ref, f32[256,128]{1,0:T(8,128)S(1)} %project_own.4.refs_0_.refs_2_), custom_call_target="tpu_custom_call" | custom-call | flops 268435456 | bytes 2097152 | tf_op jit(solution)/shard_map/project_own/pallas_call | solution.py:314
  12.2 0.0 collective-permute-done.4.fields_ref
  12.2 0.9 %project_across.2 = (bf16[192,128]{1,0:T(8,128)(2,1)S(1)}, bf16[64,128]{1,0:T(8,128)(2,1)S(1)}) custom-call(bf16[2048,1024]{1,0:T(8,128)(2,1)S(1)} %load.1.factor_ref, f32[256,128]{1,0:T(8,128)S(1)} %project_own.5.diag_ref, bf16[3,128,128]{2,1,0:T(8,128)(2,1)S(1)} %collective-permute-done.4.fields_ref, bf16[128,128]{1,0:T(8,128)(2,1)S(1)} %get-tuple-element.31.short_ref), custom_call_target="tpu_custom_call" | custom-call | flops 268435456 | bytes 2097152 | tf_op jit(solution)/shard_map/project_across/pallas_call | solution.py:348
  13.1 2.5 %collective-permute-start.6 = (bf16[192,128]{1,0:T(8,128)(2,1)S(1)}, bf16[192,128]{1,0:T(8,128)(2,1)S(1)}, u32[]{:S(2)}, u32[]{:S(2)}) collective-permute-start(bf16[192,128]{1,0:T(8,128)(2,1)S(1)} %get-tuple-element.32), channel_id=1, source_target_pairs={{0,24},{8,16},{16,8},{24,0},{1,25},{9,17},{17,9},{25,1},{2,26},{10... | collective-permute-start | bytes 147464 | tf_op jit(solution)/shard_map/ppermute | solution.py:40
  15.6 0.5 collective-permute-start.5
  16.1 0.5 collective-permute-start.7
  16.6 3.2 %collective-permute-done.7.refs_2_ = bf16[64,128]{1,0:T(8,128)(2,1)S(1)} collective-permute-done((bf16[64,128]{1,0:T(8,128)(2,1)S(1)}, bf16[64,128]{1,0:T(8,128)(2,1)S(1)}, u32[]{:S(2)}, u32[]{:S(2)}) %collective-permute-start.7) | collective-permute-done | bytes 16416 | tf_op jit(solution)/shard_map/ppermute | solution.py:40
  19.9 0.0 collective-permute-done.6.refs_1_.refs_3_
  19.9 0.0 collective-permute-done.5.refs_0_.refs_1_
  19.9 0.7 %term_first.2 = (bf16[128,2048]{1,0:T(8,128)(2,1)S(1)}, bf16[2,128,128]{2,1,0:T(8,128)(2,1)S(1)}) custom-call(f32[1,256]{1,0:T(1,128)S(1)} %bitcast.13, bf16[2048,1024]{1,0:T(8,128)(2,1)S(1)} %load.1.factor_ref, bf16[64,128]{1,0:T(8,128)(2,1)S(1)} %get-tuple-element.33.refs_0_, bf16[192,128]{1,0:T(8,128)(2,1)S(1)} %collective-permute-done.5.refs_0_.refs_1_, ...), custom_call_target="tpu_custom_call" | custom-call | flops 134217728 | bytes 2097152 | tf_op jit(solution)/shard_map/term_first/pallas_call | solution.py:357
  20.6 0.1 collective-permute-start.8
  20.7 0.0 copy-start.2
  20.7 0.8 %term.4 = (f32[2,128,128]{2,1,0:T(8,128)S(1)}, bf16[2,128,128]{2,1,0:T(8,128)(2,1)S(1)}) custom-call(bf16[128,2048]{1,0:T(8,128)(2,1)S(1)} %get-tuple-element.34.coef_ref, bf16[2048,1024]{1,0:T(8,128)(2,1)S(1)} %load.1.factor_ref), custom_call_target="tpu_custom_call" | custom-call | flops 268435456 | bytes 2097152 | tf_op jit(solution)/shard_map/term/pallas_call | solution.py:367
  21.5 0.5 collective-permute-start.9
  22.1 1.8 %collective-permute-start.10 = (bf16[1,128,128]{2,1,0:T(8,128)(2,1)S(1)}, bf16[1,128,128]{2,1,0:T(8,128)(2,1)S(1)}, u32[]{:S(2)}, u32[]{:S(2)}) collective-permute-start(bf16[1,128,128]{2,1,0:T(8,128)(2,1)S(1)} %get-tuple-element.37.refs_0_), channel_id=1, source_target_pairs={{0,5},{1,4},{2,7},{3,6},{4,1},{5,0},{6,3},{7,2},{8,13},{9,12},{10,... | collective-permute-start | bytes 98312 | tf_op jit(solution)/shard_map/ppermute | solution.py:40
  23.8 1.4 %collective-permute-start.11 = (bf16[1,128,128]{2,1,0:T(8,128)(2,1)S(1)}, bf16[1,128,128]{2,1,0:T(8,128)(2,1)S(1)}, u32[]{:S(2)}, u32[]{:S(2)}) collective-permute-start(bf16[1,128,128]{2,1,0:T(8,128)(2,1)S(1)} %get-tuple-element.38.refs_1_), channel_id=1, source_target_pairs={{0,7},{1,6},{2,5},{3,4},{4,3},{5,2},{6,1},{7,0},{8,15},{9,14},{10,... | collective-permute-start | bytes 98312 | tf_op jit(solution)/shard_map/ppermute | solution.py:40
  25.2 0.5 term.5.mine_ref
  25.8 0.1 collective-permute-start.12
  25.8 0.2 local.2.base_ref
  26.0 0.5 collective-permute-done.10.refs_1_
  26.5 2.4 %collective-permute-done.11.refs_2_ = bf16[1,128,128]{2,1,0:T(8,128)(2,1)S(1)} collective-permute-done((bf16[1,128,128]{2,1,0:T(8,128)(2,1)S(1)}, bf16[1,128,128]{2,1,0:T(8,128)(2,1)S(1)}, u32[]{:S(2)}, u32[]{:S(2)}) %collective-permute-start.11) | collective-permute-done | bytes 32800 | tf_op jit(solution)/shard_map/ppermute | solution.py:40
  29.0 1.0 %collective-permute-done.12.refs_3_ = bf16[1,128,128]{2,1,0:T(8,128)(2,1)S(1)} collective-permute-done((bf16[1,128,128]{2,1,0:T(8,128)(2,1)S(1)}, bf16[1,128,128]{2,1,0:T(8,128)(2,1)S(1)}, u32[]{:S(2)}, u32[]{:S(2)}) %collective-permute-start.12) | collective-permute-done | bytes 32800 | tf_op jit(solution)/shard_map/ppermute | solution.py:40
  30.0 1.6 %collective-permute-start.16 = (bf16[1,128,128]{2,1,0:T(8,128)(2,1)S(1)}, bf16[1,128,128]{2,1,0:T(8,128)(2,1)S(1)}, u32[]{:S(2)}, u32[]{:S(2)}) collective-permute-start(bf16[1,128,128]{2,1,0:T(8,128)(2,1)S(1)} %get-tuple-element.43.refs_0_), channel_id=1, source_target_pairs={{0,7},{1,6},{2,5},{3,4},{4,3},{5,2},{6,1},{7,0},{8,15},{9,14},{10,... | collective-permute-start | bytes 98312 | tf_op jit(solution)/shard_map/ppermute | solution.py:40
  31.6 2.2 %collective-permute-start.14 = (bf16[1,128,128]{2,1,0:T(8,128)(2,1)S(1)}, bf16[1,128,128]{2,1,0:T(8,128)(2,1)S(1)}, u32[]{:S(2)}, u32[]{:S(2)}) collective-permute-start(bf16[1,128,128]{2,1,0:T(8,128)(2,1)S(1)} %get-tuple-element.43.refs_0_), channel_id=1, source_target_pairs={{0,3},{1,2},{2,1},{3,0},{4,7},{5,6},{6,5},{7,4},{8,11},{9,10},{10,... | collective-permute-start | bytes 98312 | tf_op jit(solution)/shard_map/ppermute | solution.py:40
  33.9 0.4 collective-permute-start.13
  34.3 0.5 project_own.6.refs_0_.refs_2_
  34.7 0.5 collective-permute-done.16.refs_4_
  35.2 1.6 %collective-permute-done.15.refs_3_ = bf16[1,128,128]{2,1,0:T(8,128)(2,1)S(1)} collective-permute-done((bf16[1,128,128]{2,1,0:T(8,128)(2,1)S(1)}, bf16[1,128,128]{2,1,0:T(8,128)(2,1)S(1)}, u32[]{:S(2)}, u32[]{:S(2)}) %collective-permute-start.15) | collective-permute-done | bytes 32800 | tf_op jit(solution)/shard_map/ppermute | solution.py:40
  36.9 0.2 collective-permute-start.17
  37.1 0.3 columns.3
  37.4 0.7 %project_own.7.diag_ref = f32[256,128]{1,0:T(8,128)S(1)} custom-call(bf16[2048,1024]{1,0:T(8,128)(2,1)S(1)} %load.1.factor_ref, bf16[3,128,128]{2,1,0:T(8,128)(2,1)S(1)} %join.3.bundle_ref.refs_0_, bf16[1,128,128]{2,1,0:T(8,128)(2,1)S(1)} %collective-permute-done.13.refs_1_.twin_ref, f32[256,128]{1,0:T(8,128)S(1)} %project_own.6.refs_0_.refs_2_), custom_call_target="tpu_custom_call" | custom-call | flops 268435456 | bytes 2097152 | tf_op jit(solution)/shard_map/project_own/pallas_call | solution.py:314
  38.2 0.1 collective-permute-done.17.fields_ref
  38.3 0.9 %project_across.3 = (bf16[192,128]{1,0:T(8,128)(2,1)S(1)}, bf16[64,128]{1,0:T(8,128)(2,1)S(1)}) custom-call(bf16[2048,1024]{1,0:T(8,128)(2,1)S(1)} %load.1.factor_ref, f32[256,128]{1,0:T(8,128)S(1)} %project_own.7.diag_ref, bf16[3,128,128]{2,1,0:T(8,128)(2,1)S(1)} %collective-permute-done.17.fields_ref, bf16[128,128]{1,0:T(8,128)(2,1)S(1)} %get-tuple-element.45.short_ref), custom_call_target="tpu_custom_call" | custom-call | flops 268435456 | bytes 2097152 | tf_op jit(solution)/shard_map/project_across/pallas_call | solution.py:348
  39.1 1.5 %collective-permute-start.19 = (bf16[192,128]{1,0:T(8,128)(2,1)S(1)}, bf16[192,128]{1,0:T(8,128)(2,1)S(1)}, u32[]{:S(2)}, u32[]{:S(2)}) collective-permute-start(bf16[192,128]{1,0:T(8,128)(2,1)S(1)} %get-tuple-element.46), channel_id=1, source_target_pairs={{0,24},{8,16},{16,8},{24,0},{1,25},{9,17},{17,9},{25,1},{2,26},{10... | collective-permute-start | bytes 147464 | tf_op jit(solution)/shard_map/ppermute | solution.py:40
  40.6 0.5 collective-permute-start.18
  41.1 1.5 %collective-permute-start.20 = (bf16[64,128]{1,0:T(8,128)(2,1)S(1)}, bf16[64,128]{1,0:T(8,128)(2,1)S(1)}, u32[]{:S(2)}, u32[]{:S(2)}) collective-permute-start(bf16[64,128]{1,0:T(8,128)(2,1)S(1)} %get-tuple-element.47.refs_0_), channel_id=1, source_target_pairs={{0,16},{8,24},{16,0},{24,8},{1,17},{9,25},{17,1},{25,9},{2,18},{10... | collective-permute-start | bytes 49160 | tf_op jit(solution)/shard_map/ppermute | solution.py:40
  42.7 2.2 %collective-permute-done.20.refs_2_ = bf16[64,128]{1,0:T(8,128)(2,1)S(1)} collective-permute-done((bf16[64,128]{1,0:T(8,128)(2,1)S(1)}, bf16[64,128]{1,0:T(8,128)(2,1)S(1)}, u32[]{:S(2)}, u32[]{:S(2)}) %collective-permute-start.20) | collective-permute-done | bytes 16416 | tf_op jit(solution)/shard_map/ppermute | solution.py:40
  44.9 0.7 %term_first.3 = (bf16[128,2048]{1,0:T(8,128)(2,1)S(1)}, bf16[2,128,128]{2,1,0:T(8,128)(2,1)S(1)}) custom-call(f32[1,256]{1,0:T(1,128)S(1)} %bitcast.14, bf16[2048,1024]{1,0:T(8,128)(2,1)S(1)} %load.1.factor_ref, bf16[64,128]{1,0:T(8,128)(2,1)S(1)} %get-tuple-element.47.refs_0_, bf16[192,128]{1,0:T(8,128)(2,1)S(1)} %collective-permute-done.18.refs_0_.refs_1_, ...), custom_call_target="tpu_custom_call" | custom-call | flops 134217728 | bytes 2097152 | tf_op jit(solution)/shard_map/term_first/pallas_call | solution.py:357
  45.6 0.1 collective-permute-start.21
  45.7 0.8 %term.6 = (f32[2,128,128]{2,1,0:T(8,128)S(1)}, bf16[2,128,128]{2,1,0:T(8,128)(2,1)S(1)}) custom-call(bf16[128,2048]{1,0:T(8,128)(2,1)S(1)} %get-tuple-element.48.coef_ref, bf16[2048,1024]{1,0:T(8,128)(2,1)S(1)} %load.1.factor_ref), custom_call_target="tpu_custom_call" | custom-call | flops 268435456 | bytes 2097152 | tf_op jit(solution)/shard_map/term/pallas_call | solution.py:367
  46.5 0.6 %collective-permute-start.22 = (bf16[2,128,128]{2,1,0:T(8,128)(2,1)S(1)}, bf16[2,128,128]{2,1,0:T(8,128)(2,1)S(1)}, u32[]{:S(2)}, u32[]{:S(2)}) collective-permute-start(bf16[2,128,128]{2,1,0:T(8,128)(2,1)S(1)} %get-tuple-element.53), channel_id=1, source_target_pairs={{0,1},{1,0},{2,3},{3,2},{4,5},{5,4},{6,7},{7,6},{8,9},{9,8},{10,11... | collective-permute-start | bytes 196616 | tf_op jit(solution)/shard_map/ppermute | solution.py:40
  47.1 1.6 %collective-permute-start.23 = (bf16[1,128,128]{2,1,0:T(8,128)(2,1)S(1)}, bf16[1,128,128]{2,1,0:T(8,128)(2,1)S(1)}, u32[]{:S(2)}, u32[]{:S(2)}) collective-permute-start(bf16[1,128,128]{2,1,0:T(8,128)(2,1)S(1)} %get-tuple-element.51.refs_0_), channel_id=1, source_target_pairs={{0,7},{1,6},{2,5},{3,4},{4,3},{5,2},{6,1},{7,0},{8,15},{9,14},{10,... | collective-permute-start | bytes 98312 | tf_op jit(solution)/shard_map/ppermute | solution.py:40
  48.6 0.4 collective-permute-start.24
  49.0 0.5 term.7.mine_ref
  49.6 1.9 %collective-permute-start.25 = (bf16[1,128,128]{2,1,0:T(8,128)(2,1)S(1)}, bf16[1,128,128]{2,1,0:T(8,128)(2,1)S(1)}, u32[]{:S(2)}, u32[]{:S(2)}) collective-permute-start(bf16[1,128,128]{2,1,0:T(8,128)(2,1)S(1)} %get-tuple-element.55), channel_id=1, source_target_pairs={{0,3},{1,2},{2,1},{3,0},{4,7},{5,6},{6,5},{7,4},{8,11},{9,10},{10,... | collective-permute-start | bytes 98312 | tf_op jit(solution)/shard_map/ppermute | solution.py:40
  51.5 0.2 local.3.base_ref
  51.6 0.8 %collective-permute-done.23.refs_1_ = bf16[1,128,128]{2,1,0:T(8,128)(2,1)S(1)} collective-permute-done((bf16[1,128,128]{2,1,0:T(8,128)(2,1)S(1)}, bf16[1,128,128]{2,1,0:T(8,128)(2,1)S(1)}, u32[]{:S(2)}, u32[]{:S(2)}) %collective-permute-start.23) | collective-permute-done | bytes 32800 | tf_op jit(solution)/shard_map/ppermute | solution.py:40
  52.4 1.6 %collective-permute-done.24.refs_2_ = bf16[1,128,128]{2,1,0:T(8,128)(2,1)S(1)} collective-permute-done((bf16[1,128,128]{2,1,0:T(8,128)(2,1)S(1)}, bf16[1,128,128]{2,1,0:T(8,128)(2,1)S(1)}, u32[]{:S(2)}, u32[]{:S(2)}) %collective-permute-start.24) | collective-permute-done | bytes 32800 | tf_op jit(solution)/shard_map/ppermute | solution.py:40
  54.0 0.7 %update.3 = (f32[128,128]{1,0:T(8,128)}, f32[128,128]{1,0:T(8,128)}) custom-call(f32[128,128]{1,0:T(8,128)S(1)} %get-tuple-element.42.x_ref, f32[128,128]{1,0:T(8,128)S(1)} %local.3.base_ref, f32[1,128,128]{2,1,0:T(8,128)S(1)} %get-tuple-element.54.refs_0_, bf16[1,128,128]{2,1,0:T(8,128)(2,1)S(1)} %collective-permute-done.23.refs_1_, ...), custom_call_target="tpu_custom_call" | custom-call | bytes 262144 | tf_op jit(solution)/shard_map/update/pallas_call | solution.py:395
  (22 shorter events, 0.1 us)
Async XLA Ops:
  1.5 8.4 %collective-permute-start.3 = (bf16[1,128,128]{2,1,0:T(8,128)(2,1)S(1)}, bf16[1,128,128]{2,1,0:T(8,128)(2,1)S(1)}, u32[]{:S(2)}, u32[]{:S(2)}) collective-permute-start(bf16[1,128,128]{2,1,0:T(8,128)(2,1)S(1)} %fusion.refs_0_), channel_id=1, source_target_pairs={{0,5},{1,4},{2,7},{3,6},{4,1},{5,0},{6,3},{7,2},{8,13},{9,12},{10,... | collective-permute-start | bytes 98312 | tf_op jit(solution)/shard_map/ppermute | solution.py:40
  5.0 5.2 %collective-permute-start.2 = (bf16[1,128,128]{2,1,0:T(8,128)(2,1)S(1)}, bf16[1,128,128]{2,1,0:T(8,128)(2,1)S(1)}, u32[]{:S(2)}, u32[]{:S(2)}) collective-permute-start(bf16[1,128,128]{2,1,0:T(8,128)(2,1)S(1)} %fusion.refs_0_), channel_id=1, source_target_pairs={{0,7},{1,6},{2,5},{3,4},{4,3},{5,2},{6,1},{7,0},{8,15},{9,14},{10,... | collective-permute-start | bytes 98312 | tf_op jit(solution)/shard_map/ppermute | solution.py:40
  6.6 3.8 %collective-permute-start.1 = (bf16[1,128,128]{2,1,0:T(8,128)(2,1)S(1)}, bf16[1,128,128]{2,1,0:T(8,128)(2,1)S(1)}, u32[]{:S(2)}, u32[]{:S(2)}) collective-permute-start(bf16[1,128,128]{2,1,0:T(8,128)(2,1)S(1)} %fusion.refs_0_), channel_id=1, source_target_pairs={{0,3},{1,2},{2,1},{3,0},{4,7},{5,6},{6,5},{7,4},{8,11},{9,10},{10,... | collective-permute-start | bytes 98312 | tf_op jit(solution)/shard_map/ppermute | solution.py:40
  6.8 3.5 %collective-permute-start = (bf16[1,128,128]{2,1,0:T(8,128)(2,1)S(1)}, bf16[1,128,128]{2,1,0:T(8,128)(2,1)S(1)}, u32[]{:S(2)}, u32[]{:S(2)}) collective-permute-start(bf16[1,128,128]{2,1,0:T(8,128)(2,1)S(1)} %fusion.refs_0_), channel_id=1, source_target_pairs={{0,1},{1,0},{2,3},{3,2},{4,5},{5,4},{6,7},{7,6},{8,9},{9,8},{10,11... | collective-permute-start | bytes 98312 | tf_op jit(solution)/shard_map/ppermute | solution.py:40
  6.8 2.2 %copy-start = (bf16[256,8,1024]{2,1,0:T(8,128)(2,1)S(1)}, bf16[256,8,1024]{2,1,0:T(8,128)(2,1)}, u32[]{:S(2)}) copy-start(bf16[256,8,1024]{2,1,0:T(8,128)(2,1)} %param.6) | copy-start | bytes 12582916
  9.4 1.7 %copy-start.1 = (f32[16,8,128]{2,1,0:T(8,128)S(1)}, f32[16,8,128]{2,1,0:T(8,128)}, u32[]{:S(2)}) copy-start(f32[16,8,128]{2,1,0:T(8,128)} %param.4) | copy-start | bytes 196612
  10.4 1.8 %collective-permute-start.4 = (bf16[3,128,128]{2,1,0:T(8,128)(2,1)S(1)}, bf16[3,128,128]{2,1,0:T(8,128)(2,1)S(1)}, u32[]{:S(2)}, u32[]{:S(2)}) collective-permute-start(bf16[3,128,128]{2,1,0:T(8,128)(2,1)S(1)} %join.2.bundle_ref.refs_0_), channel_id=1, source_target_pairs={{0,1},{1,0},{2,3},{3,2},{4,5},{5,4},{6,7},{7,6},{8,9},{9,8},{10,11... | collective-permute-start | bytes 294920 | tf_op jit(solution)/shard_map/ppermute | solution.py:40
  11.5 8.4 %copy-start.3 = (f32[256]{0:T(256)S(1)}, f32[256]{0:T(256)}, u32[]{:S(2)}) copy-start(f32[256]{0:T(256)} %param.7) | copy-start | bytes 3076
  13.1 6.8 %collective-permute-start.6 = (bf16[192,128]{1,0:T(8,128)(2,1)S(1)}, bf16[192,128]{1,0:T(8,128)(2,1)S(1)}, u32[]{:S(2)}, u32[]{:S(2)}) collective-permute-start(bf16[192,128]{1,0:T(8,128)(2,1)S(1)} %get-tuple-element.32), channel_id=1, source_target_pairs={{0,24},{8,16},{16,8},{24,0},{1,25},{9,17},{17,9},{25,1},{2,26},{10... | collective-permute-start | bytes 147464 | tf_op jit(solution)/shard_map/ppermute | solution.py:40
  15.6 4.3 %collective-permute-start.5 = (bf16[192,128]{1,0:T(8,128)(2,1)S(1)}, bf16[192,128]{1,0:T(8,128)(2,1)S(1)}, u32[]{:S(2)}, u32[]{:S(2)}) collective-permute-start(bf16[192,128]{1,0:T(8,128)(2,1)S(1)} %get-tuple-element.32), channel_id=1, source_target_pairs={{0,8},{8,0},{16,24},{24,16},{1,9},{9,1},{17,25},{25,17},{2,10},{10... | collective-permute-start | bytes 147464 | tf_op jit(solution)/shard_map/ppermute | solution.py:40
  16.1 3.7 %collective-permute-start.7 = (bf16[64,128]{1,0:T(8,128)(2,1)S(1)}, bf16[64,128]{1,0:T(8,128)(2,1)S(1)}, u32[]{:S(2)}, u32[]{:S(2)}) collective-permute-start(bf16[64,128]{1,0:T(8,128)(2,1)S(1)} %get-tuple-element.33.refs_0_), channel_id=1, source_target_pairs={{0,16},{8,24},{16,0},{24,8},{1,17},{9,25},{17,1},{25,9},{2,18},{10... | collective-permute-start | bytes 49160 | tf_op jit(solution)/shard_map/ppermute | solution.py:40
  20.6 1.4 %collective-permute-start.8 = (bf16[2,128,128]{2,1,0:T(8,128)(2,1)S(1)}, bf16[2,128,128]{2,1,0:T(8,128)(2,1)S(1)}, u32[]{:S(2)}, u32[]{:S(2)}) collective-permute-start(bf16[2,128,128]{2,1,0:T(8,128)(2,1)S(1)} %get-tuple-element.36), channel_id=1, source_target_pairs={{0,1},{1,0},{2,3},{3,2},{4,5},{5,4},{6,7},{7,6},{8,9},{9,8},{10,11... | collective-permute-start | bytes 196616 | tf_op jit(solution)/shard_map/ppermute | solution.py:40
  20.7 5.2 %copy-start.2 = (f32[8,128]{1,0:T(8,128)S(1)}, f32[8,128]{1,0:T(8,128)}, u32[]{:S(2)}) copy-start(f32[8,128]{1,0:T(8,128)} %amp_ref.3) | copy-start | bytes 12292
  21.5 4.2 %collective-permute-start.9 = (bf16[2,128,128]{2,1,0:T(8,128)(2,1)S(1)}, bf16[2,128,128]{2,1,0:T(8,128)(2,1)S(1)}, u32[]{:S(2)}, u32[]{:S(2)}) collective-permute-start(bf16[2,128,128]{2,1,0:T(8,128)(2,1)S(1)} %get-tuple-element.39), channel_id=1, source_target_pairs={{0,1},{1,0},{2,3},{3,2},{4,5},{5,4},{6,7},{7,6},{8,9},{9,8},{10,11... | collective-permute-start | bytes 196616 | tf_op jit(solution)/shard_map/ppermute | solution.py:40
  22.1 4.5 %collective-permute-start.10 = (bf16[1,128,128]{2,1,0:T(8,128)(2,1)S(1)}, bf16[1,128,128]{2,1,0:T(8,128)(2,1)S(1)}, u32[]{:S(2)}, u32[]{:S(2)}) collective-permute-start(bf16[1,128,128]{2,1,0:T(8,128)(2,1)S(1)} %get-tuple-element.37.refs_0_), channel_id=1, source_target_pairs={{0,5},{1,4},{2,7},{3,6},{4,1},{5,0},{6,3},{7,2},{8,13},{9,12},{10,... | collective-permute-start | bytes 98312 | tf_op jit(solution)/shard_map/ppermute | solution.py:40
  23.8 5.1 %collective-permute-start.11 = (bf16[1,128,128]{2,1,0:T(8,128)(2,1)S(1)}, bf16[1,128,128]{2,1,0:T(8,128)(2,1)S(1)}, u32[]{:S(2)}, u32[]{:S(2)}) collective-permute-start(bf16[1,128,128]{2,1,0:T(8,128)(2,1)S(1)} %get-tuple-element.38.refs_1_), channel_id=1, source_target_pairs={{0,7},{1,6},{2,5},{3,4},{4,3},{5,2},{6,1},{7,0},{8,15},{9,14},{10,... | collective-permute-start | bytes 98312 | tf_op jit(solution)/shard_map/ppermute | solution.py:40
  25.8 4.2 %collective-permute-start.12 = (bf16[1,128,128]{2,1,0:T(8,128)(2,1)S(1)}, bf16[1,128,128]{2,1,0:T(8,128)(2,1)S(1)}, u32[]{:S(2)}, u32[]{:S(2)}) collective-permute-start(bf16[1,128,128]{2,1,0:T(8,128)(2,1)S(1)} %get-tuple-element.41), channel_id=1, source_target_pairs={{0,3},{1,2},{2,1},{3,0},{4,7},{5,6},{6,5},{7,4},{8,11},{9,10},{10,... | collective-permute-start | bytes 98312 | tf_op jit(solution)/shard_map/ppermute | solution.py:40
  30.0 5.3 %collective-permute-start.16 = (bf16[1,128,128]{2,1,0:T(8,128)(2,1)S(1)}, bf16[1,128,128]{2,1,0:T(8,128)(2,1)S(1)}, u32[]{:S(2)}, u32[]{:S(2)}) collective-permute-start(bf16[1,128,128]{2,1,0:T(8,128)(2,1)S(1)} %get-tuple-element.43.refs_0_), channel_id=1, source_target_pairs={{0,7},{1,6},{2,5},{3,4},{4,3},{5,2},{6,1},{7,0},{8,15},{9,14},{10,... | collective-permute-start | bytes 98312 | tf_op jit(solution)/shard_map/ppermute | solution.py:40
  31.6 5.3 %collective-permute-start.15 = (bf16[1,128,128]{2,1,0:T(8,128)(2,1)S(1)}, bf16[1,128,128]{2,1,0:T(8,128)(2,1)S(1)}, u32[]{:S(2)}, u32[]{:S(2)}) collective-permute-start(bf16[1,128,128]{2,1,0:T(8,128)(2,1)S(1)} %get-tuple-element.43.refs_0_), channel_id=1, source_target_pairs={{0,5},{1,4},{2,7},{3,6},{4,1},{5,0},{6,3},{7,2},{8,13},{9,12},{10,... | collective-permute-start | bytes 98312 | tf_op jit(solution)/shard_map/ppermute | solution.py:40
  31.6 5.3 %collective-permute-start.14 = (bf16[1,128,128]{2,1,0:T(8,128)(2,1)S(1)}, bf16[1,128,128]{2,1,0:T(8,128)(2,1)S(1)}, u32[]{:S(2)}, u32[]{:S(2)}) collective-permute-start(bf16[1,128,128]{2,1,0:T(8,128)(2,1)S(1)} %get-tuple-element.43.refs_0_), channel_id=1, source_target_pairs={{0,3},{1,2},{2,1},{3,0},{4,7},{5,6},{6,5},{7,4},{8,11},{9,10},{10,... | collective-permute-start | bytes 98312 | tf_op jit(solution)/shard_map/ppermute | solution.py:40
  33.9 3.0 %collective-permute-start.13 = (bf16[1,128,128]{2,1,0:T(8,128)(2,1)S(1)}, bf16[1,128,128]{2,1,0:T(8,128)(2,1)S(1)}, u32[]{:S(2)}, u32[]{:S(2)}) collective-permute-start(bf16[1,128,128]{2,1,0:T(8,128)(2,1)S(1)} %get-tuple-element.43.refs_0_), channel_id=1, source_target_pairs={{0,1},{1,0},{2,3},{3,2},{4,5},{5,4},{6,7},{7,6},{8,9},{9,8},{10,11... | collective-permute-start | bytes 98312 | tf_op jit(solution)/shard_map/ppermute | solution.py:40
  36.9 1.4 %collective-permute-start.17 = (bf16[3,128,128]{2,1,0:T(8,128)(2,1)S(1)}, bf16[3,128,128]{2,1,0:T(8,128)(2,1)S(1)}, u32[]{:S(2)}, u32[]{:S(2)}) collective-permute-start(bf16[3,128,128]{2,1,0:T(8,128)(2,1)S(1)} %join.3.bundle_ref.refs_0_), channel_id=1, source_target_pairs={{0,1},{1,0},{2,3},{3,2},{4,5},{5,4},{6,7},{7,6},{8,9},{9,8},{10,11... | collective-permute-start | bytes 294920 | tf_op jit(solution)/shard_map/ppermute | solution.py:40
  39.1 5.7 %collective-permute-start.19 = (bf16[192,128]{1,0:T(8,128)(2,1)S(1)}, bf16[192,128]{1,0:T(8,128)(2,1)S(1)}, u32[]{:S(2)}, u32[]{:S(2)}) collective-permute-start(bf16[192,128]{1,0:T(8,128)(2,1)S(1)} %get-tuple-element.46), channel_id=1, source_target_pairs={{0,24},{8,16},{16,8},{24,0},{1,25},{9,17},{17,9},{25,1},{2,26},{10... | collective-permute-start | bytes 147464 | tf_op jit(solution)/shard_map/ppermute | solution.py:40
  40.6 4.3 %collective-permute-start.18 = (bf16[192,128]{1,0:T(8,128)(2,1)S(1)}, bf16[192,128]{1,0:T(8,128)(2,1)S(1)}, u32[]{:S(2)}, u32[]{:S(2)}) collective-permute-start(bf16[192,128]{1,0:T(8,128)(2,1)S(1)} %get-tuple-element.46), channel_id=1, source_target_pairs={{0,8},{8,0},{16,24},{24,16},{1,9},{9,1},{17,25},{25,17},{2,10},{10... | collective-permute-start | bytes 147464 | tf_op jit(solution)/shard_map/ppermute | solution.py:40
  41.1 3.7 %collective-permute-start.20 = (bf16[64,128]{1,0:T(8,128)(2,1)S(1)}, bf16[64,128]{1,0:T(8,128)(2,1)S(1)}, u32[]{:S(2)}, u32[]{:S(2)}) collective-permute-start(bf16[64,128]{1,0:T(8,128)(2,1)S(1)} %get-tuple-element.47.refs_0_), channel_id=1, source_target_pairs={{0,16},{8,24},{16,0},{24,8},{1,17},{9,25},{17,1},{25,9},{2,18},{10... | collective-permute-start | bytes 49160 | tf_op jit(solution)/shard_map/ppermute | solution.py:40
  45.6 1.4 %collective-permute-start.21 = (bf16[2,128,128]{2,1,0:T(8,128)(2,1)S(1)}, bf16[2,128,128]{2,1,0:T(8,128)(2,1)S(1)}, u32[]{:S(2)}, u32[]{:S(2)}) collective-permute-start(bf16[2,128,128]{2,1,0:T(8,128)(2,1)S(1)} %get-tuple-element.50), channel_id=1, source_target_pairs={{0,1},{1,0},{2,3},{3,2},{4,5},{5,4},{6,7},{7,6},{8,9},{9,8},{10,11... | collective-permute-start | bytes 196616 | tf_op jit(solution)/shard_map/ppermute | solution.py:40
  46.5 3.1 %collective-permute-start.22 = (bf16[2,128,128]{2,1,0:T(8,128)(2,1)S(1)}, bf16[2,128,128]{2,1,0:T(8,128)(2,1)S(1)}, u32[]{:S(2)}, u32[]{:S(2)}) collective-permute-start(bf16[2,128,128]{2,1,0:T(8,128)(2,1)S(1)} %get-tuple-element.53), channel_id=1, source_target_pairs={{0,1},{1,0},{2,3},{3,2},{4,5},{5,4},{6,7},{7,6},{8,9},{9,8},{10,11... | collective-permute-start | bytes 196616 | tf_op jit(solution)/shard_map/ppermute | solution.py:40
  47.1 5.3 %collective-permute-start.23 = (bf16[1,128,128]{2,1,0:T(8,128)(2,1)S(1)}, bf16[1,128,128]{2,1,0:T(8,128)(2,1)S(1)}, u32[]{:S(2)}, u32[]{:S(2)}) collective-permute-start(bf16[1,128,128]{2,1,0:T(8,128)(2,1)S(1)} %get-tuple-element.51.refs_0_), channel_id=1, source_target_pairs={{0,7},{1,6},{2,5},{3,4},{4,3},{5,2},{6,1},{7,0},{8,15},{9,14},{10,... | collective-permute-start | bytes 98312 | tf_op jit(solution)/shard_map/ppermute | solution.py:40
  48.6 5.4 %collective-permute-start.24 = (bf16[1,128,128]{2,1,0:T(8,128)(2,1)S(1)}, bf16[1,128,128]{2,1,0:T(8,128)(2,1)S(1)}, u32[]{:S(2)}, u32[]{:S(2)}) collective-permute-start(bf16[1,128,128]{2,1,0:T(8,128)(2,1)S(1)} %get-tuple-element.52.refs_1_), channel_id=1, source_target_pairs={{0,5},{1,4},{2,7},{3,6},{4,1},{5,0},{6,3},{7,2},{8,13},{9,12},{10,... | collective-permute-start | bytes 98312 | tf_op jit(solution)/shard_map/ppermute | solution.py:40
  49.6 4.4 %collective-permute-start.25 = (bf16[1,128,128]{2,1,0:T(8,128)(2,1)S(1)}, bf16[1,128,128]{2,1,0:T(8,128)(2,1)S(1)}, u32[]{:S(2)}, u32[]{:S(2)}) collective-permute-start(bf16[1,128,128]{2,1,0:T(8,128)(2,1)S(1)} %get-tuple-element.55), channel_id=1, source_target_pairs={{0,3},{1,2},{2,1},{3,0},{4,7},{5,6},{6,5},{7,4},{8,11},{9,10},{10,... | collective-permute-start | bytes 98312 | tf_op jit(solution)/shard_map/ppermute | solution.py:40

commit v15 on v11

--- a/solution.py
+++ b/solution.py
@@ -302,7 +302,6 @@
         name="load",
     )(flat)
     half = near // 2
-    close = list(range(half))
 
     def spots_of(masks, other):
         return [(mask, other != (mask > 0)) for mask in masks]
@@ -322,7 +321,8 @@
     for step in range(ITERS):
         halve = step == 0
         last = step == ITERS - 1
-        away = sorted(range(half, near), reverse=last)
+        close = list(range(half if last else 1))
+        away = sorted(range(half, near), reverse=last) + list(range(len(close), half))
         order = list(range(1, near))
         order.sort(key=lambda mask: (mask == half, mask))
         parts = [cross(short, mask) for mask in order]
@@ -355,7 +355,7 @@
         pays = [swap(part if mask & (mask + 1) else pay, "grp", mask) for mask in range(1, groups)]
         coef, far = call(
             partial(far_kernel, rows, cols, groups, ncells_all, spots_of(away, True)),
-            (shape(bf16, lines, ranks * rows), shape(bf16, half, lines, width)),
+            (shape(bf16, lines, ranks * rows), shape(bf16, len(away), lines, width)),
             flops=work // 2,
             moved=flat.size,
             name="term_first",

time: 53.6 us -> 53.5 us (level)
  transfers between devices with their start and end apart: 26 -> 26, of which waited for: 11 -> 10; matrix products, arithmetic and copies ran while one was open for 0% -> 0% of each run, Pallas kernels for 12% -> 12%
where the time goes in v15:
time: 53.5 us; the launch traced here: 53.3 us
  starting transfers between devices  25.3 us (47%)
  waiting for transfers between devices  13.7 us (26%)
  Pallas kernels  10.4 us (19%)
  local copies, waits for them, and re-layouts  2.21 us (4%)
  between operations  0.87 us (2%)
  other arithmetic  0.85 us (2%)
    ppermute x26, starting transfers between devices, swap(): lax.ppermute(value, axis, [(i, i ^ mask) for i in range(lax.axis_size(axi...  25.3 us
    ppermute x26, waiting for transfers between devices, swap(): lax.ppermute(value, axis, [(i, i ^ mask) for i in range(lax.axis_size(axi...  13.7 us
    pallas_call x4, Pallas kernels, term(): call(partial(term_kernel, wanted, len(after)), in_specs=[pl.BlockSpec(mem...  2.45 us
    pallas_call x4, Pallas kernels, first(): call(partial(first_kernel, rows, spots, len(before)), shape(f32, blocks *...  2.37 us
    unnamed x8, local copies, waits for them, and re-layouts  2.21 us
    pallas_call x2, Pallas kernels, on_device(): call(partial(second_kernel, rows, cols, spots), (shape(bf16, pay_rows, wi...  1.75 us
    pallas_call x2, Pallas kernels, on_device(): call(partial(far_kernel, rows, cols, groups, ncells_all, spots_of(away, T...  1.59 us
  transfers between devices with their start and end apart: 26, of which 10 were waited for; matrix products, arithmetic and copies ran while one was open for 0% of the time, Pallas kernels for 12%

profile of v15, /device:TPU:0, one launch (start us, length us, event | category | flops | bytes accessed | tf_op | source)
XLA Modules:
  0.0 53.3 jit_solution(11018776063096941399)
XLA Ops:
  0.6 0.8 %fusion.refs_0_ = bf16[1,128,128]{2,1,0:T(8,128)(2,1)S(1)} fusion(f32[16,8,128]{2,1,0:T(8,128)} %param.4), kind=kLoop, calls=%fused_computation.1 | loop fusion | flops 32768 | bytes 98304 | tf_op jit(solution)/shard_map/convert_element_type | solution.py:277
  1.5 3.5 %collective-permute-start.3 = (bf16[1,128,128]{2,1,0:T(8,128)(2,1)S(1)}, bf16[1,128,128]{2,1,0:T(8,128)(2,1)S(1)}, u32[]{:S(2)}, u32[]{:S(2)}) collective-permute-start(bf16[1,128,128]{2,1,0:T(8,128)(2,1)S(1)} %fusion.refs_0_), channel_id=1, source_target_pairs={{0,5},{1,4},{2,7},{3,6},{4,1},{5,0},{6,3},{7,2},{8,13},{9,12},{10,... | collective-permute-start | bytes 98312 | tf_op jit(solution)/shard_map/ppermute | solution.py:40
  5.0 1.6 %collective-permute-start.2 = (bf16[1,128,128]{2,1,0:T(8,128)(2,1)S(1)}, bf16[1,128,128]{2,1,0:T(8,128)(2,1)S(1)}, u32[]{:S(2)}, u32[]{:S(2)}) collective-permute-start(bf16[1,128,128]{2,1,0:T(8,128)(2,1)S(1)} %fusion.refs_0_), channel_id=1, source_target_pairs={{0,7},{1,6},{2,5},{3,4},{4,3},{5,2},{6,1},{7,0},{8,15},{9,14},{10,... | collective-permute-start | bytes 98312 | tf_op jit(solution)/shard_map/ppermute | solution.py:40
  6.6 0.2 collective-permute-start.1
  6.8 0.0 collective-permute-start
  6.8 2.2 %copy-done = bf16[256,8,1024]{2,1,0:T(8,128)(2,1)S(1)} copy-done((bf16[256,8,1024]{2,1,0:T(8,128)(2,1)S(1)}, bf16[256,8,1024]{2,1,0:T(8,128)(2,1)}, u32[]{:S(2)}) %copy-start) | copy-done | bytes 4194328
  9.0 0.4 load.1.factor_ref
  9.4 0.0 copy-start.1
  9.4 0.5 project_own.4.refs_0_.refs_2_
  9.9 0.3 collective-permute-done.2.refs_3_
  10.2 0.2 collective-permute-done.1.refs_2_
  10.4 0.0 collective-permute-done.refs_1_.twin_ref
  10.4 0.7 %collective-permute-start.4 = (bf16[3,128,128]{2,1,0:T(8,128)(2,1)S(1)}, bf16[3,128,128]{2,1,0:T(8,128)(2,1)S(1)}, u32[]{:S(2)}, u32[]{:S(2)}) collective-permute-start(bf16[3,128,128]{2,1,0:T(8,128)(2,1)S(1)} %join.2.bundle_ref.refs_0_), channel_id=1, source_target_pairs={{0,1},{1,0},{2,3},{3,2},{4,5},{5,4},{6,7},{7,6},{8,9},{9,8},{10,11... | collective-permute-start | bytes 294920 | tf_op jit(solution)/shard_map/ppermute | solution.py:40
  11.1 0.4 columns.2
  11.5 0.0 copy-start.3
  11.5 0.7 %project_own.5.diag_ref = f32[256,128]{1,0:T(8,128)S(1)} custom-call(bf16[2048,1024]{1,0:T(8,128)(2,1)S(1)} %load.1.factor_ref, bf16[3,128,128]{2,1,0:T(8,128)(2,1)S(1)} %join.2.bundle_ref.refs_0_, bf16[1,128,128]{2,1,0:T(8,128)(2,1)S(1)} %collective-permute-done.refs_1_.twin_ref, f32[256,128]{1,0:T(8,128)S(1)} %project_own.4.refs_0_.refs_2_), custom_call_target="tpu_custom_call" | custom-call | flops 268435456 | bytes 2097152 | tf_op jit(solution)/shard_map/project_own/pallas_call | solution.py:313
  12.2 0.9 %project_across.2 = (bf16[192,128]{1,0:T(8,128)(2,1)S(1)}, bf16[64,128]{1,0:T(8,128)(2,1)S(1)}) custom-call(bf16[2048,1024]{1,0:T(8,128)(2,1)S(1)} %load.1.factor_ref, f32[256,128]{1,0:T(8,128)S(1)} %project_own.5.diag_ref, bf16[3,128,128]{2,1,0:T(8,128)(2,1)S(1)} %collective-permute-done.4.fields_ref, bf16[128,128]{1,0:T(8,128)(2,1)S(1)} %get-tuple-element.30.short_ref), custom_call_target="tpu_custom_call" | custom-call | flops 268435456 | bytes 2097152 | tf_op jit(solution)/shard_map/project_across/pallas_call | solution.py:347
  13.1 2.5 %collective-permute-start.6 = (bf16[192,128]{1,0:T(8,128)(2,1)S(1)}, bf16[192,128]{1,0:T(8,128)(2,1)S(1)}, u32[]{:S(2)}, u32[]{:S(2)}) collective-permute-start(bf16[192,128]{1,0:T(8,128)(2,1)S(1)} %get-tuple-element.31), channel_id=1, source_target_pairs={{0,24},{8,16},{16,8},{24,0},{1,25},{9,17},{17,9},{25,1},{2,26},{10... | collective-permute-start | bytes 147464 | tf_op jit(solution)/shard_map/ppermute | solution.py:40
  15.6 0.5 %collective-permute-start.5 = (bf16[192,128]{1,0:T(8,128)(2,1)S(1)}, bf16[192,128]{1,0:T(8,128)(2,1)S(1)}, u32[]{:S(2)}, u32[]{:S(2)}) collective-permute-start(bf16[192,128]{1,0:T(8,128)(2,1)S(1)} %get-tuple-element.31), channel_id=1, source_target_pairs={{0,8},{8,0},{16,24},{24,16},{1,9},{9,1},{17,25},{25,17},{2,10},{10... | collective-permute-start | bytes 147464 | tf_op jit(solution)/shard_map/ppermute | solution.py:40
  16.1 0.5 collective-permute-start.7
  16.6 3.2 %collective-permute-done.7.refs_2_ = bf16[64,128]{1,0:T(8,128)(2,1)S(1)} collective-permute-done((bf16[64,128]{1,0:T(8,128)(2,1)S(1)}, bf16[64,128]{1,0:T(8,128)(2,1)S(1)}, u32[]{:S(2)}, u32[]{:S(2)}) %collective-permute-start.7) | collective-permute-done | bytes 16416 | tf_op jit(solution)/shard_map/ppermute | solution.py:40
  19.9 0.0 copy-start.2
  19.9 0.9 %term_first.2 = (bf16[128,2048]{1,0:T(8,128)(2,1)S(1)}, bf16[3,128,128]{2,1,0:T(8,128)(2,1)S(1)}) custom-call(f32[1,256]{1,0:T(1,128)S(1)} %bitcast.13, bf16[2048,1024]{1,0:T(8,128)(2,1)S(1)} %load.1.factor_ref, bf16[64,128]{1,0:T(8,128)(2,1)S(1)} %get-tuple-element.32.refs_0_, bf16[192,128]{1,0:T(8,128)(2,1)S(1)} %collective-permute-done.5.refs_0_.refs_1_, ...), custom_call_target="tpu_custom_call" | custom-call | flops 134217728 | bytes 2097152 | tf_op jit(solution)/shard_map/term_first/pallas_call | solution.py:356
  20.7 0.1 collective-permute-start.8
  20.8 0.8 %term.4 = (f32[3,128,128]{2,1,0:T(8,128)S(1)}, bf16[1,128,128]{2,1,0:T(8,128)(2,1)S(1)}) custom-call(bf16[128,2048]{1,0:T(8,128)(2,1)S(1)} %get-tuple-element.33.coef_ref, bf16[2048,1024]{1,0:T(8,128)(2,1)S(1)} %load.1.factor_ref), custom_call_target="tpu_custom_call" | custom-call | flops 268435456 | bytes 2097152 | tf_op jit(solution)/shard_map/term/pallas_call | solution.py:366
  21.6 0.6 %collective-permute-start.9 = (bf16[1,128,128]{2,1,0:T(8,128)(2,1)S(1)}, bf16[1,128,128]{2,1,0:T(8,128)(2,1)S(1)}, u32[]{:S(2)}, u32[]{:S(2)}) collective-permute-start(bf16[1,128,128]{2,1,0:T(8,128)(2,1)S(1)} %get-tuple-element.39), channel_id=1, source_target_pairs={{0,1},{1,0},{2,3},{3,2},{4,5},{5,4},{6,7},{7,6},{8,9},{9,8},{10,11... | collective-permute-start | bytes 98312 | tf_op jit(solution)/shard_map/ppermute | solution.py:40
  22.2 1.8 %collective-permute-start.10 = (bf16[1,128,128]{2,1,0:T(8,128)(2,1)S(1)}, bf16[1,128,128]{2,1,0:T(8,128)(2,1)S(1)}, u32[]{:S(2)}, u32[]{:S(2)}) collective-permute-start(bf16[1,128,128]{2,1,0:T(8,128)(2,1)S(1)} %get-tuple-element.36.refs_0_), channel_id=1, source_target_pairs={{0,5},{1,4},{2,7},{3,6},{4,1},{5,0},{6,3},{7,2},{8,13},{9,12},{10,... | collective-permute-start | bytes 98312 | tf_op jit(solution)/shard_map/ppermute | solution.py:40
  24.0 1.4 %collective-permute-start.11 = (bf16[1,128,128]{2,1,0:T(8,128)(2,1)S(1)}, bf16[1,128,128]{2,1,0:T(8,128)(2,1)S(1)}, u32[]{:S(2)}, u32[]{:S(2)}) collective-permute-start(bf16[1,128,128]{2,1,0:T(8,128)(2,1)S(1)} %get-tuple-element.37.refs_1_), channel_id=1, source_target_pairs={{0,7},{1,6},{2,5},{3,4},{4,3},{5,2},{6,1},{7,0},{8,15},{9,14},{10,... | collective-permute-start | bytes 98312 | tf_op jit(solution)/shard_map/ppermute | solution.py:40
  25.4 0.0 collective-permute-start.12
  25.4 0.2 local.2.base_ref
  25.6 0.3 term.5.mine_ref
  26.0 0.7 %collective-permute-done.10.refs_1_ = bf16[1,128,128]{2,1,0:T(8,128)(2,1)S(1)} collective-permute-done((bf16[1,128,128]{2,1,0:T(8,128)(2,1)S(1)}, bf16[1,128,128]{2,1,0:T(8,128)(2,1)S(1)}, u32[]{:S(2)}, u32[]{:S(2)}) %collective-permute-start.10) | collective-permute-done | bytes 32800 | tf_op jit(solution)/shard_map/ppermute | solution.py:40
  26.6 2.6 %collective-permute-done.11.refs_2_ = bf16[1,128,128]{2,1,0:T(8,128)(2,1)S(1)} collective-permute-done((bf16[1,128,128]{2,1,0:T(8,128)(2,1)S(1)}, bf16[1,128,128]{2,1,0:T(8,128)(2,1)S(1)}, u32[]{:S(2)}, u32[]{:S(2)}) %collective-permute-start.11) | collective-permute-done | bytes 32800 | tf_op jit(solution)/shard_map/ppermute | solution.py:40
  29.3 0.0 collective-permute-done.12.refs_3_
  29.3 1.0 %collective-permute-start.16 = (bf16[1,128,128]{2,1,0:T(8,128)(2,1)S(1)}, bf16[1,128,128]{2,1,0:T(8,128)(2,1)S(1)}, u32[]{:S(2)}, u32[]{:S(2)}) collective-permute-start(bf16[1,128,128]{2,1,0:T(8,128)(2,1)S(1)} %get-tuple-element.41.refs_0_), channel_id=1, source_target_pairs={{0,5},{1,4},{2,7},{3,6},{4,1},{5,0},{6,3},{7,2},{8,13},{9,12},{10,... | collective-permute-start | bytes 98312 | tf_op jit(solution)/shard_map/ppermute | solution.py:40
  30.3 1.3 %collective-permute-start.15 = (bf16[1,128,128]{2,1,0:T(8,128)(2,1)S(1)}, bf16[1,128,128]{2,1,0:T(8,128)(2,1)S(1)}, u32[]{:S(2)}, u32[]{:S(2)}) collective-permute-start(bf16[1,128,128]{2,1,0:T(8,128)(2,1)S(1)} %get-tuple-element.41.refs_0_), channel_id=1, source_target_pairs={{0,7},{1,6},{2,5},{3,4},{4,3},{5,2},{6,1},{7,0},{8,15},{9,14},{10,... | collective-permute-start | bytes 98312 | tf_op jit(solution)/shard_map/ppermute | solution.py:40
  31.6 1.0 %collective-permute-start.14 = (bf16[1,128,128]{2,1,0:T(8,128)(2,1)S(1)}, bf16[1,128,128]{2,1,0:T(8,128)(2,1)S(1)}, u32[]{:S(2)}, u32[]{:S(2)}) collective-permute-start(bf16[1,128,128]{2,1,0:T(8,128)(2,1)S(1)} %get-tuple-element.41.refs_0_), channel_id=1, source_target_pairs={{0,3},{1,2},{2,1},{3,0},{4,7},{5,6},{6,5},{7,4},{8,11},{9,10},{10,... | collective-permute-start | bytes 98312 | tf_op jit(solution)/shard_map/ppermute | solution.py:40
  32.6 0.1 collective-permute-start.13
  32.7 0.5 project_own.6.refs_0_.refs_2_
  33.1 0.9 %collective-permute-done.16.refs_4_ = bf16[1,128,128]{2,1,0:T(8,128)(2,1)S(1)} collective-permute-done((bf16[1,128,128]{2,1,0:T(8,128)(2,1)S(1)}, bf16[1,128,128]{2,1,0:T(8,128)(2,1)S(1)}, u32[]{:S(2)}, u32[]{:S(2)}) %collective-permute-start.16) | collective-permute-done | bytes 32800 | tf_op jit(solution)/shard_map/ppermute | solution.py:40
  34.0 1.4 %collective-permute-done.15.refs_3_ = bf16[1,128,128]{2,1,0:T(8,128)(2,1)S(1)} collective-permute-done((bf16[1,128,128]{2,1,0:T(8,128)(2,1)S(1)}, bf16[1,128,128]{2,1,0:T(8,128)(2,1)S(1)}, u32[]{:S(2)}, u32[]{:S(2)}) %collective-permute-start.15) | collective-permute-done | bytes 32800 | tf_op jit(solution)/shard_map/ppermute | solution.py:40
  35.5 0.0 collective-permute-done.14.refs_2_
  35.5 0.5 collective-permute-start.17
  36.0 0.3 columns.3
  36.4 0.7 %project_own.7.diag_ref = f32[256,128]{1,0:T(8,128)S(1)} custom-call(bf16[2048,1024]{1,0:T(8,128)(2,1)S(1)} %load.1.factor_ref, bf16[3,128,128]{2,1,0:T(8,128)(2,1)S(1)} %join.3.bundle_ref.refs_0_, bf16[1,128,128]{2,1,0:T(8,128)(2,1)S(1)} %collective-permute-done.13.refs_1_.twin_ref, f32[256,128]{1,0:T(8,128)S(1)} %project_own.6.refs_0_.refs_2_), custom_call_target="tpu_custom_call" | custom-call | flops 268435456 | bytes 2097152 | tf_op jit(solution)/shard_map/project_own/pallas_call | solution.py:313
  37.1 0.0 collective-permute-done.17.fields_ref
  37.1 0.9 %project_across.3 = (bf16[192,128]{1,0:T(8,128)(2,1)S(1)}, bf16[64,128]{1,0:T(8,128)(2,1)S(1)}) custom-call(bf16[2048,1024]{1,0:T(8,128)(2,1)S(1)} %load.1.factor_ref, f32[256,128]{1,0:T(8,128)S(1)} %project_own.7.diag_ref, bf16[3,128,128]{2,1,0:T(8,128)(2,1)S(1)} %collective-permute-done.17.fields_ref, bf16[128,128]{1,0:T(8,128)(2,1)S(1)} %get-tuple-element.43.short_ref), custom_call_target="tpu_custom_call" | custom-call | flops 268435456 | bytes 2097152 | tf_op jit(solution)/shard_map/project_across/pallas_call | solution.py:347
  38.0 1.5 %collective-permute-start.19 = (bf16[192,128]{1,0:T(8,128)(2,1)S(1)}, bf16[192,128]{1,0:T(8,128)(2,1)S(1)}, u32[]{:S(2)}, u32[]{:S(2)}) collective-permute-start(bf16[192,128]{1,0:T(8,128)(2,1)S(1)} %get-tuple-element.44), channel_id=1, source_target_pairs={{0,24},{8,16},{16,8},{24,0},{1,25},{9,17},{17,9},{25,1},{2,26},{10... | collective-permute-start | bytes 147464 | tf_op jit(solution)/shard_map/ppermute | solution.py:40
  39.5 0.5 collective-permute-start.18
  40.0 1.5 %collective-permute-start.20 = (bf16[64,128]{1,0:T(8,128)(2,1)S(1)}, bf16[64,128]{1,0:T(8,128)(2,1)S(1)}, u32[]{:S(2)}, u32[]{:S(2)}) collective-permute-start(bf16[64,128]{1,0:T(8,128)(2,1)S(1)} %get-tuple-element.45.refs_0_), channel_id=1, source_target_pairs={{0,16},{8,24},{16,0},{24,8},{1,17},{9,25},{17,1},{25,9},{2,18},{10... | collective-permute-start | bytes 49160 | tf_op jit(solution)/shard_map/ppermute | solution.py:40
  41.5 2.2 %collective-permute-done.20.refs_2_ = bf16[64,128]{1,0:T(8,128)(2,1)S(1)} collective-permute-done((bf16[64,128]{1,0:T(8,128)(2,1)S(1)}, bf16[64,128]{1,0:T(8,128)(2,1)S(1)}, u32[]{:S(2)}, u32[]{:S(2)}) %collective-permute-start.20) | collective-permute-done | bytes 16416 | tf_op jit(solution)/shard_map/ppermute | solution.py:40
  43.7 0.0 collective-permute-done.19.refs_1_.refs_3_
  43.8 0.0 collective-permute-done.18.refs_0_.refs_1_
  43.8 0.7 %term_first.3 = (bf16[128,2048]{1,0:T(8,128)(2,1)S(1)}, bf16[2,128,128]{2,1,0:T(8,128)(2,1)S(1)}) custom-call(f32[1,256]{1,0:T(1,128)S(1)} %bitcast.14, bf16[2048,1024]{1,0:T(8,128)(2,1)S(1)} %load.1.factor_ref, bf16[64,128]{1,0:T(8,128)(2,1)S(1)} %get-tuple-element.45.refs_0_, bf16[192,128]{1,0:T(8,128)(2,1)S(1)} %collective-permute-done.18.refs_0_.refs_1_, ...), custom_call_target="tpu_custom_call" | custom-call | flops 134217728 | bytes 2097152 | tf_op jit(solution)/shard_map/term_first/pallas_call | solution.py:356
  44.5 0.1 collective-permute-start.21
  44.6 0.8 %term.6 = (f32[2,128,128]{2,1,0:T(8,128)S(1)}, bf16[2,128,128]{2,1,0:T(8,128)(2,1)S(1)}) custom-call(bf16[128,2048]{1,0:T(8,128)(2,1)S(1)} %get-tuple-element.46.coef_ref, bf16[2048,1024]{1,0:T(8,128)(2,1)S(1)} %load.1.factor_ref), custom_call_target="tpu_custom_call" | custom-call | flops 268435456 | bytes 2097152 | tf_op jit(solution)/shard_map/term/pallas_call | solution.py:366
  45.4 0.6 %collective-permute-start.22 = (bf16[2,128,128]{2,1,0:T(8,128)(2,1)S(1)}, bf16[2,128,128]{2,1,0:T(8,128)(2,1)S(1)}, u32[]{:S(2)}, u32[]{:S(2)}) collective-permute-start(bf16[2,128,128]{2,1,0:T(8,128)(2,1)S(1)} %get-tuple-element.51), channel_id=1, source_target_pairs={{0,1},{1,0},{2,3},{3,2},{4,5},{5,4},{6,7},{7,6},{8,9},{9,8},{10,11... | collective-permute-start | bytes 196616 | tf_op jit(solution)/shard_map/ppermute | solution.py:40
  46.0 2.1 %collective-permute-start.23 = (bf16[1,128,128]{2,1,0:T(8,128)(2,1)S(1)}, bf16[1,128,128]{2,1,0:T(8,128)(2,1)S(1)}, u32[]{:S(2)}, u32[]{:S(2)}) collective-permute-start(bf16[1,128,128]{2,1,0:T(8,128)(2,1)S(1)} %get-tuple-element.49.refs_0_), channel_id=1, source_target_pairs={{0,7},{1,6},{2,5},{3,4},{4,3},{5,2},{6,1},{7,0},{8,15},{9,14},{10,... | collective-permute-start | bytes 98312 | tf_op jit(solution)/shard_map/ppermute | solution.py:40
  48.0 0.5 term.7.mine_ref
  48.5 1.8 %collective-permute-start.25 = (bf16[1,128,128]{2,1,0:T(8,128)(2,1)S(1)}, bf16[1,128,128]{2,1,0:T(8,128)(2,1)S(1)}, u32[]{:S(2)}, u32[]{:S(2)}) collective-permute-start(bf16[1,128,128]{2,1,0:T(8,128)(2,1)S(1)} %get-tuple-element.53), channel_id=1, source_target_pairs={{0,3},{1,2},{2,1},{3,0},{4,7},{5,6},{6,5},{7,4},{8,11},{9,10},{10,... | collective-permute-start | bytes 98312 | tf_op jit(solution)/shard_map/ppermute | solution.py:40
  50.4 0.2 local.3.base_ref
  50.5 0.8 %collective-permute-done.23.refs_1_ = bf16[1,128,128]{2,1,0:T(8,128)(2,1)S(1)} collective-permute-done((bf16[1,128,128]{2,1,0:T(8,128)(2,1)S(1)}, bf16[1,128,128]{2,1,0:T(8,128)(2,1)S(1)}, u32[]{:S(2)}, u32[]{:S(2)}) %collective-permute-start.23) | collective-permute-done | bytes 32800 | tf_op jit(solution)/shard_map/ppermute | solution.py:40
  51.3 1.3 %collective-permute-done.24.refs_2_ = bf16[1,128,128]{2,1,0:T(8,128)(2,1)S(1)} collective-permute-done((bf16[1,128,128]{2,1,0:T(8,128)(2,1)S(1)}, bf16[1,128,128]{2,1,0:T(8,128)(2,1)S(1)}, u32[]{:S(2)}, u32[]{:S(2)}) %collective-permute-start.24) | collective-permute-done | bytes 32800 | tf_op jit(solution)/shard_map/ppermute | solution.py:40
  52.6 0.7 %update.3 = (f32[128,128]{1,0:T(8,128)}, f32[128,128]{1,0:T(8,128)}) custom-call(f32[128,128]{1,0:T(8,128)S(1)} %get-tuple-element.40.x_ref, f32[128,128]{1,0:T(8,128)S(1)} %local.3.base_ref, f32[1,128,128]{2,1,0:T(8,128)S(1)} %get-tuple-element.52.refs_0_, bf16[1,128,128]{2,1,0:T(8,128)(2,1)S(1)} %collective-permute-done.23.refs_1_, ...), custom_call_target="tpu_custom_call" | custom-call | bytes 262144 | tf_op jit(solution)/shard_map/update/pallas_call | solution.py:394
  (22 shorter events, 0.1 us)
Async XLA Ops:
  1.5 8.4 %collective-permute-start.3 = (bf16[1,128,128]{2,1,0:T(8,128)(2,1)S(1)}, bf16[1,128,128]{2,1,0:T(8,128)(2,1)S(1)}, u32[]{:S(2)}, u32[]{:S(2)}) collective-permute-start(bf16[1,128,128]{2,1,0:T(8,128)(2,1)S(1)} %fusion.refs_0_), channel_id=1, source_target_pairs={{0,5},{1,4},{2,7},{3,6},{4,1},{5,0},{6,3},{7,2},{8,13},{9,12},{10,... | collective-permute-start | bytes 98312 | tf_op jit(solution)/shard_map/ppermute | solution.py:40
  5.0 5.2 %collective-permute-start.2 = (bf16[1,128,128]{2,1,0:T(8,128)(2,1)S(1)}, bf16[1,128,128]{2,1,0:T(8,128)(2,1)S(1)}, u32[]{:S(2)}, u32[]{:S(2)}) collective-permute-start(bf16[1,128,128]{2,1,0:T(8,128)(2,1)S(1)} %fusion.refs_0_), channel_id=1, source_target_pairs={{0,7},{1,6},{2,5},{3,4},{4,3},{5,2},{6,1},{7,0},{8,15},{9,14},{10,... | collective-permute-start | bytes 98312 | tf_op jit(solution)/shard_map/ppermute | solution.py:40
  6.6 3.8 %collective-permute-start.1 = (bf16[1,128,128]{2,1,0:T(8,128)(2,1)S(1)}, bf16[1,128,128]{2,1,0:T(8,128)(2,1)S(1)}, u32[]{:S(2)}, u32[]{:S(2)}) collective-permute-start(bf16[1,128,128]{2,1,0:T(8,128)(2,1)S(1)} %fusion.refs_0_), channel_id=1, source_target_pairs={{0,3},{1,2},{2,1},{3,0},{4,7},{5,6},{6,5},{7,4},{8,11},{9,10},{10,... | collective-permute-start | bytes 98312 | tf_op jit(solution)/shard_map/ppermute | solution.py:40
  6.8 3.5 %collective-permute-start = (bf16[1,128,128]{2,1,0:T(8,128)(2,1)S(1)}, bf16[1,128,128]{2,1,0:T(8,128)(2,1)S(1)}, u32[]{:S(2)}, u32[]{:S(2)}) collective-permute-start(bf16[1,128,128]{2,1,0:T(8,128)(2,1)S(1)} %fusion.refs_0_), channel_id=1, source_target_pairs={{0,1},{1,0},{2,3},{3,2},{4,5},{5,4},{6,7},{7,6},{8,9},{9,8},{10,11... | collective-permute-start | bytes 98312 | tf_op jit(solution)/shard_map/ppermute | solution.py:40
  6.8 2.2 %copy-start = (bf16[256,8,1024]{2,1,0:T(8,128)(2,1)S(1)}, bf16[256,8,1024]{2,1,0:T(8,128)(2,1)}, u32[]{:S(2)}) copy-start(bf16[256,8,1024]{2,1,0:T(8,128)(2,1)} %param.6) | copy-start | bytes 12582916
  9.4 1.7 %copy-start.1 = (f32[16,8,128]{2,1,0:T(8,128)S(1)}, f32[16,8,128]{2,1,0:T(8,128)}, u32[]{:S(2)}) copy-start(f32[16,8,128]{2,1,0:T(8,128)} %param.4) | copy-start | bytes 196612
  10.4 1.8 %collective-permute-start.4 = (bf16[3,128,128]{2,1,0:T(8,128)(2,1)S(1)}, bf16[3,128,128]{2,1,0:T(8,128)(2,1)S(1)}, u32[]{:S(2)}, u32[]{:S(2)}) collective-permute-start(bf16[3,128,128]{2,1,0:T(8,128)(2,1)S(1)} %join.2.bundle_ref.refs_0_), channel_id=1, source_target_pairs={{0,1},{1,0},{2,3},{3,2},{4,5},{5,4},{6,7},{7,6},{8,9},{9,8},{10,11... | collective-permute-start | bytes 294920 | tf_op jit(solution)/shard_map/ppermute | solution.py:40
  11.5 8.4 %copy-start.3 = (f32[256]{0:T(256)S(1)}, f32[256]{0:T(256)}, u32[]{:S(2)}) copy-start(f32[256]{0:T(256)} %param.7) | copy-start | bytes 3076
  13.1 6.8 %collective-permute-start.6 = (bf16[192,128]{1,0:T(8,128)(2,1)S(1)}, bf16[192,128]{1,0:T(8,128)(2,1)S(1)}, u32[]{:S(2)}, u32[]{:S(2)}) collective-permute-start(bf16[192,128]{1,0:T(8,128)(2,1)S(1)} %get-tuple-element.31), channel_id=1, source_target_pairs={{0,24},{8,16},{16,8},{24,0},{1,25},{9,17},{17,9},{25,1},{2,26},{10... | collective-permute-start | bytes 147464 | tf_op jit(solution)/shard_map/ppermute | solution.py:40
  15.6 4.3 %collective-permute-start.5 = (bf16[192,128]{1,0:T(8,128)(2,1)S(1)}, bf16[192,128]{1,0:T(8,128)(2,1)S(1)}, u32[]{:S(2)}, u32[]{:S(2)}) collective-permute-start(bf16[192,128]{1,0:T(8,128)(2,1)S(1)} %get-tuple-element.31), channel_id=1, source_target_pairs={{0,8},{8,0},{16,24},{24,16},{1,9},{9,1},{17,25},{25,17},{2,10},{10... | collective-permute-start | bytes 147464 | tf_op jit(solution)/shard_map/ppermute | solution.py:40
  16.1 3.7 %collective-permute-start.7 = (bf16[64,128]{1,0:T(8,128)(2,1)S(1)}, bf16[64,128]{1,0:T(8,128)(2,1)S(1)}, u32[]{:S(2)}, u32[]{:S(2)}) collective-permute-start(bf16[64,128]{1,0:T(8,128)(2,1)S(1)} %get-tuple-element.32.refs_0_), channel_id=1, source_target_pairs={{0,16},{8,24},{16,0},{24,8},{1,17},{9,25},{17,1},{25,9},{2,18},{10... | collective-permute-start | bytes 49160 | tf_op jit(solution)/shard_map/ppermute | solution.py:40
  19.9 5.5 %copy-start.2 = (f32[8,128]{1,0:T(8,128)S(1)}, f32[8,128]{1,0:T(8,128)}, u32[]{:S(2)}) copy-start(f32[8,128]{1,0:T(8,128)} %amp_ref.3) | copy-start | bytes 12292
  20.7 1.4 %collective-permute-start.8 = (bf16[3,128,128]{2,1,0:T(8,128)(2,1)S(1)}, bf16[3,128,128]{2,1,0:T(8,128)(2,1)S(1)}, u32[]{:S(2)}, u32[]{:S(2)}) collective-permute-start(bf16[3,128,128]{2,1,0:T(8,128)(2,1)S(1)} %get-tuple-element.35), channel_id=1, source_target_pairs={{0,1},{1,0},{2,3},{3,2},{4,5},{5,4},{6,7},{7,6},{8,9},{9,8},{10,11... | collective-permute-start | bytes 294920 | tf_op jit(solution)/shard_map/ppermute | solution.py:40
  21.6 4.3 %collective-permute-start.9 = (bf16[1,128,128]{2,1,0:T(8,128)(2,1)S(1)}, bf16[1,128,128]{2,1,0:T(8,128)(2,1)S(1)}, u32[]{:S(2)}, u32[]{:S(2)}) collective-permute-start(bf16[1,128,128]{2,1,0:T(8,128)(2,1)S(1)} %get-tuple-element.39), channel_id=1, source_target_pairs={{0,1},{1,0},{2,3},{3,2},{4,5},{5,4},{6,7},{7,6},{8,9},{9,8},{10,11... | collective-permute-start | bytes 98312 | tf_op jit(solution)/shard_map/ppermute | solution.py:40
  22.2 4.4 %collective-permute-start.10 = (bf16[1,128,128]{2,1,0:T(8,128)(2,1)S(1)}, bf16[1,128,128]{2,1,0:T(8,128)(2,1)S(1)}, u32[]{:S(2)}, u32[]{:S(2)}) collective-permute-start(bf16[1,128,128]{2,1,0:T(8,128)(2,1)S(1)} %get-tuple-element.36.refs_0_), channel_id=1, source_target_pairs={{0,5},{1,4},{2,7},{3,6},{4,1},{5,0},{6,3},{7,2},{8,13},{9,12},{10,... | collective-permute-start | bytes 98312 | tf_op jit(solution)/shard_map/ppermute | solution.py:40
  24.0 5.2 %collective-permute-start.11 = (bf16[1,128,128]{2,1,0:T(8,128)(2,1)S(1)}, bf16[1,128,128]{2,1,0:T(8,128)(2,1)S(1)}, u32[]{:S(2)}, u32[]{:S(2)}) collective-permute-start(bf16[1,128,128]{2,1,0:T(8,128)(2,1)S(1)} %get-tuple-element.37.refs_1_), channel_id=1, source_target_pairs={{0,7},{1,6},{2,5},{3,4},{4,3},{5,2},{6,1},{7,0},{8,15},{9,14},{10,... | collective-permute-start | bytes 98312 | tf_op jit(solution)/shard_map/ppermute | solution.py:40
  25.4 3.9 %collective-permute-start.12 = (bf16[1,128,128]{2,1,0:T(8,128)(2,1)S(1)}, bf16[1,128,128]{2,1,0:T(8,128)(2,1)S(1)}, u32[]{:S(2)}, u32[]{:S(2)}) collective-permute-start(bf16[1,128,128]{2,1,0:T(8,128)(2,1)S(1)} %get-tuple-element.38.refs_2_), channel_id=1, source_target_pairs={{0,3},{1,2},{2,1},{3,0},{4,7},{5,6},{6,5},{7,4},{8,11},{9,10},{10,... | collective-permute-start | bytes 98312 | tf_op jit(solution)/shard_map/ppermute | solution.py:40
  29.3 4.7 %collective-permute-start.16 = (bf16[1,128,128]{2,1,0:T(8,128)(2,1)S(1)}, bf16[1,128,128]{2,1,0:T(8,128)(2,1)S(1)}, u32[]{:S(2)}, u32[]{:S(2)}) collective-permute-start(bf16[1,128,128]{2,1,0:T(8,128)(2,1)S(1)} %get-tuple-element.41.refs_0_), channel_id=1, source_target_pairs={{0,5},{1,4},{2,7},{3,6},{4,1},{5,0},{6,3},{7,2},{8,13},{9,12},{10,... | collective-permute-start | bytes 98312 | tf_op jit(solution)/shard_map/ppermute | solution.py:40
  30.3 5.2 %collective-permute-start.15 = (bf16[1,128,128]{2,1,0:T(8,128)(2,1)S(1)}, bf16[1,128,128]{2,1,0:T(8,128)(2,1)S(1)}, u32[]{:S(2)}, u32[]{:S(2)}) collective-permute-start(bf16[1,128,128]{2,1,0:T(8,128)(2,1)S(1)} %get-tuple-element.41.refs_0_), channel_id=1, source_target_pairs={{0,7},{1,6},{2,5},{3,4},{4,3},{5,2},{6,1},{7,0},{8,15},{9,14},{10,... | collective-permute-start | bytes 98312 | tf_op jit(solution)/shard_map/ppermute | solution.py:40
  31.6 3.9 %collective-permute-start.14 = (bf16[1,128,128]{2,1,0:T(8,128)(2,1)S(1)}, bf16[1,128,128]{2,1,0:T(8,128)(2,1)S(1)}, u32[]{:S(2)}, u32[]{:S(2)}) collective-permute-start(bf16[1,128,128]{2,1,0:T(8,128)(2,1)S(1)} %get-tuple-element.41.refs_0_), channel_id=1, source_target_pairs={{0,3},{1,2},{2,1},{3,0},{4,7},{5,6},{6,5},{7,4},{8,11},{9,10},{10,... | collective-permute-start | bytes 98312 | tf_op jit(solution)/shard_map/ppermute | solution.py:40
  32.6 2.9 %collective-permute-start.13 = (bf16[1,128,128]{2,1,0:T(8,128)(2,1)S(1)}, bf16[1,128,128]{2,1,0:T(8,128)(2,1)S(1)}, u32[]{:S(2)}, u32[]{:S(2)}) collective-permute-start(bf16[1,128,128]{2,1,0:T(8,128)(2,1)S(1)} %get-tuple-element.41.refs_0_), channel_id=1, source_target_pairs={{0,1},{1,0},{2,3},{3,2},{4,5},{5,4},{6,7},{7,6},{8,9},{9,8},{10,11... | collective-permute-start | bytes 98312 | tf_op jit(solution)/shard_map/ppermute | solution.py:40
  35.5 1.6 %collective-permute-start.17 = (bf16[3,128,128]{2,1,0:T(8,128)(2,1)S(1)}, bf16[3,128,128]{2,1,0:T(8,128)(2,1)S(1)}, u32[]{:S(2)}, u32[]{:S(2)}) collective-permute-start(bf16[3,128,128]{2,1,0:T(8,128)(2,1)S(1)} %join.3.bundle_ref.refs_0_), channel_id=1, source_target_pairs={{0,1},{1,0},{2,3},{3,2},{4,5},{5,4},{6,7},{7,6},{8,9},{9,8},{10,11... | collective-permute-start | bytes 294920 | tf_op jit(solution)/shard_map/ppermute | solution.py:40
  38.0 5.7 %collective-permute-start.19 = (bf16[192,128]{1,0:T(8,128)(2,1)S(1)}, bf16[192,128]{1,0:T(8,128)(2,1)S(1)}, u32[]{:S(2)}, u32[]{:S(2)}) collective-permute-start(bf16[192,128]{1,0:T(8,128)(2,1)S(1)} %get-tuple-element.44), channel_id=1, source_target_pairs={{0,24},{8,16},{16,8},{24,0},{1,25},{9,17},{17,9},{25,1},{2,26},{10... | collective-permute-start | bytes 147464 | tf_op jit(solution)/shard_map/ppermute | solution.py:40
  39.5 4.3 %collective-permute-start.18 = (bf16[192,128]{1,0:T(8,128)(2,1)S(1)}, bf16[192,128]{1,0:T(8,128)(2,1)S(1)}, u32[]{:S(2)}, u32[]{:S(2)}) collective-permute-start(bf16[192,128]{1,0:T(8,128)(2,1)S(1)} %get-tuple-element.44), channel_id=1, source_target_pairs={{0,8},{8,0},{16,24},{24,16},{1,9},{9,1},{17,25},{25,17},{2,10},{10... | collective-permute-start | bytes 147464 | tf_op jit(solution)/shard_map/ppermute | solution.py:40
  40.0 3.7 %collective-permute-start.20 = (bf16[64,128]{1,0:T(8,128)(2,1)S(1)}, bf16[64,128]{1,0:T(8,128)(2,1)S(1)}, u32[]{:S(2)}, u32[]{:S(2)}) collective-permute-start(bf16[64,128]{1,0:T(8,128)(2,1)S(1)} %get-tuple-element.45.refs_0_), channel_id=1, source_target_pairs={{0,16},{8,24},{16,0},{24,8},{1,17},{9,25},{17,1},{25,9},{2,18},{10... | collective-permute-start | bytes 49160 | tf_op jit(solution)/shard_map/ppermute | solution.py:40
  44.5 1.4 %collective-permute-start.21 = (bf16[2,128,128]{2,1,0:T(8,128)(2,1)S(1)}, bf16[2,128,128]{2,1,0:T(8,128)(2,1)S(1)}, u32[]{:S(2)}, u32[]{:S(2)}) collective-permute-start(bf16[2,128,128]{2,1,0:T(8,128)(2,1)S(1)} %get-tuple-element.48), channel_id=1, source_target_pairs={{0,1},{1,0},{2,3},{3,2},{4,5},{5,4},{6,7},{7,6},{8,9},{9,8},{10,11... | collective-permute-start | bytes 196616 | tf_op jit(solution)/shard_map/ppermute | solution.py:40
  45.4 3.1 %collective-permute-start.22 = (bf16[2,128,128]{2,1,0:T(8,128)(2,1)S(1)}, bf16[2,128,128]{2,1,0:T(8,128)(2,1)S(1)}, u32[]{:S(2)}, u32[]{:S(2)}) collective-permute-start(bf16[2,128,128]{2,1,0:T(8,128)(2,1)S(1)} %get-tuple-element.51), channel_id=1, source_target_pairs={{0,1},{1,0},{2,3},{3,2},{4,5},{5,4},{6,7},{7,6},{8,9},{9,8},{10,11... | collective-permute-start | bytes 196616 | tf_op jit(solution)/shard_map/ppermute | solution.py:40
  46.0 5.3 %collective-permute-start.23 = (bf16[1,128,128]{2,1,0:T(8,128)(2,1)S(1)}, bf16[1,128,128]{2,1,0:T(8,128)(2,1)S(1)}, u32[]{:S(2)}, u32[]{:S(2)}) collective-permute-start(bf16[1,128,128]{2,1,0:T(8,128)(2,1)S(1)} %get-tuple-element.49.refs_0_), channel_id=1, source_target_pairs={{0,7},{1,6},{2,5},{3,4},{4,3},{5,2},{6,1},{7,0},{8,15},{9,14},{10,... | collective-permute-start | bytes 98312 | tf_op jit(solution)/shard_map/ppermute | solution.py:40
  48.0 4.6 %collective-permute-start.24 = (bf16[1,128,128]{2,1,0:T(8,128)(2,1)S(1)}, bf16[1,128,128]{2,1,0:T(8,128)(2,1)S(1)}, u32[]{:S(2)}, u32[]{:S(2)}) collective-permute-start(bf16[1,128,128]{2,1,0:T(8,128)(2,1)S(1)} %get-tuple-element.50.refs_1_), channel_id=1, source_target_pairs={{0,5},{1,4},{2,7},{3,6},{4,1},{5,0},{6,3},{7,2},{8,13},{9,12},{10,... | collective-permute-start | bytes 98312 | tf_op jit(solution)/shard_map/ppermute | solution.py:40
  48.5 4.0 %collective-permute-start.25 = (bf16[1,128,128]{2,1,0:T(8,128)(2,1)S(1)}, bf16[1,128,128]{2,1,0:T(8,128)(2,1)S(1)}, u32[]{:S(2)}, u32[]{:S(2)}) collective-permute-start(bf16[1,128,128]{2,1,0:T(8,128)(2,1)S(1)} %get-tuple-element.53), channel_id=1, source_target_pairs={{0,3},{1,2},{2,1},{3,0},{4,7},{5,6},{6,5},{7,4},{8,11},{9,10},{10,... | collective-permute-start | bytes 98312 | tf_op jit(solution)/shard_map/ppermute | solution.py:40

commit v16 on v12

--- a/solution.py
+++ b/solution.py
@@ -304,7 +304,6 @@
         name="load",
     )(flat)
     half = near // 2
-    close = list(range(half))
 
     def spots_of(masks, other):
         return [(mask, other != (mask > 0)) for mask in masks]
@@ -324,7 +323,8 @@
     for step in range(ITERS):
         halve = step == 0
         last = step == ITERS - 1
-        away = sorted(range(half, near), reverse=last)
+        close = list(range(half if last else 1))
+        away = sorted(range(half, near), reverse=last) + list(range(len(close), half))
         order = list(range(1, near))
         order.sort(key=lambda mask: (mask == half, mask))
         parts = [cross(short, mask) for mask in order]
@@ -357,7 +357,7 @@
         pays = [swap(part if mask & (mask + 1) else pay, "grp", mask) for mask in range(1, groups)]
         coef, far = call(
             partial(far_kernel, rows, cols, groups, ncells_all, spots_of(away, True)),
-            (shape(bf16, lines, ranks * rows), shape(bf16, half, lines, width)),
+            (shape(bf16, lines, ranks * rows), shape(bf16, len(away), lines, width)),
             flops=work // 2,
             moved=flat.size,
             name="term_first",

time: 53.5 us -> 53.4 us (level)
  transfers between devices with their start and end apart: 26 -> 26, of which waited for: 11 -> 10; matrix products, arithmetic and copies ran while one was open for 0% -> 0% of each run, Pallas kernels for 12% -> 12%
where the time goes in v16:
time: 53.4 us; the launch traced here: 53.2 us
  starting transfers between devices  25.3 us (47%)
  waiting for transfers between devices  13.6 us (25%)
  Pallas kernels  10.3 us (19%)
  local copies, waits for them, and re-layouts  2.21 us (4%)
  between operations  0.86 us (2%)
  other arithmetic  0.85 us (2%)
    ppermute x26, starting transfers between devices, swap(): lax.ppermute(value, axis, [(i, i ^ mask) for i in range(lax.axis_size(axi...  25.3 us
    ppermute x26, waiting for transfers between devices, swap(): lax.ppermute(value, axis, [(i, i ^ mask) for i in range(lax.axis_size(axi...  13.6 us
    pallas_call x4, Pallas kernels, term(): call(partial(term_kernel, wanted, len(after)), in_specs=[pl.BlockSpec(mem...  2.45 us
    pallas_call x4, Pallas kernels, first(): call(partial(first_kernel, rows, spots, len(before)), shape(f32, blocks *...  2.37 us
    unnamed x8, local copies, waits for them, and re-layouts  2.21 us
    pallas_call x2, Pallas kernels, on_device(): call(partial(second_kernel, rows, cols, spots), (shape(bf16, pay_rows, wi...  1.63 us
    pallas_call x2, Pallas kernels, on_device(): call(partial(far_kernel, rows, cols, groups, ncells_all, spots_of(away, T...  1.63 us
  transfers between devices with their start and end apart: 26, of which 10 were waited for; matrix products, arithmetic and copies ran while one was open for 0% of the time, Pallas kernels for 12%

profile of v16, /device:TPU:0, one launch (start us, length us, event | category | flops | bytes accessed | tf_op | source)
XLA Modules:
  0.0 53.2 jit_solution(15269424314718132194)
XLA Ops:
  0.6 0.8 %fusion.refs_0_ = bf16[1,128,128]{2,1,0:T(8,128)(2,1)S(1)} fusion(f32[16,8,128]{2,1,0:T(8,128)} %param.4), kind=kLoop, calls=%fused_computation.1 | loop fusion | flops 32768 | bytes 98304 | tf_op jit(solution)/shard_map/convert_element_type | solution.py:279
  1.5 3.5 %collective-permute-start.3 = (bf16[1,128,128]{2,1,0:T(8,128)(2,1)S(1)}, bf16[1,128,128]{2,1,0:T(8,128)(2,1)S(1)}, u32[]{:S(2)}, u32[]{:S(2)}) collective-permute-start(bf16[1,128,128]{2,1,0:T(8,128)(2,1)S(1)} %fusion.refs_0_), channel_id=1, source_target_pairs={{0,5},{1,4},{2,7},{3,6},{4,1},{5,0},{6,3},{7,2},{8,13},{9,12},{10,... | collective-permute-start | bytes 98312 | tf_op jit(solution)/shard_map/ppermute | solution.py:40
  5.0 1.6 %collective-permute-start.2 = (bf16[1,128,128]{2,1,0:T(8,128)(2,1)S(1)}, bf16[1,128,128]{2,1,0:T(8,128)(2,1)S(1)}, u32[]{:S(2)}, u32[]{:S(2)}) collective-permute-start(bf16[1,128,128]{2,1,0:T(8,128)(2,1)S(1)} %fusion.refs_0_), channel_id=1, source_target_pairs={{0,7},{1,6},{2,5},{3,4},{4,3},{5,2},{6,1},{7,0},{8,15},{9,14},{10,... | collective-permute-start | bytes 98312 | tf_op jit(solution)/shard_map/ppermute | solution.py:40
  6.6 0.2 collective-permute-start.1
  6.8 2.2 %copy-done = bf16[256,8,1024]{2,1,0:T(8,128)(2,1)S(1)} copy-done((bf16[256,8,1024]{2,1,0:T(8,128)(2,1)S(1)}, bf16[256,8,1024]{2,1,0:T(8,128)(2,1)}, u32[]{:S(2)}) %copy-start) | copy-done | bytes 4194328
  9.0 0.4 load.1.factor_ref
  9.4 0.0 copy-start.1
  9.4 0.5 project_own.4.refs_0_.refs_2_
  9.9 0.0 collective-permute-done.3.refs_4_
  9.9 0.3 collective-permute-done.2.refs_3_
  10.2 0.2 collective-permute-done.1.refs_2_
  10.4 0.0 collective-permute-done.refs_1_.twin_ref
  10.4 0.7 %collective-permute-start.4 = (bf16[3,128,128]{2,1,0:T(8,128)(2,1)S(1)}, bf16[3,128,128]{2,1,0:T(8,128)(2,1)S(1)}, u32[]{:S(2)}, u32[]{:S(2)}) collective-permute-start(bf16[3,128,128]{2,1,0:T(8,128)(2,1)S(1)} %join.2.bundle_ref.refs_0_), channel_id=1, source_target_pairs={{0,1},{1,0},{2,3},{3,2},{4,5},{5,4},{6,7},{7,6},{8,9},{9,8},{10,11... | collective-permute-start | bytes 294920 | tf_op jit(solution)/shard_map/ppermute | solution.py:40
  11.1 0.4 columns.2
  11.5 0.0 copy-start.3
  11.5 0.7 %project_own.5.diag_ref = f32[256,128]{1,0:T(8,128)S(1)} custom-call(bf16[2048,1024]{1,0:T(8,128)(2,1)S(1)} %load.1.factor_ref, bf16[3,128,128]{2,1,0:T(8,128)(2,1)S(1)} %join.2.bundle_ref.refs_0_, bf16[1,128,128]{2,1,0:T(8,128)(2,1)S(1)} %collective-permute-done.refs_1_.twin_ref, f32[256,128]{1,0:T(8,128)S(1)} %project_own.4.refs_0_.refs_2_), custom_call_target="tpu_custom_call" | custom-call | flops 268435456 | bytes 2097152 | tf_op jit(solution)/shard_map/project_own/pallas_call | solution.py:315
  12.2 0.0 collective-permute-done.4.fields_ref
  12.2 0.8 %project_across.2 = (bf16[192,128]{1,0:T(8,128)(2,1)S(1)}, bf16[64,128]{1,0:T(8,128)(2,1)S(1)}) custom-call(bf16[2048,1024]{1,0:T(8,128)(2,1)S(1)} %load.1.factor_ref, f32[256,128]{1,0:T(8,128)S(1)} %project_own.5.diag_ref, bf16[3,128,128]{2,1,0:T(8,128)(2,1)S(1)} %collective-permute-done.4.fields_ref, bf16[128,128]{1,0:T(8,128)(2,1)S(1)} %get-tuple-element.30.short_ref), custom_call_target="tpu_custom_call" | custom-call | flops 268435456 | bytes 2097152 | tf_op jit(solution)/shard_map/project_across/pallas_call | solution.py:349
  13.0 2.5 %collective-permute-start.6 = (bf16[192,128]{1,0:T(8,128)(2,1)S(1)}, bf16[192,128]{1,0:T(8,128)(2,1)S(1)}, u32[]{:S(2)}, u32[]{:S(2)}) collective-permute-start(bf16[192,128]{1,0:T(8,128)(2,1)S(1)} %get-tuple-element.31), channel_id=1, source_target_pairs={{0,24},{8,16},{16,8},{24,0},{1,25},{9,17},{17,9},{25,1},{2,26},{10... | collective-permute-start | bytes 147464 | tf_op jit(solution)/shard_map/ppermute | solution.py:40
  15.5 0.5 %collective-permute-start.5 = (bf16[192,128]{1,0:T(8,128)(2,1)S(1)}, bf16[192,128]{1,0:T(8,128)(2,1)S(1)}, u32[]{:S(2)}, u32[]{:S(2)}) collective-permute-start(bf16[192,128]{1,0:T(8,128)(2,1)S(1)} %get-tuple-element.31), channel_id=1, source_target_pairs={{0,8},{8,0},{16,24},{24,16},{1,9},{9,1},{17,25},{25,17},{2,10},{10... | collective-permute-start | bytes 147464 | tf_op jit(solution)/shard_map/ppermute | solution.py:40
  16.1 0.5 collective-permute-start.7
  16.6 3.2 %collective-permute-done.7.refs_2_ = bf16[64,128]{1,0:T(8,128)(2,1)S(1)} collective-permute-done((bf16[64,128]{1,0:T(8,128)(2,1)S(1)}, bf16[64,128]{1,0:T(8,128)(2,1)S(1)}, u32[]{:S(2)}, u32[]{:S(2)}) %collective-permute-start.7) | collective-permute-done | bytes 16416 | tf_op jit(solution)/shard_map/ppermute | solution.py:40
  19.8 0.0 collective-permute-done.6.refs_1_.refs_3_
  19.8 0.0 copy-start.2
  19.8 0.9 %term_first.2 = (bf16[128,2048]{1,0:T(8,128)(2,1)S(1)}, bf16[3,128,128]{2,1,0:T(8,128)(2,1)S(1)}) custom-call(f32[1,256]{1,0:T(1,128)S(1)} %bitcast.13, bf16[2048,1024]{1,0:T(8,128)(2,1)S(1)} %load.1.factor_ref, bf16[64,128]{1,0:T(8,128)(2,1)S(1)} %get-tuple-element.32.refs_0_, bf16[192,128]{1,0:T(8,128)(2,1)S(1)} %collective-permute-done.5.refs_0_.refs_1_, ...), custom_call_target="tpu_custom_call" | custom-call | flops 134217728 | bytes 2097152 | tf_op jit(solution)/shard_map/term_first/pallas_call | solution.py:358
  20.7 0.1 collective-permute-start.8
  20.8 0.8 %term.4 = (f32[3,128,128]{2,1,0:T(8,128)S(1)}, bf16[1,128,128]{2,1,0:T(8,128)(2,1)S(1)}) custom-call(bf16[128,2048]{1,0:T(8,128)(2,1)S(1)} %get-tuple-element.33.coef_ref, bf16[2048,1024]{1,0:T(8,128)(2,1)S(1)} %load.1.factor_ref), custom_call_target="tpu_custom_call" | custom-call | flops 268435456 | bytes 2097152 | tf_op jit(solution)/shard_map/term/pallas_call | solution.py:368
  21.6 0.6 %collective-permute-start.9 = (bf16[1,128,128]{2,1,0:T(8,128)(2,1)S(1)}, bf16[1,128,128]{2,1,0:T(8,128)(2,1)S(1)}, u32[]{:S(2)}, u32[]{:S(2)}) collective-permute-start(bf16[1,128,128]{2,1,0:T(8,128)(2,1)S(1)} %get-tuple-element.39), channel_id=1, source_target_pairs={{0,1},{1,0},{2,3},{3,2},{4,5},{5,4},{6,7},{7,6},{8,9},{9,8},{10,11... | collective-permute-start | bytes 98312 | tf_op jit(solution)/shard_map/ppermute | solution.py:40
  22.1 0.0 collective-permute-done.8.got_ref
  22.2 1.8 %collective-permute-start.10 = (bf16[1,128,128]{2,1,0:T(8,128)(2,1)S(1)}, bf16[1,128,128]{2,1,0:T(8,128)(2,1)S(1)}, u32[]{:S(2)}, u32[]{:S(2)}) collective-permute-start(bf16[1,128,128]{2,1,0:T(8,128)(2,1)S(1)} %get-tuple-element.36.refs_0_), channel_id=1, source_target_pairs={{0,5},{1,4},{2,7},{3,6},{4,1},{5,0},{6,3},{7,2},{8,13},{9,12},{10,... | collective-permute-start | bytes 98312 | tf_op jit(solution)/shard_map/ppermute | solution.py:40
  23.9 1.4 %collective-permute-start.11 = (bf16[1,128,128]{2,1,0:T(8,128)(2,1)S(1)}, bf16[1,128,128]{2,1,0:T(8,128)(2,1)S(1)}, u32[]{:S(2)}, u32[]{:S(2)}) collective-permute-start(bf16[1,128,128]{2,1,0:T(8,128)(2,1)S(1)} %get-tuple-element.37.refs_1_), channel_id=1, source_target_pairs={{0,7},{1,6},{2,5},{3,4},{4,3},{5,2},{6,1},{7,0},{8,15},{9,14},{10,... | collective-permute-start | bytes 98312 | tf_op jit(solution)/shard_map/ppermute | solution.py:40
  25.4 0.0 collective-permute-start.12
  25.4 0.2 local.2.base_ref
  25.5 0.3 term.5.mine_ref
  25.9 0.0 collective-permute-done.9.got_ref
  25.9 0.7 %collective-permute-done.10.refs_1_ = bf16[1,128,128]{2,1,0:T(8,128)(2,1)S(1)} collective-permute-done((bf16[1,128,128]{2,1,0:T(8,128)(2,1)S(1)}, bf16[1,128,128]{2,1,0:T(8,128)(2,1)S(1)}, u32[]{:S(2)}, u32[]{:S(2)}) %collective-permute-start.10) | collective-permute-done | bytes 32800 | tf_op jit(solution)/shard_map/ppermute | solution.py:40
  26.6 2.6 %collective-permute-done.11.refs_2_ = bf16[1,128,128]{2,1,0:T(8,128)(2,1)S(1)} collective-permute-done((bf16[1,128,128]{2,1,0:T(8,128)(2,1)S(1)}, bf16[1,128,128]{2,1,0:T(8,128)(2,1)S(1)}, u32[]{:S(2)}, u32[]{:S(2)}) %collective-permute-start.11) | collective-permute-done | bytes 32800 | tf_op jit(solution)/shard_map/ppermute | solution.py:40
  29.2 0.0 collective-permute-done.12.refs_3_
  29.2 1.0 %collective-permute-start.16 = (bf16[1,128,128]{2,1,0:T(8,128)(2,1)S(1)}, bf16[1,128,128]{2,1,0:T(8,128)(2,1)S(1)}, u32[]{:S(2)}, u32[]{:S(2)}) collective-permute-start(bf16[1,128,128]{2,1,0:T(8,128)(2,1)S(1)} %get-tuple-element.41.refs_0_), channel_id=1, source_target_pairs={{0,5},{1,4},{2,7},{3,6},{4,1},{5,0},{6,3},{7,2},{8,13},{9,12},{10,... | collective-permute-start | bytes 98312 | tf_op jit(solution)/shard_map/ppermute | solution.py:40
  30.2 1.3 %collective-permute-start.15 = (bf16[1,128,128]{2,1,0:T(8,128)(2,1)S(1)}, bf16[1,128,128]{2,1,0:T(8,128)(2,1)S(1)}, u32[]{:S(2)}, u32[]{:S(2)}) collective-permute-start(bf16[1,128,128]{2,1,0:T(8,128)(2,1)S(1)} %get-tuple-element.41.refs_0_), channel_id=1, source_target_pairs={{0,7},{1,6},{2,5},{3,4},{4,3},{5,2},{6,1},{7,0},{8,15},{9,14},{10,... | collective-permute-start | bytes 98312 | tf_op jit(solution)/shard_map/ppermute | solution.py:40
  31.5 1.0 %collective-permute-start.14 = (bf16[1,128,128]{2,1,0:T(8,128)(2,1)S(1)}, bf16[1,128,128]{2,1,0:T(8,128)(2,1)S(1)}, u32[]{:S(2)}, u32[]{:S(2)}) collective-permute-start(bf16[1,128,128]{2,1,0:T(8,128)(2,1)S(1)} %get-tuple-element.41.refs_0_), channel_id=1, source_target_pairs={{0,3},{1,2},{2,1},{3,0},{4,7},{5,6},{6,5},{7,4},{8,11},{9,10},{10,... | collective-permute-start | bytes 98312 | tf_op jit(solution)/shard_map/ppermute | solution.py:40
  32.5 0.1 collective-permute-start.13
  32.6 0.5 project_own.6.refs_0_.refs_2_
  33.1 0.9 %collective-permute-done.16.refs_4_ = bf16[1,128,128]{2,1,0:T(8,128)(2,1)S(1)} collective-permute-done((bf16[1,128,128]{2,1,0:T(8,128)(2,1)S(1)}, bf16[1,128,128]{2,1,0:T(8,128)(2,1)S(1)}, u32[]{:S(2)}, u32[]{:S(2)}) %collective-permute-start.16) | collective-permute-done | bytes 32800 | tf_op jit(solution)/shard_map/ppermute | solution.py:40
  34.0 1.4 %collective-permute-done.15.refs_3_ = bf16[1,128,128]{2,1,0:T(8,128)(2,1)S(1)} collective-permute-done((bf16[1,128,128]{2,1,0:T(8,128)(2,1)S(1)}, bf16[1,128,128]{2,1,0:T(8,128)(2,1)S(1)}, u32[]{:S(2)}, u32[]{:S(2)}) %collective-permute-start.15) | collective-permute-done | bytes 32800 | tf_op jit(solution)/shard_map/ppermute | solution.py:40
  35.4 0.5 %collective-permute-start.17 = (bf16[3,128,128]{2,1,0:T(8,128)(2,1)S(1)}, bf16[3,128,128]{2,1,0:T(8,128)(2,1)S(1)}, u32[]{:S(2)}, u32[]{:S(2)}) collective-permute-start(bf16[3,128,128]{2,1,0:T(8,128)(2,1)S(1)} %join.3.bundle_ref.refs_0_), channel_id=1, source_target_pairs={{0,1},{1,0},{2,3},{3,2},{4,5},{5,4},{6,7},{7,6},{8,9},{9,8},{10,11... | collective-permute-start | bytes 294920 | tf_op jit(solution)/shard_map/ppermute | solution.py:40
  36.0 0.3 columns.3
  36.3 0.7 %project_own.7.diag_ref = f32[256,128]{1,0:T(8,128)S(1)} custom-call(bf16[2048,1024]{1,0:T(8,128)(2,1)S(1)} %load.1.factor_ref, bf16[3,128,128]{2,1,0:T(8,128)(2,1)S(1)} %join.3.bundle_ref.refs_0_, bf16[1,128,128]{2,1,0:T(8,128)(2,1)S(1)} %collective-permute-done.13.refs_1_.twin_ref, f32[256,128]{1,0:T(8,128)S(1)} %project_own.6.refs_0_.refs_2_), custom_call_target="tpu_custom_call" | custom-call | flops 268435456 | bytes 2097152 | tf_op jit(solution)/shard_map/project_own/pallas_call | solution.py:315
  37.1 0.8 %project_across.3 = (bf16[192,128]{1,0:T(8,128)(2,1)S(1)}, bf16[64,128]{1,0:T(8,128)(2,1)S(1)}) custom-call(bf16[2048,1024]{1,0:T(8,128)(2,1)S(1)} %load.1.factor_ref, f32[256,128]{1,0:T(8,128)S(1)} %project_own.7.diag_ref, bf16[3,128,128]{2,1,0:T(8,128)(2,1)S(1)} %collective-permute-done.17.fields_ref, bf16[128,128]{1,0:T(8,128)(2,1)S(1)} %get-tuple-element.43.short_ref), custom_call_target="tpu_custom_call" | custom-call | flops 268435456 | bytes 2097152 | tf_op jit(solution)/shard_map/project_across/pallas_call | solution.py:349
  37.9 1.5 %collective-permute-start.19 = (bf16[192,128]{1,0:T(8,128)(2,1)S(1)}, bf16[192,128]{1,0:T(8,128)(2,1)S(1)}, u32[]{:S(2)}, u32[]{:S(2)}) collective-permute-start(bf16[192,128]{1,0:T(8,128)(2,1)S(1)} %get-tuple-element.44), channel_id=1, source_target_pairs={{0,24},{8,16},{16,8},{24,0},{1,25},{9,17},{17,9},{25,1},{2,26},{10... | collective-permute-start | bytes 147464 | tf_op jit(solution)/shard_map/ppermute | solution.py:40
  39.3 0.5 %collective-permute-start.18 = (bf16[192,128]{1,0:T(8,128)(2,1)S(1)}, bf16[192,128]{1,0:T(8,128)(2,1)S(1)}, u32[]{:S(2)}, u32[]{:S(2)}) collective-permute-start(bf16[192,128]{1,0:T(8,128)(2,1)S(1)} %get-tuple-element.44), channel_id=1, source_target_pairs={{0,8},{8,0},{16,24},{24,16},{1,9},{9,1},{17,25},{25,17},{2,10},{10... | collective-permute-start | bytes 147464 | tf_op jit(solution)/shard_map/ppermute | solution.py:40
  39.9 1.5 %collective-permute-start.20 = (bf16[64,128]{1,0:T(8,128)(2,1)S(1)}, bf16[64,128]{1,0:T(8,128)(2,1)S(1)}, u32[]{:S(2)}, u32[]{:S(2)}) collective-permute-start(bf16[64,128]{1,0:T(8,128)(2,1)S(1)} %get-tuple-element.45.refs_0_), channel_id=1, source_target_pairs={{0,16},{8,24},{16,0},{24,8},{1,17},{9,25},{17,1},{25,9},{2,18},{10... | collective-permute-start | bytes 49160 | tf_op jit(solution)/shard_map/ppermute | solution.py:40
  41.4 2.2 %collective-permute-done.20.refs_2_ = bf16[64,128]{1,0:T(8,128)(2,1)S(1)} collective-permute-done((bf16[64,128]{1,0:T(8,128)(2,1)S(1)}, bf16[64,128]{1,0:T(8,128)(2,1)S(1)}, u32[]{:S(2)}, u32[]{:S(2)}) %collective-permute-start.20) | collective-permute-done | bytes 16416 | tf_op jit(solution)/shard_map/ppermute | solution.py:40
  43.6 0.7 %term_first.3 = (bf16[128,2048]{1,0:T(8,128)(2,1)S(1)}, bf16[2,128,128]{2,1,0:T(8,128)(2,1)S(1)}) custom-call(f32[1,256]{1,0:T(1,128)S(1)} %bitcast.14, bf16[2048,1024]{1,0:T(8,128)(2,1)S(1)} %load.1.factor_ref, bf16[64,128]{1,0:T(8,128)(2,1)S(1)} %get-tuple-element.45.refs_0_, bf16[192,128]{1,0:T(8,128)(2,1)S(1)} %collective-permute-done.18.refs_0_.refs_1_, ...), custom_call_target="tpu_custom_call" | custom-call | flops 134217728 | bytes 2097152 | tf_op jit(solution)/shard_map/term_first/pallas_call | solution.py:358
  44.4 0.1 collective-permute-start.21
  44.4 0.8 %term.6 = (f32[2,128,128]{2,1,0:T(8,128)S(1)}, bf16[2,128,128]{2,1,0:T(8,128)(2,1)S(1)}) custom-call(bf16[128,2048]{1,0:T(8,128)(2,1)S(1)} %get-tuple-element.46.coef_ref, bf16[2048,1024]{1,0:T(8,128)(2,1)S(1)} %load.1.factor_ref), custom_call_target="tpu_custom_call" | custom-call | flops 268435456 | bytes 2097152 | tf_op jit(solution)/shard_map/term/pallas_call | solution.py:368
  45.3 0.6 %collective-permute-start.22 = (bf16[2,128,128]{2,1,0:T(8,128)(2,1)S(1)}, bf16[2,128,128]{2,1,0:T(8,128)(2,1)S(1)}, u32[]{:S(2)}, u32[]{:S(2)}) collective-permute-start(bf16[2,128,128]{2,1,0:T(8,128)(2,1)S(1)} %get-tuple-element.51), channel_id=1, source_target_pairs={{0,1},{1,0},{2,3},{3,2},{4,5},{5,4},{6,7},{7,6},{8,9},{9,8},{10,11... | collective-permute-start | bytes 196616 | tf_op jit(solution)/shard_map/ppermute | solution.py:40
  45.8 2.1 %collective-permute-start.23 = (bf16[1,128,128]{2,1,0:T(8,128)(2,1)S(1)}, bf16[1,128,128]{2,1,0:T(8,128)(2,1)S(1)}, u32[]{:S(2)}, u32[]{:S(2)}) collective-permute-start(bf16[1,128,128]{2,1,0:T(8,128)(2,1)S(1)} %get-tuple-element.49.refs_0_), channel_id=1, source_target_pairs={{0,7},{1,6},{2,5},{3,4},{4,3},{5,2},{6,1},{7,0},{8,15},{9,14},{10,... | collective-permute-start | bytes 98312 | tf_op jit(solution)/shard_map/ppermute | solution.py:40
  47.9 0.5 term.7.mine_ref
  48.4 1.8 %collective-permute-start.25 = (bf16[1,128,128]{2,1,0:T(8,128)(2,1)S(1)}, bf16[1,128,128]{2,1,0:T(8,128)(2,1)S(1)}, u32[]{:S(2)}, u32[]{:S(2)}) collective-permute-start(bf16[1,128,128]{2,1,0:T(8,128)(2,1)S(1)} %get-tuple-element.53), channel_id=1, source_target_pairs={{0,3},{1,2},{2,1},{3,0},{4,7},{5,6},{6,5},{7,4},{8,11},{9,10},{10,... | collective-permute-start | bytes 98312 | tf_op jit(solution)/shard_map/ppermute | solution.py:40
  50.3 0.2 local.3.base_ref
  50.4 0.8 %collective-permute-done.23.refs_1_ = bf16[1,128,128]{2,1,0:T(8,128)(2,1)S(1)} collective-permute-done((bf16[1,128,128]{2,1,0:T(8,128)(2,1)S(1)}, bf16[1,128,128]{2,1,0:T(8,128)(2,1)S(1)}, u32[]{:S(2)}, u32[]{:S(2)}) %collective-permute-start.23) | collective-permute-done | bytes 32800 | tf_op jit(solution)/shard_map/ppermute | solution.py:40
  51.2 1.3 %collective-permute-done.24.refs_2_ = bf16[1,128,128]{2,1,0:T(8,128)(2,1)S(1)} collective-permute-done((bf16[1,128,128]{2,1,0:T(8,128)(2,1)S(1)}, bf16[1,128,128]{2,1,0:T(8,128)(2,1)S(1)}, u32[]{:S(2)}, u32[]{:S(2)}) %collective-permute-start.24) | collective-permute-done | bytes 32800 | tf_op jit(solution)/shard_map/ppermute | solution.py:40
  52.5 0.7 %update.3 = (f32[128,128]{1,0:T(8,128)}, f32[128,128]{1,0:T(8,128)}) custom-call(f32[128,128]{1,0:T(8,128)S(1)} %get-tuple-element.40.x_ref, f32[128,128]{1,0:T(8,128)S(1)} %local.3.base_ref, f32[1,128,128]{2,1,0:T(8,128)S(1)} %get-tuple-element.52.refs_0_, bf16[1,128,128]{2,1,0:T(8,128)(2,1)S(1)} %collective-permute-done.23.refs_1_, ...), custom_call_target="tpu_custom_call" | custom-call | bytes 262144 | tf_op jit(solution)/shard_map/update/pallas_call | solution.py:396
  (22 shorter events, 0.1 us)
Async XLA Ops:
  1.5 8.4 %collective-permute-start.3 = (bf16[1,128,128]{2,1,0:T(8,128)(2,1)S(1)}, bf16[1,128,128]{2,1,0:T(8,128)(2,1)S(1)}, u32[]{:S(2)}, u32[]{:S(2)}) collective-permute-start(bf16[1,128,128]{2,1,0:T(8,128)(2,1)S(1)} %fusion.refs_0_), channel_id=1, source_target_pairs={{0,5},{1,4},{2,7},{3,6},{4,1},{5,0},{6,3},{7,2},{8,13},{9,12},{10,... | collective-permute-start | bytes 98312 | tf_op jit(solution)/shard_map/ppermute | solution.py:40
  5.0 5.2 %collective-permute-start.2 = (bf16[1,128,128]{2,1,0:T(8,128)(2,1)S(1)}, bf16[1,128,128]{2,1,0:T(8,128)(2,1)S(1)}, u32[]{:S(2)}, u32[]{:S(2)}) collective-permute-start(bf16[1,128,128]{2,1,0:T(8,128)(2,1)S(1)} %fusion.refs_0_), channel_id=1, source_target_pairs={{0,7},{1,6},{2,5},{3,4},{4,3},{5,2},{6,1},{7,0},{8,15},{9,14},{10,... | collective-permute-start | bytes 98312 | tf_op jit(solution)/shard_map/ppermute | solution.py:40
  6.6 3.8 %collective-permute-start.1 = (bf16[1,128,128]{2,1,0:T(8,128)(2,1)S(1)}, bf16[1,128,128]{2,1,0:T(8,128)(2,1)S(1)}, u32[]{:S(2)}, u32[]{:S(2)}) collective-permute-start(bf16[1,128,128]{2,1,0:T(8,128)(2,1)S(1)} %fusion.refs_0_), channel_id=1, source_target_pairs={{0,3},{1,2},{2,1},{3,0},{4,7},{5,6},{6,5},{7,4},{8,11},{9,10},{10,... | collective-permute-start | bytes 98312 | tf_op jit(solution)/shard_map/ppermute | solution.py:40
  6.8 3.5 %collective-permute-start = (bf16[1,128,128]{2,1,0:T(8,128)(2,1)S(1)}, bf16[1,128,128]{2,1,0:T(8,128)(2,1)S(1)}, u32[]{:S(2)}, u32[]{:S(2)}) collective-permute-start(bf16[1,128,128]{2,1,0:T(8,128)(2,1)S(1)} %fusion.refs_0_), channel_id=1, source_target_pairs={{0,1},{1,0},{2,3},{3,2},{4,5},{5,4},{6,7},{7,6},{8,9},{9,8},{10,11... | collective-permute-start | bytes 98312 | tf_op jit(solution)/shard_map/ppermute | solution.py:40
  6.8 2.2 %copy-start = (bf16[256,8,1024]{2,1,0:T(8,128)(2,1)S(1)}, bf16[256,8,1024]{2,1,0:T(8,128)(2,1)}, u32[]{:S(2)}) copy-start(bf16[256,8,1024]{2,1,0:T(8,128)(2,1)} %param.6) | copy-start | bytes 12582916
  9.4 1.7 %copy-start.1 = (f32[16,8,128]{2,1,0:T(8,128)S(1)}, f32[16,8,128]{2,1,0:T(8,128)}, u32[]{:S(2)}) copy-start(f32[16,8,128]{2,1,0:T(8,128)} %param.4) | copy-start | bytes 196612
  10.4 1.8 %collective-permute-start.4 = (bf16[3,128,128]{2,1,0:T(8,128)(2,1)S(1)}, bf16[3,128,128]{2,1,0:T(8,128)(2,1)S(1)}, u32[]{:S(2)}, u32[]{:S(2)}) collective-permute-start(bf16[3,128,128]{2,1,0:T(8,128)(2,1)S(1)} %join.2.bundle_ref.refs_0_), channel_id=1, source_target_pairs={{0,1},{1,0},{2,3},{3,2},{4,5},{5,4},{6,7},{7,6},{8,9},{9,8},{10,11... | collective-permute-start | bytes 294920 | tf_op jit(solution)/shard_map/ppermute | solution.py:40
  11.5 8.3 %copy-start.3 = (f32[256]{0:T(256)S(1)}, f32[256]{0:T(256)}, u32[]{:S(2)}) copy-start(f32[256]{0:T(256)} %param.7) | copy-start | bytes 3076
  13.0 6.7 %collective-permute-start.6 = (bf16[192,128]{1,0:T(8,128)(2,1)S(1)}, bf16[192,128]{1,0:T(8,128)(2,1)S(1)}, u32[]{:S(2)}, u32[]{:S(2)}) collective-permute-start(bf16[192,128]{1,0:T(8,128)(2,1)S(1)} %get-tuple-element.31), channel_id=1, source_target_pairs={{0,24},{8,16},{16,8},{24,0},{1,25},{9,17},{17,9},{25,1},{2,26},{10... | collective-permute-start | bytes 147464 | tf_op jit(solution)/shard_map/ppermute | solution.py:40
  15.5 4.3 %collective-permute-start.5 = (bf16[192,128]{1,0:T(8,128)(2,1)S(1)}, bf16[192,128]{1,0:T(8,128)(2,1)S(1)}, u32[]{:S(2)}, u32[]{:S(2)}) collective-permute-start(bf16[192,128]{1,0:T(8,128)(2,1)S(1)} %get-tuple-element.31), channel_id=1, source_target_pairs={{0,8},{8,0},{16,24},{24,16},{1,9},{9,1},{17,25},{25,17},{2,10},{10... | collective-permute-start | bytes 147464 | tf_op jit(solution)/shard_map/ppermute | solution.py:40
  16.1 3.7 %collective-permute-start.7 = (bf16[64,128]{1,0:T(8,128)(2,1)S(1)}, bf16[64,128]{1,0:T(8,128)(2,1)S(1)}, u32[]{:S(2)}, u32[]{:S(2)}) collective-permute-start(bf16[64,128]{1,0:T(8,128)(2,1)S(1)} %get-tuple-element.32.refs_0_), channel_id=1, source_target_pairs={{0,16},{8,24},{16,0},{24,8},{1,17},{9,25},{17,1},{25,9},{2,18},{10... | collective-permute-start | bytes 49160 | tf_op jit(solution)/shard_map/ppermute | solution.py:40
  19.8 5.6 %copy-start.2 = (f32[8,128]{1,0:T(8,128)S(1)}, f32[8,128]{1,0:T(8,128)}, u32[]{:S(2)}) copy-start(f32[8,128]{1,0:T(8,128)} %amp_ref.3) | copy-start | bytes 12292
  20.7 1.4 %collective-permute-start.8 = (bf16[3,128,128]{2,1,0:T(8,128)(2,1)S(1)}, bf16[3,128,128]{2,1,0:T(8,128)(2,1)S(1)}, u32[]{:S(2)}, u32[]{:S(2)}) collective-permute-start(bf16[3,128,128]{2,1,0:T(8,128)(2,1)S(1)} %get-tuple-element.35), channel_id=1, source_target_pairs={{0,1},{1,0},{2,3},{3,2},{4,5},{5,4},{6,7},{7,6},{8,9},{9,8},{10,11... | collective-permute-start | bytes 294920 | tf_op jit(solution)/shard_map/ppermute | solution.py:40
  21.6 4.3 %collective-permute-start.9 = (bf16[1,128,128]{2,1,0:T(8,128)(2,1)S(1)}, bf16[1,128,128]{2,1,0:T(8,128)(2,1)S(1)}, u32[]{:S(2)}, u32[]{:S(2)}) collective-permute-start(bf16[1,128,128]{2,1,0:T(8,128)(2,1)S(1)} %get-tuple-element.39), channel_id=1, source_target_pairs={{0,1},{1,0},{2,3},{3,2},{4,5},{5,4},{6,7},{7,6},{8,9},{9,8},{10,11... | collective-permute-start | bytes 98312 | tf_op jit(solution)/shard_map/ppermute | solution.py:40
  22.2 4.4 %collective-permute-start.10 = (bf16[1,128,128]{2,1,0:T(8,128)(2,1)S(1)}, bf16[1,128,128]{2,1,0:T(8,128)(2,1)S(1)}, u32[]{:S(2)}, u32[]{:S(2)}) collective-permute-start(bf16[1,128,128]{2,1,0:T(8,128)(2,1)S(1)} %get-tuple-element.36.refs_0_), channel_id=1, source_target_pairs={{0,5},{1,4},{2,7},{3,6},{4,1},{5,0},{6,3},{7,2},{8,13},{9,12},{10,... | collective-permute-start | bytes 98312 | tf_op jit(solution)/shard_map/ppermute | solution.py:40
  23.9 5.2 %collective-permute-start.11 = (bf16[1,128,128]{2,1,0:T(8,128)(2,1)S(1)}, bf16[1,128,128]{2,1,0:T(8,128)(2,1)S(1)}, u32[]{:S(2)}, u32[]{:S(2)}) collective-permute-start(bf16[1,128,128]{2,1,0:T(8,128)(2,1)S(1)} %get-tuple-element.37.refs_1_), channel_id=1, source_target_pairs={{0,7},{1,6},{2,5},{3,4},{4,3},{5,2},{6,1},{7,0},{8,15},{9,14},{10,... | collective-permute-start | bytes 98312 | tf_op jit(solution)/shard_map/ppermute | solution.py:40
  25.4 3.8 %collective-permute-start.12 = (bf16[1,128,128]{2,1,0:T(8,128)(2,1)S(1)}, bf16[1,128,128]{2,1,0:T(8,128)(2,1)S(1)}, u32[]{:S(2)}, u32[]{:S(2)}) collective-permute-start(bf16[1,128,128]{2,1,0:T(8,128)(2,1)S(1)} %get-tuple-element.38.refs_2_), channel_id=1, source_target_pairs={{0,3},{1,2},{2,1},{3,0},{4,7},{5,6},{6,5},{7,4},{8,11},{9,10},{10,... | collective-permute-start | bytes 98312 | tf_op jit(solution)/shard_map/ppermute | solution.py:40
  29.2 4.7 %collective-permute-start.16 = (bf16[1,128,128]{2,1,0:T(8,128)(2,1)S(1)}, bf16[1,128,128]{2,1,0:T(8,128)(2,1)S(1)}, u32[]{:S(2)}, u32[]{:S(2)}) collective-permute-start(bf16[1,128,128]{2,1,0:T(8,128)(2,1)S(1)} %get-tuple-element.41.refs_0_), channel_id=1, source_target_pairs={{0,5},{1,4},{2,7},{3,6},{4,1},{5,0},{6,3},{7,2},{8,13},{9,12},{10,... | collective-permute-start | bytes 98312 | tf_op jit(solution)/shard_map/ppermute | solution.py:40
  30.2 5.2 %collective-permute-start.15 = (bf16[1,128,128]{2,1,0:T(8,128)(2,1)S(1)}, bf16[1,128,128]{2,1,0:T(8,128)(2,1)S(1)}, u32[]{:S(2)}, u32[]{:S(2)}) collective-permute-start(bf16[1,128,128]{2,1,0:T(8,128)(2,1)S(1)} %get-tuple-element.41.refs_0_), channel_id=1, source_target_pairs={{0,7},{1,6},{2,5},{3,4},{4,3},{5,2},{6,1},{7,0},{8,15},{9,14},{10,... | collective-permute-start | bytes 98312 | tf_op jit(solution)/shard_map/ppermute | solution.py:40
  31.5 3.9 %collective-permute-start.14 = (bf16[1,128,128]{2,1,0:T(8,128)(2,1)S(1)}, bf16[1,128,128]{2,1,0:T(8,128)(2,1)S(1)}, u32[]{:S(2)}, u32[]{:S(2)}) collective-permute-start(bf16[1,128,128]{2,1,0:T(8,128)(2,1)S(1)} %get-tuple-element.41.refs_0_), channel_id=1, source_target_pairs={{0,3},{1,2},{2,1},{3,0},{4,7},{5,6},{6,5},{7,4},{8,11},{9,10},{10,... | collective-permute-start | bytes 98312 | tf_op jit(solution)/shard_map/ppermute | solution.py:40
  32.5 2.9 %collective-permute-start.13 = (bf16[1,128,128]{2,1,0:T(8,128)(2,1)S(1)}, bf16[1,128,128]{2,1,0:T(8,128)(2,1)S(1)}, u32[]{:S(2)}, u32[]{:S(2)}) collective-permute-start(bf16[1,128,128]{2,1,0:T(8,128)(2,1)S(1)} %get-tuple-element.41.refs_0_), channel_id=1, source_target_pairs={{0,1},{1,0},{2,3},{3,2},{4,5},{5,4},{6,7},{7,6},{8,9},{9,8},{10,11... | collective-permute-start | bytes 98312 | tf_op jit(solution)/shard_map/ppermute | solution.py:40
  35.4 1.6 %collective-permute-start.17 = (bf16[3,128,128]{2,1,0:T(8,128)(2,1)S(1)}, bf16[3,128,128]{2,1,0:T(8,128)(2,1)S(1)}, u32[]{:S(2)}, u32[]{:S(2)}) collective-permute-start(bf16[3,128,128]{2,1,0:T(8,128)(2,1)S(1)} %join.3.bundle_ref.refs_0_), channel_id=1, source_target_pairs={{0,1},{1,0},{2,3},{3,2},{4,5},{5,4},{6,7},{7,6},{8,9},{9,8},{10,11... | collective-permute-start | bytes 294920 | tf_op jit(solution)/shard_map/ppermute | solution.py:40
  37.9 5.7 %collective-permute-start.19 = (bf16[192,128]{1,0:T(8,128)(2,1)S(1)}, bf16[192,128]{1,0:T(8,128)(2,1)S(1)}, u32[]{:S(2)}, u32[]{:S(2)}) collective-permute-start(bf16[192,128]{1,0:T(8,128)(2,1)S(1)} %get-tuple-element.44), channel_id=1, source_target_pairs={{0,24},{8,16},{16,8},{24,0},{1,25},{9,17},{17,9},{25,1},{2,26},{10... | collective-permute-start | bytes 147464 | tf_op jit(solution)/shard_map/ppermute | solution.py:40
  39.3 4.3 %collective-permute-start.18 = (bf16[192,128]{1,0:T(8,128)(2,1)S(1)}, bf16[192,128]{1,0:T(8,128)(2,1)S(1)}, u32[]{:S(2)}, u32[]{:S(2)}) collective-permute-start(bf16[192,128]{1,0:T(8,128)(2,1)S(1)} %get-tuple-element.44), channel_id=1, source_target_pairs={{0,8},{8,0},{16,24},{24,16},{1,9},{9,1},{17,25},{25,17},{2,10},{10... | collective-permute-start | bytes 147464 | tf_op jit(solution)/shard_map/ppermute | solution.py:40
  39.9 3.7 %collective-permute-start.20 = (bf16[64,128]{1,0:T(8,128)(2,1)S(1)}, bf16[64,128]{1,0:T(8,128)(2,1)S(1)}, u32[]{:S(2)}, u32[]{:S(2)}) collective-permute-start(bf16[64,128]{1,0:T(8,128)(2,1)S(1)} %get-tuple-element.45.refs_0_), channel_id=1, source_target_pairs={{0,16},{8,24},{16,0},{24,8},{1,17},{9,25},{17,1},{25,9},{2,18},{10... | collective-permute-start | bytes 49160 | tf_op jit(solution)/shard_map/ppermute | solution.py:40
  44.4 1.4 %collective-permute-start.21 = (bf16[2,128,128]{2,1,0:T(8,128)(2,1)S(1)}, bf16[2,128,128]{2,1,0:T(8,128)(2,1)S(1)}, u32[]{:S(2)}, u32[]{:S(2)}) collective-permute-start(bf16[2,128,128]{2,1,0:T(8,128)(2,1)S(1)} %get-tuple-element.48), channel_id=1, source_target_pairs={{0,1},{1,0},{2,3},{3,2},{4,5},{5,4},{6,7},{7,6},{8,9},{9,8},{10,11... | collective-permute-start | bytes 196616 | tf_op jit(solution)/shard_map/ppermute | solution.py:40
  45.3 3.1 %collective-permute-start.22 = (bf16[2,128,128]{2,1,0:T(8,128)(2,1)S(1)}, bf16[2,128,128]{2,1,0:T(8,128)(2,1)S(1)}, u32[]{:S(2)}, u32[]{:S(2)}) collective-permute-start(bf16[2,128,128]{2,1,0:T(8,128)(2,1)S(1)} %get-tuple-element.51), channel_id=1, source_target_pairs={{0,1},{1,0},{2,3},{3,2},{4,5},{5,4},{6,7},{7,6},{8,9},{9,8},{10,11... | collective-permute-start | bytes 196616 | tf_op jit(solution)/shard_map/ppermute | solution.py:40
  45.8 5.3 %collective-permute-start.23 = (bf16[1,128,128]{2,1,0:T(8,128)(2,1)S(1)}, bf16[1,128,128]{2,1,0:T(8,128)(2,1)S(1)}, u32[]{:S(2)}, u32[]{:S(2)}) collective-permute-start(bf16[1,128,128]{2,1,0:T(8,128)(2,1)S(1)} %get-tuple-element.49.refs_0_), channel_id=1, source_target_pairs={{0,7},{1,6},{2,5},{3,4},{4,3},{5,2},{6,1},{7,0},{8,15},{9,14},{10,... | collective-permute-start | bytes 98312 | tf_op jit(solution)/shard_map/ppermute | solution.py:40
  47.9 4.6 %collective-permute-start.24 = (bf16[1,128,128]{2,1,0:T(8,128)(2,1)S(1)}, bf16[1,128,128]{2,1,0:T(8,128)(2,1)S(1)}, u32[]{:S(2)}, u32[]{:S(2)}) collective-permute-start(bf16[1,128,128]{2,1,0:T(8,128)(2,1)S(1)} %get-tuple-element.50.refs_1_), channel_id=1, source_target_pairs={{0,5},{1,4},{2,7},{3,6},{4,1},{5,0},{6,3},{7,2},{8,13},{9,12},{10,... | collective-permute-start | bytes 98312 | tf_op jit(solution)/shard_map/ppermute | solution.py:40
  48.4 4.1 %collective-permute-start.25 = (bf16[1,128,128]{2,1,0:T(8,128)(2,1)S(1)}, bf16[1,128,128]{2,1,0:T(8,128)(2,1)S(1)}, u32[]{:S(2)}, u32[]{:S(2)}) collective-permute-start(bf16[1,128,128]{2,1,0:T(8,128)(2,1)S(1)} %get-tuple-element.53), channel_id=1, source_target_pairs={{0,3},{1,2},{2,1},{3,0},{4,7},{5,6},{6,5},{7,4},{8,11},{9,10},{10,... | collective-permute-start | bytes 98312 | tf_op jit(solution)/shard_map/ppermute | solution.py:40

commit v17 on v14

--- a/solution.py
+++ b/solution.py
@@ -324,7 +324,7 @@
         last = step == ITERS - 1
         away = sorted(range(half, near), reverse=last)
         order = list(range(1, near))
-        if step == 0:
+        if step:
             order.sort(key=lambda mask: (mask == half, mask))
         parts = [cross(short, mask) for mask in order]
         twin = swap(short, "tile", 1)

time: 54.9 us -> 54.4 us (level)
  transfers between devices with their start and end apart: 26 -> 26, of which waited for: 12 -> 10; matrix products, arithmetic and copies ran while one was open for 0% -> 0% of each run, Pallas kernels for 12% -> 12%
where the time goes in v17:
time: 54.4 us; the launch traced here: 54.2 us
  starting transfers between devices  25.7 us (47%)
  waiting for transfers between devices  14.2 us (26%)
  Pallas kernels  10.4 us (19%)
  local copies, waits for them, and re-layouts  2.21 us (4%)
  between operations  0.87 us (2%)
  other arithmetic  0.85 us (2%)
    ppermute x26, starting transfers between devices, swap(): lax.ppermute(value, axis, [(i, i ^ mask) for i in range(lax.axis_size(axi...  25.7 us
    ppermute x26, waiting for transfers between devices, swap(): lax.ppermute(value, axis, [(i, i ^ mask) for i in range(lax.axis_size(axi...  14.2 us
    pallas_call x4, Pallas kernels, term(): call(partial(term_kernel, wanted, len(after)), in_specs=[pl.BlockSpec(mem...  2.59 us
    pallas_call x4, Pallas kernels, first(): call(partial(first_kernel, rows, spots, len(before)), shape(f32, blocks *...  2.36 us
    unnamed x8, local copies, waits for them, and re-layouts  2.21 us
    pallas_call x2, Pallas kernels, on_device(): call(partial(second_kernel, rows, cols, spots), (shape(bf16, pay_rows, wi...  1.74 us
    pallas_call x2, Pallas kernels, on_device(): call(partial(far_kernel, rows, cols, groups, ncells_all, spots_of(away, T...  1.45 us
  transfers between devices with their start and end apart: 26, of which 10 were waited for; matrix products, arithmetic and copies ran while one was open for 0% of the time, Pallas kernels for 12%

profile of v17, /device:TPU:0, one launch (start us, length us, event | category | flops | bytes accessed | tf_op | source)
XLA Modules:
  0.0 54.2 jit_solution(1854397325454817442)
XLA Ops:
  0.6 0.8 %fusion.refs_0_ = bf16[1,128,128]{2,1,0:T(8,128)(2,1)S(1)} fusion(f32[16,8,128]{2,1,0:T(8,128)} %param.4), kind=kLoop, calls=%fused_computation.1 | loop fusion | flops 32768 | bytes 98304 | tf_op jit(solution)/shard_map/convert_element_type | solution.py:277
  1.5 4.5 %collective-permute-start.3 = (bf16[1,128,128]{2,1,0:T(8,128)(2,1)S(1)}, bf16[1,128,128]{2,1,0:T(8,128)(2,1)S(1)}, u32[]{:S(2)}, u32[]{:S(2)}) collective-permute-start(bf16[1,128,128]{2,1,0:T(8,128)(2,1)S(1)} %fusion.refs_0_), channel_id=1, source_target_pairs={{0,7},{1,6},{2,5},{3,4},{4,3},{5,2},{6,1},{7,0},{8,15},{9,14},{10,... | collective-permute-start | bytes 98312 | tf_op jit(solution)/shard_map/ppermute | solution.py:40
  6.0 0.0 collective-permute-start.2
  6.0 0.9 %collective-permute-start.1 = (bf16[1,128,128]{2,1,0:T(8,128)(2,1)S(1)}, bf16[1,128,128]{2,1,0:T(8,128)(2,1)S(1)}, u32[]{:S(2)}, u32[]{:S(2)}) collective-permute-start(bf16[1,128,128]{2,1,0:T(8,128)(2,1)S(1)} %fusion.refs_0_), channel_id=1, source_target_pairs={{0,3},{1,2},{2,1},{3,0},{4,7},{5,6},{6,5},{7,4},{8,11},{9,10},{10,... | collective-permute-start | bytes 98312 | tf_op jit(solution)/shard_map/ppermute | solution.py:40
  6.9 2.2 %copy-done = bf16[256,8,1024]{2,1,0:T(8,128)(2,1)S(1)} copy-done((bf16[256,8,1024]{2,1,0:T(8,128)(2,1)S(1)}, bf16[256,8,1024]{2,1,0:T(8,128)(2,1)}, u32[]{:S(2)}) %copy-start) | copy-done | bytes 4194328
  9.1 0.4 load.1.factor_ref
  9.4 0.0 copy-start.1
  9.5 0.5 project_own.4.refs_0_.refs_2_
  9.9 0.6 %collective-permute-done.2.refs_3_ = bf16[1,128,128]{2,1,0:T(8,128)(2,1)S(1)} collective-permute-done((bf16[1,128,128]{2,1,0:T(8,128)(2,1)S(1)}, bf16[1,128,128]{2,1,0:T(8,128)(2,1)S(1)}, u32[]{:S(2)}, u32[]{:S(2)}) %collective-permute-start.2) | collective-permute-done | bytes 32800 | tf_op jit(solution)/shard_map/ppermute | solution.py:40
  10.5 0.0 collective-permute-done.1.refs_2_
  10.5 0.0 collective-permute-done.refs_1_.twin_ref
  10.5 0.4 collective-permute-start.4
  11.0 0.4 columns.2
  11.3 0.0 copy-start.3
  11.3 0.7 %project_own.5.diag_ref = f32[256,128]{1,0:T(8,128)S(1)} custom-call(bf16[2048,1024]{1,0:T(8,128)(2,1)S(1)} %load.1.factor_ref, bf16[3,128,128]{2,1,0:T(8,128)(2,1)S(1)} %join.2.bundle_ref.refs_0_, bf16[1,128,128]{2,1,0:T(8,128)(2,1)S(1)} %collective-permute-done.refs_1_.twin_ref, f32[256,128]{1,0:T(8,128)S(1)} %project_own.4.refs_0_.refs_2_), custom_call_target="tpu_custom_call" | custom-call | flops 268435456 | bytes 2097152 | tf_op jit(solution)/shard_map/project_own/pallas_call | solution.py:314
  12.1 0.0 collective-permute-done.4.fields_ref
  12.1 0.9 %project_across.2 = (bf16[192,128]{1,0:T(8,128)(2,1)S(1)}, bf16[64,128]{1,0:T(8,128)(2,1)S(1)}) custom-call(bf16[2048,1024]{1,0:T(8,128)(2,1)S(1)} %load.1.factor_ref, f32[256,128]{1,0:T(8,128)S(1)} %project_own.5.diag_ref, bf16[3,128,128]{2,1,0:T(8,128)(2,1)S(1)} %collective-permute-done.4.fields_ref, bf16[128,128]{1,0:T(8,128)(2,1)S(1)} %get-tuple-element.31.short_ref), custom_call_target="tpu_custom_call" | custom-call | flops 268435456 | bytes 2097152 | tf_op jit(solution)/shard_map/project_across/pallas_call | solution.py:348
  13.0 2.5 %collective-permute-start.6 = (bf16[192,128]{1,0:T(8,128)(2,1)S(1)}, bf16[192,128]{1,0:T(8,128)(2,1)S(1)}, u32[]{:S(2)}, u32[]{:S(2)}) collective-permute-start(bf16[192,128]{1,0:T(8,128)(2,1)S(1)} %get-tuple-element.32), channel_id=1, source_target_pairs={{0,24},{8,16},{16,8},{24,0},{1,25},{9,17},{17,9},{25,1},{2,26},{10... | collective-permute-start | bytes 147464 | tf_op jit(solution)/shard_map/ppermute | solution.py:40
  15.4 0.5 collective-permute-start.5
  16.0 0.5 collective-permute-start.7
  16.5 3.2 %collective-permute-done.7.refs_2_ = bf16[64,128]{1,0:T(8,128)(2,1)S(1)} collective-permute-done((bf16[64,128]{1,0:T(8,128)(2,1)S(1)}, bf16[64,128]{1,0:T(8,128)(2,1)S(1)}, u32[]{:S(2)}, u32[]{:S(2)}) %collective-permute-start.7) | collective-permute-done | bytes 16416 | tf_op jit(solution)/shard_map/ppermute | solution.py:40
  19.7 0.7 %term_first.2 = (bf16[128,2048]{1,0:T(8,128)(2,1)S(1)}, bf16[2,128,128]{2,1,0:T(8,128)(2,1)S(1)}) custom-call(f32[1,256]{1,0:T(1,128)S(1)} %bitcast.13, bf16[2048,1024]{1,0:T(8,128)(2,1)S(1)} %load.1.factor_ref, bf16[64,128]{1,0:T(8,128)(2,1)S(1)} %get-tuple-element.33.refs_0_, bf16[192,128]{1,0:T(8,128)(2,1)S(1)} %collective-permute-done.5.refs_0_.refs_1_, ...), custom_call_target="tpu_custom_call" | custom-call | flops 134217728 | bytes 2097152 | tf_op jit(solution)/shard_map/term_first/pallas_call | solution.py:357
  20.5 0.1 collective-permute-start.8
  20.5 0.0 copy-start.2
  20.6 0.8 %term.4 = (f32[2,128,128]{2,1,0:T(8,128)S(1)}, bf16[2,128,128]{2,1,0:T(8,128)(2,1)S(1)}) custom-call(bf16[128,2048]{1,0:T(8,128)(2,1)S(1)} %get-tuple-element.34.coef_ref, bf16[2048,1024]{1,0:T(8,128)(2,1)S(1)} %load.1.factor_ref), custom_call_target="tpu_custom_call" | custom-call | flops 268435456 | bytes 2097152 | tf_op jit(solution)/shard_map/term/pallas_call | solution.py:367
  21.4 0.5 collective-permute-start.9
  21.9 0.0 collective-permute-done.8.got_ref
  21.9 1.9 %collective-permute-start.10 = (bf16[1,128,128]{2,1,0:T(8,128)(2,1)S(1)}, bf16[1,128,128]{2,1,0:T(8,128)(2,1)S(1)}, u32[]{:S(2)}, u32[]{:S(2)}) collective-permute-start(bf16[1,128,128]{2,1,0:T(8,128)(2,1)S(1)} %get-tuple-element.37.refs_0_), channel_id=1, source_target_pairs={{0,5},{1,4},{2,7},{3,6},{4,1},{5,0},{6,3},{7,2},{8,13},{9,12},{10,... | collective-permute-start | bytes 98312 | tf_op jit(solution)/shard_map/ppermute | solution.py:40
  23.8 1.3 %collective-permute-start.11 = (bf16[1,128,128]{2,1,0:T(8,128)(2,1)S(1)}, bf16[1,128,128]{2,1,0:T(8,128)(2,1)S(1)}, u32[]{:S(2)}, u32[]{:S(2)}) collective-permute-start(bf16[1,128,128]{2,1,0:T(8,128)(2,1)S(1)} %get-tuple-element.38.refs_1_), channel_id=1, source_target_pairs={{0,7},{1,6},{2,5},{3,4},{4,3},{5,2},{6,1},{7,0},{8,15},{9,14},{10,... | collective-permute-start | bytes 98312 | tf_op jit(solution)/shard_map/ppermute | solution.py:40
  25.1 0.5 term.5.mine_ref
  25.6 0.5 collective-permute-start.12
  26.1 0.2 local.2.base_ref
  26.3 0.1 collective-permute-done.10.refs_1_
  26.4 2.8 %collective-permute-done.11.refs_2_ = bf16[1,128,128]{2,1,0:T(8,128)(2,1)S(1)} collective-permute-done((bf16[1,128,128]{2,1,0:T(8,128)(2,1)S(1)}, bf16[1,128,128]{2,1,0:T(8,128)(2,1)S(1)}, u32[]{:S(2)}, u32[]{:S(2)}) %collective-permute-start.11) | collective-permute-done | bytes 32800 | tf_op jit(solution)/shard_map/ppermute | solution.py:40
  29.1 0.7 %collective-permute-done.12.refs_3_ = bf16[1,128,128]{2,1,0:T(8,128)(2,1)S(1)} collective-permute-done((bf16[1,128,128]{2,1,0:T(8,128)(2,1)S(1)}, bf16[1,128,128]{2,1,0:T(8,128)(2,1)S(1)}, u32[]{:S(2)}, u32[]{:S(2)}) %collective-permute-start.12) | collective-permute-done | bytes 32800 | tf_op jit(solution)/shard_map/ppermute | solution.py:40
  29.9 0.9 %collective-permute-start.16 = (bf16[1,128,128]{2,1,0:T(8,128)(2,1)S(1)}, bf16[1,128,128]{2,1,0:T(8,128)(2,1)S(1)}, u32[]{:S(2)}, u32[]{:S(2)}) collective-permute-start(bf16[1,128,128]{2,1,0:T(8,128)(2,1)S(1)} %get-tuple-element.43.refs_0_), channel_id=1, source_target_pairs={{0,5},{1,4},{2,7},{3,6},{4,1},{5,0},{6,3},{7,2},{8,13},{9,12},{10,... | collective-permute-start | bytes 98312 | tf_op jit(solution)/shard_map/ppermute | solution.py:40
  30.8 1.0 %collective-permute-start.15 = (bf16[1,128,128]{2,1,0:T(8,128)(2,1)S(1)}, bf16[1,128,128]{2,1,0:T(8,128)(2,1)S(1)}, u32[]{:S(2)}, u32[]{:S(2)}) collective-permute-start(bf16[1,128,128]{2,1,0:T(8,128)(2,1)S(1)} %get-tuple-element.43.refs_0_), channel_id=1, source_target_pairs={{0,7},{1,6},{2,5},{3,4},{4,3},{5,2},{6,1},{7,0},{8,15},{9,14},{10,... | collective-permute-start | bytes 98312 | tf_op jit(solution)/shard_map/ppermute | solution.py:40
  31.8 1.1 %collective-permute-start.14 = (bf16[1,128,128]{2,1,0:T(8,128)(2,1)S(1)}, bf16[1,128,128]{2,1,0:T(8,128)(2,1)S(1)}, u32[]{:S(2)}, u32[]{:S(2)}) collective-permute-start(bf16[1,128,128]{2,1,0:T(8,128)(2,1)S(1)} %get-tuple-element.43.refs_0_), channel_id=1, source_target_pairs={{0,3},{1,2},{2,1},{3,0},{4,7},{5,6},{6,5},{7,4},{8,11},{9,10},{10,... | collective-permute-start | bytes 98312 | tf_op jit(solution)/shard_map/ppermute | solution.py:40
  32.9 0.4 collective-permute-start.13
  33.3 0.5 project_own.6.refs_0_.refs_2_
  33.8 0.5 collective-permute-done.16.refs_4_
  34.3 1.7 %collective-permute-done.15.refs_3_ = bf16[1,128,128]{2,1,0:T(8,128)(2,1)S(1)} collective-permute-done((bf16[1,128,128]{2,1,0:T(8,128)(2,1)S(1)}, bf16[1,128,128]{2,1,0:T(8,128)(2,1)S(1)}, u32[]{:S(2)}, u32[]{:S(2)}) %collective-permute-start.15) | collective-permute-done | bytes 32800 | tf_op jit(solution)/shard_map/ppermute | solution.py:40
  36.0 0.0 collective-permute-done.14.refs_2_
  36.0 0.0 collective-permute-done.13.refs_1_.twin_ref
  36.0 0.7 %collective-permute-start.17 = (bf16[3,128,128]{2,1,0:T(8,128)(2,1)S(1)}, bf16[3,128,128]{2,1,0:T(8,128)(2,1)S(1)}, u32[]{:S(2)}, u32[]{:S(2)}) collective-permute-start(bf16[3,128,128]{2,1,0:T(8,128)(2,1)S(1)} %join.3.bundle_ref.refs_0_), channel_id=1, source_target_pairs={{0,1},{1,0},{2,3},{3,2},{4,5},{5,4},{6,7},{7,6},{8,9},{9,8},{10,11... | collective-permute-start | bytes 294920 | tf_op jit(solution)/shard_map/ppermute | solution.py:40
  36.7 0.3 columns.3
  37.0 0.7 %project_own.7.diag_ref = f32[256,128]{1,0:T(8,128)S(1)} custom-call(bf16[2048,1024]{1,0:T(8,128)(2,1)S(1)} %load.1.factor_ref, bf16[3,128,128]{2,1,0:T(8,128)(2,1)S(1)} %join.3.bundle_ref.refs_0_, bf16[1,128,128]{2,1,0:T(8,128)(2,1)S(1)} %collective-permute-done.13.refs_1_.twin_ref, f32[256,128]{1,0:T(8,128)S(1)} %project_own.6.refs_0_.refs_2_), custom_call_target="tpu_custom_call" | custom-call | flops 268435456 | bytes 2097152 | tf_op jit(solution)/shard_map/project_own/pallas_call | solution.py:314
  37.8 0.9 %project_across.3 = (bf16[192,128]{1,0:T(8,128)(2,1)S(1)}, bf16[64,128]{1,0:T(8,128)(2,1)S(1)}) custom-call(bf16[2048,1024]{1,0:T(8,128)(2,1)S(1)} %load.1.factor_ref, f32[256,128]{1,0:T(8,128)S(1)} %project_own.7.diag_ref, bf16[3,128,128]{2,1,0:T(8,128)(2,1)S(1)} %collective-permute-done.17.fields_ref, bf16[128,128]{1,0:T(8,128)(2,1)S(1)} %get-tuple-element.45.short_ref), custom_call_target="tpu_custom_call" | custom-call | flops 268435456 | bytes 2097152 | tf_op jit(solution)/shard_map/project_across/pallas_call | solution.py:348
  38.6 1.5 %collective-permute-start.19 = (bf16[192,128]{1,0:T(8,128)(2,1)S(1)}, bf16[192,128]{1,0:T(8,128)(2,1)S(1)}, u32[]{:S(2)}, u32[]{:S(2)}) collective-permute-start(bf16[192,128]{1,0:T(8,128)(2,1)S(1)} %get-tuple-element.46), channel_id=1, source_target_pairs={{0,24},{8,16},{16,8},{24,0},{1,25},{9,17},{17,9},{25,1},{2,26},{10... | collective-permute-start | bytes 147464 | tf_op jit(solution)/shard_map/ppermute | solution.py:40
  40.1 0.5 %collective-permute-start.18 = (bf16[192,128]{1,0:T(8,128)(2,1)S(1)}, bf16[192,128]{1,0:T(8,128)(2,1)S(1)}, u32[]{:S(2)}, u32[]{:S(2)}) collective-permute-start(bf16[192,128]{1,0:T(8,128)(2,1)S(1)} %get-tuple-element.46), channel_id=1, source_target_pairs={{0,8},{8,0},{16,24},{24,16},{1,9},{9,1},{17,25},{25,17},{2,10},{10... | collective-permute-start | bytes 147464 | tf_op jit(solution)/shard_map/ppermute | solution.py:40
  40.6 1.5 %collective-permute-start.20 = (bf16[64,128]{1,0:T(8,128)(2,1)S(1)}, bf16[64,128]{1,0:T(8,128)(2,1)S(1)}, u32[]{:S(2)}, u32[]{:S(2)}) collective-permute-start(bf16[64,128]{1,0:T(8,128)(2,1)S(1)} %get-tuple-element.47.refs_0_), channel_id=1, source_target_pairs={{0,16},{8,24},{16,0},{24,8},{1,17},{9,25},{17,1},{25,9},{2,18},{10... | collective-permute-start | bytes 49160 | tf_op jit(solution)/shard_map/ppermute | solution.py:40
  42.2 2.2 %collective-permute-done.20.refs_2_ = bf16[64,128]{1,0:T(8,128)(2,1)S(1)} collective-permute-done((bf16[64,128]{1,0:T(8,128)(2,1)S(1)}, bf16[64,128]{1,0:T(8,128)(2,1)S(1)}, u32[]{:S(2)}, u32[]{:S(2)}) %collective-permute-start.20) | collective-permute-done | bytes 16416 | tf_op jit(solution)/shard_map/ppermute | solution.py:40
  44.4 0.7 %term_first.3 = (bf16[128,2048]{1,0:T(8,128)(2,1)S(1)}, bf16[2,128,128]{2,1,0:T(8,128)(2,1)S(1)}) custom-call(f32[1,256]{1,0:T(1,128)S(1)} %bitcast.14, bf16[2048,1024]{1,0:T(8,128)(2,1)S(1)} %load.1.factor_ref, bf16[64,128]{1,0:T(8,128)(2,1)S(1)} %get-tuple-element.47.refs_0_, bf16[192,128]{1,0:T(8,128)(2,1)S(1)} %collective-permute-done.18.refs_0_.refs_1_, ...), custom_call_target="tpu_custom_call" | custom-call | flops 134217728 | bytes 2097152 | tf_op jit(solution)/shard_map/term_first/pallas_call | solution.py:357
  45.1 0.1 collective-permute-start.21
  45.2 0.8 %term.6 = (f32[2,128,128]{2,1,0:T(8,128)S(1)}, bf16[2,128,128]{2,1,0:T(8,128)(2,1)S(1)}) custom-call(bf16[128,2048]{1,0:T(8,128)(2,1)S(1)} %get-tuple-element.48.coef_ref, bf16[2048,1024]{1,0:T(8,128)(2,1)S(1)} %load.1.factor_ref), custom_call_target="tpu_custom_call" | custom-call | flops 268435456 | bytes 2097152 | tf_op jit(solution)/shard_map/term/pallas_call | solution.py:367
  46.0 0.6 %collective-permute-start.22 = (bf16[2,128,128]{2,1,0:T(8,128)(2,1)S(1)}, bf16[2,128,128]{2,1,0:T(8,128)(2,1)S(1)}, u32[]{:S(2)}, u32[]{:S(2)}) collective-permute-start(bf16[2,128,128]{2,1,0:T(8,128)(2,1)S(1)} %get-tuple-element.53), channel_id=1, source_target_pairs={{0,1},{1,0},{2,3},{3,2},{4,5},{5,4},{6,7},{7,6},{8,9},{9,8},{10,11... | collective-permute-start | bytes 196616 | tf_op jit(solution)/shard_map/ppermute | solution.py:40
  46.6 0.0 collective-permute-done.21.got_ref
  46.6 1.8 %collective-permute-start.23 = (bf16[1,128,128]{2,1,0:T(8,128)(2,1)S(1)}, bf16[1,128,128]{2,1,0:T(8,128)(2,1)S(1)}, u32[]{:S(2)}, u32[]{:S(2)}) collective-permute-start(bf16[1,128,128]{2,1,0:T(8,128)(2,1)S(1)} %get-tuple-element.51.refs_0_), channel_id=1, source_target_pairs={{0,7},{1,6},{2,5},{3,4},{4,3},{5,2},{6,1},{7,0},{8,15},{9,14},{10,... | collective-permute-start | bytes 98312 | tf_op jit(solution)/shard_map/ppermute | solution.py:40
  48.4 0.5 term.7.mine_ref
  48.9 2.1 %collective-permute-start.25 = (bf16[1,128,128]{2,1,0:T(8,128)(2,1)S(1)}, bf16[1,128,128]{2,1,0:T(8,128)(2,1)S(1)}, u32[]{:S(2)}, u32[]{:S(2)}) collective-permute-start(bf16[1,128,128]{2,1,0:T(8,128)(2,1)S(1)} %get-tuple-element.55), channel_id=1, source_target_pairs={{0,3},{1,2},{2,1},{3,0},{4,7},{5,6},{6,5},{7,4},{8,11},{9,10},{10,... | collective-permute-start | bytes 98312 | tf_op jit(solution)/shard_map/ppermute | solution.py:40
  51.0 0.2 local.3.base_ref
  51.2 0.8 %collective-permute-done.23.refs_1_ = bf16[1,128,128]{2,1,0:T(8,128)(2,1)S(1)} collective-permute-done((bf16[1,128,128]{2,1,0:T(8,128)(2,1)S(1)}, bf16[1,128,128]{2,1,0:T(8,128)(2,1)S(1)}, u32[]{:S(2)}, u32[]{:S(2)}) %collective-permute-start.23) | collective-permute-done | bytes 32800 | tf_op jit(solution)/shard_map/ppermute | solution.py:40
  51.9 1.6 %collective-permute-done.24.refs_2_ = bf16[1,128,128]{2,1,0:T(8,128)(2,1)S(1)} collective-permute-done((bf16[1,128,128]{2,1,0:T(8,128)(2,1)S(1)}, bf16[1,128,128]{2,1,0:T(8,128)(2,1)S(1)}, u32[]{:S(2)}, u32[]{:S(2)}) %collective-permute-start.24) | collective-permute-done | bytes 32800 | tf_op jit(solution)/shard_map/ppermute | solution.py:40
  53.5 0.7 %update.3 = (f32[128,128]{1,0:T(8,128)}, f32[128,128]{1,0:T(8,128)}) custom-call(f32[128,128]{1,0:T(8,128)S(1)} %get-tuple-element.42.x_ref, f32[128,128]{1,0:T(8,128)S(1)} %local.3.base_ref, f32[1,128,128]{2,1,0:T(8,128)S(1)} %get-tuple-element.54.refs_0_, bf16[1,128,128]{2,1,0:T(8,128)(2,1)S(1)} %collective-permute-done.23.refs_1_, ...), custom_call_target="tpu_custom_call" | custom-call | bytes 262144 | tf_op jit(solution)/shard_map/update/pallas_call | solution.py:395
  (22 shorter events, 0.1 us)
Async XLA Ops:
  1.5 8.4 %collective-permute-start.3 = (bf16[1,128,128]{2,1,0:T(8,128)(2,1)S(1)}, bf16[1,128,128]{2,1,0:T(8,128)(2,1)S(1)}, u32[]{:S(2)}, u32[]{:S(2)}) collective-permute-start(bf16[1,128,128]{2,1,0:T(8,128)(2,1)S(1)} %fusion.refs_0_), channel_id=1, source_target_pairs={{0,7},{1,6},{2,5},{3,4},{4,3},{5,2},{6,1},{7,0},{8,15},{9,14},{10,... | collective-permute-start | bytes 98312 | tf_op jit(solution)/shard_map/ppermute | solution.py:40
  6.0 4.5 %collective-permute-start.2 = (bf16[1,128,128]{2,1,0:T(8,128)(2,1)S(1)}, bf16[1,128,128]{2,1,0:T(8,128)(2,1)S(1)}, u32[]{:S(2)}, u32[]{:S(2)}) collective-permute-start(bf16[1,128,128]{2,1,0:T(8,128)(2,1)S(1)} %fusion.refs_0_), channel_id=1, source_target_pairs={{0,5},{1,4},{2,7},{3,6},{4,1},{5,0},{6,3},{7,2},{8,13},{9,12},{10,... | collective-permute-start | bytes 98312 | tf_op jit(solution)/shard_map/ppermute | solution.py:40
  6.0 4.5 %collective-permute-start.1 = (bf16[1,128,128]{2,1,0:T(8,128)(2,1)S(1)}, bf16[1,128,128]{2,1,0:T(8,128)(2,1)S(1)}, u32[]{:S(2)}, u32[]{:S(2)}) collective-permute-start(bf16[1,128,128]{2,1,0:T(8,128)(2,1)S(1)} %fusion.refs_0_), channel_id=1, source_target_pairs={{0,3},{1,2},{2,1},{3,0},{4,7},{5,6},{6,5},{7,4},{8,11},{9,10},{10,... | collective-permute-start | bytes 98312 | tf_op jit(solution)/shard_map/ppermute | solution.py:40
  6.9 3.6 %collective-permute-start = (bf16[1,128,128]{2,1,0:T(8,128)(2,1)S(1)}, bf16[1,128,128]{2,1,0:T(8,128)(2,1)S(1)}, u32[]{:S(2)}, u32[]{:S(2)}) collective-permute-start(bf16[1,128,128]{2,1,0:T(8,128)(2,1)S(1)} %fusion.refs_0_), channel_id=1, source_target_pairs={{0,1},{1,0},{2,3},{3,2},{4,5},{5,4},{6,7},{7,6},{8,9},{9,8},{10,11... | collective-permute-start | bytes 98312 | tf_op jit(solution)/shard_map/ppermute | solution.py:40
  6.9 2.2 %copy-start = (bf16[256,8,1024]{2,1,0:T(8,128)(2,1)S(1)}, bf16[256,8,1024]{2,1,0:T(8,128)(2,1)}, u32[]{:S(2)}) copy-start(bf16[256,8,1024]{2,1,0:T(8,128)(2,1)} %param.6) | copy-start | bytes 12582916
  9.4 1.5 %copy-start.1 = (f32[16,8,128]{2,1,0:T(8,128)S(1)}, f32[16,8,128]{2,1,0:T(8,128)}, u32[]{:S(2)}) copy-start(f32[16,8,128]{2,1,0:T(8,128)} %param.4) | copy-start | bytes 196612
  10.5 1.6 %collective-permute-start.4 = (bf16[3,128,128]{2,1,0:T(8,128)(2,1)S(1)}, bf16[3,128,128]{2,1,0:T(8,128)(2,1)S(1)}, u32[]{:S(2)}, u32[]{:S(2)}) collective-permute-start(bf16[3,128,128]{2,1,0:T(8,128)(2,1)S(1)} %join.2.bundle_ref.refs_0_), channel_id=1, source_target_pairs={{0,1},{1,0},{2,3},{3,2},{4,5},{5,4},{6,7},{7,6},{8,9},{9,8},{10,11... | collective-permute-start | bytes 294920 | tf_op jit(solution)/shard_map/ppermute | solution.py:40
  11.3 8.4 %copy-start.3 = (f32[256]{0:T(256)S(1)}, f32[256]{0:T(256)}, u32[]{:S(2)}) copy-start(f32[256]{0:T(256)} %param.7) | copy-start | bytes 3076
  13.0 6.8 %collective-permute-start.6 = (bf16[192,128]{1,0:T(8,128)(2,1)S(1)}, bf16[192,128]{1,0:T(8,128)(2,1)S(1)}, u32[]{:S(2)}, u32[]{:S(2)}) collective-permute-start(bf16[192,128]{1,0:T(8,128)(2,1)S(1)} %get-tuple-element.32), channel_id=1, source_target_pairs={{0,24},{8,16},{16,8},{24,0},{1,25},{9,17},{17,9},{25,1},{2,26},{10... | collective-permute-start | bytes 147464 | tf_op jit(solution)/shard_map/ppermute | solution.py:40
  15.4 4.3 %collective-permute-start.5 = (bf16[192,128]{1,0:T(8,128)(2,1)S(1)}, bf16[192,128]{1,0:T(8,128)(2,1)S(1)}, u32[]{:S(2)}, u32[]{:S(2)}) collective-permute-start(bf16[192,128]{1,0:T(8,128)(2,1)S(1)} %get-tuple-element.32), channel_id=1, source_target_pairs={{0,8},{8,0},{16,24},{24,16},{1,9},{9,1},{17,25},{25,17},{2,10},{10... | collective-permute-start | bytes 147464 | tf_op jit(solution)/shard_map/ppermute | solution.py:40
  16.0 3.7 %collective-permute-start.7 = (bf16[64,128]{1,0:T(8,128)(2,1)S(1)}, bf16[64,128]{1,0:T(8,128)(2,1)S(1)}, u32[]{:S(2)}, u32[]{:S(2)}) collective-permute-start(bf16[64,128]{1,0:T(8,128)(2,1)S(1)} %get-tuple-element.33.refs_0_), channel_id=1, source_target_pairs={{0,16},{8,24},{16,0},{24,8},{1,17},{9,25},{17,1},{25,9},{2,18},{10... | collective-permute-start | bytes 49160 | tf_op jit(solution)/shard_map/ppermute | solution.py:40
  20.5 1.4 %collective-permute-start.8 = (bf16[2,128,128]{2,1,0:T(8,128)(2,1)S(1)}, bf16[2,128,128]{2,1,0:T(8,128)(2,1)S(1)}, u32[]{:S(2)}, u32[]{:S(2)}) collective-permute-start(bf16[2,128,128]{2,1,0:T(8,128)(2,1)S(1)} %get-tuple-element.36), channel_id=1, source_target_pairs={{0,1},{1,0},{2,3},{3,2},{4,5},{5,4},{6,7},{7,6},{8,9},{9,8},{10,11... | collective-permute-start | bytes 196616 | tf_op jit(solution)/shard_map/ppermute | solution.py:40
  20.5 5.5 %copy-start.2 = (f32[8,128]{1,0:T(8,128)S(1)}, f32[8,128]{1,0:T(8,128)}, u32[]{:S(2)}) copy-start(f32[8,128]{1,0:T(8,128)} %amp_ref.3) | copy-start | bytes 12292
  21.4 4.2 %collective-permute-start.9 = (bf16[2,128,128]{2,1,0:T(8,128)(2,1)S(1)}, bf16[2,128,128]{2,1,0:T(8,128)(2,1)S(1)}, u32[]{:S(2)}, u32[]{:S(2)}) collective-permute-start(bf16[2,128,128]{2,1,0:T(8,128)(2,1)S(1)} %get-tuple-element.39), channel_id=1, source_target_pairs={{0,1},{1,0},{2,3},{3,2},{4,5},{5,4},{6,7},{7,6},{8,9},{9,8},{10,11... | collective-permute-start | bytes 196616 | tf_op jit(solution)/shard_map/ppermute | solution.py:40
  21.9 4.4 %collective-permute-start.10 = (bf16[1,128,128]{2,1,0:T(8,128)(2,1)S(1)}, bf16[1,128,128]{2,1,0:T(8,128)(2,1)S(1)}, u32[]{:S(2)}, u32[]{:S(2)}) collective-permute-start(bf16[1,128,128]{2,1,0:T(8,128)(2,1)S(1)} %get-tuple-element.37.refs_0_), channel_id=1, source_target_pairs={{0,5},{1,4},{2,7},{3,6},{4,1},{5,0},{6,3},{7,2},{8,13},{9,12},{10,... | collective-permute-start | bytes 98312 | tf_op jit(solution)/shard_map/ppermute | solution.py:40
  23.8 5.3 %collective-permute-start.11 = (bf16[1,128,128]{2,1,0:T(8,128)(2,1)S(1)}, bf16[1,128,128]{2,1,0:T(8,128)(2,1)S(1)}, u32[]{:S(2)}, u32[]{:S(2)}) collective-permute-start(bf16[1,128,128]{2,1,0:T(8,128)(2,1)S(1)} %get-tuple-element.38.refs_1_), channel_id=1, source_target_pairs={{0,7},{1,6},{2,5},{3,4},{4,3},{5,2},{6,1},{7,0},{8,15},{9,14},{10,... | collective-permute-start | bytes 98312 | tf_op jit(solution)/shard_map/ppermute | solution.py:40
  25.6 4.3 %collective-permute-start.12 = (bf16[1,128,128]{2,1,0:T(8,128)(2,1)S(1)}, bf16[1,128,128]{2,1,0:T(8,128)(2,1)S(1)}, u32[]{:S(2)}, u32[]{:S(2)}) collective-permute-start(bf16[1,128,128]{2,1,0:T(8,128)(2,1)S(1)} %get-tuple-element.41), channel_id=1, source_target_pairs={{0,3},{1,2},{2,1},{3,0},{4,7},{5,6},{6,5},{7,4},{8,11},{9,10},{10,... | collective-permute-start | bytes 98312 | tf_op jit(solution)/shard_map/ppermute | solution.py:40
  29.9 4.4 %collective-permute-start.16 = (bf16[1,128,128]{2,1,0:T(8,128)(2,1)S(1)}, bf16[1,128,128]{2,1,0:T(8,128)(2,1)S(1)}, u32[]{:S(2)}, u32[]{:S(2)}) collective-permute-start(bf16[1,128,128]{2,1,0:T(8,128)(2,1)S(1)} %get-tuple-element.43.refs_0_), channel_id=1, source_target_pairs={{0,5},{1,4},{2,7},{3,6},{4,1},{5,0},{6,3},{7,2},{8,13},{9,12},{10,... | collective-permute-start | bytes 98312 | tf_op jit(solution)/shard_map/ppermute | solution.py:40
  30.8 5.1 %collective-permute-start.15 = (bf16[1,128,128]{2,1,0:T(8,128)(2,1)S(1)}, bf16[1,128,128]{2,1,0:T(8,128)(2,1)S(1)}, u32[]{:S(2)}, u32[]{:S(2)}) collective-permute-start(bf16[1,128,128]{2,1,0:T(8,128)(2,1)S(1)} %get-tuple-element.43.refs_0_), channel_id=1, source_target_pairs={{0,7},{1,6},{2,5},{3,4},{4,3},{5,2},{6,1},{7,0},{8,15},{9,14},{10,... | collective-permute-start | bytes 98312 | tf_op jit(solution)/shard_map/ppermute | solution.py:40
  31.8 4.2 %collective-permute-start.14 = (bf16[1,128,128]{2,1,0:T(8,128)(2,1)S(1)}, bf16[1,128,128]{2,1,0:T(8,128)(2,1)S(1)}, u32[]{:S(2)}, u32[]{:S(2)}) collective-permute-start(bf16[1,128,128]{2,1,0:T(8,128)(2,1)S(1)} %get-tuple-element.43.refs_0_), channel_id=1, source_target_pairs={{0,3},{1,2},{2,1},{3,0},{4,7},{5,6},{6,5},{7,4},{8,11},{9,10},{10,... | collective-permute-start | bytes 98312 | tf_op jit(solution)/shard_map/ppermute | solution.py:40
  32.9 3.1 %collective-permute-start.13 = (bf16[1,128,128]{2,1,0:T(8,128)(2,1)S(1)}, bf16[1,128,128]{2,1,0:T(8,128)(2,1)S(1)}, u32[]{:S(2)}, u32[]{:S(2)}) collective-permute-start(bf16[1,128,128]{2,1,0:T(8,128)(2,1)S(1)} %get-tuple-element.43.refs_0_), channel_id=1, source_target_pairs={{0,1},{1,0},{2,3},{3,2},{4,5},{5,4},{6,7},{7,6},{8,9},{9,8},{10,11... | collective-permute-start | bytes 98312 | tf_op jit(solution)/shard_map/ppermute | solution.py:40
  36.0 1.8 %collective-permute-start.17 = (bf16[3,128,128]{2,1,0:T(8,128)(2,1)S(1)}, bf16[3,128,128]{2,1,0:T(8,128)(2,1)S(1)}, u32[]{:S(2)}, u32[]{:S(2)}) collective-permute-start(bf16[3,128,128]{2,1,0:T(8,128)(2,1)S(1)} %join.3.bundle_ref.refs_0_), channel_id=1, source_target_pairs={{0,1},{1,0},{2,3},{3,2},{4,5},{5,4},{6,7},{7,6},{8,9},{9,8},{10,11... | collective-permute-start | bytes 294920 | tf_op jit(solution)/shard_map/ppermute | solution.py:40
  38.6 5.8 %collective-permute-start.19 = (bf16[192,128]{1,0:T(8,128)(2,1)S(1)}, bf16[192,128]{1,0:T(8,128)(2,1)S(1)}, u32[]{:S(2)}, u32[]{:S(2)}) collective-permute-start(bf16[192,128]{1,0:T(8,128)(2,1)S(1)} %get-tuple-element.46), channel_id=1, source_target_pairs={{0,24},{8,16},{16,8},{24,0},{1,25},{9,17},{17,9},{25,1},{2,26},{10... | collective-permute-start | bytes 147464 | tf_op jit(solution)/shard_map/ppermute | solution.py:40
  40.1 4.3 %collective-permute-start.18 = (bf16[192,128]{1,0:T(8,128)(2,1)S(1)}, bf16[192,128]{1,0:T(8,128)(2,1)S(1)}, u32[]{:S(2)}, u32[]{:S(2)}) collective-permute-start(bf16[192,128]{1,0:T(8,128)(2,1)S(1)} %get-tuple-element.46), channel_id=1, source_target_pairs={{0,8},{8,0},{16,24},{24,16},{1,9},{9,1},{17,25},{25,17},{2,10},{10... | collective-permute-start | bytes 147464 | tf_op jit(solution)/shard_map/ppermute | solution.py:40
  40.6 3.7 %collective-permute-start.20 = (bf16[64,128]{1,0:T(8,128)(2,1)S(1)}, bf16[64,128]{1,0:T(8,128)(2,1)S(1)}, u32[]{:S(2)}, u32[]{:S(2)}) collective-permute-start(bf16[64,128]{1,0:T(8,128)(2,1)S(1)} %get-tuple-element.47.refs_0_), channel_id=1, source_target_pairs={{0,16},{8,24},{16,0},{24,8},{1,17},{9,25},{17,1},{25,9},{2,18},{10... | collective-permute-start | bytes 49160 | tf_op jit(solution)/shard_map/ppermute | solution.py:40
  45.1 1.4 %collective-permute-start.21 = (bf16[2,128,128]{2,1,0:T(8,128)(2,1)S(1)}, bf16[2,128,128]{2,1,0:T(8,128)(2,1)S(1)}, u32[]{:S(2)}, u32[]{:S(2)}) collective-permute-start(bf16[2,128,128]{2,1,0:T(8,128)(2,1)S(1)} %get-tuple-element.50), channel_id=1, source_target_pairs={{0,1},{1,0},{2,3},{3,2},{4,5},{5,4},{6,7},{7,6},{8,9},{9,8},{10,11... | collective-permute-start | bytes 196616 | tf_op jit(solution)/shard_map/ppermute | solution.py:40
  46.0 2.8 %collective-permute-start.22 = (bf16[2,128,128]{2,1,0:T(8,128)(2,1)S(1)}, bf16[2,128,128]{2,1,0:T(8,128)(2,1)S(1)}, u32[]{:S(2)}, u32[]{:S(2)}) collective-permute-start(bf16[2,128,128]{2,1,0:T(8,128)(2,1)S(1)} %get-tuple-element.53), channel_id=1, source_target_pairs={{0,1},{1,0},{2,3},{3,2},{4,5},{5,4},{6,7},{7,6},{8,9},{9,8},{10,11... | collective-permute-start | bytes 196616 | tf_op jit(solution)/shard_map/ppermute | solution.py:40
  46.6 5.3 %collective-permute-start.23 = (bf16[1,128,128]{2,1,0:T(8,128)(2,1)S(1)}, bf16[1,128,128]{2,1,0:T(8,128)(2,1)S(1)}, u32[]{:S(2)}, u32[]{:S(2)}) collective-permute-start(bf16[1,128,128]{2,1,0:T(8,128)(2,1)S(1)} %get-tuple-element.51.refs_0_), channel_id=1, source_target_pairs={{0,7},{1,6},{2,5},{3,4},{4,3},{5,2},{6,1},{7,0},{8,15},{9,14},{10,... | collective-permute-start | bytes 98312 | tf_op jit(solution)/shard_map/ppermute | solution.py:40
  48.4 5.2 %collective-permute-start.24 = (bf16[1,128,128]{2,1,0:T(8,128)(2,1)S(1)}, bf16[1,128,128]{2,1,0:T(8,128)(2,1)S(1)}, u32[]{:S(2)}, u32[]{:S(2)}) collective-permute-start(bf16[1,128,128]{2,1,0:T(8,128)(2,1)S(1)} %get-tuple-element.52.refs_1_), channel_id=1, source_target_pairs={{0,5},{1,4},{2,7},{3,6},{4,1},{5,0},{6,3},{7,2},{8,13},{9,12},{10,... | collective-permute-start | bytes 98312 | tf_op jit(solution)/shard_map/ppermute | solution.py:40
  48.9 4.6 %collective-permute-start.25 = (bf16[1,128,128]{2,1,0:T(8,128)(2,1)S(1)}, bf16[1,128,128]{2,1,0:T(8,128)(2,1)S(1)}, u32[]{:S(2)}, u32[]{:S(2)}) collective-permute-start(bf16[1,128,128]{2,1,0:T(8,128)(2,1)S(1)} %get-tuple-element.55), channel_id=1, source_target_pairs={{0,3},{1,2},{2,1},{3,0},{4,7},{5,6},{6,5},{7,4},{8,11},{9,10},{10,... | collective-permute-start | bytes 98312 | tf_op jit(solution)/shard_map/ppermute | solution.py:40
